TPU v7x, 32 devices: a whole 2x2x4 slice. The times are simulated.
32 devices in a mesh: groups: 2 (over x), row: 16 (over z, y, core).
Axes of the slice: x: 2, y: 2, z: 4, core: 2. Of those that a mesh axis runs over, the one named last changes fastest.
Arguments:
- tiles: bfloat16 [1536, 256, 256], P(('groups', 'row')), parts along dimension 0, may hold values from -0.375 to 0.375
- tile_rows: int32 [1536], P(('groups', 'row')), parts along dimension 0, may hold values from 0 to 7
- tile_cols: int32 [1536], P(('groups', 'row')), parts along dimension 0, may hold values from 0 to 127, as said below
- counts: int32 [32], P(('groups', 'row')), parts along dimension 0, may hold values from 4 to 48, as said below
- positions: float32 [65536, 128], P(('groups', 'row')), parts along dimension 0, may hold values from -1 to 1
- momenta: float32 [65536, 128], P(('groups', 'row')), parts along dimension 0, may hold values from -0.5 to 0.5
Outputs:
- final_positions: float32 [65536, 128], P(('groups', 'row')), parts along dimension 0
- final_momenta: float32 [65536, 128], P(('groups', 'row')), parts along dimension 0
- energy: float32 [256], P('groups'), parts along dimension 0
There are 2 independent parts, one for each index of `groups`. A program takes and returns all parts, laid end to end along the dimension named above; each array names one. Nothing has to cross between parts.
Inputs may be any that keep to these rules, and one draw needn't show every extreme that they name: `tile_cols`: among the first counts[d] slots of device d, at most 3 have column blocks held by one device (column block // 8); some device reaches 3. `counts`: some device has all 48 slots used.
All inputs are finite; a program needn't handle non-finite values.
Results may differ from a plain program's by a relative error of at most 0.0018.
Values may be sent and summed in bfloat16 or wider, within the bound.
No kernel may reach another device: no remote copies, remote signals or barrier semaphores. Data moves between devices by JAX's collectives and lax.ppermute only.
A program may use at most 64 MiB of HBM per device.

v0:
```python
import jax
import jax.numpy as jnp
from jax import lax
from jax.sharding import PartitionSpec as P

STEPS = 4


def body(tiles, tile_rows, tile_cols, counts, positions, momenta):
    slots = tiles.shape[0]
    tile = tiles.shape[1]
    repl = positions.shape[1]
    blocks = positions.shape[0] // tile
    devices = lax.axis_size("row")
    cap = (slots + devices - 1) // devices
    order = blocks * tile * devices
    slot_ids = jnp.arange(slots)
    used = slot_ids < counts[0]
    source = tile_cols // blocks
    local_col = tile_cols % blocks
    earlier = (
        (source[:, None] == source[None, :])
        & used[None, :]
        & (slot_ids[None, :] < slot_ids[:, None])
    )
    rank = jnp.sum(earlier.astype(jnp.int32), axis=1)
    key_slot = jnp.minimum(source * cap + rank, devices * cap - 1)
    matches = (key_slot[None, :] == jnp.arange(devices * cap)[:, None]) & used[None, :]
    wanted = jnp.sum(jnp.where(matches, local_col[None, :], 0), axis=1)
    asked = lax.all_to_all(
        wanted.reshape(devices, cap), "row", split_axis=0, concat_axis=0, tiled=True
    ).reshape(-1)
    onehot = ((tile_rows[None, :] == jnp.arange(blocks)[:, None]) & used[None, :]).astype(
        jnp.float32
    )
    squares = jnp.sum(jnp.square(tiles.astype(jnp.float32)), axis=(1, 2))
    local_sum = jnp.sum(jnp.where(used, squares, jnp.float32(0.0)))
    total = lax.psum(local_sum, "row")
    coeff = 0.7 * jnp.sqrt((order - 1) / total)
    xpos = positions
    ymom = momenta
    energy_part = jnp.zeros((repl,), jnp.float32)
    for step in range(STEPS):
        xb = xpos.astype(jnp.bfloat16).reshape(blocks, tile, repl)
        outgoing = xb[asked]
        received = lax.all_to_all(outgoing, "row", split_axis=0, concat_axis=0, tiled=True)
        chosen = received[key_slot]
        prods = jnp.einsum("sij,sjr->sir", tiles, chosen, preferred_element_type=jnp.float32)
        field = jnp.einsum("bs,sir->bir", onehot, prods, precision=lax.Precision.HIGHEST)
        field = field.reshape(-1, repl)
        if step == STEPS - 1:
            energy_part = -0.5 * jnp.sum(xpos * field, axis=0)
        pump = 0.4 - 0.1 * step
        ymom = ymom + 0.5 * (-(xpos * xpos + pump) * xpos + coeff * field)
        xpos = xpos + 0.5 * ymom
    energy = lax.psum(energy_part, "row")
    return (xpos, ymom, energy)


def solution(mesh):
    in_specs = (
        P(("groups", "row"), None, None),
        P(("groups", "row")),
        P(("groups", "row")),
        P(("groups", "row")),
        P(("groups", "row"), None),
        P(("groups", "row"), None),
    )
    out_specs = (P(("groups", "row"), None), P(("groups", "row"), None), P("groups"))
    return jax.shard_map(body, mesh=mesh, in_specs=in_specs, out_specs=out_specs, check_vma=False)
```

profile of v0, /device:TPU:0, one launch (start us, length us, event | category | flops | bytes accessed | tf_op | source)
XLA Modules:
  0.0 479.4 jit_solution(13191995228397818499)
XLA Ops:
  3.0 7.4 %all-to-all-start = ((s32[16,1,3]{2,1,0:T(1,128)}), s32[16,1,3]{2,1,0:T(1,128)S(1)}, u32[]{:S(2)}, u32[]{:S(2)}) async-start(s32[16,1,3]{2,1,0:T(1,128)} %bitcast.3), calls=%async_computation | async-start | bytes 16384 | tf_op jit(solution)/shard_map/all_to_all | solution.py:30
  11.6 5.0 %all-to-all-done = s32[16,1,3]{2,1,0:T(1,128)S(1)} async-done(((s32[16,1,3]{2,1,0:T(1,128)}), s32[16,1,3]{2,1,0:T(1,128)S(1)}, u32[]{:S(2)}, u32[]{:S(2)}) %all-to-all-start) | async-done | bytes 224 | tf_op jit(solution)/shard_map/all_to_all | solution.py:30
  18.0 2.7 gather_fusion
  20.7 3.7 all-to-all-start.1
  24.5 4.4 multiply_reduce_fusion
  29.4 74.8 %psum.14 = f32[]{:T(128)} all-reduce(f32[]{:T(128)} %select_reduce_fusion.1), channel_id=1, replica_groups=mesh['groups'=2,'row'=16] {'row'}, use_global_device_ids=true, to_apply=%region_2.3 | all-reduce | flops 1 | bytes 8 | tf_op jit(solution)/shard_map/psum | solution.py:38
  105.0 2.8 gather_fusion.1
  107.8 8.6 %convolution_bitcast_fusion.3 = f32[48,256,128]{1,2,0:T(8,128)} fusion(bf16[48,256,128]{2,1,0:T(8,128)(2,1)} %gather_fusion.1, bf16[48,256,256]{2,1,0:T(8,128)(2,1)} %param.6), kind=kOutput, calls=%fused_computation.12 | convolution fusion | flops 805306368 | bytes 15728640 | tf_op jit(solution)/shard_map/sij,sjr->sir/dot_general | solution.py:48
  116.4 6.6 %copy.37 = f32[48,256,128]{2,0,1:T(8,128)} copy(f32[48,256,128]{1,2,0:T(8,128)} %convolution_bitcast_fusion.3) | data formatting | bytes 12582912 | tf_op jit(solution)/shard_map/sij,sjr->sir/dot_general | solution.py:48
  123.0 4.3 convolution_multiply_fusion.2
  127.9 2.8 gather_fusion.2
  130.7 83.0 %all_to_all.29 = bf16[48,256,128]{2,1,0:T(8,128)(2,1)} all-to-all(bf16[48,256,128]{2,1,0:T(8,128)(2,1)} %gather_fusion.2), channel_id=1, replica_groups=mesh['groups'=2,'row'=16] {'row'}, dimensions={0} | all-to-all | bytes 6291456 | tf_op jit(solution)/shard_map/all_to_all | solution.py:46
  213.6 4.6 gather_fusion.3
  218.3 8.6 %convolution_bitcast_fusion.2 = f32[48,256,128]{1,2,0:T(8,128)} fusion(bf16[48,256,128]{2,1,0:T(8,128)(2,1)} %gather_fusion.3, bf16[48,256,256]{2,1,0:T(8,128)(2,1)} %param.6), kind=kOutput, calls=%fused_computation.11 | convolution fusion | flops 805306368 | bytes 15728640 | tf_op jit(solution)/shard_map/sij,sjr->sir/dot_general | solution.py:48
  226.9 6.6 %copy.40 = f32[48,256,128]{2,0,1:T(8,128)} copy(f32[48,256,128]{1,2,0:T(8,128)} %convolution_bitcast_fusion.2) | data formatting | bytes 12582912 | tf_op jit(solution)/shard_map/sij,sjr->sir/dot_general | solution.py:48
  233.5 4.3 convolution_multiply_fusion.1
  238.0 1.6 fusion.24
  239.6 2.8 gather_fusion.4
  242.4 75.1 %all_to_all.30 = bf16[48,256,128]{2,1,0:T(8,128)(2,1)} all-to-all(bf16[48,256,128]{2,1,0:T(8,128)(2,1)} %gather_fusion.4), channel_id=1, replica_groups=mesh['groups'=2,'row'=16] {'row'}, dimensions={0} | all-to-all | bytes 6291456 | tf_op jit(solution)/shard_map/all_to_all | solution.py:46
  317.4 4.6 gather_fusion.5
  322.1 8.6 %convolution_bitcast_fusion.1 = f32[48,256,128]{1,2,0:T(8,128)} fusion(bf16[48,256,128]{2,1,0:T(8,128)(2,1)} %gather_fusion.5, bf16[48,256,256]{2,1,0:T(8,128)(2,1)} %param.6), kind=kOutput, calls=%fused_computation.10 | convolution fusion | flops 805306368 | bytes 15728640 | tf_op jit(solution)/shard_map/sij,sjr->sir/dot_general | solution.py:48
  330.7 6.6 %copy.43 = f32[48,256,128]{2,0,1:T(8,128)} copy(f32[48,256,128]{1,2,0:T(8,128)} %convolution_bitcast_fusion.1) | data formatting | bytes 12582912 | tf_op jit(solution)/shard_map/sij,sjr->sir/dot_general | solution.py:48
  337.3 4.3 convolution_multiply_fusion
  341.9 1.9 fusion.21
  343.7 2.7 gather_fusion.6
  346.5 75.0 %all_to_all.31 = bf16[48,256,128]{2,1,0:T(8,128)(2,1)S(1)} all-to-all(bf16[48,256,128]{2,1,0:T(8,128)(2,1)} %gather_fusion.6), channel_id=1, replica_groups=mesh['groups'=2,'row'=16] {'row'}, dimensions={0} | all-to-all | bytes 6291456 | tf_op jit(solution)/shard_map/all_to_all | solution.py:46
  421.4 2.8 gather_fusion.7
  424.2 8.6 %convolution_bitcast_fusion = f32[48,256,128]{1,2,0:T(8,128)} fusion(bf16[48,256,128]{2,1,0:T(8,128)(2,1)} %gather_fusion.7, bf16[48,256,256]{2,1,0:T(8,128)(2,1)} %param.6), kind=kOutput, calls=%fused_computation.9 | convolution fusion | flops 805306368 | bytes 15728640 | tf_op jit(solution)/shard_map/sij,sjr->sir/dot_general | solution.py:48
  432.8 6.6 %copy.46 = f32[48,256,128]{2,0,1:T(8,128)} copy(f32[48,256,128]{1,2,0:T(8,128)} %convolution_bitcast_fusion) | data formatting | bytes 12582912 | tf_op jit(solution)/shard_map/sij,sjr->sir/dot_general | solution.py:48
  439.4 4.3 fusion.16
  443.9 1.8 multiply_add_fusion
  445.8 33.7 %psum.15 = f32[128]{0:T(128)} all-reduce(f32[128]{0:T(128)S(1)} %broadcast_multiply_fusion), channel_id=1, replica_groups=mesh['groups'=2,'row'=16] {'row'}, use_global_device_ids=true, to_apply=%region_6.7 | all-reduce | flops 128 | bytes 1024 | tf_op jit(solution)/shard_map/psum | solution.py:56
  (41 shorter events, 6.1 us)
Async XLA Ops:
  3.0 13.7 %all-to-all-start = ((s32[16,1,3]{2,1,0:T(1,128)}), s32[16,1,3]{2,1,0:T(1,128)S(1)}, u32[]{:S(2)}, u32[]{:S(2)}) async-start(s32[16,1,3]{2,1,0:T(1,128)} %bitcast.3), calls=%async_computation | async-start | bytes 16384 | tf_op jit(solution)/shard_map/all_to_all | solution.py:30
  20.7 84.3 %all-to-all-start.1 = ((bf16[48,256,128]{2,1,0:T(8,128)(2,1)}), bf16[48,256,128]{2,1,0:T(8,128)(2,1)S(1)}, u32[]{:S(2)}, u32[]{:S(2)}) async-start(bf16[48,256,128]{2,1,0:T(8,128)(2,1)} %gather_fusion), calls=%async_computation.1 | async-start | bytes 6291456 | tf_op jit(solution)/shard_map/all_to_all | solution.py:46
  116.4 6.6 %copy-start.9 = (s32[48]{0:T(128)S(1)}, s32[48]{0:T(128)}, u32[]{:S(2)}) copy-start(s32[48]{0:T(128)} %param.7) | copy-start | bytes 580
  123.0 4.6 copy-start
  123.0 4.6 copy-start.1
  233.5 4.5 copy-start.2
  238.0 1.6 copy-start.4
  337.3 4.6 copy-start.3
  337.3 4.6 copy-start.5
  337.3 4.6 copy-start.6
  439.4 4.5 copy-start.7
  439.4 4.5 copy-start.8
where the time goes:
time: 480 us; the launch traced here: 479 us
  blocking collectives  341 us (71%)
  local copies, waits for them, and re-layouts  54.3 us (11%)
  matrix products  51.6 us (11%)
  other arithmetic  13.6 us (3%)
  starting transfers between devices  11.1 us (2%)
  waiting for transfers between devices  5.05 us (1%)
    all_to_all x3, blocking collectives, body(): lax.all_to_all(outgoing, 'row', split_axis=0, concat_axis=0, tiled=True)  233 us
    psum x1, blocking collectives, body(): total = lax.psum(local_sum, 'row')  74.8 us
    dot_general x4, matrix products, body(): jnp.einsum('sij,sjr->sir', tiles, chosen, preferred_element_type=jnp.floa...  34.4 us
    psum x1, blocking collectives, body(): energy = lax.psum(energy_part, 'row')  33.7 us
    dot_general x4, local copies, waits for them, and re-layouts, body(): jnp.einsum('sij,sjr->sir', tiles, chosen, preferred_element_type=jnp.floa...  26.4 us
    dot_general x4, matrix products, body(): jnp.einsum('bs,sir->bir', onehot, prods, precision=lax.Precision.HIGHEST)  17.2 us
    gather x4, local copies, waits for them, and re-layouts, body(): chosen = received[key_slot]  14.8 us
    gather x4, local copies, waits for them, and re-layouts, body(): outgoing = xb[asked]  10.9 us
  transfers between devices with their start and end apart: 2, of which 1 were waited for; matrix products, arithmetic and copies ran while one was open for 1% of the time, Pallas kernels for 0%

commit v1 on v0

v1 whole, which is shorter than its diff:
```python
import functools

import jax
import jax.numpy as jnp
from jax import lax
from jax.experimental import pallas as pl
from jax.experimental.pallas import tpu as pltpu
from jax.sharding import PartitionSpec as P

STEPS = 4


def step_kernel(last, rows, cols, count, coeff, pump, tiles, gathered, xpos, ymom, xout, yout, extra, tbuf, xbuf, field, tsem, xsem):
    tile = tbuf.shape[1]
    used = count[0]

    def tile_copy(s):
        return pltpu.make_async_copy(tiles.at[s], tbuf.at[s], tsem.at[s])

    def block_copy(s):
        return pltpu.make_async_copy(gathered.at[cols[s]], xbuf.at[s], xsem.at[s])

    @pl.loop(0, used)
    def _(s):
        tile_copy(s).start()
        block_copy(s).start()

    field[...] = jnp.zeros_like(field)

    @pl.loop(0, used)
    def _(s):
        tile_copy(s).wait()
        block_copy(s).wait()
        here = pl.ds(pl.multiple_of(rows[s] * tile, tile), tile)
        field[here, :] += jnp.dot(tbuf[s], xbuf[s], preferred_element_type=jnp.float32)

    x = xpos[...]
    h = field[...]
    if last:
        extra[...] = -0.5 * jnp.sum(x * h, axis=0, keepdims=True)
    y = ymom[...] + 0.5 * (-(x * x + pump[0]) * x + coeff[0] * h)
    x = x + 0.5 * y
    yout[...] = y
    xout[...] = x
    if not last:
        extra[...] = x.astype(jnp.bfloat16)


def run_step(last, rows, cols, count, coeff, pump, tiles, gathered, xpos, ymom):
    slots, tile, _ = tiles.shape
    order, repl = xpos.shape
    smem = pl.BlockSpec(memory_space=pltpu.SMEM)
    vmem = pl.BlockSpec(memory_space=pltpu.VMEM)
    hbm = pl.BlockSpec(memory_space=pl.ANY)
    if last:
        extra = jax.ShapeDtypeStruct((1, repl), jnp.float32)
    else:
        extra = jax.ShapeDtypeStruct((order, repl), jnp.bfloat16)
    return pl.pallas_call(
        functools.partial(step_kernel, last),
        out_shape=(
            jax.ShapeDtypeStruct(xpos.shape, jnp.float32),
            jax.ShapeDtypeStruct(ymom.shape, jnp.float32),
            extra,
        ),
        in_specs=[smem] * 5 + [hbm, hbm, vmem, vmem],
        out_specs=(vmem, vmem, vmem),
        scratch_shapes=[
            pltpu.VMEM((slots, tile, tile), jnp.bfloat16),
            pltpu.VMEM((slots, tile, repl), jnp.bfloat16),
            pltpu.VMEM((order, repl), jnp.float32),
            pltpu.SemaphoreType.DMA((slots,)),
            pltpu.SemaphoreType.DMA((slots,)),
        ],
        compiler_params=pltpu.CompilerParams(vmem_limit_bytes=40 * 2**20),
        cost_estimate=pl.CostEstimate(
            flops=2 * slots * tile * tile * repl, bytes_accessed=slots * tile * (tile + repl) * 2, transcendentals=0
        ),
    )(rows, cols, count, coeff, pump, tiles, gathered, xpos, ymom)


def row_sum(part):
    devices = lax.axis_size("row")
    spread = jnp.broadcast_to(part, (devices,) + part.shape[1:])
    return jnp.sum(lax.all_to_all(spread, "row", split_axis=0, concat_axis=0, tiled=True), axis=0)


def body(tiles, tile_rows, tile_cols, counts, positions, momenta):
    slots = tiles.shape[0]
    tile = tiles.shape[1]
    repl = positions.shape[1]
    blocks = positions.shape[0] // tile
    devices = lax.axis_size("row")
    order = blocks * tile * devices
    xpos = positions
    ymom = momenta
    extra = xpos.astype(jnp.bfloat16)
    coeff = None
    for step in range(STEPS):
        gathered = lax.all_gather(extra, "row", tiled=True).reshape(devices * blocks, tile, repl)
        if step == 0:
            squares = jnp.sum(jnp.square(tiles.astype(jnp.float32)), axis=(1, 2))
            local_sum = jnp.sum(jnp.where(jnp.arange(slots) < counts[0], squares, jnp.float32(0.0)))
            total = row_sum(jnp.broadcast_to(local_sum, (1, repl)))[:1]
            coeff = 0.7 * jnp.sqrt((order - 1) / total)
        pump = jnp.full((1,), 0.4 - 0.1 * step, jnp.float32)
        xpos, ymom, extra = run_step(
            step == STEPS - 1, tile_rows, tile_cols, counts, coeff, pump, tiles, gathered, xpos, ymom
        )
    energy = row_sum(extra)
    return (xpos, ymom, energy)


def solution(mesh):
    in_specs = (
        P(("groups", "row"), None, None),
        P(("groups", "row")),
        P(("groups", "row")),
        P(("groups", "row")),
        P(("groups", "row"), None),
        P(("groups", "row"), None),
    )
    out_specs = (P(("groups", "row"), None), P(("groups", "row"), None), P("groups"))
    return jax.shard_map(body, mesh=mesh, in_specs=in_specs, out_specs=out_specs, check_vma=False)
```

time: 480 us -> 418 us (0.87)
  waiting for transfers between devices: 5.05 us -> 320 us
  blocking collectives: 341 us -> 37.3 us
  matrix products: 51.6 us -> 0 us
  local copies, waits for them, and re-layouts: 54.3 us -> 18.6 us
  Pallas kernels: 0 us -> 18.7 us
  between operations: 2.24 us -> 14.7 us
  starting transfers between devices: 11.1 us -> 0.16 us
  other arithmetic: 13.6 us -> 7.72 us
    all_gather x0 -> x4, waiting for transfers between devices: none -> 320 us  [body(): lax.all_gather(extra, 'row', tiled=True)]
    all_to_all x3 -> x2, blocking collectives: 233 us -> 37.3 us  [row_sum(): lax.all_to_all(spread, 'row', split_axis=0, concat_axis=0, tiled=True)]
    psum x2 -> x0, blocking collectives: 108 us -> none  [the longest x1 74.8 us: body(): total = lax.psum(local_sum, 'row')]
    dot_general x8 -> x0, matrix products: 51.6 us -> none  [the longest x4 34.4 us: body(): jnp.einsum('sij,sjr->sir', tiles, chosen, preferred_element_type=jnp.floa...]
    dot_general x5 -> x0, local copies, waits for them, and re-layouts: 26.6 us -> none  [the longest x4 26.4 us: body(): jnp.einsum('sij,sjr->sir', tiles, chosen, preferred_element_type=jnp.floa...]
    gather x8 -> x0, local copies, waits for them, and re-layouts: 25.7 us -> none  [the longest x4 14.8 us: body(): chosen = received[key_slot]]
    pallas_call x0 -> x4, Pallas kernels: none -> 18.7 us  [run_step(): pl.pallas_call(functools.partial(step_kernel, last), out_shape=(jax.Shape...]
    unnamed x20 -> x30, local copies, waits for them, and re-layouts: 0.04 us -> 17.9 us
  transfers between devices with their start and end apart: 2 -> 4, of which waited for: 1 -> 4; matrix products, arithmetic and copies ran while one was open for 1% -> 1% of each run, Pallas kernels for 0% -> 0%
where the time goes in v1:
time: 418 us; the launch traced here: 417 us
  waiting for transfers between devices  320 us (77%)
  blocking collectives  37.3 us (9%)
  Pallas kernels  18.7 us (4%)
  local copies, waits for them, and re-layouts  18.6 us (4%)
  between operations  14.7 us (4%)
  other arithmetic  7.72 us (2%)
    all_gather x4, waiting for transfers between devices, body(): lax.all_gather(extra, 'row', tiled=True)  320 us
    all_to_all x2, blocking collectives, row_sum(): lax.all_to_all(spread, 'row', split_axis=0, concat_axis=0, tiled=True)  37.3 us
    pallas_call x4, Pallas kernels, run_step(): pl.pallas_call(functools.partial(step_kernel, last), out_shape=(jax.Shape...  18.7 us
    unnamed x30, local copies, waits for them, and re-layouts  17.9 us
  transfers between devices with their start and end apart: 4, of which 4 were waited for; matrix products, arithmetic and copies ran while one was open for 1% of the time, Pallas kernels for 0%

profile of v1, /device:TPU:0, one launch (start us, length us, event | category | flops | bytes accessed | tf_op | source)
XLA Modules:
  0.0 416.8 jit_solution(1623542308150025106)
XLA Ops:
  7.2 0.0 all-gather.5.cloned.1.call-start
  7.3 2.2 convert_element_type.7
  9.5 0.0 all-gather.7.cloned.1.call-start
  10.2 4.4 %multiply_reduce_fusion = f32[48]{0:T(128)S(1)} fusion(bf16[48,256,256]{2,1,0:T(8,128)(2,1)} %tiles.7), kind=kLoop, calls=%fused_computation | loop fusion | flops 9437136 | bytes 6291648 | tf_op jit(solution)/shard_map/reduce_sum | solution.py:102
  14.6 0.6 fusion
  15.2 0.6 broadcast_in_dim_broadcast_in_dim.3
  15.8 13.7 %all_to_all.12 = f32[16,1,128]{2,1,0:T(1,128)S(1)} all-to-all(f32[16,1,128]{2,1,0:T(1,128)S(1)} %broadcast_in_dim_broadcast_in_dim.3), channel_id=1, replica_groups=mesh['groups'=2,'row'=16] {'row'}, dimensions={0} | all-to-all | bytes 16384 | tf_op jit(solution)/shard_map/all_to_all | solution.py:85
  29.7 58.9 %all-gather.5.cloned.1.call-done = bf16[32768,128]{1,0:T(8,128)(2,1)} async-done(((bf16[2048,128]{1,0:T(8,128)(2,1)}), bf16[32768,128]{1,0:T(8,128)(2,1)}) %all-gather.5.cloned.1.call-update) | async-done | bytes 8388624 | tf_op jit(solution)/shard_map/all_gather | solution.py:100
  88.6 2.8 copy-done
  91.3 4.4 %shard_map.85 = (f32[2048,128]{1,0:T(8,128)S(1)}, f32[2048,128]{1,0:T(8,128)S(1)}, bf16[2048,128]{1,0:T(8,128)(2,1)S(1)}) custom-call(s32[48]{0:T(128)S(1)} %copy-done.13, s32[48]{0:T(128)S(1)} %copy-done.14, s32[1]{0:T(128)} %copy.11.count, f32[1]{0:T(128)S(6)} %mul.3.coeff, f32[1]{0:T(128)} %constant.6.clone.1.pump, bf16[48,256,256]{2,1,0:T(8,128)(2,1)S(1)} %copy-done, ...), custom_call_target="tpu_custom_call" | custom-call | flops 805306368 | bytes 9437184 | tf_op jit(solution)/shard_map/pallas_call | solution.py:59
  95.7 1.0 copy-done.8
  96.7 0.8 copy-done.11
  97.5 0.0 all-gather.7.cloned.1.call-update
  97.5 0.0 all-gather.9.cloned.1.call-start
  97.6 86.9 %all-gather.7.cloned.1.call-done = bf16[32768,128]{1,0:T(8,128)(2,1)} async-done(((bf16[2048,128]{1,0:T(8,128)(2,1)}), bf16[32768,128]{1,0:T(8,128)(2,1)}) %all-gather.7.cloned.1.call-update) | async-done | bytes 8388624 | tf_op jit(solution)/shard_map/all_gather | solution.py:100
  184.5 2.8 copy-done.1
  187.2 1.2 copy-done.9
  188.5 4.4 %shard_map.86 = (f32[2048,128]{1,0:T(8,128)S(1)}, f32[2048,128]{1,0:T(8,128)S(1)}, bf16[2048,128]{1,0:T(8,128)(2,1)S(1)}) custom-call(s32[48]{0:T(128)S(1)} %copy-done.13, s32[48]{0:T(128)S(1)} %copy-done.14, s32[1]{0:T(128)} %copy.11.count, f32[1]{0:T(128)S(6)} %mul.3.coeff, f32[1]{0:T(128)} %constant.5.clone.1.pump, bf16[48,256,256]{2,1,0:T(8,128)(2,1)S(1)} %copy-done.1, ...), custom_call_target="tpu_custom_call" | custom-call | flops 805306368 | bytes 9437184 | tf_op jit(solution)/shard_map/pallas_call | solution.py:59
  192.9 0.8 copy-done.10
  193.6 0.0 all-gather.9.cloned.1.call-update
  193.7 0.0 all-gather.11.cloned.1.call-start
  193.7 86.9 %all-gather.9.cloned.1.call-done = bf16[32768,128]{1,0:T(8,128)(2,1)} async-done(((bf16[2048,128]{1,0:T(8,128)(2,1)}), bf16[32768,128]{1,0:T(8,128)(2,1)}) %all-gather.9.cloned.1.call-update) | async-done | bytes 8388624 | tf_op jit(solution)/shard_map/all_gather | solution.py:100
  280.6 2.8 copy-done.2
  283.4 4.4 %shard_map.87 = (f32[2048,128]{1,0:T(8,128)S(1)}, f32[2048,128]{1,0:T(8,128)S(1)}, bf16[2048,128]{1,0:T(8,128)(2,1)S(1)}) custom-call(s32[48]{0:T(128)S(1)} %copy-done.13, s32[48]{0:T(128)S(1)} %copy-done.14, s32[1]{0:T(128)} %copy.11.count, f32[1]{0:T(128)S(6)} %mul.3.coeff, f32[1]{0:T(128)} %constant.4.clone.1.pump, bf16[48,256,256]{2,1,0:T(8,128)(2,1)S(1)} %copy-done.2, ...), custom_call_target="tpu_custom_call" | custom-call | flops 805306368 | bytes 9437184 | tf_op jit(solution)/shard_map/pallas_call | solution.py:59
  287.8 1.0 copy-done.6
  288.8 0.8 copy-done.12
  289.6 87.0 %all-gather.11.cloned.1.call-done = bf16[32768,128]{1,0:T(8,128)(2,1)} async-done(((bf16[2048,128]{1,0:T(8,128)(2,1)}), bf16[32768,128]{1,0:T(8,128)(2,1)}) %all-gather.11.cloned.1.call-update) | async-done | bytes 8388624 | tf_op jit(solution)/shard_map/all_gather | solution.py:100
  376.5 2.8 copy-done.3
  379.3 1.2 copy-done.7
  380.5 5.6 %shard_map.88 = (f32[2048,128]{1,0:T(8,128)}, f32[2048,128]{1,0:T(8,128)}, f32[1,128]{1,0:T(1,128)S(1)}) custom-call(s32[48]{0:T(128)S(1)} %copy-done.13, s32[48]{0:T(128)S(1)} %copy-done.14, s32[1]{0:T(128)} %copy.11.count, f32[1]{0:T(128)S(6)} %mul.3.coeff, f32[1]{0:T(128)} %constant.3.clone.1.pump, bf16[48,256,256]{2,1,0:T(8,128)(2,1)S(1)} %copy-done.3, ...), custom_call_target="tpu_custom_call" | custom-call | flops 805306368 | bytes 9437184 | tf_op jit(solution)/shard_map/pallas_call | solution.py:59
  386.1 23.6 %all_to_all.13 = f32[16,1,128]{2,1,0:T(1,128)S(1)} all-to-all(f32[16,1,128]{2,1,0:T(1,128)S(1)} %broadcast_in_dim.10), channel_id=1, replica_groups=mesh['groups'=2,'row'=16] {'row'}, dimensions={0} | all-to-all | bytes 16384 | tf_op jit(solution)/shard_map/all_to_all | solution.py:85
  409.7 0.5 reduce_sum.39
  (23 shorter events, 0.1 us)
Async XLA Ops:
  7.2 81.4 %copy-start.4 = (f32[2048,128]{1,0:T(8,128)S(1)}, f32[2048,128]{1,0:T(8,128)}, u32[]{:S(2)}) copy-start(f32[2048,128]{1,0:T(8,128)} %xpos.1) | copy-start | bytes 3145732
  7.2 81.4 %copy-start.14 = (s32[48]{0:T(128)S(1)}, s32[48]{0:T(128)}, u32[]{:S(2)}) copy-start(s32[48]{0:T(128)} %cols.7) | copy-start | bytes 580
  7.2 81.4 %copy-start.13 = (s32[48]{0:T(128)S(1)}, s32[48]{0:T(128)}, u32[]{:S(2)}) copy-start(s32[48]{0:T(128)} %rows.7) | copy-start | bytes 580
  7.2 81.4 %copy-start.5 = (f32[2048,128]{1,0:T(8,128)S(1)}, f32[2048,128]{1,0:T(8,128)}, u32[]{:S(2)}) copy-start(f32[2048,128]{1,0:T(8,128)} %ymom.1) | copy-start | bytes 3145732
  7.2 81.3 %all-gather.5.cloned.1.call-start = ((), (), s32[]{:S(2)}) async-start(), calls=%async_computation.2 | async-start | bytes 8912896 | tf_op jit(solution)/shard_map/all_gather | solution.py:100
  9.5 175.0 %all-gather.7.cloned.1.call-start = ((), (), s32[]{:S(2)}) async-start(), calls=%async_computation.3 | async-start | bytes 8912896 | tf_op jit(solution)/shard_map/all_gather | solution.py:100
  88.6 2.8 copy-start
  95.7 1.0 copy-start.8
  96.7 0.8 copy-start.11
  97.5 183.1 %all-gather.9.cloned.1.call-start = ((), (), s32[]{:S(2)}) async-start(), calls=%async_computation.4 | async-start | bytes 8912896 | tf_op jit(solution)/shard_map/all_gather | solution.py:100
  184.5 2.8 copy-start.1
  187.2 1.2 copy-start.9
  192.8 0.8 copy-start.10
  193.7 182.9 %all-gather.11.cloned.1.call-start = ((), (), s32[]{:S(2)}) async-start(), calls=%async_computation.5 | async-start | bytes 8912896 | tf_op jit(solution)/shard_map/all_gather | solution.py:100
  280.6 2.8 copy-start.2
  287.8 1.0 copy-start.6
  288.7 0.8 copy-start.12
  376.5 2.8 copy-start.3
  379.3 1.2 copy-start.7
Sparse Core Ops, SparseCore 0:
  10.8 77.7 all-gather.4
  97.6 86.7 all-gather.6
  193.8 86.7 all-gather.8
  289.7 86.7 all-gather.10

commit v2 on v1

--- a/solution.py
+++ b/solution.py
@@ -10,27 +10,41 @@
 STEPS = 4
 
 
-def step_kernel(last, rows, cols, count, coeff, pump, tiles, gathered, xpos, ymom, xout, yout, extra, tbuf, xbuf, field, tsem, xsem):
+def step_kernel(last, nsrc, cap, rows, cols, count, table, coeff, pump, tiles, *refs):
+    sources = refs[:nsrc]
+    xpos, ymom, xout, yout, extra, tbuf, xbuf, field, tsem, xsem = refs[nsrc:]
     tile = tbuf.shape[1]
     used = count[0]
 
     def tile_copy(s):
         return pltpu.make_async_copy(tiles.at[s], tbuf.at[s], tsem.at[s])
 
-    def block_copy(s):
-        return pltpu.make_async_copy(gathered.at[cols[s]], xbuf.at[s], xsem.at[s])
+    def block_copy(source, block, s):
+        return pltpu.make_async_copy(source.at[block], xbuf.at[s], xsem.at[s])
 
     @pl.loop(0, used)
     def _(s):
         tile_copy(s).start()
-        block_copy(s).start()
+
+    if nsrc == 1:
+        @pl.loop(0, used)
+        def _(s):
+            block_copy(sources[0], cols[s], s).start()
+    else:
+        for i, source in enumerate(sources):
+            for r in range(cap):
+                s = table[i * cap + r]
+
+                @pl.when(s >= 0)
+                def _():
+                    block_copy(source, lax.rem(cols[s], source.shape[0]), s).start()
 
     field[...] = jnp.zeros_like(field)
 
     @pl.loop(0, used)
     def _(s):
         tile_copy(s).wait()
-        block_copy(s).wait()
+        block_copy(sources[0], 0, s).wait()
         here = pl.ds(pl.multiple_of(rows[s] * tile, tile), tile)
         field[here, :] += jnp.dot(tbuf[s], xbuf[s], preferred_element_type=jnp.float32)
 
@@ -46,7 +60,7 @@
         extra[...] = x.astype(jnp.bfloat16)
 
 
-def run_step(last, rows, cols, count, coeff, pump, tiles, gathered, xpos, ymom):
+def run_step(last, cap, rows, cols, count, table, coeff, pump, tiles, sources, xpos, ymom):
     slots, tile, _ = tiles.shape
     order, repl = xpos.shape
     smem = pl.BlockSpec(memory_space=pltpu.SMEM)
@@ -57,13 +71,13 @@
     else:
         extra = jax.ShapeDtypeStruct((order, repl), jnp.bfloat16)
     return pl.pallas_call(
-        functools.partial(step_kernel, last),
+        functools.partial(step_kernel, last, len(sources), cap),
         out_shape=(
             jax.ShapeDtypeStruct(xpos.shape, jnp.float32),
             jax.ShapeDtypeStruct(ymom.shape, jnp.float32),
             extra,
         ),
-        in_specs=[smem] * 5 + [hbm, hbm, vmem, vmem],
+        in_specs=[smem] * 6 + [hbm] * (1 + len(sources)) + [vmem, vmem],
         out_specs=(vmem, vmem, vmem),
         scratch_shapes=[
             pltpu.VMEM((slots, tile, tile), jnp.bfloat16),
@@ -76,13 +90,46 @@
         cost_estimate=pl.CostEstimate(
             flops=2 * slots * tile * tile * repl, bytes_accessed=slots * tile * (tile + repl) * 2, transcendentals=0
         ),
-    )(rows, cols, count, coeff, pump, tiles, gathered, xpos, ymom)
+    )(rows, cols, count, table, coeff, pump, tiles, *sources, xpos, ymom)
 
 
 def row_sum(part):
     devices = lax.axis_size("row")
     spread = jnp.broadcast_to(part, (devices,) + part.shape[1:])
     return jnp.sum(lax.all_to_all(spread, "row", split_axis=0, concat_axis=0, tiled=True), axis=0)
+
+
+def spread_out(xb):
+    me = lax.axis_index("row")
+    z, yc = me // 4, me % 4
+
+    def along_z(pairs, value):
+        return lax.ppermute(value, "row", [(a * 4 + i, b * 4 + i) for a, b in pairs for i in range(4)])
+
+    def to(flip, zs, value):
+        return lax.ppermute(value, "row", [(a * 4 + i, a * 4 + (i ^ flip)) for a in zs for i in range(4)])
+
+    everyone, inner, outer = (0, 1, 2, 3), (1, 2), (0, 3)
+    is_inner = (z == 1) | (z == 2)
+    near = along_z([(0, 1), (1, 0), (2, 3), (3, 2)], xb)
+    skip = along_z([(0, 2), (2, 0), (1, 3), (3, 1)], xb)
+    mid = along_z([(1, 2), (2, 1)], xb)
+    far = along_z([(1, 0), (2, 3)], skip)
+    yes = z >= 0
+    column = [
+        (xb, z, yes, everyone),
+        (near, z ^ 1, yes, everyone),
+        (skip, z ^ 2, yes, everyone),
+        (mid, z ^ 3, is_inner, inner),
+        (far, z ^ 3, ~is_inner, outer),
+    ]
+    found = []
+    for value, zs, valid, who in column:
+        across = to(2, who, value)
+        for y, v in ((0, value), (2, across)):
+            found.append((v, zs * 4 + (yc ^ y), valid))
+            found.append((to(1, who, v), zs * 4 + (yc ^ y ^ 1), valid))
+    return found
 
 
 def body(tiles, tile_rows, tile_cols, counts, positions, momenta):
@@ -92,20 +139,40 @@
     blocks = positions.shape[0] // tile
     devices = lax.axis_size("row")
     order = blocks * tile * devices
+    cap = (slots + devices - 1) // devices
+    slot_ids = jnp.arange(slots)
+    used = slot_ids < counts[0]
+    by_hand = devices == 16
     xpos = positions
     ymom = momenta
     extra = xpos.astype(jnp.bfloat16)
     coeff = None
     for step in range(STEPS):
-        gathered = lax.all_gather(extra, "row", tiled=True).reshape(devices * blocks, tile, repl)
+        if by_hand:
+            found = spread_out(extra)
+            sources = [v.reshape(blocks, tile, repl) for v, _, _ in found]
+        else:
+            sources = [lax.all_gather(extra, "row", tiled=True).reshape(devices * blocks, tile, repl)]
         if step == 0:
+            table = jnp.zeros((1,), jnp.int32)
+            if by_hand:
+                source = tile_cols // blocks
+                same = (source[:, None] == source[None, :]) & used[None, :]
+                rank = jnp.sum((same & (slot_ids[None, :] < slot_ids[:, None])).astype(jnp.int32), axis=1)
+                owner = jnp.stack([jnp.where(valid, src, -1) for _, src, valid in found]).astype(jnp.int32)
+                want = (
+                    (source[None, None, :] == owner[:, None, None])
+                    & (rank[None, None, :] == jnp.arange(cap)[None, :, None])
+                    & used[None, None, :]
+                )
+                table = jnp.max(jnp.where(want, slot_ids[None, None, :], -1), axis=2).astype(jnp.int32).reshape(-1)
             squares = jnp.sum(jnp.square(tiles.astype(jnp.float32)), axis=(1, 2))
-            local_sum = jnp.sum(jnp.where(jnp.arange(slots) < counts[0], squares, jnp.float32(0.0)))
+            local_sum = jnp.sum(jnp.where(used, squares, jnp.float32(0.0)))
             total = row_sum(jnp.broadcast_to(local_sum, (1, repl)))[:1]
             coeff = 0.7 * jnp.sqrt((order - 1) / total)
         pump = jnp.full((1,), 0.4 - 0.1 * step, jnp.float32)
         xpos, ymom, extra = run_step(
-            step == STEPS - 1, tile_rows, tile_cols, counts, coeff, pump, tiles, gathered, xpos, ymom
+            step == STEPS - 1, cap, tile_rows, tile_cols, counts, table, coeff, pump, tiles, sources, xpos, ymom
         )
     energy = row_sum(extra)
     return (xpos, ymom, energy)

time: 418 us -> 361 us (0.86)
  waiting for transfers between devices: 320 us -> 195 us
  starting transfers between devices: 0.16 us -> 107 us
  blocking collectives: 37.3 us -> 20.5 us
  between operations: 14.7 us -> 2.23 us
  local copies, waits for them, and re-layouts: 18.6 us -> 9.27 us
    all_gather x4 -> x0, waiting for transfers between devices: 320 us -> none  [body(): lax.all_gather(extra, 'row', tiled=True)]
    ppermute x0 -> x76, waiting for transfers between devices: none -> 195 us  [the longest x16 132 us: along_z(): lax.ppermute(value, 'row', [(a * 4 + i, b * 4 + i) for a, b in pairs for...]
    ppermute x0 -> x76, starting transfers between devices: none -> 102 us  [the longest x60 70.5 us: to(): lax.ppermute(value, 'row', [(a * 4 + i, a * 4 + (i ^ flip)) for a in zs f...]
    all_to_all x2 -> x1, blocking collectives: 37.3 us -> 20.5 us  [row_sum(): lax.all_to_all(spread, 'row', split_axis=0, concat_axis=0, tiled=True)]
    unnamed x30 -> x26, local copies, waits for them, and re-layouts: 17.9 us -> 7.75 us
    all_to_all x0 -> x1, starting transfers between devices: none -> 4.73 us  [row_sum(): lax.all_to_all(spread, 'row', split_axis=0, concat_axis=0, tiled=True)]
  transfers between devices with their start and end apart: 4 -> 77, of which waited for: 4 -> 23; matrix products, arithmetic and copies ran while one was open for 1% -> 2% of each run, Pallas kernels for 0% -> 0%
where the time goes in v2:
time: 361 us; the launch traced here: 359 us
  waiting for transfers between devices  195 us (54%)
  starting transfers between devices  107 us (30%)
  blocking collectives  20.5 us (6%)
  Pallas kernels  17.5 us (5%)
  local copies, waits for them, and re-layouts  9.27 us (3%)
  other arithmetic  7.32 us (2%)
    ppermute x16, waiting for transfers between devices, along_z(): lax.ppermute(value, 'row', [(a * 4 + i, b * 4 + i) for a, b in pairs for...  132 us
    ppermute x60, starting transfers between devices, to(): lax.ppermute(value, 'row', [(a * 4 + i, a * 4 + (i ^ flip)) for a in zs f...  70.5 us
    ppermute x60, waiting for transfers between devices, to(): lax.ppermute(value, 'row', [(a * 4 + i, a * 4 + (i ^ flip)) for a in zs f...  63.3 us
    ppermute x16, starting transfers between devices, along_z(): lax.ppermute(value, 'row', [(a * 4 + i, b * 4 + i) for a, b in pairs for...  31.4 us
    all_to_all x1, blocking collectives, row_sum(): lax.all_to_all(spread, 'row', split_axis=0, concat_axis=0, tiled=True)  20.5 us
    pallas_call x4, Pallas kernels, run_step(): pl.pallas_call(functools.partial(step_kernel, last, len(sources), cap), o...  17.5 us
    unnamed x26, local copies, waits for them, and re-layouts  7.75 us
  transfers between devices with their start and end apart: 77, of which 23 were waited for; matrix products, arithmetic and copies ran while one was open for 2% of the time, Pallas kernels for 0%

profile of v2, /device:TPU:0, one launch (start us, length us, event | category | flops | bytes accessed | tf_op | source)
XLA Modules:
  0.0 359.0 jit_solution(7612633091615593767)
XLA Ops:
  2.7 5.8 %collective-permute-start.7 = (bf16[2048,128]{1,0:T(8,128)(2,1)S(1)}, bf16[2048,128]{1,0:T(8,128)(2,1)S(1)}, u32[]{:S(2)}, u32[]{:S(2)}) collective-permute-start(bf16[2048,128]{1,0:T(8,128)(2,1)S(1)} %convert_element_type.11), channel_id=1, source_target_pairs={{0,8},{1,9},{2,10},{3,11},{8,0},{9,1},{10,2},{11,3},{4,12},{5,13},... | collective-permute-start | bytes 1572872 | tf_op jit(solution)/shard_map/ppermute | solution.py:107
  10.9 31.6 %collective-permute-done.7 = bf16[2048,128]{1,0:T(8,128)(2,1)S(1)} collective-permute-done((bf16[2048,128]{1,0:T(8,128)(2,1)S(1)}, bf16[2048,128]{1,0:T(8,128)(2,1)S(1)}, u32[]{:S(2)}, u32[]{:S(2)}) %collective-permute-start.7) | collective-permute-done | bytes 524320 | tf_op jit(solution)/shard_map/ppermute | solution.py:107
  46.8 4.4 %multiply_reduce_fusion = f32[48]{0:T(128)S(1)} fusion(bf16[48,256,256]{2,1,0:T(8,128)(2,1)} %tiles.7), kind=kLoop, calls=%fused_computation | loop fusion | flops 9437136 | bytes 6291648 | tf_op jit(solution)/shard_map/reduce_sum | solution.py:169
  53.5 4.5 %collective-permute-done.15 = bf16[2048,128]{1,0:T(8,128)(2,1)} collective-permute-done((bf16[2048,128]{1,0:T(8,128)(2,1)S(1)}, bf16[2048,128]{1,0:T(8,128)(2,1)}, u32[]{:S(2)}, u32[]{:S(2)}) %collective-permute-start.15) | collective-permute-done | bytes 524320 | tf_op jit(solution)/shard_map/ppermute | solution.py:107
  59.5 3.4 collective-permute-start.17
  64.7 4.7 %all-to-all-start = ((f32[16,1,128]{2,1,0:T(1,128)}), f32[16,1,128]{2,1,0:T(1,128)S(1)}, u32[]{:S(2)}, u32[]{:S(2)}) async-start(f32[16,1,128]{2,1,0:T(1,128)} %broadcast_in_dim_broadcast_in_dim.3), calls=%async_computation | async-start | bytes 16384 | tf_op jit(solution)/shard_map/all_to_all | solution.py:99
  74.1 5.9 %collective-permute-done.17 = bf16[2048,128]{1,0:T(8,128)(2,1)} collective-permute-done((bf16[2048,128]{1,0:T(8,128)(2,1)}, bf16[2048,128]{1,0:T(8,128)(2,1)}, u32[]{:S(2)}, u32[]{:S(2)}) %collective-permute-start.17) | collective-permute-done | bytes 524320 | tf_op jit(solution)/shard_map/ppermute | solution.py:110
  88.3 4.3 %shard_map.85 = (f32[2048,128]{1,0:T(8,128)S(1)}, f32[2048,128]{1,0:T(8,128)S(1)}, bf16[2048,128]{1,0:T(8,128)(2,1)S(1)}) custom-call(s32[48]{0:T(128)S(1)} %copy-done.11, s32[48]{0:T(128)S(1)} %copy-done.12, s32[1]{0:T(128)} %copy.13.count, s32[60]{0:T(128)S(1)} %reshape.320.table, f32[1]{0:T(128)S(6)} %mul.14.coeff, f32[1]{0:T(128)} %constant.62.clone.1.pump, ...), custom_call_target="tpu_custom_call" | custom-call | flops 805306368 | bytes 9437184 | tf_op jit(solution)/shard_map/pallas_call | solution.py:73
  94.3 6.1 %collective-permute-start.26 = (bf16[2048,128]{1,0:T(8,128)(2,1)S(1)}, bf16[2048,128]{1,0:T(8,128)(2,1)S(1)}, u32[]{:S(2)}, u32[]{:S(2)}) collective-permute-start(bf16[2048,128]{1,0:T(8,128)(2,1)S(1)} %get-tuple-element.15), channel_id=1, source_target_pairs={{0,8},{1,9},{2,10},{3,11},{8,0},{9,1},{10,2},{11,3},{4,12},{5,13},... | collective-permute-start | bytes 1572872 | tf_op jit(solution)/shard_map/ppermute | solution.py:107
  100.4 3.8 %collective-permute-start.20 = (bf16[2048,128]{1,0:T(8,128)(2,1)S(1)}, bf16[2048,128]{1,0:T(8,128)(2,1)S(1)}, u32[]{:S(2)}, u32[]{:S(2)}) collective-permute-start(bf16[2048,128]{1,0:T(8,128)(2,1)S(1)} %get-tuple-element.15), channel_id=1, source_target_pairs={{0,2},{1,3},{2,0},{3,1},{4,6},{5,7},{6,4},{7,5},{8,10},{9,11},{10,... | collective-permute-start | bytes 1572872 | tf_op jit(solution)/shard_map/ppermute | solution.py:110
  106.5 22.5 %collective-permute-done.26 = bf16[2048,128]{1,0:T(8,128)(2,1)S(1)} collective-permute-done((bf16[2048,128]{1,0:T(8,128)(2,1)S(1)}, bf16[2048,128]{1,0:T(8,128)(2,1)S(1)}, u32[]{:S(2)}, u32[]{:S(2)}) %collective-permute-start.26) | collective-permute-done | bytes 524320 | tf_op jit(solution)/shard_map/ppermute | solution.py:107
  133.3 11.3 %collective-permute-done.34 = bf16[2048,128]{1,0:T(8,128)(2,1)S(1)} collective-permute-done((bf16[2048,128]{1,0:T(8,128)(2,1)S(1)}, bf16[2048,128]{1,0:T(8,128)(2,1)S(1)}, u32[]{:S(2)}, u32[]{:S(2)}) %collective-permute-start.34) | collective-permute-done | bytes 524320 | tf_op jit(solution)/shard_map/ppermute | solution.py:107
  145.9 2.8 collective-permute-start.36
  150.8 6.3 %collective-permute-done.24 = bf16[2048,128]{1,0:T(8,128)(2,1)S(1)} collective-permute-done((bf16[2048,128]{1,0:T(8,128)(2,1)S(1)}, bf16[2048,128]{1,0:T(8,128)(2,1)S(1)}, u32[]{:S(2)}, u32[]{:S(2)}) %collective-permute-start.24) | collective-permute-done | bytes 524320 | tf_op jit(solution)/shard_map/ppermute | solution.py:110
  158.4 8.5 %collective-permute-done.36 = bf16[2048,128]{1,0:T(8,128)(2,1)S(1)} collective-permute-done((bf16[2048,128]{1,0:T(8,128)(2,1)S(1)}, bf16[2048,128]{1,0:T(8,128)(2,1)S(1)}, u32[]{:S(2)}, u32[]{:S(2)}) %collective-permute-start.36) | collective-permute-done | bytes 524320 | tf_op jit(solution)/shard_map/ppermute | solution.py:110
  170.7 4.2 %shard_map.86 = (f32[2048,128]{1,0:T(8,128)S(1)}, f32[2048,128]{1,0:T(8,128)S(1)}, bf16[2048,128]{1,0:T(8,128)(2,1)S(1)}) custom-call(s32[48]{0:T(128)S(1)} %copy-done.11, s32[48]{0:T(128)S(1)} %copy-done.12, s32[1]{0:T(128)} %copy.13.count, s32[60]{0:T(128)S(1)} %reshape.320.table, f32[1]{0:T(128)S(6)} %mul.14.coeff, f32[1]{0:T(128)} %constant.61.clone.1.pump, ...), custom_call_target="tpu_custom_call" | custom-call | flops 805306368 | bytes 9437184 | tf_op jit(solution)/shard_map/pallas_call | solution.py:73
  176.5 5.7 %collective-permute-start.45 = (bf16[2048,128]{1,0:T(8,128)(2,1)S(1)}, bf16[2048,128]{1,0:T(8,128)(2,1)S(1)}, u32[]{:S(2)}, u32[]{:S(2)}) collective-permute-start(bf16[2048,128]{1,0:T(8,128)(2,1)S(1)} %get-tuple-element.18), channel_id=1, source_target_pairs={{0,8},{1,9},{2,10},{3,11},{8,0},{9,1},{10,2},{11,3},{4,12},{5,13},... | collective-permute-start | bytes 1572872 | tf_op jit(solution)/shard_map/ppermute | solution.py:107
  182.2 5.8 %collective-permute-start.39 = (bf16[2048,128]{1,0:T(8,128)(2,1)S(1)}, bf16[2048,128]{1,0:T(8,128)(2,1)S(1)}, u32[]{:S(2)}, u32[]{:S(2)}) collective-permute-start(bf16[2048,128]{1,0:T(8,128)(2,1)S(1)} %get-tuple-element.18), channel_id=1, source_target_pairs={{0,2},{1,3},{2,0},{3,1},{4,6},{5,7},{6,4},{7,5},{8,10},{9,11},{10,... | collective-permute-start | bytes 1572872 | tf_op jit(solution)/shard_map/ppermute | solution.py:110
  191.0 19.6 %collective-permute-done.45 = bf16[2048,128]{1,0:T(8,128)(2,1)S(1)} collective-permute-done((bf16[2048,128]{1,0:T(8,128)(2,1)S(1)}, bf16[2048,128]{1,0:T(8,128)(2,1)S(1)}, u32[]{:S(2)}, u32[]{:S(2)}) %collective-permute-start.45) | collective-permute-done | bytes 524320 | tf_op jit(solution)/shard_map/ppermute | solution.py:107
  215.0 11.3 %collective-permute-done.53 = bf16[2048,128]{1,0:T(8,128)(2,1)S(1)} collective-permute-done((bf16[2048,128]{1,0:T(8,128)(2,1)S(1)}, bf16[2048,128]{1,0:T(8,128)(2,1)S(1)}, u32[]{:S(2)}, u32[]{:S(2)}) %collective-permute-start.53) | collective-permute-done | bytes 524320 | tf_op jit(solution)/shard_map/ppermute | solution.py:107
  227.5 2.7 collective-permute-start.55
  232.3 6.5 %collective-permute-done.43 = bf16[2048,128]{1,0:T(8,128)(2,1)S(1)} collective-permute-done((bf16[2048,128]{1,0:T(8,128)(2,1)S(1)}, bf16[2048,128]{1,0:T(8,128)(2,1)S(1)}, u32[]{:S(2)}, u32[]{:S(2)}) %collective-permute-start.43) | collective-permute-done | bytes 524320 | tf_op jit(solution)/shard_map/ppermute | solution.py:110
  240.1 8.5 %collective-permute-done.55 = bf16[2048,128]{1,0:T(8,128)(2,1)S(1)} collective-permute-done((bf16[2048,128]{1,0:T(8,128)(2,1)S(1)}, bf16[2048,128]{1,0:T(8,128)(2,1)S(1)}, u32[]{:S(2)}, u32[]{:S(2)}) %collective-permute-start.55) | collective-permute-done | bytes 524320 | tf_op jit(solution)/shard_map/ppermute | solution.py:110
  252.3 4.3 %shard_map.87 = (f32[2048,128]{1,0:T(8,128)S(1)}, f32[2048,128]{1,0:T(8,128)S(1)}, bf16[2048,128]{1,0:T(8,128)(2,1)S(1)}) custom-call(s32[48]{0:T(128)S(1)} %copy-done.11, s32[48]{0:T(128)S(1)} %copy-done.12, s32[1]{0:T(128)} %copy.13.count, s32[60]{0:T(128)S(1)} %reshape.320.table, f32[1]{0:T(128)S(6)} %mul.14.coeff, f32[1]{0:T(128)} %constant.60.clone.1.pump, ...), custom_call_target="tpu_custom_call" | custom-call | flops 805306368 | bytes 9437184 | tf_op jit(solution)/shard_map/pallas_call | solution.py:73
  257.4 5.7 %collective-permute-start.64 = (bf16[2048,128]{1,0:T(8,128)(2,1)S(1)}, bf16[2048,128]{1,0:T(8,128)(2,1)S(1)}, u32[]{:S(2)}, u32[]{:S(2)}) collective-permute-start(bf16[2048,128]{1,0:T(8,128)(2,1)S(1)} %get-tuple-element.21), channel_id=1, source_target_pairs={{0,8},{1,9},{2,10},{3,11},{8,0},{9,1},{10,2},{11,3},{4,12},{5,13},... | collective-permute-start | bytes 1572872 | tf_op jit(solution)/shard_map/ppermute | solution.py:107
  263.1 5.8 %collective-permute-start.58 = (bf16[2048,128]{1,0:T(8,128)(2,1)S(1)}, bf16[2048,128]{1,0:T(8,128)(2,1)S(1)}, u32[]{:S(2)}, u32[]{:S(2)}) collective-permute-start(bf16[2048,128]{1,0:T(8,128)(2,1)S(1)} %get-tuple-element.21), channel_id=1, source_target_pairs={{0,2},{1,3},{2,0},{3,1},{4,6},{5,7},{6,4},{7,5},{8,10},{9,11},{10,... | collective-permute-start | bytes 1572872 | tf_op jit(solution)/shard_map/ppermute | solution.py:110
  271.3 20.1 %collective-permute-done.64 = bf16[2048,128]{1,0:T(8,128)(2,1)S(1)} collective-permute-done((bf16[2048,128]{1,0:T(8,128)(2,1)S(1)}, bf16[2048,128]{1,0:T(8,128)(2,1)S(1)}, u32[]{:S(2)}, u32[]{:S(2)}) %collective-permute-start.64) | collective-permute-done | bytes 524320 | tf_op jit(solution)/shard_map/ppermute | solution.py:107
  295.8 11.3 %collective-permute-done.72 = bf16[2048,128]{1,0:T(8,128)(2,1)S(1)} collective-permute-done((bf16[2048,128]{1,0:T(8,128)(2,1)S(1)}, bf16[2048,128]{1,0:T(8,128)(2,1)S(1)}, u32[]{:S(2)}, u32[]{:S(2)}) %collective-permute-start.72) | collective-permute-done | bytes 524320 | tf_op jit(solution)/shard_map/ppermute | solution.py:107
  313.1 6.5 %collective-permute-done.62 = bf16[2048,128]{1,0:T(8,128)(2,1)S(1)} collective-permute-done((bf16[2048,128]{1,0:T(8,128)(2,1)S(1)}, bf16[2048,128]{1,0:T(8,128)(2,1)S(1)}, u32[]{:S(2)}, u32[]{:S(2)}) %collective-permute-start.62) | collective-permute-done | bytes 524320 | tf_op jit(solution)/shard_map/ppermute | solution.py:110
  320.9 8.5 %collective-permute-done.74 = bf16[2048,128]{1,0:T(8,128)(2,1)S(1)} collective-permute-done((bf16[2048,128]{1,0:T(8,128)(2,1)S(1)}, bf16[2048,128]{1,0:T(8,128)(2,1)S(1)}, u32[]{:S(2)}, u32[]{:S(2)}) %collective-permute-start.74) | collective-permute-done | bytes 524320 | tf_op jit(solution)/shard_map/ppermute | solution.py:110
  333.2 4.7 %shard_map.88 = (f32[2048,128]{1,0:T(8,128)}, f32[2048,128]{1,0:T(8,128)}, f32[1,128]{1,0:T(1,128)S(1)}) custom-call(s32[48]{0:T(128)S(1)} %copy-done.11, s32[48]{0:T(128)S(1)} %copy-done.12, s32[1]{0:T(128)} %copy.13.count, s32[60]{0:T(128)S(1)} %reshape.320.table, f32[1]{0:T(128)S(6)} %mul.14.coeff, f32[1]{0:T(128)} %constant.59.clone.1.pump, ...), custom_call_target="tpu_custom_call" | custom-call | flops 805306368 | bytes 9437184 | tf_op jit(solution)/shard_map/pallas_call | solution.py:73
  337.9 20.5 %all_to_all.12 = f32[16,1,128]{2,1,0:T(1,128)S(1)} all-to-all(f32[16,1,128]{2,1,0:T(1,128)S(1)} %broadcast_in_dim.21), channel_id=1, replica_groups=mesh['groups'=2,'row'=16] {'row'}, dimensions={0} | all-to-all | bytes 16384 | tf_op jit(solution)/shard_map/all_to_all | solution.py:99
  (169 shorter events, 79.0 us)
Async XLA Ops:
  2.7 39.8 %collective-permute-start.7 = (bf16[2048,128]{1,0:T(8,128)(2,1)S(1)}, bf16[2048,128]{1,0:T(8,128)(2,1)S(1)}, u32[]{:S(2)}, u32[]{:S(2)}) collective-permute-start(bf16[2048,128]{1,0:T(8,128)(2,1)S(1)} %convert_element_type.11), channel_id=1, source_target_pairs={{0,8},{1,9},{2,10},{3,11},{8,0},{9,1},{10,2},{11,3},{4,12},{5,13},... | collective-permute-start | bytes 1572872 | tf_op jit(solution)/shard_map/ppermute | solution.py:107
  8.5 34.7 %collective-permute-start.3 = (bf16[2048,128]{1,0:T(8,128)(2,1)S(1)}, bf16[2048,128]{1,0:T(8,128)(2,1)S(1)}, u32[]{:S(2)}, u32[]{:S(2)}) collective-permute-start(bf16[2048,128]{1,0:T(8,128)(2,1)S(1)} %convert_element_type.11), channel_id=1, source_target_pairs={{0,4},{1,5},{2,6},{3,7},{4,0},{5,1},{6,2},{7,3},{8,12},{9,13},{10,... | collective-permute-start | bytes 1572872 | tf_op jit(solution)/shard_map/ppermute | solution.py:107
  8.7 35.8 %collective-permute-start.1 = (bf16[2048,128]{1,0:T(8,128)(2,1)S(1)}, bf16[2048,128]{1,0:T(8,128)(2,1)}, u32[]{:S(2)}, u32[]{:S(2)}) collective-permute-start(bf16[2048,128]{1,0:T(8,128)(2,1)S(1)} %convert_element_type.11), channel_id=1, source_target_pairs={{0,2},{1,3},{2,0},{3,1},{4,6},{5,7},{6,4},{7,5},{8,10},{9,11},{10,... | collective-permute-start | bytes 1572872 | tf_op jit(solution)/shard_map/ppermute | solution.py:110
  10.2 40.9 %collective-permute-start = (bf16[2048,128]{1,0:T(8,128)(2,1)S(1)}, bf16[2048,128]{1,0:T(8,128)(2,1)S(1)}, u32[]{:S(2)}, u32[]{:S(2)}) collective-permute-start(bf16[2048,128]{1,0:T(8,128)(2,1)S(1)} %convert_element_type.11), channel_id=1, source_target_pairs={{0,1},{1,0},{2,3},{3,2},{4,5},{5,4},{6,7},{7,6},{8,9},{9,8},{10,11... | collective-permute-start | bytes 1572872 | tf_op jit(solution)/shard_map/ppermute | solution.py:110
  10.2 41.7 %collective-permute-start.13 = (bf16[2048,128]{1,0:T(8,128)(2,1)S(1)}, bf16[2048,128]{1,0:T(8,128)(2,1)S(1)}, u32[]{:S(2)}, u32[]{:S(2)}) collective-permute-start(bf16[2048,128]{1,0:T(8,128)(2,1)S(1)} %collective-permute-done.11), channel_id=1, source_target_pairs={{4,6},{5,7},{6,4},{7,5},{8,10},{9,11},{10,8},{11,9},{20,22},{21,23... | collective-permute-start | bytes 1572872 | tf_op jit(solution)/shard_map/ppermute | solution.py:110
  53.4 20.2 %collective-permute-start.4 = (bf16[2048,128]{1,0:T(8,128)(2,1)S(1)}, bf16[2048,128]{1,0:T(8,128)(2,1)}, u32[]{:S(2)}, u32[]{:S(2)}) collective-permute-start(bf16[2048,128]{1,0:T(8,128)(2,1)S(1)} %collective-permute-done.3), channel_id=1, source_target_pairs={{0,1},{1,0},{2,3},{3,2},{4,5},{5,4},{6,7},{7,6},{8,9},{9,8},{10,11... | collective-permute-start | bytes 1572872 | tf_op jit(solution)/shard_map/ppermute | solution.py:110
  59.5 20.6 %collective-permute-start.17 = (bf16[2048,128]{1,0:T(8,128)(2,1)}, bf16[2048,128]{1,0:T(8,128)(2,1)}, u32[]{:S(2)}, u32[]{:S(2)}) collective-permute-start(bf16[2048,128]{1,0:T(8,128)(2,1)} %collective-permute-done.15), channel_id=1, source_target_pairs={{0,2},{1,3},{2,0},{3,1},{12,14},{13,15},{14,12},{15,13},{16,18},{1... | collective-permute-start | bytes 1572872 | tf_op jit(solution)/shard_map/ppermute | solution.py:110
  94.3 34.7 %collective-permute-start.26 = (bf16[2048,128]{1,0:T(8,128)(2,1)S(1)}, bf16[2048,128]{1,0:T(8,128)(2,1)S(1)}, u32[]{:S(2)}, u32[]{:S(2)}) collective-permute-start(bf16[2048,128]{1,0:T(8,128)(2,1)S(1)} %get-tuple-element.15), channel_id=1, source_target_pairs={{0,8},{1,9},{2,10},{3,11},{8,0},{9,1},{10,2},{11,3},{4,12},{5,13},... | collective-permute-start | bytes 1572872 | tf_op jit(solution)/shard_map/ppermute | solution.py:107
  100.4 29.2 %collective-permute-start.22 = (bf16[2048,128]{1,0:T(8,128)(2,1)S(1)}, bf16[2048,128]{1,0:T(8,128)(2,1)S(1)}, u32[]{:S(2)}, u32[]{:S(2)}) collective-permute-start(bf16[2048,128]{1,0:T(8,128)(2,1)S(1)} %get-tuple-element.15), channel_id=1, source_target_pairs={{0,4},{1,5},{2,6},{3,7},{4,0},{5,1},{6,2},{7,3},{8,12},{9,13},{10,... | collective-permute-start | bytes 1572872 | tf_op jit(solution)/shard_map/ppermute | solution.py:107
  100.4 30.5 %collective-permute-start.20 = (bf16[2048,128]{1,0:T(8,128)(2,1)S(1)}, bf16[2048,128]{1,0:T(8,128)(2,1)S(1)}, u32[]{:S(2)}, u32[]{:S(2)}) collective-permute-start(bf16[2048,128]{1,0:T(8,128)(2,1)S(1)} %get-tuple-element.15), channel_id=1, source_target_pairs={{0,2},{1,3},{2,0},{3,1},{4,6},{5,7},{6,4},{7,5},{8,10},{9,11},{10,... | collective-permute-start | bytes 1572872 | tf_op jit(solution)/shard_map/ppermute | solution.py:110
  104.3 27.1 %collective-permute-start.19 = (bf16[2048,128]{1,0:T(8,128)(2,1)S(1)}, bf16[2048,128]{1,0:T(8,128)(2,1)S(1)}, u32[]{:S(2)}, u32[]{:S(2)}) collective-permute-start(bf16[2048,128]{1,0:T(8,128)(2,1)S(1)} %get-tuple-element.15), channel_id=1, source_target_pairs={{0,1},{1,0},{2,3},{3,2},{4,5},{5,4},{6,7},{7,6},{8,9},{9,8},{10,11... | collective-permute-start | bytes 1572872 | tf_op jit(solution)/shard_map/ppermute | solution.py:110
  105.8 26.3 %collective-permute-start.32 = (bf16[2048,128]{1,0:T(8,128)(2,1)S(1)}, bf16[2048,128]{1,0:T(8,128)(2,1)S(1)}, u32[]{:S(2)}, u32[]{:S(2)}) collective-permute-start(bf16[2048,128]{1,0:T(8,128)(2,1)S(1)} %collective-permute-done.30), channel_id=1, source_target_pairs={{4,6},{5,7},{6,4},{7,5},{8,10},{9,11},{10,8},{11,9},{20,22},{21,23... | collective-permute-start | bytes 1572872 | tf_op jit(solution)/shard_map/ppermute | solution.py:110
  132.1 25.0 %collective-permute-start.24 = (bf16[2048,128]{1,0:T(8,128)(2,1)S(1)}, bf16[2048,128]{1,0:T(8,128)(2,1)S(1)}, u32[]{:S(2)}, u32[]{:S(2)}) collective-permute-start(bf16[2048,128]{1,0:T(8,128)(2,1)S(1)} %collective-permute-done.22), channel_id=1, source_target_pairs={{0,2},{1,3},{2,0},{3,1},{4,6},{5,7},{6,4},{7,5},{8,10},{9,11},{10,... | collective-permute-start | bytes 1572872 | tf_op jit(solution)/shard_map/ppermute | solution.py:110
  133.1 24.7 %collective-permute-start.23 = (bf16[2048,128]{1,0:T(8,128)(2,1)S(1)}, bf16[2048,128]{1,0:T(8,128)(2,1)S(1)}, u32[]{:S(2)}, u32[]{:S(2)}) collective-permute-start(bf16[2048,128]{1,0:T(8,128)(2,1)S(1)} %collective-permute-done.22), channel_id=1, source_target_pairs={{0,1},{1,0},{2,3},{3,2},{4,5},{5,4},{6,7},{7,6},{8,9},{9,8},{10,11... | collective-permute-start | bytes 1572872 | tf_op jit(solution)/shard_map/ppermute | solution.py:110
  145.9 21.0 %collective-permute-start.36 = (bf16[2048,128]{1,0:T(8,128)(2,1)S(1)}, bf16[2048,128]{1,0:T(8,128)(2,1)S(1)}, u32[]{:S(2)}, u32[]{:S(2)}) collective-permute-start(bf16[2048,128]{1,0:T(8,128)(2,1)S(1)} %collective-permute-done.34), channel_id=1, source_target_pairs={{0,2},{1,3},{2,0},{3,1},{12,14},{13,15},{14,12},{15,13},{16,18},{1... | collective-permute-start | bytes 1572872 | tf_op jit(solution)/shard_map/ppermute | solution.py:110
  176.5 34.1 %collective-permute-start.45 = (bf16[2048,128]{1,0:T(8,128)(2,1)S(1)}, bf16[2048,128]{1,0:T(8,128)(2,1)S(1)}, u32[]{:S(2)}, u32[]{:S(2)}) collective-permute-start(bf16[2048,128]{1,0:T(8,128)(2,1)S(1)} %get-tuple-element.18), channel_id=1, source_target_pairs={{0,8},{1,9},{2,10},{3,11},{8,0},{9,1},{10,2},{11,3},{4,12},{5,13},... | collective-permute-start | bytes 1572872 | tf_op jit(solution)/shard_map/ppermute | solution.py:107
  182.2 29.1 %collective-permute-start.41 = (bf16[2048,128]{1,0:T(8,128)(2,1)S(1)}, bf16[2048,128]{1,0:T(8,128)(2,1)S(1)}, u32[]{:S(2)}, u32[]{:S(2)}) collective-permute-start(bf16[2048,128]{1,0:T(8,128)(2,1)S(1)} %get-tuple-element.18), channel_id=1, source_target_pairs={{0,4},{1,5},{2,6},{3,7},{4,0},{5,1},{6,2},{7,3},{8,12},{9,13},{10,... | collective-permute-start | bytes 1572872 | tf_op jit(solution)/shard_map/ppermute | solution.py:107
  182.2 30.4 %collective-permute-start.39 = (bf16[2048,128]{1,0:T(8,128)(2,1)S(1)}, bf16[2048,128]{1,0:T(8,128)(2,1)S(1)}, u32[]{:S(2)}, u32[]{:S(2)}) collective-permute-start(bf16[2048,128]{1,0:T(8,128)(2,1)S(1)} %get-tuple-element.18), channel_id=1, source_target_pairs={{0,2},{1,3},{2,0},{3,1},{4,6},{5,7},{6,4},{7,5},{8,10},{9,11},{10,... | collective-permute-start | bytes 1572872 | tf_op jit(solution)/shard_map/ppermute | solution.py:110
  188.1 24.7 %collective-permute-start.38 = (bf16[2048,128]{1,0:T(8,128)(2,1)S(1)}, bf16[2048,128]{1,0:T(8,128)(2,1)S(1)}, u32[]{:S(2)}, u32[]{:S(2)}) collective-permute-start(bf16[2048,128]{1,0:T(8,128)(2,1)S(1)} %get-tuple-element.18), channel_id=1, source_target_pairs={{0,1},{1,0},{2,3},{3,2},{4,5},{5,4},{6,7},{7,6},{8,9},{9,8},{10,11... | collective-permute-start | bytes 1572872 | tf_op jit(solution)/shard_map/ppermute | solution.py:110
  190.3 23.4 %collective-permute-start.51 = (bf16[2048,128]{1,0:T(8,128)(2,1)S(1)}, bf16[2048,128]{1,0:T(8,128)(2,1)S(1)}, u32[]{:S(2)}, u32[]{:S(2)}) collective-permute-start(bf16[2048,128]{1,0:T(8,128)(2,1)S(1)} %collective-permute-done.49), channel_id=1, source_target_pairs={{4,6},{5,7},{6,4},{7,5},{8,10},{9,11},{10,8},{11,9},{20,22},{21,23... | collective-permute-start | bytes 1572872 | tf_op jit(solution)/shard_map/ppermute | solution.py:110
  213.7 25.1 %collective-permute-start.43 = (bf16[2048,128]{1,0:T(8,128)(2,1)S(1)}, bf16[2048,128]{1,0:T(8,128)(2,1)S(1)}, u32[]{:S(2)}, u32[]{:S(2)}) collective-permute-start(bf16[2048,128]{1,0:T(8,128)(2,1)S(1)} %collective-permute-done.41), channel_id=1, source_target_pairs={{0,2},{1,3},{2,0},{3,1},{4,6},{5,7},{6,4},{7,5},{8,10},{9,11},{10,... | collective-permute-start | bytes 1572872 | tf_op jit(solution)/shard_map/ppermute | solution.py:110
  214.8 24.7 %collective-permute-start.42 = (bf16[2048,128]{1,0:T(8,128)(2,1)S(1)}, bf16[2048,128]{1,0:T(8,128)(2,1)S(1)}, u32[]{:S(2)}, u32[]{:S(2)}) collective-permute-start(bf16[2048,128]{1,0:T(8,128)(2,1)S(1)} %collective-permute-done.41), channel_id=1, source_target_pairs={{0,1},{1,0},{2,3},{3,2},{4,5},{5,4},{6,7},{7,6},{8,9},{9,8},{10,11... | collective-permute-start | bytes 1572872 | tf_op jit(solution)/shard_map/ppermute | solution.py:110
  227.5 21.0 %collective-permute-start.55 = (bf16[2048,128]{1,0:T(8,128)(2,1)S(1)}, bf16[2048,128]{1,0:T(8,128)(2,1)S(1)}, u32[]{:S(2)}, u32[]{:S(2)}) collective-permute-start(bf16[2048,128]{1,0:T(8,128)(2,1)S(1)} %collective-permute-done.53), channel_id=1, source_target_pairs={{0,2},{1,3},{2,0},{3,1},{12,14},{13,15},{14,12},{15,13},{16,18},{1... | collective-permute-start | bytes 1572872 | tf_op jit(solution)/shard_map/ppermute | solution.py:110
  230.3 20.2 %collective-permute-start.54 = (bf16[2048,128]{1,0:T(8,128)(2,1)S(1)}, bf16[2048,128]{1,0:T(8,128)(2,1)S(1)}, u32[]{:S(2)}, u32[]{:S(2)}) collective-permute-start(bf16[2048,128]{1,0:T(8,128)(2,1)S(1)} %collective-permute-done.53), channel_id=1, source_target_pairs={{0,1},{1,0},{2,3},{3,2},{12,13},{13,12},{14,15},{15,14},{16,17},{1... | collective-permute-start | bytes 1572872 | tf_op jit(solution)/shard_map/ppermute | solution.py:110
  257.4 34.1 %collective-permute-start.64 = (bf16[2048,128]{1,0:T(8,128)(2,1)S(1)}, bf16[2048,128]{1,0:T(8,128)(2,1)S(1)}, u32[]{:S(2)}, u32[]{:S(2)}) collective-permute-start(bf16[2048,128]{1,0:T(8,128)(2,1)S(1)} %get-tuple-element.21), channel_id=1, source_target_pairs={{0,8},{1,9},{2,10},{3,11},{8,0},{9,1},{10,2},{11,3},{4,12},{5,13},... | collective-permute-start | bytes 1572872 | tf_op jit(solution)/shard_map/ppermute | solution.py:107
  263.1 29.1 %collective-permute-start.60 = (bf16[2048,128]{1,0:T(8,128)(2,1)S(1)}, bf16[2048,128]{1,0:T(8,128)(2,1)S(1)}, u32[]{:S(2)}, u32[]{:S(2)}) collective-permute-start(bf16[2048,128]{1,0:T(8,128)(2,1)S(1)} %get-tuple-element.21), channel_id=1, source_target_pairs={{0,4},{1,5},{2,6},{3,7},{4,0},{5,1},{6,2},{7,3},{8,12},{9,13},{10,... | collective-permute-start | bytes 1572872 | tf_op jit(solution)/shard_map/ppermute | solution.py:107
  263.1 30.4 %collective-permute-start.58 = (bf16[2048,128]{1,0:T(8,128)(2,1)S(1)}, bf16[2048,128]{1,0:T(8,128)(2,1)S(1)}, u32[]{:S(2)}, u32[]{:S(2)}) collective-permute-start(bf16[2048,128]{1,0:T(8,128)(2,1)S(1)} %get-tuple-element.21), channel_id=1, source_target_pairs={{0,2},{1,3},{2,0},{3,1},{4,6},{5,7},{6,4},{7,5},{8,10},{9,11},{10,... | collective-permute-start | bytes 1572872 | tf_op jit(solution)/shard_map/ppermute | solution.py:110
  268.9 24.7 %collective-permute-start.57 = (bf16[2048,128]{1,0:T(8,128)(2,1)S(1)}, bf16[2048,128]{1,0:T(8,128)(2,1)S(1)}, u32[]{:S(2)}, u32[]{:S(2)}) collective-permute-start(bf16[2048,128]{1,0:T(8,128)(2,1)S(1)} %get-tuple-element.21), channel_id=1, source_target_pairs={{0,1},{1,0},{2,3},{3,2},{4,5},{5,4},{6,7},{7,6},{8,9},{9,8},{10,11... | collective-permute-start | bytes 1572872 | tf_op jit(solution)/shard_map/ppermute | solution.py:110
  270.7 23.9 %collective-permute-start.70 = (bf16[2048,128]{1,0:T(8,128)(2,1)S(1)}, bf16[2048,128]{1,0:T(8,128)(2,1)S(1)}, u32[]{:S(2)}, u32[]{:S(2)}) collective-permute-start(bf16[2048,128]{1,0:T(8,128)(2,1)S(1)} %collective-permute-done.68), channel_id=1, source_target_pairs={{4,6},{5,7},{6,4},{7,5},{8,10},{9,11},{10,8},{11,9},{20,22},{21,23... | collective-permute-start | bytes 1572872 | tf_op jit(solution)/shard_map/ppermute | solution.py:110
  294.6 25.1 %collective-permute-start.62 = (bf16[2048,128]{1,0:T(8,128)(2,1)S(1)}, bf16[2048,128]{1,0:T(8,128)(2,1)S(1)}, u32[]{:S(2)}, u32[]{:S(2)}) collective-permute-start(bf16[2048,128]{1,0:T(8,128)(2,1)S(1)} %collective-permute-done.60), channel_id=1, source_target_pairs={{0,2},{1,3},{2,0},{3,1},{4,6},{5,7},{6,4},{7,5},{8,10},{9,11},{10,... | collective-permute-start | bytes 1572872 | tf_op jit(solution)/shard_map/ppermute | solution.py:110
  295.7 24.7 %collective-permute-start.61 = (bf16[2048,128]{1,0:T(8,128)(2,1)S(1)}, bf16[2048,128]{1,0:T(8,128)(2,1)S(1)}, u32[]{:S(2)}, u32[]{:S(2)}) collective-permute-start(bf16[2048,128]{1,0:T(8,128)(2,1)S(1)} %collective-permute-done.60), channel_id=1, source_target_pairs={{0,1},{1,0},{2,3},{3,2},{4,5},{5,4},{6,7},{7,6},{8,9},{9,8},{10,11... | collective-permute-start | bytes 1572872 | tf_op jit(solution)/shard_map/ppermute | solution.py:110
  308.4 21.0 %collective-permute-start.74 = (bf16[2048,128]{1,0:T(8,128)(2,1)S(1)}, bf16[2048,128]{1,0:T(8,128)(2,1)S(1)}, u32[]{:S(2)}, u32[]{:S(2)}) collective-permute-start(bf16[2048,128]{1,0:T(8,128)(2,1)S(1)} %collective-permute-done.72), channel_id=1, source_target_pairs={{0,2},{1,3},{2,0},{3,1},{12,14},{13,15},{14,12},{15,13},{16,18},{1... | collective-permute-start | bytes 1572872 | tf_op jit(solution)/shard_map/ppermute | solution.py:110
  (58 other events, 806.9 us)

commit v3 on v2

--- a/solution.py
+++ b/solution.py
@@ -10,21 +10,17 @@
 STEPS = 4
 
 
+GROUP = 4
+
+
 def step_kernel(last, nsrc, cap, rows, cols, count, table, coeff, pump, tiles, *refs):
     sources = refs[:nsrc]
-    xpos, ymom, xout, yout, extra, tbuf, xbuf, field, tsem, xsem = refs[nsrc:]
-    tile = tbuf.shape[1]
+    xpos, ymom, xout, yout, extra, xbuf, field, xsem = refs[nsrc:]
+    slots, tile, _ = xbuf.shape
     used = count[0]
-
-    def tile_copy(s):
-        return pltpu.make_async_copy(tiles.at[s], tbuf.at[s], tsem.at[s])
 
     def block_copy(source, block, s):
         return pltpu.make_async_copy(source.at[block], xbuf.at[s], xsem.at[s])
-
-    @pl.loop(0, used)
-    def _(s):
-        tile_copy(s).start()
 
     if nsrc == 1:
         @pl.loop(0, used)
@@ -40,13 +36,24 @@
                     block_copy(source, lax.rem(cols[s], source.shape[0]), s).start()
 
     field[...] = jnp.zeros_like(field)
+    groups = (used + GROUP - 1) // GROUP
+
+    @pl.loop(used, groups * GROUP)
+    def _(s):
+        xbuf[s] = jnp.zeros(xbuf.shape[1:], xbuf.dtype)
 
     @pl.loop(0, used)
     def _(s):
-        tile_copy(s).wait()
         block_copy(sources[0], 0, s).wait()
-        here = pl.ds(pl.multiple_of(rows[s] * tile, tile), tile)
-        field[here, :] += jnp.dot(tbuf[s], xbuf[s], preferred_element_type=jnp.float32)
+
+    @pl.loop(0, groups)
+    def _(g):
+        prods = [
+            jnp.dot(tiles[g * GROUP + i], xbuf[g * GROUP + i], preferred_element_type=jnp.float32) for i in range(GROUP)
+        ]
+        for i in range(GROUP):
+            here = pl.ds(pl.multiple_of(rows[g * GROUP + i] * tile, tile), tile)
+            field[here, :] += prods[i]
 
     x = xpos[...]
     h = field[...]
@@ -77,16 +84,14 @@
             jax.ShapeDtypeStruct(ymom.shape, jnp.float32),
             extra,
         ),
-        in_specs=[smem] * 6 + [hbm] * (1 + len(sources)) + [vmem, vmem],
+        in_specs=[smem] * 6 + [vmem] + [hbm] * len(sources) + [vmem, vmem],
         out_specs=(vmem, vmem, vmem),
         scratch_shapes=[
-            pltpu.VMEM((slots, tile, tile), jnp.bfloat16),
             pltpu.VMEM((slots, tile, repl), jnp.bfloat16),
             pltpu.VMEM((order, repl), jnp.float32),
             pltpu.SemaphoreType.DMA((slots,)),
-            pltpu.SemaphoreType.DMA((slots,)),
         ],
-        compiler_params=pltpu.CompilerParams(vmem_limit_bytes=40 * 2**20),
+        compiler_params=pltpu.CompilerParams(vmem_limit_bytes=24 * 2**20),
         cost_estimate=pl.CostEstimate(
             flops=2 * slots * tile * tile * repl, bytes_accessed=slots * tile * (tile + repl) * 2, transcendentals=0
         ),
@@ -106,29 +111,18 @@
     def along_z(pairs, value):
         return lax.ppermute(value, "row", [(a * 4 + i, b * 4 + i) for a, b in pairs for i in range(4)])
 
-    def to(flip, zs, value):
-        return lax.ppermute(value, "row", [(a * 4 + i, a * 4 + (i ^ flip)) for a in zs for i in range(4)])
+    def to(flip, value):
+        return lax.ppermute(value, "row", [(a * 4 + i, a * 4 + (i ^ flip)) for a in range(4) for i in range(4)])
 
-    everyone, inner, outer = (0, 1, 2, 3), (1, 2), (0, 3)
-    is_inner = (z == 1) | (z == 2)
     near = along_z([(0, 1), (1, 0), (2, 3), (3, 2)], xb)
     skip = along_z([(0, 2), (2, 0), (1, 3), (3, 1)], xb)
-    mid = along_z([(1, 2), (2, 1)], xb)
-    far = along_z([(1, 0), (2, 3)], skip)
-    yes = z >= 0
-    column = [
-        (xb, z, yes, everyone),
-        (near, z ^ 1, yes, everyone),
-        (skip, z ^ 2, yes, everyone),
-        (mid, z ^ 3, is_inner, inner),
-        (far, z ^ 3, ~is_inner, outer),
-    ]
+    far = along_z([(0, 1), (1, 0), (2, 3), (3, 2)], skip)
     found = []
-    for value, zs, valid, who in column:
-        across = to(2, who, value)
+    for value, zs in ((xb, z), (near, z ^ 1), (skip, z ^ 2), (far, z ^ 3)):
+        across = to(2, value)
         for y, v in ((0, value), (2, across)):
-            found.append((v, zs * 4 + (yc ^ y), valid))
-            found.append((to(1, who, v), zs * 4 + (yc ^ y ^ 1), valid))
+            found.append((v, zs * 4 + (yc ^ y)))
+            found.append((to(1, v), zs * 4 + (yc ^ y ^ 1)))
     return found
 
 
@@ -150,7 +144,7 @@
     for step in range(STEPS):
         if by_hand:
             found = spread_out(extra)
-            sources = [v.reshape(blocks, tile, repl) for v, _, _ in found]
+            sources = [v.reshape(blocks, tile, repl) for v, _ in found]
         else:
             sources = [lax.all_gather(extra, "row", tiled=True).reshape(devices * blocks, tile, repl)]
         if step == 0:
@@ -159,7 +153,7 @@
                 source = tile_cols // blocks
                 same = (source[:, None] == source[None, :]) & used[None, :]
                 rank = jnp.sum((same & (slot_ids[None, :] < slot_ids[:, None])).astype(jnp.int32), axis=1)
-                owner = jnp.stack([jnp.where(valid, src, -1) for _, src, valid in found]).astype(jnp.int32)
+                owner = jnp.stack([src for _, src in found]).astype(jnp.int32)
                 want = (
                     (source[None, None, :] == owner[:, None, None])
                     & (rank[None, None, :] == jnp.arange(cap)[None, :, None])

time: 361 us -> 313 us (0.87)
  starting transfers between devices: 107 us -> 85.7 us
  waiting for transfers between devices: 195 us -> 174 us
    ppermute x16 -> x12, waiting for transfers between devices: 132 us -> 90.4 us  [along_z(): lax.ppermute(value, 'row', [(a * 4 + i, b * 4 + i) for a, b in pairs for...]
    ppermute x60 -> x48, waiting for transfers between devices: 63.3 us -> 83.3 us  [to(): lax.ppermute(value, 'row', [(a * 4 + i, a * 4 + (i ^ flip)) for a in rang...]
    ppermute x60 -> x48, starting transfers between devices: 70.5 us -> 57.9 us  [to(): lax.ppermute(value, 'row', [(a * 4 + i, a * 4 + (i ^ flip)) for a in rang...]
    ppermute x16 -> x12, starting transfers between devices: 31.4 us -> 21.9 us  [along_z(): lax.ppermute(value, 'row', [(a * 4 + i, b * 4 + i) for a, b in pairs for...]
    unnamed x26 -> x22, local copies, waits for them, and re-layouts: 7.75 us -> 7.7 us
  transfers between devices with their start and end apart: 77 -> 61, of which waited for: 23 -> 20; matrix products, arithmetic and copies ran while one was open for 2% -> 2% of each run, Pallas kernels for 0% -> 0%
where the time goes in v3:
time: 313 us; the launch traced here: 309 us
  waiting for transfers between devices  174 us (56%)
  starting transfers between devices  85.7 us (27%)
  blocking collectives  16.9 us (5%)
  Pallas kernels  14.7 us (5%)
  local copies, waits for them, and re-layouts  9.19 us (3%)
  other arithmetic  7.46 us (2%)
    ppermute x12, waiting for transfers between devices, along_z(): lax.ppermute(value, 'row', [(a * 4 + i, b * 4 + i) for a, b in pairs for...  90.4 us
    ppermute x48, waiting for transfers between devices, to(): lax.ppermute(value, 'row', [(a * 4 + i, a * 4 + (i ^ flip)) for a in rang...  83.3 us
    ppermute x48, starting transfers between devices, to(): lax.ppermute(value, 'row', [(a * 4 + i, a * 4 + (i ^ flip)) for a in rang...  57.9 us
    ppermute x12, starting transfers between devices, along_z(): lax.ppermute(value, 'row', [(a * 4 + i, b * 4 + i) for a, b in pairs for...  21.9 us
    all_to_all x1, blocking collectives, row_sum(): lax.all_to_all(spread, 'row', split_axis=0, concat_axis=0, tiled=True)  16.9 us
    pallas_call x4, Pallas kernels, run_step(): pl.pallas_call(functools.partial(step_kernel, last, len(sources), cap), o...  14.7 us
    unnamed x22, local copies, waits for them, and re-layouts  7.7 us
  transfers between devices with their start and end apart: 61, of which 20 were waited for; matrix products, arithmetic and copies ran while one was open for 2% of the time, Pallas kernels for 0%

profile of v3, /device:TPU:0, one launch (start us, length us, event | category | flops | bytes accessed | tf_op | source)
XLA Modules:
  0.0 309.4 jit_solution(7397475838150773573)
XLA Ops:
  2.0 4.1 %collective-permute-start.7 = (bf16[2048,128]{1,0:T(8,128)(2,1)S(1)}, bf16[2048,128]{1,0:T(8,128)(2,1)}, u32[]{:S(2)}, u32[]{:S(2)}) collective-permute-start(bf16[2048,128]{1,0:T(8,128)(2,1)S(1)} %convert_element_type.11), channel_id=1, source_target_pairs={{0,8},{1,9},{2,10},{3,11},{8,0},{9,1},{10,2},{11,3},{4,12},{5,13},... | collective-permute-start | bytes 1572872 | tf_op jit(solution)/shard_map/ppermute | solution.py:112
  10.0 19.5 %collective-permute-done.7 = bf16[2048,128]{1,0:T(8,128)(2,1)} collective-permute-done((bf16[2048,128]{1,0:T(8,128)(2,1)S(1)}, bf16[2048,128]{1,0:T(8,128)(2,1)}, u32[]{:S(2)}, u32[]{:S(2)}) %collective-permute-start.7) | collective-permute-done | bytes 524320 | tf_op jit(solution)/shard_map/ppermute | solution.py:112
  30.7 4.5 %multiply_reduce_fusion = f32[48]{0:T(128)S(1)} fusion(bf16[48,256,256]{2,1,0:T(8,128)(2,1)} %tiles.7), kind=kLoop, calls=%fused_computation | loop fusion | flops 9437136 | bytes 6291648 | tf_op jit(solution)/shard_map/reduce_sum | solution.py:163
  38.3 4.6 %collective-permute-done.11 = bf16[2048,128]{1,0:T(8,128)(2,1)} collective-permute-done((bf16[2048,128]{1,0:T(8,128)(2,1)}, bf16[2048,128]{1,0:T(8,128)(2,1)}, u32[]{:S(2)}, u32[]{:S(2)}) %collective-permute-start.11) | collective-permute-done | bytes 524320 | tf_op jit(solution)/shard_map/ppermute | solution.py:112
  46.0 5.9 %all-to-all-start = ((f32[16,1,128]{2,1,0:T(1,128)}), f32[16,1,128]{2,1,0:T(1,128)S(1)}, u32[]{:S(2)}, u32[]{:S(2)}) async-start(f32[16,1,128]{2,1,0:T(1,128)} %broadcast_in_dim_broadcast_in_dim.3), calls=%async_computation | async-start | bytes 16384 | tf_op jit(solution)/shard_map/all_to_all | solution.py:104
  52.8 8.9 %collective-permute-done.5 = bf16[2048,128]{1,0:T(8,128)(2,1)} collective-permute-done((bf16[2048,128]{1,0:T(8,128)(2,1)}, bf16[2048,128]{1,0:T(8,128)(2,1)}, u32[]{:S(2)}, u32[]{:S(2)}) %collective-permute-start.5) | collective-permute-done | bytes 524320 | tf_op jit(solution)/shard_map/ppermute | solution.py:115
  62.2 9.5 %collective-permute-done.13 = bf16[2048,128]{1,0:T(8,128)(2,1)} collective-permute-done((bf16[2048,128]{1,0:T(8,128)(2,1)}, bf16[2048,128]{1,0:T(8,128)(2,1)}, u32[]{:S(2)}, u32[]{:S(2)}) %collective-permute-start.13) | collective-permute-done | bytes 524320 | tf_op jit(solution)/shard_map/ppermute | solution.py:115
  80.0 3.6 %shard_map.85 = (f32[2048,128]{1,0:T(8,128)S(1)}, f32[2048,128]{1,0:T(8,128)S(1)}, bf16[2048,128]{1,0:T(8,128)(2,1)S(1)}) custom-call(s32[48]{0:T(128)S(1)} %copy-done.7, s32[48]{0:T(128)S(1)} %copy-done.8, s32[1]{0:T(128)} %copy.13.count, s32[48]{0:T(128)S(1)} %reshape.272.table, f32[1]{0:T(128)S(6)} %mul.14.coeff, f32[1]{0:T(128)} %constant.62.clone.1.pump, ...), custom_call_target="tpu_custom_call" | custom-call | flops 805306368 | bytes 9437184 | tf_op jit(solution)/shard_map/pallas_call | solution.py:80
  83.6 3.6 %collective-permute-start.22 = (bf16[2048,128]{1,0:T(8,128)(2,1)S(1)}, bf16[2048,128]{1,0:T(8,128)(2,1)S(1)}, u32[]{:S(2)}, u32[]{:S(2)}) collective-permute-start(bf16[2048,128]{1,0:T(8,128)(2,1)S(1)} %get-tuple-element.15), channel_id=1, source_target_pairs={{0,8},{1,9},{2,10},{3,11},{8,0},{9,1},{10,2},{11,3},{4,12},{5,13},... | collective-permute-start | bytes 1572872 | tf_op jit(solution)/shard_map/ppermute | solution.py:112
  87.9 4.6 %collective-permute-start.16 = (bf16[2048,128]{1,0:T(8,128)(2,1)S(1)}, bf16[2048,128]{1,0:T(8,128)(2,1)S(1)}, u32[]{:S(2)}, u32[]{:S(2)}) collective-permute-start(bf16[2048,128]{1,0:T(8,128)(2,1)S(1)} %get-tuple-element.15), channel_id=1, source_target_pairs={{0,2},{1,3},{2,0},{3,1},{4,6},{5,7},{6,4},{7,5},{8,10},{9,11},{10,... | collective-permute-start | bytes 1572872 | tf_op jit(solution)/shard_map/ppermute | solution.py:115
  92.4 18.4 %collective-permute-done.22 = bf16[2048,128]{1,0:T(8,128)(2,1)S(1)} collective-permute-done((bf16[2048,128]{1,0:T(8,128)(2,1)S(1)}, bf16[2048,128]{1,0:T(8,128)(2,1)S(1)}, u32[]{:S(2)}, u32[]{:S(2)}) %collective-permute-start.22) | collective-permute-done | bytes 524320 | tf_op jit(solution)/shard_map/ppermute | solution.py:112
  112.6 5.5 %collective-permute-start.20 = (bf16[2048,128]{1,0:T(8,128)(2,1)S(1)}, bf16[2048,128]{1,0:T(8,128)(2,1)S(1)}, u32[]{:S(2)}, u32[]{:S(2)}) collective-permute-start(bf16[2048,128]{1,0:T(8,128)(2,1)S(1)} %collective-permute-done.18), channel_id=1, source_target_pairs={{0,2},{1,3},{2,0},{3,1},{4,6},{5,7},{6,4},{7,5},{8,10},{9,11},{10,... | collective-permute-start | bytes 1572872 | tf_op jit(solution)/shard_map/ppermute | solution.py:115
  118.3 6.7 %collective-permute-done.26 = bf16[2048,128]{1,0:T(8,128)(2,1)S(1)} collective-permute-done((bf16[2048,128]{1,0:T(8,128)(2,1)S(1)}, bf16[2048,128]{1,0:T(8,128)(2,1)S(1)}, u32[]{:S(2)}, u32[]{:S(2)}) %collective-permute-start.26) | collective-permute-done | bytes 524320 | tf_op jit(solution)/shard_map/ppermute | solution.py:112
  127.9 8.9 %collective-permute-done.20 = bf16[2048,128]{1,0:T(8,128)(2,1)S(1)} collective-permute-done((bf16[2048,128]{1,0:T(8,128)(2,1)S(1)}, bf16[2048,128]{1,0:T(8,128)(2,1)S(1)}, u32[]{:S(2)}, u32[]{:S(2)}) %collective-permute-start.20) | collective-permute-done | bytes 524320 | tf_op jit(solution)/shard_map/ppermute | solution.py:115
  137.3 10.2 %collective-permute-done.28 = bf16[2048,128]{1,0:T(8,128)(2,1)S(1)} collective-permute-done((bf16[2048,128]{1,0:T(8,128)(2,1)S(1)}, bf16[2048,128]{1,0:T(8,128)(2,1)S(1)}, u32[]{:S(2)}, u32[]{:S(2)}) %collective-permute-start.28) | collective-permute-done | bytes 524320 | tf_op jit(solution)/shard_map/ppermute | solution.py:115
  149.5 3.3 %shard_map.86 = (f32[2048,128]{1,0:T(8,128)S(1)}, f32[2048,128]{1,0:T(8,128)S(1)}, bf16[2048,128]{1,0:T(8,128)(2,1)S(1)}) custom-call(s32[48]{0:T(128)S(1)} %copy-done.7, s32[48]{0:T(128)S(1)} %copy-done.8, s32[1]{0:T(128)} %copy.13.count, s32[48]{0:T(128)S(1)} %reshape.272.table, f32[1]{0:T(128)S(6)} %mul.14.coeff, f32[1]{0:T(128)} %constant.61.clone.1.pump, ...), custom_call_target="tpu_custom_call" | custom-call | flops 805306368 | bytes 9437184 | tf_op jit(solution)/shard_map/pallas_call | solution.py:80
  156.8 5.3 %collective-permute-start.31 = (bf16[2048,128]{1,0:T(8,128)(2,1)S(1)}, bf16[2048,128]{1,0:T(8,128)(2,1)S(1)}, u32[]{:S(2)}, u32[]{:S(2)}) collective-permute-start(bf16[2048,128]{1,0:T(8,128)(2,1)S(1)} %get-tuple-element.18), channel_id=1, source_target_pairs={{0,2},{1,3},{2,0},{3,1},{4,6},{5,7},{6,4},{7,5},{8,10},{9,11},{10,... | collective-permute-start | bytes 1572872 | tf_op jit(solution)/shard_map/ppermute | solution.py:115
  162.6 15.7 %collective-permute-done.37 = bf16[2048,128]{1,0:T(8,128)(2,1)S(1)} collective-permute-done((bf16[2048,128]{1,0:T(8,128)(2,1)S(1)}, bf16[2048,128]{1,0:T(8,128)(2,1)S(1)}, u32[]{:S(2)}, u32[]{:S(2)}) %collective-permute-start.37) | collective-permute-done | bytes 524320 | tf_op jit(solution)/shard_map/ppermute | solution.py:112
  180.4 6.8 %collective-permute-start.35 = (bf16[2048,128]{1,0:T(8,128)(2,1)S(1)}, bf16[2048,128]{1,0:T(8,128)(2,1)S(1)}, u32[]{:S(2)}, u32[]{:S(2)}) collective-permute-start(bf16[2048,128]{1,0:T(8,128)(2,1)S(1)} %collective-permute-done.33), channel_id=1, source_target_pairs={{0,2},{1,3},{2,0},{3,1},{4,6},{5,7},{6,4},{7,5},{8,10},{9,11},{10,... | collective-permute-start | bytes 1572872 | tf_op jit(solution)/shard_map/ppermute | solution.py:115
  187.4 5.2 %collective-permute-done.41 = bf16[2048,128]{1,0:T(8,128)(2,1)S(1)} collective-permute-done((bf16[2048,128]{1,0:T(8,128)(2,1)S(1)}, bf16[2048,128]{1,0:T(8,128)(2,1)S(1)}, u32[]{:S(2)}, u32[]{:S(2)}) %collective-permute-start.41) | collective-permute-done | bytes 524320 | tf_op jit(solution)/shard_map/ppermute | solution.py:112
  192.7 3.7 %collective-permute-start.43 = (bf16[2048,128]{1,0:T(8,128)(2,1)S(1)}, bf16[2048,128]{1,0:T(8,128)(2,1)S(1)}, u32[]{:S(2)}, u32[]{:S(2)}) collective-permute-start(bf16[2048,128]{1,0:T(8,128)(2,1)S(1)} %collective-permute-done.41), channel_id=1, source_target_pairs={{0,2},{1,3},{2,0},{3,1},{4,6},{5,7},{6,4},{7,5},{8,10},{9,11},{10,... | collective-permute-start | bytes 1572872 | tf_op jit(solution)/shard_map/ppermute | solution.py:115
  196.8 9.0 %collective-permute-done.35 = bf16[2048,128]{1,0:T(8,128)(2,1)S(1)} collective-permute-done((bf16[2048,128]{1,0:T(8,128)(2,1)S(1)}, bf16[2048,128]{1,0:T(8,128)(2,1)S(1)}, u32[]{:S(2)}, u32[]{:S(2)}) %collective-permute-start.35) | collective-permute-done | bytes 524320 | tf_op jit(solution)/shard_map/ppermute | solution.py:115
  206.4 10.1 %collective-permute-done.43 = bf16[2048,128]{1,0:T(8,128)(2,1)S(1)} collective-permute-done((bf16[2048,128]{1,0:T(8,128)(2,1)S(1)}, bf16[2048,128]{1,0:T(8,128)(2,1)S(1)}, u32[]{:S(2)}, u32[]{:S(2)}) %collective-permute-start.43) | collective-permute-done | bytes 524320 | tf_op jit(solution)/shard_map/ppermute | solution.py:115
  225.8 5.3 %collective-permute-start.46 = (bf16[2048,128]{1,0:T(8,128)(2,1)S(1)}, bf16[2048,128]{1,0:T(8,128)(2,1)S(1)}, u32[]{:S(2)}, u32[]{:S(2)}) collective-permute-start(bf16[2048,128]{1,0:T(8,128)(2,1)S(1)} %get-tuple-element.21), channel_id=1, source_target_pairs={{0,2},{1,3},{2,0},{3,1},{4,6},{5,7},{6,4},{7,5},{8,10},{9,11},{10,... | collective-permute-start | bytes 1572872 | tf_op jit(solution)/shard_map/ppermute | solution.py:115
  231.6 15.6 %collective-permute-done.52 = bf16[2048,128]{1,0:T(8,128)(2,1)S(1)} collective-permute-done((bf16[2048,128]{1,0:T(8,128)(2,1)S(1)}, bf16[2048,128]{1,0:T(8,128)(2,1)S(1)}, u32[]{:S(2)}, u32[]{:S(2)}) %collective-permute-start.52) | collective-permute-done | bytes 524320 | tf_op jit(solution)/shard_map/ppermute | solution.py:112
  249.2 7.2 %collective-permute-start.50 = (bf16[2048,128]{1,0:T(8,128)(2,1)S(1)}, bf16[2048,128]{1,0:T(8,128)(2,1)S(1)}, u32[]{:S(2)}, u32[]{:S(2)}) collective-permute-start(bf16[2048,128]{1,0:T(8,128)(2,1)S(1)} %collective-permute-done.48), channel_id=1, source_target_pairs={{0,2},{1,3},{2,0},{3,1},{4,6},{5,7},{6,4},{7,5},{8,10},{9,11},{10,... | collective-permute-start | bytes 1572872 | tf_op jit(solution)/shard_map/ppermute | solution.py:115
  256.6 4.8 %collective-permute-done.56 = bf16[2048,128]{1,0:T(8,128)(2,1)S(1)} collective-permute-done((bf16[2048,128]{1,0:T(8,128)(2,1)S(1)}, bf16[2048,128]{1,0:T(8,128)(2,1)S(1)}, u32[]{:S(2)}, u32[]{:S(2)}) %collective-permute-start.56) | collective-permute-done | bytes 524320 | tf_op jit(solution)/shard_map/ppermute | solution.py:112
  261.5 3.9 %collective-permute-start.58 = (bf16[2048,128]{1,0:T(8,128)(2,1)S(1)}, bf16[2048,128]{1,0:T(8,128)(2,1)S(1)}, u32[]{:S(2)}, u32[]{:S(2)}) collective-permute-start(bf16[2048,128]{1,0:T(8,128)(2,1)S(1)} %collective-permute-done.56), channel_id=1, source_target_pairs={{0,2},{1,3},{2,0},{3,1},{4,6},{5,7},{6,4},{7,5},{8,10},{9,11},{10,... | collective-permute-start | bytes 1572872 | tf_op jit(solution)/shard_map/ppermute | solution.py:115
  265.9 9.0 %collective-permute-done.50 = bf16[2048,128]{1,0:T(8,128)(2,1)S(1)} collective-permute-done((bf16[2048,128]{1,0:T(8,128)(2,1)S(1)}, bf16[2048,128]{1,0:T(8,128)(2,1)S(1)}, u32[]{:S(2)}, u32[]{:S(2)}) %collective-permute-start.50) | collective-permute-done | bytes 524320 | tf_op jit(solution)/shard_map/ppermute | solution.py:115
  275.4 10.1 %collective-permute-done.58 = bf16[2048,128]{1,0:T(8,128)(2,1)S(1)} collective-permute-done((bf16[2048,128]{1,0:T(8,128)(2,1)S(1)}, bf16[2048,128]{1,0:T(8,128)(2,1)S(1)}, u32[]{:S(2)}, u32[]{:S(2)}) %collective-permute-start.58) | collective-permute-done | bytes 524320 | tf_op jit(solution)/shard_map/ppermute | solution.py:115
  287.4 4.5 %shard_map.88 = (f32[2048,128]{1,0:T(8,128)}, f32[2048,128]{1,0:T(8,128)}, f32[1,128]{1,0:T(1,128)S(1)}) custom-call(s32[48]{0:T(128)S(1)} %copy-done.7, s32[48]{0:T(128)S(1)} %copy-done.8, s32[1]{0:T(128)} %copy.13.count, s32[48]{0:T(128)S(1)} %reshape.272.table, f32[1]{0:T(128)S(6)} %mul.14.coeff, f32[1]{0:T(128)} %constant.59.clone.1.pump, ...), custom_call_target="tpu_custom_call" | custom-call | flops 805306368 | bytes 9437184 | tf_op jit(solution)/shard_map/pallas_call | solution.py:80
  291.9 16.9 %all_to_all.12 = f32[16,1,128]{2,1,0:T(1,128)S(1)} all-to-all(f32[16,1,128]{2,1,0:T(1,128)S(1)} %broadcast_in_dim.21), channel_id=1, replica_groups=mesh['groups'=2,'row'=16] {'row'}, dimensions={0} | all-to-all | bytes 16384 | tf_op jit(solution)/shard_map/all_to_all | solution.py:104
  (134 shorter events, 52.7 us)
Async XLA Ops:
  2.0 27.5 %collective-permute-start.7 = (bf16[2048,128]{1,0:T(8,128)(2,1)S(1)}, bf16[2048,128]{1,0:T(8,128)(2,1)}, u32[]{:S(2)}, u32[]{:S(2)}) collective-permute-start(bf16[2048,128]{1,0:T(8,128)(2,1)S(1)} %convert_element_type.11), channel_id=1, source_target_pairs={{0,8},{1,9},{2,10},{3,11},{8,0},{9,1},{10,2},{11,3},{4,12},{5,13},... | collective-permute-start | bytes 1572872 | tf_op jit(solution)/shard_map/ppermute | solution.py:112
  6.1 30.6 %collective-permute-start.3 = (bf16[2048,128]{1,0:T(8,128)(2,1)S(1)}, bf16[2048,128]{1,0:T(8,128)(2,1)}, u32[]{:S(2)}, u32[]{:S(2)}) collective-permute-start(bf16[2048,128]{1,0:T(8,128)(2,1)S(1)} %convert_element_type.11), channel_id=1, source_target_pairs={{0,4},{1,5},{2,6},{3,7},{4,0},{5,1},{6,2},{7,3},{8,12},{9,13},{10,... | collective-permute-start | bytes 1572872 | tf_op jit(solution)/shard_map/ppermute | solution.py:112
  7.7 29.1 %collective-permute-start.1 = (bf16[2048,128]{1,0:T(8,128)(2,1)S(1)}, bf16[2048,128]{1,0:T(8,128)(2,1)}, u32[]{:S(2)}, u32[]{:S(2)}) collective-permute-start(bf16[2048,128]{1,0:T(8,128)(2,1)S(1)} %convert_element_type.11), channel_id=1, source_target_pairs={{0,2},{1,3},{2,0},{3,1},{4,6},{5,7},{6,4},{7,5},{8,10},{9,11},{10,... | collective-permute-start | bytes 1572872 | tf_op jit(solution)/shard_map/ppermute | solution.py:115
  9.2 28.1 %collective-permute-start = (bf16[2048,128]{1,0:T(8,128)(2,1)S(1)}, bf16[2048,128]{1,0:T(8,128)(2,1)S(1)}, u32[]{:S(2)}, u32[]{:S(2)}) collective-permute-start(bf16[2048,128]{1,0:T(8,128)(2,1)S(1)} %convert_element_type.11), channel_id=1, source_target_pairs={{0,1},{1,0},{2,3},{3,2},{4,5},{5,4},{6,7},{7,6},{8,9},{9,8},{10,11... | collective-permute-start | bytes 1572872 | tf_op jit(solution)/shard_map/ppermute | solution.py:115
  36.8 24.9 %collective-permute-start.5 = (bf16[2048,128]{1,0:T(8,128)(2,1)}, bf16[2048,128]{1,0:T(8,128)(2,1)}, u32[]{:S(2)}, u32[]{:S(2)}) collective-permute-start(bf16[2048,128]{1,0:T(8,128)(2,1)} %collective-permute-done.3), channel_id=1, source_target_pairs={{0,2},{1,3},{2,0},{3,1},{4,6},{5,7},{6,4},{7,5},{8,10},{9,11},{10,... | collective-permute-start | bytes 1572872 | tf_op jit(solution)/shard_map/ppermute | solution.py:115
  38.1 23.5 %collective-permute-start.4 = (bf16[2048,128]{1,0:T(8,128)(2,1)}, bf16[2048,128]{1,0:T(8,128)(2,1)}, u32[]{:S(2)}, u32[]{:S(2)}) collective-permute-start(bf16[2048,128]{1,0:T(8,128)(2,1)} %collective-permute-done.3), channel_id=1, source_target_pairs={{0,1},{1,0},{2,3},{3,2},{4,5},{5,4},{6,7},{7,6},{8,9},{9,8},{10,11... | collective-permute-start | bytes 1572872 | tf_op jit(solution)/shard_map/ppermute | solution.py:115
  42.9 28.8 %collective-permute-start.13 = (bf16[2048,128]{1,0:T(8,128)(2,1)}, bf16[2048,128]{1,0:T(8,128)(2,1)}, u32[]{:S(2)}, u32[]{:S(2)}) collective-permute-start(bf16[2048,128]{1,0:T(8,128)(2,1)} %collective-permute-done.11), channel_id=1, source_target_pairs={{0,2},{1,3},{2,0},{3,1},{4,6},{5,7},{6,4},{7,5},{8,10},{9,11},{10,... | collective-permute-start | bytes 1572872 | tf_op jit(solution)/shard_map/ppermute | solution.py:115
  46.0 26.1 %all-to-all-start = ((f32[16,1,128]{2,1,0:T(1,128)}), f32[16,1,128]{2,1,0:T(1,128)S(1)}, u32[]{:S(2)}, u32[]{:S(2)}) async-start(f32[16,1,128]{2,1,0:T(1,128)} %broadcast_in_dim_broadcast_in_dim.3), calls=%async_computation | async-start | bytes 16384 | tf_op jit(solution)/shard_map/all_to_all | solution.py:104
  83.6 27.2 %collective-permute-start.22 = (bf16[2048,128]{1,0:T(8,128)(2,1)S(1)}, bf16[2048,128]{1,0:T(8,128)(2,1)S(1)}, u32[]{:S(2)}, u32[]{:S(2)}) collective-permute-start(bf16[2048,128]{1,0:T(8,128)(2,1)S(1)} %get-tuple-element.15), channel_id=1, source_target_pairs={{0,8},{1,9},{2,10},{3,11},{8,0},{9,1},{10,2},{11,3},{4,12},{5,13},... | collective-permute-start | bytes 1572872 | tf_op jit(solution)/shard_map/ppermute | solution.py:112
  87.2 24.3 %collective-permute-start.18 = (bf16[2048,128]{1,0:T(8,128)(2,1)S(1)}, bf16[2048,128]{1,0:T(8,128)(2,1)S(1)}, u32[]{:S(2)}, u32[]{:S(2)}) collective-permute-start(bf16[2048,128]{1,0:T(8,128)(2,1)S(1)} %get-tuple-element.15), channel_id=1, source_target_pairs={{0,4},{1,5},{2,6},{3,7},{4,0},{5,1},{6,2},{7,3},{8,12},{9,13},{10,... | collective-permute-start | bytes 1572872 | tf_op jit(solution)/shard_map/ppermute | solution.py:112
  87.9 24.7 %collective-permute-start.16 = (bf16[2048,128]{1,0:T(8,128)(2,1)S(1)}, bf16[2048,128]{1,0:T(8,128)(2,1)S(1)}, u32[]{:S(2)}, u32[]{:S(2)}) collective-permute-start(bf16[2048,128]{1,0:T(8,128)(2,1)S(1)} %get-tuple-element.15), channel_id=1, source_target_pairs={{0,2},{1,3},{2,0},{3,1},{4,6},{5,7},{6,4},{7,5},{8,10},{9,11},{10,... | collective-permute-start | bytes 1572872 | tf_op jit(solution)/shard_map/ppermute | solution.py:115
  92.4 25.7 %collective-permute-start.15 = (bf16[2048,128]{1,0:T(8,128)(2,1)S(1)}, bf16[2048,128]{1,0:T(8,128)(2,1)S(1)}, u32[]{:S(2)}, u32[]{:S(2)}) collective-permute-start(bf16[2048,128]{1,0:T(8,128)(2,1)S(1)} %get-tuple-element.15), channel_id=1, source_target_pairs={{0,1},{1,0},{2,3},{3,2},{4,5},{5,4},{6,7},{7,6},{8,9},{9,8},{10,11... | collective-permute-start | bytes 1572872 | tf_op jit(solution)/shard_map/ppermute | solution.py:115
  112.6 24.3 %collective-permute-start.20 = (bf16[2048,128]{1,0:T(8,128)(2,1)S(1)}, bf16[2048,128]{1,0:T(8,128)(2,1)S(1)}, u32[]{:S(2)}, u32[]{:S(2)}) collective-permute-start(bf16[2048,128]{1,0:T(8,128)(2,1)S(1)} %collective-permute-done.18), channel_id=1, source_target_pairs={{0,2},{1,3},{2,0},{3,1},{4,6},{5,7},{6,4},{7,5},{8,10},{9,11},{10,... | collective-permute-start | bytes 1572872 | tf_op jit(solution)/shard_map/ppermute | solution.py:115
  125.0 22.6 %collective-permute-start.28 = (bf16[2048,128]{1,0:T(8,128)(2,1)S(1)}, bf16[2048,128]{1,0:T(8,128)(2,1)S(1)}, u32[]{:S(2)}, u32[]{:S(2)}) collective-permute-start(bf16[2048,128]{1,0:T(8,128)(2,1)S(1)} %collective-permute-done.26), channel_id=1, source_target_pairs={{0,2},{1,3},{2,0},{3,1},{4,6},{5,7},{6,4},{7,5},{8,10},{9,11},{10,... | collective-permute-start | bytes 1572872 | tf_op jit(solution)/shard_map/ppermute | solution.py:115
  127.4 20.2 %collective-permute-start.17 = (bf16[2048,128]{1,0:T(8,128)(2,1)S(1)}, bf16[2048,128]{1,0:T(8,128)(2,1)S(1)}, u32[]{:S(2)}, u32[]{:S(2)}) collective-permute-start(bf16[2048,128]{1,0:T(8,128)(2,1)S(1)} %collective-permute-done.16), channel_id=1, source_target_pairs={{0,1},{1,0},{2,3},{3,2},{4,5},{5,4},{6,7},{7,6},{8,9},{9,8},{10,11... | collective-permute-start | bytes 1572872 | tf_op jit(solution)/shard_map/ppermute | solution.py:115
  127.4 20.2 %collective-permute-start.27 = (bf16[2048,128]{1,0:T(8,128)(2,1)S(1)}, bf16[2048,128]{1,0:T(8,128)(2,1)S(1)}, u32[]{:S(2)}, u32[]{:S(2)}) collective-permute-start(bf16[2048,128]{1,0:T(8,128)(2,1)S(1)} %collective-permute-done.26), channel_id=1, source_target_pairs={{0,1},{1,0},{2,3},{3,2},{4,5},{5,4},{6,7},{7,6},{8,9},{9,8},{10,11... | collective-permute-start | bytes 1572872 | tf_op jit(solution)/shard_map/ppermute | solution.py:115
  152.8 25.4 %collective-permute-start.37 = (bf16[2048,128]{1,0:T(8,128)(2,1)S(1)}, bf16[2048,128]{1,0:T(8,128)(2,1)S(1)}, u32[]{:S(2)}, u32[]{:S(2)}) collective-permute-start(bf16[2048,128]{1,0:T(8,128)(2,1)S(1)} %get-tuple-element.18), channel_id=1, source_target_pairs={{0,8},{1,9},{2,10},{3,11},{8,0},{9,1},{10,2},{11,3},{4,12},{5,13},... | collective-permute-start | bytes 1572872 | tf_op jit(solution)/shard_map/ppermute | solution.py:112
  155.7 24.7 %collective-permute-start.33 = (bf16[2048,128]{1,0:T(8,128)(2,1)S(1)}, bf16[2048,128]{1,0:T(8,128)(2,1)S(1)}, u32[]{:S(2)}, u32[]{:S(2)}) collective-permute-start(bf16[2048,128]{1,0:T(8,128)(2,1)S(1)} %get-tuple-element.18), channel_id=1, source_target_pairs={{0,4},{1,5},{2,6},{3,7},{4,0},{5,1},{6,2},{7,3},{8,12},{9,13},{10,... | collective-permute-start | bytes 1572872 | tf_op jit(solution)/shard_map/ppermute | solution.py:112
  156.8 23.6 %collective-permute-start.31 = (bf16[2048,128]{1,0:T(8,128)(2,1)S(1)}, bf16[2048,128]{1,0:T(8,128)(2,1)S(1)}, u32[]{:S(2)}, u32[]{:S(2)}) collective-permute-start(bf16[2048,128]{1,0:T(8,128)(2,1)S(1)} %get-tuple-element.18), channel_id=1, source_target_pairs={{0,2},{1,3},{2,0},{3,1},{4,6},{5,7},{6,4},{7,5},{8,10},{9,11},{10,... | collective-permute-start | bytes 1572872 | tf_op jit(solution)/shard_map/ppermute | solution.py:115
  162.1 25.1 %collective-permute-start.30 = (bf16[2048,128]{1,0:T(8,128)(2,1)S(1)}, bf16[2048,128]{1,0:T(8,128)(2,1)S(1)}, u32[]{:S(2)}, u32[]{:S(2)}) collective-permute-start(bf16[2048,128]{1,0:T(8,128)(2,1)S(1)} %get-tuple-element.18), channel_id=1, source_target_pairs={{0,1},{1,0},{2,3},{3,2},{4,5},{5,4},{6,7},{7,6},{8,9},{9,8},{10,11... | collective-permute-start | bytes 1572872 | tf_op jit(solution)/shard_map/ppermute | solution.py:115
  180.4 25.5 %collective-permute-start.35 = (bf16[2048,128]{1,0:T(8,128)(2,1)S(1)}, bf16[2048,128]{1,0:T(8,128)(2,1)S(1)}, u32[]{:S(2)}, u32[]{:S(2)}) collective-permute-start(bf16[2048,128]{1,0:T(8,128)(2,1)S(1)} %collective-permute-done.33), channel_id=1, source_target_pairs={{0,2},{1,3},{2,0},{3,1},{4,6},{5,7},{6,4},{7,5},{8,10},{9,11},{10,... | collective-permute-start | bytes 1572872 | tf_op jit(solution)/shard_map/ppermute | solution.py:115
  192.7 23.9 %collective-permute-start.43 = (bf16[2048,128]{1,0:T(8,128)(2,1)S(1)}, bf16[2048,128]{1,0:T(8,128)(2,1)S(1)}, u32[]{:S(2)}, u32[]{:S(2)}) collective-permute-start(bf16[2048,128]{1,0:T(8,128)(2,1)S(1)} %collective-permute-done.41), channel_id=1, source_target_pairs={{0,2},{1,3},{2,0},{3,1},{4,6},{5,7},{6,4},{7,5},{8,10},{9,11},{10,... | collective-permute-start | bytes 1572872 | tf_op jit(solution)/shard_map/ppermute | solution.py:115
  196.3 20.2 %collective-permute-start.32 = (bf16[2048,128]{1,0:T(8,128)(2,1)S(1)}, bf16[2048,128]{1,0:T(8,128)(2,1)S(1)}, u32[]{:S(2)}, u32[]{:S(2)}) collective-permute-start(bf16[2048,128]{1,0:T(8,128)(2,1)S(1)} %collective-permute-done.31), channel_id=1, source_target_pairs={{0,1},{1,0},{2,3},{3,2},{4,5},{5,4},{6,7},{7,6},{8,9},{9,8},{10,11... | collective-permute-start | bytes 1572872 | tf_op jit(solution)/shard_map/ppermute | solution.py:115
  196.3 20.2 %collective-permute-start.42 = (bf16[2048,128]{1,0:T(8,128)(2,1)S(1)}, bf16[2048,128]{1,0:T(8,128)(2,1)S(1)}, u32[]{:S(2)}, u32[]{:S(2)}) collective-permute-start(bf16[2048,128]{1,0:T(8,128)(2,1)S(1)} %collective-permute-done.41), channel_id=1, source_target_pairs={{0,1},{1,0},{2,3},{3,2},{4,5},{5,4},{6,7},{7,6},{8,9},{9,8},{10,11... | collective-permute-start | bytes 1572872 | tf_op jit(solution)/shard_map/ppermute | solution.py:115
  221.8 25.4 %collective-permute-start.52 = (bf16[2048,128]{1,0:T(8,128)(2,1)S(1)}, bf16[2048,128]{1,0:T(8,128)(2,1)S(1)}, u32[]{:S(2)}, u32[]{:S(2)}) collective-permute-start(bf16[2048,128]{1,0:T(8,128)(2,1)S(1)} %get-tuple-element.21), channel_id=1, source_target_pairs={{0,8},{1,9},{2,10},{3,11},{8,0},{9,1},{10,2},{11,3},{4,12},{5,13},... | collective-permute-start | bytes 1572872 | tf_op jit(solution)/shard_map/ppermute | solution.py:112
  224.7 24.5 %collective-permute-start.48 = (bf16[2048,128]{1,0:T(8,128)(2,1)S(1)}, bf16[2048,128]{1,0:T(8,128)(2,1)S(1)}, u32[]{:S(2)}, u32[]{:S(2)}) collective-permute-start(bf16[2048,128]{1,0:T(8,128)(2,1)S(1)} %get-tuple-element.21), channel_id=1, source_target_pairs={{0,4},{1,5},{2,6},{3,7},{4,0},{5,1},{6,2},{7,3},{8,12},{9,13},{10,... | collective-permute-start | bytes 1572872 | tf_op jit(solution)/shard_map/ppermute | solution.py:112
  225.8 23.4 %collective-permute-start.46 = (bf16[2048,128]{1,0:T(8,128)(2,1)S(1)}, bf16[2048,128]{1,0:T(8,128)(2,1)S(1)}, u32[]{:S(2)}, u32[]{:S(2)}) collective-permute-start(bf16[2048,128]{1,0:T(8,128)(2,1)S(1)} %get-tuple-element.21), channel_id=1, source_target_pairs={{0,2},{1,3},{2,0},{3,1},{4,6},{5,7},{6,4},{7,5},{8,10},{9,11},{10,... | collective-permute-start | bytes 1572872 | tf_op jit(solution)/shard_map/ppermute | solution.py:115
  231.2 25.3 %collective-permute-start.45 = (bf16[2048,128]{1,0:T(8,128)(2,1)S(1)}, bf16[2048,128]{1,0:T(8,128)(2,1)S(1)}, u32[]{:S(2)}, u32[]{:S(2)}) collective-permute-start(bf16[2048,128]{1,0:T(8,128)(2,1)S(1)} %get-tuple-element.21), channel_id=1, source_target_pairs={{0,1},{1,0},{2,3},{3,2},{4,5},{5,4},{6,7},{7,6},{8,9},{9,8},{10,11... | collective-permute-start | bytes 1572872 | tf_op jit(solution)/shard_map/ppermute | solution.py:115
  249.2 25.6 %collective-permute-start.50 = (bf16[2048,128]{1,0:T(8,128)(2,1)S(1)}, bf16[2048,128]{1,0:T(8,128)(2,1)S(1)}, u32[]{:S(2)}, u32[]{:S(2)}) collective-permute-start(bf16[2048,128]{1,0:T(8,128)(2,1)S(1)} %collective-permute-done.48), channel_id=1, source_target_pairs={{0,2},{1,3},{2,0},{3,1},{4,6},{5,7},{6,4},{7,5},{8,10},{9,11},{10,... | collective-permute-start | bytes 1572872 | tf_op jit(solution)/shard_map/ppermute | solution.py:115
  261.5 24.0 %collective-permute-start.58 = (bf16[2048,128]{1,0:T(8,128)(2,1)S(1)}, bf16[2048,128]{1,0:T(8,128)(2,1)S(1)}, u32[]{:S(2)}, u32[]{:S(2)}) collective-permute-start(bf16[2048,128]{1,0:T(8,128)(2,1)S(1)} %collective-permute-done.56), channel_id=1, source_target_pairs={{0,2},{1,3},{2,0},{3,1},{4,6},{5,7},{6,4},{7,5},{8,10},{9,11},{10,... | collective-permute-start | bytes 1572872 | tf_op jit(solution)/shard_map/ppermute | solution.py:115
  265.4 20.2 %collective-permute-start.47 = (bf16[2048,128]{1,0:T(8,128)(2,1)S(1)}, bf16[2048,128]{1,0:T(8,128)(2,1)S(1)}, u32[]{:S(2)}, u32[]{:S(2)}) collective-permute-start(bf16[2048,128]{1,0:T(8,128)(2,1)S(1)} %collective-permute-done.46), channel_id=1, source_target_pairs={{0,1},{1,0},{2,3},{3,2},{4,5},{5,4},{6,7},{7,6},{8,9},{9,8},{10,11... | collective-permute-start | bytes 1572872 | tf_op jit(solution)/shard_map/ppermute | solution.py:115
  265.4 20.2 %collective-permute-start.57 = (bf16[2048,128]{1,0:T(8,128)(2,1)S(1)}, bf16[2048,128]{1,0:T(8,128)(2,1)S(1)}, u32[]{:S(2)}, u32[]{:S(2)}) collective-permute-start(bf16[2048,128]{1,0:T(8,128)(2,1)S(1)} %collective-permute-done.56), channel_id=1, source_target_pairs={{0,1},{1,0},{2,3},{3,2},{4,5},{5,4},{6,7},{7,6},{8,9},{9,8},{10,11... | collective-permute-start | bytes 1572872 | tf_op jit(solution)/shard_map/ppermute | solution.py:115
  (40 other events, 769.3 us)

commit v4 on v0

v4 whole, which is shorter than its diff:
```python
import functools

import jax
import jax.numpy as jnp
from jax import lax
from jax.experimental import pallas as pl
from jax.experimental.pallas import tpu as pltpu
from jax.sharding import PartitionSpec as P

STEPS = 4
GROUP = 6
LIMIT = 32 * 2**20

SMEM = pl.BlockSpec(memory_space=pltpu.SMEM)
VMEM = pl.BlockSpec(memory_space=pltpu.VMEM)
ANY = pl.BlockSpec(memory_space=pl.ANY)


def params():
    return pltpu.CompilerParams(vmem_limit_bytes=LIMIT)


def squares_kernel(count, tiles, out):
    tile = tiles.shape[1]

    def add(s, acc):
        t = tiles[s].astype(jnp.float32)
        return acc + jnp.sum((t * t).reshape(tile // 8, 8, tile), axis=0)

    acc = lax.fori_loop(0, count[0], add, jnp.zeros((8, tile), jnp.float32))
    acc = jnp.sum(acc, axis=0, keepdims=True)
    out[...] = sum(acc[:, i : i + 128] for i in range(0, tile, 128))


def squares(count, tiles):
    return pl.pallas_call(
        squares_kernel,
        out_shape=jax.ShapeDtypeStruct((1, 128), jnp.float32),
        in_specs=[SMEM, VMEM],
        out_specs=VMEM,
        compiler_params=params(),
        cost_estimate=pl.CostEstimate(flops=2 * tiles.size, bytes_accessed=2 * tiles.size, transcendentals=0),
    )(count, tiles)


def update(pump, coeff, h, x, y):
    y = y + 0.5 * (-(x * x + pump) * x + coeff * h)
    return x + 0.5 * y, y


class Layout:
    def __init__(self, cap):
        self.cap = cap
        self.inner = 0
        self.packs = 1
        self.entries = 1 + 4 * 3 * cap

    def pack(self, j, flip, r):
        return self.packs + (j * 3 + flip - 1) * self.cap + r

    def entry(self, j, flip, r):
        return self.entries + 3 * ((j * 4 + flip) * self.cap + r)


def pack_into(layout, table, j, shard, outs):
    for flip in (1, 2, 3):
        for r in range(layout.cap):
            outs[flip - 1][r] = shard[table[layout.pack(j, flip, r)]]


def pack_kernel(layout, j, nshards, table, *refs):
    shards, outs = refs[:nshards], refs[-3:]
    if len(shards) == 1:
        pack_into(layout, table, j, shards[0], outs)
        return

    @pl.when(table[layout.inner] == 1)
    def _():
        pack_into(layout, table, j, shards[0], outs)

    @pl.when(table[layout.inner] == 0)
    def _():
        pack_into(layout, table, j, shards[1], outs)


def pack(layout, j, table, shards, after):
    _, tile, repl = shards[0].shape
    out = jax.ShapeDtypeStruct((layout.cap, tile, repl), jnp.bfloat16)
    return pl.pallas_call(
        functools.partial(pack_kernel, layout, j, len(shards)),
        out_shape=(out,) * 3,
        in_specs=[SMEM] + [VMEM] * len(shards) + [ANY] * len(after),
        out_specs=(VMEM,) * 3,
        compiler_params=params(),
        cost_estimate=pl.CostEstimate(flops=0, bytes_accessed=12 * layout.cap * tile * repl, transcendentals=0),
    )(table, *shards, *after)


def take_blocks(layout, table, j, shards, packs, xbuf, first):
    cap = layout.cap

    def own(shard):
        for r in range(cap):
            xbuf[first + r] = shard[table[layout.entry(j, 0, r) + 2]]

    if len(shards) == 1:
        own(shards[0])
    else:
        pl.when(table[layout.inner] == 1)(lambda: own(shards[0]))
        pl.when(table[layout.inner] == 0)(lambda: own(shards[1]))
    for flip in (1, 2, 3):
        for r in range(cap):
            xbuf[first + flip * cap + r] = packs[flip - 1][r]


def early_kernel(layout, table, tiles, own0, own1, own2a, own2b, *refs):
    packs, (field, xbuf) = refs[:9], refs[9:]
    per = 4 * layout.cap
    for j, shards in enumerate(([own0], [own1], [own2a, own2b])):
        take_blocks(layout, table, j, shards, packs[3 * j : 3 * j + 3], xbuf, j * per)
    field[...] = jnp.zeros_like(field)

    @pl.loop(0, 3 * per // GROUP)
    def _(g):
        at = [g * GROUP + i for i in range(GROUP)]
        prods = [
            jnp.dot(tiles[table[layout.entries + 3 * e]], xbuf[e], preferred_element_type=jnp.float32) for e in at
        ]
        for e, prod in zip(at, prods):
            field[table[layout.entries + 3 * e + 1]] += prod


def early(layout, table, tiles, shards, packs):
    _, tile, _ = tiles.shape
    blocks, _, repl = shards[0].shape
    entries = 12 * layout.cap
    return pl.pallas_call(
        functools.partial(early_kernel, layout),
        out_shape=jax.ShapeDtypeStruct((blocks + 1, tile, repl), jnp.float32),
        in_specs=[SMEM] + [VMEM] * (1 + len(shards) + len(packs)),
        out_specs=VMEM,
        scratch_shapes=[pltpu.VMEM((entries, tile, repl), jnp.bfloat16)],
        compiler_params=params(),
        cost_estimate=pl.CostEstimate(
            flops=2 * entries * tile * tile * repl,
            bytes_accessed=entries * tile * (tile + repl) * 2,
            transcendentals=0,
        ),
    )(table, tiles, *shards, *packs)


def late_kernel(layout, last, table, scalars, tiles, own3a, own3b, pack1, pack2, pack3, field, xpos, ymom, *refs):
    if last:
        xout, yout, energy, xbuf, acc = refs
    else:
        xout, yout, xb, out1, out2, out3, xbuf, acc = refs
    blocks = xpos.shape[0]
    take_blocks(layout, table, 3, [own3a, own3b], [pack1, pack2, pack3], xbuf, 0)
    acc[...] = field[...]
    at = [layout.entry(3, flip, r) for flip in range(4) for r in range(layout.cap)]
    for first in range(0, len(at), GROUP):
        some = at[first : first + GROUP]
        prods = [
            jnp.dot(tiles[table[e]], xbuf[first + i], preferred_element_type=jnp.float32) for i, e in enumerate(some)
        ]
        for e, prod in zip(some, prods):
            acc[table[e + 1]] += prod
    total = jnp.zeros((1, xpos.shape[2]), jnp.float32)
    for b in range(blocks):
        x, h = xpos[b], acc[b]
        if last:
            total += jnp.sum(x * h, axis=0, keepdims=True)
        x, y = update(scalars[0], scalars[1], h, x, ymom[b])
        xout[b] = x
        yout[b] = y
        if not last:
            xb[b] = x.astype(jnp.bfloat16)
    if last:
        energy[...] = -0.5 * total
    else:
        pack_into(layout, table, 0, xb, (out1, out2, out3))


def late(layout, last, table, scalars, tiles, shards, packs, field, xpos, ymom):
    tile = tiles.shape[1]
    blocks, _, repl = xpos.shape
    entries = 4 * layout.cap
    state = jax.ShapeDtypeStruct(xpos.shape, jnp.float32)
    if last:
        extra = (jax.ShapeDtypeStruct((1, repl), jnp.float32),)
    else:
        out = jax.ShapeDtypeStruct((layout.cap, tile, repl), jnp.bfloat16)
        extra = (jax.ShapeDtypeStruct(xpos.shape, jnp.bfloat16), out, out, out)
    return pl.pallas_call(
        functools.partial(late_kernel, layout, last),
        out_shape=(state, state) + extra,
        in_specs=[SMEM, SMEM] + [VMEM] * (1 + len(shards) + len(packs) + 3),
        out_specs=(VMEM,) * (2 + len(extra)),
        scratch_shapes=[
            pltpu.VMEM((entries, tile, repl), jnp.bfloat16),
            pltpu.VMEM((blocks + 1, tile, repl), jnp.float32),
        ],
        compiler_params=params(),
        cost_estimate=pl.CostEstimate(
            flops=2 * entries * tile * tile * repl,
            bytes_accessed=entries * tile * (tile + repl) * 2 + 20 * xpos.size,
            transcendentals=0,
        ),
    )(table, scalars, tiles, *shards, *packs, field, xpos, ymom)


PAIRS = ((0, 1), (1, 0), (2, 3), (3, 2))
MIDDLE = ((1, 2), (2, 1))
OUTWARD = ((1, 0), (2, 3))


def along_z(pairs, value):
    return lax.ppermute(value, "row", [(a * 4 + i, b * 4 + i) for a, b in pairs for i in range(4)])


def across(flip, value):
    return lax.ppermute(value, "row", [(i, i ^ flip) for i in range(16)])


def send(packs):
    return [across(flip, packs[flip - 1]) for flip in (1, 2, 3)]


def row_sum_16(part):
    part = part + (across(1, part) + across(2, part) + across(3, part))
    return part + (across(4, part) + across(8, part) + across(12, part))


def make_table(layout, blocks, tile_rows, tile_cols, used):
    cap = layout.cap
    slots = tile_cols.shape[0]
    slot_ids = jnp.arange(slots)
    me = lax.axis_index("row")
    z, yc = me // 4, me % 4
    inner = (z == 1) | (z == 2)
    zs = jnp.stack([z, z ^ 1, jnp.where(inner, z ^ 3, z ^ 2), jnp.where(inner, z ^ 2, z ^ 3)])
    source = tile_cols // blocks
    local = tile_cols % blocks
    same = (source[:, None] == source[None, :]) & used[None, :]
    rank = jnp.sum((same & (slot_ids[None, :] < slot_ids[:, None])).astype(jnp.int32), axis=1)
    key = jnp.where(used, source * cap + rank, -1)
    match = key[None, :] == jnp.arange(16 * cap)[:, None]

    def pick(values, default):
        found = jnp.sum(jnp.where(match, values[None, :] - default, 0), axis=1) + default
        return found.reshape(16, cap).astype(jnp.int32)

    wants = pick(local, 0)
    asked = jnp.stack([across(flip, wants) for flip in (1, 2, 3)])
    mine = zs * 4 + yc
    packs = asked[:, mine].transpose(1, 0, 2)
    owner = zs[:, None] * 4 + (yc ^ jnp.arange(4))[None, :]
    entries = jnp.stack([pick(slot_ids, 0), pick(tile_rows, blocks), wants], axis=-1)[owner]
    return jnp.concatenate([inner.astype(jnp.int32)[None], packs.reshape(-1), entries.reshape(-1)])


def body_16(tiles, tile_rows, tile_cols, counts, positions, momenta):
    slots, tile, _ = tiles.shape
    repl = positions.shape[1]
    blocks = positions.shape[0] // tile
    cap = (slots + 15) // 16
    order = blocks * tile * 16
    layout = Layout(cap)
    used = jnp.arange(slots) < counts[0]
    xpos = positions.reshape(blocks, tile, repl)
    ymom = momenta.reshape(blocks, tile, repl)
    own0 = xpos.astype(jnp.bfloat16)
    table = make_table(layout, blocks, tile_rows, tile_cols, used)
    packs0 = pack(layout, 0, table, [own0], [])
    coeff = None
    for step in range(STEPS):
        last = step == STEPS - 1
        own1 = along_z(PAIRS, own0)
        own2a = along_z(MIDDLE, own0)
        got = [send(packs0)]
        (own1, own2a, got[0]) = lax.optimization_barrier((own1, own2a, got[0]))
        own3a = along_z(MIDDLE, own1)
        own2b = along_z(OUTWARD, own2a)
        got.append(send(pack(layout, 1, table, [own1], got[0])))
        (own3a, own2b, got[1]) = lax.optimization_barrier((own3a, own2b, got[1]))
        own3b = along_z(OUTWARD, own3a)
        got.append(send(pack(layout, 2, table, [own2a, own2b], got[1])))
        got.append(send(pack(layout, 3, table, [own3a, own3b], got[2])))
        field = early(layout, table, tiles, [own0, own1, own2a, own2b], got[0] + got[1] + got[2])
        if step == 0:
            total = jnp.sum(row_sum_16(squares(counts, tiles)))
            coeff = 0.7 * jnp.sqrt((order - 1) / total)
        scalars = jnp.stack([jnp.float32(0.4 - 0.1 * step), coeff])
        outs = late(layout, last, table, scalars, tiles, [own3a, own3b], got[3], field, xpos, ymom)
        xpos, ymom = outs[0], outs[1]
        if not last:
            own0, packs0 = outs[2], outs[3:]
    energy = row_sum_16(outs[2])
    return (xpos.reshape(positions.shape), ymom.reshape(momenta.shape), energy.reshape(repl))


def gathered_kernel(last, rows, cols, count, scalars, tiles, gathered, xpos, ymom, xout, yout, extra, xbuf, field, xsem):
    tile = xbuf.shape[1]
    used = count[0]

    def block_copy(s):
        return pltpu.make_async_copy(gathered.at[cols[s]], xbuf.at[s], xsem.at[s])

    @pl.loop(0, used)
    def _(s):
        block_copy(s).start()

    field[...] = jnp.zeros_like(field)

    @pl.loop(0, used)
    def _(s):
        block_copy(s).wait()
        here = pl.ds(pl.multiple_of(rows[s] * tile, tile), tile)
        field[here, :] += jnp.dot(tiles[s], xbuf[s], preferred_element_type=jnp.float32)

    x, h = xpos[...], field[...]
    if last:
        extra[...] = -0.5 * jnp.sum(x * h, axis=0, keepdims=True)
    x, y = update(scalars[0], scalars[1], h, x, ymom[...])
    xout[...] = x
    yout[...] = y
    if not last:
        extra[...] = x.astype(jnp.bfloat16)


def body_any(tiles, tile_rows, tile_cols, counts, positions, momenta):
    slots, tile, _ = tiles.shape
    order, repl = positions.shape
    devices = lax.axis_size("row")
    state = jax.ShapeDtypeStruct(positions.shape, jnp.float32)
    total = jnp.sum(lax.psum(squares(counts, tiles), "row"))
    coeff = 0.7 * jnp.sqrt((order * devices - 1) / total)
    xpos, ymom, extra = positions, momenta, positions.astype(jnp.bfloat16)
    for step in range(STEPS):
        last = step == STEPS - 1
        gathered = lax.all_gather(extra, "row", tiled=True).reshape(-1, tile, repl)
        scalars = jnp.stack([jnp.float32(0.4 - 0.1 * step), coeff])
        xpos, ymom, extra = pl.pallas_call(
            functools.partial(gathered_kernel, last),
            out_shape=(
                state,
                state,
                jax.ShapeDtypeStruct((1, repl), jnp.float32) if last else jax.ShapeDtypeStruct(state.shape, jnp.bfloat16),
            ),
            in_specs=[SMEM] * 4 + [VMEM, ANY, VMEM, VMEM],
            out_specs=(VMEM,) * 3,
            scratch_shapes=[
                pltpu.VMEM((slots, tile, repl), jnp.bfloat16),
                pltpu.VMEM(positions.shape, jnp.float32),
                pltpu.SemaphoreType.DMA((slots,)),
            ],
            compiler_params=params(),
        )(tile_rows, tile_cols, counts, scalars, tiles, gathered, xpos, ymom)
    return (xpos, ymom, lax.psum(extra, "row").reshape(repl))


def solution(mesh):
    in_specs = (
        P(("groups", "row"), None, None),
        P(("groups", "row")),
        P(("groups", "row")),
        P(("groups", "row")),
        P(("groups", "row"), None),
        P(("groups", "row"), None),
    )
    out_specs = (P(("groups", "row"), None), P(("groups", "row"), None), P("groups"))
    body = body_16 if mesh.shape["row"] == 16 else body_any
    return jax.shard_map(body, mesh=mesh, in_specs=in_specs, out_specs=out_specs, check_vma=False)
```

time: 480 us -> 282 us (0.59)
  blocking collectives: 341 us -> 0 us
  waiting for transfers between devices: 5.05 us -> 157 us
  starting transfers between devices: 11.1 us -> 71.9 us
  matrix products: 51.6 us -> 0 us
  local copies, waits for them, and re-layouts: 54.3 us -> 15.1 us
  Pallas kernels: 0 us -> 30.8 us
  other arithmetic: 13.6 us -> 4.22 us
    all_to_all x3 -> x0, blocking collectives: 233 us -> none  [body(): lax.all_to_all(outgoing, 'row', split_axis=0, concat_axis=0, tiled=True)]
    ppermute x0 -> x83, waiting for transfers between devices: none -> 157 us  [the longest x63 129 us: across(): return lax.ppermute(value, 'row', [(i, i ^ flip) for i in range(16)])]
    psum x2 -> x0, blocking collectives: 108 us -> none  [the longest x1 74.8 us: body(): total = lax.psum(local_sum, 'row')]
    ppermute x0 -> x83, starting transfers between devices: none -> 71.9 us  [the longest x63 47 us: across(): return lax.ppermute(value, 'row', [(i, i ^ flip) for i in range(16)])]
    dot_general x8 -> x0, matrix products: 51.6 us -> none  [the longest x4 34.4 us: body(): jnp.einsum('sij,sjr->sir', tiles, chosen, preferred_element_type=jnp.floa...]
    pallas_call x0 -> x22, Pallas kernels: none -> 30.8 us  [the longest x4 12.2 us: early(): pl.pallas_call(functools.partial(early_kernel, layout), out_shape=jax.Sha...]
    dot_general x5 -> x0, local copies, waits for them, and re-layouts: 26.6 us -> none  [the longest x4 26.4 us: body(): jnp.einsum('sij,sjr->sir', tiles, chosen, preferred_element_type=jnp.floa...]
    gather x8 -> x2, local copies, waits for them, and re-layouts: 25.7 us -> 1.17 us  [the longest x1 0.59 us: make_table(): jnp.stack([pick(slot_ids, 0), pick(tile_rows, blocks), wants], axis=-1)]
  transfers between devices with their start and end apart: 2 -> 83, of which waited for: 1 -> 44; matrix products, arithmetic and copies ran while one was open for 1% -> 2% of each run, Pallas kernels for 0% -> 7%
where the time goes in v4:
time: 282 us; the launch traced here: 281 us
  waiting for transfers between devices  157 us (56%)
  starting transfers between devices  71.9 us (25%)
  Pallas kernels  30.8 us (11%)
  local copies, waits for them, and re-layouts  15.1 us (5%)
  other arithmetic  4.22 us (1%)
    ppermute x63, waiting for transfers between devices, across(): return lax.ppermute(value, 'row', [(i, i ^ flip) for i in range(16)])  129 us
    ppermute x63, starting transfers between devices, across(): return lax.ppermute(value, 'row', [(i, i ^ flip) for i in range(16)])  47 us
    ppermute x20, waiting for transfers between devices, along_z(): lax.ppermute(value, 'row', [(a * 4 + i, b * 4 + i) for a, b in pairs for...  27.8 us
    ppermute x20, starting transfers between devices, along_z(): lax.ppermute(value, 'row', [(a * 4 + i, b * 4 + i) for a, b in pairs for...  24.9 us
    unnamed x40, local copies, waits for them, and re-layouts  12.8 us
    pallas_call x4, Pallas kernels, early(): pl.pallas_call(functools.partial(early_kernel, layout), out_shape=jax.Sha...  12.2 us
    pallas_call x4, Pallas kernels, late(): pl.pallas_call(functools.partial(late_kernel, layout, last), out_shape=(s...  9.03 us
    pallas_call x13, Pallas kernels, pack(): pl.pallas_call(functools.partial(pack_kernel, layout, j, len(shards)), ou...  8.66 us
  transfers between devices with their start and end apart: 83, of which 44 were waited for; matrix products, arithmetic and copies ran while one was open for 2% of the time, Pallas kernels for 7%

profile of v4, /device:TPU:0, one launch (start us, length us, event | category | flops | bytes accessed | tf_op | source)
XLA Modules:
  0.0 281.5 jit_solution(2688420853744616368)
XLA Ops:
  7.6 4.6 %collective-permute-start.9 = (bf16[8,256,128]{2,1,0:T(8,128)(2,1)S(1)}, bf16[8,256,128]{2,1,0:T(8,128)(2,1)S(1)}, u32[]{:S(2)}, u32[]{:S(2)}) collective-permute-start(bf16[8,256,128]{2,1,0:T(8,128)(2,1)S(1)} %convert_element_type.8.refs_0_.own0), channel_id=1, source_target_pairs={{0,4},{1,5},{2,6},{3,7},{4,0},{5,1},{6,2},{7,3},{8,12},{9,13},{10,... | collective-permute-start | bytes 1572872 | tf_op jit(solution)/shard_map/ppermute | solution.py:218
  17.5 5.9 %collective-permute-done.12.refs_2_.refs_1_ = bf16[3,256,128]{2,1,0:T(8,128)(2,1)S(1)} collective-permute-done((bf16[3,256,128]{2,1,0:T(8,128)(2,1)S(1)}, bf16[3,256,128]{2,1,0:T(8,128)(2,1)S(1)}, u32[]{:S(2)}, u32[]{:S(2)}) %collective-permute-start.12) | collective-permute-done | bytes 196640 | tf_op jit(solution)/shard_map/ppermute | solution.py:222
  23.4 3.3 %collective-permute-done.13.refs_3_.refs_2_ = bf16[3,256,128]{2,1,0:T(8,128)(2,1)S(1)} collective-permute-done((bf16[3,256,128]{2,1,0:T(8,128)(2,1)S(1)}, bf16[3,256,128]{2,1,0:T(8,128)(2,1)S(1)}, u32[]{:S(2)}, u32[]{:S(2)}) %collective-permute-start.13) | collective-permute-done | bytes 196640 | tf_op jit(solution)/shard_map/ppermute | solution.py:222
  31.3 6.1 %collective-permute-done.17.refs_3_.refs_4_ = bf16[3,256,128]{2,1,0:T(8,128)(2,1)S(1)} collective-permute-done((bf16[3,256,128]{2,1,0:T(8,128)(2,1)S(1)}, bf16[3,256,128]{2,1,0:T(8,128)(2,1)S(1)}, u32[]{:S(2)}, u32[]{:S(2)}) %collective-permute-start.17) | collective-permute-done | bytes 196640 | tf_op jit(solution)/shard_map/ppermute | solution.py:222
  40.2 3.2 %collective-permute-done.15.refs_1_.own2b = bf16[8,256,128]{2,1,0:T(8,128)(2,1)S(1)} collective-permute-done((bf16[8,256,128]{2,1,0:T(8,128)(2,1)S(1)}, bf16[8,256,128]{2,1,0:T(8,128)(2,1)S(1)}, u32[]{:S(2)}, u32[]{:S(2)}) %collective-permute-start.15) | collective-permute-done | bytes 524320 | tf_op jit(solution)/shard_map/ppermute | solution.py:218
  56.1 3.0 %collective-permute-done.21.refs_3_.refs_7_ = bf16[3,256,128]{2,1,0:T(8,128)(2,1)S(1)} collective-permute-done((bf16[3,256,128]{2,1,0:T(8,128)(2,1)S(1)}, bf16[3,256,128]{2,1,0:T(8,128)(2,1)S(1)}, u32[]{:S(2)}, u32[]{:S(2)}) %collective-permute-start.21) | collective-permute-done | bytes 196640 | tf_op jit(solution)/shard_map/ppermute | solution.py:222
  76.6 3.0 %shard_map.90.field = f32[9,256,128]{2,1,0:T(8,128)S(1)} custom-call(s32[181]{0:T(256)S(1)} %pad_add_fusion.2.table, bf16[48,256,256]{2,1,0:T(8,128)(2,1)S(1)} %copy-done.1, bf16[8,256,128]{2,1,0:T(8,128)(2,1)S(1)} %convert_element_type.8.refs_0_.own0, bf16[8,256,128]{2,1,0:T(8,128)(2,1)S(1)} %collective-permute-done.9.refs_0_.own1, ...), custom_call_target="tpu_custom_call" | custom-call | flops 603979776 | bytes 7077888 | tf_op jit(solution)/shard_map/pallas_call | solution.py:137
  87.1 6.0 %collective-permute-done.29.refs_2_.refs_1_ = bf16[3,256,128]{2,1,0:T(8,128)(2,1)S(1)} collective-permute-done((bf16[3,256,128]{2,1,0:T(8,128)(2,1)S(1)}, bf16[3,256,128]{2,1,0:T(8,128)(2,1)S(1)}, u32[]{:S(2)}, u32[]{:S(2)}) %collective-permute-start.29) | collective-permute-done | bytes 196640 | tf_op jit(solution)/shard_map/ppermute | solution.py:222
  101.6 5.9 %collective-permute-done.34.refs_3_.refs_4_ = bf16[3,256,128]{2,1,0:T(8,128)(2,1)S(1)} collective-permute-done((bf16[3,256,128]{2,1,0:T(8,128)(2,1)S(1)}, bf16[3,256,128]{2,1,0:T(8,128)(2,1)S(1)}, u32[]{:S(2)}, u32[]{:S(2)}) %collective-permute-start.34) | collective-permute-done | bytes 196640 | tf_op jit(solution)/shard_map/ppermute | solution.py:222
  107.5 3.3 %collective-permute-done.35.refs_4_.refs_5_ = bf16[3,256,128]{2,1,0:T(8,128)(2,1)S(1)} collective-permute-done((bf16[3,256,128]{2,1,0:T(8,128)(2,1)S(1)}, bf16[3,256,128]{2,1,0:T(8,128)(2,1)S(1)}, u32[]{:S(2)}, u32[]{:S(2)}) %collective-permute-start.35) | collective-permute-done | bytes 196640 | tf_op jit(solution)/shard_map/ppermute | solution.py:222
  110.8 6.2 %collective-permute-done.32.refs_1_.own2b = bf16[8,256,128]{2,1,0:T(8,128)(2,1)S(1)} collective-permute-done((bf16[8,256,128]{2,1,0:T(8,128)(2,1)S(1)}, bf16[8,256,128]{2,1,0:T(8,128)(2,1)S(1)}, u32[]{:S(2)}, u32[]{:S(2)}) %collective-permute-start.32) | collective-permute-done | bytes 524320 | tf_op jit(solution)/shard_map/ppermute | solution.py:218
  120.9 5.9 %collective-permute-done.38.refs_3_.refs_7_ = bf16[3,256,128]{2,1,0:T(8,128)(2,1)S(1)} collective-permute-done((bf16[3,256,128]{2,1,0:T(8,128)(2,1)S(1)}, bf16[3,256,128]{2,1,0:T(8,128)(2,1)S(1)}, u32[]{:S(2)}, u32[]{:S(2)}) %collective-permute-start.38) | collective-permute-done | bytes 196640 | tf_op jit(solution)/shard_map/ppermute | solution.py:222
  126.8 3.3 %collective-permute-done.39.refs_4_.refs_8_ = bf16[3,256,128]{2,1,0:T(8,128)(2,1)S(1)} collective-permute-done((bf16[3,256,128]{2,1,0:T(8,128)(2,1)S(1)}, bf16[3,256,128]{2,1,0:T(8,128)(2,1)S(1)}, u32[]{:S(2)}, u32[]{:S(2)}) %collective-permute-start.39) | collective-permute-done | bytes 196640 | tf_op jit(solution)/shard_map/ppermute | solution.py:222
  134.4 3.1 %shard_map.95.field = f32[9,256,128]{2,1,0:T(8,128)S(1)} custom-call(s32[181]{0:T(256)S(1)} %pad_add_fusion.2.table, bf16[48,256,256]{2,1,0:T(8,128)(2,1)S(1)} %bitcast.27, bf16[8,256,128]{2,1,0:T(8,128)(2,1)S(1)} %get-tuple-element.125.own0, bf16[8,256,128]{2,1,0:T(8,128)(2,1)S(1)} %collective-permute-done.26.refs_0_.own1, ...), custom_call_target="tpu_custom_call" | custom-call | flops 603979776 | bytes 7077888 | tf_op jit(solution)/shard_map/pallas_call | solution.py:137
  140.1 3.4 %collective-permute-done.42.pack3 = bf16[3,256,128]{2,1,0:T(8,128)(2,1)S(1)} collective-permute-done((bf16[3,256,128]{2,1,0:T(8,128)(2,1)S(1)}, bf16[3,256,128]{2,1,0:T(8,128)(2,1)S(1)}, u32[]{:S(2)}, u32[]{:S(2)}) %collective-permute-start.42) | collective-permute-done | bytes 196640 | tf_op jit(solution)/shard_map/ppermute | solution.py:222
  148.7 6.1 %collective-permute-done.46.refs_2_.refs_1_ = bf16[3,256,128]{2,1,0:T(8,128)(2,1)S(1)} collective-permute-done((bf16[3,256,128]{2,1,0:T(8,128)(2,1)S(1)}, bf16[3,256,128]{2,1,0:T(8,128)(2,1)S(1)}, u32[]{:S(2)}, u32[]{:S(2)}) %collective-permute-start.46) | collective-permute-done | bytes 196640 | tf_op jit(solution)/shard_map/ppermute | solution.py:222
  163.9 5.9 %collective-permute-done.51.refs_3_.refs_4_ = bf16[3,256,128]{2,1,0:T(8,128)(2,1)S(1)} collective-permute-done((bf16[3,256,128]{2,1,0:T(8,128)(2,1)S(1)}, bf16[3,256,128]{2,1,0:T(8,128)(2,1)S(1)}, u32[]{:S(2)}, u32[]{:S(2)}) %collective-permute-start.51) | collective-permute-done | bytes 196640 | tf_op jit(solution)/shard_map/ppermute | solution.py:222
  169.8 3.3 %collective-permute-done.52.refs_4_.refs_5_ = bf16[3,256,128]{2,1,0:T(8,128)(2,1)S(1)} collective-permute-done((bf16[3,256,128]{2,1,0:T(8,128)(2,1)S(1)}, bf16[3,256,128]{2,1,0:T(8,128)(2,1)S(1)}, u32[]{:S(2)}, u32[]{:S(2)}) %collective-permute-start.52) | collective-permute-done | bytes 196640 | tf_op jit(solution)/shard_map/ppermute | solution.py:222
  173.1 4.9 %collective-permute-done.49.refs_1_.own2b = bf16[8,256,128]{2,1,0:T(8,128)(2,1)S(1)} collective-permute-done((bf16[8,256,128]{2,1,0:T(8,128)(2,1)S(1)}, bf16[8,256,128]{2,1,0:T(8,128)(2,1)S(1)}, u32[]{:S(2)}, u32[]{:S(2)}) %collective-permute-start.49) | collective-permute-done | bytes 524320 | tf_op jit(solution)/shard_map/ppermute | solution.py:218
  181.8 5.9 %collective-permute-done.55.refs_3_.refs_7_ = bf16[3,256,128]{2,1,0:T(8,128)(2,1)S(1)} collective-permute-done((bf16[3,256,128]{2,1,0:T(8,128)(2,1)S(1)}, bf16[3,256,128]{2,1,0:T(8,128)(2,1)S(1)}, u32[]{:S(2)}, u32[]{:S(2)}) %collective-permute-start.55) | collective-permute-done | bytes 196640 | tf_op jit(solution)/shard_map/ppermute | solution.py:222
  187.7 3.3 %collective-permute-done.56.refs_4_.refs_8_ = bf16[3,256,128]{2,1,0:T(8,128)(2,1)S(1)} collective-permute-done((bf16[3,256,128]{2,1,0:T(8,128)(2,1)S(1)}, bf16[3,256,128]{2,1,0:T(8,128)(2,1)S(1)}, u32[]{:S(2)}, u32[]{:S(2)}) %collective-permute-start.56) | collective-permute-done | bytes 196640 | tf_op jit(solution)/shard_map/ppermute | solution.py:222
  194.9 3.1 %shard_map.100.field = f32[9,256,128]{2,1,0:T(8,128)S(1)} custom-call(s32[181]{0:T(256)S(1)} %pad_add_fusion.2.table, bf16[48,256,256]{2,1,0:T(8,128)(2,1)S(1)} %bitcast.27, bf16[8,256,128]{2,1,0:T(8,128)(2,1)S(1)} %get-tuple-element.150.own0, bf16[8,256,128]{2,1,0:T(8,128)(2,1)S(1)} %collective-permute-done.43.refs_0_.own1, ...), custom_call_target="tpu_custom_call" | custom-call | flops 603979776 | bytes 7077888 | tf_op jit(solution)/shard_map/pallas_call | solution.py:137
  200.7 3.3 %collective-permute-done.59.pack3 = bf16[3,256,128]{2,1,0:T(8,128)(2,1)S(1)} collective-permute-done((bf16[3,256,128]{2,1,0:T(8,128)(2,1)S(1)}, bf16[3,256,128]{2,1,0:T(8,128)(2,1)S(1)}, u32[]{:S(2)}, u32[]{:S(2)}) %collective-permute-start.59) | collective-permute-done | bytes 196640 | tf_op jit(solution)/shard_map/ppermute | solution.py:222
  209.9 6.0 %collective-permute-done.63.refs_2_.refs_1_ = bf16[3,256,128]{2,1,0:T(8,128)(2,1)S(1)} collective-permute-done((bf16[3,256,128]{2,1,0:T(8,128)(2,1)S(1)}, bf16[3,256,128]{2,1,0:T(8,128)(2,1)S(1)}, u32[]{:S(2)}, u32[]{:S(2)}) %collective-permute-start.63) | collective-permute-done | bytes 196640 | tf_op jit(solution)/shard_map/ppermute | solution.py:222
  224.6 5.9 %collective-permute-done.68.refs_3_.refs_4_ = bf16[3,256,128]{2,1,0:T(8,128)(2,1)S(1)} collective-permute-done((bf16[3,256,128]{2,1,0:T(8,128)(2,1)S(1)}, bf16[3,256,128]{2,1,0:T(8,128)(2,1)S(1)}, u32[]{:S(2)}, u32[]{:S(2)}) %collective-permute-start.68) | collective-permute-done | bytes 196640 | tf_op jit(solution)/shard_map/ppermute | solution.py:222
  230.5 3.3 %collective-permute-done.69.refs_4_.refs_5_ = bf16[3,256,128]{2,1,0:T(8,128)(2,1)S(1)} collective-permute-done((bf16[3,256,128]{2,1,0:T(8,128)(2,1)S(1)}, bf16[3,256,128]{2,1,0:T(8,128)(2,1)S(1)}, u32[]{:S(2)}, u32[]{:S(2)}) %collective-permute-start.69) | collective-permute-done | bytes 196640 | tf_op jit(solution)/shard_map/ppermute | solution.py:222
  233.8 5.4 %collective-permute-done.66.refs_1_.own2b = bf16[8,256,128]{2,1,0:T(8,128)(2,1)S(1)} collective-permute-done((bf16[8,256,128]{2,1,0:T(8,128)(2,1)S(1)}, bf16[8,256,128]{2,1,0:T(8,128)(2,1)S(1)}, u32[]{:S(2)}, u32[]{:S(2)}) %collective-permute-start.66) | collective-permute-done | bytes 524320 | tf_op jit(solution)/shard_map/ppermute | solution.py:218
  243.1 5.9 %collective-permute-done.72.refs_3_.refs_7_ = bf16[3,256,128]{2,1,0:T(8,128)(2,1)S(1)} collective-permute-done((bf16[3,256,128]{2,1,0:T(8,128)(2,1)S(1)}, bf16[3,256,128]{2,1,0:T(8,128)(2,1)S(1)}, u32[]{:S(2)}, u32[]{:S(2)}) %collective-permute-start.72) | collective-permute-done | bytes 196640 | tf_op jit(solution)/shard_map/ppermute | solution.py:222
  248.9 3.3 %collective-permute-done.73.refs_4_.refs_8_ = bf16[3,256,128]{2,1,0:T(8,128)(2,1)S(1)} collective-permute-done((bf16[3,256,128]{2,1,0:T(8,128)(2,1)S(1)}, bf16[3,256,128]{2,1,0:T(8,128)(2,1)S(1)}, u32[]{:S(2)}, u32[]{:S(2)}) %collective-permute-start.73) | collective-permute-done | bytes 196640 | tf_op jit(solution)/shard_map/ppermute | solution.py:222
  256.4 3.1 %shard_map.105.field = f32[9,256,128]{2,1,0:T(8,128)S(1)} custom-call(s32[181]{0:T(256)S(1)} %pad_add_fusion.2.table, bf16[48,256,256]{2,1,0:T(8,128)(2,1)S(1)} %bitcast.27, bf16[8,256,128]{2,1,0:T(8,128)(2,1)S(1)} %get-tuple-element.175.own0, bf16[8,256,128]{2,1,0:T(8,128)(2,1)S(1)} %collective-permute-done.60.refs_0_.own1, ...), custom_call_target="tpu_custom_call" | custom-call | flops 603979776 | bytes 7077888 | tf_op jit(solution)/shard_map/pallas_call | solution.py:137
  262.2 3.3 %collective-permute-done.76.pack3 = bf16[3,256,128]{2,1,0:T(8,128)(2,1)S(1)} collective-permute-done((bf16[3,256,128]{2,1,0:T(8,128)(2,1)S(1)}, bf16[3,256,128]{2,1,0:T(8,128)(2,1)S(1)}, u32[]{:S(2)}, u32[]{:S(2)}) %collective-permute-start.76) | collective-permute-done | bytes 196640 | tf_op jit(solution)/shard_map/ppermute | solution.py:222
  265.5 3.1 %shard_map.106 = (f32[8,256,128]{2,1,0:T(8,128)}, f32[8,256,128]{2,1,0:T(8,128)}, f32[1,128]{1,0:T(1,128)S(1)}) custom-call(s32[181]{0:T(256)S(1)} %pad_add_fusion.2.table, f32[2]{0:T(128)S(1)} %pad_maximum_fusion.scalars, bf16[48,256,256]{2,1,0:T(8,128)(2,1)S(1)} %bitcast.27, bf16[8,256,128]{2,1,0:T(8,128)(2,1)S(1)} %collective-permute-done.65.refs_0_.own3a, ...), custom_call_target="tpu_custom_call" | custom-call | flops 201326592 | bytes 7602176 | tf_op jit(solution)/shard_map/pallas_call | solution.py:194
  (233 shorter events, 137.6 us)
Async XLA Ops:
  2.4 11.4 %collective-permute-start = (s32[16,3]{1,0:T(8,128)S(1)}, s32[16,3]{1,0:T(8,128)S(1)}, u32[]{:S(2)}, u32[]{:S(2)}) collective-permute-start(s32[16,3]{1,0:T(8,128)S(1)} %reshape.204), channel_id=1, source_target_pairs={{0,1},{1,0},{2,3},{3,2},{4,5},{5,4},{6,7},{7,6},{8,9},{9,8},{10,11... | collective-permute-start | bytes 584 | tf_op jit(solution)/shard_map/ppermute | solution.py:222
  2.9 11.0 %collective-permute-start.1 = (s32[16,3]{1,0:T(8,128)S(1)}, s32[16,3]{1,0:T(8,128)S(1)}, u32[]{:S(2)}, u32[]{:S(2)}) collective-permute-start(s32[16,3]{1,0:T(8,128)S(1)} %reshape.204), channel_id=1, source_target_pairs={{0,2},{1,3},{2,0},{3,1},{4,6},{5,7},{6,4},{7,5},{8,10},{9,11},{10,... | collective-permute-start | bytes 584 | tf_op jit(solution)/shard_map/ppermute | solution.py:222
  6.9 19.8 %collective-permute-start.10 = (bf16[8,256,128]{2,1,0:T(8,128)(2,1)S(1)}, bf16[8,256,128]{2,1,0:T(8,128)(2,1)S(1)}, u32[]{:S(2)}, u32[]{:S(2)}) collective-permute-start(bf16[8,256,128]{2,1,0:T(8,128)(2,1)S(1)} %convert_element_type.8.refs_0_.own0), channel_id=1, source_target_pairs={{4,8},{5,9},{6,10},{7,11},{8,4},{9,5},{10,6},{11,7},{20,24},{21,25... | collective-permute-start | bytes 1572872 | tf_op jit(solution)/shard_map/ppermute | solution.py:218
  7.6 19.1 %collective-permute-start.9 = (bf16[8,256,128]{2,1,0:T(8,128)(2,1)S(1)}, bf16[8,256,128]{2,1,0:T(8,128)(2,1)S(1)}, u32[]{:S(2)}, u32[]{:S(2)}) collective-permute-start(bf16[8,256,128]{2,1,0:T(8,128)(2,1)S(1)} %convert_element_type.8.refs_0_.own0), channel_id=1, source_target_pairs={{0,4},{1,5},{2,6},{3,7},{4,0},{5,1},{6,2},{7,3},{8,12},{9,13},{10,... | collective-permute-start | bytes 1572872 | tf_op jit(solution)/shard_map/ppermute | solution.py:218
  17.2 9.5 %collective-permute-start.13 = (bf16[3,256,128]{2,1,0:T(8,128)(2,1)S(1)}, bf16[3,256,128]{2,1,0:T(8,128)(2,1)S(1)}, u32[]{:S(2)}, u32[]{:S(2)}) collective-permute-start(bf16[3,256,128]{2,1,0:T(8,128)(2,1)S(1)} %get-tuple-element.105), channel_id=1, source_target_pairs={{0,3},{1,2},{2,1},{3,0},{4,7},{5,6},{6,5},{7,4},{8,11},{9,10},{10,... | collective-permute-start | bytes 589832 | tf_op jit(solution)/shard_map/ppermute | solution.py:222
  26.7 13.5 %collective-permute-start.14 = (bf16[8,256,128]{2,1,0:T(8,128)(2,1)S(1)}, bf16[8,256,128]{2,1,0:T(8,128)(2,1)S(1)}, u32[]{:S(2)}, u32[]{:S(2)}) collective-permute-start(bf16[8,256,128]{2,1,0:T(8,128)(2,1)S(1)} %collective-permute-done.9.refs_0_.own1), channel_id=1, source_target_pairs={{4,8},{5,9},{6,10},{7,11},{8,4},{9,5},{10,6},{11,7},{20,24},{21,25... | collective-permute-start | bytes 1572872 | tf_op jit(solution)/shard_map/ppermute | solution.py:218
  27.4 16.0 %collective-permute-start.15 = (bf16[8,256,128]{2,1,0:T(8,128)(2,1)S(1)}, bf16[8,256,128]{2,1,0:T(8,128)(2,1)S(1)}, u32[]{:S(2)}, u32[]{:S(2)}) collective-permute-start(bf16[8,256,128]{2,1,0:T(8,128)(2,1)S(1)} %collective-permute-done.10.refs_0_.own2a), channel_id=1, source_target_pairs={{4,0},{5,1},{6,2},{7,3},{8,12},{9,13},{10,14},{11,15},{20,16},{21,... | collective-permute-start | bytes 1572872 | tf_op jit(solution)/shard_map/ppermute | solution.py:218
  43.4 18.3 %collective-permute-start.19 = (bf16[8,256,128]{2,1,0:T(8,128)(2,1)S(1)}, bf16[8,256,128]{2,1,0:T(8,128)(2,1)S(1)}, u32[]{:S(2)}, u32[]{:S(2)}) collective-permute-start(bf16[8,256,128]{2,1,0:T(8,128)(2,1)S(1)} %collective-permute-done.14.refs_0_.own3a), channel_id=1, source_target_pairs={{4,0},{5,1},{6,2},{7,3},{8,12},{9,13},{10,14},{11,15},{20,16},{21,... | collective-permute-start | bytes 1572872 | tf_op jit(solution)/shard_map/ppermute | solution.py:218
  52.2 9.6 %collective-permute-start.22 = (bf16[3,256,128]{2,1,0:T(8,128)(2,1)S(1)}, bf16[3,256,128]{2,1,0:T(8,128)(2,1)S(1)}, u32[]{:S(2)}, u32[]{:S(2)}) collective-permute-start(bf16[3,256,128]{2,1,0:T(8,128)(2,1)S(1)} %get-tuple-element.121), channel_id=1, source_target_pairs={{0,3},{1,2},{2,1},{3,0},{4,7},{5,6},{6,5},{7,4},{8,11},{9,10},{10,... | collective-permute-start | bytes 589832 | tf_op jit(solution)/shard_map/ppermute | solution.py:222
  52.9 12.5 %collective-permute-start.6 = (f32[1,128]{1,0:T(1,128)S(1)}, f32[1,128]{1,0:T(1,128)S(1)}, u32[]{:S(2)}, u32[]{:S(2)}) collective-permute-start(f32[1,128]{1,0:T(1,128)S(1)} %add_add_fusion.1), channel_id=1, source_target_pairs={{0,4},{1,5},{2,6},{3,7},{4,0},{5,1},{6,2},{7,3},{8,12},{9,13},{10,... | collective-permute-start | bytes 1544 | tf_op jit(solution)/shard_map/ppermute | solution.py:222
  55.2 10.7 %collective-permute-start.7 = (f32[1,128]{1,0:T(1,128)S(1)}, f32[1,128]{1,0:T(1,128)S(1)}, u32[]{:S(2)}, u32[]{:S(2)}) collective-permute-start(f32[1,128]{1,0:T(1,128)S(1)} %add_add_fusion.1), channel_id=1, source_target_pairs={{0,8},{1,9},{2,10},{3,11},{4,12},{5,13},{6,14},{7,15},{8,0},{9,1},... | collective-permute-start | bytes 1544 | tf_op jit(solution)/shard_map/ppermute | solution.py:222
  63.9 15.7 %collective-permute-start.23 = (bf16[3,256,128]{2,1,0:T(8,128)(2,1)}, bf16[3,256,128]{2,1,0:T(8,128)(2,1)}, u32[]{:S(2)}, u32[]{:S(2)}) collective-permute-start(bf16[3,256,128]{2,1,0:T(8,128)(2,1)} %get-tuple-element.122), channel_id=1, source_target_pairs={{0,1},{1,0},{2,3},{3,2},{4,5},{5,4},{6,7},{7,6},{8,9},{9,8},{10,11... | collective-permute-start | bytes 589832 | tf_op jit(solution)/shard_map/ppermute | solution.py:222
  64.5 15.1 %collective-permute-start.24 = (bf16[3,256,128]{2,1,0:T(8,128)(2,1)}, bf16[3,256,128]{2,1,0:T(8,128)(2,1)}, u32[]{:S(2)}, u32[]{:S(2)}) collective-permute-start(bf16[3,256,128]{2,1,0:T(8,128)(2,1)} %get-tuple-element.123), channel_id=1, source_target_pairs={{0,2},{1,3},{2,0},{3,1},{4,6},{5,7},{6,4},{7,5},{8,10},{9,11},{10,... | collective-permute-start | bytes 589832 | tf_op jit(solution)/shard_map/ppermute | solution.py:222
  65.4 14.3 %collective-permute-start.25 = (bf16[3,256,128]{2,1,0:T(8,128)(2,1)}, bf16[3,256,128]{2,1,0:T(8,128)(2,1)}, u32[]{:S(2)}, u32[]{:S(2)}) collective-permute-start(bf16[3,256,128]{2,1,0:T(8,128)(2,1)} %get-tuple-element.124), channel_id=1, source_target_pairs={{0,3},{1,2},{2,1},{3,0},{4,7},{5,6},{6,5},{7,4},{8,11},{9,10},{10,... | collective-permute-start | bytes 589832 | tf_op jit(solution)/shard_map/ppermute | solution.py:222
  82.1 15.0 %collective-permute-start.26 = (bf16[8,256,128]{2,1,0:T(8,128)(2,1)S(1)}, bf16[8,256,128]{2,1,0:T(8,128)(2,1)S(1)}, u32[]{:S(2)}, u32[]{:S(2)}) collective-permute-start(bf16[8,256,128]{2,1,0:T(8,128)(2,1)S(1)} %get-tuple-element.125.own0), channel_id=1, source_target_pairs={{0,4},{1,5},{2,6},{3,7},{4,0},{5,1},{6,2},{7,3},{8,12},{9,13},{10,... | collective-permute-start | bytes 1572872 | tf_op jit(solution)/shard_map/ppermute | solution.py:218
  84.5 12.6 %collective-permute-start.27 = (bf16[8,256,128]{2,1,0:T(8,128)(2,1)S(1)}, bf16[8,256,128]{2,1,0:T(8,128)(2,1)S(1)}, u32[]{:S(2)}, u32[]{:S(2)}) collective-permute-start(bf16[8,256,128]{2,1,0:T(8,128)(2,1)S(1)} %get-tuple-element.125.own0), channel_id=1, source_target_pairs={{4,8},{5,9},{6,10},{7,11},{8,4},{9,5},{10,6},{11,7},{20,24},{21,25... | collective-permute-start | bytes 1572872 | tf_op jit(solution)/shard_map/ppermute | solution.py:218
  97.1 13.8 %collective-permute-start.31 = (bf16[8,256,128]{2,1,0:T(8,128)(2,1)S(1)}, bf16[8,256,128]{2,1,0:T(8,128)(2,1)S(1)}, u32[]{:S(2)}, u32[]{:S(2)}) collective-permute-start(bf16[8,256,128]{2,1,0:T(8,128)(2,1)S(1)} %collective-permute-done.26.refs_0_.own1), channel_id=1, source_target_pairs={{4,8},{5,9},{6,10},{7,11},{8,4},{9,5},{10,6},{11,7},{20,24},{21,25... | collective-permute-start | bytes 1572872 | tf_op jit(solution)/shard_map/ppermute | solution.py:218
  97.8 19.2 %collective-permute-start.32 = (bf16[8,256,128]{2,1,0:T(8,128)(2,1)S(1)}, bf16[8,256,128]{2,1,0:T(8,128)(2,1)S(1)}, u32[]{:S(2)}, u32[]{:S(2)}) collective-permute-start(bf16[8,256,128]{2,1,0:T(8,128)(2,1)S(1)} %collective-permute-done.27.refs_0_.own2a), channel_id=1, source_target_pairs={{4,0},{5,1},{6,2},{7,3},{8,12},{9,13},{10,14},{11,15},{20,16},{21,... | collective-permute-start | bytes 1572872 | tf_op jit(solution)/shard_map/ppermute | solution.py:218
  101.3 9.5 %collective-permute-start.35 = (bf16[3,256,128]{2,1,0:T(8,128)(2,1)S(1)}, bf16[3,256,128]{2,1,0:T(8,128)(2,1)S(1)}, u32[]{:S(2)}, u32[]{:S(2)}) collective-permute-start(bf16[3,256,128]{2,1,0:T(8,128)(2,1)S(1)} %get-tuple-element.136), channel_id=1, source_target_pairs={{0,3},{1,2},{2,1},{3,0},{4,7},{5,6},{6,5},{7,4},{8,11},{9,10},{10,... | collective-permute-start | bytes 589832 | tf_op jit(solution)/shard_map/ppermute | solution.py:222
  117.0 14.6 %collective-permute-start.36 = (bf16[8,256,128]{2,1,0:T(8,128)(2,1)S(1)}, bf16[8,256,128]{2,1,0:T(8,128)(2,1)S(1)}, u32[]{:S(2)}, u32[]{:S(2)}) collective-permute-start(bf16[8,256,128]{2,1,0:T(8,128)(2,1)S(1)} %collective-permute-done.31.refs_0_.own3a), channel_id=1, source_target_pairs={{4,0},{5,1},{6,2},{7,3},{8,12},{9,13},{10,14},{11,15},{20,16},{21,... | collective-permute-start | bytes 1572872 | tf_op jit(solution)/shard_map/ppermute | solution.py:218
  120.7 9.3 %collective-permute-start.39 = (bf16[3,256,128]{2,1,0:T(8,128)(2,1)S(1)}, bf16[3,256,128]{2,1,0:T(8,128)(2,1)S(1)}, u32[]{:S(2)}, u32[]{:S(2)}) collective-permute-start(bf16[3,256,128]{2,1,0:T(8,128)(2,1)S(1)} %get-tuple-element.144), channel_id=1, source_target_pairs={{0,3},{1,2},{2,1},{3,0},{4,7},{5,6},{6,5},{7,4},{8,11},{9,10},{10,... | collective-permute-start | bytes 589832 | tf_op jit(solution)/shard_map/ppermute | solution.py:222
  134.2 9.3 %collective-permute-start.42 = (bf16[3,256,128]{2,1,0:T(8,128)(2,1)S(1)}, bf16[3,256,128]{2,1,0:T(8,128)(2,1)S(1)}, u32[]{:S(2)}, u32[]{:S(2)}) collective-permute-start(bf16[3,256,128]{2,1,0:T(8,128)(2,1)S(1)} %get-tuple-element.147), channel_id=1, source_target_pairs={{0,3},{1,2},{2,1},{3,0},{4,7},{5,6},{6,5},{7,4},{8,11},{9,10},{10,... | collective-permute-start | bytes 589832 | tf_op jit(solution)/shard_map/ppermute | solution.py:222
  145.2 14.1 %collective-permute-start.43 = (bf16[8,256,128]{2,1,0:T(8,128)(2,1)S(1)}, bf16[8,256,128]{2,1,0:T(8,128)(2,1)S(1)}, u32[]{:S(2)}, u32[]{:S(2)}) collective-permute-start(bf16[8,256,128]{2,1,0:T(8,128)(2,1)S(1)} %get-tuple-element.150.own0), channel_id=1, source_target_pairs={{0,4},{1,5},{2,6},{3,7},{4,0},{5,1},{6,2},{7,3},{8,12},{9,13},{10,... | collective-permute-start | bytes 1572872 | tf_op jit(solution)/shard_map/ppermute | solution.py:218
  146.0 13.3 %collective-permute-start.44 = (bf16[8,256,128]{2,1,0:T(8,128)(2,1)S(1)}, bf16[8,256,128]{2,1,0:T(8,128)(2,1)S(1)}, u32[]{:S(2)}, u32[]{:S(2)}) collective-permute-start(bf16[8,256,128]{2,1,0:T(8,128)(2,1)S(1)} %get-tuple-element.150.own0), channel_id=1, source_target_pairs={{4,8},{5,9},{6,10},{7,11},{8,4},{9,5},{10,6},{11,7},{20,24},{21,25... | collective-permute-start | bytes 1572872 | tf_op jit(solution)/shard_map/ppermute | solution.py:218
  159.3 13.8 %collective-permute-start.48 = (bf16[8,256,128]{2,1,0:T(8,128)(2,1)S(1)}, bf16[8,256,128]{2,1,0:T(8,128)(2,1)S(1)}, u32[]{:S(2)}, u32[]{:S(2)}) collective-permute-start(bf16[8,256,128]{2,1,0:T(8,128)(2,1)S(1)} %collective-permute-done.43.refs_0_.own1), channel_id=1, source_target_pairs={{4,8},{5,9},{6,10},{7,11},{8,4},{9,5},{10,6},{11,7},{20,24},{21,25... | collective-permute-start | bytes 1572872 | tf_op jit(solution)/shard_map/ppermute | solution.py:218
  160.0 17.9 %collective-permute-start.49 = (bf16[8,256,128]{2,1,0:T(8,128)(2,1)S(1)}, bf16[8,256,128]{2,1,0:T(8,128)(2,1)S(1)}, u32[]{:S(2)}, u32[]{:S(2)}) collective-permute-start(bf16[8,256,128]{2,1,0:T(8,128)(2,1)S(1)} %collective-permute-done.44.refs_0_.own2a), channel_id=1, source_target_pairs={{4,0},{5,1},{6,2},{7,3},{8,12},{9,13},{10,14},{11,15},{20,16},{21,... | collective-permute-start | bytes 1572872 | tf_op jit(solution)/shard_map/ppermute | solution.py:218
  178.0 14.3 %collective-permute-start.53 = (bf16[8,256,128]{2,1,0:T(8,128)(2,1)S(1)}, bf16[8,256,128]{2,1,0:T(8,128)(2,1)S(1)}, u32[]{:S(2)}, u32[]{:S(2)}) collective-permute-start(bf16[8,256,128]{2,1,0:T(8,128)(2,1)S(1)} %collective-permute-done.48.refs_0_.own3a), channel_id=1, source_target_pairs={{4,0},{5,1},{6,2},{7,3},{8,12},{9,13},{10,14},{11,15},{20,16},{21,... | collective-permute-start | bytes 1572872 | tf_op jit(solution)/shard_map/ppermute | solution.py:218
  205.9 14.2 %collective-permute-start.60 = (bf16[8,256,128]{2,1,0:T(8,128)(2,1)S(1)}, bf16[8,256,128]{2,1,0:T(8,128)(2,1)S(1)}, u32[]{:S(2)}, u32[]{:S(2)}) collective-permute-start(bf16[8,256,128]{2,1,0:T(8,128)(2,1)S(1)} %get-tuple-element.175.own0), channel_id=1, source_target_pairs={{0,4},{1,5},{2,6},{3,7},{4,0},{5,1},{6,2},{7,3},{8,12},{9,13},{10,... | collective-permute-start | bytes 1572872 | tf_op jit(solution)/shard_map/ppermute | solution.py:218
  207.2 12.9 %collective-permute-start.61 = (bf16[8,256,128]{2,1,0:T(8,128)(2,1)S(1)}, bf16[8,256,128]{2,1,0:T(8,128)(2,1)S(1)}, u32[]{:S(2)}, u32[]{:S(2)}) collective-permute-start(bf16[8,256,128]{2,1,0:T(8,128)(2,1)S(1)} %get-tuple-element.175.own0), channel_id=1, source_target_pairs={{4,8},{5,9},{6,10},{7,11},{8,4},{9,5},{10,6},{11,7},{20,24},{21,25... | collective-permute-start | bytes 1572872 | tf_op jit(solution)/shard_map/ppermute | solution.py:218
  220.1 13.8 %collective-permute-start.65 = (bf16[8,256,128]{2,1,0:T(8,128)(2,1)S(1)}, bf16[8,256,128]{2,1,0:T(8,128)(2,1)S(1)}, u32[]{:S(2)}, u32[]{:S(2)}) collective-permute-start(bf16[8,256,128]{2,1,0:T(8,128)(2,1)S(1)} %collective-permute-done.60.refs_0_.own1), channel_id=1, source_target_pairs={{4,8},{5,9},{6,10},{7,11},{8,4},{9,5},{10,6},{11,7},{20,24},{21,25... | collective-permute-start | bytes 1572872 | tf_op jit(solution)/shard_map/ppermute | solution.py:218
  220.8 18.4 %collective-permute-start.66 = (bf16[8,256,128]{2,1,0:T(8,128)(2,1)S(1)}, bf16[8,256,128]{2,1,0:T(8,128)(2,1)S(1)}, u32[]{:S(2)}, u32[]{:S(2)}) collective-permute-start(bf16[8,256,128]{2,1,0:T(8,128)(2,1)S(1)} %collective-permute-done.61.refs_0_.own2a), channel_id=1, source_target_pairs={{4,0},{5,1},{6,2},{7,3},{8,12},{9,13},{10,14},{11,15},{20,16},{21,... | collective-permute-start | bytes 1572872 | tf_op jit(solution)/shard_map/ppermute | solution.py:218
  239.2 14.5 %collective-permute-start.70 = (bf16[8,256,128]{2,1,0:T(8,128)(2,1)S(1)}, bf16[8,256,128]{2,1,0:T(8,128)(2,1)S(1)}, u32[]{:S(2)}, u32[]{:S(2)}) collective-permute-start(bf16[8,256,128]{2,1,0:T(8,128)(2,1)S(1)} %collective-permute-done.65.refs_0_.own3a), channel_id=1, source_target_pairs={{4,0},{5,1},{6,2},{7,3},{8,12},{9,13},{10,14},{11,15},{20,16},{21,... | collective-permute-start | bytes 1572872 | tf_op jit(solution)/shard_map/ppermute | solution.py:218
  (71 other events, 490.6 us)

commit v5 on v4

v5 whole, which is shorter than its diff:
```python
import functools

import jax
import jax.numpy as jnp
from jax import lax
from jax.experimental import pallas as pl
from jax.experimental.pallas import tpu as pltpu
from jax.sharding import PartitionSpec as P

STEPS = 4
GROUP = 6
LIMIT = 16 * 2**20

SMEM = pl.BlockSpec(memory_space=pltpu.SMEM)
VMEM = pl.BlockSpec(memory_space=pltpu.VMEM)
ANY = pl.BlockSpec(memory_space=pl.ANY)


def params():
    return pltpu.CompilerParams(vmem_limit_bytes=LIMIT)


def squares_kernel(count, tiles, out):
    tile = tiles.shape[1]

    def add(s, acc):
        t = tiles[s].astype(jnp.float32)
        return acc + jnp.sum((t * t).reshape(tile // 8, 8, tile), axis=0)

    acc = lax.fori_loop(0, count[0], add, jnp.zeros((8, tile), jnp.float32))
    acc = jnp.sum(acc, axis=0, keepdims=True)
    out[...] = sum(acc[:, i : i + 128] for i in range(0, tile, 128))


def squares(count, tiles):
    return pl.pallas_call(
        squares_kernel,
        out_shape=jax.ShapeDtypeStruct((1, 128), jnp.float32),
        in_specs=[SMEM, VMEM],
        out_specs=VMEM,
        compiler_params=params(),
        cost_estimate=pl.CostEstimate(flops=2 * tiles.size, bytes_accessed=2 * tiles.size, transcendentals=0),
    )(count, tiles)


def update(pump, coeff, h, x, y):
    y = y + 0.5 * (-(x * x + pump) * x + coeff * h)
    return x + 0.5 * y, y


FIRST = ((0, 2), (3, 1), (1, 0), (2, 3))
SECOND = ((0, 1), (3, 2), (1, 3), (2, 0))
FROM_FIRST = (1, 3, 0, 2)
FROM_SECOND = (2, 0, 3, 1)


class Layout:
    def __init__(self, cap):
        self.cap = cap
        self.inner = 0
        self.packs = 1
        self.entries = 1 + 13 * cap

    def pack(self, j, flip):
        return self.packs + (j * 3 + flip - 1) * self.cap

    def pack_far(self, flip):
        return self.packs + (9 + flip) * self.cap

    def entry(self, i):
        return self.entries + 3 * i


EARLY = tuple((j, flip) for j in range(3) for flip in range(4))
LATE = tuple((3, flip) for flip in range(4))


def copy_blocks(table, at, cap, shard, out):
    for r in range(cap):
        out[r] = shard[table[at + r]]


def pack_shard_kernel(layout, table, shard, *refs):
    outs = refs[-3:]
    for flip in (1, 2, 3):
        copy_blocks(table, layout.pack(1, flip), layout.cap, shard, outs[flip - 1])


def pack_own_kernel(layout, table, shard, *refs):
    outs = refs[-3:]
    for flip in (1, 2, 3):
        copy_blocks(table, layout.pack(0, flip), layout.cap, shard, outs[flip - 1])


def pack_second_kernel(layout, table, first, second, *refs):
    here, far = refs[-7:-4], refs[-4:]
    for flip in (1, 2, 3):
        copy_blocks(table, layout.pack(2, flip), layout.cap, second, here[flip - 1])

    def send(shard):
        for flip in range(4):
            copy_blocks(table, layout.pack_far(flip), layout.cap, shard, far[flip])

    pl.when(table[layout.inner] == 1)(lambda: send(first))
    pl.when(table[layout.inner] == 0)(lambda: send(second))


def pack(kernel, layout, table, shards, sizes, after=()):
    _, tile, repl = shards[0].shape
    return pl.pallas_call(
        functools.partial(kernel, layout),
        out_shape=[jax.ShapeDtypeStruct((size, tile, repl), jnp.bfloat16) for size in sizes],
        in_specs=[SMEM] + [VMEM] * len(shards) + [ANY] * len(after),
        out_specs=[VMEM] * len(sizes),
        compiler_params=params(),
        cost_estimate=pl.CostEstimate(flops=0, bytes_accessed=0, transcendentals=0),
    )(table, *shards, *after)


def multiply(layout, table, tiles, xbuf, first, number, field):
    def some(start, place):
        prods = [
            jnp.dot(tiles[table[layout.entry(start + i)]], xbuf[place + i], preferred_element_type=jnp.float32)
            for i in range(GROUP)
        ]
        for i, prod in enumerate(prods):
            field[table[layout.entry(start + i) + 1]] += prod

    if number <= 3 * GROUP:
        for place in range(0, number, GROUP):
            some(first + place, place)
    else:

        @pl.loop(0, number // GROUP)
        def _(g):
            some(first + g * GROUP, g * GROUP)


def early_kernel(layout, table, tiles, *refs):
    sources, (field, xbuf) = refs[: len(EARLY)], refs[len(EARLY) :]
    cap = layout.cap
    for i, ((_, flip), source) in enumerate(zip(EARLY, sources)):
        for r in range(cap):
            e = i * cap + r
            xbuf[e] = source[table[layout.entry(e) + 2]] if flip == 0 else source[r]
    field[...] = jnp.zeros_like(field)
    multiply(layout, table, tiles, xbuf, 0, len(EARLY) * cap, field)


def cost(entries, tile, repl, more=0):
    return pl.CostEstimate(
        flops=2 * entries * tile * tile * repl,
        bytes_accessed=entries * tile * (tile + repl) * 2 + more,
        transcendentals=0,
    )


def early(layout, table, tiles, sources):
    tile = tiles.shape[1]
    blocks, _, repl = sources[0].shape
    entries = len(EARLY) * layout.cap
    return pl.pallas_call(
        functools.partial(early_kernel, layout),
        out_shape=jax.ShapeDtypeStruct((blocks + 1, tile, repl), jnp.float32),
        in_specs=[SMEM] + [VMEM] * (1 + len(sources)),
        out_specs=VMEM,
        scratch_shapes=[pltpu.VMEM((entries, tile, repl), jnp.bfloat16)],
        compiler_params=params(),
        cost_estimate=pl.CostEstimate(flops=0, bytes_accessed=0, transcendentals=0),
    )(table, tiles, *sources)


def late_kernel(layout, last, table, scalars, tiles, far0, far1, far2, far3, field, xpos, ymom, *refs):
    if last:
        xout, yout, energy, xbuf, acc = refs
    else:
        xout, yout, xb, out1, out2, out3, xbuf, acc = refs
    blocks = xpos.shape[0]
    cap = layout.cap
    for i, far in enumerate((far0, far1, far2, far3)):
        for r in range(cap):
            xbuf[i * cap + r] = far[r]
    acc[...] = field[...]
    multiply(layout, table, tiles, xbuf, len(EARLY) * cap, len(LATE) * cap, acc)
    total = jnp.zeros((1, xpos.shape[2]), jnp.float32)
    for b in range(blocks):
        x, h = xpos[b], acc[b]
        if last:
            total += jnp.sum(x * h, axis=0, keepdims=True)
        x, y = update(scalars[0], scalars[1], h, x, ymom[b])
        xout[b] = x
        yout[b] = y
        if not last:
            xb[b] = x.astype(jnp.bfloat16)
    if last:
        energy[...] = -0.5 * total
    else:
        for flip, out in ((1, out1), (2, out2), (3, out3)):
            copy_blocks(table, layout.pack(0, flip), cap, xb, out)


def late(layout, last, table, scalars, tiles, packs, field, xpos, ymom):
    tile = tiles.shape[1]
    blocks, _, repl = xpos.shape
    entries = len(LATE) * layout.cap
    state = jax.ShapeDtypeStruct(xpos.shape, jnp.float32)
    if last:
        extra = (jax.ShapeDtypeStruct((1, repl), jnp.float32),)
    else:
        out = jax.ShapeDtypeStruct((layout.cap, tile, repl), jnp.bfloat16)
        extra = (jax.ShapeDtypeStruct(xpos.shape, jnp.bfloat16), out, out, out)
    return pl.pallas_call(
        functools.partial(late_kernel, layout, last),
        out_shape=(state, state) + extra,
        in_specs=[SMEM, SMEM] + [VMEM] * (1 + len(packs) + 3),
        out_specs=(VMEM,) * (2 + len(extra)),
        scratch_shapes=[
            pltpu.VMEM((entries, tile, repl), jnp.bfloat16),
            pltpu.VMEM((blocks + 1, tile, repl), jnp.float32),
        ],
        compiler_params=params(),
        cost_estimate=cost(entries, tile, repl, 20 * xpos.size),
    )(table, scalars, tiles, *packs, field, xpos, ymom)


def along_z(pairs, value):
    return lax.ppermute(value, "row", [(a * 4 + i, b * 4 + i) for a, b in pairs for i in range(4)])


def across(flip, value):
    return lax.ppermute(value, "row", [(i, i ^ flip) for i in range(16)])


def row_sum(part):
    devices = lax.axis_size("row")
    spread = jnp.broadcast_to(part, (devices,) + part.shape[1:])
    return jnp.sum(lax.all_to_all(spread, "row", split_axis=0, concat_axis=0, tiled=True), axis=0, keepdims=True)


def make_table(layout, blocks, tile_rows, tile_cols, used):
    cap = layout.cap
    slots = tile_cols.shape[0]
    slot_ids = jnp.arange(slots)
    me = lax.axis_index("row")
    z, yc = me // 4, me % 4
    inner = (z == 1) | (z == 2)
    zs = jnp.stack([z, jnp.array(FROM_FIRST)[z], jnp.array(FROM_SECOND)[z], z ^ 3])
    source = tile_cols // blocks
    local = tile_cols % blocks
    same = (source[:, None] == source[None, :]) & used[None, :]
    rank = jnp.sum((same & (slot_ids[None, :] < slot_ids[:, None])).astype(jnp.int32), axis=1)
    key = jnp.where(used, source * cap + rank, -1)
    match = key[None, :] == jnp.arange(16 * cap)[:, None]

    def pick(values, default):
        found = jnp.sum(jnp.where(match, values[None, :] - default, 0), axis=1) + default
        return found.reshape(16, cap).astype(jnp.int32)

    wants = pick(local, 0)
    asked = jnp.stack([wants] + [across(flip, wants) for flip in (1, 2, 3)])
    asked_far = across(4, asked)
    packs = asked[1:, zs[:3] * 4 + yc].transpose(1, 0, 2)
    packs_far = asked_far[:, (z ^ 2) * 4 + yc]
    owner = jnp.stack([zs[j] * 4 + (yc ^ flip) for j, flip in EARLY + LATE])
    entries = jnp.stack([pick(slot_ids, 0), pick(tile_rows, blocks), wants], axis=-1)[owner]
    parts = (inner.astype(jnp.int32)[None], packs, packs_far, entries)
    return jnp.concatenate([part.reshape(-1) for part in parts])


def body_16(tiles, tile_rows, tile_cols, counts, positions, momenta):
    slots, tile, _ = tiles.shape
    repl = positions.shape[1]
    blocks = positions.shape[0] // tile
    cap = (slots + 15) // 16
    order = blocks * tile * 16
    layout = Layout(cap)
    used = jnp.arange(slots) < counts[0]
    xpos = positions.reshape(blocks, tile, repl)
    ymom = momenta.reshape(blocks, tile, repl)
    own0 = xpos.astype(jnp.bfloat16)
    table = make_table(layout, blocks, tile_rows, tile_cols, used)
    packs0 = None
    coeff = None
    for step in range(STEPS):
        last = step == STEPS - 1
        own1 = along_z(FIRST, own0)
        own2 = along_z(SECOND, own0)
        if step == 0:
            part = squares(counts, tiles)
            packs0 = pack(pack_own_kernel, layout, table, [own0], [cap] * 3, [part])
        got0 = [across(flip, packs0[flip - 1]) for flip in (1, 2, 3)]
        own1, got0 = lax.optimization_barrier((own1, got0))
        packs1 = pack(pack_shard_kernel, layout, table, [own1], [cap] * 3)
        got1 = [across(flip, packs1[flip - 1]) for flip in (1, 2, 3)]
        if step == 0:
            total = jnp.sum(row_sum(part))
            coeff = 0.7 * jnp.sqrt((order - 1) / total)
        own2, got1 = lax.optimization_barrier((own2, got1))
        packs2 = pack(pack_second_kernel, layout, table, [own1, own2], [cap] * 7)
        got2 = [across(flip, packs2[flip - 1]) for flip in (1, 2, 3)]
        far = [across(4 + flip, packs2[3 + flip]) for flip in range(4)]
        sources = [own0] + got0 + [own1] + got1 + [own2] + got2
        field = early(layout, table, tiles, sources)
        scalars = jnp.stack([jnp.float32(0.4 - 0.1 * step), coeff])
        outs = late(layout, last, table, scalars, tiles, far, field, xpos, ymom)
        xpos, ymom = outs[0], outs[1]
        if not last:
            own0, packs0 = outs[2], outs[3:]
    energy = row_sum(outs[2])
    return (xpos.reshape(positions.shape), ymom.reshape(momenta.shape), energy.reshape(repl))


def gathered_kernel(last, rows, cols, count, scalars, tiles, gathered, xpos, ymom, xout, yout, extra, xbuf, field, xsem):
    tile = xbuf.shape[1]
    used = count[0]

    def block_copy(s):
        return pltpu.make_async_copy(gathered.at[cols[s]], xbuf.at[s], xsem.at[s])

    @pl.loop(0, used)
    def _(s):
        block_copy(s).start()

    field[...] = jnp.zeros_like(field)

    @pl.loop(0, used)
    def _(s):
        block_copy(s).wait()
        here = pl.ds(pl.multiple_of(rows[s] * tile, tile), tile)
        field[here, :] += jnp.dot(tiles[s], xbuf[s], preferred_element_type=jnp.float32)

    x, h = xpos[...], field[...]
    if last:
        extra[...] = -0.5 * jnp.sum(x * h, axis=0, keepdims=True)
    x, y = update(scalars[0], scalars[1], h, x, ymom[...])
    xout[...] = x
    yout[...] = y
    if not last:
        extra[...] = x.astype(jnp.bfloat16)


def body_any(tiles, tile_rows, tile_cols, counts, positions, momenta):
    slots, tile, _ = tiles.shape
    order, repl = positions.shape
    devices = lax.axis_size("row")
    state = jax.ShapeDtypeStruct(positions.shape, jnp.float32)
    total = jnp.sum(lax.psum(squares(counts, tiles), "row"))
    coeff = 0.7 * jnp.sqrt((order * devices - 1) / total)
    xpos, ymom, extra = positions, momenta, positions.astype(jnp.bfloat16)
    for step in range(STEPS):
        last = step == STEPS - 1
        gathered = lax.all_gather(extra, "row", tiled=True).reshape(-1, tile, repl)
        scalars = jnp.stack([jnp.float32(0.4 - 0.1 * step), coeff])
        xpos, ymom, extra = pl.pallas_call(
            functools.partial(gathered_kernel, last),
            out_shape=(
                state,
                state,
                jax.ShapeDtypeStruct((1, repl), jnp.float32) if last else jax.ShapeDtypeStruct(state.shape, jnp.bfloat16),
            ),
            in_specs=[SMEM] * 4 + [VMEM, ANY, VMEM, VMEM],
            out_specs=(VMEM,) * 3,
            scratch_shapes=[
                pltpu.VMEM((slots, tile, repl), jnp.bfloat16),
                pltpu.VMEM(positions.shape, jnp.float32),
                pltpu.SemaphoreType.DMA((slots,)),
            ],
            compiler_params=params(),
        )(tile_rows, tile_cols, counts, scalars, tiles, gathered, xpos, ymom)
    return (xpos, ymom, lax.psum(extra, "row").reshape(repl))


def solution(mesh):
    in_specs = (
        P(("groups", "row"), None, None),
        P(("groups", "row")),
        P(("groups", "row")),
        P(("groups", "row")),
        P(("groups", "row"), None),
        P(("groups", "row"), None),
    )
    out_specs = (P(("groups", "row"), None), P(("groups", "row"), None), P("groups"))
    body = body_16 if mesh.shape["row"] == 16 else body_any
    return jax.shard_map(body, mesh=mesh, in_specs=in_specs, out_specs=out_specs, check_vma=False)
```

time: 282 us -> 262 us (0.929)
  waiting for transfers between devices: 157 us -> 127 us
  blocking collectives: 0 us -> 26 us
  starting transfers between devices: 71.9 us -> 60.2 us
  local copies, waits for them, and re-layouts: 15.1 us -> 10.7 us
    ppermute x63 -> x56, waiting for transfers between devices: 129 us -> 94.7 us  [across(): return lax.ppermute(value, 'row', [(i, i ^ flip) for i in range(16)])]
    all_to_all x0 -> x2, blocking collectives: none -> 26 us  [row_sum(): lax.all_to_all(spread, 'row', split_axis=0, concat_axis=0, tiled=True)]
    ppermute x20 -> x8, starting transfers between devices: 24.9 us -> 10.1 us  [along_z(): lax.ppermute(value, 'row', [(a * 4 + i, b * 4 + i) for a, b in pairs for...]
    unnamed x40 -> x20, local copies, waits for them, and re-layouts: 12.8 us -> 7.22 us
    ppermute x20 -> x8, waiting for transfers between devices: 27.8 us -> 32.2 us  [along_z(): lax.ppermute(value, 'row', [(a * 4 + i, b * 4 + i) for a, b in pairs for...]
    ppermute x63 -> x56, starting transfers between devices: 47 us -> 50.1 us  [across(): return lax.ppermute(value, 'row', [(i, i ^ flip) for i in range(16)])]
    pallas_call x13 -> x9, Pallas kernels: 8.66 us -> 6.51 us  [pack(): pl.pallas_call(functools.partial(kernel, layout), out_shape=[jax.ShapeDty...]
  transfers between devices with their start and end apart: 83 -> 64, of which waited for: 44 -> 30; matrix products, arithmetic and copies ran while one was open for 2% -> 3% of each run, Pallas kernels for 7% -> 6%
where the time goes in v5:
time: 262 us
  waiting for transfers between devices  127 us (48%)
  starting transfers between devices  60.2 us (23%)
  Pallas kernels  28.8 us (11%)
  blocking collectives  26 us (10%)
  local copies, waits for them, and re-layouts  10.7 us (4%)
  other arithmetic  5.31 us (2%)
  between operations  3.77 us (1%)
    ppermute x56, waiting for transfers between devices, across(): return lax.ppermute(value, 'row', [(i, i ^ flip) for i in range(16)])  94.7 us
    ppermute x56, starting transfers between devices, across(): return lax.ppermute(value, 'row', [(i, i ^ flip) for i in range(16)])  50.1 us
    ppermute x8, waiting for transfers between devices, along_z(): lax.ppermute(value, 'row', [(a * 4 + i, b * 4 + i) for a, b in pairs for...  32.2 us
    all_to_all x2, blocking collectives, row_sum(): lax.all_to_all(spread, 'row', split_axis=0, concat_axis=0, tiled=True)  26 us
    pallas_call x4, Pallas kernels, early(): pl.pallas_call(functools.partial(early_kernel, layout), out_shape=jax.Sha...  12.7 us
    ppermute x8, starting transfers between devices, along_z(): lax.ppermute(value, 'row', [(a * 4 + i, b * 4 + i) for a, b in pairs for...  10.1 us
    pallas_call x4, Pallas kernels, late(): pl.pallas_call(functools.partial(late_kernel, layout, last), out_shape=(s...  8.61 us
    unnamed x20, local copies, waits for them, and re-layouts  7.22 us
  transfers between devices with their start and end apart: 64, of which 30 were waited for; matrix products, arithmetic and copies ran while one was open for 3% of the time, Pallas kernels for 6%

profile of v5, /device:TPU:0, one launch (start us, length us, event | category | flops | bytes accessed | tf_op | source)
XLA Modules:
  0.0 261.7 jit_solution(2929052924661478769)
XLA Ops:
  6.9 2.8 %collective-permute-start.4 = (bf16[8,256,128]{2,1,0:T(8,128)(2,1)S(1)}, bf16[8,256,128]{2,1,0:T(8,128)(2,1)S(1)}, u32[]{:S(2)}, u32[]{:S(2)}) collective-permute-start(bf16[8,256,128]{2,1,0:T(8,128)(2,1)S(1)} %convert_element_type.8.shard.refs_0_), channel_id=1, source_target_pairs={{0,8},{1,9},{2,10},{3,11},{12,4},{13,5},{14,6},{15,7},{4,0},{5,1},... | collective-permute-start | bytes 1572872 | tf_op jit(solution)/shard_map/ppermute | solution.py:227
  17.2 2.8 %copy-done = bf16[48,256,256]{2,1,0:T(8,128)(2,1)S(1)} copy-done((bf16[48,256,256]{2,1,0:T(8,128)(2,1)S(1)}, bf16[48,256,256]{2,1,0:T(8,128)(2,1)}, u32[]{:S(2)}) %copy-start) | copy-done | bytes 6291480
  21.6 11.8 %collective-permute-done.3 = s32[4,16,3]{2,1,0:T(8,128)S(1)} collective-permute-done((s32[4,16,3]{2,1,0:T(8,128)S(1)}, s32[4,16,3]{2,1,0:T(8,128)S(1)}, u32[]{:S(2)}, u32[]{:S(2)}) %collective-permute-start.3) | collective-permute-done | bytes 800 | tf_op jit(solution)/shard_map/ppermute | solution.py:231
  36.2 5.9 %collective-permute-done.6.refs_2_ = bf16[3,256,128]{2,1,0:T(8,128)(2,1)S(1)} collective-permute-done((bf16[3,256,128]{2,1,0:T(8,128)(2,1)S(1)}, bf16[3,256,128]{2,1,0:T(8,128)(2,1)S(1)}, u32[]{:S(2)}, u32[]{:S(2)}) %collective-permute-start.6) | collective-permute-done | bytes 196640 | tf_op jit(solution)/shard_map/ppermute | solution.py:231
  42.1 3.3 %collective-permute-done.7.refs_3_ = bf16[3,256,128]{2,1,0:T(8,128)(2,1)S(1)} collective-permute-done((bf16[3,256,128]{2,1,0:T(8,128)(2,1)S(1)}, bf16[3,256,128]{2,1,0:T(8,128)(2,1)S(1)}, u32[]{:S(2)}, u32[]{:S(2)}) %collective-permute-start.7) | collective-permute-done | bytes 196640 | tf_op jit(solution)/shard_map/ppermute | solution.py:231
  48.2 5.6 %collective-permute-done.10.refs_6_ = bf16[3,256,128]{2,1,0:T(8,128)(2,1)S(1)} collective-permute-done((bf16[3,256,128]{2,1,0:T(8,128)(2,1)S(1)}, bf16[3,256,128]{2,1,0:T(8,128)(2,1)S(1)}, u32[]{:S(2)}, u32[]{:S(2)}) %collective-permute-start.10) | collective-permute-done | bytes 196640 | tf_op jit(solution)/shard_map/ppermute | solution.py:231
  53.8 2.9 %collective-permute-done.11.refs_7_ = bf16[3,256,128]{2,1,0:T(8,128)(2,1)S(1)} collective-permute-done((bf16[3,256,128]{2,1,0:T(8,128)(2,1)S(1)}, bf16[3,256,128]{2,1,0:T(8,128)(2,1)S(1)}, u32[]{:S(2)}, u32[]{:S(2)}) %collective-permute-start.11) | collective-permute-done | bytes 196640 | tf_op jit(solution)/shard_map/ppermute | solution.py:231
  68.5 14.9 %all_to_all.12 = f32[16,1,128]{2,1,0:T(1,128)S(1)} all-to-all(f32[16,1,128]{2,1,0:T(1,128)S(1)} %broadcast_in_dim.58), channel_id=1, replica_groups=mesh['groups'=2,'row'=16] {'row'}, dimensions={0} | all-to-all | bytes 16384 | tf_op jit(solution)/shard_map/all_to_all | solution.py:237
  84.8 2.8 %copy-done.1 = bf16[48,256,256]{2,1,0:T(8,128)(2,1)S(1)} copy-done((bf16[48,256,256]{2,1,0:T(8,128)(2,1)S(1)}, bf16[48,256,256]{2,1,0:T(8,128)(2,1)}, u32[]{:S(2)}) %copy-start.1) | copy-done | bytes 6291480
  88.6 3.5 %shard_map.107.field = f32[9,256,128]{2,1,0:T(8,128)S(1)} custom-call(s32[184]{0:T(256)S(1)} %pad_add_fusion.2.table, bf16[48,256,256]{2,1,0:T(8,128)(2,1)S(1)} %copy-done.1, bf16[8,256,128]{2,1,0:T(8,128)(2,1)S(1)} %convert_element_type.8.shard.refs_0_, bf16[3,256,128]{2,1,0:T(8,128)(2,1)S(1)} %collective-permute-done.5.refs_1_, ...), custom_call_target="tpu_custom_call" | custom-call | tf_op jit(solution)/shard_map/pallas_call | solution.py:162
  98.3 5.8 %collective-permute-done.21.refs_2_ = bf16[3,256,128]{2,1,0:T(8,128)(2,1)S(1)} collective-permute-done((bf16[3,256,128]{2,1,0:T(8,128)(2,1)S(1)}, bf16[3,256,128]{2,1,0:T(8,128)(2,1)S(1)}, u32[]{:S(2)}, u32[]{:S(2)}) %collective-permute-start.21) | collective-permute-done | bytes 196640 | tf_op jit(solution)/shard_map/ppermute | solution.py:231
  104.2 3.4 %collective-permute-done.22.refs_3_ = bf16[3,256,128]{2,1,0:T(8,128)(2,1)S(1)} collective-permute-done((bf16[3,256,128]{2,1,0:T(8,128)(2,1)S(1)}, bf16[3,256,128]{2,1,0:T(8,128)(2,1)S(1)}, u32[]{:S(2)}, u32[]{:S(2)}) %collective-permute-start.22) | collective-permute-done | bytes 196640 | tf_op jit(solution)/shard_map/ppermute | solution.py:231
  110.9 9.6 %collective-permute-done.23.second.refs_8_ = bf16[8,256,128]{2,1,0:T(8,128)(2,1)S(1)} collective-permute-done((bf16[8,256,128]{2,1,0:T(8,128)(2,1)S(1)}, bf16[8,256,128]{2,1,0:T(8,128)(2,1)S(1)}, u32[]{:S(2)}, u32[]{:S(2)}) %collective-permute-start.23) | collective-permute-done | bytes 524320 | tf_op jit(solution)/shard_map/ppermute | solution.py:227
  132.3 3.1 %shard_map.111.field = f32[9,256,128]{2,1,0:T(8,128)S(1)} custom-call(s32[184]{0:T(256)S(1)} %pad_add_fusion.2.table, bf16[48,256,256]{2,1,0:T(8,128)(2,1)S(1)} %bitcast.42, bf16[8,256,128]{2,1,0:T(8,128)(2,1)S(1)} %get-tuple-element.120.refs_0_, bf16[3,256,128]{2,1,0:T(8,128)(2,1)S(1)} %collective-permute-done.20.refs_1_, ...), custom_call_target="tpu_custom_call" | custom-call | tf_op jit(solution)/shard_map/pallas_call | solution.py:162
  135.4 3.9 %collective-permute-done.29.far2 = bf16[3,256,128]{2,1,0:T(8,128)(2,1)S(1)} collective-permute-done((bf16[3,256,128]{2,1,0:T(8,128)(2,1)S(1)}, bf16[3,256,128]{2,1,0:T(8,128)(2,1)S(1)}, u32[]{:S(2)}, u32[]{:S(2)}) %collective-permute-start.29) | collective-permute-done | bytes 196640 | tf_op jit(solution)/shard_map/ppermute | solution.py:231
  139.3 3.9 %collective-permute-done.30.far3 = bf16[3,256,128]{2,1,0:T(8,128)(2,1)S(1)} collective-permute-done((bf16[3,256,128]{2,1,0:T(8,128)(2,1)S(1)}, bf16[3,256,128]{2,1,0:T(8,128)(2,1)S(1)}, u32[]{:S(2)}, u32[]{:S(2)}) %collective-permute-start.30) | collective-permute-done | bytes 196640 | tf_op jit(solution)/shard_map/ppermute | solution.py:231
  149.3 5.8 %collective-permute-done.36.refs_2_ = bf16[3,256,128]{2,1,0:T(8,128)(2,1)S(1)} collective-permute-done((bf16[3,256,128]{2,1,0:T(8,128)(2,1)S(1)}, bf16[3,256,128]{2,1,0:T(8,128)(2,1)S(1)}, u32[]{:S(2)}, u32[]{:S(2)}) %collective-permute-start.36) | collective-permute-done | bytes 196640 | tf_op jit(solution)/shard_map/ppermute | solution.py:231
  155.2 3.4 %collective-permute-done.37.refs_3_ = bf16[3,256,128]{2,1,0:T(8,128)(2,1)S(1)} collective-permute-done((bf16[3,256,128]{2,1,0:T(8,128)(2,1)S(1)}, bf16[3,256,128]{2,1,0:T(8,128)(2,1)S(1)}, u32[]{:S(2)}, u32[]{:S(2)}) %collective-permute-start.37) | collective-permute-done | bytes 196640 | tf_op jit(solution)/shard_map/ppermute | solution.py:231
  162.3 9.8 %collective-permute-done.38.second.refs_8_ = bf16[8,256,128]{2,1,0:T(8,128)(2,1)S(1)} collective-permute-done((bf16[8,256,128]{2,1,0:T(8,128)(2,1)S(1)}, bf16[8,256,128]{2,1,0:T(8,128)(2,1)S(1)}, u32[]{:S(2)}, u32[]{:S(2)}) %collective-permute-start.38) | collective-permute-done | bytes 524320 | tf_op jit(solution)/shard_map/ppermute | solution.py:227
  176.8 2.7 %collective-permute-start.44 = (bf16[3,256,128]{2,1,0:T(8,128)(2,1)S(1)}, bf16[3,256,128]{2,1,0:T(8,128)(2,1)S(1)}, u32[]{:S(2)}, u32[]{:S(2)}) collective-permute-start(bf16[3,256,128]{2,1,0:T(8,128)(2,1)S(1)} %get-tuple-element.155), channel_id=1, source_target_pairs={{0,6},{1,7},{2,4},{3,5},{4,2},{5,3},{6,0},{7,1},{8,14},{9,15},{10,... | collective-permute-start | bytes 589832 | tf_op jit(solution)/shard_map/ppermute | solution.py:231
  183.9 3.1 %shard_map.115.field = f32[9,256,128]{2,1,0:T(8,128)S(1)} custom-call(s32[184]{0:T(256)S(1)} %pad_add_fusion.2.table, bf16[48,256,256]{2,1,0:T(8,128)(2,1)S(1)} %bitcast.42, bf16[8,256,128]{2,1,0:T(8,128)(2,1)S(1)} %get-tuple-element.144.refs_0_, bf16[3,256,128]{2,1,0:T(8,128)(2,1)S(1)} %collective-permute-done.35.refs_1_, ...), custom_call_target="tpu_custom_call" | custom-call | tf_op jit(solution)/shard_map/pallas_call | solution.py:162
  187.0 4.9 %collective-permute-done.44.far2 = bf16[3,256,128]{2,1,0:T(8,128)(2,1)S(1)} collective-permute-done((bf16[3,256,128]{2,1,0:T(8,128)(2,1)S(1)}, bf16[3,256,128]{2,1,0:T(8,128)(2,1)S(1)}, u32[]{:S(2)}, u32[]{:S(2)}) %collective-permute-start.44) | collective-permute-done | bytes 196640 | tf_op jit(solution)/shard_map/ppermute | solution.py:231
  191.9 3.6 %collective-permute-done.45.far3 = bf16[3,256,128]{2,1,0:T(8,128)(2,1)S(1)} collective-permute-done((bf16[3,256,128]{2,1,0:T(8,128)(2,1)S(1)}, bf16[3,256,128]{2,1,0:T(8,128)(2,1)S(1)}, u32[]{:S(2)}, u32[]{:S(2)}) %collective-permute-start.45) | collective-permute-done | bytes 196640 | tf_op jit(solution)/shard_map/ppermute | solution.py:231
  201.7 5.8 %collective-permute-done.51.refs_2_ = bf16[3,256,128]{2,1,0:T(8,128)(2,1)S(1)} collective-permute-done((bf16[3,256,128]{2,1,0:T(8,128)(2,1)S(1)}, bf16[3,256,128]{2,1,0:T(8,128)(2,1)S(1)}, u32[]{:S(2)}, u32[]{:S(2)}) %collective-permute-start.51) | collective-permute-done | bytes 196640 | tf_op jit(solution)/shard_map/ppermute | solution.py:231
  207.6 3.4 %collective-permute-done.52.refs_3_ = bf16[3,256,128]{2,1,0:T(8,128)(2,1)S(1)} collective-permute-done((bf16[3,256,128]{2,1,0:T(8,128)(2,1)S(1)}, bf16[3,256,128]{2,1,0:T(8,128)(2,1)S(1)}, u32[]{:S(2)}, u32[]{:S(2)}) %collective-permute-start.52) | collective-permute-done | bytes 196640 | tf_op jit(solution)/shard_map/ppermute | solution.py:231
  214.7 9.8 %collective-permute-done.53.second.refs_8_ = bf16[8,256,128]{2,1,0:T(8,128)(2,1)S(1)} collective-permute-done((bf16[8,256,128]{2,1,0:T(8,128)(2,1)S(1)}, bf16[8,256,128]{2,1,0:T(8,128)(2,1)S(1)}, u32[]{:S(2)}, u32[]{:S(2)}) %collective-permute-start.53) | collective-permute-done | bytes 524320 | tf_op jit(solution)/shard_map/ppermute | solution.py:227
  233.5 2.8 %collective-permute-done.63.refs_11_ = bf16[3,256,128]{2,1,0:T(8,128)(2,1)S(1)} collective-permute-done((bf16[3,256,128]{2,1,0:T(8,128)(2,1)S(1)}, bf16[3,256,128]{2,1,0:T(8,128)(2,1)S(1)}, u32[]{:S(2)}, u32[]{:S(2)}) %collective-permute-start.63) | collective-permute-done | bytes 196640 | tf_op jit(solution)/shard_map/ppermute | solution.py:231
  236.4 3.0 %shard_map.119.field = f32[9,256,128]{2,1,0:T(8,128)S(1)} custom-call(s32[184]{0:T(256)S(1)} %pad_add_fusion.2.table, bf16[48,256,256]{2,1,0:T(8,128)(2,1)S(1)} %bitcast.42, bf16[8,256,128]{2,1,0:T(8,128)(2,1)S(1)} %get-tuple-element.168.refs_0_, bf16[3,256,128]{2,1,0:T(8,128)(2,1)S(1)} %collective-permute-done.50.refs_1_, ...), custom_call_target="tpu_custom_call" | custom-call | tf_op jit(solution)/shard_map/pallas_call | solution.py:162
  239.4 3.8 %collective-permute-done.59.far2 = bf16[3,256,128]{2,1,0:T(8,128)(2,1)S(1)} collective-permute-done((bf16[3,256,128]{2,1,0:T(8,128)(2,1)S(1)}, bf16[3,256,128]{2,1,0:T(8,128)(2,1)S(1)}, u32[]{:S(2)}, u32[]{:S(2)}) %collective-permute-start.59) | collective-permute-done | bytes 196640 | tf_op jit(solution)/shard_map/ppermute | solution.py:231
  243.3 3.7 %collective-permute-done.60.far3 = bf16[3,256,128]{2,1,0:T(8,128)(2,1)S(1)} collective-permute-done((bf16[3,256,128]{2,1,0:T(8,128)(2,1)S(1)}, bf16[3,256,128]{2,1,0:T(8,128)(2,1)S(1)}, u32[]{:S(2)}, u32[]{:S(2)}) %collective-permute-start.60) | collective-permute-done | bytes 196640 | tf_op jit(solution)/shard_map/ppermute | solution.py:231
  247.0 3.1 %shard_map.120 = (f32[8,256,128]{2,1,0:T(8,128)}, f32[8,256,128]{2,1,0:T(8,128)}, f32[1,128]{1,0:T(1,128)S(1)}) custom-call(s32[184]{0:T(256)S(1)} %pad_add_fusion.2.table, f32[2]{0:T(128)S(1)} %pad_maximum_fusion.scalars, bf16[48,256,256]{2,1,0:T(8,128)(2,1)S(1)} %bitcast.42, bf16[3,256,128]{2,1,0:T(8,128)(2,1)S(1)} %collective-permute-done.57.far0, ...), custom_call_target="tpu_custom_call" | custom-call | flops 201326592 | bytes 7602176 | tf_op jit(solution)/shard_map/pallas_call | solution.py:212
  250.1 11.1 %all_to_all.13 = f32[16,1,128]{2,1,0:T(1,128)S(1)} all-to-all(f32[16,1,128]{2,1,0:T(1,128)S(1)} %broadcast_in_dim.59), channel_id=1, replica_groups=mesh['groups'=2,'row'=16] {'row'}, dimensions={0} | all-to-all | bytes 16384 | tf_op jit(solution)/shard_map/all_to_all | solution.py:237
  (173 shorter events, 91.8 us)
Async XLA Ops:
  2.4 12.7 %collective-permute-start = (s32[16,3]{1,0:T(8,128)S(1)}, s32[16,3]{1,0:T(8,128)S(1)}, u32[]{:S(2)}, u32[]{:S(2)}) collective-permute-start(s32[16,3]{1,0:T(8,128)S(1)} %reshape.738), channel_id=1, source_target_pairs={{0,1},{1,0},{2,3},{3,2},{4,5},{5,4},{6,7},{7,6},{8,9},{9,8},{10,11... | collective-permute-start | bytes 584 | tf_op jit(solution)/shard_map/ppermute | solution.py:231
  2.9 12.2 %collective-permute-start.1 = (s32[16,3]{1,0:T(8,128)S(1)}, s32[16,3]{1,0:T(8,128)S(1)}, u32[]{:S(2)}, u32[]{:S(2)}) collective-permute-start(s32[16,3]{1,0:T(8,128)S(1)} %reshape.738), channel_id=1, source_target_pairs={{0,2},{1,3},{2,0},{3,1},{4,6},{5,7},{6,4},{7,5},{8,10},{9,11},{10,... | collective-permute-start | bytes 584 | tf_op jit(solution)/shard_map/ppermute | solution.py:231
  6.9 38.5 %collective-permute-start.4 = (bf16[8,256,128]{2,1,0:T(8,128)(2,1)S(1)}, bf16[8,256,128]{2,1,0:T(8,128)(2,1)S(1)}, u32[]{:S(2)}, u32[]{:S(2)}) collective-permute-start(bf16[8,256,128]{2,1,0:T(8,128)(2,1)S(1)} %convert_element_type.8.shard.refs_0_), channel_id=1, source_target_pairs={{0,8},{1,9},{2,10},{3,11},{12,4},{13,5},{14,6},{15,7},{4,0},{5,1},... | collective-permute-start | bytes 1572872 | tf_op jit(solution)/shard_map/ppermute | solution.py:227
  9.8 38.4 %collective-permute-start.8 = (bf16[8,256,128]{2,1,0:T(8,128)(2,1)S(1)}, bf16[8,256,128]{2,1,0:T(8,128)(2,1)S(1)}, u32[]{:S(2)}, u32[]{:S(2)}) collective-permute-start(bf16[8,256,128]{2,1,0:T(8,128)(2,1)S(1)} %convert_element_type.8.shard.refs_0_), channel_id=1, source_target_pairs={{0,4},{1,5},{2,6},{3,7},{12,8},{13,9},{14,10},{15,11},{4,12},{5,13... | collective-permute-start | bytes 1572872 | tf_op jit(solution)/shard_map/ppermute | solution.py:227
  15.2 18.3 %collective-permute-start.3 = (s32[4,16,3]{2,1,0:T(8,128)S(1)}, s32[4,16,3]{2,1,0:T(8,128)S(1)}, u32[]{:S(2)}, u32[]{:S(2)}) collective-permute-start(s32[4,16,3]{2,1,0:T(8,128)S(1)} %pad_add_fusion), channel_id=1, source_target_pairs={{0,4},{1,5},{2,6},{3,7},{4,0},{5,1},{6,2},{7,3},{8,12},{9,13},{10,... | collective-permute-start | bytes 2312 | tf_op jit(solution)/shard_map/ppermute | solution.py:231
  60.3 24.6 %collective-permute-start.18 = (bf16[3,256,128]{2,1,0:T(8,128)(2,1)}, bf16[3,256,128]{2,1,0:T(8,128)(2,1)}, u32[]{:S(2)}, u32[]{:S(2)}) collective-permute-start(bf16[3,256,128]{2,1,0:T(8,128)(2,1)} %get-tuple-element.119), channel_id=1, source_target_pairs={{0,3},{1,2},{2,1},{3,0},{4,7},{5,6},{6,5},{7,4},{8,11},{9,10},{10,... | collective-permute-start | bytes 589832 | tf_op jit(solution)/shard_map/ppermute | solution.py:231
  60.3 31.8 %collective-permute-start.12 = (bf16[3,256,128]{2,1,0:T(8,128)(2,1)}, bf16[3,256,128]{2,1,0:T(8,128)(2,1)S(1)}, u32[]{:S(2)}, u32[]{:S(2)}) collective-permute-start(bf16[3,256,128]{2,1,0:T(8,128)(2,1)} %get-tuple-element.107), channel_id=1, source_target_pairs={{0,4},{1,5},{2,6},{3,7},{4,0},{5,1},{6,2},{7,3},{8,12},{9,13},{10,... | collective-permute-start | bytes 589832 | tf_op jit(solution)/shard_map/ppermute | solution.py:231
  62.8 29.3 %collective-permute-start.13 = (bf16[3,256,128]{2,1,0:T(8,128)(2,1)}, bf16[3,256,128]{2,1,0:T(8,128)(2,1)S(1)}, u32[]{:S(2)}, u32[]{:S(2)}) collective-permute-start(bf16[3,256,128]{2,1,0:T(8,128)(2,1)} %get-tuple-element.108), channel_id=1, source_target_pairs={{0,5},{1,4},{2,7},{3,6},{4,1},{5,0},{6,3},{7,2},{8,13},{9,12},{10,... | collective-permute-start | bytes 589832 | tf_op jit(solution)/shard_map/ppermute | solution.py:231
  63.0 29.1 %collective-permute-start.14 = (bf16[3,256,128]{2,1,0:T(8,128)(2,1)}, bf16[3,256,128]{2,1,0:T(8,128)(2,1)S(1)}, u32[]{:S(2)}, u32[]{:S(2)}) collective-permute-start(bf16[3,256,128]{2,1,0:T(8,128)(2,1)} %get-tuple-element.109), channel_id=1, source_target_pairs={{0,6},{1,7},{2,4},{3,5},{4,2},{5,3},{6,0},{7,1},{8,14},{9,15},{10,... | collective-permute-start | bytes 589832 | tf_op jit(solution)/shard_map/ppermute | solution.py:231
  67.2 24.9 %collective-permute-start.15 = (bf16[3,256,128]{2,1,0:T(8,128)(2,1)}, bf16[3,256,128]{2,1,0:T(8,128)(2,1)}, u32[]{:S(2)}, u32[]{:S(2)}) collective-permute-start(bf16[3,256,128]{2,1,0:T(8,128)(2,1)} %get-tuple-element.110), channel_id=1, source_target_pairs={{0,7},{1,6},{2,5},{3,4},{4,3},{5,2},{6,1},{7,0},{8,15},{9,14},{10,... | collective-permute-start | bytes 589832 | tf_op jit(solution)/shard_map/ppermute | solution.py:231
  94.4 13.9 %collective-permute-start.19 = (bf16[8,256,128]{2,1,0:T(8,128)(2,1)S(1)}, bf16[8,256,128]{2,1,0:T(8,128)(2,1)S(1)}, u32[]{:S(2)}, u32[]{:S(2)}) collective-permute-start(bf16[8,256,128]{2,1,0:T(8,128)(2,1)S(1)} %get-tuple-element.120.refs_0_), channel_id=1, source_target_pairs={{0,8},{1,9},{2,10},{3,11},{12,4},{13,5},{14,6},{15,7},{4,0},{5,1},... | collective-permute-start | bytes 1572872 | tf_op jit(solution)/shard_map/ppermute | solution.py:227
  96.0 24.5 %collective-permute-start.23 = (bf16[8,256,128]{2,1,0:T(8,128)(2,1)S(1)}, bf16[8,256,128]{2,1,0:T(8,128)(2,1)S(1)}, u32[]{:S(2)}, u32[]{:S(2)}) collective-permute-start(bf16[8,256,128]{2,1,0:T(8,128)(2,1)S(1)} %get-tuple-element.120.refs_0_), channel_id=1, source_target_pairs={{0,4},{1,5},{2,6},{3,7},{12,8},{13,9},{14,10},{15,11},{4,12},{5,13... | collective-permute-start | bytes 1572872 | tf_op jit(solution)/shard_map/ppermute | solution.py:227
  108.9 11.5 %collective-permute-start.24 = (bf16[3,256,128]{2,1,0:T(8,128)(2,1)S(1)}, bf16[3,256,128]{2,1,0:T(8,128)(2,1)S(1)}, u32[]{:S(2)}, u32[]{:S(2)}) collective-permute-start(bf16[3,256,128]{2,1,0:T(8,128)(2,1)S(1)} %get-tuple-element.125), channel_id=1, source_target_pairs={{0,1},{1,0},{2,3},{3,2},{4,5},{5,4},{6,7},{7,6},{8,9},{9,8},{10,11... | collective-permute-start | bytes 589832 | tf_op jit(solution)/shard_map/ppermute | solution.py:231
  109.0 11.5 %collective-permute-start.25 = (bf16[3,256,128]{2,1,0:T(8,128)(2,1)S(1)}, bf16[3,256,128]{2,1,0:T(8,128)(2,1)S(1)}, u32[]{:S(2)}, u32[]{:S(2)}) collective-permute-start(bf16[3,256,128]{2,1,0:T(8,128)(2,1)S(1)} %get-tuple-element.126), channel_id=1, source_target_pairs={{0,2},{1,3},{2,0},{3,1},{4,6},{5,7},{6,4},{7,5},{8,10},{9,11},{10,... | collective-permute-start | bytes 589832 | tf_op jit(solution)/shard_map/ppermute | solution.py:231
  123.1 12.3 %collective-permute-start.27 = (bf16[3,256,128]{2,1,0:T(8,128)(2,1)S(1)}, bf16[3,256,128]{2,1,0:T(8,128)(2,1)S(1)}, u32[]{:S(2)}, u32[]{:S(2)}) collective-permute-start(bf16[3,256,128]{2,1,0:T(8,128)(2,1)S(1)} %get-tuple-element.129), channel_id=1, source_target_pairs={{0,4},{1,5},{2,6},{3,7},{4,0},{5,1},{6,2},{7,3},{8,12},{9,13},{10,... | collective-permute-start | bytes 589832 | tf_op jit(solution)/shard_map/ppermute | solution.py:231
  125.4 13.9 %collective-permute-start.29 = (bf16[3,256,128]{2,1,0:T(8,128)(2,1)S(1)}, bf16[3,256,128]{2,1,0:T(8,128)(2,1)S(1)}, u32[]{:S(2)}, u32[]{:S(2)}) collective-permute-start(bf16[3,256,128]{2,1,0:T(8,128)(2,1)S(1)} %get-tuple-element.131), channel_id=1, source_target_pairs={{0,6},{1,7},{2,4},{3,5},{4,2},{5,3},{6,0},{7,1},{8,14},{9,15},{10,... | collective-permute-start | bytes 589832 | tf_op jit(solution)/shard_map/ppermute | solution.py:231
  129.0 14.2 %collective-permute-start.30 = (bf16[3,256,128]{2,1,0:T(8,128)(2,1)S(1)}, bf16[3,256,128]{2,1,0:T(8,128)(2,1)S(1)}, u32[]{:S(2)}, u32[]{:S(2)}) collective-permute-start(bf16[3,256,128]{2,1,0:T(8,128)(2,1)S(1)} %get-tuple-element.132), channel_id=1, source_target_pairs={{0,7},{1,6},{2,5},{3,4},{4,3},{5,2},{6,1},{7,0},{8,15},{9,14},{10,... | collective-permute-start | bytes 589832 | tf_op jit(solution)/shard_map/ppermute | solution.py:231
  144.9 14.9 %collective-permute-start.34 = (bf16[8,256,128]{2,1,0:T(8,128)(2,1)S(1)}, bf16[8,256,128]{2,1,0:T(8,128)(2,1)S(1)}, u32[]{:S(2)}, u32[]{:S(2)}) collective-permute-start(bf16[8,256,128]{2,1,0:T(8,128)(2,1)S(1)} %get-tuple-element.144.refs_0_), channel_id=1, source_target_pairs={{0,8},{1,9},{2,10},{3,11},{12,4},{13,5},{14,6},{15,7},{4,0},{5,1},... | collective-permute-start | bytes 1572872 | tf_op jit(solution)/shard_map/ppermute | solution.py:227
  147.5 24.6 %collective-permute-start.38 = (bf16[8,256,128]{2,1,0:T(8,128)(2,1)S(1)}, bf16[8,256,128]{2,1,0:T(8,128)(2,1)S(1)}, u32[]{:S(2)}, u32[]{:S(2)}) collective-permute-start(bf16[8,256,128]{2,1,0:T(8,128)(2,1)S(1)} %get-tuple-element.144.refs_0_), channel_id=1, source_target_pairs={{0,4},{1,5},{2,6},{3,7},{12,8},{13,9},{14,10},{15,11},{4,12},{5,13... | collective-permute-start | bytes 1572872 | tf_op jit(solution)/shard_map/ppermute | solution.py:227
  160.4 11.7 %collective-permute-start.39 = (bf16[3,256,128]{2,1,0:T(8,128)(2,1)S(1)}, bf16[3,256,128]{2,1,0:T(8,128)(2,1)S(1)}, u32[]{:S(2)}, u32[]{:S(2)}) collective-permute-start(bf16[3,256,128]{2,1,0:T(8,128)(2,1)S(1)} %get-tuple-element.149), channel_id=1, source_target_pairs={{0,1},{1,0},{2,3},{3,2},{4,5},{5,4},{6,7},{7,6},{8,9},{9,8},{10,11... | collective-permute-start | bytes 589832 | tf_op jit(solution)/shard_map/ppermute | solution.py:231
  160.5 11.6 %collective-permute-start.40 = (bf16[3,256,128]{2,1,0:T(8,128)(2,1)S(1)}, bf16[3,256,128]{2,1,0:T(8,128)(2,1)S(1)}, u32[]{:S(2)}, u32[]{:S(2)}) collective-permute-start(bf16[3,256,128]{2,1,0:T(8,128)(2,1)S(1)} %get-tuple-element.150), channel_id=1, source_target_pairs={{0,2},{1,3},{2,0},{3,1},{4,6},{5,7},{6,4},{7,5},{8,10},{9,11},{10,... | collective-permute-start | bytes 589832 | tf_op jit(solution)/shard_map/ppermute | solution.py:231
  174.7 12.3 %collective-permute-start.42 = (bf16[3,256,128]{2,1,0:T(8,128)(2,1)S(1)}, bf16[3,256,128]{2,1,0:T(8,128)(2,1)S(1)}, u32[]{:S(2)}, u32[]{:S(2)}) collective-permute-start(bf16[3,256,128]{2,1,0:T(8,128)(2,1)S(1)} %get-tuple-element.153), channel_id=1, source_target_pairs={{0,4},{1,5},{2,6},{3,7},{4,0},{5,1},{6,2},{7,3},{8,12},{9,13},{10,... | collective-permute-start | bytes 589832 | tf_op jit(solution)/shard_map/ppermute | solution.py:231
  176.8 15.1 %collective-permute-start.44 = (bf16[3,256,128]{2,1,0:T(8,128)(2,1)S(1)}, bf16[3,256,128]{2,1,0:T(8,128)(2,1)S(1)}, u32[]{:S(2)}, u32[]{:S(2)}) collective-permute-start(bf16[3,256,128]{2,1,0:T(8,128)(2,1)S(1)} %get-tuple-element.155), channel_id=1, source_target_pairs={{0,6},{1,7},{2,4},{3,5},{4,2},{5,3},{6,0},{7,1},{8,14},{9,15},{10,... | collective-permute-start | bytes 589832 | tf_op jit(solution)/shard_map/ppermute | solution.py:231
  180.6 14.9 %collective-permute-start.45 = (bf16[3,256,128]{2,1,0:T(8,128)(2,1)S(1)}, bf16[3,256,128]{2,1,0:T(8,128)(2,1)S(1)}, u32[]{:S(2)}, u32[]{:S(2)}) collective-permute-start(bf16[3,256,128]{2,1,0:T(8,128)(2,1)S(1)} %get-tuple-element.156), channel_id=1, source_target_pairs={{0,7},{1,6},{2,5},{3,4},{4,3},{5,2},{6,1},{7,0},{8,15},{9,14},{10,... | collective-permute-start | bytes 589832 | tf_op jit(solution)/shard_map/ppermute | solution.py:231
  197.2 15.0 %collective-permute-start.49 = (bf16[8,256,128]{2,1,0:T(8,128)(2,1)S(1)}, bf16[8,256,128]{2,1,0:T(8,128)(2,1)S(1)}, u32[]{:S(2)}, u32[]{:S(2)}) collective-permute-start(bf16[8,256,128]{2,1,0:T(8,128)(2,1)S(1)} %get-tuple-element.168.refs_0_), channel_id=1, source_target_pairs={{0,8},{1,9},{2,10},{3,11},{12,4},{13,5},{14,6},{15,7},{4,0},{5,1},... | collective-permute-start | bytes 1572872 | tf_op jit(solution)/shard_map/ppermute | solution.py:227
  199.9 24.7 %collective-permute-start.53 = (bf16[8,256,128]{2,1,0:T(8,128)(2,1)S(1)}, bf16[8,256,128]{2,1,0:T(8,128)(2,1)S(1)}, u32[]{:S(2)}, u32[]{:S(2)}) collective-permute-start(bf16[8,256,128]{2,1,0:T(8,128)(2,1)S(1)} %get-tuple-element.168.refs_0_), channel_id=1, source_target_pairs={{0,4},{1,5},{2,6},{3,7},{12,8},{13,9},{14,10},{15,11},{4,12},{5,13... | collective-permute-start | bytes 1572872 | tf_op jit(solution)/shard_map/ppermute | solution.py:227
  212.8 11.7 %collective-permute-start.54 = (bf16[3,256,128]{2,1,0:T(8,128)(2,1)S(1)}, bf16[3,256,128]{2,1,0:T(8,128)(2,1)S(1)}, u32[]{:S(2)}, u32[]{:S(2)}) collective-permute-start(bf16[3,256,128]{2,1,0:T(8,128)(2,1)S(1)} %get-tuple-element.173), channel_id=1, source_target_pairs={{0,1},{1,0},{2,3},{3,2},{4,5},{5,4},{6,7},{7,6},{8,9},{9,8},{10,11... | collective-permute-start | bytes 589832 | tf_op jit(solution)/shard_map/ppermute | solution.py:231
  212.9 11.7 %collective-permute-start.55 = (bf16[3,256,128]{2,1,0:T(8,128)(2,1)S(1)}, bf16[3,256,128]{2,1,0:T(8,128)(2,1)S(1)}, u32[]{:S(2)}, u32[]{:S(2)}) collective-permute-start(bf16[3,256,128]{2,1,0:T(8,128)(2,1)S(1)} %get-tuple-element.174), channel_id=1, source_target_pairs={{0,2},{1,3},{2,0},{3,1},{4,6},{5,7},{6,4},{7,5},{8,10},{9,11},{10,... | collective-permute-start | bytes 589832 | tf_op jit(solution)/shard_map/ppermute | solution.py:231
  213.5 11.0 %collective-permute-start.56 = (bf16[3,256,128]{2,1,0:T(8,128)(2,1)S(1)}, bf16[3,256,128]{2,1,0:T(8,128)(2,1)S(1)}, u32[]{:S(2)}, u32[]{:S(2)}) collective-permute-start(bf16[3,256,128]{2,1,0:T(8,128)(2,1)S(1)} %get-tuple-element.175), channel_id=1, source_target_pairs={{0,3},{1,2},{2,1},{3,0},{4,7},{5,6},{6,5},{7,4},{8,11},{9,10},{10,... | collective-permute-start | bytes 589832 | tf_op jit(solution)/shard_map/ppermute | solution.py:231
  227.2 12.3 %collective-permute-start.57 = (bf16[3,256,128]{2,1,0:T(8,128)(2,1)S(1)}, bf16[3,256,128]{2,1,0:T(8,128)(2,1)S(1)}, u32[]{:S(2)}, u32[]{:S(2)}) collective-permute-start(bf16[3,256,128]{2,1,0:T(8,128)(2,1)S(1)} %get-tuple-element.177), channel_id=1, source_target_pairs={{0,4},{1,5},{2,6},{3,7},{4,0},{5,1},{6,2},{7,3},{8,12},{9,13},{10,... | collective-permute-start | bytes 589832 | tf_op jit(solution)/shard_map/ppermute | solution.py:231
  229.3 14.0 %collective-permute-start.59 = (bf16[3,256,128]{2,1,0:T(8,128)(2,1)S(1)}, bf16[3,256,128]{2,1,0:T(8,128)(2,1)S(1)}, u32[]{:S(2)}, u32[]{:S(2)}) collective-permute-start(bf16[3,256,128]{2,1,0:T(8,128)(2,1)S(1)} %get-tuple-element.179), channel_id=1, source_target_pairs={{0,6},{1,7},{2,4},{3,5},{4,2},{5,3},{6,0},{7,1},{8,14},{9,15},{10,... | collective-permute-start | bytes 589832 | tf_op jit(solution)/shard_map/ppermute | solution.py:231
  233.1 13.9 %collective-permute-start.60 = (bf16[3,256,128]{2,1,0:T(8,128)(2,1)S(1)}, bf16[3,256,128]{2,1,0:T(8,128)(2,1)S(1)}, u32[]{:S(2)}, u32[]{:S(2)}) collective-permute-start(bf16[3,256,128]{2,1,0:T(8,128)(2,1)S(1)} %get-tuple-element.180), channel_id=1, source_target_pairs={{0,7},{1,6},{2,5},{3,4},{4,3},{5,2},{6,1},{7,0},{8,15},{9,14},{10,... | collective-permute-start | bytes 589832 | tf_op jit(solution)/shard_map/ppermute | solution.py:231
  (42 other events, 358.4 us)

commit v6 on v5

--- a/solution.py
+++ b/solution.py
@@ -50,29 +50,96 @@
 
 FIRST = ((0, 2), (3, 1), (1, 0), (2, 3))
 SECOND = ((0, 1), (3, 2), (1, 3), (2, 0))
-FROM_FIRST = (1, 3, 0, 2)
-FROM_SECOND = (2, 0, 3, 1)
 
 
 class Layout:
     def __init__(self, cap):
         self.cap = cap
-        self.inner = 0
-        self.packs = 1
-        self.entries = 1 + 13 * cap
+        self.packs = 0
+        self.entries = 9 * cap
+        self.size = 9 * cap + 3 * 16 * cap
 
     def pack(self, j, flip):
         return self.packs + (j * 3 + flip - 1) * self.cap
 
-    def pack_far(self, flip):
-        return self.packs + (9 + flip) * self.cap
-
     def entry(self, i):
         return self.entries + 3 * i
 
 
+def whereabouts():
+    me = lax.axis_index("row")
+    z, yc = lax.div(me, 4), lax.rem(me, 4)
+    inner = (z == 1) | (z == 2)
+    near, skip = z ^ 1, z ^ 2
+    return z, yc, inner, (z, jnp.where(inner, skip, near), jnp.where(inner, near, skip), z ^ 3)
+
+
 EARLY = tuple((j, flip) for j in range(3) for flip in range(4))
 LATE = tuple((3, flip) for flip in range(4))
+
+
+def plan_kernel(layout, blocks, rows, cols, count, wants, mine, seen):
+    cap = layout.cap
+    keys = 16 * cap
+
+    @pl.loop(0, 16)
+    def _(d):
+        seen[d] = 0
+
+    @pl.loop(0, keys)
+    def _(k):
+        wants[k] = 0
+        mine[k] = 0
+        mine[keys + k] = blocks
+
+    @pl.loop(0, count[0])
+    def _(s):
+        source = lax.div(cols[s], blocks)
+        rank = seen[source]
+        seen[source] = rank + 1
+        key = source * cap + jnp.minimum(rank, cap - 1)
+        wants[key] = lax.rem(cols[s], blocks)
+        mine[key] = s
+        mine[keys + key] = rows[s]
+
+
+def plan(layout, blocks, rows, cols, count):
+    keys = 16 * layout.cap
+    return pl.pallas_call(
+        functools.partial(plan_kernel, layout, blocks),
+        out_shape=(jax.ShapeDtypeStruct((keys,), jnp.int32), jax.ShapeDtypeStruct((2 * keys,), jnp.int32)),
+        in_specs=[SMEM] * 3,
+        out_specs=(SMEM, SMEM),
+        scratch_shapes=[pltpu.SMEM((16,), jnp.int32)],
+        cost_estimate=pl.CostEstimate(flops=0, bytes_accessed=0, transcendentals=0),
+    )(rows, cols, count)
+
+
+def table_kernel(layout, wants, mine, near1, near2, near3, table):
+    cap = layout.cap
+    keys = 16 * cap
+    _, yc, _, zs = whereabouts()
+    for j in range(3):
+        for flip, asked in ((1, near1), (2, near2), (3, near3)):
+            for r in range(cap):
+                table[layout.pack(j, flip) + r] = asked[(zs[j] * 4 + yc) * cap + r]
+    for i, (j, flip) in enumerate(EARLY + LATE):
+        for r in range(cap):
+            key = (zs[j] * 4 + (yc ^ flip)) * cap + r
+            at = layout.entry(i * cap + r)
+            table[at] = mine[key]
+            table[at + 1] = mine[keys + key]
+            table[at + 2] = wants[key]
+
+
+def make_table(layout, wants, mine, near):
+    return pl.pallas_call(
+        functools.partial(table_kernel, layout),
+        out_shape=jax.ShapeDtypeStruct((layout.size,), jnp.int32),
+        in_specs=[SMEM] * 5,
+        out_specs=SMEM,
+        cost_estimate=pl.CostEstimate(flops=0, bytes_accessed=0, transcendentals=0),
+    )(wants, mine, *near)
 
 
 def copy_blocks(table, at, cap, shard, out):
@@ -80,41 +147,37 @@
         out[r] = shard[table[at + r]]
 
 
-def pack_shard_kernel(layout, table, shard, *refs):
+def pack_shard_kernel(layout, j, table, shard, *refs):
     outs = refs[-3:]
     for flip in (1, 2, 3):
-        copy_blocks(table, layout.pack(1, flip), layout.cap, shard, outs[flip - 1])
-
-
-def pack_own_kernel(layout, table, shard, *refs):
-    outs = refs[-3:]
+        copy_blocks(table, layout.pack(j, flip), layout.cap, shard, outs[flip - 1])
+
+
+def pack_second_kernel(layout, table, asked, first, second, *refs):
+    here, far = refs[-7:-4], refs[-4:]
+    cap = layout.cap
+    z, yc, inner, _ = whereabouts()
     for flip in (1, 2, 3):
-        copy_blocks(table, layout.pack(0, flip), layout.cap, shard, outs[flip - 1])
-
-
-def pack_second_kernel(layout, table, first, second, *refs):
-    here, far = refs[-7:-4], refs[-4:]
-    for flip in (1, 2, 3):
-        copy_blocks(table, layout.pack(2, flip), layout.cap, second, here[flip - 1])
+        copy_blocks(table, layout.pack(2, flip), cap, second, here[flip - 1])
 
     def send(shard):
         for flip in range(4):
-            copy_blocks(table, layout.pack_far(flip), layout.cap, shard, far[flip])
-
-    pl.when(table[layout.inner] == 1)(lambda: send(first))
-    pl.when(table[layout.inner] == 0)(lambda: send(second))
-
-
-def pack(kernel, layout, table, shards, sizes, after=()):
+            copy_blocks(asked, (flip * 16 + (z ^ 2) * 4 + yc) * cap, cap, shard, far[flip])
+
+    pl.when(inner)(lambda: send(first))
+    pl.when(jnp.logical_not(inner))(lambda: send(second))
+
+
+def pack(kernel, cap, number, tables, shards, after=()):
     _, tile, repl = shards[0].shape
     return pl.pallas_call(
-        functools.partial(kernel, layout),
-        out_shape=[jax.ShapeDtypeStruct((size, tile, repl), jnp.bfloat16) for size in sizes],
-        in_specs=[SMEM] + [VMEM] * len(shards) + [ANY] * len(after),
-        out_specs=[VMEM] * len(sizes),
+        kernel,
+        out_shape=[jax.ShapeDtypeStruct((cap, tile, repl), jnp.bfloat16)] * number,
+        in_specs=[SMEM] * len(tables) + [VMEM] * len(shards) + [ANY] * len(after),
+        out_specs=[VMEM] * number,
         compiler_params=params(),
         cost_estimate=pl.CostEstimate(flops=0, bytes_accessed=0, transcendentals=0),
-    )(table, *shards, *after)
+    )(*tables, *shards, *after)
 
 
 def multiply(layout, table, tiles, xbuf, first, number, field):
@@ -237,36 +300,6 @@
     return jnp.sum(lax.all_to_all(spread, "row", split_axis=0, concat_axis=0, tiled=True), axis=0, keepdims=True)
 
 
-def make_table(layout, blocks, tile_rows, tile_cols, used):
-    cap = layout.cap
-    slots = tile_cols.shape[0]
-    slot_ids = jnp.arange(slots)
-    me = lax.axis_index("row")
-    z, yc = me // 4, me % 4
-    inner = (z == 1) | (z == 2)
-    zs = jnp.stack([z, jnp.array(FROM_FIRST)[z], jnp.array(FROM_SECOND)[z], z ^ 3])
-    source = tile_cols // blocks
-    local = tile_cols % blocks
-    same = (source[:, None] == source[None, :]) & used[None, :]
-    rank = jnp.sum((same & (slot_ids[None, :] < slot_ids[:, None])).astype(jnp.int32), axis=1)
-    key = jnp.where(used, source * cap + rank, -1)
-    match = key[None, :] == jnp.arange(16 * cap)[:, None]
-
-    def pick(values, default):
-        found = jnp.sum(jnp.where(match, values[None, :] - default, 0), axis=1) + default
-        return found.reshape(16, cap).astype(jnp.int32)
-
-    wants = pick(local, 0)
-    asked = jnp.stack([wants] + [across(flip, wants) for flip in (1, 2, 3)])
-    asked_far = across(4, asked)
-    packs = asked[1:, zs[:3] * 4 + yc].transpose(1, 0, 2)
-    packs_far = asked_far[:, (z ^ 2) * 4 + yc]
-    owner = jnp.stack([zs[j] * 4 + (yc ^ flip) for j, flip in EARLY + LATE])
-    entries = jnp.stack([pick(slot_ids, 0), pick(tile_rows, blocks), wants], axis=-1)[owner]
-    parts = (inner.astype(jnp.int32)[None], packs, packs_far, entries)
-    return jnp.concatenate([part.reshape(-1) for part in parts])
-
-
 def body_16(tiles, tile_rows, tile_cols, counts, positions, momenta):
     slots, tile, _ = tiles.shape
     repl = positions.shape[1]
@@ -274,29 +307,36 @@
     cap = (slots + 15) // 16
     order = blocks * tile * 16
     layout = Layout(cap)
-    used = jnp.arange(slots) < counts[0]
+    pack_own = functools.partial(pack_shard_kernel, layout, 0)
+    pack_first = functools.partial(pack_shard_kernel, layout, 1)
+    pack_second = functools.partial(pack_second_kernel, layout)
     xpos = positions.reshape(blocks, tile, repl)
     ymom = momenta.reshape(blocks, tile, repl)
     own0 = xpos.astype(jnp.bfloat16)
-    table = make_table(layout, blocks, tile_rows, tile_cols, used)
-    packs0 = None
-    coeff = None
+    wants, mine = plan(layout, blocks, tile_rows, tile_cols, counts)
+    near = [across(flip, wants) for flip in (1, 2, 3)]
+    table = make_table(layout, wants, mine, near)
+    packs0 = pack(pack_own, cap, 3, [table], [own0])
+    asked = coeff = None
     for step in range(STEPS):
         last = step == STEPS - 1
         own1 = along_z(FIRST, own0)
         own2 = along_z(SECOND, own0)
+        got0 = [across(flip, packs0[flip - 1]) for flip in (1, 2, 3)]
+        after = []
         if step == 0:
             part = squares(counts, tiles)
-            packs0 = pack(pack_own_kernel, layout, table, [own0], [cap] * 3, [part])
-        got0 = [across(flip, packs0[flip - 1]) for flip in (1, 2, 3)]
+            after = [part]
+            near, got0 = lax.optimization_barrier((near, got0))
+            asked = across(4, jnp.concatenate([wants] + near))
         own1, got0 = lax.optimization_barrier((own1, got0))
-        packs1 = pack(pack_shard_kernel, layout, table, [own1], [cap] * 3)
+        packs1 = pack(pack_first, cap, 3, [table], [own1], after)
         got1 = [across(flip, packs1[flip - 1]) for flip in (1, 2, 3)]
         if step == 0:
-            total = jnp.sum(row_sum(part))
+            total = jnp.sum(lax.all_gather(part, "row"))
             coeff = 0.7 * jnp.sqrt((order - 1) / total)
         own2, got1 = lax.optimization_barrier((own2, got1))
-        packs2 = pack(pack_second_kernel, layout, table, [own1, own2], [cap] * 7)
+        packs2 = pack(pack_second, cap, 7, [table, asked], [own1, own2])
         got2 = [across(flip, packs2[flip - 1]) for flip in (1, 2, 3)]
         far = [across(4 + flip, packs2[3 + flip]) for flip in range(4)]
         sources = [own0] + got0 + [own1] + got1 + [own2] + got2

time: 262 us -> 266 us (1.015)
  blocking collectives: 26 us -> 37.8 us
  starting transfers between devices: 60.2 us -> 54.9 us
  Pallas kernels: 28.8 us -> 32.3 us
    all_gather x0 -> x1, blocking collectives: none -> 27.3 us  [body_16(): total = jnp.sum(lax.all_gather(part, 'row'))]
    all_to_all x2 -> x1, blocking collectives: 26 us -> 10.5 us  [row_sum(): lax.all_to_all(spread, 'row', split_axis=0, concat_axis=0, tiled=True)]
    ppermute x56, starting transfers between devices: 50.1 us -> 44.6 us  [across(): return lax.ppermute(value, 'row', [(i, i ^ flip) for i in range(16)])]
    pallas_call x9 -> x11, Pallas kernels: 6.51 us -> 10.3 us  [the longest x9 6.73 us: pack(): pl.pallas_call(kernel, out_shape=[jax.ShapeDtypeStruct((cap, tile, repl),...]
    unnamed x20 -> x34, local copies, waits for them, and re-layouts: 7.22 us -> 8.39 us
  transfers between devices with their start and end apart: 64 -> 64, of which waited for: 30 -> 33; matrix products, arithmetic and copies ran while one was open for 3% -> 0% of each run, Pallas kernels for 6% -> 8%
where the time goes in v6:
time: 266 us; the launch traced here: 265 us
  waiting for transfers between devices  126 us (47%)
  starting transfers between devices  54.9 us (21%)
  blocking collectives  37.8 us (14%)
  Pallas kernels  32.3 us (12%)
  local copies, waits for them, and re-layouts  8.4 us (3%)
  other arithmetic  2.83 us (1%)
    ppermute x56, waiting for transfers between devices, across(): return lax.ppermute(value, 'row', [(i, i ^ flip) for i in range(16)])  93.1 us
    ppermute x56, starting transfers between devices, across(): return lax.ppermute(value, 'row', [(i, i ^ flip) for i in range(16)])  44.6 us
    ppermute x8, waiting for transfers between devices, along_z(): lax.ppermute(value, 'row', [(a * 4 + i, b * 4 + i) for a, b in pairs for...  33.4 us
    all_gather x1, blocking collectives, body_16(): total = jnp.sum(lax.all_gather(part, 'row'))  27.3 us
    pallas_call x4, Pallas kernels, early(): pl.pallas_call(functools.partial(early_kernel, layout), out_shape=jax.Sha...  12.7 us
    all_to_all x1, blocking collectives, row_sum(): lax.all_to_all(spread, 'row', split_axis=0, concat_axis=0, tiled=True)  10.5 us
    ppermute x8, starting transfers between devices, along_z(): lax.ppermute(value, 'row', [(a * 4 + i, b * 4 + i) for a, b in pairs for...  10.3 us
    pallas_call x4, Pallas kernels, late(): pl.pallas_call(functools.partial(late_kernel, layout, last), out_shape=(s...  8.61 us
  transfers between devices with their start and end apart: 64, of which 33 were waited for; matrix products, arithmetic and copies ran while one was open for 0% of the time, Pallas kernels for 8%

profile of v6, /device:TPU:0, one launch (start us, length us, event | category | flops | bytes accessed | tf_op | source)
XLA Modules:
  0.0 265.1 jit_solution(2689358548159281602)
XLA Ops:
  1.9 4.1 %collective-permute-start.7 = (bf16[8,256,128]{2,1,0:T(8,128)(2,1)S(1)}, bf16[8,256,128]{2,1,0:T(8,128)(2,1)S(1)}, u32[]{:S(2)}, u32[]{:S(2)}) collective-permute-start(bf16[8,256,128]{2,1,0:T(8,128)(2,1)S(1)} %convert_element_type.3.shard.refs_0_), channel_id=1, source_target_pairs={{0,8},{1,9},{2,10},{3,11},{12,4},{13,5},{14,6},{15,7},{4,0},{5,1},... | collective-permute-start | bytes 1572872 | tf_op jit(solution)/shard_map/ppermute | solution.py:290
  18.5 2.8 %copy-done = bf16[48,256,256]{2,1,0:T(8,128)(2,1)S(1)} copy-done((bf16[48,256,256]{2,1,0:T(8,128)(2,1)S(1)}, bf16[48,256,256]{2,1,0:T(8,128)(2,1)}, u32[]{:S(2)}) %copy-start) | copy-done | bytes 6291480
  21.9 2.9 %collective-permute-done.4.refs_2_ = bf16[3,256,128]{2,1,0:T(8,128)(2,1)S(1)} collective-permute-done((bf16[3,256,128]{2,1,0:T(8,128)(2,1)S(1)}, bf16[3,256,128]{2,1,0:T(8,128)(2,1)S(1)}, u32[]{:S(2)}, u32[]{:S(2)}) %collective-permute-start.4) | collective-permute-done | bytes 196640 | tf_op jit(solution)/shard_map/ppermute | solution.py:294
  32.2 3.4 %collective-permute-done.10.refs_6_ = bf16[3,256,128]{2,1,0:T(8,128)(2,1)S(1)} collective-permute-done((bf16[3,256,128]{2,1,0:T(8,128)(2,1)S(1)}, bf16[3,256,128]{2,1,0:T(8,128)(2,1)S(1)}, u32[]{:S(2)}, u32[]{:S(2)}) %collective-permute-start.10) | collective-permute-done | bytes 196640 | tf_op jit(solution)/shard_map/ppermute | solution.py:294
  35.7 4.2 %collective-permute-done.11.refs_7_ = bf16[3,256,128]{2,1,0:T(8,128)(2,1)S(1)} collective-permute-done((bf16[3,256,128]{2,1,0:T(8,128)(2,1)S(1)}, bf16[3,256,128]{2,1,0:T(8,128)(2,1)S(1)}, u32[]{:S(2)}, u32[]{:S(2)}) %collective-permute-start.11) | collective-permute-done | bytes 196640 | tf_op jit(solution)/shard_map/ppermute | solution.py:294
  50.8 27.3 %all-gather.1 = f32[16,1,128]{2,1,0:T(1,128)S(1)} all-gather(f32[1,1,128]{2,1,0:T(1,128)S(1)} %bitcast.13), channel_id=2, replica_groups=mesh['groups'=2,'row'=16] {'row'}, dimensions={0}, use_global_device_ids=true | all-gather | bytes 8704 | tf_op jit(solution)/shard_map/all_gather | solution.py:336
  79.5 2.8 %copy-done.1 = bf16[48,256,256]{2,1,0:T(8,128)(2,1)S(1)} copy-done((bf16[48,256,256]{2,1,0:T(8,128)(2,1)S(1)}, bf16[48,256,256]{2,1,0:T(8,128)(2,1)}, u32[]{:S(2)}) %copy-start.1) | copy-done | bytes 6291480
  83.2 3.6 %shard_map.91.field = f32[9,256,128]{2,1,0:T(8,128)S(1)} custom-call(s32[171]{0:T(256)S(1)} %copy-done.5, bf16[48,256,256]{2,1,0:T(8,128)(2,1)S(1)} %copy-done.1, bf16[8,256,128]{2,1,0:T(8,128)(2,1)S(1)} %convert_element_type.3.shard.refs_0_, bf16[3,256,128]{2,1,0:T(8,128)(2,1)S(1)} %collective-permute-done.3.refs_1_, ...), custom_call_target="tpu_custom_call" | custom-call | tf_op jit(solution)/shard_map/pallas_call | solution.py:225
  93.0 5.8 %collective-permute-done.21.refs_2_ = bf16[3,256,128]{2,1,0:T(8,128)(2,1)S(1)} collective-permute-done((bf16[3,256,128]{2,1,0:T(8,128)(2,1)S(1)}, bf16[3,256,128]{2,1,0:T(8,128)(2,1)S(1)}, u32[]{:S(2)}, u32[]{:S(2)}) %collective-permute-start.21) | collective-permute-done | bytes 196640 | tf_op jit(solution)/shard_map/ppermute | solution.py:294
  98.8 3.5 %collective-permute-done.22.refs_3_ = bf16[3,256,128]{2,1,0:T(8,128)(2,1)S(1)} collective-permute-done((bf16[3,256,128]{2,1,0:T(8,128)(2,1)S(1)}, bf16[3,256,128]{2,1,0:T(8,128)(2,1)S(1)}, u32[]{:S(2)}, u32[]{:S(2)}) %collective-permute-start.22) | collective-permute-done | bytes 196640 | tf_op jit(solution)/shard_map/ppermute | solution.py:294
  102.3 12.2 %collective-permute-done.19.shard.first.refs_4_ = bf16[8,256,128]{2,1,0:T(8,128)(2,1)S(1)} collective-permute-done((bf16[8,256,128]{2,1,0:T(8,128)(2,1)S(1)}, bf16[8,256,128]{2,1,0:T(8,128)(2,1)S(1)}, u32[]{:S(2)}, u32[]{:S(2)}) %collective-permute-start.19) | collective-permute-done | bytes 524320 | tf_op jit(solution)/shard_map/ppermute | solution.py:290
  117.0 5.9 %collective-permute-done.25.refs_6_ = bf16[3,256,128]{2,1,0:T(8,128)(2,1)S(1)} collective-permute-done((bf16[3,256,128]{2,1,0:T(8,128)(2,1)S(1)}, bf16[3,256,128]{2,1,0:T(8,128)(2,1)S(1)}, u32[]{:S(2)}, u32[]{:S(2)}) %collective-permute-start.25) | collective-permute-done | bytes 196640 | tf_op jit(solution)/shard_map/ppermute | solution.py:294
  122.9 3.3 %collective-permute-done.26.refs_7_ = bf16[3,256,128]{2,1,0:T(8,128)(2,1)S(1)} collective-permute-done((bf16[3,256,128]{2,1,0:T(8,128)(2,1)S(1)}, bf16[3,256,128]{2,1,0:T(8,128)(2,1)S(1)}, u32[]{:S(2)}, u32[]{:S(2)}) %collective-permute-start.26) | collective-permute-done | bytes 196640 | tf_op jit(solution)/shard_map/ppermute | solution.py:294
  130.8 4.2 %collective-permute-done.32.refs_10_ = bf16[3,256,128]{2,1,0:T(8,128)(2,1)S(1)} collective-permute-done((bf16[3,256,128]{2,1,0:T(8,128)(2,1)S(1)}, bf16[3,256,128]{2,1,0:T(8,128)(2,1)S(1)}, u32[]{:S(2)}, u32[]{:S(2)}) %collective-permute-start.32) | collective-permute-done | bytes 196640 | tf_op jit(solution)/shard_map/ppermute | solution.py:294
  137.8 3.1 %shard_map.95.field = f32[9,256,128]{2,1,0:T(8,128)S(1)} custom-call(s32[171]{0:T(256)S(1)} %copy-done.5, bf16[48,256,256]{2,1,0:T(8,128)(2,1)S(1)} %bitcast.9, bf16[8,256,128]{2,1,0:T(8,128)(2,1)S(1)} %get-tuple-element.136.refs_0_, bf16[3,256,128]{2,1,0:T(8,128)(2,1)S(1)} %collective-permute-done.20.refs_1_, ...), custom_call_target="tpu_custom_call" | custom-call | tf_op jit(solution)/shard_map/pallas_call | solution.py:225
  140.9 4.0 %collective-permute-done.29.far2 = bf16[3,256,128]{2,1,0:T(8,128)(2,1)S(1)} collective-permute-done((bf16[3,256,128]{2,1,0:T(8,128)(2,1)S(1)}, bf16[3,256,128]{2,1,0:T(8,128)(2,1)S(1)}, u32[]{:S(2)}, u32[]{:S(2)}) %collective-permute-start.29) | collective-permute-done | bytes 196640 | tf_op jit(solution)/shard_map/ppermute | solution.py:294
  144.9 3.1 %collective-permute-done.30.far3 = bf16[3,256,128]{2,1,0:T(8,128)(2,1)S(1)} collective-permute-done((bf16[3,256,128]{2,1,0:T(8,128)(2,1)S(1)}, bf16[3,256,128]{2,1,0:T(8,128)(2,1)S(1)}, u32[]{:S(2)}, u32[]{:S(2)}) %collective-permute-start.30) | collective-permute-done | bytes 196640 | tf_op jit(solution)/shard_map/ppermute | solution.py:294
  153.9 5.6 %collective-permute-done.36.refs_2_ = bf16[3,256,128]{2,1,0:T(8,128)(2,1)S(1)} collective-permute-done((bf16[3,256,128]{2,1,0:T(8,128)(2,1)S(1)}, bf16[3,256,128]{2,1,0:T(8,128)(2,1)S(1)}, u32[]{:S(2)}, u32[]{:S(2)}) %collective-permute-start.36) | collective-permute-done | bytes 196640 | tf_op jit(solution)/shard_map/ppermute | solution.py:294
  159.5 3.8 %collective-permute-done.37.refs_3_ = bf16[3,256,128]{2,1,0:T(8,128)(2,1)S(1)} collective-permute-done((bf16[3,256,128]{2,1,0:T(8,128)(2,1)S(1)}, bf16[3,256,128]{2,1,0:T(8,128)(2,1)S(1)}, u32[]{:S(2)}, u32[]{:S(2)}) %collective-permute-start.37) | collective-permute-done | bytes 196640 | tf_op jit(solution)/shard_map/ppermute | solution.py:294
  166.8 9.0 %collective-permute-done.38.second.refs_8_ = bf16[8,256,128]{2,1,0:T(8,128)(2,1)S(1)} collective-permute-done((bf16[8,256,128]{2,1,0:T(8,128)(2,1)S(1)}, bf16[8,256,128]{2,1,0:T(8,128)(2,1)S(1)}, u32[]{:S(2)}, u32[]{:S(2)}) %collective-permute-start.38) | collective-permute-done | bytes 524320 | tf_op jit(solution)/shard_map/ppermute | solution.py:290
  180.8 2.8 %collective-permute-start.44 = (bf16[3,256,128]{2,1,0:T(8,128)(2,1)S(1)}, bf16[3,256,128]{2,1,0:T(8,128)(2,1)S(1)}, u32[]{:S(2)}, u32[]{:S(2)}) collective-permute-start(bf16[3,256,128]{2,1,0:T(8,128)(2,1)S(1)} %get-tuple-element.171), channel_id=1, source_target_pairs={{0,6},{1,7},{2,4},{3,5},{4,2},{5,3},{6,0},{7,1},{8,14},{9,15},{10,... | collective-permute-start | bytes 589832 | tf_op jit(solution)/shard_map/ppermute | solution.py:294
  187.5 3.0 %shard_map.99.field = f32[9,256,128]{2,1,0:T(8,128)S(1)} custom-call(s32[171]{0:T(256)S(1)} %copy-done.5, bf16[48,256,256]{2,1,0:T(8,128)(2,1)S(1)} %bitcast.9, bf16[8,256,128]{2,1,0:T(8,128)(2,1)S(1)} %get-tuple-element.160.refs_0_, bf16[3,256,128]{2,1,0:T(8,128)(2,1)S(1)} %collective-permute-done.35.refs_1_, ...), custom_call_target="tpu_custom_call" | custom-call | tf_op jit(solution)/shard_map/pallas_call | solution.py:225
  190.6 5.3 %collective-permute-done.44.far2 = bf16[3,256,128]{2,1,0:T(8,128)(2,1)S(1)} collective-permute-done((bf16[3,256,128]{2,1,0:T(8,128)(2,1)S(1)}, bf16[3,256,128]{2,1,0:T(8,128)(2,1)S(1)}, u32[]{:S(2)}, u32[]{:S(2)}) %collective-permute-start.44) | collective-permute-done | bytes 196640 | tf_op jit(solution)/shard_map/ppermute | solution.py:294
  196.0 3.7 %collective-permute-done.45.far3 = bf16[3,256,128]{2,1,0:T(8,128)(2,1)S(1)} collective-permute-done((bf16[3,256,128]{2,1,0:T(8,128)(2,1)S(1)}, bf16[3,256,128]{2,1,0:T(8,128)(2,1)S(1)}, u32[]{:S(2)}, u32[]{:S(2)}) %collective-permute-start.45) | collective-permute-done | bytes 196640 | tf_op jit(solution)/shard_map/ppermute | solution.py:294
  205.3 5.8 %collective-permute-done.51.refs_2_ = bf16[3,256,128]{2,1,0:T(8,128)(2,1)S(1)} collective-permute-done((bf16[3,256,128]{2,1,0:T(8,128)(2,1)S(1)}, bf16[3,256,128]{2,1,0:T(8,128)(2,1)S(1)}, u32[]{:S(2)}, u32[]{:S(2)}) %collective-permute-start.51) | collective-permute-done | bytes 196640 | tf_op jit(solution)/shard_map/ppermute | solution.py:294
  211.1 3.4 %collective-permute-done.52.refs_3_ = bf16[3,256,128]{2,1,0:T(8,128)(2,1)S(1)} collective-permute-done((bf16[3,256,128]{2,1,0:T(8,128)(2,1)S(1)}, bf16[3,256,128]{2,1,0:T(8,128)(2,1)S(1)}, u32[]{:S(2)}, u32[]{:S(2)}) %collective-permute-start.52) | collective-permute-done | bytes 196640 | tf_op jit(solution)/shard_map/ppermute | solution.py:294
  218.2 10.2 %collective-permute-done.53.second.refs_8_ = bf16[8,256,128]{2,1,0:T(8,128)(2,1)S(1)} collective-permute-done((bf16[8,256,128]{2,1,0:T(8,128)(2,1)S(1)}, bf16[8,256,128]{2,1,0:T(8,128)(2,1)S(1)}, u32[]{:S(2)}, u32[]{:S(2)}) %collective-permute-start.53) | collective-permute-done | bytes 524320 | tf_op jit(solution)/shard_map/ppermute | solution.py:290
  240.4 3.0 %shard_map.103.field = f32[9,256,128]{2,1,0:T(8,128)S(1)} custom-call(s32[171]{0:T(256)S(1)} %copy-done.5, bf16[48,256,256]{2,1,0:T(8,128)(2,1)S(1)} %bitcast.9, bf16[8,256,128]{2,1,0:T(8,128)(2,1)S(1)} %get-tuple-element.184.refs_0_, bf16[3,256,128]{2,1,0:T(8,128)(2,1)S(1)} %collective-permute-done.50.refs_1_, ...), custom_call_target="tpu_custom_call" | custom-call | tf_op jit(solution)/shard_map/pallas_call | solution.py:225
  243.5 3.9 %collective-permute-done.59.far2 = bf16[3,256,128]{2,1,0:T(8,128)(2,1)S(1)} collective-permute-done((bf16[3,256,128]{2,1,0:T(8,128)(2,1)S(1)}, bf16[3,256,128]{2,1,0:T(8,128)(2,1)S(1)}, u32[]{:S(2)}, u32[]{:S(2)}) %collective-permute-start.59) | collective-permute-done | bytes 196640 | tf_op jit(solution)/shard_map/ppermute | solution.py:294
  247.4 3.6 %collective-permute-done.60.far3 = bf16[3,256,128]{2,1,0:T(8,128)(2,1)S(1)} collective-permute-done((bf16[3,256,128]{2,1,0:T(8,128)(2,1)S(1)}, bf16[3,256,128]{2,1,0:T(8,128)(2,1)S(1)}, u32[]{:S(2)}, u32[]{:S(2)}) %collective-permute-start.60) | collective-permute-done | bytes 196640 | tf_op jit(solution)/shard_map/ppermute | solution.py:294
  251.0 3.0 %shard_map.104 = (f32[8,256,128]{2,1,0:T(8,128)}, f32[8,256,128]{2,1,0:T(8,128)}, f32[1,128]{1,0:T(1,128)S(1)}) custom-call(s32[171]{0:T(256)S(1)} %copy-done.5, f32[2]{0:T(128)S(1)} %pad_maximum_fusion.scalars, bf16[48,256,256]{2,1,0:T(8,128)(2,1)S(1)} %bitcast.9, bf16[3,256,128]{2,1,0:T(8,128)(2,1)S(1)} %collective-permute-done.57.far0, ...), custom_call_target="tpu_custom_call" | custom-call | flops 201326592 | bytes 7602176 | tf_op jit(solution)/shard_map/pallas_call | solution.py:275
  254.0 10.5 %all_to_all.6 = f32[16,1,128]{2,1,0:T(1,128)S(1)} all-to-all(f32[16,1,128]{2,1,0:T(1,128)S(1)} %broadcast_in_dim.2), channel_id=1, replica_groups=mesh['groups'=2,'row'=16] {'row'}, dimensions={0} | all-to-all | bytes 16384 | tf_op jit(solution)/shard_map/all_to_all | solution.py:300
  (162 shorter events, 89.7 us)
Async XLA Ops:
  1.9 25.3 %collective-permute-start.7 = (bf16[8,256,128]{2,1,0:T(8,128)(2,1)S(1)}, bf16[8,256,128]{2,1,0:T(8,128)(2,1)S(1)}, u32[]{:S(2)}, u32[]{:S(2)}) collective-permute-start(bf16[8,256,128]{2,1,0:T(8,128)(2,1)S(1)} %convert_element_type.3.shard.refs_0_), channel_id=1, source_target_pairs={{0,8},{1,9},{2,10},{3,11},{12,4},{13,5},{14,6},{15,7},{4,0},{5,1},... | collective-permute-start | bytes 1572872 | tf_op jit(solution)/shard_map/ppermute | solution.py:290
  6.0 26.2 %collective-permute-start.8 = (bf16[8,256,128]{2,1,0:T(8,128)(2,1)S(1)}, bf16[8,256,128]{2,1,0:T(8,128)(2,1)S(1)}, u32[]{:S(2)}, u32[]{:S(2)}) collective-permute-start(bf16[8,256,128]{2,1,0:T(8,128)(2,1)S(1)} %convert_element_type.3.shard.refs_0_), channel_id=1, source_target_pairs={{0,4},{1,5},{2,6},{3,7},{12,8},{13,9},{14,10},{15,11},{4,12},{5,13... | collective-permute-start | bytes 1572872 | tf_op jit(solution)/shard_map/ppermute | solution.py:290
  28.8 11.2 %collective-permute-start.11 = (bf16[3,256,128]{2,1,0:T(8,128)(2,1)S(1)}, bf16[3,256,128]{2,1,0:T(8,128)(2,1)S(1)}, u32[]{:S(2)}, u32[]{:S(2)}) collective-permute-start(bf16[3,256,128]{2,1,0:T(8,128)(2,1)S(1)} %get-tuple-element.121), channel_id=1, source_target_pairs={{0,3},{1,2},{2,1},{3,0},{4,7},{5,6},{6,5},{7,4},{8,11},{9,10},{10,... | collective-permute-start | bytes 589832 | tf_op jit(solution)/shard_map/ppermute | solution.py:294
  42.5 37.0 %collective-permute-start.18 = (bf16[3,256,128]{2,1,0:T(8,128)(2,1)}, bf16[3,256,128]{2,1,0:T(8,128)(2,1)}, u32[]{:S(2)}, u32[]{:S(2)}) collective-permute-start(bf16[3,256,128]{2,1,0:T(8,128)(2,1)} %get-tuple-element.135), channel_id=1, source_target_pairs={{0,3},{1,2},{2,1},{3,0},{4,7},{5,6},{6,5},{7,4},{8,11},{9,10},{10,... | collective-permute-start | bytes 589832 | tf_op jit(solution)/shard_map/ppermute | solution.py:294
  43.4 43.3 %collective-permute-start.12 = (bf16[3,256,128]{2,1,0:T(8,128)(2,1)}, bf16[3,256,128]{2,1,0:T(8,128)(2,1)S(1)}, u32[]{:S(2)}, u32[]{:S(2)}) collective-permute-start(bf16[3,256,128]{2,1,0:T(8,128)(2,1)} %get-tuple-element.123), channel_id=1, source_target_pairs={{0,4},{1,5},{2,6},{3,7},{4,0},{5,1},{6,2},{7,3},{8,12},{9,13},{10,... | collective-permute-start | bytes 589832 | tf_op jit(solution)/shard_map/ppermute | solution.py:294
  45.3 41.5 %collective-permute-start.13 = (bf16[3,256,128]{2,1,0:T(8,128)(2,1)}, bf16[3,256,128]{2,1,0:T(8,128)(2,1)S(1)}, u32[]{:S(2)}, u32[]{:S(2)}) collective-permute-start(bf16[3,256,128]{2,1,0:T(8,128)(2,1)} %get-tuple-element.124), channel_id=1, source_target_pairs={{0,5},{1,4},{2,7},{3,6},{4,1},{5,0},{6,3},{7,2},{8,13},{9,12},{10,... | collective-permute-start | bytes 589832 | tf_op jit(solution)/shard_map/ppermute | solution.py:294
  45.3 41.5 %collective-permute-start.14 = (bf16[3,256,128]{2,1,0:T(8,128)(2,1)}, bf16[3,256,128]{2,1,0:T(8,128)(2,1)S(1)}, u32[]{:S(2)}, u32[]{:S(2)}) collective-permute-start(bf16[3,256,128]{2,1,0:T(8,128)(2,1)} %get-tuple-element.125), channel_id=1, source_target_pairs={{0,6},{1,7},{2,4},{3,5},{4,2},{5,3},{6,0},{7,1},{8,14},{9,15},{10,... | collective-permute-start | bytes 589832 | tf_op jit(solution)/shard_map/ppermute | solution.py:294
  50.0 36.8 %collective-permute-start.15 = (bf16[3,256,128]{2,1,0:T(8,128)(2,1)}, bf16[3,256,128]{2,1,0:T(8,128)(2,1)}, u32[]{:S(2)}, u32[]{:S(2)}) collective-permute-start(bf16[3,256,128]{2,1,0:T(8,128)(2,1)} %get-tuple-element.126), channel_id=1, source_target_pairs={{0,7},{1,6},{2,5},{3,4},{4,3},{5,2},{6,1},{7,0},{8,15},{9,14},{10,... | collective-permute-start | bytes 589832 | tf_op jit(solution)/shard_map/ppermute | solution.py:294
  89.0 25.4 %collective-permute-start.19 = (bf16[8,256,128]{2,1,0:T(8,128)(2,1)S(1)}, bf16[8,256,128]{2,1,0:T(8,128)(2,1)S(1)}, u32[]{:S(2)}, u32[]{:S(2)}) collective-permute-start(bf16[8,256,128]{2,1,0:T(8,128)(2,1)S(1)} %get-tuple-element.136.refs_0_), channel_id=1, source_target_pairs={{0,8},{1,9},{2,10},{3,11},{12,4},{13,5},{14,6},{15,7},{4,0},{5,1},... | collective-permute-start | bytes 1572872 | tf_op jit(solution)/shard_map/ppermute | solution.py:290
  89.1 27.9 %collective-permute-start.23 = (bf16[8,256,128]{2,1,0:T(8,128)(2,1)S(1)}, bf16[8,256,128]{2,1,0:T(8,128)(2,1)S(1)}, u32[]{:S(2)}, u32[]{:S(2)}) collective-permute-start(bf16[8,256,128]{2,1,0:T(8,128)(2,1)S(1)} %get-tuple-element.136.refs_0_), channel_id=1, source_target_pairs={{0,4},{1,5},{2,6},{3,7},{12,8},{13,9},{14,10},{15,11},{4,12},{5,13... | collective-permute-start | bytes 1572872 | tf_op jit(solution)/shard_map/ppermute | solution.py:290
  91.2 11.1 %collective-permute-start.22 = (bf16[3,256,128]{2,1,0:T(8,128)(2,1)S(1)}, bf16[3,256,128]{2,1,0:T(8,128)(2,1)S(1)}, u32[]{:S(2)}, u32[]{:S(2)}) collective-permute-start(bf16[3,256,128]{2,1,0:T(8,128)(2,1)S(1)} %get-tuple-element.139), channel_id=1, source_target_pairs={{0,3},{1,2},{2,1},{3,0},{4,7},{5,6},{6,5},{7,4},{8,11},{9,10},{10,... | collective-permute-start | bytes 589832 | tf_op jit(solution)/shard_map/ppermute | solution.py:294
  115.3 10.9 %collective-permute-start.26 = (bf16[3,256,128]{2,1,0:T(8,128)(2,1)S(1)}, bf16[3,256,128]{2,1,0:T(8,128)(2,1)S(1)}, u32[]{:S(2)}, u32[]{:S(2)}) collective-permute-start(bf16[3,256,128]{2,1,0:T(8,128)(2,1)S(1)} %get-tuple-element.143), channel_id=1, source_target_pairs={{0,3},{1,2},{2,1},{3,0},{4,7},{5,6},{6,5},{7,4},{8,11},{9,10},{10,... | collective-permute-start | bytes 589832 | tf_op jit(solution)/shard_map/ppermute | solution.py:294
  128.8 12.0 %collective-permute-start.27 = (bf16[3,256,128]{2,1,0:T(8,128)(2,1)S(1)}, bf16[3,256,128]{2,1,0:T(8,128)(2,1)S(1)}, u32[]{:S(2)}, u32[]{:S(2)}) collective-permute-start(bf16[3,256,128]{2,1,0:T(8,128)(2,1)S(1)} %get-tuple-element.145), channel_id=1, source_target_pairs={{0,4},{1,5},{2,6},{3,7},{4,0},{5,1},{6,2},{7,3},{8,12},{9,13},{10,... | collective-permute-start | bytes 589832 | tf_op jit(solution)/shard_map/ppermute | solution.py:294
  128.8 12.0 %collective-permute-start.28 = (bf16[3,256,128]{2,1,0:T(8,128)(2,1)S(1)}, bf16[3,256,128]{2,1,0:T(8,128)(2,1)S(1)}, u32[]{:S(2)}, u32[]{:S(2)}) collective-permute-start(bf16[3,256,128]{2,1,0:T(8,128)(2,1)S(1)} %get-tuple-element.146), channel_id=1, source_target_pairs={{0,5},{1,4},{2,7},{3,6},{4,1},{5,0},{6,3},{7,2},{8,13},{9,12},{10,... | collective-permute-start | bytes 589832 | tf_op jit(solution)/shard_map/ppermute | solution.py:294
  130.7 14.2 %collective-permute-start.29 = (bf16[3,256,128]{2,1,0:T(8,128)(2,1)S(1)}, bf16[3,256,128]{2,1,0:T(8,128)(2,1)S(1)}, u32[]{:S(2)}, u32[]{:S(2)}) collective-permute-start(bf16[3,256,128]{2,1,0:T(8,128)(2,1)S(1)} %get-tuple-element.147), channel_id=1, source_target_pairs={{0,6},{1,7},{2,4},{3,5},{4,2},{5,3},{6,0},{7,1},{8,14},{9,15},{10,... | collective-permute-start | bytes 589832 | tf_op jit(solution)/shard_map/ppermute | solution.py:294
  135.0 13.0 %collective-permute-start.30 = (bf16[3,256,128]{2,1,0:T(8,128)(2,1)S(1)}, bf16[3,256,128]{2,1,0:T(8,128)(2,1)S(1)}, u32[]{:S(2)}, u32[]{:S(2)}) collective-permute-start(bf16[3,256,128]{2,1,0:T(8,128)(2,1)S(1)} %get-tuple-element.148), channel_id=1, source_target_pairs={{0,7},{1,6},{2,5},{3,4},{4,3},{5,2},{6,1},{7,0},{8,15},{9,14},{10,... | collective-permute-start | bytes 589832 | tf_op jit(solution)/shard_map/ppermute | solution.py:294
  149.6 14.6 %collective-permute-start.34 = (bf16[8,256,128]{2,1,0:T(8,128)(2,1)S(1)}, bf16[8,256,128]{2,1,0:T(8,128)(2,1)S(1)}, u32[]{:S(2)}, u32[]{:S(2)}) collective-permute-start(bf16[8,256,128]{2,1,0:T(8,128)(2,1)S(1)} %get-tuple-element.160.refs_0_), channel_id=1, source_target_pairs={{0,8},{1,9},{2,10},{3,11},{12,4},{13,5},{14,6},{15,7},{4,0},{5,1},... | collective-permute-start | bytes 1572872 | tf_op jit(solution)/shard_map/ppermute | solution.py:290
  149.7 26.1 %collective-permute-start.38 = (bf16[8,256,128]{2,1,0:T(8,128)(2,1)S(1)}, bf16[8,256,128]{2,1,0:T(8,128)(2,1)S(1)}, u32[]{:S(2)}, u32[]{:S(2)}) collective-permute-start(bf16[8,256,128]{2,1,0:T(8,128)(2,1)S(1)} %get-tuple-element.160.refs_0_), channel_id=1, source_target_pairs={{0,4},{1,5},{2,6},{3,7},{12,8},{13,9},{14,10},{15,11},{4,12},{5,13... | collective-permute-start | bytes 1572872 | tf_op jit(solution)/shard_map/ppermute | solution.py:290
  164.8 10.9 %collective-permute-start.39 = (bf16[3,256,128]{2,1,0:T(8,128)(2,1)S(1)}, bf16[3,256,128]{2,1,0:T(8,128)(2,1)S(1)}, u32[]{:S(2)}, u32[]{:S(2)}) collective-permute-start(bf16[3,256,128]{2,1,0:T(8,128)(2,1)S(1)} %get-tuple-element.165), channel_id=1, source_target_pairs={{0,1},{1,0},{2,3},{3,2},{4,5},{5,4},{6,7},{7,6},{8,9},{9,8},{10,11... | collective-permute-start | bytes 589832 | tf_op jit(solution)/shard_map/ppermute | solution.py:294
  164.9 10.9 %collective-permute-start.40 = (bf16[3,256,128]{2,1,0:T(8,128)(2,1)S(1)}, bf16[3,256,128]{2,1,0:T(8,128)(2,1)S(1)}, u32[]{:S(2)}, u32[]{:S(2)}) collective-permute-start(bf16[3,256,128]{2,1,0:T(8,128)(2,1)S(1)} %get-tuple-element.166), channel_id=1, source_target_pairs={{0,2},{1,3},{2,0},{3,1},{4,6},{5,7},{6,4},{7,5},{8,10},{9,11},{10,... | collective-permute-start | bytes 589832 | tf_op jit(solution)/shard_map/ppermute | solution.py:294
  178.6 12.0 %collective-permute-start.42 = (bf16[3,256,128]{2,1,0:T(8,128)(2,1)S(1)}, bf16[3,256,128]{2,1,0:T(8,128)(2,1)S(1)}, u32[]{:S(2)}, u32[]{:S(2)}) collective-permute-start(bf16[3,256,128]{2,1,0:T(8,128)(2,1)S(1)} %get-tuple-element.169), channel_id=1, source_target_pairs={{0,4},{1,5},{2,6},{3,7},{4,0},{5,1},{6,2},{7,3},{8,12},{9,13},{10,... | collective-permute-start | bytes 589832 | tf_op jit(solution)/shard_map/ppermute | solution.py:294
  180.8 15.2 %collective-permute-start.44 = (bf16[3,256,128]{2,1,0:T(8,128)(2,1)S(1)}, bf16[3,256,128]{2,1,0:T(8,128)(2,1)S(1)}, u32[]{:S(2)}, u32[]{:S(2)}) collective-permute-start(bf16[3,256,128]{2,1,0:T(8,128)(2,1)S(1)} %get-tuple-element.171), channel_id=1, source_target_pairs={{0,6},{1,7},{2,4},{3,5},{4,2},{5,3},{6,0},{7,1},{8,14},{9,15},{10,... | collective-permute-start | bytes 589832 | tf_op jit(solution)/shard_map/ppermute | solution.py:294
  184.7 15.0 %collective-permute-start.45 = (bf16[3,256,128]{2,1,0:T(8,128)(2,1)S(1)}, bf16[3,256,128]{2,1,0:T(8,128)(2,1)S(1)}, u32[]{:S(2)}, u32[]{:S(2)}) collective-permute-start(bf16[3,256,128]{2,1,0:T(8,128)(2,1)S(1)} %get-tuple-element.172), channel_id=1, source_target_pairs={{0,7},{1,6},{2,5},{3,4},{4,3},{5,2},{6,1},{7,0},{8,15},{9,14},{10,... | collective-permute-start | bytes 589832 | tf_op jit(solution)/shard_map/ppermute | solution.py:294
  201.4 14.3 %collective-permute-start.49 = (bf16[8,256,128]{2,1,0:T(8,128)(2,1)S(1)}, bf16[8,256,128]{2,1,0:T(8,128)(2,1)S(1)}, u32[]{:S(2)}, u32[]{:S(2)}) collective-permute-start(bf16[8,256,128]{2,1,0:T(8,128)(2,1)S(1)} %get-tuple-element.184.refs_0_), channel_id=1, source_target_pairs={{0,8},{1,9},{2,10},{3,11},{12,4},{13,5},{14,6},{15,7},{4,0},{5,1},... | collective-permute-start | bytes 1572872 | tf_op jit(solution)/shard_map/ppermute | solution.py:290
  202.6 25.8 %collective-permute-start.53 = (bf16[8,256,128]{2,1,0:T(8,128)(2,1)S(1)}, bf16[8,256,128]{2,1,0:T(8,128)(2,1)S(1)}, u32[]{:S(2)}, u32[]{:S(2)}) collective-permute-start(bf16[8,256,128]{2,1,0:T(8,128)(2,1)S(1)} %get-tuple-element.184.refs_0_), channel_id=1, source_target_pairs={{0,4},{1,5},{2,6},{3,7},{12,8},{13,9},{14,10},{15,11},{4,12},{5,13... | collective-permute-start | bytes 1572872 | tf_op jit(solution)/shard_map/ppermute | solution.py:290
  203.8 10.8 %collective-permute-start.52 = (bf16[3,256,128]{2,1,0:T(8,128)(2,1)S(1)}, bf16[3,256,128]{2,1,0:T(8,128)(2,1)S(1)}, u32[]{:S(2)}, u32[]{:S(2)}) collective-permute-start(bf16[3,256,128]{2,1,0:T(8,128)(2,1)S(1)} %get-tuple-element.187), channel_id=1, source_target_pairs={{0,3},{1,2},{2,1},{3,0},{4,7},{5,6},{6,5},{7,4},{8,11},{9,10},{10,... | collective-permute-start | bytes 589832 | tf_op jit(solution)/shard_map/ppermute | solution.py:294
  216.3 12.1 %collective-permute-start.54 = (bf16[3,256,128]{2,1,0:T(8,128)(2,1)S(1)}, bf16[3,256,128]{2,1,0:T(8,128)(2,1)S(1)}, u32[]{:S(2)}, u32[]{:S(2)}) collective-permute-start(bf16[3,256,128]{2,1,0:T(8,128)(2,1)S(1)} %get-tuple-element.189), channel_id=1, source_target_pairs={{0,1},{1,0},{2,3},{3,2},{4,5},{5,4},{6,7},{7,6},{8,9},{9,8},{10,11... | collective-permute-start | bytes 589832 | tf_op jit(solution)/shard_map/ppermute | solution.py:294
  216.4 12.0 %collective-permute-start.55 = (bf16[3,256,128]{2,1,0:T(8,128)(2,1)S(1)}, bf16[3,256,128]{2,1,0:T(8,128)(2,1)S(1)}, u32[]{:S(2)}, u32[]{:S(2)}) collective-permute-start(bf16[3,256,128]{2,1,0:T(8,128)(2,1)S(1)} %get-tuple-element.190), channel_id=1, source_target_pairs={{0,2},{1,3},{2,0},{3,1},{4,6},{5,7},{6,4},{7,5},{8,10},{9,11},{10,... | collective-permute-start | bytes 589832 | tf_op jit(solution)/shard_map/ppermute | solution.py:294
  216.8 11.6 %collective-permute-start.56 = (bf16[3,256,128]{2,1,0:T(8,128)(2,1)S(1)}, bf16[3,256,128]{2,1,0:T(8,128)(2,1)S(1)}, u32[]{:S(2)}, u32[]{:S(2)}) collective-permute-start(bf16[3,256,128]{2,1,0:T(8,128)(2,1)S(1)} %get-tuple-element.191), channel_id=1, source_target_pairs={{0,3},{1,2},{2,1},{3,0},{4,7},{5,6},{6,5},{7,4},{8,11},{9,10},{10,... | collective-permute-start | bytes 589832 | tf_op jit(solution)/shard_map/ppermute | solution.py:294
  231.2 12.3 %collective-permute-start.57 = (bf16[3,256,128]{2,1,0:T(8,128)(2,1)S(1)}, bf16[3,256,128]{2,1,0:T(8,128)(2,1)S(1)}, u32[]{:S(2)}, u32[]{:S(2)}) collective-permute-start(bf16[3,256,128]{2,1,0:T(8,128)(2,1)S(1)} %get-tuple-element.193), channel_id=1, source_target_pairs={{0,4},{1,5},{2,6},{3,7},{4,0},{5,1},{6,2},{7,3},{8,12},{9,13},{10,... | collective-permute-start | bytes 589832 | tf_op jit(solution)/shard_map/ppermute | solution.py:294
  233.5 13.9 %collective-permute-start.59 = (bf16[3,256,128]{2,1,0:T(8,128)(2,1)S(1)}, bf16[3,256,128]{2,1,0:T(8,128)(2,1)S(1)}, u32[]{:S(2)}, u32[]{:S(2)}) collective-permute-start(bf16[3,256,128]{2,1,0:T(8,128)(2,1)S(1)} %get-tuple-element.195), channel_id=1, source_target_pairs={{0,6},{1,7},{2,4},{3,5},{4,2},{5,3},{6,0},{7,1},{8,14},{9,15},{10,... | collective-permute-start | bytes 589832 | tf_op jit(solution)/shard_map/ppermute | solution.py:294
  237.1 13.9 %collective-permute-start.60 = (bf16[3,256,128]{2,1,0:T(8,128)(2,1)S(1)}, bf16[3,256,128]{2,1,0:T(8,128)(2,1)S(1)}, u32[]{:S(2)}, u32[]{:S(2)}) collective-permute-start(bf16[3,256,128]{2,1,0:T(8,128)(2,1)S(1)} %get-tuple-element.196), channel_id=1, source_target_pairs={{0,7},{1,6},{2,5},{3,4},{4,3},{5,2},{6,1},{7,0},{8,15},{9,14},{10,... | collective-permute-start | bytes 589832 | tf_op jit(solution)/shard_map/ppermute | solution.py:294
  (49 other events, 375.9 us)

commit v7 on v6

--- a/solution.py
+++ b/solution.py
@@ -9,6 +9,8 @@
 
 STEPS = 4
 GROUP = 6
+LANES = 128
+SUM_AT = LANES - 1
 LIMIT = 16 * 2**20
 
 SMEM = pl.BlockSpec(memory_space=pltpu.SMEM)
@@ -16,8 +18,8 @@
 ANY = pl.BlockSpec(memory_space=pl.ANY)
 
 
-def params():
-    return pltpu.CompilerParams(vmem_limit_bytes=LIMIT)
+def params(limit=LIMIT):
+    return pltpu.CompilerParams(vmem_limit_bytes=limit)
 
 
 def squares_kernel(count, tiles, out):
@@ -78,9 +80,14 @@
 LATE = tuple((3, flip) for flip in range(4))
 
 
-def plan_kernel(layout, blocks, rows, cols, count, wants, mine, seen):
+def plan_kernel(layout, blocks, rows, cols, count, tiles, mine, note, seen, buffer, sems):
     cap = layout.cap
     keys = 16 * cap
+    slots, tile, _ = buffer.shape
+    chunks = [pl.ds(first, GROUP) for first in range(0, slots, GROUP)]
+    copies = [pltpu.make_async_copy(tiles.at[c], buffer.at[c], sems.at[i]) for i, c in enumerate(chunks)]
+    for copy in copies:
+        copy.start()
 
     @pl.loop(0, 16)
     def _(d):
@@ -88,9 +95,9 @@
 
     @pl.loop(0, keys)
     def _(k):
-        wants[k] = 0
         mine[k] = 0
         mine[keys + k] = blocks
+        mine[2 * keys + k] = 0
 
     @pl.loop(0, count[0])
     def _(s):
@@ -98,48 +105,70 @@
         rank = seen[source]
         seen[source] = rank + 1
         key = source * cap + jnp.minimum(rank, cap - 1)
-        wants[key] = lax.rem(cols[s], blocks)
         mine[key] = s
         mine[keys + key] = rows[s]
-
-
-def plan(layout, blocks, rows, cols, count):
-    keys = 16 * layout.cap
+        mine[2 * keys + key] = lax.rem(cols[s], blocks)
+
+    lane = lax.broadcasted_iota(jnp.int32, note.shape, 1)
+    wants = jnp.zeros(note.shape, jnp.int32)
+    for k in range(keys):
+        wants = jnp.where(lane == k, mine[2 * keys + k], wants)
+
+    def add(s, acc):
+        t = buffer[s].astype(jnp.float32)
+        return acc + jnp.sum((t * t).reshape(tile // 8, 8, tile), axis=0)
+
+    acc = jnp.zeros((8, tile), jnp.float32)
+    for i, copy in enumerate(copies):
+        copy.wait()
+        acc = lax.fori_loop(i * GROUP, jnp.clip(count[0], i * GROUP, (i + 1) * GROUP), add, acc)
+    note[...] = jnp.where(lane == SUM_AT, jnp.sum(acc), wants.astype(jnp.float32))
+
+
+def plan(layout, blocks, rows, cols, count, tiles):
     return pl.pallas_call(
         functools.partial(plan_kernel, layout, blocks),
-        out_shape=(jax.ShapeDtypeStruct((keys,), jnp.int32), jax.ShapeDtypeStruct((2 * keys,), jnp.int32)),
-        in_specs=[SMEM] * 3,
-        out_specs=(SMEM, SMEM),
-        scratch_shapes=[pltpu.SMEM((16,), jnp.int32)],
+        out_shape=(
+            jax.ShapeDtypeStruct((3 * 16 * layout.cap,), jnp.int32),
+            jax.ShapeDtypeStruct((1, LANES), jnp.float32),
+        ),
+        in_specs=[SMEM] * 3 + [ANY],
+        out_specs=(SMEM, VMEM),
+        scratch_shapes=[
+            pltpu.SMEM((16,), jnp.int32),
+            pltpu.VMEM(tiles.shape, tiles.dtype),
+            pltpu.SemaphoreType.DMA((tiles.shape[0] // GROUP,)),
+        ],
+        compiler_params=params(59 * 2**20),
         cost_estimate=pl.CostEstimate(flops=0, bytes_accessed=0, transcendentals=0),
-    )(rows, cols, count)
-
-
-def table_kernel(layout, wants, mine, near1, near2, near3, table):
+    )(rows, cols, count, tiles)
+
+
+def table_kernel(layout, mine, asked, table):
     cap = layout.cap
     keys = 16 * cap
     _, yc, _, zs = whereabouts()
     for j in range(3):
-        for flip, asked in ((1, near1), (2, near2), (3, near3)):
+        for flip in (1, 2, 3):
             for r in range(cap):
-                table[layout.pack(j, flip) + r] = asked[(zs[j] * 4 + yc) * cap + r]
+                table[layout.pack(j, flip) + r] = asked[flip * LANES + (zs[j] * 4 + yc) * cap + r]
     for i, (j, flip) in enumerate(EARLY + LATE):
         for r in range(cap):
             key = (zs[j] * 4 + (yc ^ flip)) * cap + r
             at = layout.entry(i * cap + r)
             table[at] = mine[key]
             table[at + 1] = mine[keys + key]
-            table[at + 2] = wants[key]
-
-
-def make_table(layout, wants, mine, near):
+            table[at + 2] = mine[2 * keys + key]
+
+
+def make_table(layout, mine, asked):
     return pl.pallas_call(
         functools.partial(table_kernel, layout),
         out_shape=jax.ShapeDtypeStruct((layout.size,), jnp.int32),
-        in_specs=[SMEM] * 5,
+        in_specs=[SMEM] * 2,
         out_specs=SMEM,
         cost_estimate=pl.CostEstimate(flops=0, bytes_accessed=0, transcendentals=0),
-    )(wants, mine, *near)
+    )(mine, asked)
 
 
 def copy_blocks(table, at, cap, shard, out):
@@ -162,22 +191,22 @@
 
     def send(shard):
         for flip in range(4):
-            copy_blocks(asked, (flip * 16 + (z ^ 2) * 4 + yc) * cap, cap, shard, far[flip])
+            copy_blocks(asked, flip * LANES + ((z ^ 2) * 4 + yc) * cap, cap, shard, far[flip])
 
     pl.when(inner)(lambda: send(first))
     pl.when(jnp.logical_not(inner))(lambda: send(second))
 
 
-def pack(kernel, cap, number, tables, shards, after=()):
+def pack(kernel, cap, number, tables, shards):
     _, tile, repl = shards[0].shape
     return pl.pallas_call(
         kernel,
         out_shape=[jax.ShapeDtypeStruct((cap, tile, repl), jnp.bfloat16)] * number,
-        in_specs=[SMEM] * len(tables) + [VMEM] * len(shards) + [ANY] * len(after),
+        in_specs=[SMEM] * len(tables) + [VMEM] * len(shards),
         out_specs=[VMEM] * number,
         compiler_params=params(),
         cost_estimate=pl.CostEstimate(flops=0, bytes_accessed=0, transcendentals=0),
-    )(*tables, *shards, *after)
+    )(*tables, *shards)
 
 
 def multiply(layout, table, tiles, xbuf, first, number, field):
@@ -313,9 +342,9 @@
     xpos = positions.reshape(blocks, tile, repl)
     ymom = momenta.reshape(blocks, tile, repl)
     own0 = xpos.astype(jnp.bfloat16)
-    wants, mine = plan(layout, blocks, tile_rows, tile_cols, counts)
-    near = [across(flip, wants) for flip in (1, 2, 3)]
-    table = make_table(layout, wants, mine, near)
+    mine, note = plan(layout, blocks, tile_rows, tile_cols, counts, tiles)
+    notes = jnp.concatenate([note] + [across(flip, note) for flip in (1, 2, 3)])
+    table = make_table(layout, mine, notes.astype(jnp.int32).reshape(-1))
     packs0 = pack(pack_own, cap, 3, [table], [own0])
     asked = coeff = None
     for step in range(STEPS):
@@ -323,17 +352,16 @@
         own1 = along_z(FIRST, own0)
         own2 = along_z(SECOND, own0)
         got0 = [across(flip, packs0[flip - 1]) for flip in (1, 2, 3)]
-        after = []
         if step == 0:
-            part = squares(counts, tiles)
-            after = [part]
-            near, got0 = lax.optimization_barrier((near, got0))
-            asked = across(4, jnp.concatenate([wants] + near))
+            notes, got0 = lax.optimization_barrier((notes, got0))
+            far_notes = across(4, notes)
+            asked = far_notes.astype(jnp.int32).reshape(-1)
         own1, got0 = lax.optimization_barrier((own1, got0))
-        packs1 = pack(pack_first, cap, 3, [table], [own1], after)
+        packs1 = pack(pack_first, cap, 3, [table], [own1])
         got1 = [across(flip, packs1[flip - 1]) for flip in (1, 2, 3)]
         if step == 0:
-            total = jnp.sum(lax.all_gather(part, "row"))
+            half = jnp.broadcast_to(jnp.sum(notes[:, SUM_AT]) + jnp.sum(far_notes[:, SUM_AT]), (1, LANES))
+            total = jnp.sum((half + across(8, half))[0, 0])
             coeff = 0.7 * jnp.sqrt((order - 1) / total)
         own2, got1 = lax.optimization_barrier((own2, got1))
         packs2 = pack(pack_second, cap, 7, [table, asked], [own1, own2])
@@ -420,5 +448,10 @@
         P(("groups", "row"), None),
     )
     out_specs = (P(("groups", "row"), None), P(("groups", "row"), None), P("groups"))
-    body = body_16 if mesh.shape["row"] == 16 else body_any
+
+    def body(tiles, *args):
+        slots = tiles.shape[0]
+        by_hand = mesh.shape["row"] == 16 and slots % GROUP == 0 and slots <= 96
+        return (body_16 if by_hand else body_any)(tiles, *args)
+
     return jax.shard_map(body, mesh=mesh, in_specs=in_specs, out_specs=out_specs, check_vma=False)

time: 266 us -> 240 us (0.902)
  blocking collectives: 37.8 us -> 9.37 us
  starting transfers between devices: 54.9 us -> 59.6 us
  local copies, waits for them, and re-layouts: 8.4 us -> 4.21 us
    all_gather x1 -> x0, blocking collectives: 27.3 us -> none  [body_16(): total = jnp.sum(lax.all_gather(part, 'row'))]
    ppermute x56 -> x57, starting transfers between devices: 44.6 us -> 49.3 us  [across(): return lax.ppermute(value, 'row', [(i, i ^ flip) for i in range(16)])]
    unnamed x34 -> x20, local copies, waits for them, and re-layouts: 8.39 us -> 4.2 us
    ppermute x56 -> x57, waiting for transfers between devices: 93.1 us -> 92 us  [across(): return lax.ppermute(value, 'row', [(i, i ^ flip) for i in range(16)])]
  transfers between devices with their start and end apart: 64 -> 65, of which waited for: 33 -> 34; matrix products, arithmetic and copies ran while one was open for 0% -> 1% of each run, Pallas kernels for 8% -> 9%
where the time goes in v7:
time: 240 us
  waiting for transfers between devices  126 us (52%)
  starting transfers between devices  59.6 us (25%)
  Pallas kernels  32.5 us (14%)
  blocking collectives  9.37 us (4%)
  other arithmetic  4.78 us (2%)
  local copies, waits for them, and re-layouts  4.21 us (2%)
  between operations  3.05 us (1%)
    ppermute x57, waiting for transfers between devices, across(): return lax.ppermute(value, 'row', [(i, i ^ flip) for i in range(16)])  92 us
    ppermute x57, starting transfers between devices, across(): return lax.ppermute(value, 'row', [(i, i ^ flip) for i in range(16)])  49.3 us
    ppermute x8, waiting for transfers between devices, along_z(): lax.ppermute(value, 'row', [(a * 4 + i, b * 4 + i) for a, b in pairs for...  34.5 us
    pallas_call x4, Pallas kernels, early(): pl.pallas_call(functools.partial(early_kernel, layout), out_shape=jax.Sha...  12.2 us
    ppermute x8, starting transfers between devices, along_z(): lax.ppermute(value, 'row', [(a * 4 + i, b * 4 + i) for a, b in pairs for...  10.3 us
    all_to_all x1, blocking collectives, row_sum(): lax.all_to_all(spread, 'row', split_axis=0, concat_axis=0, tiled=True)  9.37 us
    pallas_call x4, Pallas kernels, late(): pl.pallas_call(functools.partial(late_kernel, layout, last), out_shape=(s...  8.08 us
    pallas_call x9, Pallas kernels, pack(): pl.pallas_call(kernel, out_shape=[jax.ShapeDtypeStruct((cap, tile, repl),...  6.6 us
  transfers between devices with their start and end apart: 65, of which 34 were waited for; matrix products, arithmetic and copies ran while one was open for 1% of the time, Pallas kernels for 9%

profile of v7, /device:TPU:0, one launch (start us, length us, event | category | flops | bytes accessed | tf_op | source)
XLA Modules:
  0.0 240.0 jit_solution(3687711232024819100)
XLA Ops:
  1.9 4.1 %collective-permute-start.8 = (bf16[8,256,128]{2,1,0:T(8,128)(2,1)S(1)}, bf16[8,256,128]{2,1,0:T(8,128)(2,1)S(1)}, u32[]{:S(2)}, u32[]{:S(2)}) collective-permute-start(bf16[8,256,128]{2,1,0:T(8,128)(2,1)S(1)} %convert_element_type.15.shard.refs_0_), channel_id=1, source_target_pairs={{0,8},{1,9},{2,10},{3,11},{12,4},{13,5},{14,6},{15,7},{4,0},{5,1},... | collective-permute-start | bytes 1572872 | tf_op jit(solution)/shard_map/ppermute | solution.py:319
  6.7 4.2 %shard_map.85 = (s32[144]{0:T(256)}, f32[1,128]{1,0:T(1,128)}) custom-call(s32[48]{0:T(128)} %rows.1, s32[48]{0:T(128)} %cols.1, s32[1]{0:T(128)S(6)} %copy.10.count, bf16[48,256,256]{2,1,0:T(8,128)(2,1)} %tiles.17), custom_call_target="tpu_custom_call" | custom-call | tf_op jit(solution)/shard_map/pallas_call | solution.py:129
  21.6 6.3 %collective-permute-done.4.refs_2_ = bf16[3,256,128]{2,1,0:T(8,128)(2,1)S(1)} collective-permute-done((bf16[3,256,128]{2,1,0:T(8,128)(2,1)S(1)}, bf16[3,256,128]{2,1,0:T(8,128)(2,1)S(1)}, u32[]{:S(2)}, u32[]{:S(2)}) %collective-permute-start.4) | collective-permute-done | bytes 196640 | tf_op jit(solution)/shard_map/ppermute | solution.py:323
  27.9 2.5 %collective-permute-done.5.refs_3_ = bf16[3,256,128]{2,1,0:T(8,128)(2,1)S(1)} collective-permute-done((bf16[3,256,128]{2,1,0:T(8,128)(2,1)S(1)}, bf16[3,256,128]{2,1,0:T(8,128)(2,1)S(1)}, u32[]{:S(2)}, u32[]{:S(2)}) %collective-permute-start.5) | collective-permute-done | bytes 196640 | tf_op jit(solution)/shard_map/ppermute | solution.py:323
  34.0 5.5 %collective-permute-done.11.refs_6_ = bf16[3,256,128]{2,1,0:T(8,128)(2,1)S(1)} collective-permute-done((bf16[3,256,128]{2,1,0:T(8,128)(2,1)S(1)}, bf16[3,256,128]{2,1,0:T(8,128)(2,1)S(1)}, u32[]{:S(2)}, u32[]{:S(2)}) %collective-permute-start.11) | collective-permute-done | bytes 196640 | tf_op jit(solution)/shard_map/ppermute | solution.py:323
  39.5 2.5 %collective-permute-done.12.refs_7_ = bf16[3,256,128]{2,1,0:T(8,128)(2,1)S(1)} collective-permute-done((bf16[3,256,128]{2,1,0:T(8,128)(2,1)S(1)}, bf16[3,256,128]{2,1,0:T(8,128)(2,1)S(1)}, u32[]{:S(2)}, u32[]{:S(2)}) %collective-permute-start.12) | collective-permute-done | bytes 196640 | tf_op jit(solution)/shard_map/ppermute | solution.py:323
  57.2 2.8 %copy-done = bf16[48,256,256]{2,1,0:T(8,128)(2,1)S(1)} copy-done((bf16[48,256,256]{2,1,0:T(8,128)(2,1)S(1)}, bf16[48,256,256]{2,1,0:T(8,128)(2,1)}, u32[]{:S(2)}) %copy-start) | copy-done | bytes 6291480
  59.9 3.0 %shard_map.90.field = f32[9,256,128]{2,1,0:T(8,128)S(1)} custom-call(s32[171]{0:T(256)S(1)} %copy-done.4, bf16[48,256,256]{2,1,0:T(8,128)(2,1)S(1)} %copy-done, bf16[8,256,128]{2,1,0:T(8,128)(2,1)S(1)} %convert_element_type.15.shard.refs_0_, bf16[3,256,128]{2,1,0:T(8,128)(2,1)S(1)} %collective-permute-done.3.refs_1_, ...), custom_call_target="tpu_custom_call" | custom-call | tf_op jit(solution)/shard_map/pallas_call | solution.py:254
  63.0 4.7 %collective-permute-done.15.far2 = bf16[3,256,128]{2,1,0:T(8,128)(2,1)S(1)} collective-permute-done((bf16[3,256,128]{2,1,0:T(8,128)(2,1)S(1)}, bf16[3,256,128]{2,1,0:T(8,128)(2,1)S(1)}, u32[]{:S(2)}, u32[]{:S(2)}) %collective-permute-start.15) | collective-permute-done | bytes 196640 | tf_op jit(solution)/shard_map/ppermute | solution.py:323
  67.6 3.1 %collective-permute-done.16.far3 = bf16[3,256,128]{2,1,0:T(8,128)(2,1)S(1)} collective-permute-done((bf16[3,256,128]{2,1,0:T(8,128)(2,1)S(1)}, bf16[3,256,128]{2,1,0:T(8,128)(2,1)S(1)}, u32[]{:S(2)}, u32[]{:S(2)}) %collective-permute-start.16) | collective-permute-done | bytes 196640 | tf_op jit(solution)/shard_map/ppermute | solution.py:323
  76.3 5.8 %collective-permute-done.22.refs_2_ = bf16[3,256,128]{2,1,0:T(8,128)(2,1)S(1)} collective-permute-done((bf16[3,256,128]{2,1,0:T(8,128)(2,1)S(1)}, bf16[3,256,128]{2,1,0:T(8,128)(2,1)S(1)}, u32[]{:S(2)}, u32[]{:S(2)}) %collective-permute-start.22) | collective-permute-done | bytes 196640 | tf_op jit(solution)/shard_map/ppermute | solution.py:323
  82.2 3.4 %collective-permute-done.23.refs_3_ = bf16[3,256,128]{2,1,0:T(8,128)(2,1)S(1)} collective-permute-done((bf16[3,256,128]{2,1,0:T(8,128)(2,1)S(1)}, bf16[3,256,128]{2,1,0:T(8,128)(2,1)S(1)}, u32[]{:S(2)}, u32[]{:S(2)}) %collective-permute-start.23) | collective-permute-done | bytes 196640 | tf_op jit(solution)/shard_map/ppermute | solution.py:323
  89.3 10.4 %collective-permute-done.24.second.refs_8_ = bf16[8,256,128]{2,1,0:T(8,128)(2,1)S(1)} collective-permute-done((bf16[8,256,128]{2,1,0:T(8,128)(2,1)S(1)}, bf16[8,256,128]{2,1,0:T(8,128)(2,1)S(1)}, u32[]{:S(2)}, u32[]{:S(2)}) %collective-permute-start.24) | collective-permute-done | bytes 524320 | tf_op jit(solution)/shard_map/ppermute | solution.py:319
  104.3 2.4 %collective-permute-start.30 = (bf16[3,256,128]{2,1,0:T(8,128)(2,1)S(1)}, bf16[3,256,128]{2,1,0:T(8,128)(2,1)S(1)}, u32[]{:S(2)}, u32[]{:S(2)}) collective-permute-start(bf16[3,256,128]{2,1,0:T(8,128)(2,1)S(1)} %get-tuple-element.143), channel_id=1, source_target_pairs={{0,6},{1,7},{2,4},{3,5},{4,2},{5,3},{6,0},{7,1},{8,14},{9,15},{10,... | collective-permute-start | bytes 589832 | tf_op jit(solution)/shard_map/ppermute | solution.py:323
  111.6 3.1 %shard_map.94.field = f32[9,256,128]{2,1,0:T(8,128)S(1)} custom-call(s32[171]{0:T(256)S(1)} %copy-done.4, bf16[48,256,256]{2,1,0:T(8,128)(2,1)S(1)} %bitcast.13, bf16[8,256,128]{2,1,0:T(8,128)(2,1)S(1)} %get-tuple-element.132.refs_0_, bf16[3,256,128]{2,1,0:T(8,128)(2,1)S(1)} %collective-permute-done.21.refs_1_, ...), custom_call_target="tpu_custom_call" | custom-call | tf_op jit(solution)/shard_map/pallas_call | solution.py:254
  114.7 4.5 %collective-permute-done.30.far2 = bf16[3,256,128]{2,1,0:T(8,128)(2,1)S(1)} collective-permute-done((bf16[3,256,128]{2,1,0:T(8,128)(2,1)S(1)}, bf16[3,256,128]{2,1,0:T(8,128)(2,1)S(1)}, u32[]{:S(2)}, u32[]{:S(2)}) %collective-permute-start.30) | collective-permute-done | bytes 196640 | tf_op jit(solution)/shard_map/ppermute | solution.py:323
  119.2 3.6 %collective-permute-done.31.far3 = bf16[3,256,128]{2,1,0:T(8,128)(2,1)S(1)} collective-permute-done((bf16[3,256,128]{2,1,0:T(8,128)(2,1)S(1)}, bf16[3,256,128]{2,1,0:T(8,128)(2,1)S(1)}, u32[]{:S(2)}, u32[]{:S(2)}) %collective-permute-start.31) | collective-permute-done | bytes 196640 | tf_op jit(solution)/shard_map/ppermute | solution.py:323
  128.4 5.8 %collective-permute-done.37.refs_2_ = bf16[3,256,128]{2,1,0:T(8,128)(2,1)S(1)} collective-permute-done((bf16[3,256,128]{2,1,0:T(8,128)(2,1)S(1)}, bf16[3,256,128]{2,1,0:T(8,128)(2,1)S(1)}, u32[]{:S(2)}, u32[]{:S(2)}) %collective-permute-start.37) | collective-permute-done | bytes 196640 | tf_op jit(solution)/shard_map/ppermute | solution.py:323
  134.3 3.4 %collective-permute-done.38.refs_3_ = bf16[3,256,128]{2,1,0:T(8,128)(2,1)S(1)} collective-permute-done((bf16[3,256,128]{2,1,0:T(8,128)(2,1)S(1)}, bf16[3,256,128]{2,1,0:T(8,128)(2,1)S(1)}, u32[]{:S(2)}, u32[]{:S(2)}) %collective-permute-start.38) | collective-permute-done | bytes 196640 | tf_op jit(solution)/shard_map/ppermute | solution.py:323
  141.3 10.5 %collective-permute-done.39.second.refs_8_ = bf16[8,256,128]{2,1,0:T(8,128)(2,1)S(1)} collective-permute-done((bf16[8,256,128]{2,1,0:T(8,128)(2,1)S(1)}, bf16[8,256,128]{2,1,0:T(8,128)(2,1)S(1)}, u32[]{:S(2)}, u32[]{:S(2)}) %collective-permute-start.39) | collective-permute-done | bytes 524320 | tf_op jit(solution)/shard_map/ppermute | solution.py:319
  161.1 2.5 %collective-permute-done.49.refs_11_ = bf16[3,256,128]{2,1,0:T(8,128)(2,1)S(1)} collective-permute-done((bf16[3,256,128]{2,1,0:T(8,128)(2,1)S(1)}, bf16[3,256,128]{2,1,0:T(8,128)(2,1)S(1)}, u32[]{:S(2)}, u32[]{:S(2)}) %collective-permute-start.49) | collective-permute-done | bytes 196640 | tf_op jit(solution)/shard_map/ppermute | solution.py:323
  163.6 3.1 %shard_map.98.field = f32[9,256,128]{2,1,0:T(8,128)S(1)} custom-call(s32[171]{0:T(256)S(1)} %copy-done.4, bf16[48,256,256]{2,1,0:T(8,128)(2,1)S(1)} %bitcast.13, bf16[8,256,128]{2,1,0:T(8,128)(2,1)S(1)} %get-tuple-element.156.refs_0_, bf16[3,256,128]{2,1,0:T(8,128)(2,1)S(1)} %collective-permute-done.36.refs_1_, ...), custom_call_target="tpu_custom_call" | custom-call | tf_op jit(solution)/shard_map/pallas_call | solution.py:254
  166.7 4.1 %collective-permute-done.45.far2 = bf16[3,256,128]{2,1,0:T(8,128)(2,1)S(1)} collective-permute-done((bf16[3,256,128]{2,1,0:T(8,128)(2,1)S(1)}, bf16[3,256,128]{2,1,0:T(8,128)(2,1)S(1)}, u32[]{:S(2)}, u32[]{:S(2)}) %collective-permute-start.45) | collective-permute-done | bytes 196640 | tf_op jit(solution)/shard_map/ppermute | solution.py:323
  170.8 3.8 %collective-permute-done.46.far3 = bf16[3,256,128]{2,1,0:T(8,128)(2,1)S(1)} collective-permute-done((bf16[3,256,128]{2,1,0:T(8,128)(2,1)S(1)}, bf16[3,256,128]{2,1,0:T(8,128)(2,1)S(1)}, u32[]{:S(2)}, u32[]{:S(2)}) %collective-permute-start.46) | collective-permute-done | bytes 196640 | tf_op jit(solution)/shard_map/ppermute | solution.py:323
  180.2 5.8 %collective-permute-done.52.refs_2_ = bf16[3,256,128]{2,1,0:T(8,128)(2,1)S(1)} collective-permute-done((bf16[3,256,128]{2,1,0:T(8,128)(2,1)S(1)}, bf16[3,256,128]{2,1,0:T(8,128)(2,1)S(1)}, u32[]{:S(2)}, u32[]{:S(2)}) %collective-permute-start.52) | collective-permute-done | bytes 196640 | tf_op jit(solution)/shard_map/ppermute | solution.py:323
  186.1 3.4 %collective-permute-done.53.refs_3_ = bf16[3,256,128]{2,1,0:T(8,128)(2,1)S(1)} collective-permute-done((bf16[3,256,128]{2,1,0:T(8,128)(2,1)S(1)}, bf16[3,256,128]{2,1,0:T(8,128)(2,1)S(1)}, u32[]{:S(2)}, u32[]{:S(2)}) %collective-permute-start.53) | collective-permute-done | bytes 196640 | tf_op jit(solution)/shard_map/ppermute | solution.py:323
  193.0 10.4 %collective-permute-done.54.second.refs_8_ = bf16[8,256,128]{2,1,0:T(8,128)(2,1)S(1)} collective-permute-done((bf16[8,256,128]{2,1,0:T(8,128)(2,1)S(1)}, bf16[8,256,128]{2,1,0:T(8,128)(2,1)S(1)}, u32[]{:S(2)}, u32[]{:S(2)}) %collective-permute-start.54) | collective-permute-done | bytes 524320 | tf_op jit(solution)/shard_map/ppermute | solution.py:319
  215.5 3.0 %shard_map.102.field = f32[9,256,128]{2,1,0:T(8,128)S(1)} custom-call(s32[171]{0:T(256)S(1)} %copy-done.4, bf16[48,256,256]{2,1,0:T(8,128)(2,1)S(1)} %bitcast.13, bf16[8,256,128]{2,1,0:T(8,128)(2,1)S(1)} %get-tuple-element.180.refs_0_, bf16[3,256,128]{2,1,0:T(8,128)(2,1)S(1)} %collective-permute-done.51.refs_1_, ...), custom_call_target="tpu_custom_call" | custom-call | tf_op jit(solution)/shard_map/pallas_call | solution.py:254
  218.5 4.6 %collective-permute-done.60.far2 = bf16[3,256,128]{2,1,0:T(8,128)(2,1)S(1)} collective-permute-done((bf16[3,256,128]{2,1,0:T(8,128)(2,1)S(1)}, bf16[3,256,128]{2,1,0:T(8,128)(2,1)S(1)}, u32[]{:S(2)}, u32[]{:S(2)}) %collective-permute-start.60) | collective-permute-done | bytes 196640 | tf_op jit(solution)/shard_map/ppermute | solution.py:323
  223.2 3.8 %collective-permute-done.61.far3 = bf16[3,256,128]{2,1,0:T(8,128)(2,1)S(1)} collective-permute-done((bf16[3,256,128]{2,1,0:T(8,128)(2,1)S(1)}, bf16[3,256,128]{2,1,0:T(8,128)(2,1)S(1)}, u32[]{:S(2)}, u32[]{:S(2)}) %collective-permute-start.61) | collective-permute-done | bytes 196640 | tf_op jit(solution)/shard_map/ppermute | solution.py:323
  227.0 3.0 %shard_map.103 = (f32[8,256,128]{2,1,0:T(8,128)}, f32[8,256,128]{2,1,0:T(8,128)}, f32[1,128]{1,0:T(1,128)S(1)}) custom-call(s32[171]{0:T(256)S(1)} %copy-done.4, f32[2]{0:T(128)S(1)} %pad_maximum_fusion.1.scalars, bf16[48,256,256]{2,1,0:T(8,128)(2,1)S(1)} %bitcast.13, bf16[3,256,128]{2,1,0:T(8,128)(2,1)S(1)} %collective-permute-done.58.far0, ...), custom_call_target="tpu_custom_call" | custom-call | flops 201326592 | bytes 7602176 | tf_op jit(solution)/shard_map/pallas_call | solution.py:304
  230.1 9.4 %all_to_all.6 = f32[16,1,128]{2,1,0:T(1,128)S(1)} all-to-all(f32[16,1,128]{2,1,0:T(1,128)S(1)} %broadcast_in_dim.9), channel_id=1, replica_groups=mesh['groups'=2,'row'=16] {'row'}, dimensions={0} | all-to-all | bytes 16384 | tf_op jit(solution)/shard_map/all_to_all | solution.py:329
  (152 shorter events, 88.2 us)
Async XLA Ops:
  1.9 28.4 %collective-permute-start.8 = (bf16[8,256,128]{2,1,0:T(8,128)(2,1)S(1)}, bf16[8,256,128]{2,1,0:T(8,128)(2,1)S(1)}, u32[]{:S(2)}, u32[]{:S(2)}) collective-permute-start(bf16[8,256,128]{2,1,0:T(8,128)(2,1)S(1)} %convert_element_type.15.shard.refs_0_), channel_id=1, source_target_pairs={{0,8},{1,9},{2,10},{3,11},{12,4},{13,5},{14,6},{15,7},{4,0},{5,1},... | collective-permute-start | bytes 1572872 | tf_op jit(solution)/shard_map/ppermute | solution.py:319
  12.8 21.2 %collective-permute-start.9 = (bf16[8,256,128]{2,1,0:T(8,128)(2,1)S(1)}, bf16[8,256,128]{2,1,0:T(8,128)(2,1)S(1)}, u32[]{:S(2)}, u32[]{:S(2)}) collective-permute-start(bf16[8,256,128]{2,1,0:T(8,128)(2,1)S(1)} %convert_element_type.15.shard.refs_0_), channel_id=1, source_target_pairs={{0,4},{1,5},{2,6},{3,7},{12,8},{13,9},{14,10},{15,11},{4,12},{5,13... | collective-permute-start | bytes 1572872 | tf_op jit(solution)/shard_map/ppermute | solution.py:319
  44.8 10.5 %collective-permute-start.18 = (bf16[3,256,128]{2,1,0:T(8,128)(2,1)}, bf16[3,256,128]{2,1,0:T(8,128)(2,1)S(1)}, u32[]{:S(2)}, u32[]{:S(2)}) collective-permute-start(bf16[3,256,128]{2,1,0:T(8,128)(2,1)} %get-tuple-element.130), channel_id=1, source_target_pairs={{0,2},{1,3},{2,0},{3,1},{4,6},{5,7},{6,4},{7,5},{8,10},{9,11},{10,... | collective-permute-start | bytes 589832 | tf_op jit(solution)/shard_map/ppermute | solution.py:323
  51.3 11.7 %collective-permute-start.13 = (bf16[3,256,128]{2,1,0:T(8,128)(2,1)}, bf16[3,256,128]{2,1,0:T(8,128)(2,1)S(1)}, u32[]{:S(2)}, u32[]{:S(2)}) collective-permute-start(bf16[3,256,128]{2,1,0:T(8,128)(2,1)} %copy-done.6), channel_id=1, source_target_pairs={{0,4},{1,5},{2,6},{3,7},{4,0},{5,1},{6,2},{7,3},{8,12},{9,13},{10,... | collective-permute-start | bytes 589832 | tf_op jit(solution)/shard_map/ppermute | solution.py:323
  53.5 14.2 %collective-permute-start.15 = (bf16[3,256,128]{2,1,0:T(8,128)(2,1)S(1)}, bf16[3,256,128]{2,1,0:T(8,128)(2,1)S(1)}, u32[]{:S(2)}, u32[]{:S(2)}) collective-permute-start(bf16[3,256,128]{2,1,0:T(8,128)(2,1)S(1)} %get-tuple-element.121), channel_id=1, source_target_pairs={{0,6},{1,7},{2,4},{3,5},{4,2},{5,3},{6,0},{7,1},{8,14},{9,15},{10,... | collective-permute-start | bytes 589832 | tf_op jit(solution)/shard_map/ppermute | solution.py:323
  55.3 15.4 %collective-permute-start.16 = (bf16[3,256,128]{2,1,0:T(8,128)(2,1)S(1)}, bf16[3,256,128]{2,1,0:T(8,128)(2,1)S(1)}, u32[]{:S(2)}, u32[]{:S(2)}) collective-permute-start(bf16[3,256,128]{2,1,0:T(8,128)(2,1)S(1)} %get-tuple-element.122), channel_id=1, source_target_pairs={{0,7},{1,6},{2,5},{3,4},{4,3},{5,2},{6,1},{7,0},{8,15},{9,14},{10,... | collective-permute-start | bytes 589832 | tf_op jit(solution)/shard_map/ppermute | solution.py:323
  72.4 14.4 %collective-permute-start.20 = (bf16[8,256,128]{2,1,0:T(8,128)(2,1)S(1)}, bf16[8,256,128]{2,1,0:T(8,128)(2,1)S(1)}, u32[]{:S(2)}, u32[]{:S(2)}) collective-permute-start(bf16[8,256,128]{2,1,0:T(8,128)(2,1)S(1)} %get-tuple-element.132.refs_0_), channel_id=1, source_target_pairs={{0,8},{1,9},{2,10},{3,11},{12,4},{13,5},{14,6},{15,7},{4,0},{5,1},... | collective-permute-start | bytes 1572872 | tf_op jit(solution)/shard_map/ppermute | solution.py:319
  73.7 26.0 %collective-permute-start.24 = (bf16[8,256,128]{2,1,0:T(8,128)(2,1)S(1)}, bf16[8,256,128]{2,1,0:T(8,128)(2,1)S(1)}, u32[]{:S(2)}, u32[]{:S(2)}) collective-permute-start(bf16[8,256,128]{2,1,0:T(8,128)(2,1)S(1)} %get-tuple-element.132.refs_0_), channel_id=1, source_target_pairs={{0,4},{1,5},{2,6},{3,7},{12,8},{13,9},{14,10},{15,11},{4,12},{5,13... | collective-permute-start | bytes 1572872 | tf_op jit(solution)/shard_map/ppermute | solution.py:319
  87.4 12.4 %collective-permute-start.25 = (bf16[3,256,128]{2,1,0:T(8,128)(2,1)S(1)}, bf16[3,256,128]{2,1,0:T(8,128)(2,1)S(1)}, u32[]{:S(2)}, u32[]{:S(2)}) collective-permute-start(bf16[3,256,128]{2,1,0:T(8,128)(2,1)S(1)} %get-tuple-element.137), channel_id=1, source_target_pairs={{0,1},{1,0},{2,3},{3,2},{4,5},{5,4},{6,7},{7,6},{8,9},{9,8},{10,11... | collective-permute-start | bytes 589832 | tf_op jit(solution)/shard_map/ppermute | solution.py:323
  87.5 12.3 %collective-permute-start.26 = (bf16[3,256,128]{2,1,0:T(8,128)(2,1)S(1)}, bf16[3,256,128]{2,1,0:T(8,128)(2,1)S(1)}, u32[]{:S(2)}, u32[]{:S(2)}) collective-permute-start(bf16[3,256,128]{2,1,0:T(8,128)(2,1)S(1)} %get-tuple-element.138), channel_id=1, source_target_pairs={{0,2},{1,3},{2,0},{3,1},{4,6},{5,7},{6,4},{7,5},{8,10},{9,11},{10,... | collective-permute-start | bytes 589832 | tf_op jit(solution)/shard_map/ppermute | solution.py:323
  89.1 10.6 %collective-permute-start.27 = (bf16[3,256,128]{2,1,0:T(8,128)(2,1)S(1)}, bf16[3,256,128]{2,1,0:T(8,128)(2,1)S(1)}, u32[]{:S(2)}, u32[]{:S(2)}) collective-permute-start(bf16[3,256,128]{2,1,0:T(8,128)(2,1)S(1)} %get-tuple-element.139), channel_id=1, source_target_pairs={{0,3},{1,2},{2,1},{3,0},{4,7},{5,6},{6,5},{7,4},{8,11},{9,10},{10,... | collective-permute-start | bytes 589832 | tf_op jit(solution)/shard_map/ppermute | solution.py:323
  102.4 12.3 %collective-permute-start.28 = (bf16[3,256,128]{2,1,0:T(8,128)(2,1)S(1)}, bf16[3,256,128]{2,1,0:T(8,128)(2,1)S(1)}, u32[]{:S(2)}, u32[]{:S(2)}) collective-permute-start(bf16[3,256,128]{2,1,0:T(8,128)(2,1)S(1)} %get-tuple-element.141), channel_id=1, source_target_pairs={{0,4},{1,5},{2,6},{3,7},{4,0},{5,1},{6,2},{7,3},{8,12},{9,13},{10,... | collective-permute-start | bytes 589832 | tf_op jit(solution)/shard_map/ppermute | solution.py:323
  104.2 10.6 %collective-permute-start.29 = (bf16[3,256,128]{2,1,0:T(8,128)(2,1)S(1)}, bf16[3,256,128]{2,1,0:T(8,128)(2,1)S(1)}, u32[]{:S(2)}, u32[]{:S(2)}) collective-permute-start(bf16[3,256,128]{2,1,0:T(8,128)(2,1)S(1)} %get-tuple-element.142), channel_id=1, source_target_pairs={{0,5},{1,4},{2,7},{3,6},{4,1},{5,0},{6,3},{7,2},{8,13},{9,12},{10,... | collective-permute-start | bytes 589832 | tf_op jit(solution)/shard_map/ppermute | solution.py:323
  104.3 14.9 %collective-permute-start.30 = (bf16[3,256,128]{2,1,0:T(8,128)(2,1)S(1)}, bf16[3,256,128]{2,1,0:T(8,128)(2,1)S(1)}, u32[]{:S(2)}, u32[]{:S(2)}) collective-permute-start(bf16[3,256,128]{2,1,0:T(8,128)(2,1)S(1)} %get-tuple-element.143), channel_id=1, source_target_pairs={{0,6},{1,7},{2,4},{3,5},{4,2},{5,3},{6,0},{7,1},{8,14},{9,15},{10,... | collective-permute-start | bytes 589832 | tf_op jit(solution)/shard_map/ppermute | solution.py:323
  108.3 14.5 %collective-permute-start.31 = (bf16[3,256,128]{2,1,0:T(8,128)(2,1)S(1)}, bf16[3,256,128]{2,1,0:T(8,128)(2,1)S(1)}, u32[]{:S(2)}, u32[]{:S(2)}) collective-permute-start(bf16[3,256,128]{2,1,0:T(8,128)(2,1)S(1)} %get-tuple-element.144), channel_id=1, source_target_pairs={{0,7},{1,6},{2,5},{3,4},{4,3},{5,2},{6,1},{7,0},{8,15},{9,14},{10,... | collective-permute-start | bytes 589832 | tf_op jit(solution)/shard_map/ppermute | solution.py:323
  124.5 14.2 %collective-permute-start.35 = (bf16[8,256,128]{2,1,0:T(8,128)(2,1)S(1)}, bf16[8,256,128]{2,1,0:T(8,128)(2,1)S(1)}, u32[]{:S(2)}, u32[]{:S(2)}) collective-permute-start(bf16[8,256,128]{2,1,0:T(8,128)(2,1)S(1)} %get-tuple-element.156.refs_0_), channel_id=1, source_target_pairs={{0,8},{1,9},{2,10},{3,11},{12,4},{13,5},{14,6},{15,7},{4,0},{5,1},... | collective-permute-start | bytes 1572872 | tf_op jit(solution)/shard_map/ppermute | solution.py:319
  125.9 25.8 %collective-permute-start.39 = (bf16[8,256,128]{2,1,0:T(8,128)(2,1)S(1)}, bf16[8,256,128]{2,1,0:T(8,128)(2,1)S(1)}, u32[]{:S(2)}, u32[]{:S(2)}) collective-permute-start(bf16[8,256,128]{2,1,0:T(8,128)(2,1)S(1)} %get-tuple-element.156.refs_0_), channel_id=1, source_target_pairs={{0,4},{1,5},{2,6},{3,7},{12,8},{13,9},{14,10},{15,11},{4,12},{5,13... | collective-permute-start | bytes 1572872 | tf_op jit(solution)/shard_map/ppermute | solution.py:319
  127.3 10.4 %collective-permute-start.38 = (bf16[3,256,128]{2,1,0:T(8,128)(2,1)S(1)}, bf16[3,256,128]{2,1,0:T(8,128)(2,1)S(1)}, u32[]{:S(2)}, u32[]{:S(2)}) collective-permute-start(bf16[3,256,128]{2,1,0:T(8,128)(2,1)S(1)} %get-tuple-element.159), channel_id=1, source_target_pairs={{0,3},{1,2},{2,1},{3,0},{4,7},{5,6},{6,5},{7,4},{8,11},{9,10},{10,... | collective-permute-start | bytes 589832 | tf_op jit(solution)/shard_map/ppermute | solution.py:323
  139.3 12.4 %collective-permute-start.40 = (bf16[3,256,128]{2,1,0:T(8,128)(2,1)S(1)}, bf16[3,256,128]{2,1,0:T(8,128)(2,1)S(1)}, u32[]{:S(2)}, u32[]{:S(2)}) collective-permute-start(bf16[3,256,128]{2,1,0:T(8,128)(2,1)S(1)} %get-tuple-element.161), channel_id=1, source_target_pairs={{0,1},{1,0},{2,3},{3,2},{4,5},{5,4},{6,7},{7,6},{8,9},{9,8},{10,11... | collective-permute-start | bytes 589832 | tf_op jit(solution)/shard_map/ppermute | solution.py:323
  139.4 12.4 %collective-permute-start.41 = (bf16[3,256,128]{2,1,0:T(8,128)(2,1)S(1)}, bf16[3,256,128]{2,1,0:T(8,128)(2,1)S(1)}, u32[]{:S(2)}, u32[]{:S(2)}) collective-permute-start(bf16[3,256,128]{2,1,0:T(8,128)(2,1)S(1)} %get-tuple-element.162), channel_id=1, source_target_pairs={{0,2},{1,3},{2,0},{3,1},{4,6},{5,7},{6,4},{7,5},{8,10},{9,11},{10,... | collective-permute-start | bytes 589832 | tf_op jit(solution)/shard_map/ppermute | solution.py:323
  140.2 11.6 %collective-permute-start.42 = (bf16[3,256,128]{2,1,0:T(8,128)(2,1)S(1)}, bf16[3,256,128]{2,1,0:T(8,128)(2,1)S(1)}, u32[]{:S(2)}, u32[]{:S(2)}) collective-permute-start(bf16[3,256,128]{2,1,0:T(8,128)(2,1)S(1)} %get-tuple-element.163), channel_id=1, source_target_pairs={{0,3},{1,2},{2,1},{3,0},{4,7},{5,6},{6,5},{7,4},{8,11},{9,10},{10,... | collective-permute-start | bytes 589832 | tf_op jit(solution)/shard_map/ppermute | solution.py:323
  154.4 12.3 %collective-permute-start.43 = (bf16[3,256,128]{2,1,0:T(8,128)(2,1)S(1)}, bf16[3,256,128]{2,1,0:T(8,128)(2,1)S(1)}, u32[]{:S(2)}, u32[]{:S(2)}) collective-permute-start(bf16[3,256,128]{2,1,0:T(8,128)(2,1)S(1)} %get-tuple-element.165), channel_id=1, source_target_pairs={{0,4},{1,5},{2,6},{3,7},{4,0},{5,1},{6,2},{7,3},{8,12},{9,13},{10,... | collective-permute-start | bytes 589832 | tf_op jit(solution)/shard_map/ppermute | solution.py:323
  156.6 14.2 %collective-permute-start.45 = (bf16[3,256,128]{2,1,0:T(8,128)(2,1)S(1)}, bf16[3,256,128]{2,1,0:T(8,128)(2,1)S(1)}, u32[]{:S(2)}, u32[]{:S(2)}) collective-permute-start(bf16[3,256,128]{2,1,0:T(8,128)(2,1)S(1)} %get-tuple-element.167), channel_id=1, source_target_pairs={{0,6},{1,7},{2,4},{3,5},{4,2},{5,3},{6,0},{7,1},{8,14},{9,15},{10,... | collective-permute-start | bytes 589832 | tf_op jit(solution)/shard_map/ppermute | solution.py:323
  160.3 14.3 %collective-permute-start.46 = (bf16[3,256,128]{2,1,0:T(8,128)(2,1)S(1)}, bf16[3,256,128]{2,1,0:T(8,128)(2,1)S(1)}, u32[]{:S(2)}, u32[]{:S(2)}) collective-permute-start(bf16[3,256,128]{2,1,0:T(8,128)(2,1)S(1)} %get-tuple-element.168), channel_id=1, source_target_pairs={{0,7},{1,6},{2,5},{3,4},{4,3},{5,2},{6,1},{7,0},{8,15},{9,14},{10,... | collective-permute-start | bytes 589832 | tf_op jit(solution)/shard_map/ppermute | solution.py:323
  176.3 14.2 %collective-permute-start.50 = (bf16[8,256,128]{2,1,0:T(8,128)(2,1)S(1)}, bf16[8,256,128]{2,1,0:T(8,128)(2,1)S(1)}, u32[]{:S(2)}, u32[]{:S(2)}) collective-permute-start(bf16[8,256,128]{2,1,0:T(8,128)(2,1)S(1)} %get-tuple-element.180.refs_0_), channel_id=1, source_target_pairs={{0,8},{1,9},{2,10},{3,11},{12,4},{13,5},{14,6},{15,7},{4,0},{5,1},... | collective-permute-start | bytes 1572872 | tf_op jit(solution)/shard_map/ppermute | solution.py:319
  177.6 25.8 %collective-permute-start.54 = (bf16[8,256,128]{2,1,0:T(8,128)(2,1)S(1)}, bf16[8,256,128]{2,1,0:T(8,128)(2,1)S(1)}, u32[]{:S(2)}, u32[]{:S(2)}) collective-permute-start(bf16[8,256,128]{2,1,0:T(8,128)(2,1)S(1)} %get-tuple-element.180.refs_0_), channel_id=1, source_target_pairs={{0,4},{1,5},{2,6},{3,7},{12,8},{13,9},{14,10},{15,11},{4,12},{5,13... | collective-permute-start | bytes 1572872 | tf_op jit(solution)/shard_map/ppermute | solution.py:319
  191.1 12.4 %collective-permute-start.55 = (bf16[3,256,128]{2,1,0:T(8,128)(2,1)S(1)}, bf16[3,256,128]{2,1,0:T(8,128)(2,1)S(1)}, u32[]{:S(2)}, u32[]{:S(2)}) collective-permute-start(bf16[3,256,128]{2,1,0:T(8,128)(2,1)S(1)} %get-tuple-element.185), channel_id=1, source_target_pairs={{0,1},{1,0},{2,3},{3,2},{4,5},{5,4},{6,7},{7,6},{8,9},{9,8},{10,11... | collective-permute-start | bytes 589832 | tf_op jit(solution)/shard_map/ppermute | solution.py:323
  191.1 12.3 %collective-permute-start.56 = (bf16[3,256,128]{2,1,0:T(8,128)(2,1)S(1)}, bf16[3,256,128]{2,1,0:T(8,128)(2,1)S(1)}, u32[]{:S(2)}, u32[]{:S(2)}) collective-permute-start(bf16[3,256,128]{2,1,0:T(8,128)(2,1)S(1)} %get-tuple-element.186), channel_id=1, source_target_pairs={{0,2},{1,3},{2,0},{3,1},{4,6},{5,7},{6,4},{7,5},{8,10},{9,11},{10,... | collective-permute-start | bytes 589832 | tf_op jit(solution)/shard_map/ppermute | solution.py:323
  192.5 10.9 %collective-permute-start.57 = (bf16[3,256,128]{2,1,0:T(8,128)(2,1)S(1)}, bf16[3,256,128]{2,1,0:T(8,128)(2,1)S(1)}, u32[]{:S(2)}, u32[]{:S(2)}) collective-permute-start(bf16[3,256,128]{2,1,0:T(8,128)(2,1)S(1)} %get-tuple-element.187), channel_id=1, source_target_pairs={{0,3},{1,2},{2,1},{3,0},{4,7},{5,6},{6,5},{7,4},{8,11},{9,10},{10,... | collective-permute-start | bytes 589832 | tf_op jit(solution)/shard_map/ppermute | solution.py:323
  206.3 12.3 %collective-permute-start.58 = (bf16[3,256,128]{2,1,0:T(8,128)(2,1)S(1)}, bf16[3,256,128]{2,1,0:T(8,128)(2,1)S(1)}, u32[]{:S(2)}, u32[]{:S(2)}) collective-permute-start(bf16[3,256,128]{2,1,0:T(8,128)(2,1)S(1)} %get-tuple-element.189), channel_id=1, source_target_pairs={{0,4},{1,5},{2,6},{3,7},{4,0},{5,1},{6,2},{7,3},{8,12},{9,13},{10,... | collective-permute-start | bytes 589832 | tf_op jit(solution)/shard_map/ppermute | solution.py:323
  208.4 14.7 %collective-permute-start.60 = (bf16[3,256,128]{2,1,0:T(8,128)(2,1)S(1)}, bf16[3,256,128]{2,1,0:T(8,128)(2,1)S(1)}, u32[]{:S(2)}, u32[]{:S(2)}) collective-permute-start(bf16[3,256,128]{2,1,0:T(8,128)(2,1)S(1)} %get-tuple-element.191), channel_id=1, source_target_pairs={{0,6},{1,7},{2,4},{3,5},{4,2},{5,3},{6,0},{7,1},{8,14},{9,15},{10,... | collective-permute-start | bytes 589832 | tf_op jit(solution)/shard_map/ppermute | solution.py:323
  212.2 14.8 %collective-permute-start.61 = (bf16[3,256,128]{2,1,0:T(8,128)(2,1)S(1)}, bf16[3,256,128]{2,1,0:T(8,128)(2,1)S(1)}, u32[]{:S(2)}, u32[]{:S(2)}) collective-permute-start(bf16[3,256,128]{2,1,0:T(8,128)(2,1)S(1)} %get-tuple-element.192), channel_id=1, source_target_pairs={{0,7},{1,6},{2,5},{3,4},{4,3},{5,2},{6,1},{7,0},{8,15},{9,14},{10,... | collective-permute-start | bytes 589832 | tf_op jit(solution)/shard_map/ppermute | solution.py:323
  (43 other events, 364.2 us)

commit v8 on v7

--- a/solution.py
+++ b/solution.py
@@ -52,6 +52,8 @@
 
 FIRST = ((0, 2), (3, 1), (1, 0), (2, 3))
 SECOND = ((0, 1), (3, 2), (1, 3), (2, 0))
+OUTWARD = ((1, 0), (2, 3))
+MIDDLE = ((1, 2), (2, 1))
 
 
 class Layout:
@@ -76,8 +78,9 @@
     return z, yc, inner, (z, jnp.where(inner, skip, near), jnp.where(inner, near, skip), z ^ 3)
 
 
-EARLY = tuple((j, flip) for j in range(3) for flip in range(4))
-LATE = tuple((3, flip) for flip in range(4))
+EARLY = tuple((j, flip) for j in (0, 1, 2) for flip in (0, 2))
+MEDIUM = tuple((j, flip) for j in (0, 1, 2) for flip in (1, 3))
+LATE = tuple((3, flip) for flip in (0, 2, 1, 3))
 
 
 def plan_kernel(layout, blocks, rows, cols, count, tiles, mine, note, seen, buffer, sems):
@@ -152,7 +155,7 @@
         for flip in (1, 2, 3):
             for r in range(cap):
                 table[layout.pack(j, flip) + r] = asked[flip * LANES + (zs[j] * 4 + yc) * cap + r]
-    for i, (j, flip) in enumerate(EARLY + LATE):
+    for i, (j, flip) in enumerate(EARLY + MEDIUM + LATE):
         for r in range(cap):
             key = (zs[j] * 4 + (yc ^ flip)) * cap + r
             at = layout.entry(i * cap + r)
@@ -171,42 +174,74 @@
     )(mine, asked)
 
 
-def copy_blocks(table, at, cap, shard, out):
+def copy_asked(table, at, cap, shard, out, first=0):
     for r in range(cap):
-        out[r] = shard[table[at + r]]
-
-
-def pack_shard_kernel(layout, j, table, shard, *refs):
-    outs = refs[-3:]
-    for flip in (1, 2, 3):
-        copy_blocks(table, layout.pack(j, flip), layout.cap, shard, outs[flip - 1])
-
-
-def pack_second_kernel(layout, table, asked, first, second, *refs):
-    here, far = refs[-7:-4], refs[-4:]
-    cap = layout.cap
-    z, yc, inner, _ = whereabouts()
-    for flip in (1, 2, 3):
-        copy_blocks(table, layout.pack(2, flip), cap, second, here[flip - 1])
-
-    def send(shard):
-        for flip in range(4):
-            copy_blocks(asked, flip * LANES + ((z ^ 2) * 4 + yc) * cap, cap, shard, far[flip])
-
-    pl.when(inner)(lambda: send(first))
-    pl.when(jnp.logical_not(inner))(lambda: send(second))
-
-
-def pack(kernel, cap, number, tables, shards):
-    _, tile, repl = shards[0].shape
+        out[first + r] = shard[table[at + r]]
+
+
+def copy_half(cap, source, half, out, first=0):
+    for r in range(cap):
+        out[first + r] = source[half * cap + r]
+
+
+def fill_across_y(layout, j, table, shard, out):
+    copy_asked(table, layout.pack(j, 2), layout.cap, shard, out)
+    copy_asked(table, layout.pack(j, 3), layout.cap, shard, out, layout.cap)
+
+
+def fill_far(layout, asked, z, shard, same_y, other_y):
+    cap = layout.cap
+    _, yc, _, _ = whereabouts()
+    for flip, out in enumerate((same_y, same_y, other_y, other_y)):
+        copy_asked(asked, flip * LANES + (z * 4 + yc) * cap, cap, shard, out, flip % 2 * cap)
+
+
+def across_y_kernel(layout, j, table, shard, out):
+    fill_across_y(layout, j, table, shard, out)
+
+
+def outward_kernel(layout, asked, first, same_y, other_y):
+    fill_far(layout, asked, whereabouts()[0] ^ 2, first, same_y, other_y)
+
+
+def middle_kernel(layout, asked, own, same_y, other_y):
+    fill_far(layout, asked, whereabouts()[0], own, same_y, other_y)
+
+
+def core_kernel(layout, table, *refs):
+    cap = layout.cap
+    out = refs[6]
+    for j in range(3):
+        copy_asked(table, layout.pack(j, 1), cap, refs[j], out, 2 * j * cap)
+        copy_half(cap, refs[3 + j], 1, out, (2 * j + 1) * cap)
+
+
+def by_place(pairs, use):
+    inner = whereabouts()[2]
+    pl.when(inner)(lambda: use(*pairs[:2]))
+    pl.when(jnp.logical_not(inner))(lambda: use(*pairs[2:]))
+
+
+def core_late_kernel(layout, mid_same, mid_other, out_same, out_other, out):
+    cap = layout.cap
+
+    def use(same_y, other_y):
+        copy_half(cap, same_y, 1, out)
+        copy_half(cap, other_y, 1, out, cap)
+
+    by_place((mid_same, mid_other, out_same, out_other), use)
+
+
+def pack(kernel, sizes, tables, arrays):
+    _, tile, repl = arrays[0].shape
     return pl.pallas_call(
         kernel,
-        out_shape=[jax.ShapeDtypeStruct((cap, tile, repl), jnp.bfloat16)] * number,
-        in_specs=[SMEM] * len(tables) + [VMEM] * len(shards),
-        out_specs=[VMEM] * number,
+        out_shape=[jax.ShapeDtypeStruct((size, tile, repl), jnp.bfloat16) for size in sizes],
+        in_specs=[SMEM] * len(tables) + [VMEM] * len(arrays),
+        out_specs=[VMEM] * len(sizes),
         compiler_params=params(),
         cost_estimate=pl.CostEstimate(flops=0, bytes_accessed=0, transcendentals=0),
-    )(*tables, *shards)
+    )(*tables, *arrays)
 
 
 def multiply(layout, table, tiles, xbuf, first, number, field):
@@ -228,52 +263,54 @@
             some(first + g * GROUP, g * GROUP)
 
 
+def take_own(layout, table, first, shard, xbuf, place):
+    for r in range(layout.cap):
+        xbuf[place + r] = shard[table[layout.entry(first + r) + 2]]
+
+
 def early_kernel(layout, table, tiles, *refs):
-    sources, (field, xbuf) = refs[: len(EARLY)], refs[len(EARLY) :]
-    cap = layout.cap
-    for i, ((_, flip), source) in enumerate(zip(EARLY, sources)):
-        for r in range(cap):
-            e = i * cap + r
-            xbuf[e] = source[table[layout.entry(e) + 2]] if flip == 0 else source[r]
+    cap = layout.cap
+    field, xbuf = refs[6:]
+    for j in range(3):
+        take_own(layout, table, 2 * j * cap, refs[j], xbuf, 2 * j * cap)
+        copy_half(cap, refs[3 + j], 0, xbuf, (2 * j + 1) * cap)
     field[...] = jnp.zeros_like(field)
-    multiply(layout, table, tiles, xbuf, 0, len(EARLY) * cap, field)
-
-
-def cost(entries, tile, repl, more=0):
-    return pl.CostEstimate(
-        flops=2 * entries * tile * tile * repl,
-        bytes_accessed=entries * tile * (tile + repl) * 2 + more,
-        transcendentals=0,
-    )
-
-
-def early(layout, table, tiles, sources):
-    tile = tiles.shape[1]
-    blocks, _, repl = sources[0].shape
-    entries = len(EARLY) * layout.cap
+    multiply(layout, table, tiles, xbuf, 0, 6 * cap, field)
+
+
+def medium_kernel(layout, table, tiles, core, before, field):
+    field[...] = before[...]
+    multiply(layout, table, tiles, core, 6 * layout.cap, 6 * layout.cap, field)
+
+
+def products(kernel, layout, scratch, table, tiles, arrays, blocks):
+    tile, repl = arrays[0].shape[1:]
     return pl.pallas_call(
-        functools.partial(early_kernel, layout),
+        functools.partial(kernel, layout),
         out_shape=jax.ShapeDtypeStruct((blocks + 1, tile, repl), jnp.float32),
-        in_specs=[SMEM] + [VMEM] * (1 + len(sources)),
+        in_specs=[SMEM] + [VMEM] * (1 + len(arrays)),
         out_specs=VMEM,
-        scratch_shapes=[pltpu.VMEM((entries, tile, repl), jnp.bfloat16)],
+        scratch_shapes=[pltpu.VMEM((size, tile, repl), jnp.bfloat16) for size in scratch],
         compiler_params=params(),
         cost_estimate=pl.CostEstimate(flops=0, bytes_accessed=0, transcendentals=0),
-    )(table, tiles, *sources)
-
-
-def late_kernel(layout, last, table, scalars, tiles, far0, far1, far2, far3, field, xpos, ymom, *refs):
-    if last:
-        xout, yout, energy, xbuf, acc = refs
-    else:
-        xout, yout, xb, out1, out2, out3, xbuf, acc = refs
+    )(table, tiles, *arrays)
+
+
+def late_kernel(layout, last, table, asked, scalars, tiles, *refs):
+    far, (core, field, xpos, ymom), outs, (xbuf, acc) = refs[:4], refs[4:8], refs[8:-2], refs[-2:]
+    xout, yout = outs[:2]
     blocks = xpos.shape[0]
     cap = layout.cap
-    for i, far in enumerate((far0, far1, far2, far3)):
-        for r in range(cap):
-            xbuf[i * cap + r] = far[r]
+
+    def use(same_y, other_y):
+        copy_half(cap, same_y, 0, xbuf)
+        copy_half(cap, other_y, 0, xbuf, cap)
+
+    by_place(far, use)
+    copy_half(cap, core, 0, xbuf, 2 * cap)
+    copy_half(cap, core, 1, xbuf, 3 * cap)
     acc[...] = field[...]
-    multiply(layout, table, tiles, xbuf, len(EARLY) * cap, len(LATE) * cap, acc)
+    multiply(layout, table, tiles, xbuf, 12 * cap, 4 * cap, acc)
     total = jnp.zeros((1, xpos.shape[2]), jnp.float32)
     for b in range(blocks):
         x, h = xpos[b], acc[b]
@@ -283,40 +320,45 @@
         xout[b] = x
         yout[b] = y
         if not last:
-            xb[b] = x.astype(jnp.bfloat16)
+            outs[2][b] = x.astype(jnp.bfloat16)
     if last:
-        energy[...] = -0.5 * total
+        outs[2][...] = -0.5 * total
     else:
-        for flip, out in ((1, out1), (2, out2), (3, out3)):
-            copy_blocks(table, layout.pack(0, flip), cap, xb, out)
-
-
-def late(layout, last, table, scalars, tiles, packs, field, xpos, ymom):
+        xb, y0, same_y, other_y = outs[2:]
+        fill_across_y(layout, 0, table, xb, y0)
+        fill_far(layout, asked, whereabouts()[0], xb, same_y, other_y)
+
+
+def late(layout, last, table, asked, scalars, tiles, far, core, field, xpos, ymom):
     tile = tiles.shape[1]
     blocks, _, repl = xpos.shape
-    entries = len(LATE) * layout.cap
+    entries = 4 * layout.cap
     state = jax.ShapeDtypeStruct(xpos.shape, jnp.float32)
     if last:
         extra = (jax.ShapeDtypeStruct((1, repl), jnp.float32),)
     else:
-        out = jax.ShapeDtypeStruct((layout.cap, tile, repl), jnp.bfloat16)
+        out = jax.ShapeDtypeStruct((2 * layout.cap, tile, repl), jnp.bfloat16)
         extra = (jax.ShapeDtypeStruct(xpos.shape, jnp.bfloat16), out, out, out)
     return pl.pallas_call(
         functools.partial(late_kernel, layout, last),
         out_shape=(state, state) + extra,
-        in_specs=[SMEM, SMEM] + [VMEM] * (1 + len(packs) + 3),
+        in_specs=[SMEM] * 3 + [VMEM] * (1 + len(far) + 4),
         out_specs=(VMEM,) * (2 + len(extra)),
         scratch_shapes=[
             pltpu.VMEM((entries, tile, repl), jnp.bfloat16),
             pltpu.VMEM((blocks + 1, tile, repl), jnp.float32),
         ],
         compiler_params=params(),
-        cost_estimate=cost(entries, tile, repl, 20 * xpos.size),
-    )(table, scalars, tiles, *packs, field, xpos, ymom)
-
-
-def along_z(pairs, value):
-    return lax.ppermute(value, "row", [(a * 4 + i, b * 4 + i) for a, b in pairs for i in range(4)])
+        cost_estimate=pl.CostEstimate(
+            flops=2 * entries * tile * tile * repl,
+            bytes_accessed=entries * tile * (tile + repl) * 2 + 20 * xpos.size,
+            transcendentals=0,
+        ),
+    )(table, asked, scalars, tiles, *far, core, field, xpos, ymom)
+
+
+def along_z(pairs, value, flip=0):
+    return lax.ppermute(value, "row", [(a * 4 + i, b * 4 + (i ^ flip)) for a, b in pairs for i in range(4)])
 
 
 def across(flip, value):
@@ -336,44 +378,59 @@
     cap = (slots + 15) // 16
     order = blocks * tile * 16
     layout = Layout(cap)
-    pack_own = functools.partial(pack_shard_kernel, layout, 0)
-    pack_first = functools.partial(pack_shard_kernel, layout, 1)
-    pack_second = functools.partial(pack_second_kernel, layout)
+
+    def across_y(j, shard):
+        return pack(functools.partial(across_y_kernel, layout, j), [2 * cap], [table], [shard])[0]
+
+    def far_packs(kernel, asked, shard):
+        return pack(functools.partial(kernel, layout), [2 * cap] * 2, [asked], [shard])
+
+    def to_core(kernel, size, tables, arrays):
+        return across(1, pack(functools.partial(kernel, layout), [size * cap], tables, arrays)[0])
+
     xpos = positions.reshape(blocks, tile, repl)
     ymom = momenta.reshape(blocks, tile, repl)
     own0 = xpos.astype(jnp.bfloat16)
     mine, note = plan(layout, blocks, tile_rows, tile_cols, counts, tiles)
     notes = jnp.concatenate([note] + [across(flip, note) for flip in (1, 2, 3)])
     table = make_table(layout, mine, notes.astype(jnp.int32).reshape(-1))
-    packs0 = pack(pack_own, cap, 3, [table], [own0])
-    asked = coeff = None
+    y0 = across_y(0, own0)
     for step in range(STEPS):
         last = step == STEPS - 1
         own1 = along_z(FIRST, own0)
         own2 = along_z(SECOND, own0)
-        got0 = [across(flip, packs0[flip - 1]) for flip in (1, 2, 3)]
+        y0 = across(2, y0)
         if step == 0:
-            notes, got0 = lax.optimization_barrier((notes, got0))
-            far_notes = across(4, notes)
-            asked = far_notes.astype(jnp.int32).reshape(-1)
-        own1, got0 = lax.optimization_barrier((own1, got0))
-        packs1 = pack(pack_first, cap, 3, [table], [own1])
-        got1 = [across(flip, packs1[flip - 1]) for flip in (1, 2, 3)]
+            notes, y0 = lax.optimization_barrier((notes, y0))
+            plane = jnp.broadcast_to(jnp.sum(notes[:, SUM_AT]), (1, LANES))
+            notes_out, notes_mid, plane_skip = across(4, notes), across(12, notes), across(8, plane)
+            notes_out, notes_mid, plane_skip = lax.optimization_barrier((notes_out, notes_mid, plane_skip))
+            asked_out = notes_out.astype(jnp.int32).reshape(-1)
+            asked_mid = notes_mid.astype(jnp.int32).reshape(-1)
+            mid = far_packs(middle_kernel, asked_mid, own0)
+        mid = [along_z(MIDDLE, mid[0]), along_z(MIDDLE, mid[1], 2)]
+        own1, y0 = lax.optimization_barrier((own1, y0))
+        y1 = across(2, across_y(1, own1))
+        out_same, out_other = far_packs(outward_kernel, asked_out, own1)
+        out_same = along_z(OUTWARD, out_same)
+        own2, out_other, y1 = lax.optimization_barrier((own2, out_other, y1))
+        out_other = along_z(OUTWARD, out_other, 2)
+        y2 = across(2, across_y(2, own2))
+        out_other, y2, out_same, mid = lax.optimization_barrier((out_other, y2, out_same, mid))
+        here = [own0, own1, own2, y0, y1, y2]
+        core = to_core(core_kernel, 6, [table], here)
+        far = mid + [out_same, out_other]
+        core_late = to_core(core_late_kernel, 2, [], far)
+        field = products(early_kernel, layout, [6 * cap], table, tiles, here, blocks)
+        field = products(medium_kernel, layout, [], table, tiles, [core, field], blocks)
         if step == 0:
-            half = jnp.broadcast_to(jnp.sum(notes[:, SUM_AT]) + jnp.sum(far_notes[:, SUM_AT]), (1, LANES))
-            total = jnp.sum((half + across(8, half))[0, 0])
+            total = plane[0, 0] + plane_skip[0, 0] + jnp.sum(notes_out[:, SUM_AT]) + jnp.sum(notes_mid[:, SUM_AT])
             coeff = 0.7 * jnp.sqrt((order - 1) / total)
-        own2, got1 = lax.optimization_barrier((own2, got1))
-        packs2 = pack(pack_second, cap, 7, [table, asked], [own1, own2])
-        got2 = [across(flip, packs2[flip - 1]) for flip in (1, 2, 3)]
-        far = [across(4 + flip, packs2[3 + flip]) for flip in range(4)]
-        sources = [own0] + got0 + [own1] + got1 + [own2] + got2
-        field = early(layout, table, tiles, sources)
         scalars = jnp.stack([jnp.float32(0.4 - 0.1 * step), coeff])
-        outs = late(layout, last, table, scalars, tiles, far, field, xpos, ymom)
+        outs = late(layout, last, table, asked_mid, scalars, tiles, far, core_late, field, xpos, ymom)
         xpos, ymom = outs[0], outs[1]
         if not last:
-            own0, packs0 = outs[2], outs[3:]
+            own0, y0, mid = outs[2], outs[3], outs[4:]
     energy = row_sum(outs[2])
     return (xpos.reshape(positions.shape), ymom.reshape(momenta.shape), energy.reshape(repl))
 

time: 240 us -> 272 us (1.13)
  waiting for transfers between devices: 126 us -> 146 us
  blocking collectives: 9.37 us -> 18.4 us
  starting transfers between devices: 59.6 us -> 50.6 us
  Pallas kernels: 32.5 us -> 39.9 us
    ppermute x8 -> x24, waiting for transfers between devices: 34.5 us -> 77.5 us  [along_z(): lax.ppermute(value, 'row', [(a * 4 + i, b * 4 + (i ^ flip)) for a, b in p...]
    ppermute x57 -> x26, starting transfers between devices: 49.3 us -> 16.9 us  [across(): return lax.ppermute(value, 'row', [(i, i ^ flip) for i in range(16)])]
    ppermute x8 -> x24, starting transfers between devices: 10.3 us -> 33.7 us  [along_z(): lax.ppermute(value, 'row', [(a * 4 + i, b * 4 + (i ^ flip)) for a, b in p...]
    ppermute x57 -> x26, waiting for transfers between devices: 92 us -> 68.7 us  [across(): return lax.ppermute(value, 'row', [(i, i ^ flip) for i in range(16)])]
    all_to_all x1, blocking collectives: 9.37 us -> 18.4 us  [row_sum(): lax.all_to_all(spread, 'row', split_axis=0, concat_axis=0, tiled=True)]
    pallas_call x13 -> x30, Pallas kernels: 18.8 us -> 25.2 us  [the longest x22 13 us: pack(): pl.pallas_call(kernel, out_shape=[jax.ShapeDtypeStruct((size, tile, repl)...]
    unnamed x20 -> x26, local copies, waits for them, and re-layouts: 4.2 us -> 5.48 us
  transfers between devices with their start and end apart: 65 -> 50, of which waited for: 34 -> 24; matrix products, arithmetic and copies ran while one was open for 1% -> 2% of each run, Pallas kernels for 9% -> 10%
where the time goes in v8:
time: 272 us; the launch traced here: 271 us
  waiting for transfers between devices  146 us (54%)
  starting transfers between devices  50.6 us (19%)
  Pallas kernels  39.9 us (15%)
  blocking collectives  18.4 us (7%)
  local copies, waits for them, and re-layouts  6.14 us (2%)
  other arithmetic  5.41 us (2%)
  between operations  4.5 us (2%)
    ppermute x24, waiting for transfers between devices, along_z(): lax.ppermute(value, 'row', [(a * 4 + i, b * 4 + (i ^ flip)) for a, b in p...  77.5 us
    ppermute x26, waiting for transfers between devices, across(): return lax.ppermute(value, 'row', [(i, i ^ flip) for i in range(16)])  68.7 us
    ppermute x24, starting transfers between devices, along_z(): lax.ppermute(value, 'row', [(a * 4 + i, b * 4 + (i ^ flip)) for a, b in p...  33.7 us
    all_to_all x1, blocking collectives, row_sum(): lax.all_to_all(spread, 'row', split_axis=0, concat_axis=0, tiled=True)  18.4 us
    ppermute x26, starting transfers between devices, across(): return lax.ppermute(value, 'row', [(i, i ^ flip) for i in range(16)])  16.9 us
    pallas_call x22, Pallas kernels, pack(): pl.pallas_call(kernel, out_shape=[jax.ShapeDtypeStruct((size, tile, repl)...  13 us
    pallas_call x8, Pallas kernels, products(): pl.pallas_call(functools.partial(kernel, layout), out_shape=jax.ShapeDtyp...  12.1 us
    pallas_call x4, Pallas kernels, late(): pl.pallas_call(functools.partial(late_kernel, layout, last), out_shape=(s...  8.94 us
  transfers between devices with their start and end apart: 50, of which 24 were waited for; matrix products, arithmetic and copies ran while one was open for 2% of the time, Pallas kernels for 10%

profile of v8, /device:TPU:0, one launch (start us, length us, event | category | flops | bytes accessed | tf_op | source)
XLA Modules:
  0.0 271.2 jit_solution(6245643964443175862)
XLA Ops:
  1.9 4.1 %collective-permute-start.8 = (bf16[8,256,128]{2,1,0:T(8,128)(2,1)S(1)}, bf16[8,256,128]{2,1,0:T(8,128)(2,1)S(1)}, u32[]{:S(2)}, u32[]{:S(2)}) collective-permute-start(bf16[8,256,128]{2,1,0:T(8,128)(2,1)S(1)} %convert_element_type.18.shard.own.refs_0_), channel_id=1, source_target_pairs={{0,8},{1,9},{2,10},{3,11},{12,4},{13,5},{14,6},{15,7},{4,0},{5,1},... | collective-permute-start | bytes 1572872 | tf_op jit(solution)/shard_map/ppermute | solution.py:361
  6.7 4.3 %shard_map.85 = (s32[144]{0:T(256)}, f32[1,128]{1,0:T(1,128)}) custom-call(s32[48]{0:T(128)} %rows.1, s32[48]{0:T(128)} %cols.1, s32[1]{0:T(128)S(6)} %copy.10.count, bf16[48,256,256]{2,1,0:T(8,128)(2,1)} %tiles.25), custom_call_target="tpu_custom_call" | custom-call | tf_op jit(solution)/shard_map/pallas_call | solution.py:132
  12.9 1.9 collective-permute-done.1
  20.3 10.8 %collective-permute-done.3.refs_3_ = bf16[6,256,128]{2,1,0:T(8,128)(2,1)S(1)} collective-permute-done((bf16[6,256,128]{2,1,0:T(8,128)(2,1)S(1)}, bf16[6,256,128]{2,1,0:T(8,128)(2,1)S(1)}, u32[]{:S(2)}, u32[]{:S(2)}) %collective-permute-start.3) | collective-permute-done | bytes 393248 | tf_op jit(solution)/shard_map/ppermute | solution.py:365
  32.5 2.9 %collective-permute-start.5 = (f32[4,128]{1,0:T(4,128)S(1)}, f32[4,128]{1,0:T(4,128)S(1)}, u32[]{:S(2)}, u32[]{:S(2)}) collective-permute-start(f32[4,128]{1,0:T(4,128)S(1)} %get-tuple-element.83), channel_id=1, source_target_pairs={{0,12},{1,13},{2,14},{3,15},{4,8},{5,9},{6,10},{7,11},{8,4},{9,5},... | collective-permute-start | bytes 6152 | tf_op jit(solution)/shard_map/ppermute | solution.py:365
  37.3 3.8 %collective-permute-done.6 = f32[1,128]{1,0:T(1,128)S(1)} collective-permute-done((f32[1,128]{1,0:T(1,128)S(1)}, f32[1,128]{1,0:T(1,128)S(1)}, u32[]{:S(2)}, u32[]{:S(2)}) %collective-permute-start.6) | collective-permute-done | bytes 544 | tf_op jit(solution)/shard_map/ppermute | solution.py:365
  48.7 11.3 %collective-permute-done.12.out_same.refs_2_ = bf16[6,256,128]{2,1,0:T(8,128)(2,1)S(1)} collective-permute-done((bf16[6,256,128]{2,1,0:T(8,128)(2,1)S(1)}, bf16[6,256,128]{2,1,0:T(8,128)(2,1)S(1)}, u32[]{:S(2)}, u32[]{:S(2)}) %collective-permute-start.12) | collective-permute-done | bytes 393248 | tf_op jit(solution)/shard_map/ppermute | solution.py:361
  60.1 4.7 %collective-permute-done.10.out_other.refs_3_ = bf16[6,256,128]{2,1,0:T(8,128)(2,1)S(1)} collective-permute-done((bf16[6,256,128]{2,1,0:T(8,128)(2,1)S(1)}, bf16[6,256,128]{2,1,0:T(8,128)(2,1)S(1)}, u32[]{:S(2)}, u32[]{:S(2)}) %collective-permute-start.10) | collective-permute-done | bytes 393248 | tf_op jit(solution)/shard_map/ppermute | solution.py:361
  64.8 1.7 shard_map.93
  71.7 2.8 %copy-done = bf16[48,256,256]{2,1,0:T(8,128)(2,1)S(1)} copy-done((bf16[48,256,256]{2,1,0:T(8,128)(2,1)S(1)}, bf16[48,256,256]{2,1,0:T(8,128)(2,1)}, u32[]{:S(2)}) %copy-start) | copy-done | bytes 6291480
  78.0 2.2 shard_map.95.refs_5_
  80.2 2.3 shard_map.96
  82.6 3.1 %collective-permute-start.18 = (bf16[8,256,128]{2,1,0:T(8,128)(2,1)S(1)}, bf16[8,256,128]{2,1,0:T(8,128)(2,1)S(1)}, u32[]{:S(2)}, u32[]{:S(2)}) collective-permute-start(bf16[8,256,128]{2,1,0:T(8,128)(2,1)S(1)} %get-tuple-element.102.refs_0_), channel_id=1, source_target_pairs={{0,8},{1,9},{2,10},{3,11},{12,4},{13,5},{14,6},{15,7},{4,0},{5,1},... | collective-permute-start | bytes 1572872 | tf_op jit(solution)/shard_map/ppermute | solution.py:361
  86.4 10.1 %collective-permute-done.19.refs_3_ = bf16[6,256,128]{2,1,0:T(8,128)(2,1)S(1)} collective-permute-done((bf16[6,256,128]{2,1,0:T(8,128)(2,1)S(1)}, bf16[6,256,128]{2,1,0:T(8,128)(2,1)S(1)}, u32[]{:S(2)}, u32[]{:S(2)}) %collective-permute-start.19) | collective-permute-done | bytes 393248 | tf_op jit(solution)/shard_map/ppermute | solution.py:365
  102.7 7.6 %collective-permute-done.17.shard.refs_2_ = bf16[8,256,128]{2,1,0:T(8,128)(2,1)S(1)} collective-permute-done((bf16[8,256,128]{2,1,0:T(8,128)(2,1)S(1)}, bf16[8,256,128]{2,1,0:T(8,128)(2,1)S(1)}, u32[]{:S(2)}, u32[]{:S(2)}) %collective-permute-start.17) | collective-permute-done | bytes 524320 | tf_op jit(solution)/shard_map/ppermute | solution.py:361
  112.7 7.7 %collective-permute-done.23.out_same.refs_2_ = bf16[6,256,128]{2,1,0:T(8,128)(2,1)S(1)} collective-permute-done((bf16[6,256,128]{2,1,0:T(8,128)(2,1)S(1)}, bf16[6,256,128]{2,1,0:T(8,128)(2,1)S(1)}, u32[]{:S(2)}, u32[]{:S(2)}) %collective-permute-start.23) | collective-permute-done | bytes 393248 | tf_op jit(solution)/shard_map/ppermute | solution.py:361
  120.3 9.9 %collective-permute-done.22.refs_5_ = bf16[6,256,128]{2,1,0:T(8,128)(2,1)S(1)} collective-permute-done((bf16[6,256,128]{2,1,0:T(8,128)(2,1)S(1)}, bf16[6,256,128]{2,1,0:T(8,128)(2,1)S(1)}, u32[]{:S(2)}, u32[]{:S(2)}) %collective-permute-start.22) | collective-permute-done | bytes 393248 | tf_op jit(solution)/shard_map/ppermute | solution.py:365
  135.2 1.8 shard_map.104
  137.6 1.9 collective-permute-start.28
  139.5 8.7 %collective-permute-done.30.refs_3_ = bf16[6,256,128]{2,1,0:T(8,128)(2,1)S(1)} collective-permute-done((bf16[6,256,128]{2,1,0:T(8,128)(2,1)S(1)}, bf16[6,256,128]{2,1,0:T(8,128)(2,1)S(1)}, u32[]{:S(2)}, u32[]{:S(2)}) %collective-permute-start.30) | collective-permute-done | bytes 393248 | tf_op jit(solution)/shard_map/ppermute | solution.py:365
  148.2 2.8 %collective-permute-done.29.first.shard.refs_1_ = bf16[8,256,128]{2,1,0:T(8,128)(2,1)S(1)} collective-permute-done((bf16[8,256,128]{2,1,0:T(8,128)(2,1)S(1)}, bf16[8,256,128]{2,1,0:T(8,128)(2,1)S(1)}, u32[]{:S(2)}, u32[]{:S(2)}) %collective-permute-start.29) | collective-permute-done | bytes 524320 | tf_op jit(solution)/shard_map/ppermute | solution.py:361
  155.5 7.5 %collective-permute-done.28.shard.refs_2_ = bf16[8,256,128]{2,1,0:T(8,128)(2,1)S(1)} collective-permute-done((bf16[8,256,128]{2,1,0:T(8,128)(2,1)S(1)}, bf16[8,256,128]{2,1,0:T(8,128)(2,1)S(1)}, u32[]{:S(2)}, u32[]{:S(2)}) %collective-permute-start.28) | collective-permute-done | bytes 524320 | tf_op jit(solution)/shard_map/ppermute | solution.py:361
  165.7 12.1 %collective-permute-done.34.out_same.refs_2_ = bf16[6,256,128]{2,1,0:T(8,128)(2,1)S(1)} collective-permute-done((bf16[6,256,128]{2,1,0:T(8,128)(2,1)S(1)}, bf16[6,256,128]{2,1,0:T(8,128)(2,1)S(1)}, u32[]{:S(2)}, u32[]{:S(2)}) %collective-permute-start.34) | collective-permute-done | bytes 393248 | tf_op jit(solution)/shard_map/ppermute | solution.py:361
  177.7 5.3 %collective-permute-done.33.refs_5_ = bf16[6,256,128]{2,1,0:T(8,128)(2,1)S(1)} collective-permute-done((bf16[6,256,128]{2,1,0:T(8,128)(2,1)S(1)}, bf16[6,256,128]{2,1,0:T(8,128)(2,1)S(1)}, u32[]{:S(2)}, u32[]{:S(2)}) %collective-permute-start.33) | collective-permute-done | bytes 393248 | tf_op jit(solution)/shard_map/ppermute | solution.py:365
  188.0 1.8 shard_map.112
  189.7 8.7 %collective-permute-start.40 = (bf16[8,256,128]{2,1,0:T(8,128)(2,1)S(1)}, bf16[8,256,128]{2,1,0:T(8,128)(2,1)S(1)}, u32[]{:S(2)}, u32[]{:S(2)}) collective-permute-start(bf16[8,256,128]{2,1,0:T(8,128)(2,1)S(1)} %get-tuple-element.138.refs_0_), channel_id=1, source_target_pairs={{0,8},{1,9},{2,10},{3,11},{12,4},{13,5},{14,6},{15,7},{4,0},{5,1},... | collective-permute-start | bytes 1572872 | tf_op jit(solution)/shard_map/ppermute | solution.py:361
  199.3 10.1 %collective-permute-done.41.refs_3_ = bf16[6,256,128]{2,1,0:T(8,128)(2,1)S(1)} collective-permute-done((bf16[6,256,128]{2,1,0:T(8,128)(2,1)S(1)}, bf16[6,256,128]{2,1,0:T(8,128)(2,1)S(1)}, u32[]{:S(2)}, u32[]{:S(2)}) %collective-permute-start.41) | collective-permute-done | bytes 393248 | tf_op jit(solution)/shard_map/ppermute | solution.py:365
  215.5 8.6 %collective-permute-done.39.shard.refs_2_ = bf16[8,256,128]{2,1,0:T(8,128)(2,1)S(1)} collective-permute-done((bf16[8,256,128]{2,1,0:T(8,128)(2,1)S(1)}, bf16[8,256,128]{2,1,0:T(8,128)(2,1)S(1)}, u32[]{:S(2)}, u32[]{:S(2)}) %collective-permute-start.39) | collective-permute-done | bytes 524320 | tf_op jit(solution)/shard_map/ppermute | solution.py:361
  226.8 12.1 %collective-permute-done.45.out_same.refs_2_ = bf16[6,256,128]{2,1,0:T(8,128)(2,1)S(1)} collective-permute-done((bf16[6,256,128]{2,1,0:T(8,128)(2,1)S(1)}, bf16[6,256,128]{2,1,0:T(8,128)(2,1)S(1)}, u32[]{:S(2)}, u32[]{:S(2)}) %collective-permute-start.45) | collective-permute-done | bytes 393248 | tf_op jit(solution)/shard_map/ppermute | solution.py:361
  238.9 5.3 %collective-permute-done.44.refs_5_ = bf16[6,256,128]{2,1,0:T(8,128)(2,1)S(1)} collective-permute-done((bf16[6,256,128]{2,1,0:T(8,128)(2,1)S(1)}, bf16[6,256,128]{2,1,0:T(8,128)(2,1)S(1)}, u32[]{:S(2)}, u32[]{:S(2)}) %collective-permute-start.44) | collective-permute-done | bytes 393248 | tf_op jit(solution)/shard_map/ppermute | solution.py:365
  249.1 3.1 %shard_map.120 = (f32[8,256,128]{2,1,0:T(8,128)}, f32[8,256,128]{2,1,0:T(8,128)}, f32[1,128]{1,0:T(1,128)S(1)}) custom-call(s32[171]{0:T(256)S(1)} %copy-done.8, s32[512]{0:T(512)S(1)} %get-tuple-element.162.asked, f32[2]{0:T(128)S(1)} %pad_maximum_fusion.1.scalars, bf16[48,256,256]{2,1,0:T(8,128)(2,1)S(1)} %bitcast.16, ...), custom_call_target="tpu_custom_call" | custom-call | flops 201326592 | bytes 7602176 | tf_op jit(solution)/shard_map/pallas_call | solution.py:342
  252.2 18.4 %all_to_all.6 = f32[16,1,128]{2,1,0:T(1,128)S(1)} all-to-all(f32[16,1,128]{2,1,0:T(1,128)S(1)} %broadcast_in_dim.9), channel_id=1, replica_groups=mesh['groups'=2,'row'=16] {'row'}, dimensions={0} | all-to-all | bytes 16384 | tf_op jit(solution)/shard_map/all_to_all | solution.py:371
  (144 shorter events, 67.2 us)
Async XLA Ops:
  1.9 29.2 %collective-permute-start.8 = (bf16[8,256,128]{2,1,0:T(8,128)(2,1)S(1)}, bf16[8,256,128]{2,1,0:T(8,128)(2,1)S(1)}, u32[]{:S(2)}, u32[]{:S(2)}) collective-permute-start(bf16[8,256,128]{2,1,0:T(8,128)(2,1)S(1)} %convert_element_type.18.shard.own.refs_0_), channel_id=1, source_target_pairs={{0,8},{1,9},{2,10},{3,11},{12,4},{13,5},{14,6},{15,7},{4,0},{5,1},... | collective-permute-start | bytes 1572872 | tf_op jit(solution)/shard_map/ppermute | solution.py:361
  19.6 11.5 %collective-permute-start.3 = (bf16[6,256,128]{2,1,0:T(8,128)(2,1)S(1)}, bf16[6,256,128]{2,1,0:T(8,128)(2,1)S(1)}, u32[]{:S(2)}, u32[]{:S(2)}) collective-permute-start(bf16[6,256,128]{2,1,0:T(8,128)(2,1)S(1)} %shard_map.87), channel_id=1, source_target_pairs={{0,2},{1,3},{2,0},{3,1},{4,6},{5,7},{6,4},{7,5},{8,10},{9,11},{10,... | collective-permute-start | bytes 1179656 | tf_op jit(solution)/shard_map/ppermute | solution.py:365
  20.3 24.9 %collective-permute-start.7 = (bf16[8,256,128]{2,1,0:T(8,128)(2,1)S(1)}, bf16[8,256,128]{2,1,0:T(8,128)(2,1)S(1)}, u32[]{:S(2)}, u32[]{:S(2)}) collective-permute-start(bf16[8,256,128]{2,1,0:T(8,128)(2,1)S(1)} %convert_element_type.18.shard.own.refs_0_), channel_id=1, source_target_pairs={{0,4},{1,5},{2,6},{3,7},{12,8},{13,9},{14,10},{15,11},{4,12},{5,13... | collective-permute-start | bytes 1572872 | tf_op jit(solution)/shard_map/ppermute | solution.py:361
  31.7 13.5 %collective-permute-start.9 = (bf16[6,256,128]{2,1,0:T(8,128)(2,1)S(1)}, bf16[6,256,128]{2,1,0:T(8,128)(2,1)S(1)}, u32[]{:S(2)}, u32[]{:S(2)}) collective-permute-start(bf16[6,256,128]{2,1,0:T(8,128)(2,1)S(1)} %shard_map.89), channel_id=1, source_target_pairs={{0,2},{1,3},{2,0},{3,1},{4,6},{5,7},{6,4},{7,5},{8,10},{9,11},{10,... | collective-permute-start | bytes 1179656 | tf_op jit(solution)/shard_map/ppermute | solution.py:365
  43.9 16.2 %collective-permute-start.12 = (bf16[6,256,128]{2,1,0:T(8,128)(2,1)S(1)}, bf16[6,256,128]{2,1,0:T(8,128)(2,1)S(1)}, u32[]{:S(2)}, u32[]{:S(2)}) collective-permute-start(bf16[6,256,128]{2,1,0:T(8,128)(2,1)S(1)} %get-tuple-element.92), channel_id=1, source_target_pairs={{4,0},{5,1},{6,2},{7,3},{8,12},{9,13},{10,14},{11,15},{20,16},{21,... | collective-permute-start | bytes 1179656 | tf_op jit(solution)/shard_map/ppermute | solution.py:361
  45.8 14.2 %collective-permute-start.11 = (bf16[6,256,128]{2,1,0:T(8,128)(2,1)S(1)}, bf16[6,256,128]{2,1,0:T(8,128)(2,1)S(1)}, u32[]{:S(2)}, u32[]{:S(2)}) collective-permute-start(bf16[6,256,128]{2,1,0:T(8,128)(2,1)S(1)} %shard_map.90), channel_id=1, source_target_pairs={{0,2},{1,3},{2,0},{3,1},{4,6},{5,7},{6,4},{7,5},{8,10},{9,11},{10,... | collective-permute-start | bytes 1179656 | tf_op jit(solution)/shard_map/ppermute | solution.py:365
  47.4 17.4 %collective-permute-start.10 = (bf16[6,256,128]{2,1,0:T(8,128)(2,1)S(1)}, bf16[6,256,128]{2,1,0:T(8,128)(2,1)S(1)}, u32[]{:S(2)}, u32[]{:S(2)}) collective-permute-start(bf16[6,256,128]{2,1,0:T(8,128)(2,1)S(1)} %get-tuple-element.90), channel_id=1, source_target_pairs={{4,2},{5,3},{6,0},{7,1},{8,14},{9,15},{10,12},{11,13},{20,18},{21,... | collective-permute-start | bytes 1179656 | tf_op jit(solution)/shard_map/ppermute | solution.py:361
  66.5 11.5 %collective-permute-start.16 = (bf16[18,256,128]{2,1,0:T(8,128)(2,1)}, bf16[18,256,128]{2,1,0:T(8,128)(2,1)}, u32[]{:S(2)}, u32[]{:S(2)}) collective-permute-start(bf16[18,256,128]{2,1,0:T(8,128)(2,1)} %shard_map.93), channel_id=1, source_target_pairs={{0,1},{1,0},{2,3},{3,2},{4,5},{5,4},{6,7},{7,6},{8,9},{9,8},{10,11... | collective-permute-start | bytes 3538952 | tf_op jit(solution)/shard_map/ppermute | solution.py:365
  67.3 12.9 %collective-permute-start.15 = (bf16[6,256,128]{2,1,0:T(8,128)(2,1)}, bf16[6,256,128]{2,1,0:T(8,128)(2,1)}, u32[]{:S(2)}, u32[]{:S(2)}) collective-permute-start(bf16[6,256,128]{2,1,0:T(8,128)(2,1)} %shard_map.92), channel_id=1, source_target_pairs={{0,1},{1,0},{2,3},{3,2},{4,5},{5,4},{6,7},{7,6},{8,9},{9,8},{10,11... | collective-permute-start | bytes 1179656 | tf_op jit(solution)/shard_map/ppermute | solution.py:365
  82.6 15.5 %collective-permute-start.18 = (bf16[8,256,128]{2,1,0:T(8,128)(2,1)S(1)}, bf16[8,256,128]{2,1,0:T(8,128)(2,1)S(1)}, u32[]{:S(2)}, u32[]{:S(2)}) collective-permute-start(bf16[8,256,128]{2,1,0:T(8,128)(2,1)S(1)} %get-tuple-element.102.refs_0_), channel_id=1, source_target_pairs={{0,8},{1,9},{2,10},{3,11},{12,4},{13,5},{14,6},{15,7},{4,0},{5,1},... | collective-permute-start | bytes 1572872 | tf_op jit(solution)/shard_map/ppermute | solution.py:361
  86.4 23.9 %collective-permute-start.17 = (bf16[8,256,128]{2,1,0:T(8,128)(2,1)S(1)}, bf16[8,256,128]{2,1,0:T(8,128)(2,1)S(1)}, u32[]{:S(2)}, u32[]{:S(2)}) collective-permute-start(bf16[8,256,128]{2,1,0:T(8,128)(2,1)S(1)} %get-tuple-element.102.refs_0_), channel_id=1, source_target_pairs={{0,4},{1,5},{2,6},{3,7},{12,8},{13,9},{14,10},{15,11},{4,12},{5,13... | collective-permute-start | bytes 1572872 | tf_op jit(solution)/shard_map/ppermute | solution.py:361
  98.6 11.6 %collective-permute-start.20 = (bf16[6,256,128]{2,1,0:T(8,128)(2,1)S(1)}, bf16[6,256,128]{2,1,0:T(8,128)(2,1)S(1)}, u32[]{:S(2)}, u32[]{:S(2)}) collective-permute-start(bf16[6,256,128]{2,1,0:T(8,128)(2,1)S(1)} %shard_map.98), channel_id=1, source_target_pairs={{0,2},{1,3},{2,0},{3,1},{4,6},{5,7},{6,4},{7,5},{8,10},{9,11},{10,... | collective-permute-start | bytes 1179656 | tf_op jit(solution)/shard_map/ppermute | solution.py:365
  99.4 13.3 %collective-permute-start.24 = (bf16[6,256,128]{2,1,0:T(8,128)(2,1)S(1)}, bf16[6,256,128]{2,1,0:T(8,128)(2,1)S(1)}, u32[]{:S(2)}, u32[]{:S(2)}) collective-permute-start(bf16[6,256,128]{2,1,0:T(8,128)(2,1)S(1)} %get-tuple-element.109), channel_id=1, source_target_pairs={{4,8},{5,9},{6,10},{7,11},{8,4},{9,5},{10,6},{11,7},{20,24},{21,25... | collective-permute-start | bytes 1179656 | tf_op jit(solution)/shard_map/ppermute | solution.py:361
  100.0 12.6 %collective-permute-start.25 = (bf16[6,256,128]{2,1,0:T(8,128)(2,1)S(1)}, bf16[6,256,128]{2,1,0:T(8,128)(2,1)S(1)}, u32[]{:S(2)}, u32[]{:S(2)}) collective-permute-start(bf16[6,256,128]{2,1,0:T(8,128)(2,1)S(1)} %get-tuple-element.110), channel_id=1, source_target_pairs={{4,10},{5,11},{6,8},{7,9},{8,6},{9,7},{10,4},{11,5},{20,26},{21,27... | collective-permute-start | bytes 1179656 | tf_op jit(solution)/shard_map/ppermute | solution.py:361
  101.4 19.0 %collective-permute-start.23 = (bf16[6,256,128]{2,1,0:T(8,128)(2,1)S(1)}, bf16[6,256,128]{2,1,0:T(8,128)(2,1)S(1)}, u32[]{:S(2)}, u32[]{:S(2)}) collective-permute-start(bf16[6,256,128]{2,1,0:T(8,128)(2,1)S(1)} %get-tuple-element.108), channel_id=1, source_target_pairs={{4,0},{5,1},{6,2},{7,3},{8,12},{9,13},{10,14},{11,15},{20,16},{21,... | collective-permute-start | bytes 1179656 | tf_op jit(solution)/shard_map/ppermute | solution.py:361
  110.8 19.4 %collective-permute-start.22 = (bf16[6,256,128]{2,1,0:T(8,128)(2,1)S(1)}, bf16[6,256,128]{2,1,0:T(8,128)(2,1)S(1)}, u32[]{:S(2)}, u32[]{:S(2)}) collective-permute-start(bf16[6,256,128]{2,1,0:T(8,128)(2,1)S(1)} %shard_map.99), channel_id=1, source_target_pairs={{0,2},{1,3},{2,0},{3,1},{4,6},{5,7},{6,4},{7,5},{8,10},{9,11},{10,... | collective-permute-start | bytes 1179656 | tf_op jit(solution)/shard_map/ppermute | solution.py:365
  111.4 18.9 %collective-permute-start.21 = (bf16[6,256,128]{2,1,0:T(8,128)(2,1)S(1)}, bf16[6,256,128]{2,1,0:T(8,128)(2,1)S(1)}, u32[]{:S(2)}, u32[]{:S(2)}) collective-permute-start(bf16[6,256,128]{2,1,0:T(8,128)(2,1)S(1)} %get-tuple-element.106), channel_id=1, source_target_pairs={{4,2},{5,3},{6,0},{7,1},{8,14},{9,15},{10,12},{11,13},{20,18},{21,... | collective-permute-start | bytes 1179656 | tf_op jit(solution)/shard_map/ppermute | solution.py:361
  136.9 14.1 %collective-permute-start.29 = (bf16[8,256,128]{2,1,0:T(8,128)(2,1)S(1)}, bf16[8,256,128]{2,1,0:T(8,128)(2,1)S(1)}, u32[]{:S(2)}, u32[]{:S(2)}) collective-permute-start(bf16[8,256,128]{2,1,0:T(8,128)(2,1)S(1)} %get-tuple-element.120.refs_0_), channel_id=1, source_target_pairs={{0,8},{1,9},{2,10},{3,11},{12,4},{13,5},{14,6},{15,7},{4,0},{5,1},... | collective-permute-start | bytes 1572872 | tf_op jit(solution)/shard_map/ppermute | solution.py:361
  137.6 25.5 %collective-permute-start.28 = (bf16[8,256,128]{2,1,0:T(8,128)(2,1)S(1)}, bf16[8,256,128]{2,1,0:T(8,128)(2,1)S(1)}, u32[]{:S(2)}, u32[]{:S(2)}) collective-permute-start(bf16[8,256,128]{2,1,0:T(8,128)(2,1)S(1)} %get-tuple-element.120.refs_0_), channel_id=1, source_target_pairs={{0,4},{1,5},{2,6},{3,7},{12,8},{13,9},{14,10},{15,11},{4,12},{5,13... | collective-permute-start | bytes 1572872 | tf_op jit(solution)/shard_map/ppermute | solution.py:361
  152.2 13.4 %collective-permute-start.35 = (bf16[6,256,128]{2,1,0:T(8,128)(2,1)S(1)}, bf16[6,256,128]{2,1,0:T(8,128)(2,1)S(1)}, u32[]{:S(2)}, u32[]{:S(2)}) collective-permute-start(bf16[6,256,128]{2,1,0:T(8,128)(2,1)S(1)} %get-tuple-element.127), channel_id=1, source_target_pairs={{4,8},{5,9},{6,10},{7,11},{8,4},{9,5},{10,6},{11,7},{20,24},{21,25... | collective-permute-start | bytes 1179656 | tf_op jit(solution)/shard_map/ppermute | solution.py:361
  152.9 12.8 %collective-permute-start.36 = (bf16[6,256,128]{2,1,0:T(8,128)(2,1)S(1)}, bf16[6,256,128]{2,1,0:T(8,128)(2,1)S(1)}, u32[]{:S(2)}, u32[]{:S(2)}) collective-permute-start(bf16[6,256,128]{2,1,0:T(8,128)(2,1)S(1)} %get-tuple-element.128), channel_id=1, source_target_pairs={{4,10},{5,11},{6,8},{7,9},{8,6},{9,7},{10,4},{11,5},{20,26},{21,27... | collective-permute-start | bytes 1179656 | tf_op jit(solution)/shard_map/ppermute | solution.py:361
  154.2 23.5 %collective-permute-start.34 = (bf16[6,256,128]{2,1,0:T(8,128)(2,1)S(1)}, bf16[6,256,128]{2,1,0:T(8,128)(2,1)S(1)}, u32[]{:S(2)}, u32[]{:S(2)}) collective-permute-start(bf16[6,256,128]{2,1,0:T(8,128)(2,1)S(1)} %get-tuple-element.126), channel_id=1, source_target_pairs={{4,0},{5,1},{6,2},{7,3},{8,12},{9,13},{10,14},{11,15},{20,16},{21,... | collective-permute-start | bytes 1179656 | tf_op jit(solution)/shard_map/ppermute | solution.py:361
  163.6 19.4 %collective-permute-start.33 = (bf16[6,256,128]{2,1,0:T(8,128)(2,1)S(1)}, bf16[6,256,128]{2,1,0:T(8,128)(2,1)S(1)}, u32[]{:S(2)}, u32[]{:S(2)}) collective-permute-start(bf16[6,256,128]{2,1,0:T(8,128)(2,1)S(1)} %shard_map.107), channel_id=1, source_target_pairs={{0,2},{1,3},{2,0},{3,1},{4,6},{5,7},{6,4},{7,5},{8,10},{9,11},{10,... | collective-permute-start | bytes 1179656 | tf_op jit(solution)/shard_map/ppermute | solution.py:365
  164.3 18.7 %collective-permute-start.32 = (bf16[6,256,128]{2,1,0:T(8,128)(2,1)S(1)}, bf16[6,256,128]{2,1,0:T(8,128)(2,1)S(1)}, u32[]{:S(2)}, u32[]{:S(2)}) collective-permute-start(bf16[6,256,128]{2,1,0:T(8,128)(2,1)S(1)} %get-tuple-element.124), channel_id=1, source_target_pairs={{4,2},{5,3},{6,0},{7,1},{8,14},{9,15},{10,12},{11,13},{20,18},{21,... | collective-permute-start | bytes 1179656 | tf_op jit(solution)/shard_map/ppermute | solution.py:361
  189.7 21.0 %collective-permute-start.40 = (bf16[8,256,128]{2,1,0:T(8,128)(2,1)S(1)}, bf16[8,256,128]{2,1,0:T(8,128)(2,1)S(1)}, u32[]{:S(2)}, u32[]{:S(2)}) collective-permute-start(bf16[8,256,128]{2,1,0:T(8,128)(2,1)S(1)} %get-tuple-element.138.refs_0_), channel_id=1, source_target_pairs={{0,8},{1,9},{2,10},{3,11},{12,4},{13,5},{14,6},{15,7},{4,0},{5,1},... | collective-permute-start | bytes 1572872 | tf_op jit(solution)/shard_map/ppermute | solution.py:361
  199.2 24.9 %collective-permute-start.39 = (bf16[8,256,128]{2,1,0:T(8,128)(2,1)S(1)}, bf16[8,256,128]{2,1,0:T(8,128)(2,1)S(1)}, u32[]{:S(2)}, u32[]{:S(2)}) collective-permute-start(bf16[8,256,128]{2,1,0:T(8,128)(2,1)S(1)} %get-tuple-element.138.refs_0_), channel_id=1, source_target_pairs={{0,4},{1,5},{2,6},{3,7},{12,8},{13,9},{14,10},{15,11},{4,12},{5,13... | collective-permute-start | bytes 1572872 | tf_op jit(solution)/shard_map/ppermute | solution.py:361
  211.4 12.8 %collective-permute-start.42 = (bf16[6,256,128]{2,1,0:T(8,128)(2,1)S(1)}, bf16[6,256,128]{2,1,0:T(8,128)(2,1)S(1)}, u32[]{:S(2)}, u32[]{:S(2)}) collective-permute-start(bf16[6,256,128]{2,1,0:T(8,128)(2,1)S(1)} %shard_map.114), channel_id=1, source_target_pairs={{0,2},{1,3},{2,0},{3,1},{4,6},{5,7},{6,4},{7,5},{8,10},{9,11},{10,... | collective-permute-start | bytes 1179656 | tf_op jit(solution)/shard_map/ppermute | solution.py:365
  212.2 14.5 %collective-permute-start.46 = (bf16[6,256,128]{2,1,0:T(8,128)(2,1)S(1)}, bf16[6,256,128]{2,1,0:T(8,128)(2,1)S(1)}, u32[]{:S(2)}, u32[]{:S(2)}) collective-permute-start(bf16[6,256,128]{2,1,0:T(8,128)(2,1)S(1)} %get-tuple-element.145), channel_id=1, source_target_pairs={{4,8},{5,9},{6,10},{7,11},{8,4},{9,5},{10,6},{11,7},{20,24},{21,25... | collective-permute-start | bytes 1179656 | tf_op jit(solution)/shard_map/ppermute | solution.py:361
  212.9 13.9 %collective-permute-start.47 = (bf16[6,256,128]{2,1,0:T(8,128)(2,1)S(1)}, bf16[6,256,128]{2,1,0:T(8,128)(2,1)S(1)}, u32[]{:S(2)}, u32[]{:S(2)}) collective-permute-start(bf16[6,256,128]{2,1,0:T(8,128)(2,1)S(1)} %get-tuple-element.146), channel_id=1, source_target_pairs={{4,10},{5,11},{6,8},{7,9},{8,6},{9,7},{10,4},{11,5},{20,26},{21,27... | collective-permute-start | bytes 1179656 | tf_op jit(solution)/shard_map/ppermute | solution.py:361
  214.2 24.6 %collective-permute-start.45 = (bf16[6,256,128]{2,1,0:T(8,128)(2,1)S(1)}, bf16[6,256,128]{2,1,0:T(8,128)(2,1)S(1)}, u32[]{:S(2)}, u32[]{:S(2)}) collective-permute-start(bf16[6,256,128]{2,1,0:T(8,128)(2,1)S(1)} %get-tuple-element.144), channel_id=1, source_target_pairs={{4,0},{5,1},{6,2},{7,3},{8,12},{9,13},{10,14},{11,15},{20,16},{21,... | collective-permute-start | bytes 1179656 | tf_op jit(solution)/shard_map/ppermute | solution.py:361
  224.8 19.4 %collective-permute-start.44 = (bf16[6,256,128]{2,1,0:T(8,128)(2,1)S(1)}, bf16[6,256,128]{2,1,0:T(8,128)(2,1)S(1)}, u32[]{:S(2)}, u32[]{:S(2)}) collective-permute-start(bf16[6,256,128]{2,1,0:T(8,128)(2,1)S(1)} %shard_map.115), channel_id=1, source_target_pairs={{0,2},{1,3},{2,0},{3,1},{4,6},{5,7},{6,4},{7,5},{8,10},{9,11},{10,... | collective-permute-start | bytes 1179656 | tf_op jit(solution)/shard_map/ppermute | solution.py:365
  225.5 18.7 %collective-permute-start.43 = (bf16[6,256,128]{2,1,0:T(8,128)(2,1)S(1)}, bf16[6,256,128]{2,1,0:T(8,128)(2,1)S(1)}, u32[]{:S(2)}, u32[]{:S(2)}) collective-permute-start(bf16[6,256,128]{2,1,0:T(8,128)(2,1)S(1)} %get-tuple-element.142), channel_id=1, source_target_pairs={{4,2},{5,3},{6,0},{7,1},{8,14},{9,15},{10,12},{11,13},{20,18},{21,... | collective-permute-start | bytes 1179656 | tf_op jit(solution)/shard_map/ppermute | solution.py:361
  (31 other events, 304.2 us)

commit v9 on v7

--- a/solution.py
+++ b/solution.py
@@ -52,14 +52,16 @@
 
 FIRST = ((0, 2), (3, 1), (1, 0), (2, 3))
 SECOND = ((0, 1), (3, 2), (1, 3), (2, 0))
+OUTWARD = ((1, 0), (2, 3))
+MIDDLE = ((1, 2), (2, 1))
 
 
 class Layout:
     def __init__(self, cap):
         self.cap = cap
         self.packs = 0
-        self.entries = 9 * cap
-        self.size = 9 * cap + 3 * 16 * cap
+        self.entries = 12 * cap
+        self.size = 12 * cap + 3 * 16 * cap
 
     def pack(self, j, flip):
         return self.packs + (j * 3 + flip - 1) * self.cap
@@ -148,7 +150,7 @@
     cap = layout.cap
     keys = 16 * cap
     _, yc, _, zs = whereabouts()
-    for j in range(3):
+    for j in range(4):
         for flip in (1, 2, 3):
             for r in range(cap):
                 table[layout.pack(j, flip) + r] = asked[flip * LANES + (zs[j] * 4 + yc) * cap + r]
@@ -171,42 +173,54 @@
     )(mine, asked)
 
 
-def copy_blocks(table, at, cap, shard, out):
+def copy_asked(layout, table, j, flip, shard, out, first=0):
+    at = layout.pack(j, flip)
+    for r in range(layout.cap):
+        out[first + r] = shard[table[at + r]]
+
+
+def copy_part(cap, source, part, out, first):
     for r in range(cap):
-        out[r] = shard[table[at + r]]
-
-
-def pack_shard_kernel(layout, j, table, shard, *refs):
-    outs = refs[-3:]
-    for flip in (1, 2, 3):
-        copy_blocks(table, layout.pack(j, flip), layout.cap, shard, outs[flip - 1])
-
-
-def pack_second_kernel(layout, table, asked, first, second, *refs):
-    here, far = refs[-7:-4], refs[-4:]
-    cap = layout.cap
-    z, yc, inner, _ = whereabouts()
-    for flip in (1, 2, 3):
-        copy_blocks(table, layout.pack(2, flip), cap, second, here[flip - 1])
-
-    def send(shard):
-        for flip in range(4):
-            copy_blocks(asked, flip * LANES + ((z ^ 2) * 4 + yc) * cap, cap, shard, far[flip])
-
-    pl.when(inner)(lambda: send(first))
-    pl.when(jnp.logical_not(inner))(lambda: send(second))
-
-
-def pack(kernel, cap, number, tables, shards):
-    _, tile, repl = shards[0].shape
+        out[first + r] = source[part * cap + r]
+
+
+def by_place(mid, out, use):
+    inner = whereabouts()[2]
+    pl.when(inner)(lambda: use(mid))
+    pl.when(jnp.logical_not(inner))(lambda: use(out))
+
+
+def other_y_kernel(layout, js, table, *refs):
+    shards, outs = refs[:-2], refs[-2:]
+    for i, (j, shard) in enumerate(zip(js, shards)):
+        for flip in (2, 3):
+            copy_asked(layout, table, j, flip, shard, outs[flip - 2], i * layout.cap)
+
+
+def second_kernel(layout, table, own, first, second, out2, out3, core):
+    other_y_kernel(layout, (2,), table, second, out2, out3)
+    for j, shard in enumerate((own, first, second)):
+        copy_asked(layout, table, j, 1, shard, core, j * layout.cap)
+
+
+def third_kernel(layout, table, mid, out, out2, out3, core):
+    def use(shard):
+        other_y_kernel(layout, (3,), table, shard, out2, out3)
+        copy_asked(layout, table, 3, 1, shard, core)
+
+    by_place(mid, out, use)
+
+
+def pack(kernel, sizes, table, arrays):
+    _, tile, repl = arrays[0].shape
     return pl.pallas_call(
         kernel,
-        out_shape=[jax.ShapeDtypeStruct((cap, tile, repl), jnp.bfloat16)] * number,
-        in_specs=[SMEM] * len(tables) + [VMEM] * len(shards),
-        out_specs=[VMEM] * number,
+        out_shape=[jax.ShapeDtypeStruct((size, tile, repl), jnp.bfloat16) for size in sizes],
+        in_specs=[SMEM] + [VMEM] * len(arrays),
+        out_specs=[VMEM] * len(sizes),
         compiler_params=params(),
         cost_estimate=pl.CostEstimate(flops=0, bytes_accessed=0, transcendentals=0),
-    )(*tables, *shards)
+    )(table, *arrays)
 
 
 def multiply(layout, table, tiles, xbuf, first, number, field):
@@ -228,52 +242,50 @@
             some(first + g * GROUP, g * GROUP)
 
 
-def early_kernel(layout, table, tiles, *refs):
-    sources, (field, xbuf) = refs[: len(EARLY)], refs[len(EARLY) :]
+def take_own(layout, table, entry, shard, xbuf, place):
+    for r in range(layout.cap):
+        xbuf[place + r] = shard[table[layout.entry(entry + r) + 2]]
+
+
+def early_kernel(layout, parts, table, tiles, *refs):
     cap = layout.cap
-    for i, ((_, flip), source) in enumerate(zip(EARLY, sources)):
-        for r in range(cap):
-            e = i * cap + r
-            xbuf[e] = source[table[layout.entry(e) + 2]] if flip == 0 else source[r]
+    field, xbuf = refs[-2:]
+    core = refs[3]
+    for j in range(3):
+        base = 4 * cap * j
+        take_own(layout, table, base, refs[j], xbuf, base)
+        copy_part(cap, core, j, xbuf, base + cap)
+        ref, part = parts[j]
+        copy_part(cap, refs[ref], part, xbuf, base + 2 * cap)
+        copy_part(cap, refs[ref + 1], part, xbuf, base + 3 * cap)
     field[...] = jnp.zeros_like(field)
-    multiply(layout, table, tiles, xbuf, 0, len(EARLY) * cap, field)
-
-
-def cost(entries, tile, repl, more=0):
-    return pl.CostEstimate(
-        flops=2 * entries * tile * tile * repl,
-        bytes_accessed=entries * tile * (tile + repl) * 2 + more,
-        transcendentals=0,
-    )
-
-
-def early(layout, table, tiles, sources):
+    multiply(layout, table, tiles, xbuf, 0, 12 * cap, field)
+
+
+def early(layout, parts, table, tiles, arrays):
     tile = tiles.shape[1]
-    blocks, _, repl = sources[0].shape
-    entries = len(EARLY) * layout.cap
-    return pl.pallas_call(
-        functools.partial(early_kernel, layout),
+    blocks, _, repl = arrays[0].shape
+    return pl.pallas_call(
+        functools.partial(early_kernel, layout, parts),
         out_shape=jax.ShapeDtypeStruct((blocks + 1, tile, repl), jnp.float32),
-        in_specs=[SMEM] + [VMEM] * (1 + len(sources)),
+        in_specs=[SMEM] + [VMEM] * (1 + len(arrays)),
         out_specs=VMEM,
-        scratch_shapes=[pltpu.VMEM((entries, tile, repl), jnp.bfloat16)],
+        scratch_shapes=[pltpu.VMEM((12 * layout.cap, tile, repl), jnp.bfloat16)],
         compiler_params=params(),
         cost_estimate=pl.CostEstimate(flops=0, bytes_accessed=0, transcendentals=0),
-    )(table, tiles, *sources)
-
-
-def late_kernel(layout, last, table, scalars, tiles, far0, far1, far2, far3, field, xpos, ymom, *refs):
-    if last:
-        xout, yout, energy, xbuf, acc = refs
-    else:
-        xout, yout, xb, out1, out2, out3, xbuf, acc = refs
+    )(table, tiles, *arrays)
+
+
+def late_kernel(layout, last, table, scalars, tiles, mid, out, core, got2, got3, field, xpos, ymom, *refs):
+    outs, (xbuf, acc) = refs[:-2], refs[-2:]
+    xout, yout = outs[:2]
     blocks = xpos.shape[0]
     cap = layout.cap
-    for i, far in enumerate((far0, far1, far2, far3)):
-        for r in range(cap):
-            xbuf[i * cap + r] = far[r]
+    by_place(mid, out, lambda shard: take_own(layout, table, 12 * cap, shard, xbuf, 0))
+    for i, got in enumerate((core, got2, got3)):
+        copy_part(cap, got, 0, xbuf, (1 + i) * cap)
     acc[...] = field[...]
-    multiply(layout, table, tiles, xbuf, len(EARLY) * cap, len(LATE) * cap, acc)
+    multiply(layout, table, tiles, xbuf, 12 * cap, 4 * cap, acc)
     total = jnp.zeros((1, xpos.shape[2]), jnp.float32)
     for b in range(blocks):
         x, h = xpos[b], acc[b]
@@ -283,36 +295,39 @@
         xout[b] = x
         yout[b] = y
         if not last:
-            xb[b] = x.astype(jnp.bfloat16)
+            outs[2][b] = x.astype(jnp.bfloat16)
     if last:
-        energy[...] = -0.5 * total
+        outs[2][...] = -0.5 * total
     else:
-        for flip, out in ((1, out1), (2, out2), (3, out3)):
-            copy_blocks(table, layout.pack(0, flip), cap, xb, out)
-
-
-def late(layout, last, table, scalars, tiles, packs, field, xpos, ymom):
+        other_y_kernel(layout, (0,), table, *outs[2:])
+
+
+def late(layout, last, table, scalars, tiles, sources, field, xpos, ymom):
     tile = tiles.shape[1]
     blocks, _, repl = xpos.shape
-    entries = len(LATE) * layout.cap
+    entries = 4 * layout.cap
     state = jax.ShapeDtypeStruct(xpos.shape, jnp.float32)
     if last:
         extra = (jax.ShapeDtypeStruct((1, repl), jnp.float32),)
     else:
         out = jax.ShapeDtypeStruct((layout.cap, tile, repl), jnp.bfloat16)
-        extra = (jax.ShapeDtypeStruct(xpos.shape, jnp.bfloat16), out, out, out)
+        extra = (jax.ShapeDtypeStruct(xpos.shape, jnp.bfloat16), out, out)
     return pl.pallas_call(
         functools.partial(late_kernel, layout, last),
         out_shape=(state, state) + extra,
-        in_specs=[SMEM, SMEM] + [VMEM] * (1 + len(packs) + 3),
+        in_specs=[SMEM, SMEM] + [VMEM] * (1 + len(sources) + 3),
         out_specs=(VMEM,) * (2 + len(extra)),
         scratch_shapes=[
             pltpu.VMEM((entries, tile, repl), jnp.bfloat16),
             pltpu.VMEM((blocks + 1, tile, repl), jnp.float32),
         ],
         compiler_params=params(),
-        cost_estimate=cost(entries, tile, repl, 20 * xpos.size),
-    )(table, scalars, tiles, *packs, field, xpos, ymom)
+        cost_estimate=pl.CostEstimate(
+            flops=2 * entries * tile * tile * repl,
+            bytes_accessed=entries * tile * (tile + repl) * 2 + 20 * xpos.size,
+            transcendentals=0,
+        ),
+    )(table, scalars, tiles, *sources, field, xpos, ymom)
 
 
 def along_z(pairs, value):
@@ -336,39 +351,53 @@
     cap = (slots + 15) // 16
     order = blocks * tile * 16
     layout = Layout(cap)
-    pack_own = functools.partial(pack_shard_kernel, layout, 0)
-    pack_first = functools.partial(pack_shard_kernel, layout, 1)
-    pack_second = functools.partial(pack_second_kernel, layout)
+
+    def other_y(js, shards):
+        kernel = functools.partial(other_y_kernel, layout, js)
+        return pack(kernel, [len(js) * cap] * 2, table, shards)
+
+    def to_other_y(packs):
+        return [across(2, packs[0]), across(3, packs[1])]
+
     xpos = positions.reshape(blocks, tile, repl)
     ymom = momenta.reshape(blocks, tile, repl)
     own0 = xpos.astype(jnp.bfloat16)
     mine, note = plan(layout, blocks, tile_rows, tile_cols, counts, tiles)
     notes = jnp.concatenate([note] + [across(flip, note) for flip in (1, 2, 3)])
     table = make_table(layout, mine, notes.astype(jnp.int32).reshape(-1))
-    packs0 = pack(pack_own, cap, 3, [table], [own0])
-    asked = coeff = None
+    packs0 = None
     for step in range(STEPS):
         last = step == STEPS - 1
         own1 = along_z(FIRST, own0)
         own2 = along_z(SECOND, own0)
-        got0 = [across(flip, packs0[flip - 1]) for flip in (1, 2, 3)]
+        mid = along_z(MIDDLE, own0)
         if step == 0:
-            notes, got0 = lax.optimization_barrier((notes, got0))
-            far_notes = across(4, notes)
-            asked = far_notes.astype(jnp.int32).reshape(-1)
-        own1, got0 = lax.optimization_barrier((own1, got0))
-        packs1 = pack(pack_first, cap, 3, [table], [own1])
-        got1 = [across(flip, packs1[flip - 1]) for flip in (1, 2, 3)]
+            out = along_z(OUTWARD, own1)
+            got1 = to_other_y(other_y((0, 1), [own0, own1]))
+            own2, got1 = lax.optimization_barrier((own2, got1))
+            parts = ((4, 0), (4, 1), (6, 0))
+            got = got1
+        else:
+            got0 = to_other_y(packs0)
+            own1, got0 = lax.optimization_barrier((own1, got0))
+            out = along_z(OUTWARD, own1)
+            got1 = to_other_y(other_y((1,), [own1]))
+            own2, got1 = lax.optimization_barrier((own2, got1))
+            parts = ((4, 0), (6, 0), (8, 0))
+            got = got0 + got1
+        packs2 = pack(functools.partial(second_kernel, layout), [cap, cap, 3 * cap], table, [own0, own1, own2])
+        got = got + to_other_y(packs2)
+        core = across(1, packs2[2])
         if step == 0:
-            half = jnp.broadcast_to(jnp.sum(notes[:, SUM_AT]) + jnp.sum(far_notes[:, SUM_AT]), (1, LANES))
-            total = jnp.sum((half + across(8, half))[0, 0])
+            notes, core = lax.optimization_barrier((notes, core))
+            plane = jnp.broadcast_to(jnp.sum(notes[:, SUM_AT]), (1, LANES))
+            half = plane + across(4, plane)
+        packs3 = pack(functools.partial(third_kernel, layout), [cap] * 3, table, [mid, out])
+        far = [mid, out, across(1, packs3[2])] + to_other_y(packs3)
+        field = early(layout, parts, table, tiles, [own0, own1, own2, core] + got)
+        if step == 0:
+            total = (half + across(8, half))[0, 0]
             coeff = 0.7 * jnp.sqrt((order - 1) / total)
-        own2, got1 = lax.optimization_barrier((own2, got1))
-        packs2 = pack(pack_second, cap, 7, [table, asked], [own1, own2])
-        got2 = [across(flip, packs2[flip - 1]) for flip in (1, 2, 3)]
-        far = [across(4 + flip, packs2[3 + flip]) for flip in range(4)]
-        sources = [own0] + got0 + [own1] + got1 + [own2] + got2
-        field = early(layout, table, tiles, sources)
         scalars = jnp.stack([jnp.float32(0.4 - 0.1 * step), coeff])
         outs = late(layout, last, table, scalars, tiles, far, field, xpos, ymom)
         xpos, ymom = outs[0], outs[1]

time: 240 us -> 239 us (level)
  starting transfers between devices: 59.6 us -> 49.1 us
  waiting for transfers between devices: 126 us -> 135 us
    ppermute x8 -> x16, waiting for transfers between devices: 34.5 us -> 76.8 us  [along_z(): lax.ppermute(value, 'row', [(a * 4 + i, b * 4 + i) for a, b in pairs for...]
    ppermute x57 -> x43, waiting for transfers between devices: 92 us -> 58.2 us  [across(): return lax.ppermute(value, 'row', [(i, i ^ flip) for i in range(16)])]
    ppermute x57 -> x43, starting transfers between devices: 49.3 us -> 30.6 us  [across(): return lax.ppermute(value, 'row', [(i, i ^ flip) for i in range(16)])]
    ppermute x8 -> x16, starting transfers between devices: 10.3 us -> 18.5 us  [along_z(): lax.ppermute(value, 'row', [(a * 4 + i, b * 4 + i) for a, b in pairs for...]
    pallas_call x13 -> x16, Pallas kernels: 18.8 us -> 19.4 us  [the longest x4 12.2 us: early(): pl.pallas_call(functools.partial(early_kernel, layout, parts), out_shape=...]
  transfers between devices with their start and end apart: 65 -> 59, of which waited for: 34 -> 28; matrix products, arithmetic and copies ran while one was open for 1% -> 2% of each run, Pallas kernels for 9% -> 10%
where the time goes in v9:
time: 239 us
  waiting for transfers between devices  135 us (56%)
  starting transfers between devices  49.1 us (21%)
  Pallas kernels  33.2 us (14%)
  blocking collectives  10.3 us (4%)
  other arithmetic  5.35 us (2%)
  local copies, waits for them, and re-layouts  4.09 us (2%)
    ppermute x16, waiting for transfers between devices, along_z(): lax.ppermute(value, 'row', [(a * 4 + i, b * 4 + i) for a, b in pairs for...  76.8 us
    ppermute x43, waiting for transfers between devices, across(): return lax.ppermute(value, 'row', [(i, i ^ flip) for i in range(16)])  58.2 us
    ppermute x43, starting transfers between devices, across(): return lax.ppermute(value, 'row', [(i, i ^ flip) for i in range(16)])  30.6 us
    ppermute x16, starting transfers between devices, along_z(): lax.ppermute(value, 'row', [(a * 4 + i, b * 4 + i) for a, b in pairs for...  18.5 us
    pallas_call x4, Pallas kernels, early(): pl.pallas_call(functools.partial(early_kernel, layout, parts), out_shape=...  12.2 us
    all_to_all x1, blocking collectives, row_sum(): lax.all_to_all(spread, 'row', split_axis=0, concat_axis=0, tiled=True)  10.3 us
    pallas_call x4, Pallas kernels, late(): pl.pallas_call(functools.partial(late_kernel, layout, last), out_shape=(s...  8.12 us
    pallas_call x12, Pallas kernels, pack(): pl.pallas_call(kernel, out_shape=[jax.ShapeDtypeStruct((size, tile, repl)...  7.24 us
  transfers between devices with their start and end apart: 59, of which 28 were waited for; matrix products, arithmetic and copies ran while one was open for 2% of the time, Pallas kernels for 10%

profile of v9, /device:TPU:0, one launch (start us, length us, event | category | flops | bytes accessed | tf_op | source)
XLA Modules:
  0.0 238.9 jit_solution(6809253710213733090)
XLA Ops:
  1.9 4.1 %collective-permute-start.3 = (bf16[8,256,128]{2,1,0:T(8,128)(2,1)S(1)}, bf16[8,256,128]{2,1,0:T(8,128)(2,1)S(1)}, u32[]{:S(2)}, u32[]{:S(2)}) collective-permute-start(bf16[8,256,128]{2,1,0:T(8,128)(2,1)S(1)} %convert_element_type.12.refs_0_.own), channel_id=1, source_target_pairs={{0,8},{1,9},{2,10},{3,11},{12,4},{13,5},{14,6},{15,7},{4,0},{5,1},... | collective-permute-start | bytes 1572872 | tf_op jit(solution)/shard_map/ppermute | solution.py:334
  6.7 4.2 %shard_map.85 = (s32[144]{0:T(256)}, f32[1,128]{1,0:T(1,128)}) custom-call(s32[48]{0:T(128)} %rows.1, s32[48]{0:T(128)} %cols.1, s32[1]{0:T(128)S(6)} %copy.10.count, bf16[48,256,256]{2,1,0:T(8,128)(2,1)} %tiles.17), custom_call_target="tpu_custom_call" | custom-call | tf_op jit(solution)/shard_map/pallas_call | solution.py:131
  21.5 8.7 %collective-permute-done.4.second.refs_2_ = bf16[8,256,128]{2,1,0:T(8,128)(2,1)S(1)} collective-permute-done((bf16[8,256,128]{2,1,0:T(8,128)(2,1)S(1)}, bf16[8,256,128]{2,1,0:T(8,128)(2,1)S(1)}, u32[]{:S(2)}, u32[]{:S(2)}) %collective-permute-start.4) | collective-permute-done | bytes 524320 | tf_op jit(solution)/shard_map/ppermute | solution.py:334
  31.6 7.5 %collective-permute-done.6.refs_5_ = bf16[6,256,128]{2,1,0:T(8,128)(2,1)S(1)} collective-permute-done((bf16[6,256,128]{2,1,0:T(8,128)(2,1)S(1)}, bf16[6,256,128]{2,1,0:T(8,128)(2,1)S(1)}, u32[]{:S(2)}, u32[]{:S(2)}) %collective-permute-start.6) | collective-permute-done | bytes 393248 | tf_op jit(solution)/shard_map/ppermute | solution.py:338
  43.4 4.9 %collective-permute-start.8 = (f32[1,128]{1,0:T(1,128)S(1)}, f32[1,128]{1,0:T(1,128)S(1)}, u32[]{:S(2)}, u32[]{:S(2)}) collective-permute-start(f32[1,128]{1,0:T(1,128)S(1)} %broadcast_in_dim.8), channel_id=1, source_target_pairs={{0,4},{1,5},{2,6},{3,7},{4,0},{5,1},{6,2},{7,3},{8,12},{9,13},{10,... | collective-permute-start | bytes 1544 | tf_op jit(solution)/shard_map/ppermute | solution.py:338
  49.2 9.6 %collective-permute-done.11.out = bf16[8,256,128]{2,1,0:T(8,128)(2,1)S(1)} collective-permute-done((bf16[8,256,128]{2,1,0:T(8,128)(2,1)S(1)}, bf16[8,256,128]{2,1,0:T(8,128)(2,1)S(1)}, u32[]{:S(2)}, u32[]{:S(2)}) %collective-permute-start.11) | collective-permute-done | bytes 524320 | tf_op jit(solution)/shard_map/ppermute | solution.py:334
  62.1 2.8 %copy-done = bf16[48,256,256]{2,1,0:T(8,128)(2,1)S(1)} copy-done((bf16[48,256,256]{2,1,0:T(8,128)(2,1)S(1)}, bf16[48,256,256]{2,1,0:T(8,128)(2,1)}, u32[]{:S(2)}) %copy-start) | copy-done | bytes 6291480
  64.9 3.0 %shard_map.90.field = f32[9,256,128]{2,1,0:T(8,128)S(1)} custom-call(s32[180]{0:T(256)S(1)} %copy-done.4, bf16[48,256,256]{2,1,0:T(8,128)(2,1)S(1)} %copy-done, bf16[8,256,128]{2,1,0:T(8,128)(2,1)S(1)} %convert_element_type.12.refs_0_.own, bf16[8,256,128]{2,1,0:T(8,128)(2,1)S(1)} %collective-permute-done.3.refs_1_.first, ...), custom_call_target="tpu_custom_call" | custom-call | tf_op jit(solution)/shard_map/pallas_call | solution.py:268
  68.8 2.5 %collective-permute-done.14.got3 = bf16[3,256,128]{2,1,0:T(8,128)(2,1)S(1)} collective-permute-done((bf16[3,256,128]{2,1,0:T(8,128)(2,1)S(1)}, bf16[3,256,128]{2,1,0:T(8,128)(2,1)S(1)}, u32[]{:S(2)}, u32[]{:S(2)}) %collective-permute-start.14) | collective-permute-done | bytes 196640 | tf_op jit(solution)/shard_map/ppermute | solution.py:338
  73.0 2.3 collective-permute-start.18
  77.0 6.1 %collective-permute-done.19.refs_4_ = bf16[3,256,128]{2,1,0:T(8,128)(2,1)S(1)} collective-permute-done((bf16[3,256,128]{2,1,0:T(8,128)(2,1)S(1)}, bf16[3,256,128]{2,1,0:T(8,128)(2,1)S(1)}, u32[]{:S(2)}, u32[]{:S(2)}) %collective-permute-start.19) | collective-permute-done | bytes 196640 | tf_op jit(solution)/shard_map/ppermute | solution.py:338
  83.1 2.9 %collective-permute-done.20.refs_5_ = bf16[3,256,128]{2,1,0:T(8,128)(2,1)S(1)} collective-permute-done((bf16[3,256,128]{2,1,0:T(8,128)(2,1)S(1)}, bf16[3,256,128]{2,1,0:T(8,128)(2,1)S(1)}, u32[]{:S(2)}, u32[]{:S(2)}) %collective-permute-start.20) | collective-permute-done | bytes 196640 | tf_op jit(solution)/shard_map/ppermute | solution.py:338
  91.1 9.2 %collective-permute-done.25.second.refs_2_ = bf16[8,256,128]{2,1,0:T(8,128)(2,1)S(1)} collective-permute-done((bf16[8,256,128]{2,1,0:T(8,128)(2,1)S(1)}, bf16[8,256,128]{2,1,0:T(8,128)(2,1)S(1)}, u32[]{:S(2)}, u32[]{:S(2)}) %collective-permute-start.25) | collective-permute-done | bytes 524320 | tf_op jit(solution)/shard_map/ppermute | solution.py:334
  102.8 8.5 %collective-permute-done.21.out = bf16[8,256,128]{2,1,0:T(8,128)(2,1)S(1)} collective-permute-done((bf16[8,256,128]{2,1,0:T(8,128)(2,1)S(1)}, bf16[8,256,128]{2,1,0:T(8,128)(2,1)S(1)}, u32[]{:S(2)}, u32[]{:S(2)}) %collective-permute-start.21) | collective-permute-done | bytes 524320 | tf_op jit(solution)/shard_map/ppermute | solution.py:334
  114.0 3.1 %shard_map.95.field = f32[9,256,128]{2,1,0:T(8,128)S(1)} custom-call(s32[180]{0:T(256)S(1)} %copy-done.4, bf16[48,256,256]{2,1,0:T(8,128)(2,1)S(1)} %bitcast.11, bf16[8,256,128]{2,1,0:T(8,128)(2,1)S(1)} %get-tuple-element.93.own.refs_0_, bf16[8,256,128]{2,1,0:T(8,128)(2,1)S(1)} %collective-permute-done.18.refs_0_.first.refs_1_, ...), custom_call_target="tpu_custom_call" | custom-call | tf_op jit(solution)/shard_map/pallas_call | solution.py:268
  117.1 2.8 %collective-permute-done.23.got2 = bf16[3,256,128]{2,1,0:T(8,128)(2,1)S(1)} collective-permute-done((bf16[3,256,128]{2,1,0:T(8,128)(2,1)S(1)}, bf16[3,256,128]{2,1,0:T(8,128)(2,1)S(1)}, u32[]{:S(2)}, u32[]{:S(2)}) %collective-permute-start.23) | collective-permute-done | bytes 196640 | tf_op jit(solution)/shard_map/ppermute | solution.py:338
  119.9 3.1 %collective-permute-done.24.got3 = bf16[3,256,128]{2,1,0:T(8,128)(2,1)S(1)} collective-permute-done((bf16[3,256,128]{2,1,0:T(8,128)(2,1)S(1)}, bf16[3,256,128]{2,1,0:T(8,128)(2,1)S(1)}, u32[]{:S(2)}, u32[]{:S(2)}) %collective-permute-start.24) | collective-permute-done | bytes 196640 | tf_op jit(solution)/shard_map/ppermute | solution.py:338
  128.0 6.6 %collective-permute-done.33.refs_4_ = bf16[3,256,128]{2,1,0:T(8,128)(2,1)S(1)} collective-permute-done((bf16[3,256,128]{2,1,0:T(8,128)(2,1)S(1)}, bf16[3,256,128]{2,1,0:T(8,128)(2,1)S(1)}, u32[]{:S(2)}, u32[]{:S(2)}) %collective-permute-start.33) | collective-permute-done | bytes 196640 | tf_op jit(solution)/shard_map/ppermute | solution.py:338
  136.6 2.5 %collective-permute-done.32.refs_0_.first.refs_1_ = bf16[8,256,128]{2,1,0:T(8,128)(2,1)S(1)} collective-permute-done((bf16[8,256,128]{2,1,0:T(8,128)(2,1)S(1)}, bf16[8,256,128]{2,1,0:T(8,128)(2,1)S(1)}, u32[]{:S(2)}, u32[]{:S(2)}) %collective-permute-start.32) | collective-permute-done | bytes 524320 | tf_op jit(solution)/shard_map/ppermute | solution.py:334
  142.6 8.7 %collective-permute-done.39.second.refs_2_ = bf16[8,256,128]{2,1,0:T(8,128)(2,1)S(1)} collective-permute-done((bf16[8,256,128]{2,1,0:T(8,128)(2,1)S(1)}, bf16[8,256,128]{2,1,0:T(8,128)(2,1)S(1)}, u32[]{:S(2)}, u32[]{:S(2)}) %collective-permute-start.39) | collective-permute-done | bytes 524320 | tf_op jit(solution)/shard_map/ppermute | solution.py:334
  153.9 8.4 %collective-permute-done.35.out = bf16[8,256,128]{2,1,0:T(8,128)(2,1)S(1)} collective-permute-done((bf16[8,256,128]{2,1,0:T(8,128)(2,1)S(1)}, bf16[8,256,128]{2,1,0:T(8,128)(2,1)S(1)}, u32[]{:S(2)}, u32[]{:S(2)}) %collective-permute-start.35) | collective-permute-done | bytes 524320 | tf_op jit(solution)/shard_map/ppermute | solution.py:334
  165.0 3.1 %shard_map.100.field = f32[9,256,128]{2,1,0:T(8,128)S(1)} custom-call(s32[180]{0:T(256)S(1)} %copy-done.4, bf16[48,256,256]{2,1,0:T(8,128)(2,1)S(1)} %bitcast.11, bf16[8,256,128]{2,1,0:T(8,128)(2,1)S(1)} %get-tuple-element.112.own.refs_0_, bf16[8,256,128]{2,1,0:T(8,128)(2,1)S(1)} %collective-permute-done.32.refs_0_.first.refs_1_, ...), custom_call_target="tpu_custom_call" | custom-call | tf_op jit(solution)/shard_map/pallas_call | solution.py:268
  168.0 2.9 %collective-permute-done.37.got2 = bf16[3,256,128]{2,1,0:T(8,128)(2,1)S(1)} collective-permute-done((bf16[3,256,128]{2,1,0:T(8,128)(2,1)S(1)}, bf16[3,256,128]{2,1,0:T(8,128)(2,1)S(1)}, u32[]{:S(2)}, u32[]{:S(2)}) %collective-permute-start.37) | collective-permute-done | bytes 196640 | tf_op jit(solution)/shard_map/ppermute | solution.py:338
  170.9 3.0 %collective-permute-done.38.got3 = bf16[3,256,128]{2,1,0:T(8,128)(2,1)S(1)} collective-permute-done((bf16[3,256,128]{2,1,0:T(8,128)(2,1)S(1)}, bf16[3,256,128]{2,1,0:T(8,128)(2,1)S(1)}, u32[]{:S(2)}, u32[]{:S(2)}) %collective-permute-start.38) | collective-permute-done | bytes 196640 | tf_op jit(solution)/shard_map/ppermute | solution.py:338
  179.0 6.4 %collective-permute-done.47.refs_4_ = bf16[3,256,128]{2,1,0:T(8,128)(2,1)S(1)} collective-permute-done((bf16[3,256,128]{2,1,0:T(8,128)(2,1)S(1)}, bf16[3,256,128]{2,1,0:T(8,128)(2,1)S(1)}, u32[]{:S(2)}, u32[]{:S(2)}) %collective-permute-start.47) | collective-permute-done | bytes 196640 | tf_op jit(solution)/shard_map/ppermute | solution.py:338
  193.7 8.7 %collective-permute-done.53.second.refs_2_ = bf16[8,256,128]{2,1,0:T(8,128)(2,1)S(1)} collective-permute-done((bf16[8,256,128]{2,1,0:T(8,128)(2,1)S(1)}, bf16[8,256,128]{2,1,0:T(8,128)(2,1)S(1)}, u32[]{:S(2)}, u32[]{:S(2)}) %collective-permute-start.53) | collective-permute-done | bytes 524320 | tf_op jit(solution)/shard_map/ppermute | solution.py:334
  204.9 8.4 %collective-permute-done.49.out = bf16[8,256,128]{2,1,0:T(8,128)(2,1)S(1)} collective-permute-done((bf16[8,256,128]{2,1,0:T(8,128)(2,1)S(1)}, bf16[8,256,128]{2,1,0:T(8,128)(2,1)S(1)}, u32[]{:S(2)}, u32[]{:S(2)}) %collective-permute-start.49) | collective-permute-done | bytes 524320 | tf_op jit(solution)/shard_map/ppermute | solution.py:334
  216.0 3.0 %shard_map.105.field = f32[9,256,128]{2,1,0:T(8,128)S(1)} custom-call(s32[180]{0:T(256)S(1)} %copy-done.4, bf16[48,256,256]{2,1,0:T(8,128)(2,1)S(1)} %bitcast.11, bf16[8,256,128]{2,1,0:T(8,128)(2,1)S(1)} %get-tuple-element.131.own.refs_0_, bf16[8,256,128]{2,1,0:T(8,128)(2,1)S(1)} %collective-permute-done.46.refs_0_.first.refs_1_, ...), custom_call_target="tpu_custom_call" | custom-call | tf_op jit(solution)/shard_map/pallas_call | solution.py:268
  219.1 2.9 %collective-permute-done.51.got2 = bf16[3,256,128]{2,1,0:T(8,128)(2,1)S(1)} collective-permute-done((bf16[3,256,128]{2,1,0:T(8,128)(2,1)S(1)}, bf16[3,256,128]{2,1,0:T(8,128)(2,1)S(1)}, u32[]{:S(2)}, u32[]{:S(2)}) %collective-permute-start.51) | collective-permute-done | bytes 196640 | tf_op jit(solution)/shard_map/ppermute | solution.py:338
  222.0 3.0 %collective-permute-done.52.got3 = bf16[3,256,128]{2,1,0:T(8,128)(2,1)S(1)} collective-permute-done((bf16[3,256,128]{2,1,0:T(8,128)(2,1)S(1)}, bf16[3,256,128]{2,1,0:T(8,128)(2,1)S(1)}, u32[]{:S(2)}, u32[]{:S(2)}) %collective-permute-start.52) | collective-permute-done | bytes 196640 | tf_op jit(solution)/shard_map/ppermute | solution.py:338
  225.0 3.1 %shard_map.106 = (f32[8,256,128]{2,1,0:T(8,128)}, f32[8,256,128]{2,1,0:T(8,128)}, f32[1,128]{1,0:T(1,128)S(1)}) custom-call(s32[180]{0:T(256)S(1)} %copy-done.4, f32[2]{0:T(128)S(1)} %pad_maximum_fusion.1.scalars, bf16[48,256,256]{2,1,0:T(8,128)(2,1)S(1)} %bitcast.11, bf16[8,256,128]{2,1,0:T(8,128)(2,1)S(1)} %collective-permute-done.45.mid, ...), custom_call_target="tpu_custom_call" | custom-call | flops 201326592 | bytes 7602176 | tf_op jit(solution)/shard_map/pallas_call | solution.py:315
  228.1 10.3 %all_to_all.6 = f32[16,1,128]{2,1,0:T(1,128)S(1)} all-to-all(f32[16,1,128]{2,1,0:T(1,128)S(1)} %broadcast_in_dim.9), channel_id=1, replica_groups=mesh['groups'=2,'row'=16] {'row'}, dimensions={0} | all-to-all | bytes 16384 | tf_op jit(solution)/shard_map/all_to_all | solution.py:344
  (136 shorter events, 70.7 us)
Async XLA Ops:
  1.9 16.5 %collective-permute-start.3 = (bf16[8,256,128]{2,1,0:T(8,128)(2,1)S(1)}, bf16[8,256,128]{2,1,0:T(8,128)(2,1)S(1)}, u32[]{:S(2)}, u32[]{:S(2)}) collective-permute-start(bf16[8,256,128]{2,1,0:T(8,128)(2,1)S(1)} %convert_element_type.12.refs_0_.own), channel_id=1, source_target_pairs={{0,8},{1,9},{2,10},{3,11},{12,4},{13,5},{14,6},{15,7},{4,0},{5,1},... | collective-permute-start | bytes 1572872 | tf_op jit(solution)/shard_map/ppermute | solution.py:334
  6.0 24.2 %collective-permute-start.4 = (bf16[8,256,128]{2,1,0:T(8,128)(2,1)S(1)}, bf16[8,256,128]{2,1,0:T(8,128)(2,1)S(1)}, u32[]{:S(2)}, u32[]{:S(2)}) collective-permute-start(bf16[8,256,128]{2,1,0:T(8,128)(2,1)S(1)} %convert_element_type.12.refs_0_.own), channel_id=1, source_target_pairs={{0,4},{1,5},{2,6},{3,7},{12,8},{13,9},{14,10},{15,11},{4,12},{5,13... | collective-permute-start | bytes 1572872 | tf_op jit(solution)/shard_map/ppermute | solution.py:334
  19.6 12.0 %collective-permute-start.5 = (bf16[6,256,128]{2,1,0:T(8,128)(2,1)S(1)}, bf16[6,256,128]{2,1,0:T(8,128)(2,1)S(1)}, u32[]{:S(2)}, u32[]{:S(2)}) collective-permute-start(bf16[6,256,128]{2,1,0:T(8,128)(2,1)S(1)} %get-tuple-element.80), channel_id=1, source_target_pairs={{0,2},{1,3},{2,0},{3,1},{4,6},{5,7},{6,4},{7,5},{8,10},{9,11},{10,... | collective-permute-start | bytes 1179656 | tf_op jit(solution)/shard_map/ppermute | solution.py:338
  21.2 17.9 %collective-permute-start.6 = (bf16[6,256,128]{2,1,0:T(8,128)(2,1)S(1)}, bf16[6,256,128]{2,1,0:T(8,128)(2,1)S(1)}, u32[]{:S(2)}, u32[]{:S(2)}) collective-permute-start(bf16[6,256,128]{2,1,0:T(8,128)(2,1)S(1)} %get-tuple-element.81), channel_id=1, source_target_pairs={{0,3},{1,2},{2,1},{3,0},{4,7},{5,6},{6,5},{7,4},{8,11},{9,10},{10,... | collective-permute-start | bytes 1179656 | tf_op jit(solution)/shard_map/ppermute | solution.py:338
  40.8 17.9 %collective-permute-start.11 = (bf16[8,256,128]{2,1,0:T(8,128)(2,1)S(1)}, bf16[8,256,128]{2,1,0:T(8,128)(2,1)S(1)}, u32[]{:S(2)}, u32[]{:S(2)}) collective-permute-start(bf16[8,256,128]{2,1,0:T(8,128)(2,1)S(1)} %collective-permute-done.3.refs_1_.first), channel_id=1, source_target_pairs={{4,0},{5,1},{6,2},{7,3},{8,12},{9,13},{10,14},{11,15},{20,16},{21,... | collective-permute-start | bytes 1572872 | tf_op jit(solution)/shard_map/ppermute | solution.py:334
  43.4 16.0 %collective-permute-start.8 = (f32[1,128]{1,0:T(1,128)S(1)}, f32[1,128]{1,0:T(1,128)S(1)}, u32[]{:S(2)}, u32[]{:S(2)}) collective-permute-start(f32[1,128]{1,0:T(1,128)S(1)} %broadcast_in_dim.8), channel_id=1, source_target_pairs={{0,4},{1,5},{2,6},{3,7},{4,0},{5,1},{6,2},{7,3},{8,12},{9,13},{10,... | collective-permute-start | bytes 1544 | tf_op jit(solution)/shard_map/ppermute | solution.py:338
  48.4 12.3 %collective-permute-start.15 = (bf16[3,256,128]{2,1,0:T(8,128)(2,1)S(1)}, bf16[3,256,128]{2,1,0:T(8,128)(2,1)S(1)}, u32[]{:S(2)}, u32[]{:S(2)}) collective-permute-start(bf16[3,256,128]{2,1,0:T(8,128)(2,1)S(1)} %get-tuple-element.91), channel_id=1, source_target_pairs={{0,2},{1,3},{2,0},{3,1},{4,6},{5,7},{6,4},{7,5},{8,10},{9,11},{10,... | collective-permute-start | bytes 589832 | tf_op jit(solution)/shard_map/ppermute | solution.py:338
  48.7 13.4 %collective-permute-start.16 = (bf16[3,256,128]{2,1,0:T(8,128)(2,1)S(1)}, bf16[3,256,128]{2,1,0:T(8,128)(2,1)S(1)}, u32[]{:S(2)}, u32[]{:S(2)}) collective-permute-start(bf16[3,256,128]{2,1,0:T(8,128)(2,1)S(1)} %get-tuple-element.92), channel_id=1, source_target_pairs={{0,3},{1,2},{2,1},{3,0},{4,7},{5,6},{6,5},{7,4},{8,11},{9,10},{10,... | collective-permute-start | bytes 589832 | tf_op jit(solution)/shard_map/ppermute | solution.py:338
  73.0 14.6 %collective-permute-start.18 = (bf16[8,256,128]{2,1,0:T(8,128)(2,1)S(1)}, bf16[8,256,128]{2,1,0:T(8,128)(2,1)S(1)}, u32[]{:S(2)}, u32[]{:S(2)}) collective-permute-start(bf16[8,256,128]{2,1,0:T(8,128)(2,1)S(1)} %get-tuple-element.93.own.refs_0_), channel_id=1, source_target_pairs={{0,8},{1,9},{2,10},{3,11},{12,4},{13,5},{14,6},{15,7},{4,0},{5,1},... | collective-permute-start | bytes 1572872 | tf_op jit(solution)/shard_map/ppermute | solution.py:334
  75.3 24.9 %collective-permute-start.25 = (bf16[8,256,128]{2,1,0:T(8,128)(2,1)S(1)}, bf16[8,256,128]{2,1,0:T(8,128)(2,1)S(1)}, u32[]{:S(2)}, u32[]{:S(2)}) collective-permute-start(bf16[8,256,128]{2,1,0:T(8,128)(2,1)S(1)} %get-tuple-element.93.own.refs_0_), channel_id=1, source_target_pairs={{0,4},{1,5},{2,6},{3,7},{12,8},{13,9},{14,10},{15,11},{4,12},{5,13... | collective-permute-start | bytes 1572872 | tf_op jit(solution)/shard_map/ppermute | solution.py:334
  88.2 12.1 %collective-permute-start.26 = (bf16[3,256,128]{2,1,0:T(8,128)(2,1)S(1)}, bf16[3,256,128]{2,1,0:T(8,128)(2,1)S(1)}, u32[]{:S(2)}, u32[]{:S(2)}) collective-permute-start(bf16[3,256,128]{2,1,0:T(8,128)(2,1)S(1)} %get-tuple-element.100), channel_id=1, source_target_pairs={{0,2},{1,3},{2,0},{3,1},{4,6},{5,7},{6,4},{7,5},{8,10},{9,11},{10,... | collective-permute-start | bytes 589832 | tf_op jit(solution)/shard_map/ppermute | solution.py:338
  89.1 13.8 %collective-permute-start.17 = (bf16[8,256,128]{2,1,0:T(8,128)(2,1)S(1)}, bf16[8,256,128]{2,1,0:T(8,128)(2,1)S(1)}, u32[]{:S(2)}, u32[]{:S(2)}) collective-permute-start(bf16[8,256,128]{2,1,0:T(8,128)(2,1)S(1)} %get-tuple-element.93.own.refs_0_), channel_id=1, source_target_pairs={{4,8},{5,9},{6,10},{7,11},{8,4},{9,5},{10,6},{11,7},{20,24},{21,25... | collective-permute-start | bytes 1572872 | tf_op jit(solution)/shard_map/ppermute | solution.py:334
  89.8 21.6 %collective-permute-start.21 = (bf16[8,256,128]{2,1,0:T(8,128)(2,1)S(1)}, bf16[8,256,128]{2,1,0:T(8,128)(2,1)S(1)}, u32[]{:S(2)}, u32[]{:S(2)}) collective-permute-start(bf16[8,256,128]{2,1,0:T(8,128)(2,1)S(1)} %collective-permute-done.18.refs_0_.first.refs_1_), channel_id=1, source_target_pairs={{4,0},{5,1},{6,2},{7,3},{8,12},{9,13},{10,14},{11,15},{20,16},{21,... | collective-permute-start | bytes 1572872 | tf_op jit(solution)/shard_map/ppermute | solution.py:334
  100.9 13.1 %collective-permute-start.28 = (bf16[9,256,128]{2,1,0:T(8,128)(2,1)S(1)}, bf16[9,256,128]{2,1,0:T(8,128)(2,1)S(1)}, u32[]{:S(2)}, u32[]{:S(2)}) collective-permute-start(bf16[9,256,128]{2,1,0:T(8,128)(2,1)S(1)} %get-tuple-element.103), channel_id=1, source_target_pairs={{0,1},{1,0},{2,3},{3,2},{4,5},{5,4},{6,7},{7,6},{8,9},{9,8},{10,11... | collective-permute-start | bytes 1769480 | tf_op jit(solution)/shard_map/ppermute | solution.py:338
  101.0 11.7 %collective-permute-start.29 = (bf16[3,256,128]{2,1,0:T(8,128)(2,1)S(1)}, bf16[3,256,128]{2,1,0:T(8,128)(2,1)S(1)}, u32[]{:S(2)}, u32[]{:S(2)}) collective-permute-start(bf16[3,256,128]{2,1,0:T(8,128)(2,1)S(1)} %get-tuple-element.108), channel_id=1, source_target_pairs={{0,2},{1,3},{2,0},{3,1},{4,6},{5,7},{6,4},{7,5},{8,10},{9,11},{10,... | collective-permute-start | bytes 589832 | tf_op jit(solution)/shard_map/ppermute | solution.py:338
  101.5 12.4 %collective-permute-start.30 = (bf16[3,256,128]{2,1,0:T(8,128)(2,1)S(1)}, bf16[3,256,128]{2,1,0:T(8,128)(2,1)S(1)}, u32[]{:S(2)}, u32[]{:S(2)}) collective-permute-start(bf16[3,256,128]{2,1,0:T(8,128)(2,1)S(1)} %get-tuple-element.109), channel_id=1, source_target_pairs={{0,3},{1,2},{2,1},{3,0},{4,7},{5,6},{6,5},{7,4},{8,11},{9,10},{10,... | collective-permute-start | bytes 589832 | tf_op jit(solution)/shard_map/ppermute | solution.py:338
  124.7 14.4 %collective-permute-start.32 = (bf16[8,256,128]{2,1,0:T(8,128)(2,1)S(1)}, bf16[8,256,128]{2,1,0:T(8,128)(2,1)S(1)}, u32[]{:S(2)}, u32[]{:S(2)}) collective-permute-start(bf16[8,256,128]{2,1,0:T(8,128)(2,1)S(1)} %get-tuple-element.112.own.refs_0_), channel_id=1, source_target_pairs={{0,8},{1,9},{2,10},{3,11},{12,4},{13,5},{14,6},{15,7},{4,0},{5,1},... | collective-permute-start | bytes 1572872 | tf_op jit(solution)/shard_map/ppermute | solution.py:334
  126.7 24.7 %collective-permute-start.39 = (bf16[8,256,128]{2,1,0:T(8,128)(2,1)S(1)}, bf16[8,256,128]{2,1,0:T(8,128)(2,1)S(1)}, u32[]{:S(2)}, u32[]{:S(2)}) collective-permute-start(bf16[8,256,128]{2,1,0:T(8,128)(2,1)S(1)} %get-tuple-element.112.own.refs_0_), channel_id=1, source_target_pairs={{0,4},{1,5},{2,6},{3,7},{12,8},{13,9},{14,10},{15,11},{4,12},{5,13... | collective-permute-start | bytes 1572872 | tf_op jit(solution)/shard_map/ppermute | solution.py:334
  139.6 11.7 %collective-permute-start.40 = (bf16[3,256,128]{2,1,0:T(8,128)(2,1)S(1)}, bf16[3,256,128]{2,1,0:T(8,128)(2,1)S(1)}, u32[]{:S(2)}, u32[]{:S(2)}) collective-permute-start(bf16[3,256,128]{2,1,0:T(8,128)(2,1)S(1)} %get-tuple-element.119), channel_id=1, source_target_pairs={{0,2},{1,3},{2,0},{3,1},{4,6},{5,7},{6,4},{7,5},{8,10},{9,11},{10,... | collective-permute-start | bytes 589832 | tf_op jit(solution)/shard_map/ppermute | solution.py:338
  140.6 13.3 %collective-permute-start.31 = (bf16[8,256,128]{2,1,0:T(8,128)(2,1)S(1)}, bf16[8,256,128]{2,1,0:T(8,128)(2,1)S(1)}, u32[]{:S(2)}, u32[]{:S(2)}) collective-permute-start(bf16[8,256,128]{2,1,0:T(8,128)(2,1)S(1)} %get-tuple-element.112.own.refs_0_), channel_id=1, source_target_pairs={{4,8},{5,9},{6,10},{7,11},{8,4},{9,5},{10,6},{11,7},{20,24},{21,25... | collective-permute-start | bytes 1572872 | tf_op jit(solution)/shard_map/ppermute | solution.py:334
  141.3 21.0 %collective-permute-start.35 = (bf16[8,256,128]{2,1,0:T(8,128)(2,1)S(1)}, bf16[8,256,128]{2,1,0:T(8,128)(2,1)S(1)}, u32[]{:S(2)}, u32[]{:S(2)}) collective-permute-start(bf16[8,256,128]{2,1,0:T(8,128)(2,1)S(1)} %collective-permute-done.32.refs_0_.first.refs_1_), channel_id=1, source_target_pairs={{4,0},{5,1},{6,2},{7,3},{8,12},{9,13},{10,14},{11,15},{20,16},{21,... | collective-permute-start | bytes 1572872 | tf_op jit(solution)/shard_map/ppermute | solution.py:334
  151.9 13.0 %collective-permute-start.42 = (bf16[9,256,128]{2,1,0:T(8,128)(2,1)S(1)}, bf16[9,256,128]{2,1,0:T(8,128)(2,1)S(1)}, u32[]{:S(2)}, u32[]{:S(2)}) collective-permute-start(bf16[9,256,128]{2,1,0:T(8,128)(2,1)S(1)} %get-tuple-element.122), channel_id=1, source_target_pairs={{0,1},{1,0},{2,3},{3,2},{4,5},{5,4},{6,7},{7,6},{8,9},{9,8},{10,11... | collective-permute-start | bytes 1769480 | tf_op jit(solution)/shard_map/ppermute | solution.py:338
  152.0 11.7 %collective-permute-start.43 = (bf16[3,256,128]{2,1,0:T(8,128)(2,1)S(1)}, bf16[3,256,128]{2,1,0:T(8,128)(2,1)S(1)}, u32[]{:S(2)}, u32[]{:S(2)}) collective-permute-start(bf16[3,256,128]{2,1,0:T(8,128)(2,1)S(1)} %get-tuple-element.127), channel_id=1, source_target_pairs={{0,2},{1,3},{2,0},{3,1},{4,6},{5,7},{6,4},{7,5},{8,10},{9,11},{10,... | collective-permute-start | bytes 589832 | tf_op jit(solution)/shard_map/ppermute | solution.py:338
  152.6 12.4 %collective-permute-start.44 = (bf16[3,256,128]{2,1,0:T(8,128)(2,1)S(1)}, bf16[3,256,128]{2,1,0:T(8,128)(2,1)S(1)}, u32[]{:S(2)}, u32[]{:S(2)}) collective-permute-start(bf16[3,256,128]{2,1,0:T(8,128)(2,1)S(1)} %get-tuple-element.128), channel_id=1, source_target_pairs={{0,3},{1,2},{2,1},{3,0},{4,7},{5,6},{6,5},{7,4},{8,11},{9,10},{10,... | collective-permute-start | bytes 589832 | tf_op jit(solution)/shard_map/ppermute | solution.py:338
  175.6 14.4 %collective-permute-start.46 = (bf16[8,256,128]{2,1,0:T(8,128)(2,1)S(1)}, bf16[8,256,128]{2,1,0:T(8,128)(2,1)S(1)}, u32[]{:S(2)}, u32[]{:S(2)}) collective-permute-start(bf16[8,256,128]{2,1,0:T(8,128)(2,1)S(1)} %get-tuple-element.131.own.refs_0_), channel_id=1, source_target_pairs={{0,8},{1,9},{2,10},{3,11},{12,4},{13,5},{14,6},{15,7},{4,0},{5,1},... | collective-permute-start | bytes 1572872 | tf_op jit(solution)/shard_map/ppermute | solution.py:334
  177.7 24.7 %collective-permute-start.53 = (bf16[8,256,128]{2,1,0:T(8,128)(2,1)S(1)}, bf16[8,256,128]{2,1,0:T(8,128)(2,1)S(1)}, u32[]{:S(2)}, u32[]{:S(2)}) collective-permute-start(bf16[8,256,128]{2,1,0:T(8,128)(2,1)S(1)} %get-tuple-element.131.own.refs_0_), channel_id=1, source_target_pairs={{0,4},{1,5},{2,6},{3,7},{12,8},{13,9},{14,10},{15,11},{4,12},{5,13... | collective-permute-start | bytes 1572872 | tf_op jit(solution)/shard_map/ppermute | solution.py:334
  190.6 11.7 %collective-permute-start.54 = (bf16[3,256,128]{2,1,0:T(8,128)(2,1)S(1)}, bf16[3,256,128]{2,1,0:T(8,128)(2,1)S(1)}, u32[]{:S(2)}, u32[]{:S(2)}) collective-permute-start(bf16[3,256,128]{2,1,0:T(8,128)(2,1)S(1)} %get-tuple-element.138), channel_id=1, source_target_pairs={{0,2},{1,3},{2,0},{3,1},{4,6},{5,7},{6,4},{7,5},{8,10},{9,11},{10,... | collective-permute-start | bytes 589832 | tf_op jit(solution)/shard_map/ppermute | solution.py:338
  191.7 13.2 %collective-permute-start.45 = (bf16[8,256,128]{2,1,0:T(8,128)(2,1)S(1)}, bf16[8,256,128]{2,1,0:T(8,128)(2,1)S(1)}, u32[]{:S(2)}, u32[]{:S(2)}) collective-permute-start(bf16[8,256,128]{2,1,0:T(8,128)(2,1)S(1)} %get-tuple-element.131.own.refs_0_), channel_id=1, source_target_pairs={{4,8},{5,9},{6,10},{7,11},{8,4},{9,5},{10,6},{11,7},{20,24},{21,25... | collective-permute-start | bytes 1572872 | tf_op jit(solution)/shard_map/ppermute | solution.py:334
  192.4 21.0 %collective-permute-start.49 = (bf16[8,256,128]{2,1,0:T(8,128)(2,1)S(1)}, bf16[8,256,128]{2,1,0:T(8,128)(2,1)S(1)}, u32[]{:S(2)}, u32[]{:S(2)}) collective-permute-start(bf16[8,256,128]{2,1,0:T(8,128)(2,1)S(1)} %collective-permute-done.46.refs_0_.first.refs_1_), channel_id=1, source_target_pairs={{4,0},{5,1},{6,2},{7,3},{8,12},{9,13},{10,14},{11,15},{20,16},{21,... | collective-permute-start | bytes 1572872 | tf_op jit(solution)/shard_map/ppermute | solution.py:334
  203.0 13.0 %collective-permute-start.56 = (bf16[9,256,128]{2,1,0:T(8,128)(2,1)S(1)}, bf16[9,256,128]{2,1,0:T(8,128)(2,1)S(1)}, u32[]{:S(2)}, u32[]{:S(2)}) collective-permute-start(bf16[9,256,128]{2,1,0:T(8,128)(2,1)S(1)} %get-tuple-element.141), channel_id=1, source_target_pairs={{0,1},{1,0},{2,3},{3,2},{4,5},{5,4},{6,7},{7,6},{8,9},{9,8},{10,11... | collective-permute-start | bytes 1769480 | tf_op jit(solution)/shard_map/ppermute | solution.py:338
  203.1 11.6 %collective-permute-start.57 = (bf16[3,256,128]{2,1,0:T(8,128)(2,1)S(1)}, bf16[3,256,128]{2,1,0:T(8,128)(2,1)S(1)}, u32[]{:S(2)}, u32[]{:S(2)}) collective-permute-start(bf16[3,256,128]{2,1,0:T(8,128)(2,1)S(1)} %get-tuple-element.146), channel_id=1, source_target_pairs={{0,2},{1,3},{2,0},{3,1},{4,6},{5,7},{6,4},{7,5},{8,10},{9,11},{10,... | collective-permute-start | bytes 589832 | tf_op jit(solution)/shard_map/ppermute | solution.py:338
  203.6 12.4 %collective-permute-start.58 = (bf16[3,256,128]{2,1,0:T(8,128)(2,1)S(1)}, bf16[3,256,128]{2,1,0:T(8,128)(2,1)S(1)}, u32[]{:S(2)}, u32[]{:S(2)}) collective-permute-start(bf16[3,256,128]{2,1,0:T(8,128)(2,1)S(1)} %get-tuple-element.147), channel_id=1, source_target_pairs={{0,3},{1,2},{2,1},{3,0},{4,7},{5,6},{6,5},{7,4},{8,11},{9,10},{10,... | collective-permute-start | bytes 589832 | tf_op jit(solution)/shard_map/ppermute | solution.py:338
  (34 other events, 354.0 us)

commit v10 on v9

--- a/solution.py
+++ b/solution.py
@@ -146,14 +146,14 @@
     )(rows, cols, count, tiles)
 
 
-def table_kernel(layout, mine, asked, table):
+def fill_table(layout, mine, notes, table):
     cap = layout.cap
     keys = 16 * cap
     _, yc, _, zs = whereabouts()
     for j in range(4):
-        for flip in (1, 2, 3):
+        for flip, asked in enumerate(notes, 1):
             for r in range(cap):
-                table[layout.pack(j, flip) + r] = asked[flip * LANES + (zs[j] * 4 + yc) * cap + r]
+                table[layout.pack(j, flip) + r] = asked[0, (zs[j] * 4 + yc) * cap + r].astype(jnp.int32)
     for i, (j, flip) in enumerate(EARLY + LATE):
         for r in range(cap):
             key = (zs[j] * 4 + (yc ^ flip)) * cap + r
@@ -163,14 +163,22 @@
             table[at + 2] = mine[2 * keys + key]
 
 
-def make_table(layout, mine, asked):
-    return pl.pallas_call(
-        functools.partial(table_kernel, layout),
-        out_shape=jax.ShapeDtypeStruct((layout.size,), jnp.int32),
-        in_specs=[SMEM] * 2,
-        out_specs=SMEM,
+def start_kernel(layout, mine, note1, note2, note3, own, first, table, out2, out3):
+    fill_table(layout, mine, (note1, note2, note3), table)
+    other_y_kernel(layout, (0, 1), table, own, first, out2, out3)
+
+
+def start(layout, mine, notes, own, first):
+    _, tile, repl = own.shape
+    packs = jax.ShapeDtypeStruct((2 * layout.cap, tile, repl), jnp.bfloat16)
+    return pl.pallas_call(
+        functools.partial(start_kernel, layout),
+        out_shape=(jax.ShapeDtypeStruct((layout.size,), jnp.int32), packs, packs),
+        in_specs=[SMEM] * 4 + [VMEM] * 2,
+        out_specs=(SMEM, VMEM, VMEM),
+        compiler_params=params(),
         cost_estimate=pl.CostEstimate(flops=0, bytes_accessed=0, transcendentals=0),
-    )(mine, asked)
+    )(mine, *notes, own, first)
 
 
 def copy_asked(layout, table, j, flip, shard, out, first=0):
@@ -223,23 +231,13 @@
     )(table, *arrays)
 
 
-def multiply(layout, table, tiles, xbuf, first, number, field):
-    def some(start, place):
-        prods = [
-            jnp.dot(tiles[table[layout.entry(start + i)]], xbuf[place + i], preferred_element_type=jnp.float32)
-            for i in range(GROUP)
-        ]
-        for i, prod in enumerate(prods):
-            field[table[layout.entry(start + i) + 1]] += prod
-
-    if number <= 3 * GROUP:
-        for place in range(0, number, GROUP):
-            some(first + place, place)
-    else:
-
-        @pl.loop(0, number // GROUP)
-        def _(g):
-            some(first + g * GROUP, g * GROUP)
+def multiply(layout, table, tiles, blocks, first, field):
+    prods = [
+        jnp.dot(tiles[table[layout.entry(first + i)]], block, preferred_element_type=jnp.float32)
+        for i, block in enumerate(blocks)
+    ]
+    for i, prod in enumerate(prods):
+        field[table[layout.entry(first + i) + 1]] += prod
 
 
 def take_own(layout, table, entry, shard, xbuf, place):
@@ -259,7 +257,10 @@
         copy_part(cap, refs[ref], part, xbuf, base + 2 * cap)
         copy_part(cap, refs[ref + 1], part, xbuf, base + 3 * cap)
     field[...] = jnp.zeros_like(field)
-    multiply(layout, table, tiles, xbuf, 0, 12 * cap, field)
+
+    @pl.loop(0, 12 * cap // GROUP)
+    def _(g):
+        multiply(layout, table, tiles, [xbuf[g * GROUP + i] for i in range(GROUP)], g * GROUP, field)
 
 
 def early(layout, parts, table, tiles, arrays):
@@ -282,10 +283,10 @@
     blocks = xpos.shape[0]
     cap = layout.cap
     by_place(mid, out, lambda shard: take_own(layout, table, 12 * cap, shard, xbuf, 0))
-    for i, got in enumerate((core, got2, got3)):
-        copy_part(cap, got, 0, xbuf, (1 + i) * cap)
     acc[...] = field[...]
-    multiply(layout, table, tiles, xbuf, 12 * cap, 4 * cap, acc)
+    blocks_in = [ref[r] for ref in (xbuf, core, got2, got3) for r in range(cap)]
+    for first in range(0, 4 * cap, GROUP):
+        multiply(layout, table, tiles, blocks_in[first : first + GROUP], 12 * cap + first, acc)
     total = jnp.zeros((1, xpos.shape[2]), jnp.float32)
     for b in range(blocks):
         x, h = xpos[b], acc[b]
@@ -318,7 +319,7 @@
         in_specs=[SMEM, SMEM] + [VMEM] * (1 + len(sources) + 3),
         out_specs=(VMEM,) * (2 + len(extra)),
         scratch_shapes=[
-            pltpu.VMEM((entries, tile, repl), jnp.bfloat16),
+            pltpu.VMEM((layout.cap, tile, repl), jnp.bfloat16),
             pltpu.VMEM((blocks + 1, tile, repl), jnp.float32),
         ],
         compiler_params=params(),
@@ -363,8 +364,7 @@
     ymom = momenta.reshape(blocks, tile, repl)
     own0 = xpos.astype(jnp.bfloat16)
     mine, note = plan(layout, blocks, tile_rows, tile_cols, counts, tiles)
-    notes = jnp.concatenate([note] + [across(flip, note) for flip in (1, 2, 3)])
-    table = make_table(layout, mine, notes.astype(jnp.int32).reshape(-1))
+    notes = [across(flip, note) for flip in (1, 2, 3)]
     packs0 = None
     for step in range(STEPS):
         last = step == STEPS - 1
@@ -372,9 +372,11 @@
         own2 = along_z(SECOND, own0)
         mid = along_z(MIDDLE, own0)
         if step == 0:
+            own1, notes = lax.optimization_barrier((own1, notes))
             out = along_z(OUTWARD, own1)
-            got1 = to_other_y(other_y((0, 1), [own0, own1]))
-            own2, got1 = lax.optimization_barrier((own2, got1))
+            table, *packs01 = start(layout, mine, notes, own0, own1)
+            got1 = to_other_y(packs01)
+            own2, got1, mid, out = lax.optimization_barrier((own2, got1, mid, out))
             parts = ((4, 0), (4, 1), (6, 0))
             got = got1
         else:
@@ -390,13 +392,13 @@
         core = across(1, packs2[2])
         if step == 0:
             notes, core = lax.optimization_barrier((notes, core))
-            plane = jnp.broadcast_to(jnp.sum(notes[:, SUM_AT]), (1, LANES))
+            plane = note + notes[0] + notes[1] + notes[2]
             half = plane + across(4, plane)
         packs3 = pack(functools.partial(third_kernel, layout), [cap] * 3, table, [mid, out])
         far = [mid, out, across(1, packs3[2])] + to_other_y(packs3)
         field = early(layout, parts, table, tiles, [own0, own1, own2, core] + got)
         if step == 0:
-            total = (half + across(8, half))[0, 0]
+            total = (half + across(8, half))[0, SUM_AT]
             coeff = 0.7 * jnp.sqrt((order - 1) / total)
         scalars = jnp.stack([jnp.float32(0.4 - 0.1 * step), coeff])
         outs = late(layout, last, table, scalars, tiles, far, field, xpos, ymom)

time: 239 us -> 229 us (0.958)
  waiting for transfers between devices: 135 us -> 128 us
  other arithmetic: 5.35 us -> 2.14 us
    ppermute x16, waiting for transfers between devices: 76.8 us -> 70.2 us  [along_z(): lax.ppermute(value, 'row', [(a * 4 + i, b * 4 + i) for a, b in pairs for...]
    pallas_call x12 -> x11, Pallas kernels: 7.24 us -> 6.63 us  [pack(): pl.pallas_call(kernel, out_shape=[jax.ShapeDtypeStruct((size, tile, repl)...]
  transfers between devices with their start and end apart: 59 -> 59, of which waited for: 28 -> 33; matrix products, arithmetic and copies ran while one was open for 2% -> 0% of each run, Pallas kernels for 10% -> 10%
where the time goes in v10:
time: 229 us
  waiting for transfers between devices  128 us (56%)
  starting transfers between devices  48.9 us (21%)
  Pallas kernels  32.3 us (14%)
  blocking collectives  10.8 us (5%)
  local copies, waits for them, and re-layouts  4.06 us (2%)
  between operations  2.42 us (1%)
    ppermute x16, waiting for transfers between devices, along_z(): lax.ppermute(value, 'row', [(a * 4 + i, b * 4 + i) for a, b in pairs for...  70.2 us
    ppermute x43, waiting for transfers between devices, across(): return lax.ppermute(value, 'row', [(i, i ^ flip) for i in range(16)])  58.1 us
    ppermute x43, starting transfers between devices, across(): return lax.ppermute(value, 'row', [(i, i ^ flip) for i in range(16)])  30.7 us
    ppermute x16, starting transfers between devices, along_z(): lax.ppermute(value, 'row', [(a * 4 + i, b * 4 + i) for a, b in pairs for...  18.2 us
    pallas_call x4, Pallas kernels, early(): pl.pallas_call(functools.partial(early_kernel, layout, parts), out_shape=...  12.2 us
    all_to_all x1, blocking collectives, row_sum(): lax.all_to_all(spread, 'row', split_axis=0, concat_axis=0, tiled=True)  10.8 us
    pallas_call x4, Pallas kernels, late(): pl.pallas_call(functools.partial(late_kernel, layout, last), out_shape=(s...  7.95 us
    pallas_call x11, Pallas kernels, pack(): pl.pallas_call(kernel, out_shape=[jax.ShapeDtypeStruct((size, tile, repl)...  6.63 us
  transfers between devices with their start and end apart: 59, of which 33 were waited for; matrix products, arithmetic and copies ran while one was open for 0% of the time, Pallas kernels for 10%

profile of v10, /device:TPU:0, one launch (start us, length us, event | category | flops | bytes accessed | tf_op | source)
XLA Modules:
  0.0 229.1 jit_solution(8810191313239850772)
XLA Ops:
  1.9 4.1 %collective-permute-start = (bf16[8,256,128]{2,1,0:T(8,128)(2,1)S(1)}, bf16[8,256,128]{2,1,0:T(8,128)(2,1)S(1)}, u32[]{:S(2)}, u32[]{:S(2)}) collective-permute-start(bf16[8,256,128]{2,1,0:T(8,128)(2,1)S(1)} %convert_element_type.3.own.refs_0_), channel_id=1, source_target_pairs={{0,8},{1,9},{2,10},{3,11},{12,4},{13,5},{14,6},{15,7},{4,0},{5,1},... | collective-permute-start | bytes 1572872 | tf_op jit(solution)/shard_map/ppermute | solution.py:335
  6.7 4.2 %shard_map.85 = (s32[144]{0:T(256)}, f32[1,128]{1,0:T(1,128)}) custom-call(s32[48]{0:T(128)} %rows.1, s32[48]{0:T(128)} %cols.1, s32[1]{0:T(128)S(6)} %copy.10.count, bf16[48,256,256]{2,1,0:T(8,128)(2,1)} %tiles.17), custom_call_target="tpu_custom_call" | custom-call | tf_op jit(solution)/shard_map/pallas_call | solution.py:131
  15.6 2.8 %collective-permute-done.first.refs_1_ = bf16[8,256,128]{2,1,0:T(8,128)(2,1)S(1)} collective-permute-done((bf16[8,256,128]{2,1,0:T(8,128)(2,1)S(1)}, bf16[8,256,128]{2,1,0:T(8,128)(2,1)S(1)}, u32[]{:S(2)}, u32[]{:S(2)}) %collective-permute-start) | collective-permute-done | bytes 524320 | tf_op jit(solution)/shard_map/ppermute | solution.py:335
  23.4 7.0 %collective-permute-done.4.second.refs_2_ = bf16[8,256,128]{2,1,0:T(8,128)(2,1)S(1)} collective-permute-done((bf16[8,256,128]{2,1,0:T(8,128)(2,1)S(1)}, bf16[8,256,128]{2,1,0:T(8,128)(2,1)S(1)}, u32[]{:S(2)}, u32[]{:S(2)}) %collective-permute-start.4) | collective-permute-done | bytes 524320 | tf_op jit(solution)/shard_map/ppermute | solution.py:335
  30.4 3.6 %collective-permute-done.5.refs_4_ = bf16[6,256,128]{2,1,0:T(8,128)(2,1)S(1)} collective-permute-done((bf16[6,256,128]{2,1,0:T(8,128)(2,1)S(1)}, bf16[6,256,128]{2,1,0:T(8,128)(2,1)S(1)}, u32[]{:S(2)}, u32[]{:S(2)}) %collective-permute-start.5) | collective-permute-done | bytes 393248 | tf_op jit(solution)/shard_map/ppermute | solution.py:339
  33.9 4.2 %collective-permute-done.6.refs_5_ = bf16[6,256,128]{2,1,0:T(8,128)(2,1)S(1)} collective-permute-done((bf16[6,256,128]{2,1,0:T(8,128)(2,1)S(1)}, bf16[6,256,128]{2,1,0:T(8,128)(2,1)S(1)}, u32[]{:S(2)}, u32[]{:S(2)}) %collective-permute-start.6) | collective-permute-done | bytes 393248 | tf_op jit(solution)/shard_map/ppermute | solution.py:339
  38.2 3.3 %collective-permute-done.8.out = bf16[8,256,128]{2,1,0:T(8,128)(2,1)S(1)} collective-permute-done((bf16[8,256,128]{2,1,0:T(8,128)(2,1)S(1)}, bf16[8,256,128]{2,1,0:T(8,128)(2,1)S(1)}, u32[]{:S(2)}, u32[]{:S(2)}) %collective-permute-start.8) | collective-permute-done | bytes 524320 | tf_op jit(solution)/shard_map/ppermute | solution.py:335
  53.3 2.8 %copy-done = bf16[48,256,256]{2,1,0:T(8,128)(2,1)S(1)} copy-done((bf16[48,256,256]{2,1,0:T(8,128)(2,1)S(1)}, bf16[48,256,256]{2,1,0:T(8,128)(2,1)}, u32[]{:S(2)}) %copy-start) | copy-done | bytes 6291480
  56.1 3.0 %shard_map.89.field = f32[9,256,128]{2,1,0:T(8,128)S(1)} custom-call(s32[180]{0:T(256)S(1)} %get-tuple-element.93.table, bf16[48,256,256]{2,1,0:T(8,128)(2,1)S(1)} %copy-done, bf16[8,256,128]{2,1,0:T(8,128)(2,1)S(1)} %convert_element_type.3.own.refs_0_, bf16[8,256,128]{2,1,0:T(8,128)(2,1)S(1)} %collective-permute-done.first.refs_1_, ...), custom_call_target="tpu_custom_call" | custom-call | tf_op jit(solution)/shard_map/pallas_call | solution.py:269
  67.0 6.3 %collective-permute-done.19.refs_4_ = bf16[3,256,128]{2,1,0:T(8,128)(2,1)S(1)} collective-permute-done((bf16[3,256,128]{2,1,0:T(8,128)(2,1)S(1)}, bf16[3,256,128]{2,1,0:T(8,128)(2,1)S(1)}, u32[]{:S(2)}, u32[]{:S(2)}) %collective-permute-start.19) | collective-permute-done | bytes 196640 | tf_op jit(solution)/shard_map/ppermute | solution.py:339
  75.2 2.4 %collective-permute-done.18.refs_0_.first.refs_1_ = bf16[8,256,128]{2,1,0:T(8,128)(2,1)S(1)} collective-permute-done((bf16[8,256,128]{2,1,0:T(8,128)(2,1)S(1)}, bf16[8,256,128]{2,1,0:T(8,128)(2,1)S(1)}, u32[]{:S(2)}, u32[]{:S(2)}) %collective-permute-start.18) | collective-permute-done | bytes 524320 | tf_op jit(solution)/shard_map/ppermute | solution.py:335
  81.8 8.0 %collective-permute-done.25.second.refs_2_ = bf16[8,256,128]{2,1,0:T(8,128)(2,1)S(1)} collective-permute-done((bf16[8,256,128]{2,1,0:T(8,128)(2,1)S(1)}, bf16[8,256,128]{2,1,0:T(8,128)(2,1)S(1)}, u32[]{:S(2)}, u32[]{:S(2)}) %collective-permute-start.25) | collective-permute-done | bytes 524320 | tf_op jit(solution)/shard_map/ppermute | solution.py:335
  92.4 8.5 %collective-permute-done.21.out = bf16[8,256,128]{2,1,0:T(8,128)(2,1)S(1)} collective-permute-done((bf16[8,256,128]{2,1,0:T(8,128)(2,1)S(1)}, bf16[8,256,128]{2,1,0:T(8,128)(2,1)S(1)}, u32[]{:S(2)}, u32[]{:S(2)}) %collective-permute-start.21) | collective-permute-done | bytes 524320 | tf_op jit(solution)/shard_map/ppermute | solution.py:335
  103.6 3.1 %shard_map.94.field = f32[9,256,128]{2,1,0:T(8,128)S(1)} custom-call(s32[180]{0:T(256)S(1)} %get-tuple-element.93.table, bf16[48,256,256]{2,1,0:T(8,128)(2,1)S(1)} %bitcast.8, bf16[8,256,128]{2,1,0:T(8,128)(2,1)S(1)} %get-tuple-element.111.own.refs_0_, bf16[8,256,128]{2,1,0:T(8,128)(2,1)S(1)} %collective-permute-done.18.refs_0_.first.refs_1_, ...), custom_call_target="tpu_custom_call" | custom-call | tf_op jit(solution)/shard_map/pallas_call | solution.py:269
  106.7 2.7 %collective-permute-done.23.got2 = bf16[3,256,128]{2,1,0:T(8,128)(2,1)S(1)} collective-permute-done((bf16[3,256,128]{2,1,0:T(8,128)(2,1)S(1)}, bf16[3,256,128]{2,1,0:T(8,128)(2,1)S(1)}, u32[]{:S(2)}, u32[]{:S(2)}) %collective-permute-start.23) | collective-permute-done | bytes 196640 | tf_op jit(solution)/shard_map/ppermute | solution.py:339
  109.4 3.3 %collective-permute-done.24.got3 = bf16[3,256,128]{2,1,0:T(8,128)(2,1)S(1)} collective-permute-done((bf16[3,256,128]{2,1,0:T(8,128)(2,1)S(1)}, bf16[3,256,128]{2,1,0:T(8,128)(2,1)S(1)}, u32[]{:S(2)}, u32[]{:S(2)}) %collective-permute-start.24) | collective-permute-done | bytes 196640 | tf_op jit(solution)/shard_map/ppermute | solution.py:339
  117.8 6.4 %collective-permute-done.33.refs_4_ = bf16[3,256,128]{2,1,0:T(8,128)(2,1)S(1)} collective-permute-done((bf16[3,256,128]{2,1,0:T(8,128)(2,1)S(1)}, bf16[3,256,128]{2,1,0:T(8,128)(2,1)S(1)}, u32[]{:S(2)}, u32[]{:S(2)}) %collective-permute-start.33) | collective-permute-done | bytes 196640 | tf_op jit(solution)/shard_map/ppermute | solution.py:339
  126.2 2.4 %collective-permute-done.32.refs_0_.first.refs_1_ = bf16[8,256,128]{2,1,0:T(8,128)(2,1)S(1)} collective-permute-done((bf16[8,256,128]{2,1,0:T(8,128)(2,1)S(1)}, bf16[8,256,128]{2,1,0:T(8,128)(2,1)S(1)}, u32[]{:S(2)}, u32[]{:S(2)}) %collective-permute-start.32) | collective-permute-done | bytes 524320 | tf_op jit(solution)/shard_map/ppermute | solution.py:335
  132.7 8.1 %collective-permute-done.39.second.refs_2_ = bf16[8,256,128]{2,1,0:T(8,128)(2,1)S(1)} collective-permute-done((bf16[8,256,128]{2,1,0:T(8,128)(2,1)S(1)}, bf16[8,256,128]{2,1,0:T(8,128)(2,1)S(1)}, u32[]{:S(2)}, u32[]{:S(2)}) %collective-permute-start.39) | collective-permute-done | bytes 524320 | tf_op jit(solution)/shard_map/ppermute | solution.py:335
  143.4 8.5 %collective-permute-done.35.out = bf16[8,256,128]{2,1,0:T(8,128)(2,1)S(1)} collective-permute-done((bf16[8,256,128]{2,1,0:T(8,128)(2,1)S(1)}, bf16[8,256,128]{2,1,0:T(8,128)(2,1)S(1)}, u32[]{:S(2)}, u32[]{:S(2)}) %collective-permute-start.35) | collective-permute-done | bytes 524320 | tf_op jit(solution)/shard_map/ppermute | solution.py:335
  154.6 3.1 %shard_map.99.field = f32[9,256,128]{2,1,0:T(8,128)S(1)} custom-call(s32[180]{0:T(256)S(1)} %get-tuple-element.93.table, bf16[48,256,256]{2,1,0:T(8,128)(2,1)S(1)} %bitcast.8, bf16[8,256,128]{2,1,0:T(8,128)(2,1)S(1)} %get-tuple-element.130.own.refs_0_, bf16[8,256,128]{2,1,0:T(8,128)(2,1)S(1)} %collective-permute-done.32.refs_0_.first.refs_1_, ...), custom_call_target="tpu_custom_call" | custom-call | tf_op jit(solution)/shard_map/pallas_call | solution.py:269
  157.7 2.8 %collective-permute-done.37.got2 = bf16[3,256,128]{2,1,0:T(8,128)(2,1)S(1)} collective-permute-done((bf16[3,256,128]{2,1,0:T(8,128)(2,1)S(1)}, bf16[3,256,128]{2,1,0:T(8,128)(2,1)S(1)}, u32[]{:S(2)}, u32[]{:S(2)}) %collective-permute-start.37) | collective-permute-done | bytes 196640 | tf_op jit(solution)/shard_map/ppermute | solution.py:339
  160.4 3.3 %collective-permute-done.38.got3 = bf16[3,256,128]{2,1,0:T(8,128)(2,1)S(1)} collective-permute-done((bf16[3,256,128]{2,1,0:T(8,128)(2,1)S(1)}, bf16[3,256,128]{2,1,0:T(8,128)(2,1)S(1)}, u32[]{:S(2)}, u32[]{:S(2)}) %collective-permute-start.38) | collective-permute-done | bytes 196640 | tf_op jit(solution)/shard_map/ppermute | solution.py:339
  168.8 6.5 %collective-permute-done.47.refs_4_ = bf16[3,256,128]{2,1,0:T(8,128)(2,1)S(1)} collective-permute-done((bf16[3,256,128]{2,1,0:T(8,128)(2,1)S(1)}, bf16[3,256,128]{2,1,0:T(8,128)(2,1)S(1)}, u32[]{:S(2)}, u32[]{:S(2)}) %collective-permute-start.47) | collective-permute-done | bytes 196640 | tf_op jit(solution)/shard_map/ppermute | solution.py:339
  177.2 2.4 %collective-permute-done.46.refs_0_.first.refs_1_ = bf16[8,256,128]{2,1,0:T(8,128)(2,1)S(1)} collective-permute-done((bf16[8,256,128]{2,1,0:T(8,128)(2,1)S(1)}, bf16[8,256,128]{2,1,0:T(8,128)(2,1)S(1)}, u32[]{:S(2)}, u32[]{:S(2)}) %collective-permute-start.46) | collective-permute-done | bytes 524320 | tf_op jit(solution)/shard_map/ppermute | solution.py:335
  183.7 8.1 %collective-permute-done.53.second.refs_2_ = bf16[8,256,128]{2,1,0:T(8,128)(2,1)S(1)} collective-permute-done((bf16[8,256,128]{2,1,0:T(8,128)(2,1)S(1)}, bf16[8,256,128]{2,1,0:T(8,128)(2,1)S(1)}, u32[]{:S(2)}, u32[]{:S(2)}) %collective-permute-start.53) | collective-permute-done | bytes 524320 | tf_op jit(solution)/shard_map/ppermute | solution.py:335
  194.4 8.5 %collective-permute-done.49.out = bf16[8,256,128]{2,1,0:T(8,128)(2,1)S(1)} collective-permute-done((bf16[8,256,128]{2,1,0:T(8,128)(2,1)S(1)}, bf16[8,256,128]{2,1,0:T(8,128)(2,1)S(1)}, u32[]{:S(2)}, u32[]{:S(2)}) %collective-permute-start.49) | collective-permute-done | bytes 524320 | tf_op jit(solution)/shard_map/ppermute | solution.py:335
  205.6 3.1 %shard_map.104.field = f32[9,256,128]{2,1,0:T(8,128)S(1)} custom-call(s32[180]{0:T(256)S(1)} %get-tuple-element.93.table, bf16[48,256,256]{2,1,0:T(8,128)(2,1)S(1)} %bitcast.8, bf16[8,256,128]{2,1,0:T(8,128)(2,1)S(1)} %get-tuple-element.149.own.refs_0_, bf16[8,256,128]{2,1,0:T(8,128)(2,1)S(1)} %collective-permute-done.46.refs_0_.first.refs_1_, ...), custom_call_target="tpu_custom_call" | custom-call | tf_op jit(solution)/shard_map/pallas_call | solution.py:269
  208.6 2.8 %collective-permute-done.51.got2 = bf16[3,256,128]{2,1,0:T(8,128)(2,1)S(1)} collective-permute-done((bf16[3,256,128]{2,1,0:T(8,128)(2,1)S(1)}, bf16[3,256,128]{2,1,0:T(8,128)(2,1)S(1)}, u32[]{:S(2)}, u32[]{:S(2)}) %collective-permute-start.51) | collective-permute-done | bytes 196640 | tf_op jit(solution)/shard_map/ppermute | solution.py:339
  211.4 3.3 %collective-permute-done.52.got3 = bf16[3,256,128]{2,1,0:T(8,128)(2,1)S(1)} collective-permute-done((bf16[3,256,128]{2,1,0:T(8,128)(2,1)S(1)}, bf16[3,256,128]{2,1,0:T(8,128)(2,1)S(1)}, u32[]{:S(2)}, u32[]{:S(2)}) %collective-permute-start.52) | collective-permute-done | bytes 196640 | tf_op jit(solution)/shard_map/ppermute | solution.py:339
  214.7 3.0 %shard_map.105 = (f32[8,256,128]{2,1,0:T(8,128)}, f32[8,256,128]{2,1,0:T(8,128)}, f32[1,128]{1,0:T(1,128)S(1)}) custom-call(s32[180]{0:T(256)S(1)} %get-tuple-element.93.table, f32[2]{0:T(128)S(1)} %pad_maximum_fusion.scalars, bf16[48,256,256]{2,1,0:T(8,128)(2,1)S(1)} %bitcast.8, bf16[8,256,128]{2,1,0:T(8,128)(2,1)S(1)} %collective-permute-done.45.mid, ...), custom_call_target="tpu_custom_call" | custom-call | flops 201326592 | bytes 7602176 | tf_op jit(solution)/shard_map/pallas_call | solution.py:316
  217.7 10.8 %all_to_all.6 = f32[16,1,128]{2,1,0:T(1,128)S(1)} all-to-all(f32[16,1,128]{2,1,0:T(1,128)S(1)} %broadcast_in_dim.2), channel_id=1, replica_groups=mesh['groups'=2,'row'=16] {'row'}, dimensions={0} | all-to-all | bytes 16384 | tf_op jit(solution)/shard_map/all_to_all | solution.py:345
  (134 shorter events, 74.3 us)
Async XLA Ops:
  1.9 16.5 %collective-permute-start = (bf16[8,256,128]{2,1,0:T(8,128)(2,1)S(1)}, bf16[8,256,128]{2,1,0:T(8,128)(2,1)S(1)}, u32[]{:S(2)}, u32[]{:S(2)}) collective-permute-start(bf16[8,256,128]{2,1,0:T(8,128)(2,1)S(1)} %convert_element_type.3.own.refs_0_), channel_id=1, source_target_pairs={{0,8},{1,9},{2,10},{3,11},{12,4},{13,5},{14,6},{15,7},{4,0},{5,1},... | collective-permute-start | bytes 1572872 | tf_op jit(solution)/shard_map/ppermute | solution.py:335
  12.8 17.6 %collective-permute-start.4 = (bf16[8,256,128]{2,1,0:T(8,128)(2,1)S(1)}, bf16[8,256,128]{2,1,0:T(8,128)(2,1)S(1)}, u32[]{:S(2)}, u32[]{:S(2)}) collective-permute-start(bf16[8,256,128]{2,1,0:T(8,128)(2,1)S(1)} %convert_element_type.3.own.refs_0_), channel_id=1, source_target_pairs={{0,4},{1,5},{2,6},{3,7},{12,8},{13,9},{14,10},{15,11},{4,12},{5,13... | collective-permute-start | bytes 1572872 | tf_op jit(solution)/shard_map/ppermute | solution.py:335
  12.8 17.6 %collective-permute-start.7 = (bf16[8,256,128]{2,1,0:T(8,128)(2,1)S(1)}, bf16[8,256,128]{2,1,0:T(8,128)(2,1)S(1)}, u32[]{:S(2)}, u32[]{:S(2)}) collective-permute-start(bf16[8,256,128]{2,1,0:T(8,128)(2,1)S(1)} %convert_element_type.3.own.refs_0_), channel_id=1, source_target_pairs={{4,8},{5,9},{6,10},{7,11},{8,4},{9,5},{10,6},{11,7},{20,24},{21,25... | collective-permute-start | bytes 1572872 | tf_op jit(solution)/shard_map/ppermute | solution.py:335
  18.4 23.1 %collective-permute-start.8 = (bf16[8,256,128]{2,1,0:T(8,128)(2,1)S(1)}, bf16[8,256,128]{2,1,0:T(8,128)(2,1)S(1)}, u32[]{:S(2)}, u32[]{:S(2)}) collective-permute-start(bf16[8,256,128]{2,1,0:T(8,128)(2,1)S(1)} %collective-permute-done.first.refs_1_), channel_id=1, source_target_pairs={{4,0},{5,1},{6,2},{7,3},{8,12},{9,13},{10,14},{11,15},{20,16},{21,... | collective-permute-start | bytes 1572872 | tf_op jit(solution)/shard_map/ppermute | solution.py:335
  21.8 12.1 %collective-permute-start.5 = (bf16[6,256,128]{2,1,0:T(8,128)(2,1)S(1)}, bf16[6,256,128]{2,1,0:T(8,128)(2,1)S(1)}, u32[]{:S(2)}, u32[]{:S(2)}) collective-permute-start(bf16[6,256,128]{2,1,0:T(8,128)(2,1)S(1)} %get-tuple-element.94), channel_id=1, source_target_pairs={{0,2},{1,3},{2,0},{3,1},{4,6},{5,7},{6,4},{7,5},{8,10},{9,11},{10,... | collective-permute-start | bytes 1179656 | tf_op jit(solution)/shard_map/ppermute | solution.py:339
  23.4 14.8 %collective-permute-start.6 = (bf16[6,256,128]{2,1,0:T(8,128)(2,1)S(1)}, bf16[6,256,128]{2,1,0:T(8,128)(2,1)S(1)}, u32[]{:S(2)}, u32[]{:S(2)}) collective-permute-start(bf16[6,256,128]{2,1,0:T(8,128)(2,1)S(1)} %get-tuple-element.95), channel_id=1, source_target_pairs={{0,3},{1,2},{2,1},{3,0},{4,7},{5,6},{6,5},{7,4},{8,11},{9,10},{10,... | collective-permute-start | bytes 1179656 | tf_op jit(solution)/shard_map/ppermute | solution.py:339
  45.5 15.0 %collective-permute-start.12 = (bf16[3,256,128]{2,1,0:T(8,128)(2,1)S(1)}, bf16[3,256,128]{2,1,0:T(8,128)(2,1)S(1)}, u32[]{:S(2)}, u32[]{:S(2)}) collective-permute-start(bf16[3,256,128]{2,1,0:T(8,128)(2,1)S(1)} %get-tuple-element.103), channel_id=1, source_target_pairs={{0,1},{1,0},{2,3},{3,2},{4,5},{5,4},{6,7},{7,6},{8,9},{9,8},{10,11... | collective-permute-start | bytes 589832 | tf_op jit(solution)/shard_map/ppermute | solution.py:339
  45.6 14.9 %collective-permute-start.13 = (bf16[3,256,128]{2,1,0:T(8,128)(2,1)S(1)}, bf16[3,256,128]{2,1,0:T(8,128)(2,1)S(1)}, u32[]{:S(2)}, u32[]{:S(2)}) collective-permute-start(bf16[3,256,128]{2,1,0:T(8,128)(2,1)S(1)} %get-tuple-element.104), channel_id=1, source_target_pairs={{0,2},{1,3},{2,0},{3,1},{4,6},{5,7},{6,4},{7,5},{8,10},{9,11},{10,... | collective-permute-start | bytes 589832 | tf_op jit(solution)/shard_map/ppermute | solution.py:339
  47.8 13.9 %collective-permute-start.14 = (bf16[3,256,128]{2,1,0:T(8,128)(2,1)S(1)}, bf16[3,256,128]{2,1,0:T(8,128)(2,1)S(1)}, u32[]{:S(2)}, u32[]{:S(2)}) collective-permute-start(bf16[3,256,128]{2,1,0:T(8,128)(2,1)S(1)} %get-tuple-element.105), channel_id=1, source_target_pairs={{0,3},{1,2},{2,1},{3,0},{4,7},{5,6},{6,5},{7,4},{8,11},{9,10},{10,... | collective-permute-start | bytes 589832 | tf_op jit(solution)/shard_map/ppermute | solution.py:339
  63.4 14.3 %collective-permute-start.18 = (bf16[8,256,128]{2,1,0:T(8,128)(2,1)S(1)}, bf16[8,256,128]{2,1,0:T(8,128)(2,1)S(1)}, u32[]{:S(2)}, u32[]{:S(2)}) collective-permute-start(bf16[8,256,128]{2,1,0:T(8,128)(2,1)S(1)} %get-tuple-element.111.own.refs_0_), channel_id=1, source_target_pairs={{0,8},{1,9},{2,10},{3,11},{12,4},{13,5},{14,6},{15,7},{4,0},{5,1},... | collective-permute-start | bytes 1572872 | tf_op jit(solution)/shard_map/ppermute | solution.py:335
  64.7 25.1 %collective-permute-start.25 = (bf16[8,256,128]{2,1,0:T(8,128)(2,1)S(1)}, bf16[8,256,128]{2,1,0:T(8,128)(2,1)S(1)}, u32[]{:S(2)}, u32[]{:S(2)}) collective-permute-start(bf16[8,256,128]{2,1,0:T(8,128)(2,1)S(1)} %get-tuple-element.111.own.refs_0_), channel_id=1, source_target_pairs={{0,4},{1,5},{2,6},{3,7},{12,8},{13,9},{14,10},{15,11},{4,12},{5,13... | collective-permute-start | bytes 1572872 | tf_op jit(solution)/shard_map/ppermute | solution.py:335
  78.2 11.6 %collective-permute-start.26 = (bf16[3,256,128]{2,1,0:T(8,128)(2,1)S(1)}, bf16[3,256,128]{2,1,0:T(8,128)(2,1)S(1)}, u32[]{:S(2)}, u32[]{:S(2)}) collective-permute-start(bf16[3,256,128]{2,1,0:T(8,128)(2,1)S(1)} %get-tuple-element.118), channel_id=1, source_target_pairs={{0,2},{1,3},{2,0},{3,1},{4,6},{5,7},{6,4},{7,5},{8,10},{9,11},{10,... | collective-permute-start | bytes 589832 | tf_op jit(solution)/shard_map/ppermute | solution.py:339
  79.8 12.6 %collective-permute-start.17 = (bf16[8,256,128]{2,1,0:T(8,128)(2,1)S(1)}, bf16[8,256,128]{2,1,0:T(8,128)(2,1)S(1)}, u32[]{:S(2)}, u32[]{:S(2)}) collective-permute-start(bf16[8,256,128]{2,1,0:T(8,128)(2,1)S(1)} %get-tuple-element.111.own.refs_0_), channel_id=1, source_target_pairs={{4,8},{5,9},{6,10},{7,11},{8,4},{9,5},{10,6},{11,7},{20,24},{21,25... | collective-permute-start | bytes 1572872 | tf_op jit(solution)/shard_map/ppermute | solution.py:335
  80.5 20.5 %collective-permute-start.21 = (bf16[8,256,128]{2,1,0:T(8,128)(2,1)S(1)}, bf16[8,256,128]{2,1,0:T(8,128)(2,1)S(1)}, u32[]{:S(2)}, u32[]{:S(2)}) collective-permute-start(bf16[8,256,128]{2,1,0:T(8,128)(2,1)S(1)} %collective-permute-done.18.refs_0_.first.refs_1_), channel_id=1, source_target_pairs={{4,0},{5,1},{6,2},{7,3},{8,12},{9,13},{10,14},{11,15},{20,16},{21,... | collective-permute-start | bytes 1572872 | tf_op jit(solution)/shard_map/ppermute | solution.py:335
  90.4 13.1 %collective-permute-start.28 = (bf16[9,256,128]{2,1,0:T(8,128)(2,1)S(1)}, bf16[9,256,128]{2,1,0:T(8,128)(2,1)S(1)}, u32[]{:S(2)}, u32[]{:S(2)}) collective-permute-start(bf16[9,256,128]{2,1,0:T(8,128)(2,1)S(1)} %get-tuple-element.121), channel_id=1, source_target_pairs={{0,1},{1,0},{2,3},{3,2},{4,5},{5,4},{6,7},{7,6},{8,9},{9,8},{10,11... | collective-permute-start | bytes 1769480 | tf_op jit(solution)/shard_map/ppermute | solution.py:339
  90.5 12.7 %collective-permute-start.29 = (bf16[3,256,128]{2,1,0:T(8,128)(2,1)S(1)}, bf16[3,256,128]{2,1,0:T(8,128)(2,1)S(1)}, u32[]{:S(2)}, u32[]{:S(2)}) collective-permute-start(bf16[3,256,128]{2,1,0:T(8,128)(2,1)S(1)} %get-tuple-element.126), channel_id=1, source_target_pairs={{0,2},{1,3},{2,0},{3,1},{4,6},{5,7},{6,4},{7,5},{8,10},{9,11},{10,... | collective-permute-start | bytes 589832 | tf_op jit(solution)/shard_map/ppermute | solution.py:339
  92.1 11.5 %collective-permute-start.30 = (bf16[3,256,128]{2,1,0:T(8,128)(2,1)S(1)}, bf16[3,256,128]{2,1,0:T(8,128)(2,1)S(1)}, u32[]{:S(2)}, u32[]{:S(2)}) collective-permute-start(bf16[3,256,128]{2,1,0:T(8,128)(2,1)S(1)} %get-tuple-element.127), channel_id=1, source_target_pairs={{0,3},{1,2},{2,1},{3,0},{4,7},{5,6},{6,5},{7,4},{8,11},{9,10},{10,... | collective-permute-start | bytes 589832 | tf_op jit(solution)/shard_map/ppermute | solution.py:339
  114.4 14.3 %collective-permute-start.32 = (bf16[8,256,128]{2,1,0:T(8,128)(2,1)S(1)}, bf16[8,256,128]{2,1,0:T(8,128)(2,1)S(1)}, u32[]{:S(2)}, u32[]{:S(2)}) collective-permute-start(bf16[8,256,128]{2,1,0:T(8,128)(2,1)S(1)} %get-tuple-element.130.own.refs_0_), channel_id=1, source_target_pairs={{0,8},{1,9},{2,10},{3,11},{12,4},{13,5},{14,6},{15,7},{4,0},{5,1},... | collective-permute-start | bytes 1572872 | tf_op jit(solution)/shard_map/ppermute | solution.py:335
  116.0 24.8 %collective-permute-start.39 = (bf16[8,256,128]{2,1,0:T(8,128)(2,1)S(1)}, bf16[8,256,128]{2,1,0:T(8,128)(2,1)S(1)}, u32[]{:S(2)}, u32[]{:S(2)}) collective-permute-start(bf16[8,256,128]{2,1,0:T(8,128)(2,1)S(1)} %get-tuple-element.130.own.refs_0_), channel_id=1, source_target_pairs={{0,4},{1,5},{2,6},{3,7},{12,8},{13,9},{14,10},{15,11},{4,12},{5,13... | collective-permute-start | bytes 1572872 | tf_op jit(solution)/shard_map/ppermute | solution.py:335
  129.2 11.6 %collective-permute-start.40 = (bf16[3,256,128]{2,1,0:T(8,128)(2,1)S(1)}, bf16[3,256,128]{2,1,0:T(8,128)(2,1)S(1)}, u32[]{:S(2)}, u32[]{:S(2)}) collective-permute-start(bf16[3,256,128]{2,1,0:T(8,128)(2,1)S(1)} %get-tuple-element.137), channel_id=1, source_target_pairs={{0,2},{1,3},{2,0},{3,1},{4,6},{5,7},{6,4},{7,5},{8,10},{9,11},{10,... | collective-permute-start | bytes 589832 | tf_op jit(solution)/shard_map/ppermute | solution.py:339
  130.7 12.7 %collective-permute-start.31 = (bf16[8,256,128]{2,1,0:T(8,128)(2,1)S(1)}, bf16[8,256,128]{2,1,0:T(8,128)(2,1)S(1)}, u32[]{:S(2)}, u32[]{:S(2)}) collective-permute-start(bf16[8,256,128]{2,1,0:T(8,128)(2,1)S(1)} %get-tuple-element.130.own.refs_0_), channel_id=1, source_target_pairs={{4,8},{5,9},{6,10},{7,11},{8,4},{9,5},{10,6},{11,7},{20,24},{21,25... | collective-permute-start | bytes 1572872 | tf_op jit(solution)/shard_map/ppermute | solution.py:335
  131.4 20.5 %collective-permute-start.35 = (bf16[8,256,128]{2,1,0:T(8,128)(2,1)S(1)}, bf16[8,256,128]{2,1,0:T(8,128)(2,1)S(1)}, u32[]{:S(2)}, u32[]{:S(2)}) collective-permute-start(bf16[8,256,128]{2,1,0:T(8,128)(2,1)S(1)} %collective-permute-done.32.refs_0_.first.refs_1_), channel_id=1, source_target_pairs={{4,0},{5,1},{6,2},{7,3},{8,12},{9,13},{10,14},{11,15},{20,16},{21,... | collective-permute-start | bytes 1572872 | tf_op jit(solution)/shard_map/ppermute | solution.py:335
  141.5 13.1 %collective-permute-start.42 = (bf16[9,256,128]{2,1,0:T(8,128)(2,1)S(1)}, bf16[9,256,128]{2,1,0:T(8,128)(2,1)S(1)}, u32[]{:S(2)}, u32[]{:S(2)}) collective-permute-start(bf16[9,256,128]{2,1,0:T(8,128)(2,1)S(1)} %get-tuple-element.140), channel_id=1, source_target_pairs={{0,1},{1,0},{2,3},{3,2},{4,5},{5,4},{6,7},{7,6},{8,9},{9,8},{10,11... | collective-permute-start | bytes 1769480 | tf_op jit(solution)/shard_map/ppermute | solution.py:339
  141.5 12.7 %collective-permute-start.43 = (bf16[3,256,128]{2,1,0:T(8,128)(2,1)S(1)}, bf16[3,256,128]{2,1,0:T(8,128)(2,1)S(1)}, u32[]{:S(2)}, u32[]{:S(2)}) collective-permute-start(bf16[3,256,128]{2,1,0:T(8,128)(2,1)S(1)} %get-tuple-element.145), channel_id=1, source_target_pairs={{0,2},{1,3},{2,0},{3,1},{4,6},{5,7},{6,4},{7,5},{8,10},{9,11},{10,... | collective-permute-start | bytes 589832 | tf_op jit(solution)/shard_map/ppermute | solution.py:339
  143.1 11.4 %collective-permute-start.44 = (bf16[3,256,128]{2,1,0:T(8,128)(2,1)S(1)}, bf16[3,256,128]{2,1,0:T(8,128)(2,1)S(1)}, u32[]{:S(2)}, u32[]{:S(2)}) collective-permute-start(bf16[3,256,128]{2,1,0:T(8,128)(2,1)S(1)} %get-tuple-element.146), channel_id=1, source_target_pairs={{0,3},{1,2},{2,1},{3,0},{4,7},{5,6},{6,5},{7,4},{8,11},{9,10},{10,... | collective-permute-start | bytes 589832 | tf_op jit(solution)/shard_map/ppermute | solution.py:339
  165.3 14.3 %collective-permute-start.46 = (bf16[8,256,128]{2,1,0:T(8,128)(2,1)S(1)}, bf16[8,256,128]{2,1,0:T(8,128)(2,1)S(1)}, u32[]{:S(2)}, u32[]{:S(2)}) collective-permute-start(bf16[8,256,128]{2,1,0:T(8,128)(2,1)S(1)} %get-tuple-element.149.own.refs_0_), channel_id=1, source_target_pairs={{0,8},{1,9},{2,10},{3,11},{12,4},{13,5},{14,6},{15,7},{4,0},{5,1},... | collective-permute-start | bytes 1572872 | tf_op jit(solution)/shard_map/ppermute | solution.py:335
  167.0 24.8 %collective-permute-start.53 = (bf16[8,256,128]{2,1,0:T(8,128)(2,1)S(1)}, bf16[8,256,128]{2,1,0:T(8,128)(2,1)S(1)}, u32[]{:S(2)}, u32[]{:S(2)}) collective-permute-start(bf16[8,256,128]{2,1,0:T(8,128)(2,1)S(1)} %get-tuple-element.149.own.refs_0_), channel_id=1, source_target_pairs={{0,4},{1,5},{2,6},{3,7},{12,8},{13,9},{14,10},{15,11},{4,12},{5,13... | collective-permute-start | bytes 1572872 | tf_op jit(solution)/shard_map/ppermute | solution.py:335
  180.2 11.6 %collective-permute-start.54 = (bf16[3,256,128]{2,1,0:T(8,128)(2,1)S(1)}, bf16[3,256,128]{2,1,0:T(8,128)(2,1)S(1)}, u32[]{:S(2)}, u32[]{:S(2)}) collective-permute-start(bf16[3,256,128]{2,1,0:T(8,128)(2,1)S(1)} %get-tuple-element.156), channel_id=1, source_target_pairs={{0,2},{1,3},{2,0},{3,1},{4,6},{5,7},{6,4},{7,5},{8,10},{9,11},{10,... | collective-permute-start | bytes 589832 | tf_op jit(solution)/shard_map/ppermute | solution.py:339
  181.7 12.6 %collective-permute-start.45 = (bf16[8,256,128]{2,1,0:T(8,128)(2,1)S(1)}, bf16[8,256,128]{2,1,0:T(8,128)(2,1)S(1)}, u32[]{:S(2)}, u32[]{:S(2)}) collective-permute-start(bf16[8,256,128]{2,1,0:T(8,128)(2,1)S(1)} %get-tuple-element.149.own.refs_0_), channel_id=1, source_target_pairs={{4,8},{5,9},{6,10},{7,11},{8,4},{9,5},{10,6},{11,7},{20,24},{21,25... | collective-permute-start | bytes 1572872 | tf_op jit(solution)/shard_map/ppermute | solution.py:335
  182.4 20.5 %collective-permute-start.49 = (bf16[8,256,128]{2,1,0:T(8,128)(2,1)S(1)}, bf16[8,256,128]{2,1,0:T(8,128)(2,1)S(1)}, u32[]{:S(2)}, u32[]{:S(2)}) collective-permute-start(bf16[8,256,128]{2,1,0:T(8,128)(2,1)S(1)} %collective-permute-done.46.refs_0_.first.refs_1_), channel_id=1, source_target_pairs={{4,0},{5,1},{6,2},{7,3},{8,12},{9,13},{10,14},{11,15},{20,16},{21,... | collective-permute-start | bytes 1572872 | tf_op jit(solution)/shard_map/ppermute | solution.py:335
  192.4 13.1 %collective-permute-start.56 = (bf16[9,256,128]{2,1,0:T(8,128)(2,1)S(1)}, bf16[9,256,128]{2,1,0:T(8,128)(2,1)S(1)}, u32[]{:S(2)}, u32[]{:S(2)}) collective-permute-start(bf16[9,256,128]{2,1,0:T(8,128)(2,1)S(1)} %get-tuple-element.159), channel_id=1, source_target_pairs={{0,1},{1,0},{2,3},{3,2},{4,5},{5,4},{6,7},{7,6},{8,9},{9,8},{10,11... | collective-permute-start | bytes 1769480 | tf_op jit(solution)/shard_map/ppermute | solution.py:339
  192.5 12.7 %collective-permute-start.57 = (bf16[3,256,128]{2,1,0:T(8,128)(2,1)S(1)}, bf16[3,256,128]{2,1,0:T(8,128)(2,1)S(1)}, u32[]{:S(2)}, u32[]{:S(2)}) collective-permute-start(bf16[3,256,128]{2,1,0:T(8,128)(2,1)S(1)} %get-tuple-element.164), channel_id=1, source_target_pairs={{0,2},{1,3},{2,0},{3,1},{4,6},{5,7},{6,4},{7,5},{8,10},{9,11},{10,... | collective-permute-start | bytes 589832 | tf_op jit(solution)/shard_map/ppermute | solution.py:339
  (34 other events, 320.0 us)

commit v11 on v10

--- a/solution.py
+++ b/solution.py
@@ -78,8 +78,8 @@
     return z, yc, inner, (z, jnp.where(inner, skip, near), jnp.where(inner, near, skip), z ^ 3)
 
 
-EARLY = tuple((j, flip) for j in range(3) for flip in range(4))
-LATE = tuple((3, flip) for flip in range(4))
+EARLY = tuple((j, flip) for j in range(3) for flip in range(4)) + ((3, 0), (3, 1))
+LATE = ((3, 2), (3, 3))
 
 
 def plan_kernel(layout, blocks, rows, cols, count, tiles, mine, note, seen, buffer, sems):
@@ -245,20 +245,21 @@
         xbuf[place + r] = shard[table[layout.entry(entry + r) + 2]]
 
 
-def early_kernel(layout, parts, table, tiles, *refs):
+def early_kernel(layout, parts, table, tiles, own, first, second, mid, out, core, core3, *refs):
     cap = layout.cap
     field, xbuf = refs[-2:]
-    core = refs[3]
-    for j in range(3):
+    for j, shard in enumerate((own, first, second)):
         base = 4 * cap * j
-        take_own(layout, table, base, refs[j], xbuf, base)
+        take_own(layout, table, base, shard, xbuf, base)
         copy_part(cap, core, j, xbuf, base + cap)
         ref, part = parts[j]
         copy_part(cap, refs[ref], part, xbuf, base + 2 * cap)
         copy_part(cap, refs[ref + 1], part, xbuf, base + 3 * cap)
+    by_place(mid, out, lambda shard: take_own(layout, table, 12 * cap, shard, xbuf, 12 * cap))
+    copy_part(cap, core3, 0, xbuf, 13 * cap)
     field[...] = jnp.zeros_like(field)
 
-    @pl.loop(0, 12 * cap // GROUP)
+    @pl.loop(0, len(EARLY) * cap // GROUP)
     def _(g):
         multiply(layout, table, tiles, [xbuf[g * GROUP + i] for i in range(GROUP)], g * GROUP, field)
 
@@ -271,34 +272,43 @@
         out_shape=jax.ShapeDtypeStruct((blocks + 1, tile, repl), jnp.float32),
         in_specs=[SMEM] + [VMEM] * (1 + len(arrays)),
         out_specs=VMEM,
-        scratch_shapes=[pltpu.VMEM((12 * layout.cap, tile, repl), jnp.bfloat16)],
+        scratch_shapes=[pltpu.VMEM((len(EARLY) * layout.cap, tile, repl), jnp.bfloat16)],
         compiler_params=params(),
         cost_estimate=pl.CostEstimate(flops=0, bytes_accessed=0, transcendentals=0),
     )(table, tiles, *arrays)
 
 
-def late_kernel(layout, last, table, scalars, tiles, mid, out, core, got2, got3, field, xpos, ymom, *refs):
-    outs, (xbuf, acc) = refs[:-2], refs[-2:]
+def late_kernel(layout, last, table, scalars, tiles, got2, got3, field, xpos, ymom, *refs):
+    cap = layout.cap
+    blocks, _, repl = xpos.shape
+    outs, acc = (refs[:3], refs[3]) if last else (refs[:5], refs[5])
     xout, yout = outs[:2]
-    blocks = xpos.shape[0]
-    cap = layout.cap
-    by_place(mid, out, lambda shard: take_own(layout, table, 12 * cap, shard, xbuf, 0))
     acc[...] = field[...]
-    blocks_in = [ref[r] for ref in (xbuf, core, got2, got3) for r in range(cap)]
-    for first in range(0, 4 * cap, GROUP):
-        multiply(layout, table, tiles, blocks_in[first : first + GROUP], 12 * cap + first, acc)
-    total = jnp.zeros((1, xpos.shape[2]), jnp.float32)
+    multiply(layout, table, tiles, [ref[r] for ref in (got2, got3) for r in range(cap)], len(EARLY) * cap, acc)
+    if last:
+        xnew, ynew, sems = refs[4:]
+    else:
+        xnew, ynew = xout, yout
+    total = jnp.zeros((1, repl), jnp.float32)
+    copies = []
     for b in range(blocks):
         x, h = xpos[b], acc[b]
         if last:
             total += jnp.sum(x * h, axis=0, keepdims=True)
         x, y = update(scalars[0], scalars[1], h, x, ymom[b])
-        xout[b] = x
-        yout[b] = y
-        if not last:
+        xnew[b] = x
+        ynew[b] = y
+        if last:
+            copies.append(pltpu.make_async_copy(xnew.at[b], xout.at[b], sems.at[0, b]))
+            copies.append(pltpu.make_async_copy(ynew.at[b], yout.at[b], sems.at[1, b]))
+            copies[-2].start()
+            copies[-1].start()
+        else:
             outs[2][b] = x.astype(jnp.bfloat16)
     if last:
         outs[2][...] = -0.5 * total
+        for copy in copies:
+            copy.wait()
     else:
         other_y_kernel(layout, (0,), table, *outs[2:])
 
@@ -306,10 +316,12 @@
 def late(layout, last, table, scalars, tiles, sources, field, xpos, ymom):
     tile = tiles.shape[1]
     blocks, _, repl = xpos.shape
-    entries = 4 * layout.cap
+    entries = len(LATE) * layout.cap
     state = jax.ShapeDtypeStruct(xpos.shape, jnp.float32)
+    scratch = [pltpu.VMEM((blocks + 1, tile, repl), jnp.float32)]
     if last:
         extra = (jax.ShapeDtypeStruct((1, repl), jnp.float32),)
+        scratch += [pltpu.VMEM(xpos.shape, jnp.float32)] * 2 + [pltpu.SemaphoreType.DMA((2, blocks))]
     else:
         out = jax.ShapeDtypeStruct((layout.cap, tile, repl), jnp.bfloat16)
         extra = (jax.ShapeDtypeStruct(xpos.shape, jnp.bfloat16), out, out)
@@ -317,11 +329,8 @@
         functools.partial(late_kernel, layout, last),
         out_shape=(state, state) + extra,
         in_specs=[SMEM, SMEM] + [VMEM] * (1 + len(sources) + 3),
-        out_specs=(VMEM,) * (2 + len(extra)),
-        scratch_shapes=[
-            pltpu.VMEM((layout.cap, tile, repl), jnp.bfloat16),
-            pltpu.VMEM((blocks + 1, tile, repl), jnp.float32),
-        ],
+        out_specs=((ANY, ANY) if last else (VMEM, VMEM)) + (VMEM,) * len(extra),
+        scratch_shapes=scratch,
         compiler_params=params(),
         cost_estimate=pl.CostEstimate(
             flops=2 * entries * tile * tile * repl,
@@ -376,8 +385,11 @@
             out = along_z(OUTWARD, own1)
             table, *packs01 = start(layout, mine, notes, own0, own1)
             got1 = to_other_y(packs01)
-            own2, got1, mid, out = lax.optimization_barrier((own2, got1, mid, out))
-            parts = ((4, 0), (4, 1), (6, 0))
+            plane = note + notes[0] + notes[1] + notes[2]
+            half = across(4, plane)
+            own2, got1, half = lax.optimization_barrier((own2, got1, half))
+            half = plane + half
+            parts = ((0, 0), (0, 1), (2, 0))
             got = got1
         else:
             got0 = to_other_y(packs0)
@@ -385,23 +397,20 @@
             out = along_z(OUTWARD, own1)
             got1 = to_other_y(other_y((1,), [own1]))
             own2, got1 = lax.optimization_barrier((own2, got1))
-            parts = ((4, 0), (6, 0), (8, 0))
+            parts = ((0, 0), (2, 0), (4, 0))
             got = got0 + got1
         packs2 = pack(functools.partial(second_kernel, layout), [cap, cap, 3 * cap], table, [own0, own1, own2])
-        got = got + to_other_y(packs2)
+        got2 = to_other_y(packs2)
         core = across(1, packs2[2])
-        if step == 0:
-            notes, core = lax.optimization_barrier((notes, core))
-            plane = note + notes[0] + notes[1] + notes[2]
-            half = plane + across(4, plane)
         packs3 = pack(functools.partial(third_kernel, layout), [cap] * 3, table, [mid, out])
-        far = [mid, out, across(1, packs3[2])] + to_other_y(packs3)
-        field = early(layout, parts, table, tiles, [own0, own1, own2, core] + got)
+        core3 = across(1, packs3[2])
+        got3 = to_other_y(packs3)
+        field = early(layout, parts, table, tiles, [own0, own1, own2, mid, out, core, core3] + got + got2)
         if step == 0:
             total = (half + across(8, half))[0, SUM_AT]
             coeff = 0.7 * jnp.sqrt((order - 1) / total)
         scalars = jnp.stack([jnp.float32(0.4 - 0.1 * step), coeff])
-        outs = late(layout, last, table, scalars, tiles, far, field, xpos, ymom)
+        outs = late(layout, last, table, scalars, tiles, got3, field, xpos, ymom)
         xpos, ymom = outs[0], outs[1]
         if not last:
             own0, packs0 = outs[2], outs[3:]

time: 229 us -> 248 us (1.083)
  waiting for transfers between devices: 128 us -> 139 us
  blocking collectives: 10.8 us -> 17.5 us
    all_to_all x1, blocking collectives: 10.8 us -> 17.5 us  [row_sum(): lax.all_to_all(spread, 'row', split_axis=0, concat_axis=0, tiled=True)]
    ppermute x16, starting transfers between devices: 18.2 us -> 24 us  [along_z(): lax.ppermute(value, 'row', [(a * 4 + i, b * 4 + i) for a, b in pairs for...]
    ppermute x43, starting transfers between devices: 30.7 us -> 25.2 us  [across(): return lax.ppermute(value, 'row', [(i, i ^ flip) for i in range(16)])]
    ppermute x16, waiting for transfers between devices: 70.2 us -> 75.6 us  [along_z(): lax.ppermute(value, 'row', [(a * 4 + i, b * 4 + i) for a, b in pairs for...]
    ppermute x43, waiting for transfers between devices: 58.1 us -> 63.5 us  [across(): return lax.ppermute(value, 'row', [(i, i ^ flip) for i in range(16)])]
  transfers between devices with their start and end apart: 59 -> 59, of which waited for: 33 -> 30; matrix products, arithmetic and copies ran while one was open for 0% -> 1% of each run, Pallas kernels for 10% -> 11%
where the time goes in v11:
time: 248 us
  waiting for transfers between devices  139 us (56%)
  starting transfers between devices  49.2 us (20%)
  Pallas kernels  32.9 us (13%)
  blocking collectives  17.5 us (7%)
  local copies, waits for them, and re-layouts  4.07 us (2%)
  other arithmetic  2.8 us (1%)
    ppermute x16, waiting for transfers between devices, along_z(): lax.ppermute(value, 'row', [(a * 4 + i, b * 4 + i) for a, b in pairs for...  75.6 us
    ppermute x43, waiting for transfers between devices, across(): return lax.ppermute(value, 'row', [(i, i ^ flip) for i in range(16)])  63.5 us
    ppermute x43, starting transfers between devices, across(): return lax.ppermute(value, 'row', [(i, i ^ flip) for i in range(16)])  25.2 us
    ppermute x16, starting transfers between devices, along_z(): lax.ppermute(value, 'row', [(a * 4 + i, b * 4 + i) for a, b in pairs for...  24 us
    all_to_all x1, blocking collectives, row_sum(): lax.all_to_all(spread, 'row', split_axis=0, concat_axis=0, tiled=True)  17.5 us
    pallas_call x4, Pallas kernels, early(): pl.pallas_call(functools.partial(early_kernel, layout, parts), out_shape=...  13.8 us
    pallas_call x4, Pallas kernels, late(): pl.pallas_call(functools.partial(late_kernel, layout, last), out_shape=(s...  6.81 us
    pallas_call x11, Pallas kernels, pack(): pl.pallas_call(kernel, out_shape=[jax.ShapeDtypeStruct((size, tile, repl)...  6.64 us
  transfers between devices with their start and end apart: 59, of which 30 were waited for; matrix products, arithmetic and copies ran while one was open for 1% of the time, Pallas kernels for 11%

profile of v11, /device:TPU:0, one launch (start us, length us, event | category | flops | bytes accessed | tf_op | source)
XLA Modules:
  0.0 247.9 jit_solution(11523322198572338072)
XLA Ops:
  1.9 4.1 %collective-permute-start = (bf16[8,256,128]{2,1,0:T(8,128)(2,1)S(1)}, bf16[8,256,128]{2,1,0:T(8,128)(2,1)S(1)}, u32[]{:S(2)}, u32[]{:S(2)}) collective-permute-start(bf16[8,256,128]{2,1,0:T(8,128)(2,1)S(1)} %convert_element_type.3.own), channel_id=1, source_target_pairs={{0,8},{1,9},{2,10},{3,11},{12,4},{13,5},{14,6},{15,7},{4,0},{5,1},... | collective-permute-start | bytes 1572872 | tf_op jit(solution)/shard_map/ppermute | solution.py:344
  6.7 4.2 %shard_map.85 = (s32[144]{0:T(256)}, f32[1,128]{1,0:T(1,128)}) custom-call(s32[48]{0:T(128)} %rows.1, s32[48]{0:T(128)} %cols.1, s32[1]{0:T(128)S(6)} %copy.10.count, bf16[48,256,256]{2,1,0:T(8,128)(2,1)} %tiles.17), custom_call_target="tpu_custom_call" | custom-call | tf_op jit(solution)/shard_map/pallas_call | solution.py:131
  15.6 2.8 %collective-permute-done.first = bf16[8,256,128]{2,1,0:T(8,128)(2,1)S(1)} collective-permute-done((bf16[8,256,128]{2,1,0:T(8,128)(2,1)S(1)}, bf16[8,256,128]{2,1,0:T(8,128)(2,1)S(1)}, u32[]{:S(2)}, u32[]{:S(2)}) %collective-permute-start) | collective-permute-done | bytes 524320 | tf_op jit(solution)/shard_map/ppermute | solution.py:344
  24.8 5.6 %collective-permute-done.4.second = bf16[8,256,128]{2,1,0:T(8,128)(2,1)S(1)} collective-permute-done((bf16[8,256,128]{2,1,0:T(8,128)(2,1)S(1)}, bf16[8,256,128]{2,1,0:T(8,128)(2,1)S(1)}, u32[]{:S(2)}, u32[]{:S(2)}) %collective-permute-start.4) | collective-permute-done | bytes 524320 | tf_op jit(solution)/shard_map/ppermute | solution.py:344
  31.0 10.7 %collective-permute-done.7 = f32[1,128]{1,0:T(1,128)S(1)} collective-permute-done((f32[1,128]{1,0:T(1,128)S(1)}, f32[1,128]{1,0:T(1,128)S(1)}, u32[]{:S(2)}, u32[]{:S(2)}) %collective-permute-start.7) | collective-permute-done | bytes 544 | tf_op jit(solution)/shard_map/ppermute | solution.py:348
  45.7 2.4 collective-permute-done.8
  53.5 2.8 %copy-done = bf16[48,256,256]{2,1,0:T(8,128)(2,1)S(1)} copy-done((bf16[48,256,256]{2,1,0:T(8,128)(2,1)S(1)}, bf16[48,256,256]{2,1,0:T(8,128)(2,1)}, u32[]{:S(2)}) %copy-start) | copy-done | bytes 6291480
  56.3 3.4 %shard_map.89.field = f32[9,256,128]{2,1,0:T(8,128)S(1)} custom-call(s32[180]{0:T(256)S(1)} %get-tuple-element.88.table, bf16[48,256,256]{2,1,0:T(8,128)(2,1)S(1)} %copy-done, bf16[8,256,128]{2,1,0:T(8,128)(2,1)S(1)} %convert_element_type.3.own, bf16[8,256,128]{2,1,0:T(8,128)(2,1)S(1)} %collective-permute-done.first, ...), custom_call_target="tpu_custom_call" | custom-call | tf_op jit(solution)/shard_map/pallas_call | solution.py:270
  66.6 6.6 %collective-permute-done.19.refs_0_ = bf16[3,256,128]{2,1,0:T(8,128)(2,1)S(1)} collective-permute-done((bf16[3,256,128]{2,1,0:T(8,128)(2,1)S(1)}, bf16[3,256,128]{2,1,0:T(8,128)(2,1)S(1)}, u32[]{:S(2)}, u32[]{:S(2)}) %collective-permute-start.19) | collective-permute-done | bytes 196640 | tf_op jit(solution)/shard_map/ppermute | solution.py:348
  74.9 2.9 %collective-permute-done.18.refs_0_.first = bf16[8,256,128]{2,1,0:T(8,128)(2,1)S(1)} collective-permute-done((bf16[8,256,128]{2,1,0:T(8,128)(2,1)S(1)}, bf16[8,256,128]{2,1,0:T(8,128)(2,1)S(1)}, u32[]{:S(2)}, u32[]{:S(2)}) %collective-permute-start.18) | collective-permute-done | bytes 524320 | tf_op jit(solution)/shard_map/ppermute | solution.py:344
  81.4 8.1 %collective-permute-done.24.second = bf16[8,256,128]{2,1,0:T(8,128)(2,1)S(1)} collective-permute-done((bf16[8,256,128]{2,1,0:T(8,128)(2,1)S(1)}, bf16[8,256,128]{2,1,0:T(8,128)(2,1)S(1)}, u32[]{:S(2)}, u32[]{:S(2)}) %collective-permute-start.24) | collective-permute-done | bytes 524320 | tf_op jit(solution)/shard_map/ppermute | solution.py:344
  92.1 8.5 %collective-permute-done.21.out = bf16[8,256,128]{2,1,0:T(8,128)(2,1)S(1)} collective-permute-done((bf16[8,256,128]{2,1,0:T(8,128)(2,1)S(1)}, bf16[8,256,128]{2,1,0:T(8,128)(2,1)S(1)}, u32[]{:S(2)}, u32[]{:S(2)}) %collective-permute-start.21) | collective-permute-done | bytes 524320 | tf_op jit(solution)/shard_map/ppermute | solution.py:344
  103.3 3.5 %shard_map.94.field = f32[9,256,128]{2,1,0:T(8,128)S(1)} custom-call(s32[180]{0:T(256)S(1)} %get-tuple-element.88.table, bf16[48,256,256]{2,1,0:T(8,128)(2,1)S(1)} %bitcast.8, bf16[8,256,128]{2,1,0:T(8,128)(2,1)S(1)} %get-tuple-element.101.own, bf16[8,256,128]{2,1,0:T(8,128)(2,1)S(1)} %collective-permute-done.18.refs_0_.first, ...), custom_call_target="tpu_custom_call" | custom-call | tf_op jit(solution)/shard_map/pallas_call | solution.py:270
  106.7 2.4 collective-permute-done.22.got2
  109.1 3.1 %collective-permute-done.23.got3 = bf16[3,256,128]{2,1,0:T(8,128)(2,1)S(1)} collective-permute-done((bf16[3,256,128]{2,1,0:T(8,128)(2,1)S(1)}, bf16[3,256,128]{2,1,0:T(8,128)(2,1)S(1)}, u32[]{:S(2)}, u32[]{:S(2)}) %collective-permute-start.23) | collective-permute-done | bytes 196640 | tf_op jit(solution)/shard_map/ppermute | solution.py:348
  113.7 7.9 %collective-permute-start.32 = (bf16[8,256,128]{2,1,0:T(8,128)(2,1)S(1)}, bf16[8,256,128]{2,1,0:T(8,128)(2,1)S(1)}, u32[]{:S(2)}, u32[]{:S(2)}) collective-permute-start(bf16[8,256,128]{2,1,0:T(8,128)(2,1)S(1)} %get-tuple-element.120.own), channel_id=1, source_target_pairs={{0,8},{1,9},{2,10},{3,11},{12,4},{13,5},{14,6},{15,7},{4,0},{5,1},... | collective-permute-start | bytes 1572872 | tf_op jit(solution)/shard_map/ppermute | solution.py:344
  122.9 6.4 %collective-permute-done.33.refs_0_ = bf16[3,256,128]{2,1,0:T(8,128)(2,1)S(1)} collective-permute-done((bf16[3,256,128]{2,1,0:T(8,128)(2,1)S(1)}, bf16[3,256,128]{2,1,0:T(8,128)(2,1)S(1)}, u32[]{:S(2)}, u32[]{:S(2)}) %collective-permute-start.33) | collective-permute-done | bytes 196640 | tf_op jit(solution)/shard_map/ppermute | solution.py:348
  129.3 2.3 collective-permute-done.34.refs_1_
  136.7 10.4 %collective-permute-done.38.second = bf16[8,256,128]{2,1,0:T(8,128)(2,1)S(1)} collective-permute-done((bf16[8,256,128]{2,1,0:T(8,128)(2,1)S(1)}, bf16[8,256,128]{2,1,0:T(8,128)(2,1)S(1)}, u32[]{:S(2)}, u32[]{:S(2)}) %collective-permute-start.38) | collective-permute-done | bytes 524320 | tf_op jit(solution)/shard_map/ppermute | solution.py:344
  149.6 14.6 %collective-permute-done.35.out = bf16[8,256,128]{2,1,0:T(8,128)(2,1)S(1)} collective-permute-done((bf16[8,256,128]{2,1,0:T(8,128)(2,1)S(1)}, bf16[8,256,128]{2,1,0:T(8,128)(2,1)S(1)}, u32[]{:S(2)}, u32[]{:S(2)}) %collective-permute-start.35) | collective-permute-done | bytes 524320 | tf_op jit(solution)/shard_map/ppermute | solution.py:344
  166.8 3.5 %shard_map.99.field = f32[9,256,128]{2,1,0:T(8,128)S(1)} custom-call(s32[180]{0:T(256)S(1)} %get-tuple-element.88.table, bf16[48,256,256]{2,1,0:T(8,128)(2,1)S(1)} %bitcast.8, bf16[8,256,128]{2,1,0:T(8,128)(2,1)S(1)} %get-tuple-element.120.own, bf16[8,256,128]{2,1,0:T(8,128)(2,1)S(1)} %collective-permute-done.32.refs_0_.first, ...), custom_call_target="tpu_custom_call" | custom-call | tf_op jit(solution)/shard_map/pallas_call | solution.py:270
  170.3 2.3 collective-permute-done.36.got2
  172.6 3.3 %collective-permute-done.37.got3 = bf16[3,256,128]{2,1,0:T(8,128)(2,1)S(1)} collective-permute-done((bf16[3,256,128]{2,1,0:T(8,128)(2,1)S(1)}, bf16[3,256,128]{2,1,0:T(8,128)(2,1)S(1)}, u32[]{:S(2)}, u32[]{:S(2)}) %collective-permute-start.37) | collective-permute-done | bytes 196640 | tf_op jit(solution)/shard_map/ppermute | solution.py:348
  180.5 6.7 %collective-permute-done.47.refs_0_ = bf16[3,256,128]{2,1,0:T(8,128)(2,1)S(1)} collective-permute-done((bf16[3,256,128]{2,1,0:T(8,128)(2,1)S(1)}, bf16[3,256,128]{2,1,0:T(8,128)(2,1)S(1)}, u32[]{:S(2)}, u32[]{:S(2)}) %collective-permute-start.47) | collective-permute-done | bytes 196640 | tf_op jit(solution)/shard_map/ppermute | solution.py:348
  188.9 2.7 %collective-permute-done.46.refs_0_.first = bf16[8,256,128]{2,1,0:T(8,128)(2,1)S(1)} collective-permute-done((bf16[8,256,128]{2,1,0:T(8,128)(2,1)S(1)}, bf16[8,256,128]{2,1,0:T(8,128)(2,1)S(1)}, u32[]{:S(2)}, u32[]{:S(2)}) %collective-permute-start.46) | collective-permute-done | bytes 524320 | tf_op jit(solution)/shard_map/ppermute | solution.py:344
  195.1 9.3 %collective-permute-done.52.second = bf16[8,256,128]{2,1,0:T(8,128)(2,1)S(1)} collective-permute-done((bf16[8,256,128]{2,1,0:T(8,128)(2,1)S(1)}, bf16[8,256,128]{2,1,0:T(8,128)(2,1)S(1)}, u32[]{:S(2)}, u32[]{:S(2)}) %collective-permute-start.52) | collective-permute-done | bytes 524320 | tf_op jit(solution)/shard_map/ppermute | solution.py:344
  206.9 8.5 %collective-permute-done.49.out = bf16[8,256,128]{2,1,0:T(8,128)(2,1)S(1)} collective-permute-done((bf16[8,256,128]{2,1,0:T(8,128)(2,1)S(1)}, bf16[8,256,128]{2,1,0:T(8,128)(2,1)S(1)}, u32[]{:S(2)}, u32[]{:S(2)}) %collective-permute-start.49) | collective-permute-done | bytes 524320 | tf_op jit(solution)/shard_map/ppermute | solution.py:344
  218.1 3.5 %shard_map.104.field = f32[9,256,128]{2,1,0:T(8,128)S(1)} custom-call(s32[180]{0:T(256)S(1)} %get-tuple-element.88.table, bf16[48,256,256]{2,1,0:T(8,128)(2,1)S(1)} %bitcast.8, bf16[8,256,128]{2,1,0:T(8,128)(2,1)S(1)} %get-tuple-element.139.own, bf16[8,256,128]{2,1,0:T(8,128)(2,1)S(1)} %collective-permute-done.46.refs_0_.first, ...), custom_call_target="tpu_custom_call" | custom-call | tf_op jit(solution)/shard_map/pallas_call | solution.py:270
  221.6 2.3 collective-permute-done.50.got2
  223.9 3.3 %collective-permute-done.51.got3 = bf16[3,256,128]{2,1,0:T(8,128)(2,1)S(1)} collective-permute-done((bf16[3,256,128]{2,1,0:T(8,128)(2,1)S(1)}, bf16[3,256,128]{2,1,0:T(8,128)(2,1)S(1)}, u32[]{:S(2)}, u32[]{:S(2)}) %collective-permute-start.51) | collective-permute-done | bytes 196640 | tf_op jit(solution)/shard_map/ppermute | solution.py:348
  227.2 2.7 %shard_map.105 = (f32[8,256,128]{2,1,0:T(8,128)}, f32[8,256,128]{2,1,0:T(8,128)}, f32[1,128]{1,0:T(1,128)S(1)}) custom-call(s32[180]{0:T(256)S(1)} %get-tuple-element.88.table, f32[2]{0:T(128)S(1)} %pad_maximum_fusion.scalars, bf16[48,256,256]{2,1,0:T(8,128)(2,1)S(1)} %bitcast.8, bf16[3,256,128]{2,1,0:T(8,128)(2,1)S(1)} %collective-permute-done.50.got2, ...), custom_call_target="tpu_custom_call" | custom-call | flops 100663296 | bytes 6422528 | tf_op jit(solution)/shard_map/pallas_call | solution.py:328
  229.9 17.5 %all_to_all.6 = f32[16,1,128]{2,1,0:T(1,128)S(1)} all-to-all(f32[16,1,128]{2,1,0:T(1,128)S(1)} %broadcast_in_dim.2), channel_id=1, replica_groups=mesh['groups'=2,'row'=16] {'row'}, dimensions={0} | all-to-all | bytes 16384 | tf_op jit(solution)/shard_map/all_to_all | solution.py:354
  (132 shorter events, 67.3 us)
Async XLA Ops:
  1.9 16.5 %collective-permute-start = (bf16[8,256,128]{2,1,0:T(8,128)(2,1)S(1)}, bf16[8,256,128]{2,1,0:T(8,128)(2,1)S(1)}, u32[]{:S(2)}, u32[]{:S(2)}) collective-permute-start(bf16[8,256,128]{2,1,0:T(8,128)(2,1)S(1)} %convert_element_type.3.own), channel_id=1, source_target_pairs={{0,8},{1,9},{2,10},{3,11},{12,4},{13,5},{14,6},{15,7},{4,0},{5,1},... | collective-permute-start | bytes 1572872 | tf_op jit(solution)/shard_map/ppermute | solution.py:344
  6.0 24.3 %collective-permute-start.4 = (bf16[8,256,128]{2,1,0:T(8,128)(2,1)S(1)}, bf16[8,256,128]{2,1,0:T(8,128)(2,1)S(1)}, u32[]{:S(2)}, u32[]{:S(2)}) collective-permute-start(bf16[8,256,128]{2,1,0:T(8,128)(2,1)S(1)} %convert_element_type.3.own), channel_id=1, source_target_pairs={{0,4},{1,5},{2,6},{3,7},{12,8},{13,9},{14,10},{15,11},{4,12},{5,13... | collective-permute-start | bytes 1572872 | tf_op jit(solution)/shard_map/ppermute | solution.py:344
  20.5 21.2 %collective-permute-start.5 = (bf16[6,256,128]{2,1,0:T(8,128)(2,1)S(1)}, bf16[6,256,128]{2,1,0:T(8,128)(2,1)S(1)}, u32[]{:S(2)}, u32[]{:S(2)}) collective-permute-start(bf16[6,256,128]{2,1,0:T(8,128)(2,1)S(1)} %get-tuple-element.89), channel_id=1, source_target_pairs={{0,2},{1,3},{2,0},{3,1},{4,6},{5,7},{6,4},{7,5},{8,10},{9,11},{10,... | collective-permute-start | bytes 1179656 | tf_op jit(solution)/shard_map/ppermute | solution.py:348
  22.1 19.6 %collective-permute-start.6 = (bf16[6,256,128]{2,1,0:T(8,128)(2,1)S(1)}, bf16[6,256,128]{2,1,0:T(8,128)(2,1)S(1)}, u32[]{:S(2)}, u32[]{:S(2)}) collective-permute-start(bf16[6,256,128]{2,1,0:T(8,128)(2,1)S(1)} %get-tuple-element.90), channel_id=1, source_target_pairs={{0,3},{1,2},{2,1},{3,0},{4,7},{5,6},{6,5},{7,4},{8,11},{9,10},{10,... | collective-permute-start | bytes 1179656 | tf_op jit(solution)/shard_map/ppermute | solution.py:348
  22.1 22.4 %collective-permute-start.9 = (bf16[8,256,128]{2,1,0:T(8,128)(2,1)S(1)}, bf16[8,256,128]{2,1,0:T(8,128)(2,1)S(1)}, u32[]{:S(2)}, u32[]{:S(2)}) collective-permute-start(bf16[8,256,128]{2,1,0:T(8,128)(2,1)S(1)} %convert_element_type.3.own), channel_id=1, source_target_pairs={{4,8},{5,9},{6,10},{7,11},{8,4},{9,5},{10,6},{11,7},{20,24},{21,25... | collective-permute-start | bytes 1572872 | tf_op jit(solution)/shard_map/ppermute | solution.py:344
  22.8 21.7 %collective-permute-start.10 = (bf16[8,256,128]{2,1,0:T(8,128)(2,1)S(1)}, bf16[8,256,128]{2,1,0:T(8,128)(2,1)S(1)}, u32[]{:S(2)}, u32[]{:S(2)}) collective-permute-start(bf16[8,256,128]{2,1,0:T(8,128)(2,1)S(1)} %collective-permute-done.first), channel_id=1, source_target_pairs={{4,0},{5,1},{6,2},{7,3},{8,12},{9,13},{10,14},{11,15},{20,16},{21,... | collective-permute-start | bytes 1572872 | tf_op jit(solution)/shard_map/ppermute | solution.py:344
  48.1 11.6 %collective-permute-start.11 = (bf16[3,256,128]{2,1,0:T(8,128)(2,1)S(1)}, bf16[3,256,128]{2,1,0:T(8,128)(2,1)S(1)}, u32[]{:S(2)}, u32[]{:S(2)}) collective-permute-start(bf16[3,256,128]{2,1,0:T(8,128)(2,1)S(1)} %get-tuple-element.92), channel_id=1, source_target_pairs={{0,2},{1,3},{2,0},{3,1},{4,6},{5,7},{6,4},{7,5},{8,10},{9,11},{10,... | collective-permute-start | bytes 589832 | tf_op jit(solution)/shard_map/ppermute | solution.py:348
  50.2 11.7 %collective-permute-start.12 = (bf16[3,256,128]{2,1,0:T(8,128)(2,1)S(1)}, bf16[3,256,128]{2,1,0:T(8,128)(2,1)S(1)}, u32[]{:S(2)}, u32[]{:S(2)}) collective-permute-start(bf16[3,256,128]{2,1,0:T(8,128)(2,1)S(1)} %get-tuple-element.93), channel_id=1, source_target_pairs={{0,3},{1,2},{2,1},{3,0},{4,7},{5,6},{6,5},{7,4},{8,11},{9,10},{10,... | collective-permute-start | bytes 589832 | tf_op jit(solution)/shard_map/ppermute | solution.py:348
  63.3 14.4 %collective-permute-start.18 = (bf16[8,256,128]{2,1,0:T(8,128)(2,1)S(1)}, bf16[8,256,128]{2,1,0:T(8,128)(2,1)S(1)}, u32[]{:S(2)}, u32[]{:S(2)}) collective-permute-start(bf16[8,256,128]{2,1,0:T(8,128)(2,1)S(1)} %get-tuple-element.101.own), channel_id=1, source_target_pairs={{0,8},{1,9},{2,10},{3,11},{12,4},{13,5},{14,6},{15,7},{4,0},{5,1},... | collective-permute-start | bytes 1572872 | tf_op jit(solution)/shard_map/ppermute | solution.py:344
  63.8 25.7 %collective-permute-start.24 = (bf16[8,256,128]{2,1,0:T(8,128)(2,1)S(1)}, bf16[8,256,128]{2,1,0:T(8,128)(2,1)S(1)}, u32[]{:S(2)}, u32[]{:S(2)}) collective-permute-start(bf16[8,256,128]{2,1,0:T(8,128)(2,1)S(1)} %get-tuple-element.101.own), channel_id=1, source_target_pairs={{0,4},{1,5},{2,6},{3,7},{12,8},{13,9},{14,10},{15,11},{4,12},{5,13... | collective-permute-start | bytes 1572872 | tf_op jit(solution)/shard_map/ppermute | solution.py:344
  79.4 12.6 %collective-permute-start.17 = (bf16[8,256,128]{2,1,0:T(8,128)(2,1)S(1)}, bf16[8,256,128]{2,1,0:T(8,128)(2,1)S(1)}, u32[]{:S(2)}, u32[]{:S(2)}) collective-permute-start(bf16[8,256,128]{2,1,0:T(8,128)(2,1)S(1)} %get-tuple-element.101.own), channel_id=1, source_target_pairs={{4,8},{5,9},{6,10},{7,11},{8,4},{9,5},{10,6},{11,7},{20,24},{21,25... | collective-permute-start | bytes 1572872 | tf_op jit(solution)/shard_map/ppermute | solution.py:344
  80.1 20.5 %collective-permute-start.21 = (bf16[8,256,128]{2,1,0:T(8,128)(2,1)S(1)}, bf16[8,256,128]{2,1,0:T(8,128)(2,1)S(1)}, u32[]{:S(2)}, u32[]{:S(2)}) collective-permute-start(bf16[8,256,128]{2,1,0:T(8,128)(2,1)S(1)} %collective-permute-done.18.refs_0_.first), channel_id=1, source_target_pairs={{4,0},{5,1},{6,2},{7,3},{8,12},{9,13},{10,14},{11,15},{20,16},{21,... | collective-permute-start | bytes 1572872 | tf_op jit(solution)/shard_map/ppermute | solution.py:344
  90.1 13.1 %collective-permute-start.27 = (bf16[9,256,128]{2,1,0:T(8,128)(2,1)S(1)}, bf16[9,256,128]{2,1,0:T(8,128)(2,1)S(1)}, u32[]{:S(2)}, u32[]{:S(2)}) collective-permute-start(bf16[9,256,128]{2,1,0:T(8,128)(2,1)S(1)} %get-tuple-element.110), channel_id=1, source_target_pairs={{0,1},{1,0},{2,3},{3,2},{4,5},{5,4},{6,7},{7,6},{8,9},{9,8},{10,11... | collective-permute-start | bytes 1769480 | tf_op jit(solution)/shard_map/ppermute | solution.py:348
  90.2 12.6 %collective-permute-start.29 = (bf16[3,256,128]{2,1,0:T(8,128)(2,1)S(1)}, bf16[3,256,128]{2,1,0:T(8,128)(2,1)S(1)}, u32[]{:S(2)}, u32[]{:S(2)}) collective-permute-start(bf16[3,256,128]{2,1,0:T(8,128)(2,1)S(1)} %get-tuple-element.116), channel_id=1, source_target_pairs={{0,2},{1,3},{2,0},{3,1},{4,6},{5,7},{6,4},{7,5},{8,10},{9,11},{10,... | collective-permute-start | bytes 589832 | tf_op jit(solution)/shard_map/ppermute | solution.py:348
  91.6 11.6 %collective-permute-start.30 = (bf16[3,256,128]{2,1,0:T(8,128)(2,1)S(1)}, bf16[3,256,128]{2,1,0:T(8,128)(2,1)S(1)}, u32[]{:S(2)}, u32[]{:S(2)}) collective-permute-start(bf16[3,256,128]{2,1,0:T(8,128)(2,1)S(1)} %get-tuple-element.117), channel_id=1, source_target_pairs={{0,3},{1,2},{2,1},{3,0},{4,7},{5,6},{6,5},{7,4},{8,11},{9,10},{10,... | collective-permute-start | bytes 589832 | tf_op jit(solution)/shard_map/ppermute | solution.py:348
  113.7 20.2 %collective-permute-start.32 = (bf16[8,256,128]{2,1,0:T(8,128)(2,1)S(1)}, bf16[8,256,128]{2,1,0:T(8,128)(2,1)S(1)}, u32[]{:S(2)}, u32[]{:S(2)}) collective-permute-start(bf16[8,256,128]{2,1,0:T(8,128)(2,1)S(1)} %get-tuple-element.120.own), channel_id=1, source_target_pairs={{0,8},{1,9},{2,10},{3,11},{12,4},{13,5},{14,6},{15,7},{4,0},{5,1},... | collective-permute-start | bytes 1572872 | tf_op jit(solution)/shard_map/ppermute | solution.py:344
  121.5 25.5 %collective-permute-start.38 = (bf16[8,256,128]{2,1,0:T(8,128)(2,1)S(1)}, bf16[8,256,128]{2,1,0:T(8,128)(2,1)S(1)}, u32[]{:S(2)}, u32[]{:S(2)}) collective-permute-start(bf16[8,256,128]{2,1,0:T(8,128)(2,1)S(1)} %get-tuple-element.120.own), channel_id=1, source_target_pairs={{0,4},{1,5},{2,6},{3,7},{12,8},{13,9},{14,10},{15,11},{4,12},{5,13... | collective-permute-start | bytes 1572872 | tf_op jit(solution)/shard_map/ppermute | solution.py:344
  134.4 12.6 %collective-permute-start.39 = (bf16[3,256,128]{2,1,0:T(8,128)(2,1)S(1)}, bf16[3,256,128]{2,1,0:T(8,128)(2,1)S(1)}, u32[]{:S(2)}, u32[]{:S(2)}) collective-permute-start(bf16[3,256,128]{2,1,0:T(8,128)(2,1)S(1)} %get-tuple-element.126), channel_id=1, source_target_pairs={{0,2},{1,3},{2,0},{3,1},{4,6},{5,7},{6,4},{7,5},{8,10},{9,11},{10,... | collective-permute-start | bytes 589832 | tf_op jit(solution)/shard_map/ppermute | solution.py:348
  134.6 12.4 %collective-permute-start.40 = (bf16[3,256,128]{2,1,0:T(8,128)(2,1)S(1)}, bf16[3,256,128]{2,1,0:T(8,128)(2,1)S(1)}, u32[]{:S(2)}, u32[]{:S(2)}) collective-permute-start(bf16[3,256,128]{2,1,0:T(8,128)(2,1)S(1)} %get-tuple-element.127), channel_id=1, source_target_pairs={{0,3},{1,2},{2,1},{3,0},{4,7},{5,6},{6,5},{7,4},{8,11},{9,10},{10,... | collective-permute-start | bytes 589832 | tf_op jit(solution)/shard_map/ppermute | solution.py:348
  134.7 14.9 %collective-permute-start.31 = (bf16[8,256,128]{2,1,0:T(8,128)(2,1)S(1)}, bf16[8,256,128]{2,1,0:T(8,128)(2,1)S(1)}, u32[]{:S(2)}, u32[]{:S(2)}) collective-permute-start(bf16[8,256,128]{2,1,0:T(8,128)(2,1)S(1)} %get-tuple-element.120.own), channel_id=1, source_target_pairs={{4,8},{5,9},{6,10},{7,11},{8,4},{9,5},{10,6},{11,7},{20,24},{21,25... | collective-permute-start | bytes 1572872 | tf_op jit(solution)/shard_map/ppermute | solution.py:344
  135.4 28.8 %collective-permute-start.35 = (bf16[8,256,128]{2,1,0:T(8,128)(2,1)S(1)}, bf16[8,256,128]{2,1,0:T(8,128)(2,1)S(1)}, u32[]{:S(2)}, u32[]{:S(2)}) collective-permute-start(bf16[8,256,128]{2,1,0:T(8,128)(2,1)S(1)} %collective-permute-done.32.refs_0_.first), channel_id=1, source_target_pairs={{4,0},{5,1},{6,2},{7,3},{8,12},{9,13},{10,14},{11,15},{20,16},{21,... | collective-permute-start | bytes 1572872 | tf_op jit(solution)/shard_map/ppermute | solution.py:344
  147.7 19.1 %collective-permute-start.41 = (bf16[9,256,128]{2,1,0:T(8,128)(2,1)S(1)}, bf16[9,256,128]{2,1,0:T(8,128)(2,1)S(1)}, u32[]{:S(2)}, u32[]{:S(2)}) collective-permute-start(bf16[9,256,128]{2,1,0:T(8,128)(2,1)S(1)} %get-tuple-element.129), channel_id=1, source_target_pairs={{0,1},{1,0},{2,3},{3,2},{4,5},{5,4},{6,7},{7,6},{8,9},{9,8},{10,11... | collective-permute-start | bytes 1769480 | tf_op jit(solution)/shard_map/ppermute | solution.py:348
  147.8 17.8 %collective-permute-start.43 = (bf16[3,256,128]{2,1,0:T(8,128)(2,1)S(1)}, bf16[3,256,128]{2,1,0:T(8,128)(2,1)S(1)}, u32[]{:S(2)}, u32[]{:S(2)}) collective-permute-start(bf16[3,256,128]{2,1,0:T(8,128)(2,1)S(1)} %get-tuple-element.135), channel_id=1, source_target_pairs={{0,2},{1,3},{2,0},{3,1},{4,6},{5,7},{6,4},{7,5},{8,10},{9,11},{10,... | collective-permute-start | bytes 589832 | tf_op jit(solution)/shard_map/ppermute | solution.py:348
  148.7 18.1 %collective-permute-start.44 = (bf16[3,256,128]{2,1,0:T(8,128)(2,1)S(1)}, bf16[3,256,128]{2,1,0:T(8,128)(2,1)S(1)}, u32[]{:S(2)}, u32[]{:S(2)}) collective-permute-start(bf16[3,256,128]{2,1,0:T(8,128)(2,1)S(1)} %get-tuple-element.136), channel_id=1, source_target_pairs={{0,3},{1,2},{2,1},{3,0},{4,7},{5,6},{6,5},{7,4},{8,11},{9,10},{10,... | collective-permute-start | bytes 589832 | tf_op jit(solution)/shard_map/ppermute | solution.py:348
  177.3 14.2 %collective-permute-start.46 = (bf16[8,256,128]{2,1,0:T(8,128)(2,1)S(1)}, bf16[8,256,128]{2,1,0:T(8,128)(2,1)S(1)}, u32[]{:S(2)}, u32[]{:S(2)}) collective-permute-start(bf16[8,256,128]{2,1,0:T(8,128)(2,1)S(1)} %get-tuple-element.139.own), channel_id=1, source_target_pairs={{0,8},{1,9},{2,10},{3,11},{12,4},{13,5},{14,6},{15,7},{4,0},{5,1},... | collective-permute-start | bytes 1572872 | tf_op jit(solution)/shard_map/ppermute | solution.py:344
  178.3 26.0 %collective-permute-start.52 = (bf16[8,256,128]{2,1,0:T(8,128)(2,1)S(1)}, bf16[8,256,128]{2,1,0:T(8,128)(2,1)S(1)}, u32[]{:S(2)}, u32[]{:S(2)}) collective-permute-start(bf16[8,256,128]{2,1,0:T(8,128)(2,1)S(1)} %get-tuple-element.139.own), channel_id=1, source_target_pairs={{0,4},{1,5},{2,6},{3,7},{12,8},{13,9},{14,10},{15,11},{4,12},{5,13... | collective-permute-start | bytes 1572872 | tf_op jit(solution)/shard_map/ppermute | solution.py:344
  192.2 12.2 %collective-permute-start.53 = (bf16[3,256,128]{2,1,0:T(8,128)(2,1)S(1)}, bf16[3,256,128]{2,1,0:T(8,128)(2,1)S(1)}, u32[]{:S(2)}, u32[]{:S(2)}) collective-permute-start(bf16[3,256,128]{2,1,0:T(8,128)(2,1)S(1)} %get-tuple-element.145), channel_id=1, source_target_pairs={{0,2},{1,3},{2,0},{3,1},{4,6},{5,7},{6,4},{7,5},{8,10},{9,11},{10,... | collective-permute-start | bytes 589832 | tf_op jit(solution)/shard_map/ppermute | solution.py:348
  193.1 13.9 %collective-permute-start.45 = (bf16[8,256,128]{2,1,0:T(8,128)(2,1)S(1)}, bf16[8,256,128]{2,1,0:T(8,128)(2,1)S(1)}, u32[]{:S(2)}, u32[]{:S(2)}) collective-permute-start(bf16[8,256,128]{2,1,0:T(8,128)(2,1)S(1)} %get-tuple-element.139.own), channel_id=1, source_target_pairs={{4,8},{5,9},{6,10},{7,11},{8,4},{9,5},{10,6},{11,7},{20,24},{21,25... | collective-permute-start | bytes 1572872 | tf_op jit(solution)/shard_map/ppermute | solution.py:344
  193.8 21.7 %collective-permute-start.49 = (bf16[8,256,128]{2,1,0:T(8,128)(2,1)S(1)}, bf16[8,256,128]{2,1,0:T(8,128)(2,1)S(1)}, u32[]{:S(2)}, u32[]{:S(2)}) collective-permute-start(bf16[8,256,128]{2,1,0:T(8,128)(2,1)S(1)} %collective-permute-done.46.refs_0_.first), channel_id=1, source_target_pairs={{4,0},{5,1},{6,2},{7,3},{8,12},{9,13},{10,14},{11,15},{20,16},{21,... | collective-permute-start | bytes 1572872 | tf_op jit(solution)/shard_map/ppermute | solution.py:344
  205.0 13.1 %collective-permute-start.55 = (bf16[9,256,128]{2,1,0:T(8,128)(2,1)S(1)}, bf16[9,256,128]{2,1,0:T(8,128)(2,1)S(1)}, u32[]{:S(2)}, u32[]{:S(2)}) collective-permute-start(bf16[9,256,128]{2,1,0:T(8,128)(2,1)S(1)} %get-tuple-element.148), channel_id=1, source_target_pairs={{0,1},{1,0},{2,3},{3,2},{4,5},{5,4},{6,7},{7,6},{8,9},{9,8},{10,11... | collective-permute-start | bytes 1769480 | tf_op jit(solution)/shard_map/ppermute | solution.py:348
  205.1 12.6 %collective-permute-start.57 = (bf16[3,256,128]{2,1,0:T(8,128)(2,1)S(1)}, bf16[3,256,128]{2,1,0:T(8,128)(2,1)S(1)}, u32[]{:S(2)}, u32[]{:S(2)}) collective-permute-start(bf16[3,256,128]{2,1,0:T(8,128)(2,1)S(1)} %get-tuple-element.154), channel_id=1, source_target_pairs={{0,2},{1,3},{2,0},{3,1},{4,6},{5,7},{6,4},{7,5},{8,10},{9,11},{10,... | collective-permute-start | bytes 589832 | tf_op jit(solution)/shard_map/ppermute | solution.py:348
  206.5 11.6 %collective-permute-start.58 = (bf16[3,256,128]{2,1,0:T(8,128)(2,1)S(1)}, bf16[3,256,128]{2,1,0:T(8,128)(2,1)S(1)}, u32[]{:S(2)}, u32[]{:S(2)}) collective-permute-start(bf16[3,256,128]{2,1,0:T(8,128)(2,1)S(1)} %get-tuple-element.155), channel_id=1, source_target_pairs={{0,3},{1,2},{2,1},{3,0},{4,7},{5,6},{6,5},{7,4},{8,11},{9,10},{10,... | collective-permute-start | bytes 589832 | tf_op jit(solution)/shard_map/ppermute | solution.py:348
  (33 other events, 300.0 us)

commit v12 on v11

--- a/solution.py
+++ b/solution.py
@@ -378,21 +378,21 @@
     for step in range(STEPS):
         last = step == STEPS - 1
         own1 = along_z(FIRST, own0)
-        own2 = along_z(SECOND, own0)
         mid = along_z(MIDDLE, own0)
         if step == 0:
+            again, notes = lax.optimization_barrier((own0, notes))
+            own2 = along_z(SECOND, again)
             own1, notes = lax.optimization_barrier((own1, notes))
             out = along_z(OUTWARD, own1)
             table, *packs01 = start(layout, mine, notes, own0, own1)
             got1 = to_other_y(packs01)
-            plane = note + notes[0] + notes[1] + notes[2]
-            half = across(4, plane)
-            own2, got1, half = lax.optimization_barrier((own2, got1, half))
-            half = plane + half
+            own2, got1, mid, out = lax.optimization_barrier((own2, got1, mid, out))
             parts = ((0, 0), (0, 1), (2, 0))
             got = got1
         else:
             got0 = to_other_y(packs0)
+            again, got0 = lax.optimization_barrier((own0, got0))
+            own2 = along_z(SECOND, again)
             own1, got0 = lax.optimization_barrier((own1, got0))
             out = along_z(OUTWARD, own1)
             got1 = to_other_y(other_y((1,), [own1]))
@@ -402,6 +402,10 @@
         packs2 = pack(functools.partial(second_kernel, layout), [cap, cap, 3 * cap], table, [own0, own1, own2])
         got2 = to_other_y(packs2)
         core = across(1, packs2[2])
+        if step == 0:
+            note, core = lax.optimization_barrier((note, core))
+            plane = note + notes[0] + notes[1] + notes[2]
+            half = plane + across(4, plane)
         packs3 = pack(functools.partial(third_kernel, layout), [cap] * 3, table, [mid, out])
         core3 = across(1, packs3[2])
         got3 = to_other_y(packs3)

time: 248 us -> 233 us (0.940)
  waiting for transfers between devices: 139 us -> 130 us
  blocking collectives: 17.5 us -> 10.7 us
    ppermute x16, waiting for transfers between devices: 75.6 us -> 60.3 us  [along_z(): lax.ppermute(value, 'row', [(a * 4 + i, b * 4 + i) for a, b in pairs for...]
    all_to_all x1, blocking collectives: 17.5 us -> 10.7 us  [row_sum(): lax.all_to_all(spread, 'row', split_axis=0, concat_axis=0, tiled=True)]
    ppermute x43, waiting for transfers between devices: 63.5 us -> 69.8 us  [across(): return lax.ppermute(value, 'row', [(i, i ^ flip) for i in range(16)])]
    ppermute x43, starting transfers between devices: 25.2 us -> 31.2 us  [across(): return lax.ppermute(value, 'row', [(i, i ^ flip) for i in range(16)])]
    ppermute x16, starting transfers between devices: 24 us -> 19 us  [along_z(): lax.ppermute(value, 'row', [(a * 4 + i, b * 4 + i) for a, b in pairs for...]
  transfers between devices with their start and end apart: 59 -> 59, of which waited for: 30 -> 34; matrix products, arithmetic and copies ran while one was open for 1% -> 0% of each run, Pallas kernels for 11% -> 11%
where the time goes in v12:
time: 233 us; the launch traced here: 232 us
  waiting for transfers between devices  130 us (56%)
  starting transfers between devices  50.2 us (22%)
  Pallas kernels  32.8 us (14%)
  blocking collectives  10.7 us (5%)
  local copies, waits for them, and re-layouts  4.06 us (2%)
  between operations  2.44 us (1%)
    ppermute x43, waiting for transfers between devices, across(): return lax.ppermute(value, 'row', [(i, i ^ flip) for i in range(16)])  69.8 us
    ppermute x16, waiting for transfers between devices, along_z(): lax.ppermute(value, 'row', [(a * 4 + i, b * 4 + i) for a, b in pairs for...  60.3 us
    ppermute x43, starting transfers between devices, across(): return lax.ppermute(value, 'row', [(i, i ^ flip) for i in range(16)])  31.2 us
    ppermute x16, starting transfers between devices, along_z(): lax.ppermute(value, 'row', [(a * 4 + i, b * 4 + i) for a, b in pairs for...  19 us
    pallas_call x4, Pallas kernels, early(): pl.pallas_call(functools.partial(early_kernel, layout, parts), out_shape=...  13.8 us
    all_to_all x1, blocking collectives, row_sum(): lax.all_to_all(spread, 'row', split_axis=0, concat_axis=0, tiled=True)  10.7 us
    pallas_call x4, Pallas kernels, late(): pl.pallas_call(functools.partial(late_kernel, layout, last), out_shape=(s...  6.81 us
    pallas_call x11, Pallas kernels, pack(): pl.pallas_call(kernel, out_shape=[jax.ShapeDtypeStruct((size, tile, repl)...  6.63 us
  transfers between devices with their start and end apart: 59, of which 34 were waited for; matrix products, arithmetic and copies ran while one was open for 0% of the time, Pallas kernels for 11%

profile of v12, /device:TPU:0, one launch (start us, length us, event | category | flops | bytes accessed | tf_op | source)
XLA Modules:
  0.0 232.4 jit_solution(8624555027300098144)
XLA Ops:
  1.9 4.1 %collective-permute-start = (bf16[8,256,128]{2,1,0:T(8,128)(2,1)S(1)}, bf16[8,256,128]{2,1,0:T(8,128)(2,1)S(1)}, u32[]{:S(2)}, u32[]{:S(2)}) collective-permute-start(bf16[8,256,128]{2,1,0:T(8,128)(2,1)S(1)} %convert_element_type.3.own), channel_id=1, source_target_pairs={{0,8},{1,9},{2,10},{3,11},{12,4},{13,5},{14,6},{15,7},{4,0},{5,1},... | collective-permute-start | bytes 1572872 | tf_op jit(solution)/shard_map/ppermute | solution.py:344
  6.7 4.2 %shard_map.85 = (s32[144]{0:T(256)}, f32[1,128]{1,0:T(1,128)}) custom-call(s32[48]{0:T(128)} %rows.1, s32[48]{0:T(128)} %cols.1, s32[1]{0:T(128)S(6)} %copy.10.count, bf16[48,256,256]{2,1,0:T(8,128)(2,1)} %tiles.17), custom_call_target="tpu_custom_call" | custom-call | tf_op jit(solution)/shard_map/pallas_call | solution.py:131
  22.2 19.4 %collective-permute-done.4.second = bf16[8,256,128]{2,1,0:T(8,128)(2,1)S(1)} collective-permute-done((bf16[8,256,128]{2,1,0:T(8,128)(2,1)S(1)}, bf16[8,256,128]{2,1,0:T(8,128)(2,1)S(1)}, u32[]{:S(2)}, u32[]{:S(2)}) %collective-permute-start.4) | collective-permute-done | bytes 524320 | tf_op jit(solution)/shard_map/ppermute | solution.py:344
  53.4 3.2 %collective-permute-done.16.refs_3_ = bf16[3,256,128]{2,1,0:T(8,128)(2,1)S(1)} collective-permute-done((bf16[3,256,128]{2,1,0:T(8,128)(2,1)S(1)}, bf16[3,256,128]{2,1,0:T(8,128)(2,1)S(1)}, u32[]{:S(2)}, u32[]{:S(2)}) %collective-permute-start.16) | collective-permute-done | bytes 196640 | tf_op jit(solution)/shard_map/ppermute | solution.py:348
  56.6 2.8 %copy-done = bf16[48,256,256]{2,1,0:T(8,128)(2,1)S(1)} copy-done((bf16[48,256,256]{2,1,0:T(8,128)(2,1)S(1)}, bf16[48,256,256]{2,1,0:T(8,128)(2,1)}, u32[]{:S(2)}) %copy-start) | copy-done | bytes 6291480
  59.3 3.4 %shard_map.89.field = f32[9,256,128]{2,1,0:T(8,128)S(1)} custom-call(s32[180]{0:T(256)S(1)} %get-tuple-element.107.table, bf16[48,256,256]{2,1,0:T(8,128)(2,1)S(1)} %copy-done, bf16[8,256,128]{2,1,0:T(8,128)(2,1)S(1)} %convert_element_type.3.own, bf16[8,256,128]{2,1,0:T(8,128)(2,1)S(1)} %collective-permute-done.first, ...), custom_call_target="tpu_custom_call" | custom-call | tf_op jit(solution)/shard_map/pallas_call | solution.py:270
  68.6 5.8 %collective-permute-done.19.refs_0_ = bf16[3,256,128]{2,1,0:T(8,128)(2,1)S(1)} collective-permute-done((bf16[3,256,128]{2,1,0:T(8,128)(2,1)S(1)}, bf16[3,256,128]{2,1,0:T(8,128)(2,1)S(1)}, u32[]{:S(2)}, u32[]{:S(2)}) %collective-permute-start.19) | collective-permute-done | bytes 196640 | tf_op jit(solution)/shard_map/ppermute | solution.py:348
  74.4 3.4 %collective-permute-done.20.refs_1_ = bf16[3,256,128]{2,1,0:T(8,128)(2,1)S(1)} collective-permute-done((bf16[3,256,128]{2,1,0:T(8,128)(2,1)S(1)}, bf16[3,256,128]{2,1,0:T(8,128)(2,1)S(1)}, u32[]{:S(2)}, u32[]{:S(2)}) %collective-permute-start.20) | collective-permute-done | bytes 196640 | tf_op jit(solution)/shard_map/ppermute | solution.py:348
  84.4 4.3 %collective-permute-done.25.refs_2_ = bf16[3,256,128]{2,1,0:T(8,128)(2,1)S(1)} collective-permute-done((bf16[3,256,128]{2,1,0:T(8,128)(2,1)S(1)}, bf16[3,256,128]{2,1,0:T(8,128)(2,1)S(1)}, u32[]{:S(2)}, u32[]{:S(2)}) %collective-permute-start.25) | collective-permute-done | bytes 196640 | tf_op jit(solution)/shard_map/ppermute | solution.py:348
  90.9 2.6 %collective-permute-done.24.second = bf16[8,256,128]{2,1,0:T(8,128)(2,1)S(1)} collective-permute-done((bf16[8,256,128]{2,1,0:T(8,128)(2,1)S(1)}, bf16[8,256,128]{2,1,0:T(8,128)(2,1)S(1)}, u32[]{:S(2)}, u32[]{:S(2)}) %collective-permute-start.24) | collective-permute-done | bytes 524320 | tf_op jit(solution)/shard_map/ppermute | solution.py:344
  96.1 8.2 %collective-permute-done.21.out = bf16[8,256,128]{2,1,0:T(8,128)(2,1)S(1)} collective-permute-done((bf16[8,256,128]{2,1,0:T(8,128)(2,1)S(1)}, bf16[8,256,128]{2,1,0:T(8,128)(2,1)S(1)}, u32[]{:S(2)}, u32[]{:S(2)}) %collective-permute-start.21) | collective-permute-done | bytes 524320 | tf_op jit(solution)/shard_map/ppermute | solution.py:344
  107.0 3.5 %shard_map.94.field = f32[9,256,128]{2,1,0:T(8,128)S(1)} custom-call(s32[180]{0:T(256)S(1)} %get-tuple-element.107.table, bf16[48,256,256]{2,1,0:T(8,128)(2,1)S(1)} %bitcast.8, bf16[8,256,128]{2,1,0:T(8,128)(2,1)S(1)} %get-tuple-element.132.own, bf16[8,256,128]{2,1,0:T(8,128)(2,1)S(1)} %collective-permute-done.18.refs_0_.first, ...), custom_call_target="tpu_custom_call" | custom-call | tf_op jit(solution)/shard_map/pallas_call | solution.py:270
  110.5 2.3 collective-permute-done.22.got2
  112.8 3.3 %collective-permute-done.23.got3 = bf16[3,256,128]{2,1,0:T(8,128)(2,1)S(1)} collective-permute-done((bf16[3,256,128]{2,1,0:T(8,128)(2,1)S(1)}, bf16[3,256,128]{2,1,0:T(8,128)(2,1)S(1)}, u32[]{:S(2)}, u32[]{:S(2)}) %collective-permute-start.23) | collective-permute-done | bytes 196640 | tf_op jit(solution)/shard_map/ppermute | solution.py:348
  120.5 6.2 %collective-permute-done.33.refs_0_ = bf16[3,256,128]{2,1,0:T(8,128)(2,1)S(1)} collective-permute-done((bf16[3,256,128]{2,1,0:T(8,128)(2,1)S(1)}, bf16[3,256,128]{2,1,0:T(8,128)(2,1)S(1)}, u32[]{:S(2)}, u32[]{:S(2)}) %collective-permute-start.33) | collective-permute-done | bytes 196640 | tf_op jit(solution)/shard_map/ppermute | solution.py:348
  126.7 2.3 collective-permute-done.34.refs_1_
  135.8 4.3 %collective-permute-done.39.refs_2_ = bf16[3,256,128]{2,1,0:T(8,128)(2,1)S(1)} collective-permute-done((bf16[3,256,128]{2,1,0:T(8,128)(2,1)S(1)}, bf16[3,256,128]{2,1,0:T(8,128)(2,1)S(1)}, u32[]{:S(2)}, u32[]{:S(2)}) %collective-permute-start.39) | collective-permute-done | bytes 196640 | tf_op jit(solution)/shard_map/ppermute | solution.py:348
  141.8 2.8 %collective-permute-done.38.second = bf16[8,256,128]{2,1,0:T(8,128)(2,1)S(1)} collective-permute-done((bf16[8,256,128]{2,1,0:T(8,128)(2,1)S(1)}, bf16[8,256,128]{2,1,0:T(8,128)(2,1)S(1)}, u32[]{:S(2)}, u32[]{:S(2)}) %collective-permute-start.38) | collective-permute-done | bytes 524320 | tf_op jit(solution)/shard_map/ppermute | solution.py:344
  147.3 8.7 %collective-permute-done.35.out = bf16[8,256,128]{2,1,0:T(8,128)(2,1)S(1)} collective-permute-done((bf16[8,256,128]{2,1,0:T(8,128)(2,1)S(1)}, bf16[8,256,128]{2,1,0:T(8,128)(2,1)S(1)}, u32[]{:S(2)}, u32[]{:S(2)}) %collective-permute-start.35) | collective-permute-done | bytes 524320 | tf_op jit(solution)/shard_map/ppermute | solution.py:344
  158.6 3.5 %shard_map.99.field = f32[9,256,128]{2,1,0:T(8,128)S(1)} custom-call(s32[180]{0:T(256)S(1)} %get-tuple-element.107.table, bf16[48,256,256]{2,1,0:T(8,128)(2,1)S(1)} %bitcast.8, bf16[8,256,128]{2,1,0:T(8,128)(2,1)S(1)} %get-tuple-element.154.own, bf16[8,256,128]{2,1,0:T(8,128)(2,1)S(1)} %collective-permute-done.32.refs_0_.first, ...), custom_call_target="tpu_custom_call" | custom-call | tf_op jit(solution)/shard_map/pallas_call | solution.py:270
  162.1 2.3 %collective-permute-done.36.got2 = bf16[3,256,128]{2,1,0:T(8,128)(2,1)S(1)} collective-permute-done((bf16[3,256,128]{2,1,0:T(8,128)(2,1)S(1)}, bf16[3,256,128]{2,1,0:T(8,128)(2,1)S(1)}, u32[]{:S(2)}, u32[]{:S(2)}) %collective-permute-start.36) | collective-permute-done | bytes 196640 | tf_op jit(solution)/shard_map/ppermute | solution.py:348
  164.4 3.3 %collective-permute-done.37.got3 = bf16[3,256,128]{2,1,0:T(8,128)(2,1)S(1)} collective-permute-done((bf16[3,256,128]{2,1,0:T(8,128)(2,1)S(1)}, bf16[3,256,128]{2,1,0:T(8,128)(2,1)S(1)}, u32[]{:S(2)}, u32[]{:S(2)}) %collective-permute-start.37) | collective-permute-done | bytes 196640 | tf_op jit(solution)/shard_map/ppermute | solution.py:348
  171.1 6.2 %collective-permute-done.47.refs_0_ = bf16[3,256,128]{2,1,0:T(8,128)(2,1)S(1)} collective-permute-done((bf16[3,256,128]{2,1,0:T(8,128)(2,1)S(1)}, bf16[3,256,128]{2,1,0:T(8,128)(2,1)S(1)}, u32[]{:S(2)}, u32[]{:S(2)}) %collective-permute-start.47) | collective-permute-done | bytes 196640 | tf_op jit(solution)/shard_map/ppermute | solution.py:348
  177.3 2.7 %collective-permute-done.48.refs_1_ = bf16[3,256,128]{2,1,0:T(8,128)(2,1)S(1)} collective-permute-done((bf16[3,256,128]{2,1,0:T(8,128)(2,1)S(1)}, bf16[3,256,128]{2,1,0:T(8,128)(2,1)S(1)}, u32[]{:S(2)}, u32[]{:S(2)}) %collective-permute-start.48) | collective-permute-done | bytes 196640 | tf_op jit(solution)/shard_map/ppermute | solution.py:348
  187.4 4.4 %collective-permute-done.53.refs_2_ = bf16[3,256,128]{2,1,0:T(8,128)(2,1)S(1)} collective-permute-done((bf16[3,256,128]{2,1,0:T(8,128)(2,1)S(1)}, bf16[3,256,128]{2,1,0:T(8,128)(2,1)S(1)}, u32[]{:S(2)}, u32[]{:S(2)}) %collective-permute-start.53) | collective-permute-done | bytes 196640 | tf_op jit(solution)/shard_map/ppermute | solution.py:348
  193.5 2.3 collective-permute-done.52.second
  198.3 8.5 %collective-permute-done.49.out = bf16[8,256,128]{2,1,0:T(8,128)(2,1)S(1)} collective-permute-done((bf16[8,256,128]{2,1,0:T(8,128)(2,1)S(1)}, bf16[8,256,128]{2,1,0:T(8,128)(2,1)S(1)}, u32[]{:S(2)}, u32[]{:S(2)}) %collective-permute-start.49) | collective-permute-done | bytes 524320 | tf_op jit(solution)/shard_map/ppermute | solution.py:344
  209.5 3.5 %shard_map.104.field = f32[9,256,128]{2,1,0:T(8,128)S(1)} custom-call(s32[180]{0:T(256)S(1)} %get-tuple-element.107.table, bf16[48,256,256]{2,1,0:T(8,128)(2,1)S(1)} %bitcast.8, bf16[8,256,128]{2,1,0:T(8,128)(2,1)S(1)} %get-tuple-element.176.own, bf16[8,256,128]{2,1,0:T(8,128)(2,1)S(1)} %collective-permute-done.46.refs_0_.first, ...), custom_call_target="tpu_custom_call" | custom-call | tf_op jit(solution)/shard_map/pallas_call | solution.py:270
  212.9 2.4 %collective-permute-done.50.got2 = bf16[3,256,128]{2,1,0:T(8,128)(2,1)S(1)} collective-permute-done((bf16[3,256,128]{2,1,0:T(8,128)(2,1)S(1)}, bf16[3,256,128]{2,1,0:T(8,128)(2,1)S(1)}, u32[]{:S(2)}, u32[]{:S(2)}) %collective-permute-start.50) | collective-permute-done | bytes 196640 | tf_op jit(solution)/shard_map/ppermute | solution.py:348
  215.3 3.3 %collective-permute-done.51.got3 = bf16[3,256,128]{2,1,0:T(8,128)(2,1)S(1)} collective-permute-done((bf16[3,256,128]{2,1,0:T(8,128)(2,1)S(1)}, bf16[3,256,128]{2,1,0:T(8,128)(2,1)S(1)}, u32[]{:S(2)}, u32[]{:S(2)}) %collective-permute-start.51) | collective-permute-done | bytes 196640 | tf_op jit(solution)/shard_map/ppermute | solution.py:348
  218.6 2.7 %shard_map.105 = (f32[8,256,128]{2,1,0:T(8,128)}, f32[8,256,128]{2,1,0:T(8,128)}, f32[1,128]{1,0:T(1,128)S(1)}) custom-call(s32[180]{0:T(256)S(1)} %get-tuple-element.107.table, f32[2]{0:T(128)S(1)} %pad_maximum_fusion.scalars, bf16[48,256,256]{2,1,0:T(8,128)(2,1)S(1)} %bitcast.8, bf16[3,256,128]{2,1,0:T(8,128)(2,1)S(1)} %collective-permute-done.50.got2, ...), custom_call_target="tpu_custom_call" | custom-call | flops 100663296 | bytes 6422528 | tf_op jit(solution)/shard_map/pallas_call | solution.py:328
  221.2 10.7 %all_to_all.6 = f32[16,1,128]{2,1,0:T(1,128)S(1)} all-to-all(f32[16,1,128]{2,1,0:T(1,128)S(1)} %broadcast_in_dim.2), channel_id=1, replica_groups=mesh['groups'=2,'row'=16] {'row'}, dimensions={0} | all-to-all | bytes 16384 | tf_op jit(solution)/shard_map/all_to_all | solution.py:354
  (134 shorter events, 79.6 us)
Async XLA Ops:
  1.9 15.3 %collective-permute-start = (bf16[8,256,128]{2,1,0:T(8,128)(2,1)S(1)}, bf16[8,256,128]{2,1,0:T(8,128)(2,1)S(1)}, u32[]{:S(2)}, u32[]{:S(2)}) collective-permute-start(bf16[8,256,128]{2,1,0:T(8,128)(2,1)S(1)} %convert_element_type.3.own), channel_id=1, source_target_pairs={{0,8},{1,9},{2,10},{3,11},{12,4},{13,5},{14,6},{15,7},{4,0},{5,1},... | collective-permute-start | bytes 1572872 | tf_op jit(solution)/shard_map/ppermute | solution.py:344
  15.8 25.8 %collective-permute-start.4 = (bf16[8,256,128]{2,1,0:T(8,128)(2,1)S(1)}, bf16[8,256,128]{2,1,0:T(8,128)(2,1)S(1)}, u32[]{:S(2)}, u32[]{:S(2)}) collective-permute-start(bf16[8,256,128]{2,1,0:T(8,128)(2,1)S(1)} %convert_element_type.3.own), channel_id=1, source_target_pairs={{0,4},{1,5},{2,6},{3,7},{12,8},{13,9},{14,10},{15,11},{4,12},{5,13... | collective-permute-start | bytes 1572872 | tf_op jit(solution)/shard_map/ppermute | solution.py:344
  17.2 26.4 %collective-permute-start.8 = (bf16[8,256,128]{2,1,0:T(8,128)(2,1)S(1)}, bf16[8,256,128]{2,1,0:T(8,128)(2,1)S(1)}, u32[]{:S(2)}, u32[]{:S(2)}) collective-permute-start(bf16[8,256,128]{2,1,0:T(8,128)(2,1)S(1)} %collective-permute-done.first), channel_id=1, source_target_pairs={{4,0},{5,1},{6,2},{7,3},{8,12},{9,13},{10,14},{11,15},{20,16},{21,... | collective-permute-start | bytes 1572872 | tf_op jit(solution)/shard_map/ppermute | solution.py:344
  20.6 21.0 %collective-permute-start.5 = (bf16[6,256,128]{2,1,0:T(8,128)(2,1)S(1)}, bf16[6,256,128]{2,1,0:T(8,128)(2,1)S(1)}, u32[]{:S(2)}, u32[]{:S(2)}) collective-permute-start(bf16[6,256,128]{2,1,0:T(8,128)(2,1)S(1)} %get-tuple-element.109), channel_id=1, source_target_pairs={{0,2},{1,3},{2,0},{3,1},{4,6},{5,7},{6,4},{7,5},{8,10},{9,11},{10,... | collective-permute-start | bytes 1179656 | tf_op jit(solution)/shard_map/ppermute | solution.py:348
  22.2 19.4 %collective-permute-start.6 = (bf16[6,256,128]{2,1,0:T(8,128)(2,1)S(1)}, bf16[6,256,128]{2,1,0:T(8,128)(2,1)S(1)}, u32[]{:S(2)}, u32[]{:S(2)}) collective-permute-start(bf16[6,256,128]{2,1,0:T(8,128)(2,1)S(1)} %get-tuple-element.110), channel_id=1, source_target_pairs={{0,3},{1,2},{2,1},{3,0},{4,7},{5,6},{6,5},{7,4},{8,11},{9,10},{10,... | collective-permute-start | bytes 1179656 | tf_op jit(solution)/shard_map/ppermute | solution.py:348
  47.1 9.5 %collective-permute-start.16 = (bf16[3,256,128]{2,1,0:T(8,128)(2,1)S(1)}, bf16[3,256,128]{2,1,0:T(8,128)(2,1)S(1)}, u32[]{:S(2)}, u32[]{:S(2)}) collective-permute-start(bf16[3,256,128]{2,1,0:T(8,128)(2,1)S(1)} %get-tuple-element.123), channel_id=1, source_target_pairs={{0,3},{1,2},{2,1},{3,0},{4,7},{5,6},{6,5},{7,4},{8,11},{9,10},{10,... | collective-permute-start | bytes 589832 | tf_op jit(solution)/shard_map/ppermute | solution.py:348
  47.2 17.0 %collective-permute-start.12 = (bf16[3,256,128]{2,1,0:T(8,128)(2,1)S(1)}, bf16[3,256,128]{2,1,0:T(8,128)(2,1)S(1)}, u32[]{:S(2)}, u32[]{:S(2)}) collective-permute-start(bf16[3,256,128]{2,1,0:T(8,128)(2,1)S(1)} %get-tuple-element.116), channel_id=1, source_target_pairs={{0,2},{1,3},{2,0},{3,1},{4,6},{5,7},{6,4},{7,5},{8,10},{9,11},{10,... | collective-permute-start | bytes 589832 | tf_op jit(solution)/shard_map/ppermute | solution.py:348
  50.7 13.5 %collective-permute-start.13 = (bf16[3,256,128]{2,1,0:T(8,128)(2,1)S(1)}, bf16[3,256,128]{2,1,0:T(8,128)(2,1)S(1)}, u32[]{:S(2)}, u32[]{:S(2)}) collective-permute-start(bf16[3,256,128]{2,1,0:T(8,128)(2,1)S(1)} %get-tuple-element.117), channel_id=1, source_target_pairs={{0,3},{1,2},{2,1},{3,0},{4,7},{5,6},{6,5},{7,4},{8,11},{9,10},{10,... | collective-permute-start | bytes 589832 | tf_op jit(solution)/shard_map/ppermute | solution.py:348
  51.6 11.2 %collective-permute-start.11 = (f32[1,128]{1,0:T(1,128)S(1)}, f32[1,128]{1,0:T(1,128)S(1)}, u32[]{:S(2)}, u32[]{:S(2)}) collective-permute-start(f32[1,128]{1,0:T(1,128)S(1)} %add.18), channel_id=1, source_target_pairs={{0,8},{1,9},{2,10},{3,11},{4,12},{5,13},{6,14},{7,15},{8,0},{9,1},... | collective-permute-start | bytes 1544 | tf_op jit(solution)/shard_map/ppermute | solution.py:348
  65.6 14.7 %collective-permute-start.18 = (bf16[8,256,128]{2,1,0:T(8,128)(2,1)S(1)}, bf16[8,256,128]{2,1,0:T(8,128)(2,1)S(1)}, u32[]{:S(2)}, u32[]{:S(2)}) collective-permute-start(bf16[8,256,128]{2,1,0:T(8,128)(2,1)S(1)} %get-tuple-element.132.own), channel_id=1, source_target_pairs={{0,8},{1,9},{2,10},{3,11},{12,4},{13,5},{14,6},{15,7},{4,0},{5,1},... | collective-permute-start | bytes 1572872 | tf_op jit(solution)/shard_map/ppermute | solution.py:344
  68.2 9.6 %collective-permute-start.20 = (bf16[3,256,128]{2,1,0:T(8,128)(2,1)S(1)}, bf16[3,256,128]{2,1,0:T(8,128)(2,1)S(1)}, u32[]{:S(2)}, u32[]{:S(2)}) collective-permute-start(bf16[3,256,128]{2,1,0:T(8,128)(2,1)S(1)} %get-tuple-element.126), channel_id=1, source_target_pairs={{0,3},{1,2},{2,1},{3,0},{4,7},{5,6},{6,5},{7,4},{8,11},{9,10},{10,... | collective-permute-start | bytes 589832 | tf_op jit(solution)/shard_map/ppermute | solution.py:348
  77.8 15.7 %collective-permute-start.24 = (bf16[8,256,128]{2,1,0:T(8,128)(2,1)S(1)}, bf16[8,256,128]{2,1,0:T(8,128)(2,1)S(1)}, u32[]{:S(2)}, u32[]{:S(2)}) collective-permute-start(bf16[8,256,128]{2,1,0:T(8,128)(2,1)S(1)} %get-tuple-element.132.own), channel_id=1, source_target_pairs={{0,4},{1,5},{2,6},{3,7},{12,8},{13,9},{14,10},{15,11},{4,12},{5,13... | collective-permute-start | bytes 1572872 | tf_op jit(solution)/shard_map/ppermute | solution.py:344
  82.4 13.6 %collective-permute-start.17 = (bf16[8,256,128]{2,1,0:T(8,128)(2,1)S(1)}, bf16[8,256,128]{2,1,0:T(8,128)(2,1)S(1)}, u32[]{:S(2)}, u32[]{:S(2)}) collective-permute-start(bf16[8,256,128]{2,1,0:T(8,128)(2,1)S(1)} %get-tuple-element.132.own), channel_id=1, source_target_pairs={{4,8},{5,9},{6,10},{7,11},{8,4},{9,5},{10,6},{11,7},{20,24},{21,25... | collective-permute-start | bytes 1572872 | tf_op jit(solution)/shard_map/ppermute | solution.py:344
  83.1 21.2 %collective-permute-start.21 = (bf16[8,256,128]{2,1,0:T(8,128)(2,1)S(1)}, bf16[8,256,128]{2,1,0:T(8,128)(2,1)S(1)}, u32[]{:S(2)}, u32[]{:S(2)}) collective-permute-start(bf16[8,256,128]{2,1,0:T(8,128)(2,1)S(1)} %collective-permute-done.18.refs_0_.first), channel_id=1, source_target_pairs={{4,0},{5,1},{6,2},{7,3},{8,12},{9,13},{10,14},{11,15},{20,16},{21,... | collective-permute-start | bytes 1572872 | tf_op jit(solution)/shard_map/ppermute | solution.py:344
  94.1 12.8 %collective-permute-start.27 = (bf16[9,256,128]{2,1,0:T(8,128)(2,1)S(1)}, bf16[9,256,128]{2,1,0:T(8,128)(2,1)S(1)}, u32[]{:S(2)}, u32[]{:S(2)}) collective-permute-start(bf16[9,256,128]{2,1,0:T(8,128)(2,1)S(1)} %get-tuple-element.136), channel_id=1, source_target_pairs={{0,1},{1,0},{2,3},{3,2},{4,5},{5,4},{6,7},{7,6},{8,9},{9,8},{10,11... | collective-permute-start | bytes 1769480 | tf_op jit(solution)/shard_map/ppermute | solution.py:348
  94.2 12.4 %collective-permute-start.29 = (bf16[3,256,128]{2,1,0:T(8,128)(2,1)S(1)}, bf16[3,256,128]{2,1,0:T(8,128)(2,1)S(1)}, u32[]{:S(2)}, u32[]{:S(2)}) collective-permute-start(bf16[3,256,128]{2,1,0:T(8,128)(2,1)S(1)} %get-tuple-element.142), channel_id=1, source_target_pairs={{0,2},{1,3},{2,0},{3,1},{4,6},{5,7},{6,4},{7,5},{8,10},{9,11},{10,... | collective-permute-start | bytes 589832 | tf_op jit(solution)/shard_map/ppermute | solution.py:348
  95.8 11.2 %collective-permute-start.30 = (bf16[3,256,128]{2,1,0:T(8,128)(2,1)S(1)}, bf16[3,256,128]{2,1,0:T(8,128)(2,1)S(1)}, u32[]{:S(2)}, u32[]{:S(2)}) collective-permute-start(bf16[3,256,128]{2,1,0:T(8,128)(2,1)S(1)} %get-tuple-element.143), channel_id=1, source_target_pairs={{0,3},{1,2},{2,1},{3,0},{4,7},{5,6},{6,5},{7,4},{8,11},{9,10},{10,... | collective-permute-start | bytes 589832 | tf_op jit(solution)/shard_map/ppermute | solution.py:348
  106.6 9.4 %collective-permute-start.23 = (bf16[3,256,128]{2,1,0:T(8,128)(2,1)S(1)}, bf16[3,256,128]{2,1,0:T(8,128)(2,1)S(1)}, u32[]{:S(2)}, u32[]{:S(2)}) collective-permute-start(bf16[3,256,128]{2,1,0:T(8,128)(2,1)S(1)} %get-tuple-element.131), channel_id=1, source_target_pairs={{0,3},{1,2},{2,1},{3,0},{4,7},{5,6},{6,5},{7,4},{8,11},{9,10},{10,... | collective-permute-start | bytes 589832 | tf_op jit(solution)/shard_map/ppermute | solution.py:348
  117.5 14.2 %collective-permute-start.32 = (bf16[8,256,128]{2,1,0:T(8,128)(2,1)S(1)}, bf16[8,256,128]{2,1,0:T(8,128)(2,1)S(1)}, u32[]{:S(2)}, u32[]{:S(2)}) collective-permute-start(bf16[8,256,128]{2,1,0:T(8,128)(2,1)S(1)} %get-tuple-element.154.own), channel_id=1, source_target_pairs={{0,8},{1,9},{2,10},{3,11},{12,4},{13,5},{14,6},{15,7},{4,0},{5,1},... | collective-permute-start | bytes 1572872 | tf_op jit(solution)/shard_map/ppermute | solution.py:344
  129.0 15.7 %collective-permute-start.38 = (bf16[8,256,128]{2,1,0:T(8,128)(2,1)S(1)}, bf16[8,256,128]{2,1,0:T(8,128)(2,1)S(1)}, u32[]{:S(2)}, u32[]{:S(2)}) collective-permute-start(bf16[8,256,128]{2,1,0:T(8,128)(2,1)S(1)} %get-tuple-element.154.own), channel_id=1, source_target_pairs={{0,4},{1,5},{2,6},{3,7},{12,8},{13,9},{14,10},{15,11},{4,12},{5,13... | collective-permute-start | bytes 1572872 | tf_op jit(solution)/shard_map/ppermute | solution.py:344
  133.8 13.4 %collective-permute-start.31 = (bf16[8,256,128]{2,1,0:T(8,128)(2,1)S(1)}, bf16[8,256,128]{2,1,0:T(8,128)(2,1)S(1)}, u32[]{:S(2)}, u32[]{:S(2)}) collective-permute-start(bf16[8,256,128]{2,1,0:T(8,128)(2,1)S(1)} %get-tuple-element.154.own), channel_id=1, source_target_pairs={{4,8},{5,9},{6,10},{7,11},{8,4},{9,5},{10,6},{11,7},{20,24},{21,25... | collective-permute-start | bytes 1572872 | tf_op jit(solution)/shard_map/ppermute | solution.py:344
  134.5 21.4 %collective-permute-start.35 = (bf16[8,256,128]{2,1,0:T(8,128)(2,1)S(1)}, bf16[8,256,128]{2,1,0:T(8,128)(2,1)S(1)}, u32[]{:S(2)}, u32[]{:S(2)}) collective-permute-start(bf16[8,256,128]{2,1,0:T(8,128)(2,1)S(1)} %collective-permute-done.32.refs_0_.first), channel_id=1, source_target_pairs={{4,0},{5,1},{6,2},{7,3},{8,12},{9,13},{10,14},{11,15},{20,16},{21,... | collective-permute-start | bytes 1572872 | tf_op jit(solution)/shard_map/ppermute | solution.py:344
  145.3 13.3 %collective-permute-start.41 = (bf16[9,256,128]{2,1,0:T(8,128)(2,1)S(1)}, bf16[9,256,128]{2,1,0:T(8,128)(2,1)S(1)}, u32[]{:S(2)}, u32[]{:S(2)}) collective-permute-start(bf16[9,256,128]{2,1,0:T(8,128)(2,1)S(1)} %get-tuple-element.158), channel_id=1, source_target_pairs={{0,1},{1,0},{2,3},{3,2},{4,5},{5,4},{6,7},{7,6},{8,9},{9,8},{10,11... | collective-permute-start | bytes 1769480 | tf_op jit(solution)/shard_map/ppermute | solution.py:348
  145.4 12.8 %collective-permute-start.43 = (bf16[3,256,128]{2,1,0:T(8,128)(2,1)S(1)}, bf16[3,256,128]{2,1,0:T(8,128)(2,1)S(1)}, u32[]{:S(2)}, u32[]{:S(2)}) collective-permute-start(bf16[3,256,128]{2,1,0:T(8,128)(2,1)S(1)} %get-tuple-element.164), channel_id=1, source_target_pairs={{0,2},{1,3},{2,0},{3,1},{4,6},{5,7},{6,4},{7,5},{8,10},{9,11},{10,... | collective-permute-start | bytes 589832 | tf_op jit(solution)/shard_map/ppermute | solution.py:348
  147.0 11.6 %collective-permute-start.44 = (bf16[3,256,128]{2,1,0:T(8,128)(2,1)S(1)}, bf16[3,256,128]{2,1,0:T(8,128)(2,1)S(1)}, u32[]{:S(2)}, u32[]{:S(2)}) collective-permute-start(bf16[3,256,128]{2,1,0:T(8,128)(2,1)S(1)} %get-tuple-element.165), channel_id=1, source_target_pairs={{0,3},{1,2},{2,1},{3,0},{4,7},{5,6},{6,5},{7,4},{8,11},{9,10},{10,... | collective-permute-start | bytes 589832 | tf_op jit(solution)/shard_map/ppermute | solution.py:348
  169.1 14.2 %collective-permute-start.46 = (bf16[8,256,128]{2,1,0:T(8,128)(2,1)S(1)}, bf16[8,256,128]{2,1,0:T(8,128)(2,1)S(1)}, u32[]{:S(2)}, u32[]{:S(2)}) collective-permute-start(bf16[8,256,128]{2,1,0:T(8,128)(2,1)S(1)} %get-tuple-element.176.own), channel_id=1, source_target_pairs={{0,8},{1,9},{2,10},{3,11},{12,4},{13,5},{14,6},{15,7},{4,0},{5,1},... | collective-permute-start | bytes 1572872 | tf_op jit(solution)/shard_map/ppermute | solution.py:344
  180.0 15.7 %collective-permute-start.52 = (bf16[8,256,128]{2,1,0:T(8,128)(2,1)S(1)}, bf16[8,256,128]{2,1,0:T(8,128)(2,1)S(1)}, u32[]{:S(2)}, u32[]{:S(2)}) collective-permute-start(bf16[8,256,128]{2,1,0:T(8,128)(2,1)S(1)} %get-tuple-element.176.own), channel_id=1, source_target_pairs={{0,4},{1,5},{2,6},{3,7},{12,8},{13,9},{14,10},{15,11},{4,12},{5,13... | collective-permute-start | bytes 1572872 | tf_op jit(solution)/shard_map/ppermute | solution.py:344
  185.4 12.9 %collective-permute-start.45 = (bf16[8,256,128]{2,1,0:T(8,128)(2,1)S(1)}, bf16[8,256,128]{2,1,0:T(8,128)(2,1)S(1)}, u32[]{:S(2)}, u32[]{:S(2)}) collective-permute-start(bf16[8,256,128]{2,1,0:T(8,128)(2,1)S(1)} %get-tuple-element.176.own), channel_id=1, source_target_pairs={{4,8},{5,9},{6,10},{7,11},{8,4},{9,5},{10,6},{11,7},{20,24},{21,25... | collective-permute-start | bytes 1572872 | tf_op jit(solution)/shard_map/ppermute | solution.py:344
  186.1 20.8 %collective-permute-start.49 = (bf16[8,256,128]{2,1,0:T(8,128)(2,1)S(1)}, bf16[8,256,128]{2,1,0:T(8,128)(2,1)S(1)}, u32[]{:S(2)}, u32[]{:S(2)}) collective-permute-start(bf16[8,256,128]{2,1,0:T(8,128)(2,1)S(1)} %collective-permute-done.46.refs_0_.first), channel_id=1, source_target_pairs={{4,0},{5,1},{6,2},{7,3},{8,12},{9,13},{10,14},{11,15},{20,16},{21,... | collective-permute-start | bytes 1572872 | tf_op jit(solution)/shard_map/ppermute | solution.py:344
  196.3 13.1 %collective-permute-start.55 = (bf16[9,256,128]{2,1,0:T(8,128)(2,1)S(1)}, bf16[9,256,128]{2,1,0:T(8,128)(2,1)S(1)}, u32[]{:S(2)}, u32[]{:S(2)}) collective-permute-start(bf16[9,256,128]{2,1,0:T(8,128)(2,1)S(1)} %get-tuple-element.180), channel_id=1, source_target_pairs={{0,1},{1,0},{2,3},{3,2},{4,5},{5,4},{6,7},{7,6},{8,9},{9,8},{10,11... | collective-permute-start | bytes 1769480 | tf_op jit(solution)/shard_map/ppermute | solution.py:348
  196.4 12.7 %collective-permute-start.57 = (bf16[3,256,128]{2,1,0:T(8,128)(2,1)S(1)}, bf16[3,256,128]{2,1,0:T(8,128)(2,1)S(1)}, u32[]{:S(2)}, u32[]{:S(2)}) collective-permute-start(bf16[3,256,128]{2,1,0:T(8,128)(2,1)S(1)} %get-tuple-element.186), channel_id=1, source_target_pairs={{0,2},{1,3},{2,0},{3,1},{4,6},{5,7},{6,4},{7,5},{8,10},{9,11},{10,... | collective-permute-start | bytes 589832 | tf_op jit(solution)/shard_map/ppermute | solution.py:348
  198.0 11.5 %collective-permute-start.58 = (bf16[3,256,128]{2,1,0:T(8,128)(2,1)S(1)}, bf16[3,256,128]{2,1,0:T(8,128)(2,1)S(1)}, u32[]{:S(2)}, u32[]{:S(2)}) collective-permute-start(bf16[3,256,128]{2,1,0:T(8,128)(2,1)S(1)} %get-tuple-element.187), channel_id=1, source_target_pairs={{0,3},{1,2},{2,1},{3,0},{4,7},{5,6},{6,5},{7,4},{8,11},{9,10},{10,... | collective-permute-start | bytes 589832 | tf_op jit(solution)/shard_map/ppermute | solution.py:348
  (34 other events, 278.9 us)

commit v13 on v12

--- a/solution.py
+++ b/solution.py
@@ -378,11 +378,11 @@
     for step in range(STEPS):
         last = step == STEPS - 1
         own1 = along_z(FIRST, own0)
-        mid = along_z(MIDDLE, own0)
         if step == 0:
             again, notes = lax.optimization_barrier((own0, notes))
             own2 = along_z(SECOND, again)
-            own1, notes = lax.optimization_barrier((own1, notes))
+            again, own1 = lax.optimization_barrier((again, own1))
+            mid = along_z(MIDDLE, again)
             out = along_z(OUTWARD, own1)
             table, *packs01 = start(layout, mine, notes, own0, own1)
             got1 = to_other_y(packs01)
@@ -390,6 +390,7 @@
             parts = ((0, 0), (0, 1), (2, 0))
             got = got1
         else:
+            mid = along_z(MIDDLE, own0)
             got0 = to_other_y(packs0)
             again, got0 = lax.optimization_barrier((own0, got0))
             own2 = along_z(SECOND, again)

time: 233 us -> 234 us (level)
  starting transfers between devices: 50.2 us -> 54.7 us
  waiting for transfers between devices: 130 us -> 126 us
    ppermute x16, waiting for transfers between devices: 60.3 us -> 52.3 us  [along_z(): lax.ppermute(value, 'row', [(a * 4 + i, b * 4 + i) for a, b in pairs for...]
    ppermute x43, waiting for transfers between devices: 69.8 us -> 73.8 us  [across(): return lax.ppermute(value, 'row', [(i, i ^ flip) for i in range(16)])]
    ppermute x43, starting transfers between devices: 31.2 us -> 34.3 us  [across(): return lax.ppermute(value, 'row', [(i, i ^ flip) for i in range(16)])]
  transfers between devices with their start and end apart: 59 -> 59, of which waited for: 34 -> 36; matrix products, arithmetic and copies ran while one was open for 0% -> 0% of each run, Pallas kernels for 11% -> 11%
where the time goes in v13:
time: 234 us; the launch traced here: 233 us
  waiting for transfers between devices  126 us (54%)
  starting transfers between devices  54.7 us (23%)
  Pallas kernels  33 us (14%)
  blocking collectives  10.8 us (5%)
  local copies, waits for them, and re-layouts  4.06 us (2%)
  between operations  2.39 us (1%)
    ppermute x43, waiting for transfers between devices, across(): return lax.ppermute(value, 'row', [(i, i ^ flip) for i in range(16)])  73.8 us
    ppermute x16, waiting for transfers between devices, along_z(): lax.ppermute(value, 'row', [(a * 4 + i, b * 4 + i) for a, b in pairs for...  52.3 us
    ppermute x43, starting transfers between devices, across(): return lax.ppermute(value, 'row', [(i, i ^ flip) for i in range(16)])  34.3 us
    ppermute x16, starting transfers between devices, along_z(): lax.ppermute(value, 'row', [(a * 4 + i, b * 4 + i) for a, b in pairs for...  20.4 us
    pallas_call x4, Pallas kernels, early(): pl.pallas_call(functools.partial(early_kernel, layout, parts), out_shape=...  13.8 us
    all_to_all x1, blocking collectives, row_sum(): lax.all_to_all(spread, 'row', split_axis=0, concat_axis=0, tiled=True)  10.8 us
    pallas_call x4, Pallas kernels, late(): pl.pallas_call(functools.partial(late_kernel, layout, last), out_shape=(s...  6.81 us
    pallas_call x11, Pallas kernels, pack(): pl.pallas_call(kernel, out_shape=[jax.ShapeDtypeStruct((size, tile, repl)...  6.63 us
  transfers between devices with their start and end apart: 59, of which 36 were waited for; matrix products, arithmetic and copies ran while one was open for 0% of the time, Pallas kernels for 11%

profile of v13, /device:TPU:0, one launch (start us, length us, event | category | flops | bytes accessed | tf_op | source)
XLA Modules:
  0.0 233.2 jit_solution(15358127860061805390)
XLA Ops:
  1.9 4.1 %collective-permute-start.3 = (bf16[8,256,128]{2,1,0:T(8,128)(2,1)S(1)}, bf16[8,256,128]{2,1,0:T(8,128)(2,1)S(1)}, u32[]{:S(2)}, u32[]{:S(2)}) collective-permute-start(bf16[8,256,128]{2,1,0:T(8,128)(2,1)S(1)} %convert_element_type.3.own), channel_id=1, source_target_pairs={{0,8},{1,9},{2,10},{3,11},{12,4},{13,5},{14,6},{15,7},{4,0},{5,1},... | collective-permute-start | bytes 1572872 | tf_op jit(solution)/shard_map/ppermute | solution.py:344
  6.7 4.3 %shard_map.85 = (s32[144]{0:T(256)}, f32[1,128]{1,0:T(1,128)}) custom-call(s32[48]{0:T(128)} %rows.1, s32[48]{0:T(128)} %cols.1, s32[1]{0:T(128)S(6)} %copy.10.count, bf16[48,256,256]{2,1,0:T(8,128)(2,1)} %tiles.17), custom_call_target="tpu_custom_call" | custom-call | tf_op jit(solution)/shard_map/pallas_call | solution.py:131
  24.0 7.2 %collective-permute-done.4.second = bf16[8,256,128]{2,1,0:T(8,128)(2,1)S(1)} collective-permute-done((bf16[8,256,128]{2,1,0:T(8,128)(2,1)S(1)}, bf16[8,256,128]{2,1,0:T(8,128)(2,1)S(1)}, u32[]{:S(2)}, u32[]{:S(2)}) %collective-permute-start.4) | collective-permute-done | bytes 524320 | tf_op jit(solution)/shard_map/ppermute | solution.py:344
  31.3 2.8 %collective-permute-done.5.refs_0_ = bf16[6,256,128]{2,1,0:T(8,128)(2,1)S(1)} collective-permute-done((bf16[6,256,128]{2,1,0:T(8,128)(2,1)S(1)}, bf16[6,256,128]{2,1,0:T(8,128)(2,1)S(1)}, u32[]{:S(2)}, u32[]{:S(2)}) %collective-permute-start.5) | collective-permute-done | bytes 393248 | tf_op jit(solution)/shard_map/ppermute | solution.py:348
  34.1 4.7 %collective-permute-done.6.refs_1_ = bf16[6,256,128]{2,1,0:T(8,128)(2,1)S(1)} collective-permute-done((bf16[6,256,128]{2,1,0:T(8,128)(2,1)S(1)}, bf16[6,256,128]{2,1,0:T(8,128)(2,1)S(1)}, u32[]{:S(2)}, u32[]{:S(2)}) %collective-permute-start.6) | collective-permute-done | bytes 393248 | tf_op jit(solution)/shard_map/ppermute | solution.py:348
  38.8 3.2 %collective-permute-done.8.out = bf16[8,256,128]{2,1,0:T(8,128)(2,1)S(1)} collective-permute-done((bf16[8,256,128]{2,1,0:T(8,128)(2,1)S(1)}, bf16[8,256,128]{2,1,0:T(8,128)(2,1)S(1)}, u32[]{:S(2)}, u32[]{:S(2)}) %collective-permute-start.8) | collective-permute-done | bytes 524320 | tf_op jit(solution)/shard_map/ppermute | solution.py:344
  45.4 3.5 %collective-permute-start.10 = (f32[1,128]{1,0:T(1,128)S(1)}, f32[1,128]{1,0:T(1,128)S(1)}, u32[]{:S(2)}, u32[]{:S(2)}) collective-permute-start(f32[1,128]{1,0:T(1,128)S(1)} %add_add_fusion), channel_id=1, source_target_pairs={{0,4},{1,5},{2,6},{3,7},{4,0},{5,1},{6,2},{7,3},{8,12},{9,13},{10,... | collective-permute-start | bytes 1544 | tf_op jit(solution)/shard_map/ppermute | solution.py:348
  54.4 2.8 %copy-done = bf16[48,256,256]{2,1,0:T(8,128)(2,1)S(1)} copy-done((bf16[48,256,256]{2,1,0:T(8,128)(2,1)S(1)}, bf16[48,256,256]{2,1,0:T(8,128)(2,1)}, u32[]{:S(2)}) %copy-start) | copy-done | bytes 6291480
  57.2 3.4 %shard_map.89.field = f32[9,256,128]{2,1,0:T(8,128)S(1)} custom-call(s32[180]{0:T(256)S(1)} %get-tuple-element.103.table, bf16[48,256,256]{2,1,0:T(8,128)(2,1)S(1)} %copy-done, bf16[8,256,128]{2,1,0:T(8,128)(2,1)S(1)} %convert_element_type.3.own, bf16[8,256,128]{2,1,0:T(8,128)(2,1)S(1)} %collective-permute-done.3.first, ...), custom_call_target="tpu_custom_call" | custom-call | tf_op jit(solution)/shard_map/pallas_call | solution.py:270
  64.0 3.6 %collective-permute-start.18 = (bf16[8,256,128]{2,1,0:T(8,128)(2,1)S(1)}, bf16[8,256,128]{2,1,0:T(8,128)(2,1)S(1)}, u32[]{:S(2)}, u32[]{:S(2)}) collective-permute-start(bf16[8,256,128]{2,1,0:T(8,128)(2,1)S(1)} %get-tuple-element.128.own), channel_id=1, source_target_pairs={{0,8},{1,9},{2,10},{3,11},{12,4},{13,5},{14,6},{15,7},{4,0},{5,1},... | collective-permute-start | bytes 1572872 | tf_op jit(solution)/shard_map/ppermute | solution.py:344
  69.1 6.2 %collective-permute-done.19.refs_0_ = bf16[3,256,128]{2,1,0:T(8,128)(2,1)S(1)} collective-permute-done((bf16[3,256,128]{2,1,0:T(8,128)(2,1)S(1)}, bf16[3,256,128]{2,1,0:T(8,128)(2,1)S(1)}, u32[]{:S(2)}, u32[]{:S(2)}) %collective-permute-start.19) | collective-permute-done | bytes 196640 | tf_op jit(solution)/shard_map/ppermute | solution.py:348
  84.4 4.3 %collective-permute-done.25.refs_2_ = bf16[3,256,128]{2,1,0:T(8,128)(2,1)S(1)} collective-permute-done((bf16[3,256,128]{2,1,0:T(8,128)(2,1)S(1)}, bf16[3,256,128]{2,1,0:T(8,128)(2,1)S(1)}, u32[]{:S(2)}, u32[]{:S(2)}) %collective-permute-start.25) | collective-permute-done | bytes 196640 | tf_op jit(solution)/shard_map/ppermute | solution.py:348
  90.8 2.9 %collective-permute-done.24.second = bf16[8,256,128]{2,1,0:T(8,128)(2,1)S(1)} collective-permute-done((bf16[8,256,128]{2,1,0:T(8,128)(2,1)S(1)}, bf16[8,256,128]{2,1,0:T(8,128)(2,1)S(1)}, u32[]{:S(2)}, u32[]{:S(2)}) %collective-permute-start.24) | collective-permute-done | bytes 524320 | tf_op jit(solution)/shard_map/ppermute | solution.py:344
  96.2 8.6 %collective-permute-done.21.out = bf16[8,256,128]{2,1,0:T(8,128)(2,1)S(1)} collective-permute-done((bf16[8,256,128]{2,1,0:T(8,128)(2,1)S(1)}, bf16[8,256,128]{2,1,0:T(8,128)(2,1)S(1)}, u32[]{:S(2)}, u32[]{:S(2)}) %collective-permute-start.21) | collective-permute-done | bytes 524320 | tf_op jit(solution)/shard_map/ppermute | solution.py:344
  107.5 3.5 %shard_map.94.field = f32[9,256,128]{2,1,0:T(8,128)S(1)} custom-call(s32[180]{0:T(256)S(1)} %get-tuple-element.103.table, bf16[48,256,256]{2,1,0:T(8,128)(2,1)S(1)} %bitcast.8, bf16[8,256,128]{2,1,0:T(8,128)(2,1)S(1)} %get-tuple-element.128.own, bf16[8,256,128]{2,1,0:T(8,128)(2,1)S(1)} %collective-permute-done.18.refs_0_.first, ...), custom_call_target="tpu_custom_call" | custom-call | tf_op jit(solution)/shard_map/pallas_call | solution.py:270
  113.3 3.3 %collective-permute-done.23.got3 = bf16[3,256,128]{2,1,0:T(8,128)(2,1)S(1)} collective-permute-done((bf16[3,256,128]{2,1,0:T(8,128)(2,1)S(1)}, bf16[3,256,128]{2,1,0:T(8,128)(2,1)S(1)}, u32[]{:S(2)}, u32[]{:S(2)}) %collective-permute-start.23) | collective-permute-done | bytes 196640 | tf_op jit(solution)/shard_map/ppermute | solution.py:348
  120.9 6.3 %collective-permute-done.33.refs_0_ = bf16[3,256,128]{2,1,0:T(8,128)(2,1)S(1)} collective-permute-done((bf16[3,256,128]{2,1,0:T(8,128)(2,1)S(1)}, bf16[3,256,128]{2,1,0:T(8,128)(2,1)S(1)}, u32[]{:S(2)}, u32[]{:S(2)}) %collective-permute-start.33) | collective-permute-done | bytes 196640 | tf_op jit(solution)/shard_map/ppermute | solution.py:348
  127.2 2.5 %collective-permute-done.34.refs_1_ = bf16[3,256,128]{2,1,0:T(8,128)(2,1)S(1)} collective-permute-done((bf16[3,256,128]{2,1,0:T(8,128)(2,1)S(1)}, bf16[3,256,128]{2,1,0:T(8,128)(2,1)S(1)}, u32[]{:S(2)}, u32[]{:S(2)}) %collective-permute-start.34) | collective-permute-done | bytes 196640 | tf_op jit(solution)/shard_map/ppermute | solution.py:348
  136.2 4.4 %collective-permute-done.39.refs_2_ = bf16[3,256,128]{2,1,0:T(8,128)(2,1)S(1)} collective-permute-done((bf16[3,256,128]{2,1,0:T(8,128)(2,1)S(1)}, bf16[3,256,128]{2,1,0:T(8,128)(2,1)S(1)}, u32[]{:S(2)}, u32[]{:S(2)}) %collective-permute-start.39) | collective-permute-done | bytes 196640 | tf_op jit(solution)/shard_map/ppermute | solution.py:348
  142.3 3.0 %collective-permute-done.38.second = bf16[8,256,128]{2,1,0:T(8,128)(2,1)S(1)} collective-permute-done((bf16[8,256,128]{2,1,0:T(8,128)(2,1)S(1)}, bf16[8,256,128]{2,1,0:T(8,128)(2,1)S(1)}, u32[]{:S(2)}, u32[]{:S(2)}) %collective-permute-start.38) | collective-permute-done | bytes 524320 | tf_op jit(solution)/shard_map/ppermute | solution.py:344
  148.0 8.6 %collective-permute-done.35.out = bf16[8,256,128]{2,1,0:T(8,128)(2,1)S(1)} collective-permute-done((bf16[8,256,128]{2,1,0:T(8,128)(2,1)S(1)}, bf16[8,256,128]{2,1,0:T(8,128)(2,1)S(1)}, u32[]{:S(2)}, u32[]{:S(2)}) %collective-permute-start.35) | collective-permute-done | bytes 524320 | tf_op jit(solution)/shard_map/ppermute | solution.py:344
  159.2 3.5 %shard_map.99.field = f32[9,256,128]{2,1,0:T(8,128)S(1)} custom-call(s32[180]{0:T(256)S(1)} %get-tuple-element.103.table, bf16[48,256,256]{2,1,0:T(8,128)(2,1)S(1)} %bitcast.8, bf16[8,256,128]{2,1,0:T(8,128)(2,1)S(1)} %get-tuple-element.150.own, bf16[8,256,128]{2,1,0:T(8,128)(2,1)S(1)} %collective-permute-done.32.refs_0_.first, ...), custom_call_target="tpu_custom_call" | custom-call | tf_op jit(solution)/shard_map/pallas_call | solution.py:270
  165.0 3.3 %collective-permute-done.37.got3 = bf16[3,256,128]{2,1,0:T(8,128)(2,1)S(1)} collective-permute-done((bf16[3,256,128]{2,1,0:T(8,128)(2,1)S(1)}, bf16[3,256,128]{2,1,0:T(8,128)(2,1)S(1)}, u32[]{:S(2)}, u32[]{:S(2)}) %collective-permute-start.37) | collective-permute-done | bytes 196640 | tf_op jit(solution)/shard_map/ppermute | solution.py:348
  171.8 6.2 %collective-permute-done.47.refs_0_ = bf16[3,256,128]{2,1,0:T(8,128)(2,1)S(1)} collective-permute-done((bf16[3,256,128]{2,1,0:T(8,128)(2,1)S(1)}, bf16[3,256,128]{2,1,0:T(8,128)(2,1)S(1)}, u32[]{:S(2)}, u32[]{:S(2)}) %collective-permute-start.47) | collective-permute-done | bytes 196640 | tf_op jit(solution)/shard_map/ppermute | solution.py:348
  178.0 2.5 %collective-permute-done.48.refs_1_ = bf16[3,256,128]{2,1,0:T(8,128)(2,1)S(1)} collective-permute-done((bf16[3,256,128]{2,1,0:T(8,128)(2,1)S(1)}, bf16[3,256,128]{2,1,0:T(8,128)(2,1)S(1)}, u32[]{:S(2)}, u32[]{:S(2)}) %collective-permute-start.48) | collective-permute-done | bytes 196640 | tf_op jit(solution)/shard_map/ppermute | solution.py:348
  188.0 4.4 %collective-permute-done.53.refs_2_ = bf16[3,256,128]{2,1,0:T(8,128)(2,1)S(1)} collective-permute-done((bf16[3,256,128]{2,1,0:T(8,128)(2,1)S(1)}, bf16[3,256,128]{2,1,0:T(8,128)(2,1)S(1)}, u32[]{:S(2)}, u32[]{:S(2)}) %collective-permute-start.53) | collective-permute-done | bytes 196640 | tf_op jit(solution)/shard_map/ppermute | solution.py:348
  198.9 8.6 %collective-permute-done.49.out = bf16[8,256,128]{2,1,0:T(8,128)(2,1)S(1)} collective-permute-done((bf16[8,256,128]{2,1,0:T(8,128)(2,1)S(1)}, bf16[8,256,128]{2,1,0:T(8,128)(2,1)S(1)}, u32[]{:S(2)}, u32[]{:S(2)}) %collective-permute-start.49) | collective-permute-done | bytes 524320 | tf_op jit(solution)/shard_map/ppermute | solution.py:344
  210.1 3.5 %shard_map.104.field = f32[9,256,128]{2,1,0:T(8,128)S(1)} custom-call(s32[180]{0:T(256)S(1)} %get-tuple-element.103.table, bf16[48,256,256]{2,1,0:T(8,128)(2,1)S(1)} %bitcast.8, bf16[8,256,128]{2,1,0:T(8,128)(2,1)S(1)} %get-tuple-element.172.own, bf16[8,256,128]{2,1,0:T(8,128)(2,1)S(1)} %collective-permute-done.46.refs_0_.first, ...), custom_call_target="tpu_custom_call" | custom-call | tf_op jit(solution)/shard_map/pallas_call | solution.py:270
  213.6 2.4 %collective-permute-done.50.got2 = bf16[3,256,128]{2,1,0:T(8,128)(2,1)S(1)} collective-permute-done((bf16[3,256,128]{2,1,0:T(8,128)(2,1)S(1)}, bf16[3,256,128]{2,1,0:T(8,128)(2,1)S(1)}, u32[]{:S(2)}, u32[]{:S(2)}) %collective-permute-start.50) | collective-permute-done | bytes 196640 | tf_op jit(solution)/shard_map/ppermute | solution.py:348
  215.9 3.3 %collective-permute-done.51.got3 = bf16[3,256,128]{2,1,0:T(8,128)(2,1)S(1)} collective-permute-done((bf16[3,256,128]{2,1,0:T(8,128)(2,1)S(1)}, bf16[3,256,128]{2,1,0:T(8,128)(2,1)S(1)}, u32[]{:S(2)}, u32[]{:S(2)}) %collective-permute-start.51) | collective-permute-done | bytes 196640 | tf_op jit(solution)/shard_map/ppermute | solution.py:348
  219.2 2.7 %shard_map.105 = (f32[8,256,128]{2,1,0:T(8,128)}, f32[8,256,128]{2,1,0:T(8,128)}, f32[1,128]{1,0:T(1,128)S(1)}) custom-call(s32[180]{0:T(256)S(1)} %get-tuple-element.103.table, f32[2]{0:T(128)S(1)} %pad_maximum_fusion.scalars, bf16[48,256,256]{2,1,0:T(8,128)(2,1)S(1)} %bitcast.8, bf16[3,256,128]{2,1,0:T(8,128)(2,1)S(1)} %collective-permute-done.50.got2, ...), custom_call_target="tpu_custom_call" | custom-call | flops 100663296 | bytes 6422528 | tf_op jit(solution)/shard_map/pallas_call | solution.py:328
  221.9 10.8 %all_to_all.6 = f32[16,1,128]{2,1,0:T(1,128)S(1)} all-to-all(f32[16,1,128]{2,1,0:T(1,128)S(1)} %broadcast_in_dim.2), channel_id=1, replica_groups=mesh['groups'=2,'row'=16] {'row'}, dimensions={0} | all-to-all | bytes 16384 | tf_op jit(solution)/shard_map/all_to_all | solution.py:354
  (134 shorter events, 86.6 us)
Async XLA Ops:
  1.9 15.9 %collective-permute-start.3 = (bf16[8,256,128]{2,1,0:T(8,128)(2,1)S(1)}, bf16[8,256,128]{2,1,0:T(8,128)(2,1)S(1)}, u32[]{:S(2)}, u32[]{:S(2)}) collective-permute-start(bf16[8,256,128]{2,1,0:T(8,128)(2,1)S(1)} %convert_element_type.3.own), channel_id=1, source_target_pairs={{0,8},{1,9},{2,10},{3,11},{12,4},{13,5},{14,6},{15,7},{4,0},{5,1},... | collective-permute-start | bytes 1572872 | tf_op jit(solution)/shard_map/ppermute | solution.py:344
  15.6 15.7 %collective-permute-start.4 = (bf16[8,256,128]{2,1,0:T(8,128)(2,1)S(1)}, bf16[8,256,128]{2,1,0:T(8,128)(2,1)S(1)}, u32[]{:S(2)}, u32[]{:S(2)}) collective-permute-start(bf16[8,256,128]{2,1,0:T(8,128)(2,1)S(1)} %convert_element_type.3.own), channel_id=1, source_target_pairs={{0,4},{1,5},{2,6},{3,7},{12,8},{13,9},{14,10},{15,11},{4,12},{5,13... | collective-permute-start | bytes 1572872 | tf_op jit(solution)/shard_map/ppermute | solution.py:344
  17.9 24.2 %collective-permute-start.8 = (bf16[8,256,128]{2,1,0:T(8,128)(2,1)S(1)}, bf16[8,256,128]{2,1,0:T(8,128)(2,1)S(1)}, u32[]{:S(2)}, u32[]{:S(2)}) collective-permute-start(bf16[8,256,128]{2,1,0:T(8,128)(2,1)S(1)} %collective-permute-done.3.first), channel_id=1, source_target_pairs={{4,0},{5,1},{6,2},{7,3},{8,12},{9,13},{10,14},{11,15},{20,16},{21,... | collective-permute-start | bytes 1572872 | tf_op jit(solution)/shard_map/ppermute | solution.py:344
  19.2 22.9 %collective-permute-start.7 = (bf16[8,256,128]{2,1,0:T(8,128)(2,1)S(1)}, bf16[8,256,128]{2,1,0:T(8,128)(2,1)S(1)}, u32[]{:S(2)}, u32[]{:S(2)}) collective-permute-start(bf16[8,256,128]{2,1,0:T(8,128)(2,1)S(1)} %convert_element_type.3.own), channel_id=1, source_target_pairs={{4,8},{5,9},{6,10},{7,11},{8,4},{9,5},{10,6},{11,7},{20,24},{21,25... | collective-permute-start | bytes 1572872 | tf_op jit(solution)/shard_map/ppermute | solution.py:344
  22.0 12.1 %collective-permute-start.5 = (bf16[6,256,128]{2,1,0:T(8,128)(2,1)S(1)}, bf16[6,256,128]{2,1,0:T(8,128)(2,1)S(1)}, u32[]{:S(2)}, u32[]{:S(2)}) collective-permute-start(bf16[6,256,128]{2,1,0:T(8,128)(2,1)S(1)} %get-tuple-element.104), channel_id=1, source_target_pairs={{0,2},{1,3},{2,0},{3,1},{4,6},{5,7},{6,4},{7,5},{8,10},{9,11},{10,... | collective-permute-start | bytes 1179656 | tf_op jit(solution)/shard_map/ppermute | solution.py:348
  24.0 14.8 %collective-permute-start.6 = (bf16[6,256,128]{2,1,0:T(8,128)(2,1)S(1)}, bf16[6,256,128]{2,1,0:T(8,128)(2,1)S(1)}, u32[]{:S(2)}, u32[]{:S(2)}) collective-permute-start(bf16[6,256,128]{2,1,0:T(8,128)(2,1)S(1)} %get-tuple-element.105), channel_id=1, source_target_pairs={{0,3},{1,2},{2,1},{3,0},{4,7},{5,6},{6,5},{7,4},{8,11},{9,10},{10,... | collective-permute-start | bytes 1179656 | tf_op jit(solution)/shard_map/ppermute | solution.py:348
  44.9 9.5 %collective-permute-start.16 = (bf16[3,256,128]{2,1,0:T(8,128)(2,1)S(1)}, bf16[3,256,128]{2,1,0:T(8,128)(2,1)S(1)}, u32[]{:S(2)}, u32[]{:S(2)}) collective-permute-start(bf16[3,256,128]{2,1,0:T(8,128)(2,1)S(1)} %get-tuple-element.119), channel_id=1, source_target_pairs={{0,3},{1,2},{2,1},{3,0},{4,7},{5,6},{6,5},{7,4},{8,11},{9,10},{10,... | collective-permute-start | bytes 589832 | tf_op jit(solution)/shard_map/ppermute | solution.py:348
  48.9 13.1 %collective-permute-start.12 = (bf16[3,256,128]{2,1,0:T(8,128)(2,1)S(1)}, bf16[3,256,128]{2,1,0:T(8,128)(2,1)S(1)}, u32[]{:S(2)}, u32[]{:S(2)}) collective-permute-start(bf16[3,256,128]{2,1,0:T(8,128)(2,1)S(1)} %get-tuple-element.112), channel_id=1, source_target_pairs={{0,2},{1,3},{2,0},{3,1},{4,6},{5,7},{6,4},{7,5},{8,10},{9,11},{10,... | collective-permute-start | bytes 589832 | tf_op jit(solution)/shard_map/ppermute | solution.py:348
  50.4 12.2 %collective-permute-start.13 = (bf16[3,256,128]{2,1,0:T(8,128)(2,1)S(1)}, bf16[3,256,128]{2,1,0:T(8,128)(2,1)S(1)}, u32[]{:S(2)}, u32[]{:S(2)}) collective-permute-start(bf16[3,256,128]{2,1,0:T(8,128)(2,1)S(1)} %get-tuple-element.113), channel_id=1, source_target_pairs={{0,3},{1,2},{2,1},{3,0},{4,7},{5,6},{6,5},{7,4},{8,11},{9,10},{10,... | collective-permute-start | bytes 589832 | tf_op jit(solution)/shard_map/ppermute | solution.py:348
  64.0 16.3 %collective-permute-start.18 = (bf16[8,256,128]{2,1,0:T(8,128)(2,1)S(1)}, bf16[8,256,128]{2,1,0:T(8,128)(2,1)S(1)}, u32[]{:S(2)}, u32[]{:S(2)}) collective-permute-start(bf16[8,256,128]{2,1,0:T(8,128)(2,1)S(1)} %get-tuple-element.128.own), channel_id=1, source_target_pairs={{0,8},{1,9},{2,10},{3,11},{12,4},{13,5},{14,6},{15,7},{4,0},{5,1},... | collective-permute-start | bytes 1572872 | tf_op jit(solution)/shard_map/ppermute | solution.py:344
  77.7 16.0 %collective-permute-start.24 = (bf16[8,256,128]{2,1,0:T(8,128)(2,1)S(1)}, bf16[8,256,128]{2,1,0:T(8,128)(2,1)S(1)}, u32[]{:S(2)}, u32[]{:S(2)}) collective-permute-start(bf16[8,256,128]{2,1,0:T(8,128)(2,1)S(1)} %get-tuple-element.128.own), channel_id=1, source_target_pairs={{0,4},{1,5},{2,6},{3,7},{12,8},{13,9},{14,10},{15,11},{4,12},{5,13... | collective-permute-start | bytes 1572872 | tf_op jit(solution)/shard_map/ppermute | solution.py:344
  82.4 13.8 %collective-permute-start.17 = (bf16[8,256,128]{2,1,0:T(8,128)(2,1)S(1)}, bf16[8,256,128]{2,1,0:T(8,128)(2,1)S(1)}, u32[]{:S(2)}, u32[]{:S(2)}) collective-permute-start(bf16[8,256,128]{2,1,0:T(8,128)(2,1)S(1)} %get-tuple-element.128.own), channel_id=1, source_target_pairs={{4,8},{5,9},{6,10},{7,11},{8,4},{9,5},{10,6},{11,7},{20,24},{21,25... | collective-permute-start | bytes 1572872 | tf_op jit(solution)/shard_map/ppermute | solution.py:344
  83.1 21.7 %collective-permute-start.21 = (bf16[8,256,128]{2,1,0:T(8,128)(2,1)S(1)}, bf16[8,256,128]{2,1,0:T(8,128)(2,1)S(1)}, u32[]{:S(2)}, u32[]{:S(2)}) collective-permute-start(bf16[8,256,128]{2,1,0:T(8,128)(2,1)S(1)} %collective-permute-done.18.refs_0_.first), channel_id=1, source_target_pairs={{4,0},{5,1},{6,2},{7,3},{8,12},{9,13},{10,14},{11,15},{20,16},{21,... | collective-permute-start | bytes 1572872 | tf_op jit(solution)/shard_map/ppermute | solution.py:344
  94.3 13.2 %collective-permute-start.27 = (bf16[9,256,128]{2,1,0:T(8,128)(2,1)S(1)}, bf16[9,256,128]{2,1,0:T(8,128)(2,1)S(1)}, u32[]{:S(2)}, u32[]{:S(2)}) collective-permute-start(bf16[9,256,128]{2,1,0:T(8,128)(2,1)S(1)} %get-tuple-element.132), channel_id=1, source_target_pairs={{0,1},{1,0},{2,3},{3,2},{4,5},{5,4},{6,7},{7,6},{8,9},{9,8},{10,11... | collective-permute-start | bytes 1769480 | tf_op jit(solution)/shard_map/ppermute | solution.py:348
  94.4 12.7 %collective-permute-start.29 = (bf16[3,256,128]{2,1,0:T(8,128)(2,1)S(1)}, bf16[3,256,128]{2,1,0:T(8,128)(2,1)S(1)}, u32[]{:S(2)}, u32[]{:S(2)}) collective-permute-start(bf16[3,256,128]{2,1,0:T(8,128)(2,1)S(1)} %get-tuple-element.138), channel_id=1, source_target_pairs={{0,2},{1,3},{2,0},{3,1},{4,6},{5,7},{6,4},{7,5},{8,10},{9,11},{10,... | collective-permute-start | bytes 589832 | tf_op jit(solution)/shard_map/ppermute | solution.py:348
  95.9 11.5 %collective-permute-start.30 = (bf16[3,256,128]{2,1,0:T(8,128)(2,1)S(1)}, bf16[3,256,128]{2,1,0:T(8,128)(2,1)S(1)}, u32[]{:S(2)}, u32[]{:S(2)}) collective-permute-start(bf16[3,256,128]{2,1,0:T(8,128)(2,1)S(1)} %get-tuple-element.139), channel_id=1, source_target_pairs={{0,3},{1,2},{2,1},{3,0},{4,7},{5,6},{6,5},{7,4},{8,11},{9,10},{10,... | collective-permute-start | bytes 589832 | tf_op jit(solution)/shard_map/ppermute | solution.py:348
  118.0 14.2 %collective-permute-start.32 = (bf16[8,256,128]{2,1,0:T(8,128)(2,1)S(1)}, bf16[8,256,128]{2,1,0:T(8,128)(2,1)S(1)}, u32[]{:S(2)}, u32[]{:S(2)}) collective-permute-start(bf16[8,256,128]{2,1,0:T(8,128)(2,1)S(1)} %get-tuple-element.150.own), channel_id=1, source_target_pairs={{0,8},{1,9},{2,10},{3,11},{12,4},{13,5},{14,6},{15,7},{4,0},{5,1},... | collective-permute-start | bytes 1572872 | tf_op jit(solution)/shard_map/ppermute | solution.py:344
  129.6 15.8 %collective-permute-start.38 = (bf16[8,256,128]{2,1,0:T(8,128)(2,1)S(1)}, bf16[8,256,128]{2,1,0:T(8,128)(2,1)S(1)}, u32[]{:S(2)}, u32[]{:S(2)}) collective-permute-start(bf16[8,256,128]{2,1,0:T(8,128)(2,1)S(1)} %get-tuple-element.150.own), channel_id=1, source_target_pairs={{0,4},{1,5},{2,6},{3,7},{12,8},{13,9},{14,10},{15,11},{4,12},{5,13... | collective-permute-start | bytes 1572872 | tf_op jit(solution)/shard_map/ppermute | solution.py:344
  134.2 13.7 %collective-permute-start.31 = (bf16[8,256,128]{2,1,0:T(8,128)(2,1)S(1)}, bf16[8,256,128]{2,1,0:T(8,128)(2,1)S(1)}, u32[]{:S(2)}, u32[]{:S(2)}) collective-permute-start(bf16[8,256,128]{2,1,0:T(8,128)(2,1)S(1)} %get-tuple-element.150.own), channel_id=1, source_target_pairs={{4,8},{5,9},{6,10},{7,11},{8,4},{9,5},{10,6},{11,7},{20,24},{21,25... | collective-permute-start | bytes 1572872 | tf_op jit(solution)/shard_map/ppermute | solution.py:344
  134.9 21.6 %collective-permute-start.35 = (bf16[8,256,128]{2,1,0:T(8,128)(2,1)S(1)}, bf16[8,256,128]{2,1,0:T(8,128)(2,1)S(1)}, u32[]{:S(2)}, u32[]{:S(2)}) collective-permute-start(bf16[8,256,128]{2,1,0:T(8,128)(2,1)S(1)} %collective-permute-done.32.refs_0_.first), channel_id=1, source_target_pairs={{4,0},{5,1},{6,2},{7,3},{8,12},{9,13},{10,14},{11,15},{20,16},{21,... | collective-permute-start | bytes 1572872 | tf_op jit(solution)/shard_map/ppermute | solution.py:344
  146.0 13.2 %collective-permute-start.41 = (bf16[9,256,128]{2,1,0:T(8,128)(2,1)S(1)}, bf16[9,256,128]{2,1,0:T(8,128)(2,1)S(1)}, u32[]{:S(2)}, u32[]{:S(2)}) collective-permute-start(bf16[9,256,128]{2,1,0:T(8,128)(2,1)S(1)} %get-tuple-element.154), channel_id=1, source_target_pairs={{0,1},{1,0},{2,3},{3,2},{4,5},{5,4},{6,7},{7,6},{8,9},{9,8},{10,11... | collective-permute-start | bytes 1769480 | tf_op jit(solution)/shard_map/ppermute | solution.py:348
  146.1 12.7 %collective-permute-start.43 = (bf16[3,256,128]{2,1,0:T(8,128)(2,1)S(1)}, bf16[3,256,128]{2,1,0:T(8,128)(2,1)S(1)}, u32[]{:S(2)}, u32[]{:S(2)}) collective-permute-start(bf16[3,256,128]{2,1,0:T(8,128)(2,1)S(1)} %get-tuple-element.160), channel_id=1, source_target_pairs={{0,2},{1,3},{2,0},{3,1},{4,6},{5,7},{6,4},{7,5},{8,10},{9,11},{10,... | collective-permute-start | bytes 589832 | tf_op jit(solution)/shard_map/ppermute | solution.py:348
  147.7 11.5 %collective-permute-start.44 = (bf16[3,256,128]{2,1,0:T(8,128)(2,1)S(1)}, bf16[3,256,128]{2,1,0:T(8,128)(2,1)S(1)}, u32[]{:S(2)}, u32[]{:S(2)}) collective-permute-start(bf16[3,256,128]{2,1,0:T(8,128)(2,1)S(1)} %get-tuple-element.161), channel_id=1, source_target_pairs={{0,3},{1,2},{2,1},{3,0},{4,7},{5,6},{6,5},{7,4},{8,11},{9,10},{10,... | collective-permute-start | bytes 589832 | tf_op jit(solution)/shard_map/ppermute | solution.py:348
  158.9 9.4 %collective-permute-start.37 = (bf16[3,256,128]{2,1,0:T(8,128)(2,1)S(1)}, bf16[3,256,128]{2,1,0:T(8,128)(2,1)S(1)}, u32[]{:S(2)}, u32[]{:S(2)}) collective-permute-start(bf16[3,256,128]{2,1,0:T(8,128)(2,1)S(1)} %get-tuple-element.149), channel_id=1, source_target_pairs={{0,3},{1,2},{2,1},{3,0},{4,7},{5,6},{6,5},{7,4},{8,11},{9,10},{10,... | collective-permute-start | bytes 589832 | tf_op jit(solution)/shard_map/ppermute | solution.py:348
  169.7 14.2 %collective-permute-start.46 = (bf16[8,256,128]{2,1,0:T(8,128)(2,1)S(1)}, bf16[8,256,128]{2,1,0:T(8,128)(2,1)S(1)}, u32[]{:S(2)}, u32[]{:S(2)}) collective-permute-start(bf16[8,256,128]{2,1,0:T(8,128)(2,1)S(1)} %get-tuple-element.172.own), channel_id=1, source_target_pairs={{0,8},{1,9},{2,10},{3,11},{12,4},{13,5},{14,6},{15,7},{4,0},{5,1},... | collective-permute-start | bytes 1572872 | tf_op jit(solution)/shard_map/ppermute | solution.py:344
  180.5 15.8 %collective-permute-start.52 = (bf16[8,256,128]{2,1,0:T(8,128)(2,1)S(1)}, bf16[8,256,128]{2,1,0:T(8,128)(2,1)S(1)}, u32[]{:S(2)}, u32[]{:S(2)}) collective-permute-start(bf16[8,256,128]{2,1,0:T(8,128)(2,1)S(1)} %get-tuple-element.172.own), channel_id=1, source_target_pairs={{0,4},{1,5},{2,6},{3,7},{12,8},{13,9},{14,10},{15,11},{4,12},{5,13... | collective-permute-start | bytes 1572872 | tf_op jit(solution)/shard_map/ppermute | solution.py:344
  186.0 12.8 %collective-permute-start.45 = (bf16[8,256,128]{2,1,0:T(8,128)(2,1)S(1)}, bf16[8,256,128]{2,1,0:T(8,128)(2,1)S(1)}, u32[]{:S(2)}, u32[]{:S(2)}) collective-permute-start(bf16[8,256,128]{2,1,0:T(8,128)(2,1)S(1)} %get-tuple-element.172.own), channel_id=1, source_target_pairs={{4,8},{5,9},{6,10},{7,11},{8,4},{9,5},{10,6},{11,7},{20,24},{21,25... | collective-permute-start | bytes 1572872 | tf_op jit(solution)/shard_map/ppermute | solution.py:344
  186.7 20.7 %collective-permute-start.49 = (bf16[8,256,128]{2,1,0:T(8,128)(2,1)S(1)}, bf16[8,256,128]{2,1,0:T(8,128)(2,1)S(1)}, u32[]{:S(2)}, u32[]{:S(2)}) collective-permute-start(bf16[8,256,128]{2,1,0:T(8,128)(2,1)S(1)} %collective-permute-done.46.refs_0_.first), channel_id=1, source_target_pairs={{4,0},{5,1},{6,2},{7,3},{8,12},{9,13},{10,14},{11,15},{20,16},{21,... | collective-permute-start | bytes 1572872 | tf_op jit(solution)/shard_map/ppermute | solution.py:344
  196.9 13.2 %collective-permute-start.55 = (bf16[9,256,128]{2,1,0:T(8,128)(2,1)S(1)}, bf16[9,256,128]{2,1,0:T(8,128)(2,1)S(1)}, u32[]{:S(2)}, u32[]{:S(2)}) collective-permute-start(bf16[9,256,128]{2,1,0:T(8,128)(2,1)S(1)} %get-tuple-element.176), channel_id=1, source_target_pairs={{0,1},{1,0},{2,3},{3,2},{4,5},{5,4},{6,7},{7,6},{8,9},{9,8},{10,11... | collective-permute-start | bytes 1769480 | tf_op jit(solution)/shard_map/ppermute | solution.py:348
  197.0 12.7 %collective-permute-start.57 = (bf16[3,256,128]{2,1,0:T(8,128)(2,1)S(1)}, bf16[3,256,128]{2,1,0:T(8,128)(2,1)S(1)}, u32[]{:S(2)}, u32[]{:S(2)}) collective-permute-start(bf16[3,256,128]{2,1,0:T(8,128)(2,1)S(1)} %get-tuple-element.182), channel_id=1, source_target_pairs={{0,2},{1,3},{2,0},{3,1},{4,6},{5,7},{6,4},{7,5},{8,10},{9,11},{10,... | collective-permute-start | bytes 589832 | tf_op jit(solution)/shard_map/ppermute | solution.py:348
  198.6 11.5 %collective-permute-start.58 = (bf16[3,256,128]{2,1,0:T(8,128)(2,1)S(1)}, bf16[3,256,128]{2,1,0:T(8,128)(2,1)S(1)}, u32[]{:S(2)}, u32[]{:S(2)}) collective-permute-start(bf16[3,256,128]{2,1,0:T(8,128)(2,1)S(1)} %get-tuple-element.183), channel_id=1, source_target_pairs={{0,3},{1,2},{2,1},{3,0},{4,7},{5,6},{6,5},{7,4},{8,11},{9,10},{10,... | collective-permute-start | bytes 589832 | tf_op jit(solution)/shard_map/ppermute | solution.py:348
  209.8 9.4 %collective-permute-start.51 = (bf16[3,256,128]{2,1,0:T(8,128)(2,1)S(1)}, bf16[3,256,128]{2,1,0:T(8,128)(2,1)S(1)}, u32[]{:S(2)}, u32[]{:S(2)}) collective-permute-start(bf16[3,256,128]{2,1,0:T(8,128)(2,1)S(1)} %get-tuple-element.171), channel_id=1, source_target_pairs={{0,3},{1,2},{2,1},{3,0},{4,7},{5,6},{6,5},{7,4},{8,11},{9,10},{10,... | collective-permute-start | bytes 589832 | tf_op jit(solution)/shard_map/ppermute | solution.py:348
  (34 other events, 286.0 us)

commit v14 on v12

--- a/solution.py
+++ b/solution.py
@@ -205,10 +205,11 @@
             copy_asked(layout, table, j, flip, shard, outs[flip - 2], i * layout.cap)
 
 
-def second_kernel(layout, table, own, first, second, out2, out3, core):
-    other_y_kernel(layout, (2,), table, second, out2, out3)
-    for j, shard in enumerate((own, first, second)):
-        copy_asked(layout, table, j, 1, shard, core, j * layout.cap)
+def second_kernel(layout, js, table, *refs):
+    shards, (out2, out3, core) = refs[:-3], refs[-3:]
+    other_y_kernel(layout, (2,), table, shards[-1], out2, out3)
+    for i, (j, shard) in enumerate(zip(js, shards)):
+        copy_asked(layout, table, j, 1, shard, core, i * layout.cap)
 
 
 def third_kernel(layout, table, mid, out, out2, out3, core):
@@ -251,7 +252,12 @@
     for j, shard in enumerate((own, first, second)):
         base = 4 * cap * j
         take_own(layout, table, base, shard, xbuf, base)
-        copy_part(cap, core, j, xbuf, base + cap)
+        if core.shape[0] == 3 * cap:
+            copy_part(cap, core, j, xbuf, base + cap)
+        elif j == 0:
+            copy_part(cap, refs[-3], 0, xbuf, base + cap)
+        else:
+            copy_part(cap, core, j - 1, xbuf, base + cap)
         ref, part = parts[j]
         copy_part(cap, refs[ref], part, xbuf, base + 2 * cap)
         copy_part(cap, refs[ref + 1], part, xbuf, base + 3 * cap)
@@ -281,7 +287,7 @@
 def late_kernel(layout, last, table, scalars, tiles, got2, got3, field, xpos, ymom, *refs):
     cap = layout.cap
     blocks, _, repl = xpos.shape
-    outs, acc = (refs[:3], refs[3]) if last else (refs[:5], refs[5])
+    outs, acc = (refs[:3], refs[3]) if last else (refs[:6], refs[6])
     xout, yout = outs[:2]
     acc[...] = field[...]
     multiply(layout, table, tiles, [ref[r] for ref in (got2, got3) for r in range(cap)], len(EARLY) * cap, acc)
@@ -310,7 +316,8 @@
         for copy in copies:
             copy.wait()
     else:
-        other_y_kernel(layout, (0,), table, *outs[2:])
+        other_y_kernel(layout, (0,), table, *outs[2:5])
+        copy_asked(layout, table, 0, 1, outs[2], outs[5])
 
 
 def late(layout, last, table, scalars, tiles, sources, field, xpos, ymom):
@@ -324,7 +331,7 @@
         scratch += [pltpu.VMEM(xpos.shape, jnp.float32)] * 2 + [pltpu.SemaphoreType.DMA((2, blocks))]
     else:
         out = jax.ShapeDtypeStruct((layout.cap, tile, repl), jnp.bfloat16)
-        extra = (jax.ShapeDtypeStruct(xpos.shape, jnp.bfloat16), out, out)
+        extra = (jax.ShapeDtypeStruct(xpos.shape, jnp.bfloat16), out, out, out)
     return pl.pallas_call(
         functools.partial(late_kernel, layout, last),
         out_shape=(state, state) + extra,
@@ -378,28 +385,34 @@
     for step in range(STEPS):
         last = step == STEPS - 1
         own1 = along_z(FIRST, own0)
-        mid = along_z(MIDDLE, own0)
         if step == 0:
-            again, notes = lax.optimization_barrier((own0, notes))
+            again, notes[0] = lax.optimization_barrier((own0, notes[0]))
             own2 = along_z(SECOND, again)
+            again, notes = lax.optimization_barrier((again, notes))
+            mid = along_z(MIDDLE, again)
             own1, notes = lax.optimization_barrier((own1, notes))
             out = along_z(OUTWARD, own1)
             table, *packs01 = start(layout, mine, notes, own0, own1)
             got1 = to_other_y(packs01)
             own2, got1, mid, out = lax.optimization_barrier((own2, got1, mid, out))
-            parts = ((0, 0), (0, 1), (2, 0))
+            parts, cores = ((0, 0), (0, 1), (2, 0)), []
             got = got1
         else:
+            core0 = across(1, packs0[2])
+            again, core0 = lax.optimization_barrier((own0, core0))
+            own2 = along_z(SECOND, again)
             got0 = to_other_y(packs0)
-            again, got0 = lax.optimization_barrier((own0, got0))
-            own2 = along_z(SECOND, again)
+            again, got0 = lax.optimization_barrier((again, got0))
             own1, got0 = lax.optimization_barrier((own1, got0))
+            packs1 = other_y((1,), [own1])
             out = along_z(OUTWARD, own1)
-            got1 = to_other_y(other_y((1,), [own1]))
+            got1 = to_other_y(packs1)
+            mid = along_z(MIDDLE, again)
             own2, got1 = lax.optimization_barrier((own2, got1))
-            parts = ((0, 0), (2, 0), (4, 0))
+            parts, cores = ((0, 0), (2, 0), (4, 0)), [core0]
             got = got0 + got1
-        packs2 = pack(functools.partial(second_kernel, layout), [cap, cap, 3 * cap], table, [own0, own1, own2])
+        js, shards = ((0, 1, 2), [own0, own1, own2]) if step == 0 else ((1, 2), [own1, own2])
+        packs2 = pack(functools.partial(second_kernel, layout, js), [cap, cap, len(js) * cap], table, shards)
         got2 = to_other_y(packs2)
         core = across(1, packs2[2])
         if step == 0:
@@ -409,7 +422,7 @@
         packs3 = pack(functools.partial(third_kernel, layout), [cap] * 3, table, [mid, out])
         core3 = across(1, packs3[2])
         got3 = to_other_y(packs3)
-        field = early(layout, parts, table, tiles, [own0, own1, own2, mid, out, core, core3] + got + got2)
+        field = early(layout, parts, table, tiles, [own0, own1, own2, mid, out, core, core3] + got + got2 + cores)
         if step == 0:
             total = (half + across(8, half))[0, SUM_AT]
             coeff = 0.7 * jnp.sqrt((order - 1) / total)

time: 233 us -> 230 us (0.987)
  waiting for transfers between devices: 130 us -> 127 us
    ppermute x16, waiting for transfers between devices: 60.3 us -> 43.7 us  [along_z(): lax.ppermute(value, 'row', [(a * 4 + i, b * 4 + i) for a, b in pairs for...]
    ppermute x43 -> x46, waiting for transfers between devices: 69.8 us -> 83.7 us  [across(): return lax.ppermute(value, 'row', [(i, i ^ flip) for i in range(16)])]
    ppermute x43 -> x46, starting transfers between devices: 31.2 us -> 31.3 us  [across(): return lax.ppermute(value, 'row', [(i, i ^ flip) for i in range(16)])]
  transfers between devices with their start and end apart: 59 -> 62, of which waited for: 34 -> 37; matrix products, arithmetic and copies ran while one was open for 0% -> 0% of each run, Pallas kernels for 11% -> 11%
where the time goes in v14:
time: 230 us; the launch traced here: 229 us
  waiting for transfers between devices  127 us (55%)
  starting transfers between devices  49.6 us (22%)
  Pallas kernels  32.8 us (14%)
  blocking collectives  10.6 us (5%)
  local copies, waits for them, and re-layouts  4.07 us (2%)
  between operations  2.41 us (1%)
    ppermute x46, waiting for transfers between devices, across(): return lax.ppermute(value, 'row', [(i, i ^ flip) for i in range(16)])  83.7 us
    ppermute x16, waiting for transfers between devices, along_z(): lax.ppermute(value, 'row', [(a * 4 + i, b * 4 + i) for a, b in pairs for...  43.7 us
    ppermute x46, starting transfers between devices, across(): return lax.ppermute(value, 'row', [(i, i ^ flip) for i in range(16)])  31.3 us
    ppermute x16, starting transfers between devices, along_z(): lax.ppermute(value, 'row', [(a * 4 + i, b * 4 + i) for a, b in pairs for...  18.3 us
    pallas_call x4, Pallas kernels, early(): pl.pallas_call(functools.partial(early_kernel, layout, parts), out_shape=...  13.8 us
    all_to_all x1, blocking collectives, row_sum(): lax.all_to_all(spread, 'row', split_axis=0, concat_axis=0, tiled=True)  10.6 us
    pallas_call x4, Pallas kernels, late(): pl.pallas_call(functools.partial(late_kernel, layout, last), out_shape=(s...  6.84 us
    pallas_call x11, Pallas kernels, pack(): pl.pallas_call(kernel, out_shape=[jax.ShapeDtypeStruct((size, tile, repl)...  6.59 us
  transfers between devices with their start and end apart: 62, of which 37 were waited for; matrix products, arithmetic and copies ran while one was open for 0% of the time, Pallas kernels for 11%

profile of v14, /device:TPU:0, one launch (start us, length us, event | category | flops | bytes accessed | tf_op | source)
XLA Modules:
  0.0 229.2 jit_solution(1699282920236001154)
XLA Ops:
  1.9 4.1 %collective-permute-start = (bf16[8,256,128]{2,1,0:T(8,128)(2,1)S(1)}, bf16[8,256,128]{2,1,0:T(8,128)(2,1)S(1)}, u32[]{:S(2)}, u32[]{:S(2)}) collective-permute-start(bf16[8,256,128]{2,1,0:T(8,128)(2,1)S(1)} %convert_element_type.3.own.refs_0_), channel_id=1, source_target_pairs={{0,8},{1,9},{2,10},{3,11},{12,4},{13,5},{14,6},{15,7},{4,0},{5,1},... | collective-permute-start | bytes 1572872 | tf_op jit(solution)/shard_map/ppermute | solution.py:351
  6.7 4.2 %shard_map.85 = (s32[144]{0:T(256)}, f32[1,128]{1,0:T(1,128)}) custom-call(s32[48]{0:T(128)} %rows.1, s32[48]{0:T(128)} %cols.1, s32[1]{0:T(128)S(6)} %copy.10.count, bf16[48,256,256]{2,1,0:T(8,128)(2,1)} %tiles.17), custom_call_target="tpu_custom_call" | custom-call | tf_op jit(solution)/shard_map/pallas_call | solution.py:131
  23.4 7.0 %collective-permute-done.4.refs_2_.second = bf16[8,256,128]{2,1,0:T(8,128)(2,1)S(1)} collective-permute-done((bf16[8,256,128]{2,1,0:T(8,128)(2,1)S(1)}, bf16[8,256,128]{2,1,0:T(8,128)(2,1)S(1)}, u32[]{:S(2)}, u32[]{:S(2)}) %collective-permute-start.4) | collective-permute-done | bytes 524320 | tf_op jit(solution)/shard_map/ppermute | solution.py:351
  30.4 3.6 %collective-permute-done.5.refs_0_ = bf16[6,256,128]{2,1,0:T(8,128)(2,1)S(1)} collective-permute-done((bf16[6,256,128]{2,1,0:T(8,128)(2,1)S(1)}, bf16[6,256,128]{2,1,0:T(8,128)(2,1)S(1)}, u32[]{:S(2)}, u32[]{:S(2)}) %collective-permute-start.5) | collective-permute-done | bytes 393248 | tf_op jit(solution)/shard_map/ppermute | solution.py:355
  33.9 4.3 %collective-permute-done.6.refs_1_ = bf16[6,256,128]{2,1,0:T(8,128)(2,1)S(1)} collective-permute-done((bf16[6,256,128]{2,1,0:T(8,128)(2,1)S(1)}, bf16[6,256,128]{2,1,0:T(8,128)(2,1)S(1)}, u32[]{:S(2)}, u32[]{:S(2)}) %collective-permute-start.6) | collective-permute-done | bytes 393248 | tf_op jit(solution)/shard_map/ppermute | solution.py:355
  38.2 3.3 %collective-permute-done.8.out = bf16[8,256,128]{2,1,0:T(8,128)(2,1)S(1)} collective-permute-done((bf16[8,256,128]{2,1,0:T(8,128)(2,1)S(1)}, bf16[8,256,128]{2,1,0:T(8,128)(2,1)S(1)}, u32[]{:S(2)}, u32[]{:S(2)}) %collective-permute-start.8) | collective-permute-done | bytes 524320 | tf_op jit(solution)/shard_map/ppermute | solution.py:351
  51.1 3.3 %collective-permute-done.16.refs_3_ = bf16[3,256,128]{2,1,0:T(8,128)(2,1)S(1)} collective-permute-done((bf16[3,256,128]{2,1,0:T(8,128)(2,1)S(1)}, bf16[3,256,128]{2,1,0:T(8,128)(2,1)S(1)}, u32[]{:S(2)}, u32[]{:S(2)}) %collective-permute-start.16) | collective-permute-done | bytes 196640 | tf_op jit(solution)/shard_map/ppermute | solution.py:355
  54.4 2.8 %copy-done = bf16[48,256,256]{2,1,0:T(8,128)(2,1)S(1)} copy-done((bf16[48,256,256]{2,1,0:T(8,128)(2,1)S(1)}, bf16[48,256,256]{2,1,0:T(8,128)(2,1)}, u32[]{:S(2)}) %copy-start) | copy-done | bytes 6291480
  57.2 3.4 %shard_map.89.field = f32[9,256,128]{2,1,0:T(8,128)S(1)} custom-call(s32[180]{0:T(256)S(1)} %get-tuple-element.120.table, bf16[48,256,256]{2,1,0:T(8,128)(2,1)S(1)} %copy-done, bf16[8,256,128]{2,1,0:T(8,128)(2,1)S(1)} %convert_element_type.3.own.refs_0_, bf16[8,256,128]{2,1,0:T(8,128)(2,1)S(1)} %collective-permute-done.first.refs_1_, ...), custom_call_target="tpu_custom_call" | custom-call | tf_op jit(solution)/shard_map/pallas_call | solution.py:276
  67.6 5.9 %collective-permute-done.18.refs_0_ = bf16[3,256,128]{2,1,0:T(8,128)(2,1)S(1)} collective-permute-done((bf16[3,256,128]{2,1,0:T(8,128)(2,1)S(1)}, bf16[3,256,128]{2,1,0:T(8,128)(2,1)S(1)}, u32[]{:S(2)}, u32[]{:S(2)}) %collective-permute-start.18) | collective-permute-done | bytes 196640 | tf_op jit(solution)/shard_map/ppermute | solution.py:355
  73.5 3.1 %collective-permute-done.19.refs_1_ = bf16[3,256,128]{2,1,0:T(8,128)(2,1)S(1)} collective-permute-done((bf16[3,256,128]{2,1,0:T(8,128)(2,1)S(1)}, bf16[3,256,128]{2,1,0:T(8,128)(2,1)S(1)}, u32[]{:S(2)}, u32[]{:S(2)}) %collective-permute-start.19) | collective-permute-done | bytes 196640 | tf_op jit(solution)/shard_map/ppermute | solution.py:355
  81.7 6.3 %collective-permute-done.26.refs_2_ = bf16[3,256,128]{2,1,0:T(8,128)(2,1)S(1)} collective-permute-done((bf16[3,256,128]{2,1,0:T(8,128)(2,1)S(1)}, bf16[3,256,128]{2,1,0:T(8,128)(2,1)S(1)}, u32[]{:S(2)}, u32[]{:S(2)}) %collective-permute-start.26) | collective-permute-done | bytes 196640 | tf_op jit(solution)/shard_map/ppermute | solution.py:355
  93.5 8.6 %collective-permute-done.22.out = bf16[8,256,128]{2,1,0:T(8,128)(2,1)S(1)} collective-permute-done((bf16[8,256,128]{2,1,0:T(8,128)(2,1)S(1)}, bf16[8,256,128]{2,1,0:T(8,128)(2,1)S(1)}, u32[]{:S(2)}, u32[]{:S(2)}) %collective-permute-start.22) | collective-permute-done | bytes 524320 | tf_op jit(solution)/shard_map/ppermute | solution.py:351
  104.7 3.5 %shard_map.94.field = f32[9,256,128]{2,1,0:T(8,128)S(1)} custom-call(s32[180]{0:T(256)S(1)} %get-tuple-element.120.table, bf16[48,256,256]{2,1,0:T(8,128)(2,1)S(1)} %bitcast.8, bf16[8,256,128]{2,1,0:T(8,128)(2,1)S(1)} %get-tuple-element.142.own, bf16[8,256,128]{2,1,0:T(8,128)(2,1)S(1)} %collective-permute-done.21.refs_0_.first, ...), custom_call_target="tpu_custom_call" | custom-call | tf_op jit(solution)/shard_map/pallas_call | solution.py:276
  108.2 2.3 %collective-permute-done.23.got2 = bf16[3,256,128]{2,1,0:T(8,128)(2,1)S(1)} collective-permute-done((bf16[3,256,128]{2,1,0:T(8,128)(2,1)S(1)}, bf16[3,256,128]{2,1,0:T(8,128)(2,1)S(1)}, u32[]{:S(2)}, u32[]{:S(2)}) %collective-permute-start.23) | collective-permute-done | bytes 196640 | tf_op jit(solution)/shard_map/ppermute | solution.py:355
  110.5 3.3 %collective-permute-done.24.got3 = bf16[3,256,128]{2,1,0:T(8,128)(2,1)S(1)} collective-permute-done((bf16[3,256,128]{2,1,0:T(8,128)(2,1)S(1)}, bf16[3,256,128]{2,1,0:T(8,128)(2,1)S(1)}, u32[]{:S(2)}, u32[]{:S(2)}) %collective-permute-start.24) | collective-permute-done | bytes 196640 | tf_op jit(solution)/shard_map/ppermute | solution.py:355
  119.2 5.1 %collective-permute-done.33.refs_0_ = bf16[3,256,128]{2,1,0:T(8,128)(2,1)S(1)} collective-permute-done((bf16[3,256,128]{2,1,0:T(8,128)(2,1)S(1)}, bf16[3,256,128]{2,1,0:T(8,128)(2,1)S(1)}, u32[]{:S(2)}, u32[]{:S(2)}) %collective-permute-start.33) | collective-permute-done | bytes 196640 | tf_op jit(solution)/shard_map/ppermute | solution.py:355
  124.2 3.4 %collective-permute-done.34.refs_1_ = bf16[3,256,128]{2,1,0:T(8,128)(2,1)S(1)} collective-permute-done((bf16[3,256,128]{2,1,0:T(8,128)(2,1)S(1)}, bf16[3,256,128]{2,1,0:T(8,128)(2,1)S(1)}, u32[]{:S(2)}, u32[]{:S(2)}) %collective-permute-start.34) | collective-permute-done | bytes 196640 | tf_op jit(solution)/shard_map/ppermute | solution.py:355
  132.5 6.8 %collective-permute-done.41.refs_2_ = bf16[3,256,128]{2,1,0:T(8,128)(2,1)S(1)} collective-permute-done((bf16[3,256,128]{2,1,0:T(8,128)(2,1)S(1)}, bf16[3,256,128]{2,1,0:T(8,128)(2,1)S(1)}, u32[]{:S(2)}, u32[]{:S(2)}) %collective-permute-start.41) | collective-permute-done | bytes 196640 | tf_op jit(solution)/shard_map/ppermute | solution.py:355
  144.2 8.6 %collective-permute-done.37.out = bf16[8,256,128]{2,1,0:T(8,128)(2,1)S(1)} collective-permute-done((bf16[8,256,128]{2,1,0:T(8,128)(2,1)S(1)}, bf16[8,256,128]{2,1,0:T(8,128)(2,1)S(1)}, u32[]{:S(2)}, u32[]{:S(2)}) %collective-permute-start.37) | collective-permute-done | bytes 524320 | tf_op jit(solution)/shard_map/ppermute | solution.py:351
  155.5 3.5 %shard_map.99.field = f32[9,256,128]{2,1,0:T(8,128)S(1)} custom-call(s32[180]{0:T(256)S(1)} %get-tuple-element.120.table, bf16[48,256,256]{2,1,0:T(8,128)(2,1)S(1)} %bitcast.8, bf16[8,256,128]{2,1,0:T(8,128)(2,1)S(1)} %get-tuple-element.167.own, bf16[8,256,128]{2,1,0:T(8,128)(2,1)S(1)} %collective-permute-done.36.refs_0_.first, ...), custom_call_target="tpu_custom_call" | custom-call | tf_op jit(solution)/shard_map/pallas_call | solution.py:276
  158.9 2.3 %collective-permute-done.38.got2 = bf16[3,256,128]{2,1,0:T(8,128)(2,1)S(1)} collective-permute-done((bf16[3,256,128]{2,1,0:T(8,128)(2,1)S(1)}, bf16[3,256,128]{2,1,0:T(8,128)(2,1)S(1)}, u32[]{:S(2)}, u32[]{:S(2)}) %collective-permute-start.38) | collective-permute-done | bytes 196640 | tf_op jit(solution)/shard_map/ppermute | solution.py:355
  161.3 3.3 %collective-permute-done.39.got3 = bf16[3,256,128]{2,1,0:T(8,128)(2,1)S(1)} collective-permute-done((bf16[3,256,128]{2,1,0:T(8,128)(2,1)S(1)}, bf16[3,256,128]{2,1,0:T(8,128)(2,1)S(1)}, u32[]{:S(2)}, u32[]{:S(2)}) %collective-permute-start.39) | collective-permute-done | bytes 196640 | tf_op jit(solution)/shard_map/ppermute | solution.py:355
  169.9 5.1 %collective-permute-done.48.refs_0_ = bf16[3,256,128]{2,1,0:T(8,128)(2,1)S(1)} collective-permute-done((bf16[3,256,128]{2,1,0:T(8,128)(2,1)S(1)}, bf16[3,256,128]{2,1,0:T(8,128)(2,1)S(1)}, u32[]{:S(2)}, u32[]{:S(2)}) %collective-permute-start.48) | collective-permute-done | bytes 196640 | tf_op jit(solution)/shard_map/ppermute | solution.py:355
  175.0 3.4 %collective-permute-done.49.refs_1_ = bf16[3,256,128]{2,1,0:T(8,128)(2,1)S(1)} collective-permute-done((bf16[3,256,128]{2,1,0:T(8,128)(2,1)S(1)}, bf16[3,256,128]{2,1,0:T(8,128)(2,1)S(1)}, u32[]{:S(2)}, u32[]{:S(2)}) %collective-permute-start.49) | collective-permute-done | bytes 196640 | tf_op jit(solution)/shard_map/ppermute | solution.py:355
  183.2 6.8 %collective-permute-done.56.refs_2_ = bf16[3,256,128]{2,1,0:T(8,128)(2,1)S(1)} collective-permute-done((bf16[3,256,128]{2,1,0:T(8,128)(2,1)S(1)}, bf16[3,256,128]{2,1,0:T(8,128)(2,1)S(1)}, u32[]{:S(2)}, u32[]{:S(2)}) %collective-permute-start.56) | collective-permute-done | bytes 196640 | tf_op jit(solution)/shard_map/ppermute | solution.py:355
  195.0 8.6 %collective-permute-done.52.out = bf16[8,256,128]{2,1,0:T(8,128)(2,1)S(1)} collective-permute-done((bf16[8,256,128]{2,1,0:T(8,128)(2,1)S(1)}, bf16[8,256,128]{2,1,0:T(8,128)(2,1)S(1)}, u32[]{:S(2)}, u32[]{:S(2)}) %collective-permute-start.52) | collective-permute-done | bytes 524320 | tf_op jit(solution)/shard_map/ppermute | solution.py:351
  206.2 3.5 %shard_map.104.field = f32[9,256,128]{2,1,0:T(8,128)S(1)} custom-call(s32[180]{0:T(256)S(1)} %get-tuple-element.120.table, bf16[48,256,256]{2,1,0:T(8,128)(2,1)S(1)} %bitcast.8, bf16[8,256,128]{2,1,0:T(8,128)(2,1)S(1)} %get-tuple-element.192.own, bf16[8,256,128]{2,1,0:T(8,128)(2,1)S(1)} %collective-permute-done.51.refs_0_.first, ...), custom_call_target="tpu_custom_call" | custom-call | tf_op jit(solution)/shard_map/pallas_call | solution.py:276
  209.7 2.3 %collective-permute-done.53.got2 = bf16[3,256,128]{2,1,0:T(8,128)(2,1)S(1)} collective-permute-done((bf16[3,256,128]{2,1,0:T(8,128)(2,1)S(1)}, bf16[3,256,128]{2,1,0:T(8,128)(2,1)S(1)}, u32[]{:S(2)}, u32[]{:S(2)}) %collective-permute-start.53) | collective-permute-done | bytes 196640 | tf_op jit(solution)/shard_map/ppermute | solution.py:355
  212.0 3.3 %collective-permute-done.54.got3 = bf16[3,256,128]{2,1,0:T(8,128)(2,1)S(1)} collective-permute-done((bf16[3,256,128]{2,1,0:T(8,128)(2,1)S(1)}, bf16[3,256,128]{2,1,0:T(8,128)(2,1)S(1)}, u32[]{:S(2)}, u32[]{:S(2)}) %collective-permute-start.54) | collective-permute-done | bytes 196640 | tf_op jit(solution)/shard_map/ppermute | solution.py:355
  215.3 2.6 %shard_map.105 = (f32[8,256,128]{2,1,0:T(8,128)}, f32[8,256,128]{2,1,0:T(8,128)}, f32[1,128]{1,0:T(1,128)S(1)}) custom-call(s32[180]{0:T(256)S(1)} %get-tuple-element.120.table, f32[2]{0:T(128)S(1)} %pad_maximum_fusion.scalars, bf16[48,256,256]{2,1,0:T(8,128)(2,1)S(1)} %bitcast.8, bf16[3,256,128]{2,1,0:T(8,128)(2,1)S(1)} %collective-permute-done.53.got2, ...), custom_call_target="tpu_custom_call" | custom-call | flops 100663296 | bytes 6422528 | tf_op jit(solution)/shard_map/pallas_call | solution.py:335
  218.0 10.6 %all_to_all.6 = f32[16,1,128]{2,1,0:T(1,128)S(1)} all-to-all(f32[16,1,128]{2,1,0:T(1,128)S(1)} %broadcast_in_dim.2), channel_id=1, replica_groups=mesh['groups'=2,'row'=16] {'row'}, dimensions={0} | all-to-all | bytes 16384 | tf_op jit(solution)/shard_map/all_to_all | solution.py:361
  (140 shorter events, 78.7 us)
Async XLA Ops:
  1.9 16.5 %collective-permute-start = (bf16[8,256,128]{2,1,0:T(8,128)(2,1)S(1)}, bf16[8,256,128]{2,1,0:T(8,128)(2,1)S(1)}, u32[]{:S(2)}, u32[]{:S(2)}) collective-permute-start(bf16[8,256,128]{2,1,0:T(8,128)(2,1)S(1)} %convert_element_type.3.own.refs_0_), channel_id=1, source_target_pairs={{0,8},{1,9},{2,10},{3,11},{12,4},{13,5},{14,6},{15,7},{4,0},{5,1},... | collective-permute-start | bytes 1572872 | tf_op jit(solution)/shard_map/ppermute | solution.py:351
  12.8 17.6 %collective-permute-start.4 = (bf16[8,256,128]{2,1,0:T(8,128)(2,1)S(1)}, bf16[8,256,128]{2,1,0:T(8,128)(2,1)S(1)}, u32[]{:S(2)}, u32[]{:S(2)}) collective-permute-start(bf16[8,256,128]{2,1,0:T(8,128)(2,1)S(1)} %convert_element_type.3.own.refs_0_), channel_id=1, source_target_pairs={{0,4},{1,5},{2,6},{3,7},{12,8},{13,9},{14,10},{15,11},{4,12},{5,13... | collective-permute-start | bytes 1572872 | tf_op jit(solution)/shard_map/ppermute | solution.py:351
  18.4 23.1 %collective-permute-start.8 = (bf16[8,256,128]{2,1,0:T(8,128)(2,1)S(1)}, bf16[8,256,128]{2,1,0:T(8,128)(2,1)S(1)}, u32[]{:S(2)}, u32[]{:S(2)}) collective-permute-start(bf16[8,256,128]{2,1,0:T(8,128)(2,1)S(1)} %collective-permute-done.first.refs_1_), channel_id=1, source_target_pairs={{4,0},{5,1},{6,2},{7,3},{8,12},{9,13},{10,14},{11,15},{20,16},{21,... | collective-permute-start | bytes 1572872 | tf_op jit(solution)/shard_map/ppermute | solution.py:351
  21.8 12.1 %collective-permute-start.5 = (bf16[6,256,128]{2,1,0:T(8,128)(2,1)S(1)}, bf16[6,256,128]{2,1,0:T(8,128)(2,1)S(1)}, u32[]{:S(2)}, u32[]{:S(2)}) collective-permute-start(bf16[6,256,128]{2,1,0:T(8,128)(2,1)S(1)} %get-tuple-element.121), channel_id=1, source_target_pairs={{0,2},{1,3},{2,0},{3,1},{4,6},{5,7},{6,4},{7,5},{8,10},{9,11},{10,... | collective-permute-start | bytes 1179656 | tf_op jit(solution)/shard_map/ppermute | solution.py:355
  23.4 14.8 %collective-permute-start.6 = (bf16[6,256,128]{2,1,0:T(8,128)(2,1)S(1)}, bf16[6,256,128]{2,1,0:T(8,128)(2,1)S(1)}, u32[]{:S(2)}, u32[]{:S(2)}) collective-permute-start(bf16[6,256,128]{2,1,0:T(8,128)(2,1)S(1)} %get-tuple-element.122), channel_id=1, source_target_pairs={{0,3},{1,2},{2,1},{3,0},{4,7},{5,6},{6,5},{7,4},{8,11},{9,10},{10,... | collective-permute-start | bytes 1179656 | tf_op jit(solution)/shard_map/ppermute | solution.py:355
  46.1 15.9 %collective-permute-start.12 = (bf16[3,256,128]{2,1,0:T(8,128)(2,1)S(1)}, bf16[3,256,128]{2,1,0:T(8,128)(2,1)S(1)}, u32[]{:S(2)}, u32[]{:S(2)}) collective-permute-start(bf16[3,256,128]{2,1,0:T(8,128)(2,1)S(1)} %get-tuple-element.129), channel_id=1, source_target_pairs={{0,2},{1,3},{2,0},{3,1},{4,6},{5,7},{6,4},{7,5},{8,10},{9,11},{10,... | collective-permute-start | bytes 589832 | tf_op jit(solution)/shard_map/ppermute | solution.py:355
  48.5 13.5 %collective-permute-start.13 = (bf16[3,256,128]{2,1,0:T(8,128)(2,1)S(1)}, bf16[3,256,128]{2,1,0:T(8,128)(2,1)S(1)}, u32[]{:S(2)}, u32[]{:S(2)}) collective-permute-start(bf16[3,256,128]{2,1,0:T(8,128)(2,1)S(1)} %get-tuple-element.130), channel_id=1, source_target_pairs={{0,3},{1,2},{2,1},{3,0},{4,7},{5,6},{6,5},{7,4},{8,11},{9,10},{10,... | collective-permute-start | bytes 589832 | tf_op jit(solution)/shard_map/ppermute | solution.py:355
  49.4 11.2 %collective-permute-start.11 = (f32[1,128]{1,0:T(1,128)S(1)}, f32[1,128]{1,0:T(1,128)S(1)}, u32[]{:S(2)}, u32[]{:S(2)}) collective-permute-start(f32[1,128]{1,0:T(1,128)S(1)} %add.18), channel_id=1, source_target_pairs={{0,8},{1,9},{2,10},{3,11},{4,12},{5,13},{6,14},{7,15},{8,0},{9,1},... | collective-permute-start | bytes 1544 | tf_op jit(solution)/shard_map/ppermute | solution.py:355
  63.4 14.8 %collective-permute-start.21 = (bf16[8,256,128]{2,1,0:T(8,128)(2,1)S(1)}, bf16[8,256,128]{2,1,0:T(8,128)(2,1)S(1)}, u32[]{:S(2)}, u32[]{:S(2)}) collective-permute-start(bf16[8,256,128]{2,1,0:T(8,128)(2,1)S(1)} %get-tuple-element.142.own), channel_id=1, source_target_pairs={{0,8},{1,9},{2,10},{3,11},{12,4},{13,5},{14,6},{15,7},{4,0},{5,1},... | collective-permute-start | bytes 1572872 | tf_op jit(solution)/shard_map/ppermute | solution.py:351
  67.5 23.5 %collective-permute-start.25 = (bf16[8,256,128]{2,1,0:T(8,128)(2,1)S(1)}, bf16[8,256,128]{2,1,0:T(8,128)(2,1)S(1)}, u32[]{:S(2)}, u32[]{:S(2)}) collective-permute-start(bf16[8,256,128]{2,1,0:T(8,128)(2,1)S(1)} %get-tuple-element.142.own), channel_id=1, source_target_pairs={{0,4},{1,5},{2,6},{3,7},{12,8},{13,9},{14,10},{15,11},{4,12},{5,13... | collective-permute-start | bytes 1572872 | tf_op jit(solution)/shard_map/ppermute | solution.py:351
  76.6 16.9 %collective-permute-start.20 = (bf16[8,256,128]{2,1,0:T(8,128)(2,1)S(1)}, bf16[8,256,128]{2,1,0:T(8,128)(2,1)S(1)}, u32[]{:S(2)}, u32[]{:S(2)}) collective-permute-start(bf16[8,256,128]{2,1,0:T(8,128)(2,1)S(1)} %get-tuple-element.142.own), channel_id=1, source_target_pairs={{4,8},{5,9},{6,10},{7,11},{8,4},{9,5},{10,6},{11,7},{20,24},{21,25... | collective-permute-start | bytes 1572872 | tf_op jit(solution)/shard_map/ppermute | solution.py:351
  78.2 23.8 %collective-permute-start.22 = (bf16[8,256,128]{2,1,0:T(8,128)(2,1)S(1)}, bf16[8,256,128]{2,1,0:T(8,128)(2,1)S(1)}, u32[]{:S(2)}, u32[]{:S(2)}) collective-permute-start(bf16[8,256,128]{2,1,0:T(8,128)(2,1)S(1)} %collective-permute-done.21.refs_0_.first), channel_id=1, source_target_pairs={{4,0},{5,1},{6,2},{7,3},{8,12},{9,13},{10,14},{11,15},{20,16},{21,... | collective-permute-start | bytes 1572872 | tf_op jit(solution)/shard_map/ppermute | solution.py:351
  91.5 13.2 %collective-permute-start.28 = (bf16[6,256,128]{2,1,0:T(8,128)(2,1)S(1)}, bf16[6,256,128]{2,1,0:T(8,128)(2,1)S(1)}, u32[]{:S(2)}, u32[]{:S(2)}) collective-permute-start(bf16[6,256,128]{2,1,0:T(8,128)(2,1)S(1)} %get-tuple-element.151), channel_id=1, source_target_pairs={{0,1},{1,0},{2,3},{3,2},{4,5},{5,4},{6,7},{7,6},{8,9},{9,8},{10,11... | collective-permute-start | bytes 1179656 | tf_op jit(solution)/shard_map/ppermute | solution.py:355
  91.9 11.9 %collective-permute-start.30 = (bf16[3,256,128]{2,1,0:T(8,128)(2,1)S(1)}, bf16[3,256,128]{2,1,0:T(8,128)(2,1)S(1)}, u32[]{:S(2)}, u32[]{:S(2)}) collective-permute-start(bf16[3,256,128]{2,1,0:T(8,128)(2,1)S(1)} %get-tuple-element.157), channel_id=1, source_target_pairs={{0,2},{1,3},{2,0},{3,1},{4,6},{5,7},{6,4},{7,5},{8,10},{9,11},{10,... | collective-permute-start | bytes 589832 | tf_op jit(solution)/shard_map/ppermute | solution.py:355
  93.4 11.3 %collective-permute-start.31 = (bf16[3,256,128]{2,1,0:T(8,128)(2,1)S(1)}, bf16[3,256,128]{2,1,0:T(8,128)(2,1)S(1)}, u32[]{:S(2)}, u32[]{:S(2)}) collective-permute-start(bf16[3,256,128]{2,1,0:T(8,128)(2,1)S(1)} %get-tuple-element.158), channel_id=1, source_target_pairs={{0,3},{1,2},{2,1},{3,0},{4,7},{5,6},{6,5},{7,4},{8,11},{9,10},{10,... | collective-permute-start | bytes 589832 | tf_op jit(solution)/shard_map/ppermute | solution.py:355
  103.8 10.0 %collective-permute-start.24 = (bf16[3,256,128]{2,1,0:T(8,128)(2,1)S(1)}, bf16[3,256,128]{2,1,0:T(8,128)(2,1)S(1)}, u32[]{:S(2)}, u32[]{:S(2)}) collective-permute-start(bf16[3,256,128]{2,1,0:T(8,128)(2,1)S(1)} %get-tuple-element.147), channel_id=1, source_target_pairs={{0,3},{1,2},{2,1},{3,0},{4,7},{5,6},{6,5},{7,4},{8,11},{9,10},{10,... | collective-permute-start | bytes 589832 | tf_op jit(solution)/shard_map/ppermute | solution.py:355
  115.2 14.3 %collective-permute-start.36 = (bf16[8,256,128]{2,1,0:T(8,128)(2,1)S(1)}, bf16[8,256,128]{2,1,0:T(8,128)(2,1)S(1)}, u32[]{:S(2)}, u32[]{:S(2)}) collective-permute-start(bf16[8,256,128]{2,1,0:T(8,128)(2,1)S(1)} %get-tuple-element.167.own), channel_id=1, source_target_pairs={{0,8},{1,9},{2,10},{3,11},{12,4},{13,5},{14,6},{15,7},{4,0},{5,1},... | collective-permute-start | bytes 1572872 | tf_op jit(solution)/shard_map/ppermute | solution.py:351
  118.4 23.3 %collective-permute-start.40 = (bf16[8,256,128]{2,1,0:T(8,128)(2,1)S(1)}, bf16[8,256,128]{2,1,0:T(8,128)(2,1)S(1)}, u32[]{:S(2)}, u32[]{:S(2)}) collective-permute-start(bf16[8,256,128]{2,1,0:T(8,128)(2,1)S(1)} %get-tuple-element.167.own), channel_id=1, source_target_pairs={{0,4},{1,5},{2,6},{3,7},{12,8},{13,9},{14,10},{15,11},{4,12},{5,13... | collective-permute-start | bytes 1572872 | tf_op jit(solution)/shard_map/ppermute | solution.py:351
  127.7 16.5 %collective-permute-start.35 = (bf16[8,256,128]{2,1,0:T(8,128)(2,1)S(1)}, bf16[8,256,128]{2,1,0:T(8,128)(2,1)S(1)}, u32[]{:S(2)}, u32[]{:S(2)}) collective-permute-start(bf16[8,256,128]{2,1,0:T(8,128)(2,1)S(1)} %get-tuple-element.167.own), channel_id=1, source_target_pairs={{4,8},{5,9},{6,10},{7,11},{8,4},{9,5},{10,6},{11,7},{20,24},{21,25... | collective-permute-start | bytes 1572872 | tf_op jit(solution)/shard_map/ppermute | solution.py:351
  129.5 23.3 %collective-permute-start.37 = (bf16[8,256,128]{2,1,0:T(8,128)(2,1)S(1)}, bf16[8,256,128]{2,1,0:T(8,128)(2,1)S(1)}, u32[]{:S(2)}, u32[]{:S(2)}) collective-permute-start(bf16[8,256,128]{2,1,0:T(8,128)(2,1)S(1)} %collective-permute-done.36.refs_0_.first), channel_id=1, source_target_pairs={{4,0},{5,1},{6,2},{7,3},{8,12},{9,13},{10,14},{11,15},{20,16},{21,... | collective-permute-start | bytes 1572872 | tf_op jit(solution)/shard_map/ppermute | solution.py:351
  142.3 13.2 %collective-permute-start.43 = (bf16[6,256,128]{2,1,0:T(8,128)(2,1)S(1)}, bf16[6,256,128]{2,1,0:T(8,128)(2,1)S(1)}, u32[]{:S(2)}, u32[]{:S(2)}) collective-permute-start(bf16[6,256,128]{2,1,0:T(8,128)(2,1)S(1)} %get-tuple-element.176), channel_id=1, source_target_pairs={{0,1},{1,0},{2,3},{3,2},{4,5},{5,4},{6,7},{7,6},{8,9},{9,8},{10,11... | collective-permute-start | bytes 1179656 | tf_op jit(solution)/shard_map/ppermute | solution.py:355
  142.7 11.9 %collective-permute-start.45 = (bf16[3,256,128]{2,1,0:T(8,128)(2,1)S(1)}, bf16[3,256,128]{2,1,0:T(8,128)(2,1)S(1)}, u32[]{:S(2)}, u32[]{:S(2)}) collective-permute-start(bf16[3,256,128]{2,1,0:T(8,128)(2,1)S(1)} %get-tuple-element.182), channel_id=1, source_target_pairs={{0,2},{1,3},{2,0},{3,1},{4,6},{5,7},{6,4},{7,5},{8,10},{9,11},{10,... | collective-permute-start | bytes 589832 | tf_op jit(solution)/shard_map/ppermute | solution.py:355
  144.1 11.3 %collective-permute-start.46 = (bf16[3,256,128]{2,1,0:T(8,128)(2,1)S(1)}, bf16[3,256,128]{2,1,0:T(8,128)(2,1)S(1)}, u32[]{:S(2)}, u32[]{:S(2)}) collective-permute-start(bf16[3,256,128]{2,1,0:T(8,128)(2,1)S(1)} %get-tuple-element.183), channel_id=1, source_target_pairs={{0,3},{1,2},{2,1},{3,0},{4,7},{5,6},{6,5},{7,4},{8,11},{9,10},{10,... | collective-permute-start | bytes 589832 | tf_op jit(solution)/shard_map/ppermute | solution.py:355
  154.6 10.0 %collective-permute-start.39 = (bf16[3,256,128]{2,1,0:T(8,128)(2,1)S(1)}, bf16[3,256,128]{2,1,0:T(8,128)(2,1)S(1)}, u32[]{:S(2)}, u32[]{:S(2)}) collective-permute-start(bf16[3,256,128]{2,1,0:T(8,128)(2,1)S(1)} %get-tuple-element.172), channel_id=1, source_target_pairs={{0,3},{1,2},{2,1},{3,0},{4,7},{5,6},{6,5},{7,4},{8,11},{9,10},{10,... | collective-permute-start | bytes 589832 | tf_op jit(solution)/shard_map/ppermute | solution.py:355
  166.0 14.3 %collective-permute-start.51 = (bf16[8,256,128]{2,1,0:T(8,128)(2,1)S(1)}, bf16[8,256,128]{2,1,0:T(8,128)(2,1)S(1)}, u32[]{:S(2)}, u32[]{:S(2)}) collective-permute-start(bf16[8,256,128]{2,1,0:T(8,128)(2,1)S(1)} %get-tuple-element.192.own), channel_id=1, source_target_pairs={{0,8},{1,9},{2,10},{3,11},{12,4},{13,5},{14,6},{15,7},{4,0},{5,1},... | collective-permute-start | bytes 1572872 | tf_op jit(solution)/shard_map/ppermute | solution.py:351
  169.1 23.3 %collective-permute-start.55 = (bf16[8,256,128]{2,1,0:T(8,128)(2,1)S(1)}, bf16[8,256,128]{2,1,0:T(8,128)(2,1)S(1)}, u32[]{:S(2)}, u32[]{:S(2)}) collective-permute-start(bf16[8,256,128]{2,1,0:T(8,128)(2,1)S(1)} %get-tuple-element.192.own), channel_id=1, source_target_pairs={{0,4},{1,5},{2,6},{3,7},{12,8},{13,9},{14,10},{15,11},{4,12},{5,13... | collective-permute-start | bytes 1572872 | tf_op jit(solution)/shard_map/ppermute | solution.py:351
  178.4 16.6 %collective-permute-start.50 = (bf16[8,256,128]{2,1,0:T(8,128)(2,1)S(1)}, bf16[8,256,128]{2,1,0:T(8,128)(2,1)S(1)}, u32[]{:S(2)}, u32[]{:S(2)}) collective-permute-start(bf16[8,256,128]{2,1,0:T(8,128)(2,1)S(1)} %get-tuple-element.192.own), channel_id=1, source_target_pairs={{4,8},{5,9},{6,10},{7,11},{8,4},{9,5},{10,6},{11,7},{20,24},{21,25... | collective-permute-start | bytes 1572872 | tf_op jit(solution)/shard_map/ppermute | solution.py:351
  180.2 23.3 %collective-permute-start.52 = (bf16[8,256,128]{2,1,0:T(8,128)(2,1)S(1)}, bf16[8,256,128]{2,1,0:T(8,128)(2,1)S(1)}, u32[]{:S(2)}, u32[]{:S(2)}) collective-permute-start(bf16[8,256,128]{2,1,0:T(8,128)(2,1)S(1)} %collective-permute-done.51.refs_0_.first), channel_id=1, source_target_pairs={{4,0},{5,1},{6,2},{7,3},{8,12},{9,13},{10,14},{11,15},{20,16},{21,... | collective-permute-start | bytes 1572872 | tf_op jit(solution)/shard_map/ppermute | solution.py:351
  193.0 13.2 %collective-permute-start.58 = (bf16[6,256,128]{2,1,0:T(8,128)(2,1)S(1)}, bf16[6,256,128]{2,1,0:T(8,128)(2,1)S(1)}, u32[]{:S(2)}, u32[]{:S(2)}) collective-permute-start(bf16[6,256,128]{2,1,0:T(8,128)(2,1)S(1)} %get-tuple-element.201), channel_id=1, source_target_pairs={{0,1},{1,0},{2,3},{3,2},{4,5},{5,4},{6,7},{7,6},{8,9},{9,8},{10,11... | collective-permute-start | bytes 1179656 | tf_op jit(solution)/shard_map/ppermute | solution.py:355
  193.5 11.9 %collective-permute-start.60 = (bf16[3,256,128]{2,1,0:T(8,128)(2,1)S(1)}, bf16[3,256,128]{2,1,0:T(8,128)(2,1)S(1)}, u32[]{:S(2)}, u32[]{:S(2)}) collective-permute-start(bf16[3,256,128]{2,1,0:T(8,128)(2,1)S(1)} %get-tuple-element.207), channel_id=1, source_target_pairs={{0,2},{1,3},{2,0},{3,1},{4,6},{5,7},{6,4},{7,5},{8,10},{9,11},{10,... | collective-permute-start | bytes 589832 | tf_op jit(solution)/shard_map/ppermute | solution.py:355
  194.9 11.3 %collective-permute-start.61 = (bf16[3,256,128]{2,1,0:T(8,128)(2,1)S(1)}, bf16[3,256,128]{2,1,0:T(8,128)(2,1)S(1)}, u32[]{:S(2)}, u32[]{:S(2)}) collective-permute-start(bf16[3,256,128]{2,1,0:T(8,128)(2,1)S(1)} %get-tuple-element.208), channel_id=1, source_target_pairs={{0,3},{1,2},{2,1},{3,0},{4,7},{5,6},{6,5},{7,4},{8,11},{9,10},{10,... | collective-permute-start | bytes 589832 | tf_op jit(solution)/shard_map/ppermute | solution.py:355
  205.3 10.0 %collective-permute-start.54 = (bf16[3,256,128]{2,1,0:T(8,128)(2,1)S(1)}, bf16[3,256,128]{2,1,0:T(8,128)(2,1)S(1)}, u32[]{:S(2)}, u32[]{:S(2)}) collective-permute-start(bf16[3,256,128]{2,1,0:T(8,128)(2,1)S(1)} %get-tuple-element.197), channel_id=1, source_target_pairs={{0,3},{1,2},{2,1},{3,0},{4,7},{5,6},{6,5},{7,4},{8,11},{9,10},{10,... | collective-permute-start | bytes 589832 | tf_op jit(solution)/shard_map/ppermute | solution.py:355
  (37 other events, 284.3 us)

commit v15 on v14

--- a/solution.py
+++ b/solution.py
@@ -220,16 +220,21 @@
     by_place(mid, out, use)
 
 
-def pack(kernel, sizes, table, arrays):
+def pack(kernel, sizes, table, arrays, after=()):
     _, tile, repl = arrays[0].shape
-    return pl.pallas_call(
-        kernel,
+    first_out = 1 + len(arrays) + len(after)
+
+    def picked(*refs):
+        kernel(*refs[: 1 + len(arrays)], *refs[first_out:])
+
+    return pl.pallas_call(
+        picked,
         out_shape=[jax.ShapeDtypeStruct((size, tile, repl), jnp.bfloat16) for size in sizes],
-        in_specs=[SMEM] + [VMEM] * len(arrays),
+        in_specs=[SMEM] + [VMEM] * len(arrays) + [ANY] * len(after),
         out_specs=[VMEM] * len(sizes),
         compiler_params=params(),
         cost_estimate=pl.CostEstimate(flops=0, bytes_accessed=0, transcendentals=0),
-    )(table, *arrays)
+    )(table, *arrays, *after)
 
 
 def multiply(layout, table, tiles, blocks, first, field):
@@ -394,8 +399,9 @@
             out = along_z(OUTWARD, own1)
             table, *packs01 = start(layout, mine, notes, own0, own1)
             got1 = to_other_y(packs01)
-            own2, got1, mid, out = lax.optimization_barrier((own2, got1, mid, out))
-            parts, cores = ((0, 0), (0, 1), (2, 0)), []
+            corner = touch(tiles, own2)
+            own2, got1 = lax.optimization_barrier((own2, got1))
+            parts, cores, after = ((0, 0), (0, 1), (2, 0)), [], [corner]
             got = got1
         else:
             core0 = across(1, packs0[2])
@@ -409,19 +415,21 @@
             got1 = to_other_y(packs1)
             mid = along_z(MIDDLE, again)
             own2, got1 = lax.optimization_barrier((own2, got1))
-            parts, cores = ((0, 0), (2, 0), (4, 0)), [core0]
+            parts, cores, after = ((0, 0), (2, 0), (4, 0)), [core0], []
             got = got0 + got1
         js, shards = ((0, 1, 2), [own0, own1, own2]) if step == 0 else ((1, 2), [own1, own2])
-        packs2 = pack(functools.partial(second_kernel, layout, js), [cap, cap, len(js) * cap], table, shards)
+        packs2 = pack(functools.partial(second_kernel, layout, js), [cap, cap, len(js) * cap], table, shards, after)
         got2 = to_other_y(packs2)
         core = across(1, packs2[2])
+        packs3 = pack(functools.partial(third_kernel, layout), [cap] * 3, table, [mid, out])
         if step == 0:
-            note, core = lax.optimization_barrier((note, core))
+            note, packs3 = lax.optimization_barrier((note, packs3))
             plane = note + notes[0] + notes[1] + notes[2]
             half = plane + across(4, plane)
-        packs3 = pack(functools.partial(third_kernel, layout), [cap] * 3, table, [mid, out])
         core3 = across(1, packs3[2])
         got3 = to_other_y(packs3)
+        if step == 0:
+            got2, half = lax.optimization_barrier((got2, half))
         field = early(layout, parts, table, tiles, [own0, own1, own2, mid, out, core, core3] + got + got2 + cores)
         if step == 0:
             total = (half + across(8, half))[0, SUM_AT]
@@ -433,6 +441,21 @@
             own0, packs0 = outs[2], outs[3:]
     energy = row_sum(outs[2])
     return (xpos.reshape(positions.shape), ymom.reshape(momenta.shape), energy.reshape(repl))
+
+
+def touch_kernel(tiles, own, out):
+    out[...] = tiles[0, :8, :128]
+
+
+def touch(tiles, own):
+    return pl.pallas_call(
+        touch_kernel,
+        out_shape=jax.ShapeDtypeStruct((8, 128), tiles.dtype),
+        in_specs=[VMEM, ANY],
+        out_specs=VMEM,
+        compiler_params=params(),
+        cost_estimate=pl.CostEstimate(flops=0, bytes_accessed=0, transcendentals=0),
+    )(tiles, own)
 
 
 def gathered_kernel(last, rows, cols, count, scalars, tiles, gathered, xpos, ymom, xout, yout, extra, xbuf, field, xsem):

time: 230 us -> 227 us (0.987)
  waiting for transfers between devices: 127 us -> 120 us
  starting transfers between devices: 49.6 us -> 54.6 us
    ppermute x16, waiting for transfers between devices: 43.7 us -> 35.9 us  [along_z(): lax.ppermute(value, 'row', [(a * 4 + i, b * 4 + i) for a, b in pairs for...]
    ppermute x46, starting transfers between devices: 31.3 us -> 35.5 us  [across(): return lax.ppermute(value, 'row', [(i, i ^ flip) for i in range(16)])]
    pallas_call x11 -> x12, Pallas kernels: 6.59 us -> 6.6 us  [the longest x11 6.59 us: pack(): pl.pallas_call(picked, out_shape=[jax.ShapeDtypeStruct((size, tile, repl)...]
  transfers between devices with their start and end apart: 62 -> 62, of which waited for: 37 -> 37; matrix products, arithmetic and copies ran while one was open for 0% -> 0% of each run, Pallas kernels for 11% -> 12%
where the time goes in v15:
time: 227 us
  waiting for transfers between devices  120 us (53%)
  starting transfers between devices  54.6 us (24%)
  Pallas kernels  32.9 us (14%)
  blocking collectives  11 us (5%)
  local copies, waits for them, and re-layouts  4.07 us (2%)
  between operations  2.4 us (1%)
    ppermute x46, waiting for transfers between devices, across(): return lax.ppermute(value, 'row', [(i, i ^ flip) for i in range(16)])  83.6 us
    ppermute x16, waiting for transfers between devices, along_z(): lax.ppermute(value, 'row', [(a * 4 + i, b * 4 + i) for a, b in pairs for...  35.9 us
    ppermute x46, starting transfers between devices, across(): return lax.ppermute(value, 'row', [(i, i ^ flip) for i in range(16)])  35.5 us
    ppermute x16, starting transfers between devices, along_z(): lax.ppermute(value, 'row', [(a * 4 + i, b * 4 + i) for a, b in pairs for...  19.1 us
    pallas_call x4, Pallas kernels, early(): pl.pallas_call(functools.partial(early_kernel, layout, parts), out_shape=...  13.9 us
    all_to_all x1, blocking collectives, row_sum(): lax.all_to_all(spread, 'row', split_axis=0, concat_axis=0, tiled=True)  11 us
    pallas_call x4, Pallas kernels, late(): pl.pallas_call(functools.partial(late_kernel, layout, last), out_shape=(s...  6.84 us
    pallas_call x11, Pallas kernels, pack(): pl.pallas_call(picked, out_shape=[jax.ShapeDtypeStruct((size, tile, repl)...  6.59 us
  transfers between devices with their start and end apart: 62, of which 37 were waited for; matrix products, arithmetic and copies ran while one was open for 0% of the time, Pallas kernels for 12%

profile of v15, /device:TPU:0, one launch (start us, length us, event | category | flops | bytes accessed | tf_op | source)
XLA Modules:
  0.0 226.6 jit_solution(14014127147660021104)
XLA Ops:
  1.9 4.1 %collective-permute-start = (bf16[8,256,128]{2,1,0:T(8,128)(2,1)S(1)}, bf16[8,256,128]{2,1,0:T(8,128)(2,1)S(1)}, u32[]{:S(2)}, u32[]{:S(2)}) collective-permute-start(bf16[8,256,128]{2,1,0:T(8,128)(2,1)S(1)} %convert_element_type.3.own.refs_1_), channel_id=1, source_target_pairs={{0,8},{1,9},{2,10},{3,11},{12,4},{13,5},{14,6},{15,7},{4,0},{5,1},... | collective-permute-start | bytes 1572872 | tf_op jit(solution)/shard_map/ppermute | solution.py:356
  6.7 4.2 %shard_map.85 = (s32[144]{0:T(256)}, f32[1,128]{1,0:T(1,128)}) custom-call(s32[48]{0:T(128)} %rows.1, s32[48]{0:T(128)} %cols.1, s32[1]{0:T(128)S(6)} %copy.10.count, bf16[48,256,256]{2,1,0:T(8,128)(2,1)} %tiles.19), custom_call_target="tpu_custom_call" | custom-call | tf_op jit(solution)/shard_map/pallas_call | solution.py:131
  24.1 6.2 %collective-permute-done.4.own.refs_3_.second = bf16[8,256,128]{2,1,0:T(8,128)(2,1)S(1)} collective-permute-done((bf16[8,256,128]{2,1,0:T(8,128)(2,1)S(1)}, bf16[8,256,128]{2,1,0:T(8,128)(2,1)S(1)}, u32[]{:S(2)}, u32[]{:S(2)}) %collective-permute-start.4) | collective-permute-done | bytes 524320 | tf_op jit(solution)/shard_map/ppermute | solution.py:356
  30.3 2.8 %copy-done = bf16[48,256,256]{2,1,0:T(8,128)(2,1)S(1)} copy-done((bf16[48,256,256]{2,1,0:T(8,128)(2,1)S(1)}, bf16[48,256,256]{2,1,0:T(8,128)(2,1)}, u32[]{:S(2)}) %copy-start) | copy-done | bytes 6291480
  33.1 3.8 %collective-permute-done.6.refs_1_ = bf16[6,256,128]{2,1,0:T(8,128)(2,1)S(1)} collective-permute-done((bf16[6,256,128]{2,1,0:T(8,128)(2,1)S(1)}, bf16[6,256,128]{2,1,0:T(8,128)(2,1)S(1)}, u32[]{:S(2)}, u32[]{:S(2)}) %collective-permute-start.6) | collective-permute-done | bytes 393248 | tf_op jit(solution)/shard_map/ppermute | solution.py:360
  47.2 2.5 %collective-permute-done.8.refs_3_ = bf16[3,256,128]{2,1,0:T(8,128)(2,1)S(1)} collective-permute-done((bf16[3,256,128]{2,1,0:T(8,128)(2,1)S(1)}, bf16[3,256,128]{2,1,0:T(8,128)(2,1)S(1)}, u32[]{:S(2)}, u32[]{:S(2)}) %collective-permute-start.8) | collective-permute-done | bytes 196640 | tf_op jit(solution)/shard_map/ppermute | solution.py:360
  49.7 3.4 %collective-permute-start.12 = (f32[1,128]{1,0:T(1,128)S(1)}, f32[1,128]{1,0:T(1,128)S(1)}, u32[]{:S(2)}, u32[]{:S(2)}) collective-permute-start(f32[1,128]{1,0:T(1,128)S(1)} %add.18), channel_id=1, source_target_pairs={{0,8},{1,9},{2,10},{3,11},{4,12},{5,13},{6,14},{7,15},{8,0},{9,1},... | collective-permute-start | bytes 1544 | tf_op jit(solution)/shard_map/ppermute | solution.py:360
  56.0 3.5 %shard_map.90.field = f32[9,256,128]{2,1,0:T(8,128)S(1)} custom-call(s32[180]{0:T(256)S(1)} %get-tuple-element.123.refs_0_.table, bf16[48,256,256]{2,1,0:T(8,128)(2,1)S(1)} %copy-done.1, bf16[8,256,128]{2,1,0:T(8,128)(2,1)S(1)} %convert_element_type.3.own.refs_1_, bf16[8,256,128]{2,1,0:T(8,128)(2,1)S(1)} %collective-permute-done.first.refs_2_, ...), custom_call_target="tpu_custom_call" | custom-call | tf_op jit(solution)/shard_map/pallas_call | solution.py:281
  60.9 3.0 %collective-permute-start.21 = (bf16[8,256,128]{2,1,0:T(8,128)(2,1)S(1)}, bf16[8,256,128]{2,1,0:T(8,128)(2,1)S(1)}, u32[]{:S(2)}, u32[]{:S(2)}) collective-permute-start(bf16[8,256,128]{2,1,0:T(8,128)(2,1)S(1)} %get-tuple-element.148.own), channel_id=1, source_target_pairs={{0,8},{1,9},{2,10},{3,11},{12,4},{13,5},{14,6},{15,7},{4,0},{5,1},... | collective-permute-start | bytes 1572872 | tf_op jit(solution)/shard_map/ppermute | solution.py:356
  65.8 5.8 %collective-permute-done.18.refs_0_ = bf16[3,256,128]{2,1,0:T(8,128)(2,1)S(1)} collective-permute-done((bf16[3,256,128]{2,1,0:T(8,128)(2,1)S(1)}, bf16[3,256,128]{2,1,0:T(8,128)(2,1)S(1)}, u32[]{:S(2)}, u32[]{:S(2)}) %collective-permute-start.18) | collective-permute-done | bytes 196640 | tf_op jit(solution)/shard_map/ppermute | solution.py:360
  71.6 3.4 %collective-permute-done.19.refs_1_ = bf16[3,256,128]{2,1,0:T(8,128)(2,1)S(1)} collective-permute-done((bf16[3,256,128]{2,1,0:T(8,128)(2,1)S(1)}, bf16[3,256,128]{2,1,0:T(8,128)(2,1)S(1)}, u32[]{:S(2)}, u32[]{:S(2)}) %collective-permute-start.19) | collective-permute-done | bytes 196640 | tf_op jit(solution)/shard_map/ppermute | solution.py:360
  79.6 6.5 %collective-permute-done.26.refs_2_ = bf16[3,256,128]{2,1,0:T(8,128)(2,1)S(1)} collective-permute-done((bf16[3,256,128]{2,1,0:T(8,128)(2,1)S(1)}, bf16[3,256,128]{2,1,0:T(8,128)(2,1)S(1)}, u32[]{:S(2)}, u32[]{:S(2)}) %collective-permute-start.26) | collective-permute-done | bytes 196640 | tf_op jit(solution)/shard_map/ppermute | solution.py:360
  91.5 7.8 %collective-permute-done.22.refs_2_.out = bf16[8,256,128]{2,1,0:T(8,128)(2,1)S(1)} collective-permute-done((bf16[8,256,128]{2,1,0:T(8,128)(2,1)S(1)}, bf16[8,256,128]{2,1,0:T(8,128)(2,1)S(1)}, u32[]{:S(2)}, u32[]{:S(2)}) %collective-permute-start.22) | collective-permute-done | bytes 524320 | tf_op jit(solution)/shard_map/ppermute | solution.py:356
  101.9 3.5 %shard_map.95.field = f32[9,256,128]{2,1,0:T(8,128)S(1)} custom-call(s32[180]{0:T(256)S(1)} %get-tuple-element.123.refs_0_.table, bf16[48,256,256]{2,1,0:T(8,128)(2,1)S(1)} %copy-done.1, bf16[8,256,128]{2,1,0:T(8,128)(2,1)S(1)} %get-tuple-element.148.own, bf16[8,256,128]{2,1,0:T(8,128)(2,1)S(1)} %collective-permute-done.21.refs_1_.first, ...), custom_call_target="tpu_custom_call" | custom-call | tf_op jit(solution)/shard_map/pallas_call | solution.py:281
  105.3 2.3 %collective-permute-done.23.got2 = bf16[3,256,128]{2,1,0:T(8,128)(2,1)S(1)} collective-permute-done((bf16[3,256,128]{2,1,0:T(8,128)(2,1)S(1)}, bf16[3,256,128]{2,1,0:T(8,128)(2,1)S(1)}, u32[]{:S(2)}, u32[]{:S(2)}) %collective-permute-start.23) | collective-permute-done | bytes 196640 | tf_op jit(solution)/shard_map/ppermute | solution.py:360
  107.7 3.3 %collective-permute-done.24.got3 = bf16[3,256,128]{2,1,0:T(8,128)(2,1)S(1)} collective-permute-done((bf16[3,256,128]{2,1,0:T(8,128)(2,1)S(1)}, bf16[3,256,128]{2,1,0:T(8,128)(2,1)S(1)}, u32[]{:S(2)}, u32[]{:S(2)}) %collective-permute-start.24) | collective-permute-done | bytes 196640 | tf_op jit(solution)/shard_map/ppermute | solution.py:360
  116.3 5.4 %collective-permute-done.33.refs_0_ = bf16[3,256,128]{2,1,0:T(8,128)(2,1)S(1)} collective-permute-done((bf16[3,256,128]{2,1,0:T(8,128)(2,1)S(1)}, bf16[3,256,128]{2,1,0:T(8,128)(2,1)S(1)}, u32[]{:S(2)}, u32[]{:S(2)}) %collective-permute-start.33) | collective-permute-done | bytes 196640 | tf_op jit(solution)/shard_map/ppermute | solution.py:360
  121.8 3.4 %collective-permute-done.34.refs_1_ = bf16[3,256,128]{2,1,0:T(8,128)(2,1)S(1)} collective-permute-done((bf16[3,256,128]{2,1,0:T(8,128)(2,1)S(1)}, bf16[3,256,128]{2,1,0:T(8,128)(2,1)S(1)}, u32[]{:S(2)}, u32[]{:S(2)}) %collective-permute-start.34) | collective-permute-done | bytes 196640 | tf_op jit(solution)/shard_map/ppermute | solution.py:360
  130.1 6.3 %collective-permute-done.41.refs_2_ = bf16[3,256,128]{2,1,0:T(8,128)(2,1)S(1)} collective-permute-done((bf16[3,256,128]{2,1,0:T(8,128)(2,1)S(1)}, bf16[3,256,128]{2,1,0:T(8,128)(2,1)S(1)}, u32[]{:S(2)}, u32[]{:S(2)}) %collective-permute-start.41) | collective-permute-done | bytes 196640 | tf_op jit(solution)/shard_map/ppermute | solution.py:360
  141.7 8.3 %collective-permute-done.37.refs_2_.out = bf16[8,256,128]{2,1,0:T(8,128)(2,1)S(1)} collective-permute-done((bf16[8,256,128]{2,1,0:T(8,128)(2,1)S(1)}, bf16[8,256,128]{2,1,0:T(8,128)(2,1)S(1)}, u32[]{:S(2)}, u32[]{:S(2)}) %collective-permute-start.37) | collective-permute-done | bytes 524320 | tf_op jit(solution)/shard_map/ppermute | solution.py:356
  152.6 3.5 %shard_map.100.field = f32[9,256,128]{2,1,0:T(8,128)S(1)} custom-call(s32[180]{0:T(256)S(1)} %get-tuple-element.123.refs_0_.table, bf16[48,256,256]{2,1,0:T(8,128)(2,1)S(1)} %copy-done.1, bf16[8,256,128]{2,1,0:T(8,128)(2,1)S(1)} %get-tuple-element.173.own, bf16[8,256,128]{2,1,0:T(8,128)(2,1)S(1)} %collective-permute-done.36.refs_1_.first, ...), custom_call_target="tpu_custom_call" | custom-call | tf_op jit(solution)/shard_map/pallas_call | solution.py:281
  156.1 2.3 %collective-permute-done.38.got2 = bf16[3,256,128]{2,1,0:T(8,128)(2,1)S(1)} collective-permute-done((bf16[3,256,128]{2,1,0:T(8,128)(2,1)S(1)}, bf16[3,256,128]{2,1,0:T(8,128)(2,1)S(1)}, u32[]{:S(2)}, u32[]{:S(2)}) %collective-permute-start.38) | collective-permute-done | bytes 196640 | tf_op jit(solution)/shard_map/ppermute | solution.py:360
  158.4 3.3 %collective-permute-done.39.got3 = bf16[3,256,128]{2,1,0:T(8,128)(2,1)S(1)} collective-permute-done((bf16[3,256,128]{2,1,0:T(8,128)(2,1)S(1)}, bf16[3,256,128]{2,1,0:T(8,128)(2,1)S(1)}, u32[]{:S(2)}, u32[]{:S(2)}) %collective-permute-start.39) | collective-permute-done | bytes 196640 | tf_op jit(solution)/shard_map/ppermute | solution.py:360
  167.1 5.4 %collective-permute-done.48.refs_0_ = bf16[3,256,128]{2,1,0:T(8,128)(2,1)S(1)} collective-permute-done((bf16[3,256,128]{2,1,0:T(8,128)(2,1)S(1)}, bf16[3,256,128]{2,1,0:T(8,128)(2,1)S(1)}, u32[]{:S(2)}, u32[]{:S(2)}) %collective-permute-start.48) | collective-permute-done | bytes 196640 | tf_op jit(solution)/shard_map/ppermute | solution.py:360
  172.5 3.4 %collective-permute-done.49.refs_1_ = bf16[3,256,128]{2,1,0:T(8,128)(2,1)S(1)} collective-permute-done((bf16[3,256,128]{2,1,0:T(8,128)(2,1)S(1)}, bf16[3,256,128]{2,1,0:T(8,128)(2,1)S(1)}, u32[]{:S(2)}, u32[]{:S(2)}) %collective-permute-start.49) | collective-permute-done | bytes 196640 | tf_op jit(solution)/shard_map/ppermute | solution.py:360
  180.8 6.3 %collective-permute-done.56.refs_2_ = bf16[3,256,128]{2,1,0:T(8,128)(2,1)S(1)} collective-permute-done((bf16[3,256,128]{2,1,0:T(8,128)(2,1)S(1)}, bf16[3,256,128]{2,1,0:T(8,128)(2,1)S(1)}, u32[]{:S(2)}, u32[]{:S(2)}) %collective-permute-start.56) | collective-permute-done | bytes 196640 | tf_op jit(solution)/shard_map/ppermute | solution.py:360
  192.4 8.3 %collective-permute-done.52.refs_2_.out = bf16[8,256,128]{2,1,0:T(8,128)(2,1)S(1)} collective-permute-done((bf16[8,256,128]{2,1,0:T(8,128)(2,1)S(1)}, bf16[8,256,128]{2,1,0:T(8,128)(2,1)S(1)}, u32[]{:S(2)}, u32[]{:S(2)}) %collective-permute-start.52) | collective-permute-done | bytes 524320 | tf_op jit(solution)/shard_map/ppermute | solution.py:356
  203.4 3.5 %shard_map.105.field = f32[9,256,128]{2,1,0:T(8,128)S(1)} custom-call(s32[180]{0:T(256)S(1)} %get-tuple-element.123.refs_0_.table, bf16[48,256,256]{2,1,0:T(8,128)(2,1)S(1)} %copy-done.1, bf16[8,256,128]{2,1,0:T(8,128)(2,1)S(1)} %get-tuple-element.198.own, bf16[8,256,128]{2,1,0:T(8,128)(2,1)S(1)} %collective-permute-done.51.refs_1_.first, ...), custom_call_target="tpu_custom_call" | custom-call | tf_op jit(solution)/shard_map/pallas_call | solution.py:281
  206.8 2.3 %collective-permute-done.53.got2 = bf16[3,256,128]{2,1,0:T(8,128)(2,1)S(1)} collective-permute-done((bf16[3,256,128]{2,1,0:T(8,128)(2,1)S(1)}, bf16[3,256,128]{2,1,0:T(8,128)(2,1)S(1)}, u32[]{:S(2)}, u32[]{:S(2)}) %collective-permute-start.53) | collective-permute-done | bytes 196640 | tf_op jit(solution)/shard_map/ppermute | solution.py:360
  209.2 3.3 %collective-permute-done.54.got3 = bf16[3,256,128]{2,1,0:T(8,128)(2,1)S(1)} collective-permute-done((bf16[3,256,128]{2,1,0:T(8,128)(2,1)S(1)}, bf16[3,256,128]{2,1,0:T(8,128)(2,1)S(1)}, u32[]{:S(2)}, u32[]{:S(2)}) %collective-permute-start.54) | collective-permute-done | bytes 196640 | tf_op jit(solution)/shard_map/ppermute | solution.py:360
  212.5 2.6 %shard_map.106 = (f32[8,256,128]{2,1,0:T(8,128)}, f32[8,256,128]{2,1,0:T(8,128)}, f32[1,128]{1,0:T(1,128)S(1)}) custom-call(s32[180]{0:T(256)S(1)} %get-tuple-element.123.refs_0_.table, f32[2]{0:T(128)S(1)} %pad_maximum_fusion.scalars, bf16[48,256,256]{2,1,0:T(8,128)(2,1)S(1)} %copy-done.1, bf16[3,256,128]{2,1,0:T(8,128)(2,1)S(1)} %collective-permute-done.53.got2, ...), custom_call_target="tpu_custom_call" | custom-call | flops 100663296 | bytes 6422528 | tf_op jit(solution)/shard_map/pallas_call | solution.py:340
  215.1 11.0 %all_to_all.6 = f32[16,1,128]{2,1,0:T(1,128)S(1)} all-to-all(f32[16,1,128]{2,1,0:T(1,128)S(1)} %broadcast_in_dim.2), channel_id=1, replica_groups=mesh['groups'=2,'row'=16] {'row'}, dimensions={0} | all-to-all | bytes 16384 | tf_op jit(solution)/shard_map/all_to_all | solution.py:366
  (138 shorter events, 79.5 us)
Async XLA Ops:
  1.9 16.5 %collective-permute-start = (bf16[8,256,128]{2,1,0:T(8,128)(2,1)S(1)}, bf16[8,256,128]{2,1,0:T(8,128)(2,1)S(1)}, u32[]{:S(2)}, u32[]{:S(2)}) collective-permute-start(bf16[8,256,128]{2,1,0:T(8,128)(2,1)S(1)} %convert_element_type.3.own.refs_1_), channel_id=1, source_target_pairs={{0,8},{1,9},{2,10},{3,11},{12,4},{13,5},{14,6},{15,7},{4,0},{5,1},... | collective-permute-start | bytes 1572872 | tf_op jit(solution)/shard_map/ppermute | solution.py:356
  12.2 18.1 %collective-permute-start.4 = (bf16[8,256,128]{2,1,0:T(8,128)(2,1)S(1)}, bf16[8,256,128]{2,1,0:T(8,128)(2,1)S(1)}, u32[]{:S(2)}, u32[]{:S(2)}) collective-permute-start(bf16[8,256,128]{2,1,0:T(8,128)(2,1)S(1)} %convert_element_type.3.own.refs_1_), channel_id=1, source_target_pairs={{0,4},{1,5},{2,6},{3,7},{12,8},{13,9},{14,10},{15,11},{4,12},{5,13... | collective-permute-start | bytes 1572872 | tf_op jit(solution)/shard_map/ppermute | solution.py:356
  20.5 12.6 %collective-permute-start.5 = (bf16[6,256,128]{2,1,0:T(8,128)(2,1)S(1)}, bf16[6,256,128]{2,1,0:T(8,128)(2,1)S(1)}, u32[]{:S(2)}, u32[]{:S(2)}) collective-permute-start(bf16[6,256,128]{2,1,0:T(8,128)(2,1)S(1)} %get-tuple-element.124), channel_id=1, source_target_pairs={{0,2},{1,3},{2,0},{3,1},{4,6},{5,7},{6,4},{7,5},{8,10},{9,11},{10,... | collective-permute-start | bytes 1179656 | tf_op jit(solution)/shard_map/ppermute | solution.py:360
  22.1 14.8 %collective-permute-start.6 = (bf16[6,256,128]{2,1,0:T(8,128)(2,1)S(1)}, bf16[6,256,128]{2,1,0:T(8,128)(2,1)S(1)}, u32[]{:S(2)}, u32[]{:S(2)}) collective-permute-start(bf16[6,256,128]{2,1,0:T(8,128)(2,1)S(1)} %get-tuple-element.125), channel_id=1, source_target_pairs={{0,3},{1,2},{2,1},{3,0},{4,7},{5,6},{6,5},{7,4},{8,11},{9,10},{10,... | collective-permute-start | bytes 1179656 | tf_op jit(solution)/shard_map/ppermute | solution.py:360
  22.1 18.8 %collective-permute-start.9 = (bf16[8,256,128]{2,1,0:T(8,128)(2,1)S(1)}, bf16[8,256,128]{2,1,0:T(8,128)(2,1)S(1)}, u32[]{:S(2)}, u32[]{:S(2)}) collective-permute-start(bf16[8,256,128]{2,1,0:T(8,128)(2,1)S(1)} %convert_element_type.3.own.refs_1_), channel_id=1, source_target_pairs={{4,8},{5,9},{6,10},{7,11},{8,4},{9,5},{10,6},{11,7},{20,24},{21,25... | collective-permute-start | bytes 1572872 | tf_op jit(solution)/shard_map/ppermute | solution.py:356
  22.8 18.9 %collective-permute-start.10 = (bf16[8,256,128]{2,1,0:T(8,128)(2,1)S(1)}, bf16[8,256,128]{2,1,0:T(8,128)(2,1)S(1)}, u32[]{:S(2)}, u32[]{:S(2)}) collective-permute-start(bf16[8,256,128]{2,1,0:T(8,128)(2,1)S(1)} %collective-permute-done.first.refs_2_), channel_id=1, source_target_pairs={{4,0},{5,1},{6,2},{7,3},{8,12},{9,13},{10,14},{11,15},{20,16},{21,... | collective-permute-start | bytes 1572872 | tf_op jit(solution)/shard_map/ppermute | solution.py:356
  37.5 18.5 %collective-permute-start.15 = (bf16[9,256,128]{2,1,0:T(8,128)(2,1)S(1)}, bf16[9,256,128]{2,1,0:T(8,128)(2,1)S(1)}, u32[]{:S(2)}, u32[]{:S(2)}) collective-permute-start(bf16[9,256,128]{2,1,0:T(8,128)(2,1)S(1)} %get-tuple-element.137), channel_id=1, source_target_pairs={{0,1},{1,0},{2,3},{3,2},{4,5},{5,4},{6,7},{7,6},{8,9},{9,8},{10,11... | collective-permute-start | bytes 1769480 | tf_op jit(solution)/shard_map/ppermute | solution.py:360
  43.3 12.7 %collective-permute-start.16 = (bf16[3,256,128]{2,1,0:T(8,128)(2,1)S(1)}, bf16[3,256,128]{2,1,0:T(8,128)(2,1)S(1)}, u32[]{:S(2)}, u32[]{:S(2)}) collective-permute-start(bf16[3,256,128]{2,1,0:T(8,128)(2,1)S(1)} %get-tuple-element.138), channel_id=1, source_target_pairs={{0,1},{1,0},{2,3},{3,2},{4,5},{5,4},{6,7},{7,6},{8,9},{9,8},{10,11... | collective-permute-start | bytes 589832 | tf_op jit(solution)/shard_map/ppermute | solution.py:360
  45.9 13.6 %collective-permute-start.13 = (bf16[3,256,128]{2,1,0:T(8,128)(2,1)S(1)}, bf16[3,256,128]{2,1,0:T(8,128)(2,1)S(1)}, u32[]{:S(2)}, u32[]{:S(2)}) collective-permute-start(bf16[3,256,128]{2,1,0:T(8,128)(2,1)S(1)} %get-tuple-element.135), channel_id=1, source_target_pairs={{0,2},{1,3},{2,0},{3,1},{4,6},{5,7},{6,4},{7,5},{8,10},{9,11},{10,... | collective-permute-start | bytes 589832 | tf_op jit(solution)/shard_map/ppermute | solution.py:360
  47.2 12.3 %collective-permute-start.14 = (bf16[3,256,128]{2,1,0:T(8,128)(2,1)S(1)}, bf16[3,256,128]{2,1,0:T(8,128)(2,1)S(1)}, u32[]{:S(2)}, u32[]{:S(2)}) collective-permute-start(bf16[3,256,128]{2,1,0:T(8,128)(2,1)S(1)} %get-tuple-element.136), channel_id=1, source_target_pairs={{0,3},{1,2},{2,1},{3,0},{4,7},{5,6},{6,5},{7,4},{8,11},{9,10},{10,... | collective-permute-start | bytes 589832 | tf_op jit(solution)/shard_map/ppermute | solution.py:360
  60.9 15.4 %collective-permute-start.21 = (bf16[8,256,128]{2,1,0:T(8,128)(2,1)S(1)}, bf16[8,256,128]{2,1,0:T(8,128)(2,1)S(1)}, u32[]{:S(2)}, u32[]{:S(2)}) collective-permute-start(bf16[8,256,128]{2,1,0:T(8,128)(2,1)S(1)} %get-tuple-element.148.own), channel_id=1, source_target_pairs={{0,8},{1,9},{2,10},{3,11},{12,4},{13,5},{14,6},{15,7},{4,0},{5,1},... | collective-permute-start | bytes 1572872 | tf_op jit(solution)/shard_map/ppermute | solution.py:356
  64.8 10.3 %collective-permute-start.19 = (bf16[3,256,128]{2,1,0:T(8,128)(2,1)S(1)}, bf16[3,256,128]{2,1,0:T(8,128)(2,1)S(1)}, u32[]{:S(2)}, u32[]{:S(2)}) collective-permute-start(bf16[3,256,128]{2,1,0:T(8,128)(2,1)S(1)} %get-tuple-element.147), channel_id=1, source_target_pairs={{0,3},{1,2},{2,1},{3,0},{4,7},{5,6},{6,5},{7,4},{8,11},{9,10},{10,... | collective-permute-start | bytes 589832 | tf_op jit(solution)/shard_map/ppermute | solution.py:360
  65.8 22.4 %collective-permute-start.25 = (bf16[8,256,128]{2,1,0:T(8,128)(2,1)S(1)}, bf16[8,256,128]{2,1,0:T(8,128)(2,1)S(1)}, u32[]{:S(2)}, u32[]{:S(2)}) collective-permute-start(bf16[8,256,128]{2,1,0:T(8,128)(2,1)S(1)} %get-tuple-element.148.own), channel_id=1, source_target_pairs={{0,4},{1,5},{2,6},{3,7},{12,8},{13,9},{14,10},{15,11},{4,12},{5,13... | collective-permute-start | bytes 1572872 | tf_op jit(solution)/shard_map/ppermute | solution.py:356
  75.0 16.4 %collective-permute-start.20 = (bf16[8,256,128]{2,1,0:T(8,128)(2,1)S(1)}, bf16[8,256,128]{2,1,0:T(8,128)(2,1)S(1)}, u32[]{:S(2)}, u32[]{:S(2)}) collective-permute-start(bf16[8,256,128]{2,1,0:T(8,128)(2,1)S(1)} %get-tuple-element.148.own), channel_id=1, source_target_pairs={{4,8},{5,9},{6,10},{7,11},{8,4},{9,5},{10,6},{11,7},{20,24},{21,25... | collective-permute-start | bytes 1572872 | tf_op jit(solution)/shard_map/ppermute | solution.py:356
  76.3 22.9 %collective-permute-start.22 = (bf16[8,256,128]{2,1,0:T(8,128)(2,1)S(1)}, bf16[8,256,128]{2,1,0:T(8,128)(2,1)S(1)}, u32[]{:S(2)}, u32[]{:S(2)}) collective-permute-start(bf16[8,256,128]{2,1,0:T(8,128)(2,1)S(1)} %collective-permute-done.21.refs_1_.first), channel_id=1, source_target_pairs={{4,0},{5,1},{6,2},{7,3},{8,12},{9,13},{10,14},{11,15},{20,16},{21,... | collective-permute-start | bytes 1572872 | tf_op jit(solution)/shard_map/ppermute | solution.py:356
  88.8 13.0 %collective-permute-start.28 = (bf16[6,256,128]{2,1,0:T(8,128)(2,1)S(1)}, bf16[6,256,128]{2,1,0:T(8,128)(2,1)S(1)}, u32[]{:S(2)}, u32[]{:S(2)}) collective-permute-start(bf16[6,256,128]{2,1,0:T(8,128)(2,1)S(1)} %get-tuple-element.157), channel_id=1, source_target_pairs={{0,1},{1,0},{2,3},{3,2},{4,5},{5,4},{6,7},{7,6},{8,9},{9,8},{10,11... | collective-permute-start | bytes 1179656 | tf_op jit(solution)/shard_map/ppermute | solution.py:360
  90.0 11.4 %collective-permute-start.30 = (bf16[3,256,128]{2,1,0:T(8,128)(2,1)S(1)}, bf16[3,256,128]{2,1,0:T(8,128)(2,1)S(1)}, u32[]{:S(2)}, u32[]{:S(2)}) collective-permute-start(bf16[3,256,128]{2,1,0:T(8,128)(2,1)S(1)} %get-tuple-element.163), channel_id=1, source_target_pairs={{0,2},{1,3},{2,0},{3,1},{4,6},{5,7},{6,4},{7,5},{8,10},{9,11},{10,... | collective-permute-start | bytes 589832 | tf_op jit(solution)/shard_map/ppermute | solution.py:360
  90.7 11.1 %collective-permute-start.31 = (bf16[3,256,128]{2,1,0:T(8,128)(2,1)S(1)}, bf16[3,256,128]{2,1,0:T(8,128)(2,1)S(1)}, u32[]{:S(2)}, u32[]{:S(2)}) collective-permute-start(bf16[3,256,128]{2,1,0:T(8,128)(2,1)S(1)} %get-tuple-element.164), channel_id=1, source_target_pairs={{0,3},{1,2},{2,1},{3,0},{4,7},{5,6},{6,5},{7,4},{8,11},{9,10},{10,... | collective-permute-start | bytes 589832 | tf_op jit(solution)/shard_map/ppermute | solution.py:360
  112.4 14.3 %collective-permute-start.36 = (bf16[8,256,128]{2,1,0:T(8,128)(2,1)S(1)}, bf16[8,256,128]{2,1,0:T(8,128)(2,1)S(1)}, u32[]{:S(2)}, u32[]{:S(2)}) collective-permute-start(bf16[8,256,128]{2,1,0:T(8,128)(2,1)S(1)} %get-tuple-element.173.own), channel_id=1, source_target_pairs={{0,8},{1,9},{2,10},{3,11},{12,4},{13,5},{14,6},{15,7},{4,0},{5,1},... | collective-permute-start | bytes 1572872 | tf_op jit(solution)/shard_map/ppermute | solution.py:356
  115.9 22.9 %collective-permute-start.40 = (bf16[8,256,128]{2,1,0:T(8,128)(2,1)S(1)}, bf16[8,256,128]{2,1,0:T(8,128)(2,1)S(1)}, u32[]{:S(2)}, u32[]{:S(2)}) collective-permute-start(bf16[8,256,128]{2,1,0:T(8,128)(2,1)S(1)} %get-tuple-element.173.own), channel_id=1, source_target_pairs={{0,4},{1,5},{2,6},{3,7},{12,8},{13,9},{14,10},{15,11},{4,12},{5,13... | collective-permute-start | bytes 1572872 | tf_op jit(solution)/shard_map/ppermute | solution.py:356
  125.2 16.5 %collective-permute-start.35 = (bf16[8,256,128]{2,1,0:T(8,128)(2,1)S(1)}, bf16[8,256,128]{2,1,0:T(8,128)(2,1)S(1)}, u32[]{:S(2)}, u32[]{:S(2)}) collective-permute-start(bf16[8,256,128]{2,1,0:T(8,128)(2,1)S(1)} %get-tuple-element.173.own), channel_id=1, source_target_pairs={{4,8},{5,9},{6,10},{7,11},{8,4},{9,5},{10,6},{11,7},{20,24},{21,25... | collective-permute-start | bytes 1572872 | tf_op jit(solution)/shard_map/ppermute | solution.py:356
  126.6 23.3 %collective-permute-start.37 = (bf16[8,256,128]{2,1,0:T(8,128)(2,1)S(1)}, bf16[8,256,128]{2,1,0:T(8,128)(2,1)S(1)}, u32[]{:S(2)}, u32[]{:S(2)}) collective-permute-start(bf16[8,256,128]{2,1,0:T(8,128)(2,1)S(1)} %collective-permute-done.36.refs_1_.first), channel_id=1, source_target_pairs={{4,0},{5,1},{6,2},{7,3},{8,12},{9,13},{10,14},{11,15},{20,16},{21,... | collective-permute-start | bytes 1572872 | tf_op jit(solution)/shard_map/ppermute | solution.py:356
  139.4 13.2 %collective-permute-start.43 = (bf16[6,256,128]{2,1,0:T(8,128)(2,1)S(1)}, bf16[6,256,128]{2,1,0:T(8,128)(2,1)S(1)}, u32[]{:S(2)}, u32[]{:S(2)}) collective-permute-start(bf16[6,256,128]{2,1,0:T(8,128)(2,1)S(1)} %get-tuple-element.182), channel_id=1, source_target_pairs={{0,1},{1,0},{2,3},{3,2},{4,5},{5,4},{6,7},{7,6},{8,9},{9,8},{10,11... | collective-permute-start | bytes 1179656 | tf_op jit(solution)/shard_map/ppermute | solution.py:360
  140.2 12.0 %collective-permute-start.45 = (bf16[3,256,128]{2,1,0:T(8,128)(2,1)S(1)}, bf16[3,256,128]{2,1,0:T(8,128)(2,1)S(1)}, u32[]{:S(2)}, u32[]{:S(2)}) collective-permute-start(bf16[3,256,128]{2,1,0:T(8,128)(2,1)S(1)} %get-tuple-element.188), channel_id=1, source_target_pairs={{0,2},{1,3},{2,0},{3,1},{4,6},{5,7},{6,4},{7,5},{8,10},{9,11},{10,... | collective-permute-start | bytes 589832 | tf_op jit(solution)/shard_map/ppermute | solution.py:360
  141.7 10.9 %collective-permute-start.46 = (bf16[3,256,128]{2,1,0:T(8,128)(2,1)S(1)}, bf16[3,256,128]{2,1,0:T(8,128)(2,1)S(1)}, u32[]{:S(2)}, u32[]{:S(2)}) collective-permute-start(bf16[3,256,128]{2,1,0:T(8,128)(2,1)S(1)} %get-tuple-element.189), channel_id=1, source_target_pairs={{0,3},{1,2},{2,1},{3,0},{4,7},{5,6},{6,5},{7,4},{8,11},{9,10},{10,... | collective-permute-start | bytes 589832 | tf_op jit(solution)/shard_map/ppermute | solution.py:360
  163.1 14.3 %collective-permute-start.51 = (bf16[8,256,128]{2,1,0:T(8,128)(2,1)S(1)}, bf16[8,256,128]{2,1,0:T(8,128)(2,1)S(1)}, u32[]{:S(2)}, u32[]{:S(2)}) collective-permute-start(bf16[8,256,128]{2,1,0:T(8,128)(2,1)S(1)} %get-tuple-element.198.own), channel_id=1, source_target_pairs={{0,8},{1,9},{2,10},{3,11},{12,4},{13,5},{14,6},{15,7},{4,0},{5,1},... | collective-permute-start | bytes 1572872 | tf_op jit(solution)/shard_map/ppermute | solution.py:356
  166.7 22.9 %collective-permute-start.55 = (bf16[8,256,128]{2,1,0:T(8,128)(2,1)S(1)}, bf16[8,256,128]{2,1,0:T(8,128)(2,1)S(1)}, u32[]{:S(2)}, u32[]{:S(2)}) collective-permute-start(bf16[8,256,128]{2,1,0:T(8,128)(2,1)S(1)} %get-tuple-element.198.own), channel_id=1, source_target_pairs={{0,4},{1,5},{2,6},{3,7},{12,8},{13,9},{14,10},{15,11},{4,12},{5,13... | collective-permute-start | bytes 1572872 | tf_op jit(solution)/shard_map/ppermute | solution.py:356
  176.0 16.5 %collective-permute-start.50 = (bf16[8,256,128]{2,1,0:T(8,128)(2,1)S(1)}, bf16[8,256,128]{2,1,0:T(8,128)(2,1)S(1)}, u32[]{:S(2)}, u32[]{:S(2)}) collective-permute-start(bf16[8,256,128]{2,1,0:T(8,128)(2,1)S(1)} %get-tuple-element.198.own), channel_id=1, source_target_pairs={{4,8},{5,9},{6,10},{7,11},{8,4},{9,5},{10,6},{11,7},{20,24},{21,25... | collective-permute-start | bytes 1572872 | tf_op jit(solution)/shard_map/ppermute | solution.py:356
  177.4 23.3 %collective-permute-start.52 = (bf16[8,256,128]{2,1,0:T(8,128)(2,1)S(1)}, bf16[8,256,128]{2,1,0:T(8,128)(2,1)S(1)}, u32[]{:S(2)}, u32[]{:S(2)}) collective-permute-start(bf16[8,256,128]{2,1,0:T(8,128)(2,1)S(1)} %collective-permute-done.51.refs_1_.first), channel_id=1, source_target_pairs={{4,0},{5,1},{6,2},{7,3},{8,12},{9,13},{10,14},{11,15},{20,16},{21,... | collective-permute-start | bytes 1572872 | tf_op jit(solution)/shard_map/ppermute | solution.py:356
  190.2 13.2 %collective-permute-start.58 = (bf16[6,256,128]{2,1,0:T(8,128)(2,1)S(1)}, bf16[6,256,128]{2,1,0:T(8,128)(2,1)S(1)}, u32[]{:S(2)}, u32[]{:S(2)}) collective-permute-start(bf16[6,256,128]{2,1,0:T(8,128)(2,1)S(1)} %get-tuple-element.207), channel_id=1, source_target_pairs={{0,1},{1,0},{2,3},{3,2},{4,5},{5,4},{6,7},{7,6},{8,9},{9,8},{10,11... | collective-permute-start | bytes 1179656 | tf_op jit(solution)/shard_map/ppermute | solution.py:360
  190.9 12.0 %collective-permute-start.60 = (bf16[3,256,128]{2,1,0:T(8,128)(2,1)S(1)}, bf16[3,256,128]{2,1,0:T(8,128)(2,1)S(1)}, u32[]{:S(2)}, u32[]{:S(2)}) collective-permute-start(bf16[3,256,128]{2,1,0:T(8,128)(2,1)S(1)} %get-tuple-element.213), channel_id=1, source_target_pairs={{0,2},{1,3},{2,0},{3,1},{4,6},{5,7},{6,4},{7,5},{8,10},{9,11},{10,... | collective-permute-start | bytes 589832 | tf_op jit(solution)/shard_map/ppermute | solution.py:360
  192.4 10.9 %collective-permute-start.61 = (bf16[3,256,128]{2,1,0:T(8,128)(2,1)S(1)}, bf16[3,256,128]{2,1,0:T(8,128)(2,1)S(1)}, u32[]{:S(2)}, u32[]{:S(2)}) collective-permute-start(bf16[3,256,128]{2,1,0:T(8,128)(2,1)S(1)} %get-tuple-element.214), channel_id=1, source_target_pairs={{0,3},{1,2},{2,1},{3,0},{4,7},{5,6},{6,5},{7,4},{8,11},{9,10},{10,... | collective-permute-start | bytes 589832 | tf_op jit(solution)/shard_map/ppermute | solution.py:360
  (36 other events, 228.2 us)

commit v16 on v15

--- a/solution.py
+++ b/solution.py
@@ -289,60 +289,35 @@
     )(table, tiles, *arrays)
 
 
-def late_kernel(layout, last, table, scalars, tiles, got2, got3, field, xpos, ymom, *refs):
+def late_field(layout, table, tiles, got2, got3, field, acc):
     cap = layout.cap
-    blocks, _, repl = xpos.shape
-    outs, acc = (refs[:3], refs[3]) if last else (refs[:6], refs[6])
-    xout, yout = outs[:2]
     acc[...] = field[...]
     multiply(layout, table, tiles, [ref[r] for ref in (got2, got3) for r in range(cap)], len(EARLY) * cap, acc)
-    if last:
-        xnew, ynew, sems = refs[4:]
-    else:
-        xnew, ynew = xout, yout
-    total = jnp.zeros((1, repl), jnp.float32)
-    copies = []
-    for b in range(blocks):
-        x, h = xpos[b], acc[b]
-        if last:
-            total += jnp.sum(x * h, axis=0, keepdims=True)
-        x, y = update(scalars[0], scalars[1], h, x, ymom[b])
-        xnew[b] = x
-        ynew[b] = y
-        if last:
-            copies.append(pltpu.make_async_copy(xnew.at[b], xout.at[b], sems.at[0, b]))
-            copies.append(pltpu.make_async_copy(ynew.at[b], yout.at[b], sems.at[1, b]))
-            copies[-2].start()
-            copies[-1].start()
-        else:
-            outs[2][b] = x.astype(jnp.bfloat16)
-    if last:
-        outs[2][...] = -0.5 * total
-        for copy in copies:
-            copy.wait()
-    else:
-        other_y_kernel(layout, (0,), table, *outs[2:5])
-        copy_asked(layout, table, 0, 1, outs[2], outs[5])
-
-
-def late(layout, last, table, scalars, tiles, sources, field, xpos, ymom):
+
+
+def late_kernel(layout, table, scalars, tiles, got2, got3, field, xpos, ymom, xout, yout, xb, out2, out3, core, acc):
+    late_field(layout, table, tiles, got2, got3, field, acc)
+    for b in range(xpos.shape[0]):
+        x, y = update(scalars[0], scalars[1], acc[b], xpos[b], ymom[b])
+        xout[b] = x
+        yout[b] = y
+        xb[b] = x.astype(jnp.bfloat16)
+    other_y_kernel(layout, (0,), table, xb, out2, out3)
+    copy_asked(layout, table, 0, 1, xb, core)
+
+
+def late(layout, table, scalars, tiles, sources, field, xpos, ymom):
     tile = tiles.shape[1]
     blocks, _, repl = xpos.shape
     entries = len(LATE) * layout.cap
     state = jax.ShapeDtypeStruct(xpos.shape, jnp.float32)
-    scratch = [pltpu.VMEM((blocks + 1, tile, repl), jnp.float32)]
-    if last:
-        extra = (jax.ShapeDtypeStruct((1, repl), jnp.float32),)
-        scratch += [pltpu.VMEM(xpos.shape, jnp.float32)] * 2 + [pltpu.SemaphoreType.DMA((2, blocks))]
-    else:
-        out = jax.ShapeDtypeStruct((layout.cap, tile, repl), jnp.bfloat16)
-        extra = (jax.ShapeDtypeStruct(xpos.shape, jnp.bfloat16), out, out, out)
-    return pl.pallas_call(
-        functools.partial(late_kernel, layout, last),
-        out_shape=(state, state) + extra,
+    out = jax.ShapeDtypeStruct((layout.cap, tile, repl), jnp.bfloat16)
+    return pl.pallas_call(
+        functools.partial(late_kernel, layout),
+        out_shape=(state, state, jax.ShapeDtypeStruct(xpos.shape, jnp.bfloat16), out, out, out),
         in_specs=[SMEM, SMEM] + [VMEM] * (1 + len(sources) + 3),
-        out_specs=((ANY, ANY) if last else (VMEM, VMEM)) + (VMEM,) * len(extra),
-        scratch_shapes=scratch,
+        out_specs=(VMEM,) * 6,
+        scratch_shapes=[pltpu.VMEM((blocks + 1, tile, repl), jnp.float32)],
         compiler_params=params(),
         cost_estimate=pl.CostEstimate(
             flops=2 * entries * tile * tile * repl,
@@ -350,6 +325,54 @@
             transcendentals=0,
         ),
     )(table, scalars, tiles, *sources, field, xpos, ymom)
+
+
+def energy_kernel(layout, table, tiles, got2, got3, field, xpos, energy, acc):
+    late_field(layout, table, tiles, got2, got3, field, acc)
+    total = jnp.zeros(xpos.shape[1:], jnp.float32)
+    for b in range(xpos.shape[0]):
+        total += xpos[b] * acc[b]
+    energy[...] = -0.5 * jnp.sum(total, axis=0, keepdims=True)
+
+
+def last_field(layout, table, tiles, sources, field, xpos):
+    return pl.pallas_call(
+        functools.partial(energy_kernel, layout),
+        out_shape=(
+            jax.ShapeDtypeStruct((1, xpos.shape[2]), jnp.float32),
+            jax.ShapeDtypeStruct(field.shape, jnp.float32),
+        ),
+        in_specs=[SMEM] + [VMEM] * (1 + len(sources) + 2),
+        out_specs=(VMEM, VMEM),
+        compiler_params=params(),
+        cost_estimate=pl.CostEstimate(flops=0, bytes_accessed=0, transcendentals=0),
+    )(table, tiles, *sources, field, xpos)
+
+
+def update_kernel(scalars, field, xpos, ymom, xout, yout, xnew, ynew, sems):
+    copies = []
+    for b in range(xpos.shape[0]):
+        x, y = update(scalars[0], scalars[1], field[b], xpos[b], ymom[b])
+        xnew[b] = x
+        ynew[b] = y
+        for i, (new, out) in enumerate(((xnew, xout), (ynew, yout))):
+            copies.append(pltpu.make_async_copy(new.at[b], out.at[b], sems.at[i, b]))
+            copies[-1].start()
+    for copy in copies:
+        copy.wait()
+
+
+def last_update(scalars, field, xpos, ymom):
+    state = jax.ShapeDtypeStruct(xpos.shape, jnp.float32)
+    return pl.pallas_call(
+        update_kernel,
+        out_shape=(state, state),
+        in_specs=[SMEM] + [VMEM] * 3,
+        out_specs=(ANY, ANY),
+        scratch_shapes=[pltpu.VMEM(xpos.shape, jnp.float32)] * 2 + [pltpu.SemaphoreType.DMA((2, xpos.shape[0]))],
+        compiler_params=params(),
+        cost_estimate=pl.CostEstimate(flops=10 * xpos.size, bytes_accessed=20 * xpos.size, transcendentals=0),
+    )(scalars, field, xpos, ymom)
 
 
 def along_z(pairs, value):
@@ -435,11 +458,12 @@
             total = (half + across(8, half))[0, SUM_AT]
             coeff = 0.7 * jnp.sqrt((order - 1) / total)
         scalars = jnp.stack([jnp.float32(0.4 - 0.1 * step), coeff])
-        outs = late(layout, last, table, scalars, tiles, got3, field, xpos, ymom)
-        xpos, ymom = outs[0], outs[1]
-        if not last:
-            own0, packs0 = outs[2], outs[3:]
-    energy = row_sum(outs[2])
+        if last:
+            part, field = last_field(layout, table, tiles, got3, field, xpos)
+            energy = row_sum(part)
+            xpos, ymom = last_update(scalars, field, xpos, ymom)
+        else:
+            xpos, ymom, own0, *packs0 = late(layout, table, scalars, tiles, got3, field, xpos, ymom)
     return (xpos.reshape(positions.shape), ymom.reshape(momenta.shape), energy.reshape(repl))
 
 

time: 227 us -> 226 us (level)
  blocking collectives: 11 us -> 0 us
  starting transfers between devices: 54.6 us -> 59.3 us
  waiting for transfers between devices: 120 us -> 124 us
    all_to_all x1 -> x0, blocking collectives: 11 us -> none  [row_sum(): lax.all_to_all(spread, 'row', split_axis=0, concat_axis=0, tiled=True)]
    all_to_all x0 -> x1, starting transfers between devices: none -> 4.76 us  [row_sum(): lax.all_to_all(spread, 'row', split_axis=0, concat_axis=0, tiled=True)]
    all_to_all x0 -> x1, waiting for transfers between devices: none -> 4.29 us  [row_sum(): lax.all_to_all(spread, 'row', split_axis=0, concat_axis=0, tiled=True)]
    pallas_call x4 -> x5, Pallas kernels: 6.84 us -> 7.29 us  [the longest x3 4.2 us: late(): pl.pallas_call(functools.partial(late_kernel, layout), out_shape=(state,...]
  transfers between devices with their start and end apart: 62 -> 63, of which waited for: 37 -> 38; matrix products, arithmetic and copies ran while one was open for 0% -> 0% of each run, Pallas kernels for 12% -> 12%
where the time goes in v16:
time: 226 us
  waiting for transfers between devices  124 us (55%)
  starting transfers between devices  59.3 us (26%)
  Pallas kernels  33.4 us (15%)
  local copies, waits for them, and re-layouts  4.67 us (2%)
  between operations  2.4 us (1%)
    ppermute x46, waiting for transfers between devices, across(): return lax.ppermute(value, 'row', [(i, i ^ flip) for i in range(16)])  83.7 us
    ppermute x16, waiting for transfers between devices, along_z(): lax.ppermute(value, 'row', [(a * 4 + i, b * 4 + i) for a, b in pairs for...  36 us
    ppermute x46, starting transfers between devices, across(): return lax.ppermute(value, 'row', [(i, i ^ flip) for i in range(16)])  35.4 us
    ppermute x16, starting transfers between devices, along_z(): lax.ppermute(value, 'row', [(a * 4 + i, b * 4 + i) for a, b in pairs for...  19.1 us
    pallas_call x4, Pallas kernels, early(): pl.pallas_call(functools.partial(early_kernel, layout, parts), out_shape=...  13.9 us
    pallas_call x11, Pallas kernels, pack(): pl.pallas_call(picked, out_shape=[jax.ShapeDtypeStruct((size, tile, repl)...  6.59 us
    all_to_all x1, starting transfers between devices, row_sum(): lax.all_to_all(spread, 'row', split_axis=0, concat_axis=0, tiled=True)  4.76 us
  transfers between devices with their start and end apart: 63, of which 38 were waited for; matrix products, arithmetic and copies ran while one was open for 0% of the time, Pallas kernels for 12%

profile of v16, /device:TPU:0, one launch (start us, length us, event | category | flops | bytes accessed | tf_op | source)
XLA Modules:
  0.0 225.8 jit_solution(8430680939604296200)
XLA Ops:
  1.9 4.1 %collective-permute-start = (bf16[8,256,128]{2,1,0:T(8,128)(2,1)S(1)}, bf16[8,256,128]{2,1,0:T(8,128)(2,1)S(1)}, u32[]{:S(2)}, u32[]{:S(2)}) collective-permute-start(bf16[8,256,128]{2,1,0:T(8,128)(2,1)S(1)} %convert_element_type.3.own.refs_1_), channel_id=1, source_target_pairs={{0,8},{1,9},{2,10},{3,11},{12,4},{13,5},{14,6},{15,7},{4,0},{5,1},... | collective-permute-start | bytes 1572872 | tf_op jit(solution)/shard_map/ppermute | solution.py:379
  6.7 4.2 %shard_map.85 = (s32[144]{0:T(256)}, f32[1,128]{1,0:T(1,128)}) custom-call(s32[48]{0:T(128)} %rows.1, s32[48]{0:T(128)} %cols.1, s32[1]{0:T(128)S(6)} %copy.10.count, bf16[48,256,256]{2,1,0:T(8,128)(2,1)} %tiles.19), custom_call_target="tpu_custom_call" | custom-call | tf_op jit(solution)/shard_map/pallas_call | solution.py:131
  24.1 6.2 %collective-permute-done.4.own.refs_3_.second = bf16[8,256,128]{2,1,0:T(8,128)(2,1)S(1)} collective-permute-done((bf16[8,256,128]{2,1,0:T(8,128)(2,1)S(1)}, bf16[8,256,128]{2,1,0:T(8,128)(2,1)S(1)}, u32[]{:S(2)}, u32[]{:S(2)}) %collective-permute-start.4) | collective-permute-done | bytes 524320 | tf_op jit(solution)/shard_map/ppermute | solution.py:379
  30.3 2.8 %copy-done = bf16[48,256,256]{2,1,0:T(8,128)(2,1)S(1)} copy-done((bf16[48,256,256]{2,1,0:T(8,128)(2,1)S(1)}, bf16[48,256,256]{2,1,0:T(8,128)(2,1)}, u32[]{:S(2)}) %copy-start) | copy-done | bytes 6291480
  33.1 3.8 %collective-permute-done.6.refs_1_ = bf16[6,256,128]{2,1,0:T(8,128)(2,1)S(1)} collective-permute-done((bf16[6,256,128]{2,1,0:T(8,128)(2,1)S(1)}, bf16[6,256,128]{2,1,0:T(8,128)(2,1)S(1)}, u32[]{:S(2)}, u32[]{:S(2)}) %collective-permute-start.6) | collective-permute-done | bytes 393248 | tf_op jit(solution)/shard_map/ppermute | solution.py:383
  47.2 2.5 %collective-permute-done.8.refs_3_ = bf16[3,256,128]{2,1,0:T(8,128)(2,1)S(1)} collective-permute-done((bf16[3,256,128]{2,1,0:T(8,128)(2,1)S(1)}, bf16[3,256,128]{2,1,0:T(8,128)(2,1)S(1)}, u32[]{:S(2)}, u32[]{:S(2)}) %collective-permute-start.8) | collective-permute-done | bytes 196640 | tf_op jit(solution)/shard_map/ppermute | solution.py:383
  49.7 3.4 %collective-permute-start.12 = (f32[1,128]{1,0:T(1,128)S(1)}, f32[1,128]{1,0:T(1,128)S(1)}, u32[]{:S(2)}, u32[]{:S(2)}) collective-permute-start(f32[1,128]{1,0:T(1,128)S(1)} %add.18), channel_id=1, source_target_pairs={{0,8},{1,9},{2,10},{3,11},{4,12},{5,13},{6,14},{7,15},{8,0},{9,1},... | collective-permute-start | bytes 1544 | tf_op jit(solution)/shard_map/ppermute | solution.py:383
  56.0 3.5 %shard_map.90.field = f32[9,256,128]{2,1,0:T(8,128)S(1)} custom-call(s32[180]{0:T(256)S(1)} %get-tuple-element.124.refs_0_.table, bf16[48,256,256]{2,1,0:T(8,128)(2,1)S(1)} %copy-done.1, bf16[8,256,128]{2,1,0:T(8,128)(2,1)S(1)} %convert_element_type.3.own.refs_1_, bf16[8,256,128]{2,1,0:T(8,128)(2,1)S(1)} %collective-permute-done.first.refs_2_, ...), custom_call_target="tpu_custom_call" | custom-call | tf_op jit(solution)/shard_map/pallas_call | solution.py:281
  60.9 3.0 %collective-permute-start.21 = (bf16[8,256,128]{2,1,0:T(8,128)(2,1)S(1)}, bf16[8,256,128]{2,1,0:T(8,128)(2,1)S(1)}, u32[]{:S(2)}, u32[]{:S(2)}) collective-permute-start(bf16[8,256,128]{2,1,0:T(8,128)(2,1)S(1)} %get-tuple-element.149.own), channel_id=1, source_target_pairs={{0,8},{1,9},{2,10},{3,11},{12,4},{13,5},{14,6},{15,7},{4,0},{5,1},... | collective-permute-start | bytes 1572872 | tf_op jit(solution)/shard_map/ppermute | solution.py:379
  65.8 5.8 %collective-permute-done.18.refs_0_ = bf16[3,256,128]{2,1,0:T(8,128)(2,1)S(1)} collective-permute-done((bf16[3,256,128]{2,1,0:T(8,128)(2,1)S(1)}, bf16[3,256,128]{2,1,0:T(8,128)(2,1)S(1)}, u32[]{:S(2)}, u32[]{:S(2)}) %collective-permute-start.18) | collective-permute-done | bytes 196640 | tf_op jit(solution)/shard_map/ppermute | solution.py:383
  71.6 3.4 %collective-permute-done.19.refs_1_ = bf16[3,256,128]{2,1,0:T(8,128)(2,1)S(1)} collective-permute-done((bf16[3,256,128]{2,1,0:T(8,128)(2,1)S(1)}, bf16[3,256,128]{2,1,0:T(8,128)(2,1)S(1)}, u32[]{:S(2)}, u32[]{:S(2)}) %collective-permute-start.19) | collective-permute-done | bytes 196640 | tf_op jit(solution)/shard_map/ppermute | solution.py:383
  79.6 6.5 %collective-permute-done.26.refs_2_ = bf16[3,256,128]{2,1,0:T(8,128)(2,1)S(1)} collective-permute-done((bf16[3,256,128]{2,1,0:T(8,128)(2,1)S(1)}, bf16[3,256,128]{2,1,0:T(8,128)(2,1)S(1)}, u32[]{:S(2)}, u32[]{:S(2)}) %collective-permute-start.26) | collective-permute-done | bytes 196640 | tf_op jit(solution)/shard_map/ppermute | solution.py:383
  91.5 7.8 %collective-permute-done.22.refs_2_.out = bf16[8,256,128]{2,1,0:T(8,128)(2,1)S(1)} collective-permute-done((bf16[8,256,128]{2,1,0:T(8,128)(2,1)S(1)}, bf16[8,256,128]{2,1,0:T(8,128)(2,1)S(1)}, u32[]{:S(2)}, u32[]{:S(2)}) %collective-permute-start.22) | collective-permute-done | bytes 524320 | tf_op jit(solution)/shard_map/ppermute | solution.py:379
  101.9 3.5 %shard_map.95.field = f32[9,256,128]{2,1,0:T(8,128)S(1)} custom-call(s32[180]{0:T(256)S(1)} %get-tuple-element.124.refs_0_.table, bf16[48,256,256]{2,1,0:T(8,128)(2,1)S(1)} %copy-done.1, bf16[8,256,128]{2,1,0:T(8,128)(2,1)S(1)} %get-tuple-element.149.own, bf16[8,256,128]{2,1,0:T(8,128)(2,1)S(1)} %collective-permute-done.21.refs_1_.first, ...), custom_call_target="tpu_custom_call" | custom-call | tf_op jit(solution)/shard_map/pallas_call | solution.py:281
  105.3 2.3 %collective-permute-done.23.got2 = bf16[3,256,128]{2,1,0:T(8,128)(2,1)S(1)} collective-permute-done((bf16[3,256,128]{2,1,0:T(8,128)(2,1)S(1)}, bf16[3,256,128]{2,1,0:T(8,128)(2,1)S(1)}, u32[]{:S(2)}, u32[]{:S(2)}) %collective-permute-start.23) | collective-permute-done | bytes 196640 | tf_op jit(solution)/shard_map/ppermute | solution.py:383
  107.7 3.3 %collective-permute-done.24.got3 = bf16[3,256,128]{2,1,0:T(8,128)(2,1)S(1)} collective-permute-done((bf16[3,256,128]{2,1,0:T(8,128)(2,1)S(1)}, bf16[3,256,128]{2,1,0:T(8,128)(2,1)S(1)}, u32[]{:S(2)}, u32[]{:S(2)}) %collective-permute-start.24) | collective-permute-done | bytes 196640 | tf_op jit(solution)/shard_map/ppermute | solution.py:383
  116.3 5.4 %collective-permute-done.33.refs_0_ = bf16[3,256,128]{2,1,0:T(8,128)(2,1)S(1)} collective-permute-done((bf16[3,256,128]{2,1,0:T(8,128)(2,1)S(1)}, bf16[3,256,128]{2,1,0:T(8,128)(2,1)S(1)}, u32[]{:S(2)}, u32[]{:S(2)}) %collective-permute-start.33) | collective-permute-done | bytes 196640 | tf_op jit(solution)/shard_map/ppermute | solution.py:383
  121.8 3.4 %collective-permute-done.34.refs_1_ = bf16[3,256,128]{2,1,0:T(8,128)(2,1)S(1)} collective-permute-done((bf16[3,256,128]{2,1,0:T(8,128)(2,1)S(1)}, bf16[3,256,128]{2,1,0:T(8,128)(2,1)S(1)}, u32[]{:S(2)}, u32[]{:S(2)}) %collective-permute-start.34) | collective-permute-done | bytes 196640 | tf_op jit(solution)/shard_map/ppermute | solution.py:383
  130.1 6.3 %collective-permute-done.41.refs_2_ = bf16[3,256,128]{2,1,0:T(8,128)(2,1)S(1)} collective-permute-done((bf16[3,256,128]{2,1,0:T(8,128)(2,1)S(1)}, bf16[3,256,128]{2,1,0:T(8,128)(2,1)S(1)}, u32[]{:S(2)}, u32[]{:S(2)}) %collective-permute-start.41) | collective-permute-done | bytes 196640 | tf_op jit(solution)/shard_map/ppermute | solution.py:383
  141.7 8.3 %collective-permute-done.37.refs_2_.out = bf16[8,256,128]{2,1,0:T(8,128)(2,1)S(1)} collective-permute-done((bf16[8,256,128]{2,1,0:T(8,128)(2,1)S(1)}, bf16[8,256,128]{2,1,0:T(8,128)(2,1)S(1)}, u32[]{:S(2)}, u32[]{:S(2)}) %collective-permute-start.37) | collective-permute-done | bytes 524320 | tf_op jit(solution)/shard_map/ppermute | solution.py:379
  152.6 3.5 %shard_map.100.field = f32[9,256,128]{2,1,0:T(8,128)S(1)} custom-call(s32[180]{0:T(256)S(1)} %get-tuple-element.124.refs_0_.table, bf16[48,256,256]{2,1,0:T(8,128)(2,1)S(1)} %copy-done.1, bf16[8,256,128]{2,1,0:T(8,128)(2,1)S(1)} %get-tuple-element.174.own, bf16[8,256,128]{2,1,0:T(8,128)(2,1)S(1)} %collective-permute-done.36.refs_1_.first, ...), custom_call_target="tpu_custom_call" | custom-call | tf_op jit(solution)/shard_map/pallas_call | solution.py:281
  156.1 2.3 %collective-permute-done.38.got2 = bf16[3,256,128]{2,1,0:T(8,128)(2,1)S(1)} collective-permute-done((bf16[3,256,128]{2,1,0:T(8,128)(2,1)S(1)}, bf16[3,256,128]{2,1,0:T(8,128)(2,1)S(1)}, u32[]{:S(2)}, u32[]{:S(2)}) %collective-permute-start.38) | collective-permute-done | bytes 196640 | tf_op jit(solution)/shard_map/ppermute | solution.py:383
  158.4 3.3 %collective-permute-done.39.got3 = bf16[3,256,128]{2,1,0:T(8,128)(2,1)S(1)} collective-permute-done((bf16[3,256,128]{2,1,0:T(8,128)(2,1)S(1)}, bf16[3,256,128]{2,1,0:T(8,128)(2,1)S(1)}, u32[]{:S(2)}, u32[]{:S(2)}) %collective-permute-start.39) | collective-permute-done | bytes 196640 | tf_op jit(solution)/shard_map/ppermute | solution.py:383
  167.1 5.4 %collective-permute-done.48.refs_0_ = bf16[3,256,128]{2,1,0:T(8,128)(2,1)S(1)} collective-permute-done((bf16[3,256,128]{2,1,0:T(8,128)(2,1)S(1)}, bf16[3,256,128]{2,1,0:T(8,128)(2,1)S(1)}, u32[]{:S(2)}, u32[]{:S(2)}) %collective-permute-start.48) | collective-permute-done | bytes 196640 | tf_op jit(solution)/shard_map/ppermute | solution.py:383
  172.5 3.4 %collective-permute-done.49.refs_1_ = bf16[3,256,128]{2,1,0:T(8,128)(2,1)S(1)} collective-permute-done((bf16[3,256,128]{2,1,0:T(8,128)(2,1)S(1)}, bf16[3,256,128]{2,1,0:T(8,128)(2,1)S(1)}, u32[]{:S(2)}, u32[]{:S(2)}) %collective-permute-start.49) | collective-permute-done | bytes 196640 | tf_op jit(solution)/shard_map/ppermute | solution.py:383
  180.8 6.3 %collective-permute-done.56.refs_2_ = bf16[3,256,128]{2,1,0:T(8,128)(2,1)S(1)} collective-permute-done((bf16[3,256,128]{2,1,0:T(8,128)(2,1)S(1)}, bf16[3,256,128]{2,1,0:T(8,128)(2,1)S(1)}, u32[]{:S(2)}, u32[]{:S(2)}) %collective-permute-start.56) | collective-permute-done | bytes 196640 | tf_op jit(solution)/shard_map/ppermute | solution.py:383
  192.4 8.3 %collective-permute-done.52.refs_2_.out = bf16[8,256,128]{2,1,0:T(8,128)(2,1)S(1)} collective-permute-done((bf16[8,256,128]{2,1,0:T(8,128)(2,1)S(1)}, bf16[8,256,128]{2,1,0:T(8,128)(2,1)S(1)}, u32[]{:S(2)}, u32[]{:S(2)}) %collective-permute-start.52) | collective-permute-done | bytes 524320 | tf_op jit(solution)/shard_map/ppermute | solution.py:379
  203.3 3.5 %shard_map.105.field = f32[9,256,128]{2,1,0:T(8,128)S(1)} custom-call(s32[180]{0:T(256)S(1)} %get-tuple-element.124.refs_0_.table, bf16[48,256,256]{2,1,0:T(8,128)(2,1)S(1)} %copy-done.1, bf16[8,256,128]{2,1,0:T(8,128)(2,1)S(1)} %get-tuple-element.199.own, bf16[8,256,128]{2,1,0:T(8,128)(2,1)S(1)} %collective-permute-done.51.refs_1_.first, ...), custom_call_target="tpu_custom_call" | custom-call | tf_op jit(solution)/shard_map/pallas_call | solution.py:281
  206.8 2.4 %collective-permute-done.53.got2 = bf16[3,256,128]{2,1,0:T(8,128)(2,1)S(1)} collective-permute-done((bf16[3,256,128]{2,1,0:T(8,128)(2,1)S(1)}, bf16[3,256,128]{2,1,0:T(8,128)(2,1)S(1)}, u32[]{:S(2)}, u32[]{:S(2)}) %collective-permute-start.53) | collective-permute-done | bytes 196640 | tf_op jit(solution)/shard_map/ppermute | solution.py:383
  209.2 3.3 %collective-permute-done.54.got3 = bf16[3,256,128]{2,1,0:T(8,128)(2,1)S(1)} collective-permute-done((bf16[3,256,128]{2,1,0:T(8,128)(2,1)S(1)}, bf16[3,256,128]{2,1,0:T(8,128)(2,1)S(1)}, u32[]{:S(2)}, u32[]{:S(2)}) %collective-permute-start.54) | collective-permute-done | bytes 196640 | tf_op jit(solution)/shard_map/ppermute | solution.py:383
  214.1 4.8 %all-to-all-start = ((f32[16,1,128]{2,1,0:T(1,128)}), f32[16,1,128]{2,1,0:T(1,128)S(1)}, u32[]{:S(2)}, u32[]{:S(2)}) async-start(f32[16,1,128]{2,1,0:T(1,128)} %broadcast_in_dim.2), calls=%async_computation | async-start | bytes 16384 | tf_op jit(solution)/shard_map/all_to_all | solution.py:389
  221.0 4.3 %all-to-all-done = f32[16,1,128]{2,1,0:T(1,128)S(1)} async-done(((f32[16,1,128]{2,1,0:T(1,128)}), f32[16,1,128]{2,1,0:T(1,128)S(1)}, u32[]{:S(2)}, u32[]{:S(2)}) %all-to-all-start) | async-done | bytes 8224 | tf_op jit(solution)/shard_map/all_to_all | solution.py:389
  (140 shorter events, 83.1 us)
Async XLA Ops:
  1.9 16.5 %collective-permute-start = (bf16[8,256,128]{2,1,0:T(8,128)(2,1)S(1)}, bf16[8,256,128]{2,1,0:T(8,128)(2,1)S(1)}, u32[]{:S(2)}, u32[]{:S(2)}) collective-permute-start(bf16[8,256,128]{2,1,0:T(8,128)(2,1)S(1)} %convert_element_type.3.own.refs_1_), channel_id=1, source_target_pairs={{0,8},{1,9},{2,10},{3,11},{12,4},{13,5},{14,6},{15,7},{4,0},{5,1},... | collective-permute-start | bytes 1572872 | tf_op jit(solution)/shard_map/ppermute | solution.py:379
  12.2 18.1 %collective-permute-start.4 = (bf16[8,256,128]{2,1,0:T(8,128)(2,1)S(1)}, bf16[8,256,128]{2,1,0:T(8,128)(2,1)S(1)}, u32[]{:S(2)}, u32[]{:S(2)}) collective-permute-start(bf16[8,256,128]{2,1,0:T(8,128)(2,1)S(1)} %convert_element_type.3.own.refs_1_), channel_id=1, source_target_pairs={{0,4},{1,5},{2,6},{3,7},{12,8},{13,9},{14,10},{15,11},{4,12},{5,13... | collective-permute-start | bytes 1572872 | tf_op jit(solution)/shard_map/ppermute | solution.py:379
  20.5 12.6 %collective-permute-start.5 = (bf16[6,256,128]{2,1,0:T(8,128)(2,1)S(1)}, bf16[6,256,128]{2,1,0:T(8,128)(2,1)S(1)}, u32[]{:S(2)}, u32[]{:S(2)}) collective-permute-start(bf16[6,256,128]{2,1,0:T(8,128)(2,1)S(1)} %get-tuple-element.125), channel_id=1, source_target_pairs={{0,2},{1,3},{2,0},{3,1},{4,6},{5,7},{6,4},{7,5},{8,10},{9,11},{10,... | collective-permute-start | bytes 1179656 | tf_op jit(solution)/shard_map/ppermute | solution.py:383
  22.1 14.8 %collective-permute-start.6 = (bf16[6,256,128]{2,1,0:T(8,128)(2,1)S(1)}, bf16[6,256,128]{2,1,0:T(8,128)(2,1)S(1)}, u32[]{:S(2)}, u32[]{:S(2)}) collective-permute-start(bf16[6,256,128]{2,1,0:T(8,128)(2,1)S(1)} %get-tuple-element.126), channel_id=1, source_target_pairs={{0,3},{1,2},{2,1},{3,0},{4,7},{5,6},{6,5},{7,4},{8,11},{9,10},{10,... | collective-permute-start | bytes 1179656 | tf_op jit(solution)/shard_map/ppermute | solution.py:383
  22.1 18.8 %collective-permute-start.9 = (bf16[8,256,128]{2,1,0:T(8,128)(2,1)S(1)}, bf16[8,256,128]{2,1,0:T(8,128)(2,1)S(1)}, u32[]{:S(2)}, u32[]{:S(2)}) collective-permute-start(bf16[8,256,128]{2,1,0:T(8,128)(2,1)S(1)} %convert_element_type.3.own.refs_1_), channel_id=1, source_target_pairs={{4,8},{5,9},{6,10},{7,11},{8,4},{9,5},{10,6},{11,7},{20,24},{21,25... | collective-permute-start | bytes 1572872 | tf_op jit(solution)/shard_map/ppermute | solution.py:379
  22.8 18.9 %collective-permute-start.10 = (bf16[8,256,128]{2,1,0:T(8,128)(2,1)S(1)}, bf16[8,256,128]{2,1,0:T(8,128)(2,1)S(1)}, u32[]{:S(2)}, u32[]{:S(2)}) collective-permute-start(bf16[8,256,128]{2,1,0:T(8,128)(2,1)S(1)} %collective-permute-done.first.refs_2_), channel_id=1, source_target_pairs={{4,0},{5,1},{6,2},{7,3},{8,12},{9,13},{10,14},{11,15},{20,16},{21,... | collective-permute-start | bytes 1572872 | tf_op jit(solution)/shard_map/ppermute | solution.py:379
  37.5 18.5 %collective-permute-start.15 = (bf16[9,256,128]{2,1,0:T(8,128)(2,1)S(1)}, bf16[9,256,128]{2,1,0:T(8,128)(2,1)S(1)}, u32[]{:S(2)}, u32[]{:S(2)}) collective-permute-start(bf16[9,256,128]{2,1,0:T(8,128)(2,1)S(1)} %get-tuple-element.138), channel_id=1, source_target_pairs={{0,1},{1,0},{2,3},{3,2},{4,5},{5,4},{6,7},{7,6},{8,9},{9,8},{10,11... | collective-permute-start | bytes 1769480 | tf_op jit(solution)/shard_map/ppermute | solution.py:383
  43.3 12.7 %collective-permute-start.16 = (bf16[3,256,128]{2,1,0:T(8,128)(2,1)S(1)}, bf16[3,256,128]{2,1,0:T(8,128)(2,1)S(1)}, u32[]{:S(2)}, u32[]{:S(2)}) collective-permute-start(bf16[3,256,128]{2,1,0:T(8,128)(2,1)S(1)} %get-tuple-element.139), channel_id=1, source_target_pairs={{0,1},{1,0},{2,3},{3,2},{4,5},{5,4},{6,7},{7,6},{8,9},{9,8},{10,11... | collective-permute-start | bytes 589832 | tf_op jit(solution)/shard_map/ppermute | solution.py:383
  45.9 13.6 %collective-permute-start.13 = (bf16[3,256,128]{2,1,0:T(8,128)(2,1)S(1)}, bf16[3,256,128]{2,1,0:T(8,128)(2,1)S(1)}, u32[]{:S(2)}, u32[]{:S(2)}) collective-permute-start(bf16[3,256,128]{2,1,0:T(8,128)(2,1)S(1)} %get-tuple-element.136), channel_id=1, source_target_pairs={{0,2},{1,3},{2,0},{3,1},{4,6},{5,7},{6,4},{7,5},{8,10},{9,11},{10,... | collective-permute-start | bytes 589832 | tf_op jit(solution)/shard_map/ppermute | solution.py:383
  47.2 12.3 %collective-permute-start.14 = (bf16[3,256,128]{2,1,0:T(8,128)(2,1)S(1)}, bf16[3,256,128]{2,1,0:T(8,128)(2,1)S(1)}, u32[]{:S(2)}, u32[]{:S(2)}) collective-permute-start(bf16[3,256,128]{2,1,0:T(8,128)(2,1)S(1)} %get-tuple-element.137), channel_id=1, source_target_pairs={{0,3},{1,2},{2,1},{3,0},{4,7},{5,6},{6,5},{7,4},{8,11},{9,10},{10,... | collective-permute-start | bytes 589832 | tf_op jit(solution)/shard_map/ppermute | solution.py:383
  60.9 15.4 %collective-permute-start.21 = (bf16[8,256,128]{2,1,0:T(8,128)(2,1)S(1)}, bf16[8,256,128]{2,1,0:T(8,128)(2,1)S(1)}, u32[]{:S(2)}, u32[]{:S(2)}) collective-permute-start(bf16[8,256,128]{2,1,0:T(8,128)(2,1)S(1)} %get-tuple-element.149.own), channel_id=1, source_target_pairs={{0,8},{1,9},{2,10},{3,11},{12,4},{13,5},{14,6},{15,7},{4,0},{5,1},... | collective-permute-start | bytes 1572872 | tf_op jit(solution)/shard_map/ppermute | solution.py:379
  65.8 22.4 %collective-permute-start.25 = (bf16[8,256,128]{2,1,0:T(8,128)(2,1)S(1)}, bf16[8,256,128]{2,1,0:T(8,128)(2,1)S(1)}, u32[]{:S(2)}, u32[]{:S(2)}) collective-permute-start(bf16[8,256,128]{2,1,0:T(8,128)(2,1)S(1)} %get-tuple-element.149.own), channel_id=1, source_target_pairs={{0,4},{1,5},{2,6},{3,7},{12,8},{13,9},{14,10},{15,11},{4,12},{5,13... | collective-permute-start | bytes 1572872 | tf_op jit(solution)/shard_map/ppermute | solution.py:379
  75.0 16.4 %collective-permute-start.20 = (bf16[8,256,128]{2,1,0:T(8,128)(2,1)S(1)}, bf16[8,256,128]{2,1,0:T(8,128)(2,1)S(1)}, u32[]{:S(2)}, u32[]{:S(2)}) collective-permute-start(bf16[8,256,128]{2,1,0:T(8,128)(2,1)S(1)} %get-tuple-element.149.own), channel_id=1, source_target_pairs={{4,8},{5,9},{6,10},{7,11},{8,4},{9,5},{10,6},{11,7},{20,24},{21,25... | collective-permute-start | bytes 1572872 | tf_op jit(solution)/shard_map/ppermute | solution.py:379
  76.3 22.9 %collective-permute-start.22 = (bf16[8,256,128]{2,1,0:T(8,128)(2,1)S(1)}, bf16[8,256,128]{2,1,0:T(8,128)(2,1)S(1)}, u32[]{:S(2)}, u32[]{:S(2)}) collective-permute-start(bf16[8,256,128]{2,1,0:T(8,128)(2,1)S(1)} %collective-permute-done.21.refs_1_.first), channel_id=1, source_target_pairs={{4,0},{5,1},{6,2},{7,3},{8,12},{9,13},{10,14},{11,15},{20,16},{21,... | collective-permute-start | bytes 1572872 | tf_op jit(solution)/shard_map/ppermute | solution.py:379
  88.8 13.0 %collective-permute-start.28 = (bf16[6,256,128]{2,1,0:T(8,128)(2,1)S(1)}, bf16[6,256,128]{2,1,0:T(8,128)(2,1)S(1)}, u32[]{:S(2)}, u32[]{:S(2)}) collective-permute-start(bf16[6,256,128]{2,1,0:T(8,128)(2,1)S(1)} %get-tuple-element.158), channel_id=1, source_target_pairs={{0,1},{1,0},{2,3},{3,2},{4,5},{5,4},{6,7},{7,6},{8,9},{9,8},{10,11... | collective-permute-start | bytes 1179656 | tf_op jit(solution)/shard_map/ppermute | solution.py:383
  90.0 11.4 %collective-permute-start.30 = (bf16[3,256,128]{2,1,0:T(8,128)(2,1)S(1)}, bf16[3,256,128]{2,1,0:T(8,128)(2,1)S(1)}, u32[]{:S(2)}, u32[]{:S(2)}) collective-permute-start(bf16[3,256,128]{2,1,0:T(8,128)(2,1)S(1)} %get-tuple-element.164), channel_id=1, source_target_pairs={{0,2},{1,3},{2,0},{3,1},{4,6},{5,7},{6,4},{7,5},{8,10},{9,11},{10,... | collective-permute-start | bytes 589832 | tf_op jit(solution)/shard_map/ppermute | solution.py:383
  90.7 11.1 %collective-permute-start.31 = (bf16[3,256,128]{2,1,0:T(8,128)(2,1)S(1)}, bf16[3,256,128]{2,1,0:T(8,128)(2,1)S(1)}, u32[]{:S(2)}, u32[]{:S(2)}) collective-permute-start(bf16[3,256,128]{2,1,0:T(8,128)(2,1)S(1)} %get-tuple-element.165), channel_id=1, source_target_pairs={{0,3},{1,2},{2,1},{3,0},{4,7},{5,6},{6,5},{7,4},{8,11},{9,10},{10,... | collective-permute-start | bytes 589832 | tf_op jit(solution)/shard_map/ppermute | solution.py:383
  112.4 14.3 %collective-permute-start.36 = (bf16[8,256,128]{2,1,0:T(8,128)(2,1)S(1)}, bf16[8,256,128]{2,1,0:T(8,128)(2,1)S(1)}, u32[]{:S(2)}, u32[]{:S(2)}) collective-permute-start(bf16[8,256,128]{2,1,0:T(8,128)(2,1)S(1)} %get-tuple-element.174.own), channel_id=1, source_target_pairs={{0,8},{1,9},{2,10},{3,11},{12,4},{13,5},{14,6},{15,7},{4,0},{5,1},... | collective-permute-start | bytes 1572872 | tf_op jit(solution)/shard_map/ppermute | solution.py:379
  115.9 22.9 %collective-permute-start.40 = (bf16[8,256,128]{2,1,0:T(8,128)(2,1)S(1)}, bf16[8,256,128]{2,1,0:T(8,128)(2,1)S(1)}, u32[]{:S(2)}, u32[]{:S(2)}) collective-permute-start(bf16[8,256,128]{2,1,0:T(8,128)(2,1)S(1)} %get-tuple-element.174.own), channel_id=1, source_target_pairs={{0,4},{1,5},{2,6},{3,7},{12,8},{13,9},{14,10},{15,11},{4,12},{5,13... | collective-permute-start | bytes 1572872 | tf_op jit(solution)/shard_map/ppermute | solution.py:379
  125.2 16.5 %collective-permute-start.35 = (bf16[8,256,128]{2,1,0:T(8,128)(2,1)S(1)}, bf16[8,256,128]{2,1,0:T(8,128)(2,1)S(1)}, u32[]{:S(2)}, u32[]{:S(2)}) collective-permute-start(bf16[8,256,128]{2,1,0:T(8,128)(2,1)S(1)} %get-tuple-element.174.own), channel_id=1, source_target_pairs={{4,8},{5,9},{6,10},{7,11},{8,4},{9,5},{10,6},{11,7},{20,24},{21,25... | collective-permute-start | bytes 1572872 | tf_op jit(solution)/shard_map/ppermute | solution.py:379
  126.6 23.3 %collective-permute-start.37 = (bf16[8,256,128]{2,1,0:T(8,128)(2,1)S(1)}, bf16[8,256,128]{2,1,0:T(8,128)(2,1)S(1)}, u32[]{:S(2)}, u32[]{:S(2)}) collective-permute-start(bf16[8,256,128]{2,1,0:T(8,128)(2,1)S(1)} %collective-permute-done.36.refs_1_.first), channel_id=1, source_target_pairs={{4,0},{5,1},{6,2},{7,3},{8,12},{9,13},{10,14},{11,15},{20,16},{21,... | collective-permute-start | bytes 1572872 | tf_op jit(solution)/shard_map/ppermute | solution.py:379
  139.4 13.2 %collective-permute-start.43 = (bf16[6,256,128]{2,1,0:T(8,128)(2,1)S(1)}, bf16[6,256,128]{2,1,0:T(8,128)(2,1)S(1)}, u32[]{:S(2)}, u32[]{:S(2)}) collective-permute-start(bf16[6,256,128]{2,1,0:T(8,128)(2,1)S(1)} %get-tuple-element.183), channel_id=1, source_target_pairs={{0,1},{1,0},{2,3},{3,2},{4,5},{5,4},{6,7},{7,6},{8,9},{9,8},{10,11... | collective-permute-start | bytes 1179656 | tf_op jit(solution)/shard_map/ppermute | solution.py:383
  140.2 12.0 %collective-permute-start.45 = (bf16[3,256,128]{2,1,0:T(8,128)(2,1)S(1)}, bf16[3,256,128]{2,1,0:T(8,128)(2,1)S(1)}, u32[]{:S(2)}, u32[]{:S(2)}) collective-permute-start(bf16[3,256,128]{2,1,0:T(8,128)(2,1)S(1)} %get-tuple-element.189), channel_id=1, source_target_pairs={{0,2},{1,3},{2,0},{3,1},{4,6},{5,7},{6,4},{7,5},{8,10},{9,11},{10,... | collective-permute-start | bytes 589832 | tf_op jit(solution)/shard_map/ppermute | solution.py:383
  141.7 10.9 %collective-permute-start.46 = (bf16[3,256,128]{2,1,0:T(8,128)(2,1)S(1)}, bf16[3,256,128]{2,1,0:T(8,128)(2,1)S(1)}, u32[]{:S(2)}, u32[]{:S(2)}) collective-permute-start(bf16[3,256,128]{2,1,0:T(8,128)(2,1)S(1)} %get-tuple-element.190), channel_id=1, source_target_pairs={{0,3},{1,2},{2,1},{3,0},{4,7},{5,6},{6,5},{7,4},{8,11},{9,10},{10,... | collective-permute-start | bytes 589832 | tf_op jit(solution)/shard_map/ppermute | solution.py:383
  163.1 14.3 %collective-permute-start.51 = (bf16[8,256,128]{2,1,0:T(8,128)(2,1)S(1)}, bf16[8,256,128]{2,1,0:T(8,128)(2,1)S(1)}, u32[]{:S(2)}, u32[]{:S(2)}) collective-permute-start(bf16[8,256,128]{2,1,0:T(8,128)(2,1)S(1)} %get-tuple-element.199.own), channel_id=1, source_target_pairs={{0,8},{1,9},{2,10},{3,11},{12,4},{13,5},{14,6},{15,7},{4,0},{5,1},... | collective-permute-start | bytes 1572872 | tf_op jit(solution)/shard_map/ppermute | solution.py:379
  166.7 22.9 %collective-permute-start.55 = (bf16[8,256,128]{2,1,0:T(8,128)(2,1)S(1)}, bf16[8,256,128]{2,1,0:T(8,128)(2,1)S(1)}, u32[]{:S(2)}, u32[]{:S(2)}) collective-permute-start(bf16[8,256,128]{2,1,0:T(8,128)(2,1)S(1)} %get-tuple-element.199.own), channel_id=1, source_target_pairs={{0,4},{1,5},{2,6},{3,7},{12,8},{13,9},{14,10},{15,11},{4,12},{5,13... | collective-permute-start | bytes 1572872 | tf_op jit(solution)/shard_map/ppermute | solution.py:379
  175.9 16.5 %collective-permute-start.50 = (bf16[8,256,128]{2,1,0:T(8,128)(2,1)S(1)}, bf16[8,256,128]{2,1,0:T(8,128)(2,1)S(1)}, u32[]{:S(2)}, u32[]{:S(2)}) collective-permute-start(bf16[8,256,128]{2,1,0:T(8,128)(2,1)S(1)} %get-tuple-element.199.own), channel_id=1, source_target_pairs={{4,8},{5,9},{6,10},{7,11},{8,4},{9,5},{10,6},{11,7},{20,24},{21,25... | collective-permute-start | bytes 1572872 | tf_op jit(solution)/shard_map/ppermute | solution.py:379
  177.4 23.3 %collective-permute-start.52 = (bf16[8,256,128]{2,1,0:T(8,128)(2,1)S(1)}, bf16[8,256,128]{2,1,0:T(8,128)(2,1)S(1)}, u32[]{:S(2)}, u32[]{:S(2)}) collective-permute-start(bf16[8,256,128]{2,1,0:T(8,128)(2,1)S(1)} %collective-permute-done.51.refs_1_.first), channel_id=1, source_target_pairs={{4,0},{5,1},{6,2},{7,3},{8,12},{9,13},{10,14},{11,15},{20,16},{21,... | collective-permute-start | bytes 1572872 | tf_op jit(solution)/shard_map/ppermute | solution.py:379
  190.2 13.1 %collective-permute-start.58 = (bf16[6,256,128]{2,1,0:T(8,128)(2,1)S(1)}, bf16[6,256,128]{2,1,0:T(8,128)(2,1)S(1)}, u32[]{:S(2)}, u32[]{:S(2)}) collective-permute-start(bf16[6,256,128]{2,1,0:T(8,128)(2,1)S(1)} %get-tuple-element.208), channel_id=1, source_target_pairs={{0,1},{1,0},{2,3},{3,2},{4,5},{5,4},{6,7},{7,6},{8,9},{9,8},{10,11... | collective-permute-start | bytes 1179656 | tf_op jit(solution)/shard_map/ppermute | solution.py:383
  190.9 12.0 %collective-permute-start.60 = (bf16[3,256,128]{2,1,0:T(8,128)(2,1)S(1)}, bf16[3,256,128]{2,1,0:T(8,128)(2,1)S(1)}, u32[]{:S(2)}, u32[]{:S(2)}) collective-permute-start(bf16[3,256,128]{2,1,0:T(8,128)(2,1)S(1)} %get-tuple-element.214), channel_id=1, source_target_pairs={{0,2},{1,3},{2,0},{3,1},{4,6},{5,7},{6,4},{7,5},{8,10},{9,11},{10,... | collective-permute-start | bytes 589832 | tf_op jit(solution)/shard_map/ppermute | solution.py:383
  192.4 10.9 %collective-permute-start.61 = (bf16[3,256,128]{2,1,0:T(8,128)(2,1)S(1)}, bf16[3,256,128]{2,1,0:T(8,128)(2,1)S(1)}, u32[]{:S(2)}, u32[]{:S(2)}) collective-permute-start(bf16[3,256,128]{2,1,0:T(8,128)(2,1)S(1)} %get-tuple-element.215), channel_id=1, source_target_pairs={{0,3},{1,2},{2,1},{3,0},{4,7},{5,6},{6,5},{7,4},{8,11},{9,10},{10,... | collective-permute-start | bytes 589832 | tf_op jit(solution)/shard_map/ppermute | solution.py:383
  214.1 11.2 %all-to-all-start = ((f32[16,1,128]{2,1,0:T(1,128)}), f32[16,1,128]{2,1,0:T(1,128)S(1)}, u32[]{:S(2)}, u32[]{:S(2)}) async-start(f32[16,1,128]{2,1,0:T(1,128)} %broadcast_in_dim.2), calls=%async_computation | async-start | bytes 16384 | tf_op jit(solution)/shard_map/all_to_all | solution.py:389
  (37 other events, 238.4 us)

commit v17 on v16

--- a/solution.py
+++ b/solution.py
@@ -332,14 +332,16 @@
     total = jnp.zeros(xpos.shape[1:], jnp.float32)
     for b in range(xpos.shape[0]):
         total += xpos[b] * acc[b]
-    energy[...] = -0.5 * jnp.sum(total, axis=0, keepdims=True)
+    part = -0.5 * jnp.sum(total, axis=0, keepdims=True)
+    for i in range(energy.shape[0]):
+        energy[i] = part
 
 
 def last_field(layout, table, tiles, sources, field, xpos):
     return pl.pallas_call(
         functools.partial(energy_kernel, layout),
         out_shape=(
-            jax.ShapeDtypeStruct((1, xpos.shape[2]), jnp.float32),
+            jax.ShapeDtypeStruct((16, 1, xpos.shape[2]), jnp.float32),
             jax.ShapeDtypeStruct(field.shape, jnp.float32),
         ),
         in_specs=[SMEM] + [VMEM] * (1 + len(sources) + 2),
@@ -383,10 +385,8 @@
     return lax.ppermute(value, "row", [(i, i ^ flip) for i in range(16)])
 
 
-def row_sum(part):
-    devices = lax.axis_size("row")
-    spread = jnp.broadcast_to(part, (devices,) + part.shape[1:])
-    return jnp.sum(lax.all_to_all(spread, "row", split_axis=0, concat_axis=0, tiled=True), axis=0, keepdims=True)
+def row_sum(parts):
+    return jnp.sum(lax.all_to_all(parts, "row", split_axis=0, concat_axis=0, tiled=True), axis=0)
 
 
 def body_16(tiles, tile_rows, tile_cols, counts, positions, momenta):
@@ -453,9 +453,11 @@
         got3 = to_other_y(packs3)
         if step == 0:
             got2, half = lax.optimization_barrier((got2, half))
+            sums = across(8, half)
         field = early(layout, parts, table, tiles, [own0, own1, own2, mid, out, core, core3] + got + got2 + cores)
         if step == 0:
-            total = (half + across(8, half))[0, SUM_AT]
+            field, sums = lax.optimization_barrier((field, sums))
+            total = (half + sums)[0, SUM_AT]
             coeff = 0.7 * jnp.sqrt((order - 1) / total)
         scalars = jnp.stack([jnp.float32(0.4 - 0.1 * step), coeff])
         if last:

time: 226 us -> 226 us (level)
    ppermute x46, waiting for transfers between devices: 83.7 us -> 81.4 us  [across(): return lax.ppermute(value, 'row', [(i, i ^ flip) for i in range(16)])]
where the time goes in v17:
time: 226 us; the launch traced here: 225 us
  waiting for transfers between devices  124 us (55%)
  starting transfers between devices  58.7 us (26%)
  Pallas kernels  34 us (15%)
  local copies, waits for them, and re-layouts  4.06 us (2%)
  between operations  2.41 us (1%)
    ppermute x46, waiting for transfers between devices, across(): return lax.ppermute(value, 'row', [(i, i ^ flip) for i in range(16)])  81.4 us
    ppermute x16, waiting for transfers between devices, along_z(): lax.ppermute(value, 'row', [(a * 4 + i, b * 4 + i) for a, b in pairs for...  38.1 us
    ppermute x46, starting transfers between devices, across(): return lax.ppermute(value, 'row', [(i, i ^ flip) for i in range(16)])  35.2 us
    ppermute x16, starting transfers between devices, along_z(): lax.ppermute(value, 'row', [(a * 4 + i, b * 4 + i) for a, b in pairs for...  18.8 us
    pallas_call x4, Pallas kernels, early(): pl.pallas_call(functools.partial(early_kernel, layout, parts), out_shape=...  13.9 us
    pallas_call x11, Pallas kernels, pack(): pl.pallas_call(picked, out_shape=[jax.ShapeDtypeStruct((size, tile, repl)...  6.59 us
    all_to_all x1, starting transfers between devices, row_sum(): lax.all_to_all(parts, 'row', split_axis=0, concat_axis=0, tiled=True)  4.74 us
  transfers between devices with their start and end apart: 63, of which 38 were waited for; matrix products, arithmetic and copies ran while one was open for 0% of the time, Pallas kernels for 12%

profile of v17, /device:TPU:0, one launch (start us, length us, event | category | flops | bytes accessed | tf_op | source)
XLA Modules:
  0.0 225.2 jit_solution(13142749856264720106)
XLA Ops:
  1.9 4.1 %collective-permute-start = (bf16[8,256,128]{2,1,0:T(8,128)(2,1)S(1)}, bf16[8,256,128]{2,1,0:T(8,128)(2,1)S(1)}, u32[]{:S(2)}, u32[]{:S(2)}) collective-permute-start(bf16[8,256,128]{2,1,0:T(8,128)(2,1)S(1)} %convert_element_type.3.own.refs_1_), channel_id=1, source_target_pairs={{0,8},{1,9},{2,10},{3,11},{12,4},{13,5},{14,6},{15,7},{4,0},{5,1},... | collective-permute-start | bytes 1572872 | tf_op jit(solution)/shard_map/ppermute | solution.py:381
  6.7 4.2 %shard_map.85 = (s32[144]{0:T(256)}, f32[1,128]{1,0:T(1,128)}) custom-call(s32[48]{0:T(128)} %rows.1, s32[48]{0:T(128)} %cols.1, s32[1]{0:T(128)S(6)} %copy.9.count, bf16[48,256,256]{2,1,0:T(8,128)(2,1)} %tiles.19), custom_call_target="tpu_custom_call" | custom-call | tf_op jit(solution)/shard_map/pallas_call | solution.py:131
  24.1 6.2 %collective-permute-done.4.own.refs_3_.second = bf16[8,256,128]{2,1,0:T(8,128)(2,1)S(1)} collective-permute-done((bf16[8,256,128]{2,1,0:T(8,128)(2,1)S(1)}, bf16[8,256,128]{2,1,0:T(8,128)(2,1)S(1)}, u32[]{:S(2)}, u32[]{:S(2)}) %collective-permute-start.4) | collective-permute-done | bytes 524320 | tf_op jit(solution)/shard_map/ppermute | solution.py:381
  30.3 2.8 %copy-done = bf16[48,256,256]{2,1,0:T(8,128)(2,1)S(1)} copy-done((bf16[48,256,256]{2,1,0:T(8,128)(2,1)S(1)}, bf16[48,256,256]{2,1,0:T(8,128)(2,1)}, u32[]{:S(2)}) %copy-start) | copy-done | bytes 6291480
  33.1 3.8 %collective-permute-done.6.refs_1_ = bf16[6,256,128]{2,1,0:T(8,128)(2,1)S(1)} collective-permute-done((bf16[6,256,128]{2,1,0:T(8,128)(2,1)S(1)}, bf16[6,256,128]{2,1,0:T(8,128)(2,1)S(1)}, u32[]{:S(2)}, u32[]{:S(2)}) %collective-permute-start.6) | collective-permute-done | bytes 393248 | tf_op jit(solution)/shard_map/ppermute | solution.py:385
  47.3 2.4 %collective-permute-done.8.refs_3_ = bf16[3,256,128]{2,1,0:T(8,128)(2,1)S(1)} collective-permute-done((bf16[3,256,128]{2,1,0:T(8,128)(2,1)S(1)}, bf16[3,256,128]{2,1,0:T(8,128)(2,1)S(1)}, u32[]{:S(2)}, u32[]{:S(2)}) %collective-permute-start.8) | collective-permute-done | bytes 196640 | tf_op jit(solution)/shard_map/ppermute | solution.py:385
  49.7 3.4 %collective-permute-start.14 = (f32[1,128]{1,0:T(1,128)S(1)}, f32[1,128]{1,0:T(1,128)S(1)}, u32[]{:S(2)}, u32[]{:S(2)}) collective-permute-start(f32[1,128]{1,0:T(1,128)S(1)} %add.18), channel_id=1, source_target_pairs={{0,8},{1,9},{2,10},{3,11},{4,12},{5,13},{6,14},{7,15},{8,0},{9,1},... | collective-permute-start | bytes 1544 | tf_op jit(solution)/shard_map/ppermute | solution.py:385
  53.1 3.5 %shard_map.90.field = f32[9,256,128]{2,1,0:T(8,128)S(1)} custom-call(s32[180]{0:T(256)S(1)} %get-tuple-element.126.refs_0_.table, bf16[48,256,256]{2,1,0:T(8,128)(2,1)S(1)} %copy-done.1, bf16[8,256,128]{2,1,0:T(8,128)(2,1)S(1)} %convert_element_type.3.own.refs_1_, bf16[8,256,128]{2,1,0:T(8,128)(2,1)S(1)} %collective-permute-done.first.refs_2_, ...), custom_call_target="tpu_custom_call" | custom-call | tf_op jit(solution)/shard_map/pallas_call | solution.py:281
  59.5 2.7 %collective-permute-start.21 = (bf16[8,256,128]{2,1,0:T(8,128)(2,1)S(1)}, bf16[8,256,128]{2,1,0:T(8,128)(2,1)S(1)}, u32[]{:S(2)}, u32[]{:S(2)}) collective-permute-start(bf16[8,256,128]{2,1,0:T(8,128)(2,1)S(1)} %get-tuple-element.153.own), channel_id=1, source_target_pairs={{0,8},{1,9},{2,10},{3,11},{12,4},{13,5},{14,6},{15,7},{4,0},{5,1},... | collective-permute-start | bytes 1572872 | tf_op jit(solution)/shard_map/ppermute | solution.py:381
  64.1 6.3 %collective-permute-done.18.refs_0_ = bf16[3,256,128]{2,1,0:T(8,128)(2,1)S(1)} collective-permute-done((bf16[3,256,128]{2,1,0:T(8,128)(2,1)S(1)}, bf16[3,256,128]{2,1,0:T(8,128)(2,1)S(1)}, u32[]{:S(2)}, u32[]{:S(2)}) %collective-permute-start.18) | collective-permute-done | bytes 196640 | tf_op jit(solution)/shard_map/ppermute | solution.py:385
  70.4 2.5 %collective-permute-done.19.refs_1_ = bf16[3,256,128]{2,1,0:T(8,128)(2,1)S(1)} collective-permute-done((bf16[3,256,128]{2,1,0:T(8,128)(2,1)S(1)}, bf16[3,256,128]{2,1,0:T(8,128)(2,1)S(1)}, u32[]{:S(2)}, u32[]{:S(2)}) %collective-permute-start.19) | collective-permute-done | bytes 196640 | tf_op jit(solution)/shard_map/ppermute | solution.py:385
  77.9 6.3 %collective-permute-done.26.refs_2_ = bf16[3,256,128]{2,1,0:T(8,128)(2,1)S(1)} collective-permute-done((bf16[3,256,128]{2,1,0:T(8,128)(2,1)S(1)}, bf16[3,256,128]{2,1,0:T(8,128)(2,1)S(1)}, u32[]{:S(2)}, u32[]{:S(2)}) %collective-permute-start.26) | collective-permute-done | bytes 196640 | tf_op jit(solution)/shard_map/ppermute | solution.py:385
  89.9 8.6 %collective-permute-done.22.refs_2_.out = bf16[8,256,128]{2,1,0:T(8,128)(2,1)S(1)} collective-permute-done((bf16[8,256,128]{2,1,0:T(8,128)(2,1)S(1)}, bf16[8,256,128]{2,1,0:T(8,128)(2,1)S(1)}, u32[]{:S(2)}, u32[]{:S(2)}) %collective-permute-start.22) | collective-permute-done | bytes 524320 | tf_op jit(solution)/shard_map/ppermute | solution.py:381
  101.2 3.5 %shard_map.95.field = f32[9,256,128]{2,1,0:T(8,128)S(1)} custom-call(s32[180]{0:T(256)S(1)} %get-tuple-element.126.refs_0_.table, bf16[48,256,256]{2,1,0:T(8,128)(2,1)S(1)} %copy-done.1, bf16[8,256,128]{2,1,0:T(8,128)(2,1)S(1)} %get-tuple-element.153.own, bf16[8,256,128]{2,1,0:T(8,128)(2,1)S(1)} %collective-permute-done.21.refs_1_.first, ...), custom_call_target="tpu_custom_call" | custom-call | tf_op jit(solution)/shard_map/pallas_call | solution.py:281
  104.7 2.3 %collective-permute-done.23.got2 = bf16[3,256,128]{2,1,0:T(8,128)(2,1)S(1)} collective-permute-done((bf16[3,256,128]{2,1,0:T(8,128)(2,1)S(1)}, bf16[3,256,128]{2,1,0:T(8,128)(2,1)S(1)}, u32[]{:S(2)}, u32[]{:S(2)}) %collective-permute-start.23) | collective-permute-done | bytes 196640 | tf_op jit(solution)/shard_map/ppermute | solution.py:385
  107.0 3.3 %collective-permute-done.24.got3 = bf16[3,256,128]{2,1,0:T(8,128)(2,1)S(1)} collective-permute-done((bf16[3,256,128]{2,1,0:T(8,128)(2,1)S(1)}, bf16[3,256,128]{2,1,0:T(8,128)(2,1)S(1)}, u32[]{:S(2)}, u32[]{:S(2)}) %collective-permute-start.24) | collective-permute-done | bytes 196640 | tf_op jit(solution)/shard_map/ppermute | solution.py:385
  115.7 5.4 %collective-permute-done.33.refs_0_ = bf16[3,256,128]{2,1,0:T(8,128)(2,1)S(1)} collective-permute-done((bf16[3,256,128]{2,1,0:T(8,128)(2,1)S(1)}, bf16[3,256,128]{2,1,0:T(8,128)(2,1)S(1)}, u32[]{:S(2)}, u32[]{:S(2)}) %collective-permute-start.33) | collective-permute-done | bytes 196640 | tf_op jit(solution)/shard_map/ppermute | solution.py:385
  121.1 3.4 %collective-permute-done.34.refs_1_ = bf16[3,256,128]{2,1,0:T(8,128)(2,1)S(1)} collective-permute-done((bf16[3,256,128]{2,1,0:T(8,128)(2,1)S(1)}, bf16[3,256,128]{2,1,0:T(8,128)(2,1)S(1)}, u32[]{:S(2)}, u32[]{:S(2)}) %collective-permute-start.34) | collective-permute-done | bytes 196640 | tf_op jit(solution)/shard_map/ppermute | solution.py:385
  129.4 6.3 %collective-permute-done.41.refs_2_ = bf16[3,256,128]{2,1,0:T(8,128)(2,1)S(1)} collective-permute-done((bf16[3,256,128]{2,1,0:T(8,128)(2,1)S(1)}, bf16[3,256,128]{2,1,0:T(8,128)(2,1)S(1)}, u32[]{:S(2)}, u32[]{:S(2)}) %collective-permute-start.41) | collective-permute-done | bytes 196640 | tf_op jit(solution)/shard_map/ppermute | solution.py:385
  141.0 8.3 %collective-permute-done.37.refs_2_.out = bf16[8,256,128]{2,1,0:T(8,128)(2,1)S(1)} collective-permute-done((bf16[8,256,128]{2,1,0:T(8,128)(2,1)S(1)}, bf16[8,256,128]{2,1,0:T(8,128)(2,1)S(1)}, u32[]{:S(2)}, u32[]{:S(2)}) %collective-permute-start.37) | collective-permute-done | bytes 524320 | tf_op jit(solution)/shard_map/ppermute | solution.py:381
  151.9 3.5 %shard_map.100.field = f32[9,256,128]{2,1,0:T(8,128)S(1)} custom-call(s32[180]{0:T(256)S(1)} %get-tuple-element.126.refs_0_.table, bf16[48,256,256]{2,1,0:T(8,128)(2,1)S(1)} %copy-done.1, bf16[8,256,128]{2,1,0:T(8,128)(2,1)S(1)} %get-tuple-element.178.own, bf16[8,256,128]{2,1,0:T(8,128)(2,1)S(1)} %collective-permute-done.36.refs_1_.first, ...), custom_call_target="tpu_custom_call" | custom-call | tf_op jit(solution)/shard_map/pallas_call | solution.py:281
  155.4 2.3 %collective-permute-done.38.got2 = bf16[3,256,128]{2,1,0:T(8,128)(2,1)S(1)} collective-permute-done((bf16[3,256,128]{2,1,0:T(8,128)(2,1)S(1)}, bf16[3,256,128]{2,1,0:T(8,128)(2,1)S(1)}, u32[]{:S(2)}, u32[]{:S(2)}) %collective-permute-start.38) | collective-permute-done | bytes 196640 | tf_op jit(solution)/shard_map/ppermute | solution.py:385
  157.7 3.3 %collective-permute-done.39.got3 = bf16[3,256,128]{2,1,0:T(8,128)(2,1)S(1)} collective-permute-done((bf16[3,256,128]{2,1,0:T(8,128)(2,1)S(1)}, bf16[3,256,128]{2,1,0:T(8,128)(2,1)S(1)}, u32[]{:S(2)}, u32[]{:S(2)}) %collective-permute-start.39) | collective-permute-done | bytes 196640 | tf_op jit(solution)/shard_map/ppermute | solution.py:385
  166.4 5.4 %collective-permute-done.48.refs_0_ = bf16[3,256,128]{2,1,0:T(8,128)(2,1)S(1)} collective-permute-done((bf16[3,256,128]{2,1,0:T(8,128)(2,1)S(1)}, bf16[3,256,128]{2,1,0:T(8,128)(2,1)S(1)}, u32[]{:S(2)}, u32[]{:S(2)}) %collective-permute-start.48) | collective-permute-done | bytes 196640 | tf_op jit(solution)/shard_map/ppermute | solution.py:385
  171.8 3.4 %collective-permute-done.49.refs_1_ = bf16[3,256,128]{2,1,0:T(8,128)(2,1)S(1)} collective-permute-done((bf16[3,256,128]{2,1,0:T(8,128)(2,1)S(1)}, bf16[3,256,128]{2,1,0:T(8,128)(2,1)S(1)}, u32[]{:S(2)}, u32[]{:S(2)}) %collective-permute-start.49) | collective-permute-done | bytes 196640 | tf_op jit(solution)/shard_map/ppermute | solution.py:385
  180.1 6.3 %collective-permute-done.56.refs_2_ = bf16[3,256,128]{2,1,0:T(8,128)(2,1)S(1)} collective-permute-done((bf16[3,256,128]{2,1,0:T(8,128)(2,1)S(1)}, bf16[3,256,128]{2,1,0:T(8,128)(2,1)S(1)}, u32[]{:S(2)}, u32[]{:S(2)}) %collective-permute-start.56) | collective-permute-done | bytes 196640 | tf_op jit(solution)/shard_map/ppermute | solution.py:385
  191.7 8.3 %collective-permute-done.52.refs_2_.out = bf16[8,256,128]{2,1,0:T(8,128)(2,1)S(1)} collective-permute-done((bf16[8,256,128]{2,1,0:T(8,128)(2,1)S(1)}, bf16[8,256,128]{2,1,0:T(8,128)(2,1)S(1)}, u32[]{:S(2)}, u32[]{:S(2)}) %collective-permute-start.52) | collective-permute-done | bytes 524320 | tf_op jit(solution)/shard_map/ppermute | solution.py:381
  202.6 3.5 %shard_map.105.field = f32[9,256,128]{2,1,0:T(8,128)S(1)} custom-call(s32[180]{0:T(256)S(1)} %get-tuple-element.126.refs_0_.table, bf16[48,256,256]{2,1,0:T(8,128)(2,1)S(1)} %copy-done.1, bf16[8,256,128]{2,1,0:T(8,128)(2,1)S(1)} %get-tuple-element.203.own, bf16[8,256,128]{2,1,0:T(8,128)(2,1)S(1)} %collective-permute-done.51.refs_1_.first, ...), custom_call_target="tpu_custom_call" | custom-call | tf_op jit(solution)/shard_map/pallas_call | solution.py:281
  206.1 2.4 %collective-permute-done.53.got2 = bf16[3,256,128]{2,1,0:T(8,128)(2,1)S(1)} collective-permute-done((bf16[3,256,128]{2,1,0:T(8,128)(2,1)S(1)}, bf16[3,256,128]{2,1,0:T(8,128)(2,1)S(1)}, u32[]{:S(2)}, u32[]{:S(2)}) %collective-permute-start.53) | collective-permute-done | bytes 196640 | tf_op jit(solution)/shard_map/ppermute | solution.py:385
  208.5 3.3 %collective-permute-done.54.got3 = bf16[3,256,128]{2,1,0:T(8,128)(2,1)S(1)} collective-permute-done((bf16[3,256,128]{2,1,0:T(8,128)(2,1)S(1)}, bf16[3,256,128]{2,1,0:T(8,128)(2,1)S(1)}, u32[]{:S(2)}, u32[]{:S(2)}) %collective-permute-start.54) | collective-permute-done | bytes 196640 | tf_op jit(solution)/shard_map/ppermute | solution.py:385
  213.5 4.7 %all-to-all-start = ((f32[16,1,128]{2,1,0:T(1,128)}), f32[16,1,128]{2,1,0:T(1,128)S(1)}, u32[]{:S(2)}, u32[]{:S(2)}) async-start(f32[16,1,128]{2,1,0:T(1,128)} %get-tuple-element.226), calls=%async_computation | async-start | bytes 16384 | tf_op jit(solution)/shard_map/all_to_all | solution.py:389
  220.3 4.3 %all-to-all-done = f32[16,1,128]{2,1,0:T(1,128)S(1)} async-done(((f32[16,1,128]{2,1,0:T(1,128)}), f32[16,1,128]{2,1,0:T(1,128)S(1)}, u32[]{:S(2)}, u32[]{:S(2)}) %all-to-all-start) | async-done | bytes 8224 | tf_op jit(solution)/shard_map/all_to_all | solution.py:389
  (139 shorter events, 82.6 us)
Async XLA Ops:
  1.9 16.5 %collective-permute-start = (bf16[8,256,128]{2,1,0:T(8,128)(2,1)S(1)}, bf16[8,256,128]{2,1,0:T(8,128)(2,1)S(1)}, u32[]{:S(2)}, u32[]{:S(2)}) collective-permute-start(bf16[8,256,128]{2,1,0:T(8,128)(2,1)S(1)} %convert_element_type.3.own.refs_1_), channel_id=1, source_target_pairs={{0,8},{1,9},{2,10},{3,11},{12,4},{13,5},{14,6},{15,7},{4,0},{5,1},... | collective-permute-start | bytes 1572872 | tf_op jit(solution)/shard_map/ppermute | solution.py:381
  12.2 18.1 %collective-permute-start.4 = (bf16[8,256,128]{2,1,0:T(8,128)(2,1)S(1)}, bf16[8,256,128]{2,1,0:T(8,128)(2,1)S(1)}, u32[]{:S(2)}, u32[]{:S(2)}) collective-permute-start(bf16[8,256,128]{2,1,0:T(8,128)(2,1)S(1)} %convert_element_type.3.own.refs_1_), channel_id=1, source_target_pairs={{0,4},{1,5},{2,6},{3,7},{12,8},{13,9},{14,10},{15,11},{4,12},{5,13... | collective-permute-start | bytes 1572872 | tf_op jit(solution)/shard_map/ppermute | solution.py:381
  20.5 12.6 %collective-permute-start.5 = (bf16[6,256,128]{2,1,0:T(8,128)(2,1)S(1)}, bf16[6,256,128]{2,1,0:T(8,128)(2,1)S(1)}, u32[]{:S(2)}, u32[]{:S(2)}) collective-permute-start(bf16[6,256,128]{2,1,0:T(8,128)(2,1)S(1)} %get-tuple-element.127), channel_id=1, source_target_pairs={{0,2},{1,3},{2,0},{3,1},{4,6},{5,7},{6,4},{7,5},{8,10},{9,11},{10,... | collective-permute-start | bytes 1179656 | tf_op jit(solution)/shard_map/ppermute | solution.py:385
  22.1 14.8 %collective-permute-start.6 = (bf16[6,256,128]{2,1,0:T(8,128)(2,1)S(1)}, bf16[6,256,128]{2,1,0:T(8,128)(2,1)S(1)}, u32[]{:S(2)}, u32[]{:S(2)}) collective-permute-start(bf16[6,256,128]{2,1,0:T(8,128)(2,1)S(1)} %get-tuple-element.128), channel_id=1, source_target_pairs={{0,3},{1,2},{2,1},{3,0},{4,7},{5,6},{6,5},{7,4},{8,11},{9,10},{10,... | collective-permute-start | bytes 1179656 | tf_op jit(solution)/shard_map/ppermute | solution.py:385
  22.1 18.8 %collective-permute-start.9 = (bf16[8,256,128]{2,1,0:T(8,128)(2,1)S(1)}, bf16[8,256,128]{2,1,0:T(8,128)(2,1)S(1)}, u32[]{:S(2)}, u32[]{:S(2)}) collective-permute-start(bf16[8,256,128]{2,1,0:T(8,128)(2,1)S(1)} %convert_element_type.3.own.refs_1_), channel_id=1, source_target_pairs={{4,8},{5,9},{6,10},{7,11},{8,4},{9,5},{10,6},{11,7},{20,24},{21,25... | collective-permute-start | bytes 1572872 | tf_op jit(solution)/shard_map/ppermute | solution.py:381
  22.8 18.9 %collective-permute-start.10 = (bf16[8,256,128]{2,1,0:T(8,128)(2,1)S(1)}, bf16[8,256,128]{2,1,0:T(8,128)(2,1)S(1)}, u32[]{:S(2)}, u32[]{:S(2)}) collective-permute-start(bf16[8,256,128]{2,1,0:T(8,128)(2,1)S(1)} %collective-permute-done.first.refs_2_), channel_id=1, source_target_pairs={{4,0},{5,1},{6,2},{7,3},{8,12},{9,13},{10,14},{11,15},{20,16},{21,... | collective-permute-start | bytes 1572872 | tf_op jit(solution)/shard_map/ppermute | solution.py:381
  37.5 15.6 %collective-permute-start.12 = (bf16[9,256,128]{2,1,0:T(8,128)(2,1)S(1)}, bf16[9,256,128]{2,1,0:T(8,128)(2,1)S(1)}, u32[]{:S(2)}, u32[]{:S(2)}) collective-permute-start(bf16[9,256,128]{2,1,0:T(8,128)(2,1)S(1)} %get-tuple-element.138), channel_id=1, source_target_pairs={{0,1},{1,0},{2,3},{3,2},{4,5},{5,4},{6,7},{7,6},{8,9},{9,8},{10,11... | collective-permute-start | bytes 1769480 | tf_op jit(solution)/shard_map/ppermute | solution.py:385
  42.3 10.8 %collective-permute-start.13 = (bf16[3,256,128]{2,1,0:T(8,128)(2,1)S(1)}, bf16[3,256,128]{2,1,0:T(8,128)(2,1)S(1)}, u32[]{:S(2)}, u32[]{:S(2)}) collective-permute-start(bf16[3,256,128]{2,1,0:T(8,128)(2,1)S(1)} %get-tuple-element.139), channel_id=1, source_target_pairs={{0,1},{1,0},{2,3},{3,2},{4,5},{5,4},{6,7},{7,6},{8,9},{9,8},{10,11... | collective-permute-start | bytes 589832 | tf_op jit(solution)/shard_map/ppermute | solution.py:385
  46.0 12.0 %collective-permute-start.15 = (bf16[3,256,128]{2,1,0:T(8,128)(2,1)S(1)}, bf16[3,256,128]{2,1,0:T(8,128)(2,1)S(1)}, u32[]{:S(2)}, u32[]{:S(2)}) collective-permute-start(bf16[3,256,128]{2,1,0:T(8,128)(2,1)S(1)} %get-tuple-element.145), channel_id=1, source_target_pairs={{0,2},{1,3},{2,0},{3,1},{4,6},{5,7},{6,4},{7,5},{8,10},{9,11},{10,... | collective-permute-start | bytes 589832 | tf_op jit(solution)/shard_map/ppermute | solution.py:385
  47.2 10.9 %collective-permute-start.16 = (bf16[3,256,128]{2,1,0:T(8,128)(2,1)S(1)}, bf16[3,256,128]{2,1,0:T(8,128)(2,1)S(1)}, u32[]{:S(2)}, u32[]{:S(2)}) collective-permute-start(bf16[3,256,128]{2,1,0:T(8,128)(2,1)S(1)} %get-tuple-element.146), channel_id=1, source_target_pairs={{0,3},{1,2},{2,1},{3,0},{4,7},{5,6},{6,5},{7,4},{8,11},{9,10},{10,... | collective-permute-start | bytes 589832 | tf_op jit(solution)/shard_map/ppermute | solution.py:385
  59.5 15.1 %collective-permute-start.21 = (bf16[8,256,128]{2,1,0:T(8,128)(2,1)S(1)}, bf16[8,256,128]{2,1,0:T(8,128)(2,1)S(1)}, u32[]{:S(2)}, u32[]{:S(2)}) collective-permute-start(bf16[8,256,128]{2,1,0:T(8,128)(2,1)S(1)} %get-tuple-element.153.own), channel_id=1, source_target_pairs={{0,8},{1,9},{2,10},{3,11},{12,4},{13,5},{14,6},{15,7},{4,0},{5,1},... | collective-permute-start | bytes 1572872 | tf_op jit(solution)/shard_map/ppermute | solution.py:381
  64.1 23.3 %collective-permute-start.25 = (bf16[8,256,128]{2,1,0:T(8,128)(2,1)S(1)}, bf16[8,256,128]{2,1,0:T(8,128)(2,1)S(1)}, u32[]{:S(2)}, u32[]{:S(2)}) collective-permute-start(bf16[8,256,128]{2,1,0:T(8,128)(2,1)S(1)} %get-tuple-element.153.own), channel_id=1, source_target_pairs={{0,4},{1,5},{2,6},{3,7},{12,8},{13,9},{14,10},{15,11},{4,12},{5,13... | collective-permute-start | bytes 1572872 | tf_op jit(solution)/shard_map/ppermute | solution.py:381
  72.9 17.1 %collective-permute-start.20 = (bf16[8,256,128]{2,1,0:T(8,128)(2,1)S(1)}, bf16[8,256,128]{2,1,0:T(8,128)(2,1)S(1)}, u32[]{:S(2)}, u32[]{:S(2)}) collective-permute-start(bf16[8,256,128]{2,1,0:T(8,128)(2,1)S(1)} %get-tuple-element.153.own), channel_id=1, source_target_pairs={{4,8},{5,9},{6,10},{7,11},{8,4},{9,5},{10,6},{11,7},{20,24},{21,25... | collective-permute-start | bytes 1572872 | tf_op jit(solution)/shard_map/ppermute | solution.py:381
  74.6 24.0 %collective-permute-start.22 = (bf16[8,256,128]{2,1,0:T(8,128)(2,1)S(1)}, bf16[8,256,128]{2,1,0:T(8,128)(2,1)S(1)}, u32[]{:S(2)}, u32[]{:S(2)}) collective-permute-start(bf16[8,256,128]{2,1,0:T(8,128)(2,1)S(1)} %collective-permute-done.21.refs_1_.first), channel_id=1, source_target_pairs={{4,0},{5,1},{6,2},{7,3},{8,12},{9,13},{10,14},{11,15},{20,16},{21,... | collective-permute-start | bytes 1572872 | tf_op jit(solution)/shard_map/ppermute | solution.py:381
  88.0 13.2 %collective-permute-start.28 = (bf16[6,256,128]{2,1,0:T(8,128)(2,1)S(1)}, bf16[6,256,128]{2,1,0:T(8,128)(2,1)S(1)}, u32[]{:S(2)}, u32[]{:S(2)}) collective-permute-start(bf16[6,256,128]{2,1,0:T(8,128)(2,1)S(1)} %get-tuple-element.162), channel_id=1, source_target_pairs={{0,1},{1,0},{2,3},{3,2},{4,5},{5,4},{6,7},{7,6},{8,9},{9,8},{10,11... | collective-permute-start | bytes 1179656 | tf_op jit(solution)/shard_map/ppermute | solution.py:385
  88.3 12.4 %collective-permute-start.30 = (bf16[3,256,128]{2,1,0:T(8,128)(2,1)S(1)}, bf16[3,256,128]{2,1,0:T(8,128)(2,1)S(1)}, u32[]{:S(2)}, u32[]{:S(2)}) collective-permute-start(bf16[3,256,128]{2,1,0:T(8,128)(2,1)S(1)} %get-tuple-element.168), channel_id=1, source_target_pairs={{0,2},{1,3},{2,0},{3,1},{4,6},{5,7},{6,4},{7,5},{8,10},{9,11},{10,... | collective-permute-start | bytes 589832 | tf_op jit(solution)/shard_map/ppermute | solution.py:385
  89.8 11.4 %collective-permute-start.31 = (bf16[3,256,128]{2,1,0:T(8,128)(2,1)S(1)}, bf16[3,256,128]{2,1,0:T(8,128)(2,1)S(1)}, u32[]{:S(2)}, u32[]{:S(2)}) collective-permute-start(bf16[3,256,128]{2,1,0:T(8,128)(2,1)S(1)} %get-tuple-element.169), channel_id=1, source_target_pairs={{0,3},{1,2},{2,1},{3,0},{4,7},{5,6},{6,5},{7,4},{8,11},{9,10},{10,... | collective-permute-start | bytes 589832 | tf_op jit(solution)/shard_map/ppermute | solution.py:385
  111.7 14.3 %collective-permute-start.36 = (bf16[8,256,128]{2,1,0:T(8,128)(2,1)S(1)}, bf16[8,256,128]{2,1,0:T(8,128)(2,1)S(1)}, u32[]{:S(2)}, u32[]{:S(2)}) collective-permute-start(bf16[8,256,128]{2,1,0:T(8,128)(2,1)S(1)} %get-tuple-element.178.own), channel_id=1, source_target_pairs={{0,8},{1,9},{2,10},{3,11},{12,4},{13,5},{14,6},{15,7},{4,0},{5,1},... | collective-permute-start | bytes 1572872 | tf_op jit(solution)/shard_map/ppermute | solution.py:381
  115.2 22.9 %collective-permute-start.40 = (bf16[8,256,128]{2,1,0:T(8,128)(2,1)S(1)}, bf16[8,256,128]{2,1,0:T(8,128)(2,1)S(1)}, u32[]{:S(2)}, u32[]{:S(2)}) collective-permute-start(bf16[8,256,128]{2,1,0:T(8,128)(2,1)S(1)} %get-tuple-element.178.own), channel_id=1, source_target_pairs={{0,4},{1,5},{2,6},{3,7},{12,8},{13,9},{14,10},{15,11},{4,12},{5,13... | collective-permute-start | bytes 1572872 | tf_op jit(solution)/shard_map/ppermute | solution.py:381
  124.5 16.5 %collective-permute-start.35 = (bf16[8,256,128]{2,1,0:T(8,128)(2,1)S(1)}, bf16[8,256,128]{2,1,0:T(8,128)(2,1)S(1)}, u32[]{:S(2)}, u32[]{:S(2)}) collective-permute-start(bf16[8,256,128]{2,1,0:T(8,128)(2,1)S(1)} %get-tuple-element.178.own), channel_id=1, source_target_pairs={{4,8},{5,9},{6,10},{7,11},{8,4},{9,5},{10,6},{11,7},{20,24},{21,25... | collective-permute-start | bytes 1572872 | tf_op jit(solution)/shard_map/ppermute | solution.py:381
  126.0 23.3 %collective-permute-start.37 = (bf16[8,256,128]{2,1,0:T(8,128)(2,1)S(1)}, bf16[8,256,128]{2,1,0:T(8,128)(2,1)S(1)}, u32[]{:S(2)}, u32[]{:S(2)}) collective-permute-start(bf16[8,256,128]{2,1,0:T(8,128)(2,1)S(1)} %collective-permute-done.36.refs_1_.first), channel_id=1, source_target_pairs={{4,0},{5,1},{6,2},{7,3},{8,12},{9,13},{10,14},{11,15},{20,16},{21,... | collective-permute-start | bytes 1572872 | tf_op jit(solution)/shard_map/ppermute | solution.py:381
  138.8 13.2 %collective-permute-start.43 = (bf16[6,256,128]{2,1,0:T(8,128)(2,1)S(1)}, bf16[6,256,128]{2,1,0:T(8,128)(2,1)S(1)}, u32[]{:S(2)}, u32[]{:S(2)}) collective-permute-start(bf16[6,256,128]{2,1,0:T(8,128)(2,1)S(1)} %get-tuple-element.187), channel_id=1, source_target_pairs={{0,1},{1,0},{2,3},{3,2},{4,5},{5,4},{6,7},{7,6},{8,9},{9,8},{10,11... | collective-permute-start | bytes 1179656 | tf_op jit(solution)/shard_map/ppermute | solution.py:385
  139.5 12.0 %collective-permute-start.45 = (bf16[3,256,128]{2,1,0:T(8,128)(2,1)S(1)}, bf16[3,256,128]{2,1,0:T(8,128)(2,1)S(1)}, u32[]{:S(2)}, u32[]{:S(2)}) collective-permute-start(bf16[3,256,128]{2,1,0:T(8,128)(2,1)S(1)} %get-tuple-element.193), channel_id=1, source_target_pairs={{0,2},{1,3},{2,0},{3,1},{4,6},{5,7},{6,4},{7,5},{8,10},{9,11},{10,... | collective-permute-start | bytes 589832 | tf_op jit(solution)/shard_map/ppermute | solution.py:385
  141.0 11.0 %collective-permute-start.46 = (bf16[3,256,128]{2,1,0:T(8,128)(2,1)S(1)}, bf16[3,256,128]{2,1,0:T(8,128)(2,1)S(1)}, u32[]{:S(2)}, u32[]{:S(2)}) collective-permute-start(bf16[3,256,128]{2,1,0:T(8,128)(2,1)S(1)} %get-tuple-element.194), channel_id=1, source_target_pairs={{0,3},{1,2},{2,1},{3,0},{4,7},{5,6},{6,5},{7,4},{8,11},{9,10},{10,... | collective-permute-start | bytes 589832 | tf_op jit(solution)/shard_map/ppermute | solution.py:385
  162.5 14.3 %collective-permute-start.51 = (bf16[8,256,128]{2,1,0:T(8,128)(2,1)S(1)}, bf16[8,256,128]{2,1,0:T(8,128)(2,1)S(1)}, u32[]{:S(2)}, u32[]{:S(2)}) collective-permute-start(bf16[8,256,128]{2,1,0:T(8,128)(2,1)S(1)} %get-tuple-element.203.own), channel_id=1, source_target_pairs={{0,8},{1,9},{2,10},{3,11},{12,4},{13,5},{14,6},{15,7},{4,0},{5,1},... | collective-permute-start | bytes 1572872 | tf_op jit(solution)/shard_map/ppermute | solution.py:381
  166.0 22.9 %collective-permute-start.55 = (bf16[8,256,128]{2,1,0:T(8,128)(2,1)S(1)}, bf16[8,256,128]{2,1,0:T(8,128)(2,1)S(1)}, u32[]{:S(2)}, u32[]{:S(2)}) collective-permute-start(bf16[8,256,128]{2,1,0:T(8,128)(2,1)S(1)} %get-tuple-element.203.own), channel_id=1, source_target_pairs={{0,4},{1,5},{2,6},{3,7},{12,8},{13,9},{14,10},{15,11},{4,12},{5,13... | collective-permute-start | bytes 1572872 | tf_op jit(solution)/shard_map/ppermute | solution.py:381
  175.3 16.4 %collective-permute-start.50 = (bf16[8,256,128]{2,1,0:T(8,128)(2,1)S(1)}, bf16[8,256,128]{2,1,0:T(8,128)(2,1)S(1)}, u32[]{:S(2)}, u32[]{:S(2)}) collective-permute-start(bf16[8,256,128]{2,1,0:T(8,128)(2,1)S(1)} %get-tuple-element.203.own), channel_id=1, source_target_pairs={{4,8},{5,9},{6,10},{7,11},{8,4},{9,5},{10,6},{11,7},{20,24},{21,25... | collective-permute-start | bytes 1572872 | tf_op jit(solution)/shard_map/ppermute | solution.py:381
  176.7 23.3 %collective-permute-start.52 = (bf16[8,256,128]{2,1,0:T(8,128)(2,1)S(1)}, bf16[8,256,128]{2,1,0:T(8,128)(2,1)S(1)}, u32[]{:S(2)}, u32[]{:S(2)}) collective-permute-start(bf16[8,256,128]{2,1,0:T(8,128)(2,1)S(1)} %collective-permute-done.51.refs_1_.first), channel_id=1, source_target_pairs={{4,0},{5,1},{6,2},{7,3},{8,12},{9,13},{10,14},{11,15},{20,16},{21,... | collective-permute-start | bytes 1572872 | tf_op jit(solution)/shard_map/ppermute | solution.py:381
  189.5 13.1 %collective-permute-start.58 = (bf16[6,256,128]{2,1,0:T(8,128)(2,1)S(1)}, bf16[6,256,128]{2,1,0:T(8,128)(2,1)S(1)}, u32[]{:S(2)}, u32[]{:S(2)}) collective-permute-start(bf16[6,256,128]{2,1,0:T(8,128)(2,1)S(1)} %get-tuple-element.212), channel_id=1, source_target_pairs={{0,1},{1,0},{2,3},{3,2},{4,5},{5,4},{6,7},{7,6},{8,9},{9,8},{10,11... | collective-permute-start | bytes 1179656 | tf_op jit(solution)/shard_map/ppermute | solution.py:385
  190.3 12.0 %collective-permute-start.60 = (bf16[3,256,128]{2,1,0:T(8,128)(2,1)S(1)}, bf16[3,256,128]{2,1,0:T(8,128)(2,1)S(1)}, u32[]{:S(2)}, u32[]{:S(2)}) collective-permute-start(bf16[3,256,128]{2,1,0:T(8,128)(2,1)S(1)} %get-tuple-element.218), channel_id=1, source_target_pairs={{0,2},{1,3},{2,0},{3,1},{4,6},{5,7},{6,4},{7,5},{8,10},{9,11},{10,... | collective-permute-start | bytes 589832 | tf_op jit(solution)/shard_map/ppermute | solution.py:385
  191.7 10.9 %collective-permute-start.61 = (bf16[3,256,128]{2,1,0:T(8,128)(2,1)S(1)}, bf16[3,256,128]{2,1,0:T(8,128)(2,1)S(1)}, u32[]{:S(2)}, u32[]{:S(2)}) collective-permute-start(bf16[3,256,128]{2,1,0:T(8,128)(2,1)S(1)} %get-tuple-element.219), channel_id=1, source_target_pairs={{0,3},{1,2},{2,1},{3,0},{4,7},{5,6},{6,5},{7,4},{8,11},{9,10},{10,... | collective-permute-start | bytes 589832 | tf_op jit(solution)/shard_map/ppermute | solution.py:385
  213.5 11.1 %all-to-all-start = ((f32[16,1,128]{2,1,0:T(1,128)}), f32[16,1,128]{2,1,0:T(1,128)S(1)}, u32[]{:S(2)}, u32[]{:S(2)}) async-start(f32[16,1,128]{2,1,0:T(1,128)} %get-tuple-element.226), calls=%async_computation | async-start | bytes 16384 | tf_op jit(solution)/shard_map/all_to_all | solution.py:389
  (37 other events, 250.1 us)

commit v18 on v17

--- a/solution.py
+++ b/solution.py
@@ -118,9 +118,9 @@
 
     def add(s, acc):
         t = buffer[s].astype(jnp.float32)
-        return acc + jnp.sum((t * t).reshape(tile // 8, 8, tile), axis=0)
-
-    acc = jnp.zeros((8, tile), jnp.float32)
+        return acc + jnp.sum((t * t).reshape(tile // 64, 64, tile), axis=0)
+
+    acc = jnp.zeros((64, tile), jnp.float32)
     for i, copy in enumerate(copies):
         copy.wait()
         acc = lax.fori_loop(i * GROUP, jnp.clip(count[0], i * GROUP, (i + 1) * GROUP), add, acc)
@@ -333,8 +333,7 @@
     for b in range(xpos.shape[0]):
         total += xpos[b] * acc[b]
     part = -0.5 * jnp.sum(total, axis=0, keepdims=True)
-    for i in range(energy.shape[0]):
-        energy[i] = part
+    energy[...] = jnp.broadcast_to(part[None], energy.shape)
 
 
 def last_field(layout, table, tiles, sources, field, xpos):

time: 226 us -> 226 us (level)
  no operation moved by 1% of the time
where the time goes in v18:
time: 226 us; the launch traced here: 225 us
  waiting for transfers between devices  124 us (55%)
  starting transfers between devices  58.7 us (26%)
  Pallas kernels  34 us (15%)
  local copies, waits for them, and re-layouts  4.06 us (2%)
  between operations  2.4 us (1%)
    ppermute x46, waiting for transfers between devices, across(): return lax.ppermute(value, 'row', [(i, i ^ flip) for i in range(16)])  81.4 us
    ppermute x16, waiting for transfers between devices, along_z(): lax.ppermute(value, 'row', [(a * 4 + i, b * 4 + i) for a, b in pairs for...  38.1 us
    ppermute x46, starting transfers between devices, across(): return lax.ppermute(value, 'row', [(i, i ^ flip) for i in range(16)])  35.1 us
    ppermute x16, starting transfers between devices, along_z(): lax.ppermute(value, 'row', [(a * 4 + i, b * 4 + i) for a, b in pairs for...  18.8 us
    pallas_call x4, Pallas kernels, early(): pl.pallas_call(functools.partial(early_kernel, layout, parts), out_shape=...  13.9 us
    pallas_call x11, Pallas kernels, pack(): pl.pallas_call(picked, out_shape=[jax.ShapeDtypeStruct((size, tile, repl)...  6.59 us
    all_to_all x1, starting transfers between devices, row_sum(): lax.all_to_all(parts, 'row', split_axis=0, concat_axis=0, tiled=True)  4.73 us
  transfers between devices with their start and end apart: 63, of which 38 were waited for; matrix products, arithmetic and copies ran while one was open for 0% of the time, Pallas kernels for 12%

profile of v18, /device:TPU:0, one launch (start us, length us, event | category | flops | bytes accessed | tf_op | source)
XLA Modules:
  0.0 225.2 jit_solution(1727155277996455175)
XLA Ops:
  1.9 4.1 %collective-permute-start = (bf16[8,256,128]{2,1,0:T(8,128)(2,1)S(1)}, bf16[8,256,128]{2,1,0:T(8,128)(2,1)S(1)}, u32[]{:S(2)}, u32[]{:S(2)}) collective-permute-start(bf16[8,256,128]{2,1,0:T(8,128)(2,1)S(1)} %convert_element_type.3.own.refs_1_), channel_id=1, source_target_pairs={{0,8},{1,9},{2,10},{3,11},{12,4},{13,5},{14,6},{15,7},{4,0},{5,1},... | collective-permute-start | bytes 1572872 | tf_op jit(solution)/shard_map/ppermute | solution.py:380
  6.7 4.2 %shard_map.85 = (s32[144]{0:T(256)}, f32[1,128]{1,0:T(1,128)}) custom-call(s32[48]{0:T(128)} %rows.1, s32[48]{0:T(128)} %cols.1, s32[1]{0:T(128)S(6)} %copy.9.count, bf16[48,256,256]{2,1,0:T(8,128)(2,1)} %tiles.19), custom_call_target="tpu_custom_call" | custom-call | tf_op jit(solution)/shard_map/pallas_call | solution.py:131
  24.1 6.2 %collective-permute-done.4.own.refs_3_.second = bf16[8,256,128]{2,1,0:T(8,128)(2,1)S(1)} collective-permute-done((bf16[8,256,128]{2,1,0:T(8,128)(2,1)S(1)}, bf16[8,256,128]{2,1,0:T(8,128)(2,1)S(1)}, u32[]{:S(2)}, u32[]{:S(2)}) %collective-permute-start.4) | collective-permute-done | bytes 524320 | tf_op jit(solution)/shard_map/ppermute | solution.py:380
  30.3 2.8 %copy-done = bf16[48,256,256]{2,1,0:T(8,128)(2,1)S(1)} copy-done((bf16[48,256,256]{2,1,0:T(8,128)(2,1)S(1)}, bf16[48,256,256]{2,1,0:T(8,128)(2,1)}, u32[]{:S(2)}) %copy-start) | copy-done | bytes 6291480
  33.1 3.8 %collective-permute-done.6.refs_1_ = bf16[6,256,128]{2,1,0:T(8,128)(2,1)S(1)} collective-permute-done((bf16[6,256,128]{2,1,0:T(8,128)(2,1)S(1)}, bf16[6,256,128]{2,1,0:T(8,128)(2,1)S(1)}, u32[]{:S(2)}, u32[]{:S(2)}) %collective-permute-start.6) | collective-permute-done | bytes 393248 | tf_op jit(solution)/shard_map/ppermute | solution.py:384
  47.3 2.4 %collective-permute-done.8.refs_3_ = bf16[3,256,128]{2,1,0:T(8,128)(2,1)S(1)} collective-permute-done((bf16[3,256,128]{2,1,0:T(8,128)(2,1)S(1)}, bf16[3,256,128]{2,1,0:T(8,128)(2,1)S(1)}, u32[]{:S(2)}, u32[]{:S(2)}) %collective-permute-start.8) | collective-permute-done | bytes 196640 | tf_op jit(solution)/shard_map/ppermute | solution.py:384
  49.7 3.4 %collective-permute-start.14 = (f32[1,128]{1,0:T(1,128)S(1)}, f32[1,128]{1,0:T(1,128)S(1)}, u32[]{:S(2)}, u32[]{:S(2)}) collective-permute-start(f32[1,128]{1,0:T(1,128)S(1)} %add.18), channel_id=1, source_target_pairs={{0,8},{1,9},{2,10},{3,11},{4,12},{5,13},{6,14},{7,15},{8,0},{9,1},... | collective-permute-start | bytes 1544 | tf_op jit(solution)/shard_map/ppermute | solution.py:384
  53.1 3.5 %shard_map.90.field = f32[9,256,128]{2,1,0:T(8,128)S(1)} custom-call(s32[180]{0:T(256)S(1)} %get-tuple-element.126.refs_0_.table, bf16[48,256,256]{2,1,0:T(8,128)(2,1)S(1)} %copy-done.1, bf16[8,256,128]{2,1,0:T(8,128)(2,1)S(1)} %convert_element_type.3.own.refs_1_, bf16[8,256,128]{2,1,0:T(8,128)(2,1)S(1)} %collective-permute-done.first.refs_2_, ...), custom_call_target="tpu_custom_call" | custom-call | tf_op jit(solution)/shard_map/pallas_call | solution.py:281
  59.5 2.7 %collective-permute-start.21 = (bf16[8,256,128]{2,1,0:T(8,128)(2,1)S(1)}, bf16[8,256,128]{2,1,0:T(8,128)(2,1)S(1)}, u32[]{:S(2)}, u32[]{:S(2)}) collective-permute-start(bf16[8,256,128]{2,1,0:T(8,128)(2,1)S(1)} %get-tuple-element.153.own), channel_id=1, source_target_pairs={{0,8},{1,9},{2,10},{3,11},{12,4},{13,5},{14,6},{15,7},{4,0},{5,1},... | collective-permute-start | bytes 1572872 | tf_op jit(solution)/shard_map/ppermute | solution.py:380
  64.1 6.3 %collective-permute-done.18.refs_0_ = bf16[3,256,128]{2,1,0:T(8,128)(2,1)S(1)} collective-permute-done((bf16[3,256,128]{2,1,0:T(8,128)(2,1)S(1)}, bf16[3,256,128]{2,1,0:T(8,128)(2,1)S(1)}, u32[]{:S(2)}, u32[]{:S(2)}) %collective-permute-start.18) | collective-permute-done | bytes 196640 | tf_op jit(solution)/shard_map/ppermute | solution.py:384
  70.4 2.5 %collective-permute-done.19.refs_1_ = bf16[3,256,128]{2,1,0:T(8,128)(2,1)S(1)} collective-permute-done((bf16[3,256,128]{2,1,0:T(8,128)(2,1)S(1)}, bf16[3,256,128]{2,1,0:T(8,128)(2,1)S(1)}, u32[]{:S(2)}, u32[]{:S(2)}) %collective-permute-start.19) | collective-permute-done | bytes 196640 | tf_op jit(solution)/shard_map/ppermute | solution.py:384
  77.9 6.4 %collective-permute-done.26.refs_2_ = bf16[3,256,128]{2,1,0:T(8,128)(2,1)S(1)} collective-permute-done((bf16[3,256,128]{2,1,0:T(8,128)(2,1)S(1)}, bf16[3,256,128]{2,1,0:T(8,128)(2,1)S(1)}, u32[]{:S(2)}, u32[]{:S(2)}) %collective-permute-start.26) | collective-permute-done | bytes 196640 | tf_op jit(solution)/shard_map/ppermute | solution.py:384
  90.0 8.6 %collective-permute-done.22.refs_2_.out = bf16[8,256,128]{2,1,0:T(8,128)(2,1)S(1)} collective-permute-done((bf16[8,256,128]{2,1,0:T(8,128)(2,1)S(1)}, bf16[8,256,128]{2,1,0:T(8,128)(2,1)S(1)}, u32[]{:S(2)}, u32[]{:S(2)}) %collective-permute-start.22) | collective-permute-done | bytes 524320 | tf_op jit(solution)/shard_map/ppermute | solution.py:380
  101.2 3.5 %shard_map.95.field = f32[9,256,128]{2,1,0:T(8,128)S(1)} custom-call(s32[180]{0:T(256)S(1)} %get-tuple-element.126.refs_0_.table, bf16[48,256,256]{2,1,0:T(8,128)(2,1)S(1)} %copy-done.1, bf16[8,256,128]{2,1,0:T(8,128)(2,1)S(1)} %get-tuple-element.153.own, bf16[8,256,128]{2,1,0:T(8,128)(2,1)S(1)} %collective-permute-done.21.refs_1_.first, ...), custom_call_target="tpu_custom_call" | custom-call | tf_op jit(solution)/shard_map/pallas_call | solution.py:281
  104.7 2.3 %collective-permute-done.23.got2 = bf16[3,256,128]{2,1,0:T(8,128)(2,1)S(1)} collective-permute-done((bf16[3,256,128]{2,1,0:T(8,128)(2,1)S(1)}, bf16[3,256,128]{2,1,0:T(8,128)(2,1)S(1)}, u32[]{:S(2)}, u32[]{:S(2)}) %collective-permute-start.23) | collective-permute-done | bytes 196640 | tf_op jit(solution)/shard_map/ppermute | solution.py:384
  107.0 3.3 %collective-permute-done.24.got3 = bf16[3,256,128]{2,1,0:T(8,128)(2,1)S(1)} collective-permute-done((bf16[3,256,128]{2,1,0:T(8,128)(2,1)S(1)}, bf16[3,256,128]{2,1,0:T(8,128)(2,1)S(1)}, u32[]{:S(2)}, u32[]{:S(2)}) %collective-permute-start.24) | collective-permute-done | bytes 196640 | tf_op jit(solution)/shard_map/ppermute | solution.py:384
  115.7 5.4 %collective-permute-done.33.refs_0_ = bf16[3,256,128]{2,1,0:T(8,128)(2,1)S(1)} collective-permute-done((bf16[3,256,128]{2,1,0:T(8,128)(2,1)S(1)}, bf16[3,256,128]{2,1,0:T(8,128)(2,1)S(1)}, u32[]{:S(2)}, u32[]{:S(2)}) %collective-permute-start.33) | collective-permute-done | bytes 196640 | tf_op jit(solution)/shard_map/ppermute | solution.py:384
  121.1 3.4 %collective-permute-done.34.refs_1_ = bf16[3,256,128]{2,1,0:T(8,128)(2,1)S(1)} collective-permute-done((bf16[3,256,128]{2,1,0:T(8,128)(2,1)S(1)}, bf16[3,256,128]{2,1,0:T(8,128)(2,1)S(1)}, u32[]{:S(2)}, u32[]{:S(2)}) %collective-permute-start.34) | collective-permute-done | bytes 196640 | tf_op jit(solution)/shard_map/ppermute | solution.py:384
  129.4 6.4 %collective-permute-done.41.refs_2_ = bf16[3,256,128]{2,1,0:T(8,128)(2,1)S(1)} collective-permute-done((bf16[3,256,128]{2,1,0:T(8,128)(2,1)S(1)}, bf16[3,256,128]{2,1,0:T(8,128)(2,1)S(1)}, u32[]{:S(2)}, u32[]{:S(2)}) %collective-permute-start.41) | collective-permute-done | bytes 196640 | tf_op jit(solution)/shard_map/ppermute | solution.py:384
  141.0 8.3 %collective-permute-done.37.refs_2_.out = bf16[8,256,128]{2,1,0:T(8,128)(2,1)S(1)} collective-permute-done((bf16[8,256,128]{2,1,0:T(8,128)(2,1)S(1)}, bf16[8,256,128]{2,1,0:T(8,128)(2,1)S(1)}, u32[]{:S(2)}, u32[]{:S(2)}) %collective-permute-start.37) | collective-permute-done | bytes 524320 | tf_op jit(solution)/shard_map/ppermute | solution.py:380
  151.9 3.5 %shard_map.100.field = f32[9,256,128]{2,1,0:T(8,128)S(1)} custom-call(s32[180]{0:T(256)S(1)} %get-tuple-element.126.refs_0_.table, bf16[48,256,256]{2,1,0:T(8,128)(2,1)S(1)} %copy-done.1, bf16[8,256,128]{2,1,0:T(8,128)(2,1)S(1)} %get-tuple-element.178.own, bf16[8,256,128]{2,1,0:T(8,128)(2,1)S(1)} %collective-permute-done.36.refs_1_.first, ...), custom_call_target="tpu_custom_call" | custom-call | tf_op jit(solution)/shard_map/pallas_call | solution.py:281
  155.4 2.3 %collective-permute-done.38.got2 = bf16[3,256,128]{2,1,0:T(8,128)(2,1)S(1)} collective-permute-done((bf16[3,256,128]{2,1,0:T(8,128)(2,1)S(1)}, bf16[3,256,128]{2,1,0:T(8,128)(2,1)S(1)}, u32[]{:S(2)}, u32[]{:S(2)}) %collective-permute-start.38) | collective-permute-done | bytes 196640 | tf_op jit(solution)/shard_map/ppermute | solution.py:384
  157.8 3.3 %collective-permute-done.39.got3 = bf16[3,256,128]{2,1,0:T(8,128)(2,1)S(1)} collective-permute-done((bf16[3,256,128]{2,1,0:T(8,128)(2,1)S(1)}, bf16[3,256,128]{2,1,0:T(8,128)(2,1)S(1)}, u32[]{:S(2)}, u32[]{:S(2)}) %collective-permute-start.39) | collective-permute-done | bytes 196640 | tf_op jit(solution)/shard_map/ppermute | solution.py:384
  166.4 5.4 %collective-permute-done.48.refs_0_ = bf16[3,256,128]{2,1,0:T(8,128)(2,1)S(1)} collective-permute-done((bf16[3,256,128]{2,1,0:T(8,128)(2,1)S(1)}, bf16[3,256,128]{2,1,0:T(8,128)(2,1)S(1)}, u32[]{:S(2)}, u32[]{:S(2)}) %collective-permute-start.48) | collective-permute-done | bytes 196640 | tf_op jit(solution)/shard_map/ppermute | solution.py:384
  171.9 3.4 %collective-permute-done.49.refs_1_ = bf16[3,256,128]{2,1,0:T(8,128)(2,1)S(1)} collective-permute-done((bf16[3,256,128]{2,1,0:T(8,128)(2,1)S(1)}, bf16[3,256,128]{2,1,0:T(8,128)(2,1)S(1)}, u32[]{:S(2)}, u32[]{:S(2)}) %collective-permute-start.49) | collective-permute-done | bytes 196640 | tf_op jit(solution)/shard_map/ppermute | solution.py:384
  180.1 6.4 %collective-permute-done.56.refs_2_ = bf16[3,256,128]{2,1,0:T(8,128)(2,1)S(1)} collective-permute-done((bf16[3,256,128]{2,1,0:T(8,128)(2,1)S(1)}, bf16[3,256,128]{2,1,0:T(8,128)(2,1)S(1)}, u32[]{:S(2)}, u32[]{:S(2)}) %collective-permute-start.56) | collective-permute-done | bytes 196640 | tf_op jit(solution)/shard_map/ppermute | solution.py:384
  191.7 8.3 %collective-permute-done.52.refs_2_.out = bf16[8,256,128]{2,1,0:T(8,128)(2,1)S(1)} collective-permute-done((bf16[8,256,128]{2,1,0:T(8,128)(2,1)S(1)}, bf16[8,256,128]{2,1,0:T(8,128)(2,1)S(1)}, u32[]{:S(2)}, u32[]{:S(2)}) %collective-permute-start.52) | collective-permute-done | bytes 524320 | tf_op jit(solution)/shard_map/ppermute | solution.py:380
  202.6 3.5 %shard_map.105.field = f32[9,256,128]{2,1,0:T(8,128)S(1)} custom-call(s32[180]{0:T(256)S(1)} %get-tuple-element.126.refs_0_.table, bf16[48,256,256]{2,1,0:T(8,128)(2,1)S(1)} %copy-done.1, bf16[8,256,128]{2,1,0:T(8,128)(2,1)S(1)} %get-tuple-element.203.own, bf16[8,256,128]{2,1,0:T(8,128)(2,1)S(1)} %collective-permute-done.51.refs_1_.first, ...), custom_call_target="tpu_custom_call" | custom-call | tf_op jit(solution)/shard_map/pallas_call | solution.py:281
  206.1 2.4 %collective-permute-done.53.got2 = bf16[3,256,128]{2,1,0:T(8,128)(2,1)S(1)} collective-permute-done((bf16[3,256,128]{2,1,0:T(8,128)(2,1)S(1)}, bf16[3,256,128]{2,1,0:T(8,128)(2,1)S(1)}, u32[]{:S(2)}, u32[]{:S(2)}) %collective-permute-start.53) | collective-permute-done | bytes 196640 | tf_op jit(solution)/shard_map/ppermute | solution.py:384
  208.5 3.3 %collective-permute-done.54.got3 = bf16[3,256,128]{2,1,0:T(8,128)(2,1)S(1)} collective-permute-done((bf16[3,256,128]{2,1,0:T(8,128)(2,1)S(1)}, bf16[3,256,128]{2,1,0:T(8,128)(2,1)S(1)}, u32[]{:S(2)}, u32[]{:S(2)}) %collective-permute-start.54) | collective-permute-done | bytes 196640 | tf_op jit(solution)/shard_map/ppermute | solution.py:384
  213.5 4.7 %all-to-all-start = ((f32[16,1,128]{2,1,0:T(1,128)}), f32[16,1,128]{2,1,0:T(1,128)S(1)}, u32[]{:S(2)}, u32[]{:S(2)}) async-start(f32[16,1,128]{2,1,0:T(1,128)} %get-tuple-element.226), calls=%async_computation | async-start | bytes 16384 | tf_op jit(solution)/shard_map/all_to_all | solution.py:388
  220.3 4.3 %all-to-all-done = f32[16,1,128]{2,1,0:T(1,128)S(1)} async-done(((f32[16,1,128]{2,1,0:T(1,128)}), f32[16,1,128]{2,1,0:T(1,128)S(1)}, u32[]{:S(2)}, u32[]{:S(2)}) %all-to-all-start) | async-done | bytes 8224 | tf_op jit(solution)/shard_map/all_to_all | solution.py:388
  (139 shorter events, 82.5 us)
Async XLA Ops:
  1.9 16.5 %collective-permute-start = (bf16[8,256,128]{2,1,0:T(8,128)(2,1)S(1)}, bf16[8,256,128]{2,1,0:T(8,128)(2,1)S(1)}, u32[]{:S(2)}, u32[]{:S(2)}) collective-permute-start(bf16[8,256,128]{2,1,0:T(8,128)(2,1)S(1)} %convert_element_type.3.own.refs_1_), channel_id=1, source_target_pairs={{0,8},{1,9},{2,10},{3,11},{12,4},{13,5},{14,6},{15,7},{4,0},{5,1},... | collective-permute-start | bytes 1572872 | tf_op jit(solution)/shard_map/ppermute | solution.py:380
  12.2 18.1 %collective-permute-start.4 = (bf16[8,256,128]{2,1,0:T(8,128)(2,1)S(1)}, bf16[8,256,128]{2,1,0:T(8,128)(2,1)S(1)}, u32[]{:S(2)}, u32[]{:S(2)}) collective-permute-start(bf16[8,256,128]{2,1,0:T(8,128)(2,1)S(1)} %convert_element_type.3.own.refs_1_), channel_id=1, source_target_pairs={{0,4},{1,5},{2,6},{3,7},{12,8},{13,9},{14,10},{15,11},{4,12},{5,13... | collective-permute-start | bytes 1572872 | tf_op jit(solution)/shard_map/ppermute | solution.py:380
  20.5 12.6 %collective-permute-start.5 = (bf16[6,256,128]{2,1,0:T(8,128)(2,1)S(1)}, bf16[6,256,128]{2,1,0:T(8,128)(2,1)S(1)}, u32[]{:S(2)}, u32[]{:S(2)}) collective-permute-start(bf16[6,256,128]{2,1,0:T(8,128)(2,1)S(1)} %get-tuple-element.127), channel_id=1, source_target_pairs={{0,2},{1,3},{2,0},{3,1},{4,6},{5,7},{6,4},{7,5},{8,10},{9,11},{10,... | collective-permute-start | bytes 1179656 | tf_op jit(solution)/shard_map/ppermute | solution.py:384
  22.1 14.8 %collective-permute-start.6 = (bf16[6,256,128]{2,1,0:T(8,128)(2,1)S(1)}, bf16[6,256,128]{2,1,0:T(8,128)(2,1)S(1)}, u32[]{:S(2)}, u32[]{:S(2)}) collective-permute-start(bf16[6,256,128]{2,1,0:T(8,128)(2,1)S(1)} %get-tuple-element.128), channel_id=1, source_target_pairs={{0,3},{1,2},{2,1},{3,0},{4,7},{5,6},{6,5},{7,4},{8,11},{9,10},{10,... | collective-permute-start | bytes 1179656 | tf_op jit(solution)/shard_map/ppermute | solution.py:384
  22.1 18.8 %collective-permute-start.9 = (bf16[8,256,128]{2,1,0:T(8,128)(2,1)S(1)}, bf16[8,256,128]{2,1,0:T(8,128)(2,1)S(1)}, u32[]{:S(2)}, u32[]{:S(2)}) collective-permute-start(bf16[8,256,128]{2,1,0:T(8,128)(2,1)S(1)} %convert_element_type.3.own.refs_1_), channel_id=1, source_target_pairs={{4,8},{5,9},{6,10},{7,11},{8,4},{9,5},{10,6},{11,7},{20,24},{21,25... | collective-permute-start | bytes 1572872 | tf_op jit(solution)/shard_map/ppermute | solution.py:380
  22.8 18.9 %collective-permute-start.10 = (bf16[8,256,128]{2,1,0:T(8,128)(2,1)S(1)}, bf16[8,256,128]{2,1,0:T(8,128)(2,1)S(1)}, u32[]{:S(2)}, u32[]{:S(2)}) collective-permute-start(bf16[8,256,128]{2,1,0:T(8,128)(2,1)S(1)} %collective-permute-done.first.refs_2_), channel_id=1, source_target_pairs={{4,0},{5,1},{6,2},{7,3},{8,12},{9,13},{10,14},{11,15},{20,16},{21,... | collective-permute-start | bytes 1572872 | tf_op jit(solution)/shard_map/ppermute | solution.py:380
  37.5 15.6 %collective-permute-start.12 = (bf16[9,256,128]{2,1,0:T(8,128)(2,1)S(1)}, bf16[9,256,128]{2,1,0:T(8,128)(2,1)S(1)}, u32[]{:S(2)}, u32[]{:S(2)}) collective-permute-start(bf16[9,256,128]{2,1,0:T(8,128)(2,1)S(1)} %get-tuple-element.138), channel_id=1, source_target_pairs={{0,1},{1,0},{2,3},{3,2},{4,5},{5,4},{6,7},{7,6},{8,9},{9,8},{10,11... | collective-permute-start | bytes 1769480 | tf_op jit(solution)/shard_map/ppermute | solution.py:384
  42.3 10.8 %collective-permute-start.13 = (bf16[3,256,128]{2,1,0:T(8,128)(2,1)S(1)}, bf16[3,256,128]{2,1,0:T(8,128)(2,1)S(1)}, u32[]{:S(2)}, u32[]{:S(2)}) collective-permute-start(bf16[3,256,128]{2,1,0:T(8,128)(2,1)S(1)} %get-tuple-element.139), channel_id=1, source_target_pairs={{0,1},{1,0},{2,3},{3,2},{4,5},{5,4},{6,7},{7,6},{8,9},{9,8},{10,11... | collective-permute-start | bytes 589832 | tf_op jit(solution)/shard_map/ppermute | solution.py:384
  46.0 12.0 %collective-permute-start.15 = (bf16[3,256,128]{2,1,0:T(8,128)(2,1)S(1)}, bf16[3,256,128]{2,1,0:T(8,128)(2,1)S(1)}, u32[]{:S(2)}, u32[]{:S(2)}) collective-permute-start(bf16[3,256,128]{2,1,0:T(8,128)(2,1)S(1)} %get-tuple-element.145), channel_id=1, source_target_pairs={{0,2},{1,3},{2,0},{3,1},{4,6},{5,7},{6,4},{7,5},{8,10},{9,11},{10,... | collective-permute-start | bytes 589832 | tf_op jit(solution)/shard_map/ppermute | solution.py:384
  47.2 10.9 %collective-permute-start.16 = (bf16[3,256,128]{2,1,0:T(8,128)(2,1)S(1)}, bf16[3,256,128]{2,1,0:T(8,128)(2,1)S(1)}, u32[]{:S(2)}, u32[]{:S(2)}) collective-permute-start(bf16[3,256,128]{2,1,0:T(8,128)(2,1)S(1)} %get-tuple-element.146), channel_id=1, source_target_pairs={{0,3},{1,2},{2,1},{3,0},{4,7},{5,6},{6,5},{7,4},{8,11},{9,10},{10,... | collective-permute-start | bytes 589832 | tf_op jit(solution)/shard_map/ppermute | solution.py:384
  59.5 15.1 %collective-permute-start.21 = (bf16[8,256,128]{2,1,0:T(8,128)(2,1)S(1)}, bf16[8,256,128]{2,1,0:T(8,128)(2,1)S(1)}, u32[]{:S(2)}, u32[]{:S(2)}) collective-permute-start(bf16[8,256,128]{2,1,0:T(8,128)(2,1)S(1)} %get-tuple-element.153.own), channel_id=1, source_target_pairs={{0,8},{1,9},{2,10},{3,11},{12,4},{13,5},{14,6},{15,7},{4,0},{5,1},... | collective-permute-start | bytes 1572872 | tf_op jit(solution)/shard_map/ppermute | solution.py:380
  64.1 23.3 %collective-permute-start.25 = (bf16[8,256,128]{2,1,0:T(8,128)(2,1)S(1)}, bf16[8,256,128]{2,1,0:T(8,128)(2,1)S(1)}, u32[]{:S(2)}, u32[]{:S(2)}) collective-permute-start(bf16[8,256,128]{2,1,0:T(8,128)(2,1)S(1)} %get-tuple-element.153.own), channel_id=1, source_target_pairs={{0,4},{1,5},{2,6},{3,7},{12,8},{13,9},{14,10},{15,11},{4,12},{5,13... | collective-permute-start | bytes 1572872 | tf_op jit(solution)/shard_map/ppermute | solution.py:380
  72.9 17.1 %collective-permute-start.20 = (bf16[8,256,128]{2,1,0:T(8,128)(2,1)S(1)}, bf16[8,256,128]{2,1,0:T(8,128)(2,1)S(1)}, u32[]{:S(2)}, u32[]{:S(2)}) collective-permute-start(bf16[8,256,128]{2,1,0:T(8,128)(2,1)S(1)} %get-tuple-element.153.own), channel_id=1, source_target_pairs={{4,8},{5,9},{6,10},{7,11},{8,4},{9,5},{10,6},{11,7},{20,24},{21,25... | collective-permute-start | bytes 1572872 | tf_op jit(solution)/shard_map/ppermute | solution.py:380
  74.6 24.0 %collective-permute-start.22 = (bf16[8,256,128]{2,1,0:T(8,128)(2,1)S(1)}, bf16[8,256,128]{2,1,0:T(8,128)(2,1)S(1)}, u32[]{:S(2)}, u32[]{:S(2)}) collective-permute-start(bf16[8,256,128]{2,1,0:T(8,128)(2,1)S(1)} %collective-permute-done.21.refs_1_.first), channel_id=1, source_target_pairs={{4,0},{5,1},{6,2},{7,3},{8,12},{9,13},{10,14},{11,15},{20,16},{21,... | collective-permute-start | bytes 1572872 | tf_op jit(solution)/shard_map/ppermute | solution.py:380
  88.0 13.2 %collective-permute-start.28 = (bf16[6,256,128]{2,1,0:T(8,128)(2,1)S(1)}, bf16[6,256,128]{2,1,0:T(8,128)(2,1)S(1)}, u32[]{:S(2)}, u32[]{:S(2)}) collective-permute-start(bf16[6,256,128]{2,1,0:T(8,128)(2,1)S(1)} %get-tuple-element.162), channel_id=1, source_target_pairs={{0,1},{1,0},{2,3},{3,2},{4,5},{5,4},{6,7},{7,6},{8,9},{9,8},{10,11... | collective-permute-start | bytes 1179656 | tf_op jit(solution)/shard_map/ppermute | solution.py:384
  88.4 12.4 %collective-permute-start.30 = (bf16[3,256,128]{2,1,0:T(8,128)(2,1)S(1)}, bf16[3,256,128]{2,1,0:T(8,128)(2,1)S(1)}, u32[]{:S(2)}, u32[]{:S(2)}) collective-permute-start(bf16[3,256,128]{2,1,0:T(8,128)(2,1)S(1)} %get-tuple-element.168), channel_id=1, source_target_pairs={{0,2},{1,3},{2,0},{3,1},{4,6},{5,7},{6,4},{7,5},{8,10},{9,11},{10,... | collective-permute-start | bytes 589832 | tf_op jit(solution)/shard_map/ppermute | solution.py:384
  89.7 11.4 %collective-permute-start.31 = (bf16[3,256,128]{2,1,0:T(8,128)(2,1)S(1)}, bf16[3,256,128]{2,1,0:T(8,128)(2,1)S(1)}, u32[]{:S(2)}, u32[]{:S(2)}) collective-permute-start(bf16[3,256,128]{2,1,0:T(8,128)(2,1)S(1)} %get-tuple-element.169), channel_id=1, source_target_pairs={{0,3},{1,2},{2,1},{3,0},{4,7},{5,6},{6,5},{7,4},{8,11},{9,10},{10,... | collective-permute-start | bytes 589832 | tf_op jit(solution)/shard_map/ppermute | solution.py:384
  111.7 14.2 %collective-permute-start.36 = (bf16[8,256,128]{2,1,0:T(8,128)(2,1)S(1)}, bf16[8,256,128]{2,1,0:T(8,128)(2,1)S(1)}, u32[]{:S(2)}, u32[]{:S(2)}) collective-permute-start(bf16[8,256,128]{2,1,0:T(8,128)(2,1)S(1)} %get-tuple-element.178.own), channel_id=1, source_target_pairs={{0,8},{1,9},{2,10},{3,11},{12,4},{13,5},{14,6},{15,7},{4,0},{5,1},... | collective-permute-start | bytes 1572872 | tf_op jit(solution)/shard_map/ppermute | solution.py:380
  115.3 22.9 %collective-permute-start.40 = (bf16[8,256,128]{2,1,0:T(8,128)(2,1)S(1)}, bf16[8,256,128]{2,1,0:T(8,128)(2,1)S(1)}, u32[]{:S(2)}, u32[]{:S(2)}) collective-permute-start(bf16[8,256,128]{2,1,0:T(8,128)(2,1)S(1)} %get-tuple-element.178.own), channel_id=1, source_target_pairs={{0,4},{1,5},{2,6},{3,7},{12,8},{13,9},{14,10},{15,11},{4,12},{5,13... | collective-permute-start | bytes 1572872 | tf_op jit(solution)/shard_map/ppermute | solution.py:380
  124.5 16.4 %collective-permute-start.35 = (bf16[8,256,128]{2,1,0:T(8,128)(2,1)S(1)}, bf16[8,256,128]{2,1,0:T(8,128)(2,1)S(1)}, u32[]{:S(2)}, u32[]{:S(2)}) collective-permute-start(bf16[8,256,128]{2,1,0:T(8,128)(2,1)S(1)} %get-tuple-element.178.own), channel_id=1, source_target_pairs={{4,8},{5,9},{6,10},{7,11},{8,4},{9,5},{10,6},{11,7},{20,24},{21,25... | collective-permute-start | bytes 1572872 | tf_op jit(solution)/shard_map/ppermute | solution.py:380
  126.0 23.3 %collective-permute-start.37 = (bf16[8,256,128]{2,1,0:T(8,128)(2,1)S(1)}, bf16[8,256,128]{2,1,0:T(8,128)(2,1)S(1)}, u32[]{:S(2)}, u32[]{:S(2)}) collective-permute-start(bf16[8,256,128]{2,1,0:T(8,128)(2,1)S(1)} %collective-permute-done.36.refs_1_.first), channel_id=1, source_target_pairs={{4,0},{5,1},{6,2},{7,3},{8,12},{9,13},{10,14},{11,15},{20,16},{21,... | collective-permute-start | bytes 1572872 | tf_op jit(solution)/shard_map/ppermute | solution.py:380
  138.8 13.2 %collective-permute-start.43 = (bf16[6,256,128]{2,1,0:T(8,128)(2,1)S(1)}, bf16[6,256,128]{2,1,0:T(8,128)(2,1)S(1)}, u32[]{:S(2)}, u32[]{:S(2)}) collective-permute-start(bf16[6,256,128]{2,1,0:T(8,128)(2,1)S(1)} %get-tuple-element.187), channel_id=1, source_target_pairs={{0,1},{1,0},{2,3},{3,2},{4,5},{5,4},{6,7},{7,6},{8,9},{9,8},{10,11... | collective-permute-start | bytes 1179656 | tf_op jit(solution)/shard_map/ppermute | solution.py:384
  139.5 12.0 %collective-permute-start.45 = (bf16[3,256,128]{2,1,0:T(8,128)(2,1)S(1)}, bf16[3,256,128]{2,1,0:T(8,128)(2,1)S(1)}, u32[]{:S(2)}, u32[]{:S(2)}) collective-permute-start(bf16[3,256,128]{2,1,0:T(8,128)(2,1)S(1)} %get-tuple-element.193), channel_id=1, source_target_pairs={{0,2},{1,3},{2,0},{3,1},{4,6},{5,7},{6,4},{7,5},{8,10},{9,11},{10,... | collective-permute-start | bytes 589832 | tf_op jit(solution)/shard_map/ppermute | solution.py:384
  140.9 11.0 %collective-permute-start.46 = (bf16[3,256,128]{2,1,0:T(8,128)(2,1)S(1)}, bf16[3,256,128]{2,1,0:T(8,128)(2,1)S(1)}, u32[]{:S(2)}, u32[]{:S(2)}) collective-permute-start(bf16[3,256,128]{2,1,0:T(8,128)(2,1)S(1)} %get-tuple-element.194), channel_id=1, source_target_pairs={{0,3},{1,2},{2,1},{3,0},{4,7},{5,6},{6,5},{7,4},{8,11},{9,10},{10,... | collective-permute-start | bytes 589832 | tf_op jit(solution)/shard_map/ppermute | solution.py:384
  162.5 14.3 %collective-permute-start.51 = (bf16[8,256,128]{2,1,0:T(8,128)(2,1)S(1)}, bf16[8,256,128]{2,1,0:T(8,128)(2,1)S(1)}, u32[]{:S(2)}, u32[]{:S(2)}) collective-permute-start(bf16[8,256,128]{2,1,0:T(8,128)(2,1)S(1)} %get-tuple-element.203.own), channel_id=1, source_target_pairs={{0,8},{1,9},{2,10},{3,11},{12,4},{13,5},{14,6},{15,7},{4,0},{5,1},... | collective-permute-start | bytes 1572872 | tf_op jit(solution)/shard_map/ppermute | solution.py:380
  166.0 22.9 %collective-permute-start.55 = (bf16[8,256,128]{2,1,0:T(8,128)(2,1)S(1)}, bf16[8,256,128]{2,1,0:T(8,128)(2,1)S(1)}, u32[]{:S(2)}, u32[]{:S(2)}) collective-permute-start(bf16[8,256,128]{2,1,0:T(8,128)(2,1)S(1)} %get-tuple-element.203.own), channel_id=1, source_target_pairs={{0,4},{1,5},{2,6},{3,7},{12,8},{13,9},{14,10},{15,11},{4,12},{5,13... | collective-permute-start | bytes 1572872 | tf_op jit(solution)/shard_map/ppermute | solution.py:380
  175.3 16.4 %collective-permute-start.50 = (bf16[8,256,128]{2,1,0:T(8,128)(2,1)S(1)}, bf16[8,256,128]{2,1,0:T(8,128)(2,1)S(1)}, u32[]{:S(2)}, u32[]{:S(2)}) collective-permute-start(bf16[8,256,128]{2,1,0:T(8,128)(2,1)S(1)} %get-tuple-element.203.own), channel_id=1, source_target_pairs={{4,8},{5,9},{6,10},{7,11},{8,4},{9,5},{10,6},{11,7},{20,24},{21,25... | collective-permute-start | bytes 1572872 | tf_op jit(solution)/shard_map/ppermute | solution.py:380
  176.7 23.3 %collective-permute-start.52 = (bf16[8,256,128]{2,1,0:T(8,128)(2,1)S(1)}, bf16[8,256,128]{2,1,0:T(8,128)(2,1)S(1)}, u32[]{:S(2)}, u32[]{:S(2)}) collective-permute-start(bf16[8,256,128]{2,1,0:T(8,128)(2,1)S(1)} %collective-permute-done.51.refs_1_.first), channel_id=1, source_target_pairs={{4,0},{5,1},{6,2},{7,3},{8,12},{9,13},{10,14},{11,15},{20,16},{21,... | collective-permute-start | bytes 1572872 | tf_op jit(solution)/shard_map/ppermute | solution.py:380
  189.5 13.1 %collective-permute-start.58 = (bf16[6,256,128]{2,1,0:T(8,128)(2,1)S(1)}, bf16[6,256,128]{2,1,0:T(8,128)(2,1)S(1)}, u32[]{:S(2)}, u32[]{:S(2)}) collective-permute-start(bf16[6,256,128]{2,1,0:T(8,128)(2,1)S(1)} %get-tuple-element.212), channel_id=1, source_target_pairs={{0,1},{1,0},{2,3},{3,2},{4,5},{5,4},{6,7},{7,6},{8,9},{9,8},{10,11... | collective-permute-start | bytes 1179656 | tf_op jit(solution)/shard_map/ppermute | solution.py:384
  190.3 12.0 %collective-permute-start.60 = (bf16[3,256,128]{2,1,0:T(8,128)(2,1)S(1)}, bf16[3,256,128]{2,1,0:T(8,128)(2,1)S(1)}, u32[]{:S(2)}, u32[]{:S(2)}) collective-permute-start(bf16[3,256,128]{2,1,0:T(8,128)(2,1)S(1)} %get-tuple-element.218), channel_id=1, source_target_pairs={{0,2},{1,3},{2,0},{3,1},{4,6},{5,7},{6,4},{7,5},{8,10},{9,11},{10,... | collective-permute-start | bytes 589832 | tf_op jit(solution)/shard_map/ppermute | solution.py:384
  191.7 10.9 %collective-permute-start.61 = (bf16[3,256,128]{2,1,0:T(8,128)(2,1)S(1)}, bf16[3,256,128]{2,1,0:T(8,128)(2,1)S(1)}, u32[]{:S(2)}, u32[]{:S(2)}) collective-permute-start(bf16[3,256,128]{2,1,0:T(8,128)(2,1)S(1)} %get-tuple-element.219), channel_id=1, source_target_pairs={{0,3},{1,2},{2,1},{3,0},{4,7},{5,6},{6,5},{7,4},{8,11},{9,10},{10,... | collective-permute-start | bytes 589832 | tf_op jit(solution)/shard_map/ppermute | solution.py:384
  213.5 11.1 %all-to-all-start = ((f32[16,1,128]{2,1,0:T(1,128)}), f32[16,1,128]{2,1,0:T(1,128)S(1)}, u32[]{:S(2)}, u32[]{:S(2)}) async-start(f32[16,1,128]{2,1,0:T(1,128)} %get-tuple-element.226), calls=%async_computation | async-start | bytes 16384 | tf_op jit(solution)/shard_map/all_to_all | solution.py:388
  (37 other events, 250.3 us)

commit v19 on v17

--- a/solution.py
+++ b/solution.py
@@ -88,8 +88,8 @@
     slots, tile, _ = buffer.shape
     chunks = [pl.ds(first, GROUP) for first in range(0, slots, GROUP)]
     copies = [pltpu.make_async_copy(tiles.at[c], buffer.at[c], sems.at[i]) for i, c in enumerate(chunks)]
-    for copy in copies:
-        copy.start()
+    for i, copy in enumerate(copies):
+        pl.when(count[0] > i * GROUP)(copy.start)
 
     @pl.loop(0, 16)
     def _(d):
@@ -122,7 +122,7 @@
 
     acc = jnp.zeros((8, tile), jnp.float32)
     for i, copy in enumerate(copies):
-        copy.wait()
+        pl.when(count[0] > i * GROUP)(copy.wait)
         acc = lax.fori_loop(i * GROUP, jnp.clip(count[0], i * GROUP, (i + 1) * GROUP), add, acc)
     note[...] = jnp.where(lane == SUM_AT, jnp.sum(acc), wants.astype(jnp.float32))
 

time: 226 us -> 226 us (level)
  transfers between devices with their start and end apart: 63 -> 63, of which waited for: 38 -> 37; matrix products, arithmetic and copies ran while one was open for 0% -> 0% of each run, Pallas kernels for 12% -> 12%
where the time goes in v19:
time: 226 us; the launch traced here: 225 us
  waiting for transfers between devices  124 us (55%)
  starting transfers between devices  60.2 us (27%)
  Pallas kernels  32.5 us (14%)
  local copies, waits for them, and re-layouts  4.06 us (2%)
  between operations  2.42 us (1%)
    ppermute x46, waiting for transfers between devices, across(): return lax.ppermute(value, 'row', [(i, i ^ flip) for i in range(16)])  81.2 us
    ppermute x16, waiting for transfers between devices, along_z(): lax.ppermute(value, 'row', [(a * 4 + i, b * 4 + i) for a, b in pairs for...  38.3 us
    ppermute x46, starting transfers between devices, across(): return lax.ppermute(value, 'row', [(i, i ^ flip) for i in range(16)])  36.4 us
    ppermute x16, starting transfers between devices, along_z(): lax.ppermute(value, 'row', [(a * 4 + i, b * 4 + i) for a, b in pairs for...  18.9 us
    pallas_call x4, Pallas kernels, early(): pl.pallas_call(functools.partial(early_kernel, layout, parts), out_shape=...  13.9 us
    pallas_call x11, Pallas kernels, pack(): pl.pallas_call(picked, out_shape=[jax.ShapeDtypeStruct((size, tile, repl)...  6.59 us
    all_to_all x1, starting transfers between devices, row_sum(): lax.all_to_all(parts, 'row', split_axis=0, concat_axis=0, tiled=True)  4.81 us
  transfers between devices with their start and end apart: 63, of which 37 were waited for; matrix products, arithmetic and copies ran while one was open for 0% of the time, Pallas kernels for 12%

profile of v19, /device:TPU:0, one launch (start us, length us, event | category | flops | bytes accessed | tf_op | source)
XLA Modules:
  0.0 225.2 jit_solution(54782983439731578)
XLA Ops:
  1.9 4.1 %collective-permute-start = (bf16[8,256,128]{2,1,0:T(8,128)(2,1)S(1)}, bf16[8,256,128]{2,1,0:T(8,128)(2,1)S(1)}, u32[]{:S(2)}, u32[]{:S(2)}) collective-permute-start(bf16[8,256,128]{2,1,0:T(8,128)(2,1)S(1)} %convert_element_type.3.own.refs_1_), channel_id=1, source_target_pairs={{0,8},{1,9},{2,10},{3,11},{12,4},{13,5},{14,6},{15,7},{4,0},{5,1},... | collective-permute-start | bytes 1572872 | tf_op jit(solution)/shard_map/ppermute | solution.py:381
  6.7 2.7 %shard_map.85 = (s32[144]{0:T(256)}, f32[1,128]{1,0:T(1,128)}) custom-call(s32[48]{0:T(128)} %rows.1, s32[48]{0:T(128)} %cols.1, s32[1]{0:T(128)S(6)} %copy.9.count, bf16[48,256,256]{2,1,0:T(8,128)(2,1)} %tiles.19), custom_call_target="tpu_custom_call" | custom-call | tf_op jit(solution)/shard_map/pallas_call | solution.py:131
  10.8 2.7 %collective-permute-start.2 = (f32[1,128]{1,0:T(1,128)}, f32[1,128]{1,0:T(1,128)S(1)}, u32[]{:S(2)}, u32[]{:S(2)}) collective-permute-start(f32[1,128]{1,0:T(1,128)} %get-tuple-element.136), channel_id=1, source_target_pairs={{0,2},{1,3},{2,0},{3,1},{4,6},{5,7},{6,4},{7,5},{8,10},{9,11},{10,... | collective-permute-start | bytes 1544 | tf_op jit(solution)/shard_map/ppermute | solution.py:385
  24.1 6.2 %collective-permute-done.4.own.refs_3_.second = bf16[8,256,128]{2,1,0:T(8,128)(2,1)S(1)} collective-permute-done((bf16[8,256,128]{2,1,0:T(8,128)(2,1)S(1)}, bf16[8,256,128]{2,1,0:T(8,128)(2,1)S(1)}, u32[]{:S(2)}, u32[]{:S(2)}) %collective-permute-start.4) | collective-permute-done | bytes 524320 | tf_op jit(solution)/shard_map/ppermute | solution.py:381
  30.3 2.8 %copy-done = bf16[48,256,256]{2,1,0:T(8,128)(2,1)S(1)} copy-done((bf16[48,256,256]{2,1,0:T(8,128)(2,1)S(1)}, bf16[48,256,256]{2,1,0:T(8,128)(2,1)}, u32[]{:S(2)}) %copy-start) | copy-done | bytes 6291480
  33.1 3.8 %collective-permute-done.6.refs_1_ = bf16[6,256,128]{2,1,0:T(8,128)(2,1)S(1)} collective-permute-done((bf16[6,256,128]{2,1,0:T(8,128)(2,1)S(1)}, bf16[6,256,128]{2,1,0:T(8,128)(2,1)S(1)}, u32[]{:S(2)}, u32[]{:S(2)}) %collective-permute-start.6) | collective-permute-done | bytes 393248 | tf_op jit(solution)/shard_map/ppermute | solution.py:385
  47.3 2.4 %collective-permute-done.8.refs_3_ = bf16[3,256,128]{2,1,0:T(8,128)(2,1)S(1)} collective-permute-done((bf16[3,256,128]{2,1,0:T(8,128)(2,1)S(1)}, bf16[3,256,128]{2,1,0:T(8,128)(2,1)S(1)}, u32[]{:S(2)}, u32[]{:S(2)}) %collective-permute-start.8) | collective-permute-done | bytes 196640 | tf_op jit(solution)/shard_map/ppermute | solution.py:385
  49.7 3.4 %collective-permute-start.14 = (f32[1,128]{1,0:T(1,128)S(1)}, f32[1,128]{1,0:T(1,128)S(1)}, u32[]{:S(2)}, u32[]{:S(2)}) collective-permute-start(f32[1,128]{1,0:T(1,128)S(1)} %add.18), channel_id=1, source_target_pairs={{0,8},{1,9},{2,10},{3,11},{4,12},{5,13},{6,14},{7,15},{8,0},{9,1},... | collective-permute-start | bytes 1544 | tf_op jit(solution)/shard_map/ppermute | solution.py:385
  53.0 3.5 %shard_map.90.field = f32[9,256,128]{2,1,0:T(8,128)S(1)} custom-call(s32[180]{0:T(256)S(1)} %get-tuple-element.126.refs_0_.table, bf16[48,256,256]{2,1,0:T(8,128)(2,1)S(1)} %copy-done.1, bf16[8,256,128]{2,1,0:T(8,128)(2,1)S(1)} %convert_element_type.3.own.refs_1_, bf16[8,256,128]{2,1,0:T(8,128)(2,1)S(1)} %collective-permute-done.first.refs_2_, ...), custom_call_target="tpu_custom_call" | custom-call | tf_op jit(solution)/shard_map/pallas_call | solution.py:281
  59.4 2.8 %collective-permute-start.21 = (bf16[8,256,128]{2,1,0:T(8,128)(2,1)S(1)}, bf16[8,256,128]{2,1,0:T(8,128)(2,1)S(1)}, u32[]{:S(2)}, u32[]{:S(2)}) collective-permute-start(bf16[8,256,128]{2,1,0:T(8,128)(2,1)S(1)} %get-tuple-element.153.own), channel_id=1, source_target_pairs={{0,8},{1,9},{2,10},{3,11},{12,4},{13,5},{14,6},{15,7},{4,0},{5,1},... | collective-permute-start | bytes 1572872 | tf_op jit(solution)/shard_map/ppermute | solution.py:381
  64.1 6.2 %collective-permute-done.18.refs_0_ = bf16[3,256,128]{2,1,0:T(8,128)(2,1)S(1)} collective-permute-done((bf16[3,256,128]{2,1,0:T(8,128)(2,1)S(1)}, bf16[3,256,128]{2,1,0:T(8,128)(2,1)S(1)}, u32[]{:S(2)}, u32[]{:S(2)}) %collective-permute-start.18) | collective-permute-done | bytes 196640 | tf_op jit(solution)/shard_map/ppermute | solution.py:385
  70.3 2.5 %collective-permute-done.19.refs_1_ = bf16[3,256,128]{2,1,0:T(8,128)(2,1)S(1)} collective-permute-done((bf16[3,256,128]{2,1,0:T(8,128)(2,1)S(1)}, bf16[3,256,128]{2,1,0:T(8,128)(2,1)S(1)}, u32[]{:S(2)}, u32[]{:S(2)}) %collective-permute-start.19) | collective-permute-done | bytes 196640 | tf_op jit(solution)/shard_map/ppermute | solution.py:385
  78.0 6.2 %collective-permute-done.26.refs_2_ = bf16[3,256,128]{2,1,0:T(8,128)(2,1)S(1)} collective-permute-done((bf16[3,256,128]{2,1,0:T(8,128)(2,1)S(1)}, bf16[3,256,128]{2,1,0:T(8,128)(2,1)S(1)}, u32[]{:S(2)}, u32[]{:S(2)}) %collective-permute-start.26) | collective-permute-done | bytes 196640 | tf_op jit(solution)/shard_map/ppermute | solution.py:385
  89.9 8.6 %collective-permute-done.22.refs_2_.out = bf16[8,256,128]{2,1,0:T(8,128)(2,1)S(1)} collective-permute-done((bf16[8,256,128]{2,1,0:T(8,128)(2,1)S(1)}, bf16[8,256,128]{2,1,0:T(8,128)(2,1)S(1)}, u32[]{:S(2)}, u32[]{:S(2)}) %collective-permute-start.22) | collective-permute-done | bytes 524320 | tf_op jit(solution)/shard_map/ppermute | solution.py:381
  101.1 3.5 %shard_map.95.field = f32[9,256,128]{2,1,0:T(8,128)S(1)} custom-call(s32[180]{0:T(256)S(1)} %get-tuple-element.126.refs_0_.table, bf16[48,256,256]{2,1,0:T(8,128)(2,1)S(1)} %copy-done.1, bf16[8,256,128]{2,1,0:T(8,128)(2,1)S(1)} %get-tuple-element.153.own, bf16[8,256,128]{2,1,0:T(8,128)(2,1)S(1)} %collective-permute-done.21.refs_1_.first, ...), custom_call_target="tpu_custom_call" | custom-call | tf_op jit(solution)/shard_map/pallas_call | solution.py:281
  104.6 2.3 %collective-permute-done.23.got2 = bf16[3,256,128]{2,1,0:T(8,128)(2,1)S(1)} collective-permute-done((bf16[3,256,128]{2,1,0:T(8,128)(2,1)S(1)}, bf16[3,256,128]{2,1,0:T(8,128)(2,1)S(1)}, u32[]{:S(2)}, u32[]{:S(2)}) %collective-permute-start.23) | collective-permute-done | bytes 196640 | tf_op jit(solution)/shard_map/ppermute | solution.py:385
  106.9 3.3 %collective-permute-done.24.got3 = bf16[3,256,128]{2,1,0:T(8,128)(2,1)S(1)} collective-permute-done((bf16[3,256,128]{2,1,0:T(8,128)(2,1)S(1)}, bf16[3,256,128]{2,1,0:T(8,128)(2,1)S(1)}, u32[]{:S(2)}, u32[]{:S(2)}) %collective-permute-start.24) | collective-permute-done | bytes 196640 | tf_op jit(solution)/shard_map/ppermute | solution.py:385
  115.6 5.4 %collective-permute-done.33.refs_0_ = bf16[3,256,128]{2,1,0:T(8,128)(2,1)S(1)} collective-permute-done((bf16[3,256,128]{2,1,0:T(8,128)(2,1)S(1)}, bf16[3,256,128]{2,1,0:T(8,128)(2,1)S(1)}, u32[]{:S(2)}, u32[]{:S(2)}) %collective-permute-start.33) | collective-permute-done | bytes 196640 | tf_op jit(solution)/shard_map/ppermute | solution.py:385
  121.0 3.4 %collective-permute-done.34.refs_1_ = bf16[3,256,128]{2,1,0:T(8,128)(2,1)S(1)} collective-permute-done((bf16[3,256,128]{2,1,0:T(8,128)(2,1)S(1)}, bf16[3,256,128]{2,1,0:T(8,128)(2,1)S(1)}, u32[]{:S(2)}, u32[]{:S(2)}) %collective-permute-start.34) | collective-permute-done | bytes 196640 | tf_op jit(solution)/shard_map/ppermute | solution.py:385
  129.4 6.3 %collective-permute-done.41.refs_2_ = bf16[3,256,128]{2,1,0:T(8,128)(2,1)S(1)} collective-permute-done((bf16[3,256,128]{2,1,0:T(8,128)(2,1)S(1)}, bf16[3,256,128]{2,1,0:T(8,128)(2,1)S(1)}, u32[]{:S(2)}, u32[]{:S(2)}) %collective-permute-start.41) | collective-permute-done | bytes 196640 | tf_op jit(solution)/shard_map/ppermute | solution.py:385
  140.9 8.3 %collective-permute-done.37.refs_2_.out = bf16[8,256,128]{2,1,0:T(8,128)(2,1)S(1)} collective-permute-done((bf16[8,256,128]{2,1,0:T(8,128)(2,1)S(1)}, bf16[8,256,128]{2,1,0:T(8,128)(2,1)S(1)}, u32[]{:S(2)}, u32[]{:S(2)}) %collective-permute-start.37) | collective-permute-done | bytes 524320 | tf_op jit(solution)/shard_map/ppermute | solution.py:381
  151.9 3.5 %shard_map.100.field = f32[9,256,128]{2,1,0:T(8,128)S(1)} custom-call(s32[180]{0:T(256)S(1)} %get-tuple-element.126.refs_0_.table, bf16[48,256,256]{2,1,0:T(8,128)(2,1)S(1)} %copy-done.1, bf16[8,256,128]{2,1,0:T(8,128)(2,1)S(1)} %get-tuple-element.178.own, bf16[8,256,128]{2,1,0:T(8,128)(2,1)S(1)} %collective-permute-done.36.refs_1_.first, ...), custom_call_target="tpu_custom_call" | custom-call | tf_op jit(solution)/shard_map/pallas_call | solution.py:281
  157.7 3.3 %collective-permute-done.39.got3 = bf16[3,256,128]{2,1,0:T(8,128)(2,1)S(1)} collective-permute-done((bf16[3,256,128]{2,1,0:T(8,128)(2,1)S(1)}, bf16[3,256,128]{2,1,0:T(8,128)(2,1)S(1)}, u32[]{:S(2)}, u32[]{:S(2)}) %collective-permute-start.39) | collective-permute-done | bytes 196640 | tf_op jit(solution)/shard_map/ppermute | solution.py:385
  166.3 5.4 %collective-permute-done.48.refs_0_ = bf16[3,256,128]{2,1,0:T(8,128)(2,1)S(1)} collective-permute-done((bf16[3,256,128]{2,1,0:T(8,128)(2,1)S(1)}, bf16[3,256,128]{2,1,0:T(8,128)(2,1)S(1)}, u32[]{:S(2)}, u32[]{:S(2)}) %collective-permute-start.48) | collective-permute-done | bytes 196640 | tf_op jit(solution)/shard_map/ppermute | solution.py:385
  171.8 3.4 %collective-permute-done.49.refs_1_ = bf16[3,256,128]{2,1,0:T(8,128)(2,1)S(1)} collective-permute-done((bf16[3,256,128]{2,1,0:T(8,128)(2,1)S(1)}, bf16[3,256,128]{2,1,0:T(8,128)(2,1)S(1)}, u32[]{:S(2)}, u32[]{:S(2)}) %collective-permute-start.49) | collective-permute-done | bytes 196640 | tf_op jit(solution)/shard_map/ppermute | solution.py:385
  180.1 6.3 %collective-permute-done.56.refs_2_ = bf16[3,256,128]{2,1,0:T(8,128)(2,1)S(1)} collective-permute-done((bf16[3,256,128]{2,1,0:T(8,128)(2,1)S(1)}, bf16[3,256,128]{2,1,0:T(8,128)(2,1)S(1)}, u32[]{:S(2)}, u32[]{:S(2)}) %collective-permute-start.56) | collective-permute-done | bytes 196640 | tf_op jit(solution)/shard_map/ppermute | solution.py:385
  191.7 8.3 %collective-permute-done.52.refs_2_.out = bf16[8,256,128]{2,1,0:T(8,128)(2,1)S(1)} collective-permute-done((bf16[8,256,128]{2,1,0:T(8,128)(2,1)S(1)}, bf16[8,256,128]{2,1,0:T(8,128)(2,1)S(1)}, u32[]{:S(2)}, u32[]{:S(2)}) %collective-permute-start.52) | collective-permute-done | bytes 524320 | tf_op jit(solution)/shard_map/ppermute | solution.py:381
  202.5 3.5 %shard_map.105.field = f32[9,256,128]{2,1,0:T(8,128)S(1)} custom-call(s32[180]{0:T(256)S(1)} %get-tuple-element.126.refs_0_.table, bf16[48,256,256]{2,1,0:T(8,128)(2,1)S(1)} %copy-done.1, bf16[8,256,128]{2,1,0:T(8,128)(2,1)S(1)} %get-tuple-element.203.own, bf16[8,256,128]{2,1,0:T(8,128)(2,1)S(1)} %collective-permute-done.51.refs_1_.first, ...), custom_call_target="tpu_custom_call" | custom-call | tf_op jit(solution)/shard_map/pallas_call | solution.py:281
  206.0 2.4 %collective-permute-done.53.got2 = bf16[3,256,128]{2,1,0:T(8,128)(2,1)S(1)} collective-permute-done((bf16[3,256,128]{2,1,0:T(8,128)(2,1)S(1)}, bf16[3,256,128]{2,1,0:T(8,128)(2,1)S(1)}, u32[]{:S(2)}, u32[]{:S(2)}) %collective-permute-start.53) | collective-permute-done | bytes 196640 | tf_op jit(solution)/shard_map/ppermute | solution.py:385
  208.4 3.3 %collective-permute-done.54.got3 = bf16[3,256,128]{2,1,0:T(8,128)(2,1)S(1)} collective-permute-done((bf16[3,256,128]{2,1,0:T(8,128)(2,1)S(1)}, bf16[3,256,128]{2,1,0:T(8,128)(2,1)S(1)}, u32[]{:S(2)}, u32[]{:S(2)}) %collective-permute-start.54) | collective-permute-done | bytes 196640 | tf_op jit(solution)/shard_map/ppermute | solution.py:385
  213.4 4.8 %all-to-all-start = ((f32[16,1,128]{2,1,0:T(1,128)}), f32[16,1,128]{2,1,0:T(1,128)S(1)}, u32[]{:S(2)}, u32[]{:S(2)}) async-start(f32[16,1,128]{2,1,0:T(1,128)} %get-tuple-element.226), calls=%async_computation | async-start | bytes 16384 | tf_op jit(solution)/shard_map/all_to_all | solution.py:389
  220.3 4.3 %all-to-all-done = f32[16,1,128]{2,1,0:T(1,128)S(1)} async-done(((f32[16,1,128]{2,1,0:T(1,128)}), f32[16,1,128]{2,1,0:T(1,128)S(1)}, u32[]{:S(2)}, u32[]{:S(2)}) %all-to-all-start) | async-done | bytes 8224 | tf_op jit(solution)/shard_map/all_to_all | solution.py:389
  (139 shorter events, 83.9 us)
Async XLA Ops:
  1.9 16.5 %collective-permute-start = (bf16[8,256,128]{2,1,0:T(8,128)(2,1)S(1)}, bf16[8,256,128]{2,1,0:T(8,128)(2,1)S(1)}, u32[]{:S(2)}, u32[]{:S(2)}) collective-permute-start(bf16[8,256,128]{2,1,0:T(8,128)(2,1)S(1)} %convert_element_type.3.own.refs_1_), channel_id=1, source_target_pairs={{0,8},{1,9},{2,10},{3,11},{12,4},{13,5},{14,6},{15,7},{4,0},{5,1},... | collective-permute-start | bytes 1572872 | tf_op jit(solution)/shard_map/ppermute | solution.py:381
  10.7 19.6 %collective-permute-start.4 = (bf16[8,256,128]{2,1,0:T(8,128)(2,1)S(1)}, bf16[8,256,128]{2,1,0:T(8,128)(2,1)S(1)}, u32[]{:S(2)}, u32[]{:S(2)}) collective-permute-start(bf16[8,256,128]{2,1,0:T(8,128)(2,1)S(1)} %convert_element_type.3.own.refs_1_), channel_id=1, source_target_pairs={{0,4},{1,5},{2,6},{3,7},{12,8},{13,9},{14,10},{15,11},{4,12},{5,13... | collective-permute-start | bytes 1572872 | tf_op jit(solution)/shard_map/ppermute | solution.py:381
  20.5 12.6 %collective-permute-start.5 = (bf16[6,256,128]{2,1,0:T(8,128)(2,1)S(1)}, bf16[6,256,128]{2,1,0:T(8,128)(2,1)S(1)}, u32[]{:S(2)}, u32[]{:S(2)}) collective-permute-start(bf16[6,256,128]{2,1,0:T(8,128)(2,1)S(1)} %get-tuple-element.127), channel_id=1, source_target_pairs={{0,2},{1,3},{2,0},{3,1},{4,6},{5,7},{6,4},{7,5},{8,10},{9,11},{10,... | collective-permute-start | bytes 1179656 | tf_op jit(solution)/shard_map/ppermute | solution.py:385
  22.1 14.8 %collective-permute-start.6 = (bf16[6,256,128]{2,1,0:T(8,128)(2,1)S(1)}, bf16[6,256,128]{2,1,0:T(8,128)(2,1)S(1)}, u32[]{:S(2)}, u32[]{:S(2)}) collective-permute-start(bf16[6,256,128]{2,1,0:T(8,128)(2,1)S(1)} %get-tuple-element.128), channel_id=1, source_target_pairs={{0,3},{1,2},{2,1},{3,0},{4,7},{5,6},{6,5},{7,4},{8,11},{9,10},{10,... | collective-permute-start | bytes 1179656 | tf_op jit(solution)/shard_map/ppermute | solution.py:385
  22.1 18.6 %collective-permute-start.9 = (bf16[8,256,128]{2,1,0:T(8,128)(2,1)S(1)}, bf16[8,256,128]{2,1,0:T(8,128)(2,1)S(1)}, u32[]{:S(2)}, u32[]{:S(2)}) collective-permute-start(bf16[8,256,128]{2,1,0:T(8,128)(2,1)S(1)} %convert_element_type.3.own.refs_1_), channel_id=1, source_target_pairs={{4,8},{5,9},{6,10},{7,11},{8,4},{9,5},{10,6},{11,7},{20,24},{21,25... | collective-permute-start | bytes 1572872 | tf_op jit(solution)/shard_map/ppermute | solution.py:381
  22.8 18.9 %collective-permute-start.10 = (bf16[8,256,128]{2,1,0:T(8,128)(2,1)S(1)}, bf16[8,256,128]{2,1,0:T(8,128)(2,1)S(1)}, u32[]{:S(2)}, u32[]{:S(2)}) collective-permute-start(bf16[8,256,128]{2,1,0:T(8,128)(2,1)S(1)} %collective-permute-done.first.refs_2_), channel_id=1, source_target_pairs={{4,0},{5,1},{6,2},{7,3},{8,12},{9,13},{10,14},{11,15},{20,16},{21,... | collective-permute-start | bytes 1572872 | tf_op jit(solution)/shard_map/ppermute | solution.py:381
  37.5 15.5 %collective-permute-start.12 = (bf16[9,256,128]{2,1,0:T(8,128)(2,1)S(1)}, bf16[9,256,128]{2,1,0:T(8,128)(2,1)S(1)}, u32[]{:S(2)}, u32[]{:S(2)}) collective-permute-start(bf16[9,256,128]{2,1,0:T(8,128)(2,1)S(1)} %get-tuple-element.138), channel_id=1, source_target_pairs={{0,1},{1,0},{2,3},{3,2},{4,5},{5,4},{6,7},{7,6},{8,9},{9,8},{10,11... | collective-permute-start | bytes 1769480 | tf_op jit(solution)/shard_map/ppermute | solution.py:385
  42.3 10.8 %collective-permute-start.13 = (bf16[3,256,128]{2,1,0:T(8,128)(2,1)S(1)}, bf16[3,256,128]{2,1,0:T(8,128)(2,1)S(1)}, u32[]{:S(2)}, u32[]{:S(2)}) collective-permute-start(bf16[3,256,128]{2,1,0:T(8,128)(2,1)S(1)} %get-tuple-element.139), channel_id=1, source_target_pairs={{0,1},{1,0},{2,3},{3,2},{4,5},{5,4},{6,7},{7,6},{8,9},{9,8},{10,11... | collective-permute-start | bytes 589832 | tf_op jit(solution)/shard_map/ppermute | solution.py:385
  46.0 12.0 %collective-permute-start.15 = (bf16[3,256,128]{2,1,0:T(8,128)(2,1)S(1)}, bf16[3,256,128]{2,1,0:T(8,128)(2,1)S(1)}, u32[]{:S(2)}, u32[]{:S(2)}) collective-permute-start(bf16[3,256,128]{2,1,0:T(8,128)(2,1)S(1)} %get-tuple-element.145), channel_id=1, source_target_pairs={{0,2},{1,3},{2,0},{3,1},{4,6},{5,7},{6,4},{7,5},{8,10},{9,11},{10,... | collective-permute-start | bytes 589832 | tf_op jit(solution)/shard_map/ppermute | solution.py:385
  47.2 10.7 %collective-permute-start.16 = (bf16[3,256,128]{2,1,0:T(8,128)(2,1)S(1)}, bf16[3,256,128]{2,1,0:T(8,128)(2,1)S(1)}, u32[]{:S(2)}, u32[]{:S(2)}) collective-permute-start(bf16[3,256,128]{2,1,0:T(8,128)(2,1)S(1)} %get-tuple-element.146), channel_id=1, source_target_pairs={{0,3},{1,2},{2,1},{3,0},{4,7},{5,6},{6,5},{7,4},{8,11},{9,10},{10,... | collective-permute-start | bytes 589832 | tf_op jit(solution)/shard_map/ppermute | solution.py:385
  59.4 15.1 %collective-permute-start.21 = (bf16[8,256,128]{2,1,0:T(8,128)(2,1)S(1)}, bf16[8,256,128]{2,1,0:T(8,128)(2,1)S(1)}, u32[]{:S(2)}, u32[]{:S(2)}) collective-permute-start(bf16[8,256,128]{2,1,0:T(8,128)(2,1)S(1)} %get-tuple-element.153.own), channel_id=1, source_target_pairs={{0,8},{1,9},{2,10},{3,11},{12,4},{13,5},{14,6},{15,7},{4,0},{5,1},... | collective-permute-start | bytes 1572872 | tf_op jit(solution)/shard_map/ppermute | solution.py:381
  64.1 23.2 %collective-permute-start.25 = (bf16[8,256,128]{2,1,0:T(8,128)(2,1)S(1)}, bf16[8,256,128]{2,1,0:T(8,128)(2,1)S(1)}, u32[]{:S(2)}, u32[]{:S(2)}) collective-permute-start(bf16[8,256,128]{2,1,0:T(8,128)(2,1)S(1)} %get-tuple-element.153.own), channel_id=1, source_target_pairs={{0,4},{1,5},{2,6},{3,7},{12,8},{13,9},{14,10},{15,11},{4,12},{5,13... | collective-permute-start | bytes 1572872 | tf_op jit(solution)/shard_map/ppermute | solution.py:381
  72.8 17.1 %collective-permute-start.20 = (bf16[8,256,128]{2,1,0:T(8,128)(2,1)S(1)}, bf16[8,256,128]{2,1,0:T(8,128)(2,1)S(1)}, u32[]{:S(2)}, u32[]{:S(2)}) collective-permute-start(bf16[8,256,128]{2,1,0:T(8,128)(2,1)S(1)} %get-tuple-element.153.own), channel_id=1, source_target_pairs={{4,8},{5,9},{6,10},{7,11},{8,4},{9,5},{10,6},{11,7},{20,24},{21,25... | collective-permute-start | bytes 1572872 | tf_op jit(solution)/shard_map/ppermute | solution.py:381
  74.5 24.0 %collective-permute-start.22 = (bf16[8,256,128]{2,1,0:T(8,128)(2,1)S(1)}, bf16[8,256,128]{2,1,0:T(8,128)(2,1)S(1)}, u32[]{:S(2)}, u32[]{:S(2)}) collective-permute-start(bf16[8,256,128]{2,1,0:T(8,128)(2,1)S(1)} %collective-permute-done.21.refs_1_.first), channel_id=1, source_target_pairs={{4,0},{5,1},{6,2},{7,3},{8,12},{9,13},{10,14},{11,15},{20,16},{21,... | collective-permute-start | bytes 1572872 | tf_op jit(solution)/shard_map/ppermute | solution.py:381
  87.9 13.2 %collective-permute-start.28 = (bf16[6,256,128]{2,1,0:T(8,128)(2,1)S(1)}, bf16[6,256,128]{2,1,0:T(8,128)(2,1)S(1)}, u32[]{:S(2)}, u32[]{:S(2)}) collective-permute-start(bf16[6,256,128]{2,1,0:T(8,128)(2,1)S(1)} %get-tuple-element.162), channel_id=1, source_target_pairs={{0,1},{1,0},{2,3},{3,2},{4,5},{5,4},{6,7},{7,6},{8,9},{9,8},{10,11... | collective-permute-start | bytes 1179656 | tf_op jit(solution)/shard_map/ppermute | solution.py:385
  88.3 12.5 %collective-permute-start.30 = (bf16[3,256,128]{2,1,0:T(8,128)(2,1)S(1)}, bf16[3,256,128]{2,1,0:T(8,128)(2,1)S(1)}, u32[]{:S(2)}, u32[]{:S(2)}) collective-permute-start(bf16[3,256,128]{2,1,0:T(8,128)(2,1)S(1)} %get-tuple-element.168), channel_id=1, source_target_pairs={{0,2},{1,3},{2,0},{3,1},{4,6},{5,7},{6,4},{7,5},{8,10},{9,11},{10,... | collective-permute-start | bytes 589832 | tf_op jit(solution)/shard_map/ppermute | solution.py:385
  89.8 11.3 %collective-permute-start.31 = (bf16[3,256,128]{2,1,0:T(8,128)(2,1)S(1)}, bf16[3,256,128]{2,1,0:T(8,128)(2,1)S(1)}, u32[]{:S(2)}, u32[]{:S(2)}) collective-permute-start(bf16[3,256,128]{2,1,0:T(8,128)(2,1)S(1)} %get-tuple-element.169), channel_id=1, source_target_pairs={{0,3},{1,2},{2,1},{3,0},{4,7},{5,6},{6,5},{7,4},{8,11},{9,10},{10,... | collective-permute-start | bytes 589832 | tf_op jit(solution)/shard_map/ppermute | solution.py:385
  111.6 14.3 %collective-permute-start.36 = (bf16[8,256,128]{2,1,0:T(8,128)(2,1)S(1)}, bf16[8,256,128]{2,1,0:T(8,128)(2,1)S(1)}, u32[]{:S(2)}, u32[]{:S(2)}) collective-permute-start(bf16[8,256,128]{2,1,0:T(8,128)(2,1)S(1)} %get-tuple-element.178.own), channel_id=1, source_target_pairs={{0,8},{1,9},{2,10},{3,11},{12,4},{13,5},{14,6},{15,7},{4,0},{5,1},... | collective-permute-start | bytes 1572872 | tf_op jit(solution)/shard_map/ppermute | solution.py:381
  115.2 22.9 %collective-permute-start.40 = (bf16[8,256,128]{2,1,0:T(8,128)(2,1)S(1)}, bf16[8,256,128]{2,1,0:T(8,128)(2,1)S(1)}, u32[]{:S(2)}, u32[]{:S(2)}) collective-permute-start(bf16[8,256,128]{2,1,0:T(8,128)(2,1)S(1)} %get-tuple-element.178.own), channel_id=1, source_target_pairs={{0,4},{1,5},{2,6},{3,7},{12,8},{13,9},{14,10},{15,11},{4,12},{5,13... | collective-permute-start | bytes 1572872 | tf_op jit(solution)/shard_map/ppermute | solution.py:381
  124.4 16.5 %collective-permute-start.35 = (bf16[8,256,128]{2,1,0:T(8,128)(2,1)S(1)}, bf16[8,256,128]{2,1,0:T(8,128)(2,1)S(1)}, u32[]{:S(2)}, u32[]{:S(2)}) collective-permute-start(bf16[8,256,128]{2,1,0:T(8,128)(2,1)S(1)} %get-tuple-element.178.own), channel_id=1, source_target_pairs={{4,8},{5,9},{6,10},{7,11},{8,4},{9,5},{10,6},{11,7},{20,24},{21,25... | collective-permute-start | bytes 1572872 | tf_op jit(solution)/shard_map/ppermute | solution.py:381
  125.9 23.3 %collective-permute-start.37 = (bf16[8,256,128]{2,1,0:T(8,128)(2,1)S(1)}, bf16[8,256,128]{2,1,0:T(8,128)(2,1)S(1)}, u32[]{:S(2)}, u32[]{:S(2)}) collective-permute-start(bf16[8,256,128]{2,1,0:T(8,128)(2,1)S(1)} %collective-permute-done.36.refs_1_.first), channel_id=1, source_target_pairs={{4,0},{5,1},{6,2},{7,3},{8,12},{9,13},{10,14},{11,15},{20,16},{21,... | collective-permute-start | bytes 1572872 | tf_op jit(solution)/shard_map/ppermute | solution.py:381
  138.7 13.2 %collective-permute-start.43 = (bf16[6,256,128]{2,1,0:T(8,128)(2,1)S(1)}, bf16[6,256,128]{2,1,0:T(8,128)(2,1)S(1)}, u32[]{:S(2)}, u32[]{:S(2)}) collective-permute-start(bf16[6,256,128]{2,1,0:T(8,128)(2,1)S(1)} %get-tuple-element.187), channel_id=1, source_target_pairs={{0,1},{1,0},{2,3},{3,2},{4,5},{5,4},{6,7},{7,6},{8,9},{9,8},{10,11... | collective-permute-start | bytes 1179656 | tf_op jit(solution)/shard_map/ppermute | solution.py:385
  139.4 12.1 %collective-permute-start.45 = (bf16[3,256,128]{2,1,0:T(8,128)(2,1)S(1)}, bf16[3,256,128]{2,1,0:T(8,128)(2,1)S(1)}, u32[]{:S(2)}, u32[]{:S(2)}) collective-permute-start(bf16[3,256,128]{2,1,0:T(8,128)(2,1)S(1)} %get-tuple-element.193), channel_id=1, source_target_pairs={{0,2},{1,3},{2,0},{3,1},{4,6},{5,7},{6,4},{7,5},{8,10},{9,11},{10,... | collective-permute-start | bytes 589832 | tf_op jit(solution)/shard_map/ppermute | solution.py:385
  140.9 10.9 %collective-permute-start.46 = (bf16[3,256,128]{2,1,0:T(8,128)(2,1)S(1)}, bf16[3,256,128]{2,1,0:T(8,128)(2,1)S(1)}, u32[]{:S(2)}, u32[]{:S(2)}) collective-permute-start(bf16[3,256,128]{2,1,0:T(8,128)(2,1)S(1)} %get-tuple-element.194), channel_id=1, source_target_pairs={{0,3},{1,2},{2,1},{3,0},{4,7},{5,6},{6,5},{7,4},{8,11},{9,10},{10,... | collective-permute-start | bytes 589832 | tf_op jit(solution)/shard_map/ppermute | solution.py:385
  162.4 14.3 %collective-permute-start.51 = (bf16[8,256,128]{2,1,0:T(8,128)(2,1)S(1)}, bf16[8,256,128]{2,1,0:T(8,128)(2,1)S(1)}, u32[]{:S(2)}, u32[]{:S(2)}) collective-permute-start(bf16[8,256,128]{2,1,0:T(8,128)(2,1)S(1)} %get-tuple-element.203.own), channel_id=1, source_target_pairs={{0,8},{1,9},{2,10},{3,11},{12,4},{13,5},{14,6},{15,7},{4,0},{5,1},... | collective-permute-start | bytes 1572872 | tf_op jit(solution)/shard_map/ppermute | solution.py:381
  165.9 22.9 %collective-permute-start.55 = (bf16[8,256,128]{2,1,0:T(8,128)(2,1)S(1)}, bf16[8,256,128]{2,1,0:T(8,128)(2,1)S(1)}, u32[]{:S(2)}, u32[]{:S(2)}) collective-permute-start(bf16[8,256,128]{2,1,0:T(8,128)(2,1)S(1)} %get-tuple-element.203.own), channel_id=1, source_target_pairs={{0,4},{1,5},{2,6},{3,7},{12,8},{13,9},{14,10},{15,11},{4,12},{5,13... | collective-permute-start | bytes 1572872 | tf_op jit(solution)/shard_map/ppermute | solution.py:381
  175.2 16.5 %collective-permute-start.50 = (bf16[8,256,128]{2,1,0:T(8,128)(2,1)S(1)}, bf16[8,256,128]{2,1,0:T(8,128)(2,1)S(1)}, u32[]{:S(2)}, u32[]{:S(2)}) collective-permute-start(bf16[8,256,128]{2,1,0:T(8,128)(2,1)S(1)} %get-tuple-element.203.own), channel_id=1, source_target_pairs={{4,8},{5,9},{6,10},{7,11},{8,4},{9,5},{10,6},{11,7},{20,24},{21,25... | collective-permute-start | bytes 1572872 | tf_op jit(solution)/shard_map/ppermute | solution.py:381
  176.6 23.3 %collective-permute-start.52 = (bf16[8,256,128]{2,1,0:T(8,128)(2,1)S(1)}, bf16[8,256,128]{2,1,0:T(8,128)(2,1)S(1)}, u32[]{:S(2)}, u32[]{:S(2)}) collective-permute-start(bf16[8,256,128]{2,1,0:T(8,128)(2,1)S(1)} %collective-permute-done.51.refs_1_.first), channel_id=1, source_target_pairs={{4,0},{5,1},{6,2},{7,3},{8,12},{9,13},{10,14},{11,15},{20,16},{21,... | collective-permute-start | bytes 1572872 | tf_op jit(solution)/shard_map/ppermute | solution.py:381
  189.5 13.1 %collective-permute-start.58 = (bf16[6,256,128]{2,1,0:T(8,128)(2,1)S(1)}, bf16[6,256,128]{2,1,0:T(8,128)(2,1)S(1)}, u32[]{:S(2)}, u32[]{:S(2)}) collective-permute-start(bf16[6,256,128]{2,1,0:T(8,128)(2,1)S(1)} %get-tuple-element.212), channel_id=1, source_target_pairs={{0,1},{1,0},{2,3},{3,2},{4,5},{5,4},{6,7},{7,6},{8,9},{9,8},{10,11... | collective-permute-start | bytes 1179656 | tf_op jit(solution)/shard_map/ppermute | solution.py:385
  190.2 12.1 %collective-permute-start.60 = (bf16[3,256,128]{2,1,0:T(8,128)(2,1)S(1)}, bf16[3,256,128]{2,1,0:T(8,128)(2,1)S(1)}, u32[]{:S(2)}, u32[]{:S(2)}) collective-permute-start(bf16[3,256,128]{2,1,0:T(8,128)(2,1)S(1)} %get-tuple-element.218), channel_id=1, source_target_pairs={{0,2},{1,3},{2,0},{3,1},{4,6},{5,7},{6,4},{7,5},{8,10},{9,11},{10,... | collective-permute-start | bytes 589832 | tf_op jit(solution)/shard_map/ppermute | solution.py:385
  191.7 10.8 %collective-permute-start.61 = (bf16[3,256,128]{2,1,0:T(8,128)(2,1)S(1)}, bf16[3,256,128]{2,1,0:T(8,128)(2,1)S(1)}, u32[]{:S(2)}, u32[]{:S(2)}) collective-permute-start(bf16[3,256,128]{2,1,0:T(8,128)(2,1)S(1)} %get-tuple-element.219), channel_id=1, source_target_pairs={{0,3},{1,2},{2,1},{3,0},{4,7},{5,6},{6,5},{7,4},{8,11},{9,10},{10,... | collective-permute-start | bytes 589832 | tf_op jit(solution)/shard_map/ppermute | solution.py:385
  213.4 11.2 %all-to-all-start = ((f32[16,1,128]{2,1,0:T(1,128)}), f32[16,1,128]{2,1,0:T(1,128)S(1)}, u32[]{:S(2)}, u32[]{:S(2)}) async-start(f32[16,1,128]{2,1,0:T(1,128)} %get-tuple-element.226), calls=%async_computation | async-start | bytes 16384 | tf_op jit(solution)/shard_map/all_to_all | solution.py:389
  (37 other events, 250.2 us)

commit v20 on v17

--- a/solution.py
+++ b/solution.py
@@ -431,8 +431,7 @@
             again, core0 = lax.optimization_barrier((own0, core0))
             own2 = along_z(SECOND, again)
             got0 = to_other_y(packs0)
-            again, got0 = lax.optimization_barrier((again, got0))
-            own1, got0 = lax.optimization_barrier((own1, got0))
+            again, own1, got0 = lax.optimization_barrier((again, own1, got0))
             packs1 = other_y((1,), [own1])
             out = along_z(OUTWARD, own1)
             got1 = to_other_y(packs1)

time: 226 us -> 228 us (level)
    ppermute x16, waiting for transfers between devices: 38.1 us -> 40.7 us  [along_z(): lax.ppermute(value, 'row', [(a * 4 + i, b * 4 + i) for a, b in pairs for...]
where the time goes in v20:
time: 228 us; the launch traced here: 227 us
  waiting for transfers between devices  126 us (55%)
  starting transfers between devices  59 us (26%)
  Pallas kernels  34 us (15%)
  local copies, waits for them, and re-layouts  4.06 us (2%)
  between operations  2.41 us (1%)
    ppermute x46, waiting for transfers between devices, across(): return lax.ppermute(value, 'row', [(i, i ^ flip) for i in range(16)])  80.8 us
    ppermute x16, waiting for transfers between devices, along_z(): lax.ppermute(value, 'row', [(a * 4 + i, b * 4 + i) for a, b in pairs for...  40.7 us
    ppermute x46, starting transfers between devices, across(): return lax.ppermute(value, 'row', [(i, i ^ flip) for i in range(16)])  35.1 us
    ppermute x16, starting transfers between devices, along_z(): lax.ppermute(value, 'row', [(a * 4 + i, b * 4 + i) for a, b in pairs for...  19 us
    pallas_call x4, Pallas kernels, early(): pl.pallas_call(functools.partial(early_kernel, layout, parts), out_shape=...  13.9 us
    pallas_call x11, Pallas kernels, pack(): pl.pallas_call(picked, out_shape=[jax.ShapeDtypeStruct((size, tile, repl)...  6.59 us
    all_to_all x1, starting transfers between devices, row_sum(): lax.all_to_all(parts, 'row', split_axis=0, concat_axis=0, tiled=True)  4.83 us
  transfers between devices with their start and end apart: 63, of which 38 were waited for; matrix products, arithmetic and copies ran while one was open for 0% of the time, Pallas kernels for 12%

profile of v20, /device:TPU:0, one launch (start us, length us, event | category | flops | bytes accessed | tf_op | source)
XLA Modules:
  0.0 227.4 jit_solution(14872520844233252298)
XLA Ops:
  1.9 4.1 %collective-permute-start = (bf16[8,256,128]{2,1,0:T(8,128)(2,1)S(1)}, bf16[8,256,128]{2,1,0:T(8,128)(2,1)S(1)}, u32[]{:S(2)}, u32[]{:S(2)}) collective-permute-start(bf16[8,256,128]{2,1,0:T(8,128)(2,1)S(1)} %convert_element_type.3.own.refs_1_), channel_id=1, source_target_pairs={{0,8},{1,9},{2,10},{3,11},{12,4},{13,5},{14,6},{15,7},{4,0},{5,1},... | collective-permute-start | bytes 1572872 | tf_op jit(solution)/shard_map/ppermute | solution.py:381
  6.7 4.2 %shard_map.85 = (s32[144]{0:T(256)}, f32[1,128]{1,0:T(1,128)}) custom-call(s32[48]{0:T(128)} %rows.1, s32[48]{0:T(128)} %cols.1, s32[1]{0:T(128)S(6)} %copy.9.count, bf16[48,256,256]{2,1,0:T(8,128)(2,1)} %tiles.19), custom_call_target="tpu_custom_call" | custom-call | tf_op jit(solution)/shard_map/pallas_call | solution.py:131
  24.1 6.2 %collective-permute-done.4.own.refs_3_.second = bf16[8,256,128]{2,1,0:T(8,128)(2,1)S(1)} collective-permute-done((bf16[8,256,128]{2,1,0:T(8,128)(2,1)S(1)}, bf16[8,256,128]{2,1,0:T(8,128)(2,1)S(1)}, u32[]{:S(2)}, u32[]{:S(2)}) %collective-permute-start.4) | collective-permute-done | bytes 524320 | tf_op jit(solution)/shard_map/ppermute | solution.py:381
  30.3 2.8 %copy-done = bf16[48,256,256]{2,1,0:T(8,128)(2,1)S(1)} copy-done((bf16[48,256,256]{2,1,0:T(8,128)(2,1)S(1)}, bf16[48,256,256]{2,1,0:T(8,128)(2,1)}, u32[]{:S(2)}) %copy-start) | copy-done | bytes 6291480
  33.1 3.8 %collective-permute-done.6.refs_1_ = bf16[6,256,128]{2,1,0:T(8,128)(2,1)S(1)} collective-permute-done((bf16[6,256,128]{2,1,0:T(8,128)(2,1)S(1)}, bf16[6,256,128]{2,1,0:T(8,128)(2,1)S(1)}, u32[]{:S(2)}, u32[]{:S(2)}) %collective-permute-start.6) | collective-permute-done | bytes 393248 | tf_op jit(solution)/shard_map/ppermute | solution.py:385
  47.3 2.4 %collective-permute-done.8.refs_3_ = bf16[3,256,128]{2,1,0:T(8,128)(2,1)S(1)} collective-permute-done((bf16[3,256,128]{2,1,0:T(8,128)(2,1)S(1)}, bf16[3,256,128]{2,1,0:T(8,128)(2,1)S(1)}, u32[]{:S(2)}, u32[]{:S(2)}) %collective-permute-start.8) | collective-permute-done | bytes 196640 | tf_op jit(solution)/shard_map/ppermute | solution.py:385
  49.7 3.4 %collective-permute-start.14 = (f32[1,128]{1,0:T(1,128)S(1)}, f32[1,128]{1,0:T(1,128)S(1)}, u32[]{:S(2)}, u32[]{:S(2)}) collective-permute-start(f32[1,128]{1,0:T(1,128)S(1)} %add.18), channel_id=1, source_target_pairs={{0,8},{1,9},{2,10},{3,11},{4,12},{5,13},{6,14},{7,15},{8,0},{9,1},... | collective-permute-start | bytes 1544 | tf_op jit(solution)/shard_map/ppermute | solution.py:385
  53.1 3.5 %shard_map.90.field = f32[9,256,128]{2,1,0:T(8,128)S(1)} custom-call(s32[180]{0:T(256)S(1)} %get-tuple-element.120.refs_0_.table, bf16[48,256,256]{2,1,0:T(8,128)(2,1)S(1)} %copy-done.1, bf16[8,256,128]{2,1,0:T(8,128)(2,1)S(1)} %convert_element_type.3.own.refs_1_, bf16[8,256,128]{2,1,0:T(8,128)(2,1)S(1)} %collective-permute-done.first.refs_2_, ...), custom_call_target="tpu_custom_call" | custom-call | tf_op jit(solution)/shard_map/pallas_call | solution.py:281
  59.5 2.7 %collective-permute-start.18 = (bf16[8,256,128]{2,1,0:T(8,128)(2,1)S(1)}, bf16[8,256,128]{2,1,0:T(8,128)(2,1)S(1)}, u32[]{:S(2)}, u32[]{:S(2)}) collective-permute-start(bf16[8,256,128]{2,1,0:T(8,128)(2,1)S(1)} %get-tuple-element.147.own), channel_id=1, source_target_pairs={{0,8},{1,9},{2,10},{3,11},{12,4},{13,5},{14,6},{15,7},{4,0},{5,1},... | collective-permute-start | bytes 1572872 | tf_op jit(solution)/shard_map/ppermute | solution.py:381
  64.1 6.3 %collective-permute-done.19.refs_0_ = bf16[3,256,128]{2,1,0:T(8,128)(2,1)S(1)} collective-permute-done((bf16[3,256,128]{2,1,0:T(8,128)(2,1)S(1)}, bf16[3,256,128]{2,1,0:T(8,128)(2,1)S(1)}, u32[]{:S(2)}, u32[]{:S(2)}) %collective-permute-start.19) | collective-permute-done | bytes 196640 | tf_op jit(solution)/shard_map/ppermute | solution.py:385
  70.4 2.5 %collective-permute-done.20.refs_1_ = bf16[3,256,128]{2,1,0:T(8,128)(2,1)S(1)} collective-permute-done((bf16[3,256,128]{2,1,0:T(8,128)(2,1)S(1)}, bf16[3,256,128]{2,1,0:T(8,128)(2,1)S(1)}, u32[]{:S(2)}, u32[]{:S(2)}) %collective-permute-start.20) | collective-permute-done | bytes 196640 | tf_op jit(solution)/shard_map/ppermute | solution.py:385
  78.6 6.4 %collective-permute-done.26.refs_2_ = bf16[3,256,128]{2,1,0:T(8,128)(2,1)S(1)} collective-permute-done((bf16[3,256,128]{2,1,0:T(8,128)(2,1)S(1)}, bf16[3,256,128]{2,1,0:T(8,128)(2,1)S(1)}, u32[]{:S(2)}, u32[]{:S(2)}) %collective-permute-start.26) | collective-permute-done | bytes 196640 | tf_op jit(solution)/shard_map/ppermute | solution.py:385
  90.1 8.4 %collective-permute-done.22.refs_2_.out = bf16[8,256,128]{2,1,0:T(8,128)(2,1)S(1)} collective-permute-done((bf16[8,256,128]{2,1,0:T(8,128)(2,1)S(1)}, bf16[8,256,128]{2,1,0:T(8,128)(2,1)S(1)}, u32[]{:S(2)}, u32[]{:S(2)}) %collective-permute-start.22) | collective-permute-done | bytes 524320 | tf_op jit(solution)/shard_map/ppermute | solution.py:381
  101.2 3.5 %shard_map.95.field = f32[9,256,128]{2,1,0:T(8,128)S(1)} custom-call(s32[180]{0:T(256)S(1)} %get-tuple-element.120.refs_0_.table, bf16[48,256,256]{2,1,0:T(8,128)(2,1)S(1)} %copy-done.1, bf16[8,256,128]{2,1,0:T(8,128)(2,1)S(1)} %get-tuple-element.147.own, bf16[8,256,128]{2,1,0:T(8,128)(2,1)S(1)} %collective-permute-done.18.refs_1_.first, ...), custom_call_target="tpu_custom_call" | custom-call | tf_op jit(solution)/shard_map/pallas_call | solution.py:281
  104.7 2.3 %collective-permute-done.23.got2 = bf16[3,256,128]{2,1,0:T(8,128)(2,1)S(1)} collective-permute-done((bf16[3,256,128]{2,1,0:T(8,128)(2,1)S(1)}, bf16[3,256,128]{2,1,0:T(8,128)(2,1)S(1)}, u32[]{:S(2)}, u32[]{:S(2)}) %collective-permute-start.23) | collective-permute-done | bytes 196640 | tf_op jit(solution)/shard_map/ppermute | solution.py:385
  107.0 3.3 %collective-permute-done.24.got3 = bf16[3,256,128]{2,1,0:T(8,128)(2,1)S(1)} collective-permute-done((bf16[3,256,128]{2,1,0:T(8,128)(2,1)S(1)}, bf16[3,256,128]{2,1,0:T(8,128)(2,1)S(1)}, u32[]{:S(2)}, u32[]{:S(2)}) %collective-permute-start.24) | collective-permute-done | bytes 196640 | tf_op jit(solution)/shard_map/ppermute | solution.py:385
  115.9 5.7 %collective-permute-done.34.refs_0_ = bf16[3,256,128]{2,1,0:T(8,128)(2,1)S(1)} collective-permute-done((bf16[3,256,128]{2,1,0:T(8,128)(2,1)S(1)}, bf16[3,256,128]{2,1,0:T(8,128)(2,1)S(1)}, u32[]{:S(2)}, u32[]{:S(2)}) %collective-permute-start.34) | collective-permute-done | bytes 196640 | tf_op jit(solution)/shard_map/ppermute | solution.py:385
  121.6 3.4 %collective-permute-done.35.refs_1_ = bf16[3,256,128]{2,1,0:T(8,128)(2,1)S(1)} collective-permute-done((bf16[3,256,128]{2,1,0:T(8,128)(2,1)S(1)}, bf16[3,256,128]{2,1,0:T(8,128)(2,1)S(1)}, u32[]{:S(2)}, u32[]{:S(2)}) %collective-permute-start.35) | collective-permute-done | bytes 196640 | tf_op jit(solution)/shard_map/ppermute | solution.py:385
  130.6 6.3 %collective-permute-done.41.refs_2_ = bf16[3,256,128]{2,1,0:T(8,128)(2,1)S(1)} collective-permute-done((bf16[3,256,128]{2,1,0:T(8,128)(2,1)S(1)}, bf16[3,256,128]{2,1,0:T(8,128)(2,1)S(1)}, u32[]{:S(2)}, u32[]{:S(2)}) %collective-permute-start.41) | collective-permute-done | bytes 196640 | tf_op jit(solution)/shard_map/ppermute | solution.py:385
  142.4 8.5 %collective-permute-done.37.refs_2_.out = bf16[8,256,128]{2,1,0:T(8,128)(2,1)S(1)} collective-permute-done((bf16[8,256,128]{2,1,0:T(8,128)(2,1)S(1)}, bf16[8,256,128]{2,1,0:T(8,128)(2,1)S(1)}, u32[]{:S(2)}, u32[]{:S(2)}) %collective-permute-start.37) | collective-permute-done | bytes 524320 | tf_op jit(solution)/shard_map/ppermute | solution.py:381
  153.6 3.5 %shard_map.100.field = f32[9,256,128]{2,1,0:T(8,128)S(1)} custom-call(s32[180]{0:T(256)S(1)} %get-tuple-element.120.refs_0_.table, bf16[48,256,256]{2,1,0:T(8,128)(2,1)S(1)} %copy-done.1, bf16[8,256,128]{2,1,0:T(8,128)(2,1)S(1)} %get-tuple-element.170.own, bf16[8,256,128]{2,1,0:T(8,128)(2,1)S(1)} %collective-permute-done.33.refs_1_.first, ...), custom_call_target="tpu_custom_call" | custom-call | tf_op jit(solution)/shard_map/pallas_call | solution.py:281
  157.1 2.3 %collective-permute-done.38.got2 = bf16[3,256,128]{2,1,0:T(8,128)(2,1)S(1)} collective-permute-done((bf16[3,256,128]{2,1,0:T(8,128)(2,1)S(1)}, bf16[3,256,128]{2,1,0:T(8,128)(2,1)S(1)}, u32[]{:S(2)}, u32[]{:S(2)}) %collective-permute-start.38) | collective-permute-done | bytes 196640 | tf_op jit(solution)/shard_map/ppermute | solution.py:385
  159.4 3.3 %collective-permute-done.39.got3 = bf16[3,256,128]{2,1,0:T(8,128)(2,1)S(1)} collective-permute-done((bf16[3,256,128]{2,1,0:T(8,128)(2,1)S(1)}, bf16[3,256,128]{2,1,0:T(8,128)(2,1)S(1)}, u32[]{:S(2)}, u32[]{:S(2)}) %collective-permute-start.39) | collective-permute-done | bytes 196640 | tf_op jit(solution)/shard_map/ppermute | solution.py:385
  168.1 6.0 %collective-permute-done.49.refs_0_ = bf16[3,256,128]{2,1,0:T(8,128)(2,1)S(1)} collective-permute-done((bf16[3,256,128]{2,1,0:T(8,128)(2,1)S(1)}, bf16[3,256,128]{2,1,0:T(8,128)(2,1)S(1)}, u32[]{:S(2)}, u32[]{:S(2)}) %collective-permute-start.49) | collective-permute-done | bytes 196640 | tf_op jit(solution)/shard_map/ppermute | solution.py:385
  174.1 2.5 %collective-permute-done.50.refs_1_ = bf16[3,256,128]{2,1,0:T(8,128)(2,1)S(1)} collective-permute-done((bf16[3,256,128]{2,1,0:T(8,128)(2,1)S(1)}, bf16[3,256,128]{2,1,0:T(8,128)(2,1)S(1)}, u32[]{:S(2)}, u32[]{:S(2)}) %collective-permute-start.50) | collective-permute-done | bytes 196640 | tf_op jit(solution)/shard_map/ppermute | solution.py:385
  182.5 6.4 %collective-permute-done.56.refs_2_ = bf16[3,256,128]{2,1,0:T(8,128)(2,1)S(1)} collective-permute-done((bf16[3,256,128]{2,1,0:T(8,128)(2,1)S(1)}, bf16[3,256,128]{2,1,0:T(8,128)(2,1)S(1)}, u32[]{:S(2)}, u32[]{:S(2)}) %collective-permute-start.56) | collective-permute-done | bytes 196640 | tf_op jit(solution)/shard_map/ppermute | solution.py:385
  193.8 8.4 %collective-permute-done.52.refs_2_.out = bf16[8,256,128]{2,1,0:T(8,128)(2,1)S(1)} collective-permute-done((bf16[8,256,128]{2,1,0:T(8,128)(2,1)S(1)}, bf16[8,256,128]{2,1,0:T(8,128)(2,1)S(1)}, u32[]{:S(2)}, u32[]{:S(2)}) %collective-permute-start.52) | collective-permute-done | bytes 524320 | tf_op jit(solution)/shard_map/ppermute | solution.py:381
  204.7 3.5 %shard_map.105.field = f32[9,256,128]{2,1,0:T(8,128)S(1)} custom-call(s32[180]{0:T(256)S(1)} %get-tuple-element.120.refs_0_.table, bf16[48,256,256]{2,1,0:T(8,128)(2,1)S(1)} %copy-done.1, bf16[8,256,128]{2,1,0:T(8,128)(2,1)S(1)} %get-tuple-element.193.own, bf16[8,256,128]{2,1,0:T(8,128)(2,1)S(1)} %collective-permute-done.48.refs_1_.first, ...), custom_call_target="tpu_custom_call" | custom-call | tf_op jit(solution)/shard_map/pallas_call | solution.py:281
  208.2 2.4 %collective-permute-done.53.got2 = bf16[3,256,128]{2,1,0:T(8,128)(2,1)S(1)} collective-permute-done((bf16[3,256,128]{2,1,0:T(8,128)(2,1)S(1)}, bf16[3,256,128]{2,1,0:T(8,128)(2,1)S(1)}, u32[]{:S(2)}, u32[]{:S(2)}) %collective-permute-start.53) | collective-permute-done | bytes 196640 | tf_op jit(solution)/shard_map/ppermute | solution.py:385
  210.6 3.3 %collective-permute-done.54.got3 = bf16[3,256,128]{2,1,0:T(8,128)(2,1)S(1)} collective-permute-done((bf16[3,256,128]{2,1,0:T(8,128)(2,1)S(1)}, bf16[3,256,128]{2,1,0:T(8,128)(2,1)S(1)}, u32[]{:S(2)}, u32[]{:S(2)}) %collective-permute-start.54) | collective-permute-done | bytes 196640 | tf_op jit(solution)/shard_map/ppermute | solution.py:385
  215.6 4.8 %all-to-all-start = ((f32[16,1,128]{2,1,0:T(1,128)}), f32[16,1,128]{2,1,0:T(1,128)S(1)}, u32[]{:S(2)}, u32[]{:S(2)}) async-start(f32[16,1,128]{2,1,0:T(1,128)} %get-tuple-element.214), calls=%async_computation | async-start | bytes 16384 | tf_op jit(solution)/shard_map/all_to_all | solution.py:389
  222.6 4.3 %all-to-all-done = f32[16,1,128]{2,1,0:T(1,128)S(1)} async-done(((f32[16,1,128]{2,1,0:T(1,128)}), f32[16,1,128]{2,1,0:T(1,128)S(1)}, u32[]{:S(2)}, u32[]{:S(2)}) %all-to-all-start) | async-done | bytes 8224 | tf_op jit(solution)/shard_map/all_to_all | solution.py:389
  (139 shorter events, 84.6 us)
Async XLA Ops:
  1.9 16.5 %collective-permute-start = (bf16[8,256,128]{2,1,0:T(8,128)(2,1)S(1)}, bf16[8,256,128]{2,1,0:T(8,128)(2,1)S(1)}, u32[]{:S(2)}, u32[]{:S(2)}) collective-permute-start(bf16[8,256,128]{2,1,0:T(8,128)(2,1)S(1)} %convert_element_type.3.own.refs_1_), channel_id=1, source_target_pairs={{0,8},{1,9},{2,10},{3,11},{12,4},{13,5},{14,6},{15,7},{4,0},{5,1},... | collective-permute-start | bytes 1572872 | tf_op jit(solution)/shard_map/ppermute | solution.py:381
  12.2 18.1 %collective-permute-start.4 = (bf16[8,256,128]{2,1,0:T(8,128)(2,1)S(1)}, bf16[8,256,128]{2,1,0:T(8,128)(2,1)S(1)}, u32[]{:S(2)}, u32[]{:S(2)}) collective-permute-start(bf16[8,256,128]{2,1,0:T(8,128)(2,1)S(1)} %convert_element_type.3.own.refs_1_), channel_id=1, source_target_pairs={{0,4},{1,5},{2,6},{3,7},{12,8},{13,9},{14,10},{15,11},{4,12},{5,13... | collective-permute-start | bytes 1572872 | tf_op jit(solution)/shard_map/ppermute | solution.py:381
  20.5 12.6 %collective-permute-start.5 = (bf16[6,256,128]{2,1,0:T(8,128)(2,1)S(1)}, bf16[6,256,128]{2,1,0:T(8,128)(2,1)S(1)}, u32[]{:S(2)}, u32[]{:S(2)}) collective-permute-start(bf16[6,256,128]{2,1,0:T(8,128)(2,1)S(1)} %get-tuple-element.121), channel_id=1, source_target_pairs={{0,2},{1,3},{2,0},{3,1},{4,6},{5,7},{6,4},{7,5},{8,10},{9,11},{10,... | collective-permute-start | bytes 1179656 | tf_op jit(solution)/shard_map/ppermute | solution.py:385
  22.1 14.8 %collective-permute-start.6 = (bf16[6,256,128]{2,1,0:T(8,128)(2,1)S(1)}, bf16[6,256,128]{2,1,0:T(8,128)(2,1)S(1)}, u32[]{:S(2)}, u32[]{:S(2)}) collective-permute-start(bf16[6,256,128]{2,1,0:T(8,128)(2,1)S(1)} %get-tuple-element.122), channel_id=1, source_target_pairs={{0,3},{1,2},{2,1},{3,0},{4,7},{5,6},{6,5},{7,4},{8,11},{9,10},{10,... | collective-permute-start | bytes 1179656 | tf_op jit(solution)/shard_map/ppermute | solution.py:385
  22.1 18.8 %collective-permute-start.9 = (bf16[8,256,128]{2,1,0:T(8,128)(2,1)S(1)}, bf16[8,256,128]{2,1,0:T(8,128)(2,1)S(1)}, u32[]{:S(2)}, u32[]{:S(2)}) collective-permute-start(bf16[8,256,128]{2,1,0:T(8,128)(2,1)S(1)} %convert_element_type.3.own.refs_1_), channel_id=1, source_target_pairs={{4,8},{5,9},{6,10},{7,11},{8,4},{9,5},{10,6},{11,7},{20,24},{21,25... | collective-permute-start | bytes 1572872 | tf_op jit(solution)/shard_map/ppermute | solution.py:381
  22.8 18.9 %collective-permute-start.10 = (bf16[8,256,128]{2,1,0:T(8,128)(2,1)S(1)}, bf16[8,256,128]{2,1,0:T(8,128)(2,1)S(1)}, u32[]{:S(2)}, u32[]{:S(2)}) collective-permute-start(bf16[8,256,128]{2,1,0:T(8,128)(2,1)S(1)} %collective-permute-done.first.refs_2_), channel_id=1, source_target_pairs={{4,0},{5,1},{6,2},{7,3},{8,12},{9,13},{10,14},{11,15},{20,16},{21,... | collective-permute-start | bytes 1572872 | tf_op jit(solution)/shard_map/ppermute | solution.py:381
  37.5 15.6 %collective-permute-start.12 = (bf16[9,256,128]{2,1,0:T(8,128)(2,1)S(1)}, bf16[9,256,128]{2,1,0:T(8,128)(2,1)S(1)}, u32[]{:S(2)}, u32[]{:S(2)}) collective-permute-start(bf16[9,256,128]{2,1,0:T(8,128)(2,1)S(1)} %get-tuple-element.132), channel_id=1, source_target_pairs={{0,1},{1,0},{2,3},{3,2},{4,5},{5,4},{6,7},{7,6},{8,9},{9,8},{10,11... | collective-permute-start | bytes 1769480 | tf_op jit(solution)/shard_map/ppermute | solution.py:385
  42.3 10.8 %collective-permute-start.13 = (bf16[3,256,128]{2,1,0:T(8,128)(2,1)S(1)}, bf16[3,256,128]{2,1,0:T(8,128)(2,1)S(1)}, u32[]{:S(2)}, u32[]{:S(2)}) collective-permute-start(bf16[3,256,128]{2,1,0:T(8,128)(2,1)S(1)} %get-tuple-element.133), channel_id=1, source_target_pairs={{0,1},{1,0},{2,3},{3,2},{4,5},{5,4},{6,7},{7,6},{8,9},{9,8},{10,11... | collective-permute-start | bytes 589832 | tf_op jit(solution)/shard_map/ppermute | solution.py:385
  46.0 12.0 %collective-permute-start.15 = (bf16[3,256,128]{2,1,0:T(8,128)(2,1)S(1)}, bf16[3,256,128]{2,1,0:T(8,128)(2,1)S(1)}, u32[]{:S(2)}, u32[]{:S(2)}) collective-permute-start(bf16[3,256,128]{2,1,0:T(8,128)(2,1)S(1)} %get-tuple-element.139), channel_id=1, source_target_pairs={{0,2},{1,3},{2,0},{3,1},{4,6},{5,7},{6,4},{7,5},{8,10},{9,11},{10,... | collective-permute-start | bytes 589832 | tf_op jit(solution)/shard_map/ppermute | solution.py:385
  47.2 10.9 %collective-permute-start.16 = (bf16[3,256,128]{2,1,0:T(8,128)(2,1)S(1)}, bf16[3,256,128]{2,1,0:T(8,128)(2,1)S(1)}, u32[]{:S(2)}, u32[]{:S(2)}) collective-permute-start(bf16[3,256,128]{2,1,0:T(8,128)(2,1)S(1)} %get-tuple-element.140), channel_id=1, source_target_pairs={{0,3},{1,2},{2,1},{3,0},{4,7},{5,6},{6,5},{7,4},{8,11},{9,10},{10,... | collective-permute-start | bytes 589832 | tf_op jit(solution)/shard_map/ppermute | solution.py:385
  59.5 15.1 %collective-permute-start.18 = (bf16[8,256,128]{2,1,0:T(8,128)(2,1)S(1)}, bf16[8,256,128]{2,1,0:T(8,128)(2,1)S(1)}, u32[]{:S(2)}, u32[]{:S(2)}) collective-permute-start(bf16[8,256,128]{2,1,0:T(8,128)(2,1)S(1)} %get-tuple-element.147.own), channel_id=1, source_target_pairs={{0,8},{1,9},{2,10},{3,11},{12,4},{13,5},{14,6},{15,7},{4,0},{5,1},... | collective-permute-start | bytes 1572872 | tf_op jit(solution)/shard_map/ppermute | solution.py:381
  64.1 23.3 %collective-permute-start.25 = (bf16[8,256,128]{2,1,0:T(8,128)(2,1)S(1)}, bf16[8,256,128]{2,1,0:T(8,128)(2,1)S(1)}, u32[]{:S(2)}, u32[]{:S(2)}) collective-permute-start(bf16[8,256,128]{2,1,0:T(8,128)(2,1)S(1)} %get-tuple-element.147.own), channel_id=1, source_target_pairs={{0,4},{1,5},{2,6},{3,7},{12,8},{13,9},{14,10},{15,11},{4,12},{5,13... | collective-permute-start | bytes 1572872 | tf_op jit(solution)/shard_map/ppermute | solution.py:381
  74.6 15.5 %collective-permute-start.21 = (bf16[8,256,128]{2,1,0:T(8,128)(2,1)S(1)}, bf16[8,256,128]{2,1,0:T(8,128)(2,1)S(1)}, u32[]{:S(2)}, u32[]{:S(2)}) collective-permute-start(bf16[8,256,128]{2,1,0:T(8,128)(2,1)S(1)} %get-tuple-element.147.own), channel_id=1, source_target_pairs={{4,8},{5,9},{6,10},{7,11},{8,4},{9,5},{10,6},{11,7},{20,24},{21,25... | collective-permute-start | bytes 1572872 | tf_op jit(solution)/shard_map/ppermute | solution.py:381
  75.3 23.3 %collective-permute-start.22 = (bf16[8,256,128]{2,1,0:T(8,128)(2,1)S(1)}, bf16[8,256,128]{2,1,0:T(8,128)(2,1)S(1)}, u32[]{:S(2)}, u32[]{:S(2)}) collective-permute-start(bf16[8,256,128]{2,1,0:T(8,128)(2,1)S(1)} %collective-permute-done.18.refs_1_.first), channel_id=1, source_target_pairs={{4,0},{5,1},{6,2},{7,3},{8,12},{9,13},{10,14},{11,15},{20,16},{21,... | collective-permute-start | bytes 1572872 | tf_op jit(solution)/shard_map/ppermute | solution.py:381
  88.0 13.2 %collective-permute-start.28 = (bf16[6,256,128]{2,1,0:T(8,128)(2,1)S(1)}, bf16[6,256,128]{2,1,0:T(8,128)(2,1)S(1)}, u32[]{:S(2)}, u32[]{:S(2)}) collective-permute-start(bf16[6,256,128]{2,1,0:T(8,128)(2,1)S(1)} %get-tuple-element.154), channel_id=1, source_target_pairs={{0,1},{1,0},{2,3},{3,2},{4,5},{5,4},{6,7},{7,6},{8,9},{9,8},{10,11... | collective-permute-start | bytes 1179656 | tf_op jit(solution)/shard_map/ppermute | solution.py:385
  88.6 12.1 %collective-permute-start.30 = (bf16[3,256,128]{2,1,0:T(8,128)(2,1)S(1)}, bf16[3,256,128]{2,1,0:T(8,128)(2,1)S(1)}, u32[]{:S(2)}, u32[]{:S(2)}) collective-permute-start(bf16[3,256,128]{2,1,0:T(8,128)(2,1)S(1)} %get-tuple-element.160), channel_id=1, source_target_pairs={{0,2},{1,3},{2,0},{3,1},{4,6},{5,7},{6,4},{7,5},{8,10},{9,11},{10,... | collective-permute-start | bytes 589832 | tf_op jit(solution)/shard_map/ppermute | solution.py:385
  90.1 11.1 %collective-permute-start.31 = (bf16[3,256,128]{2,1,0:T(8,128)(2,1)S(1)}, bf16[3,256,128]{2,1,0:T(8,128)(2,1)S(1)}, u32[]{:S(2)}, u32[]{:S(2)}) collective-permute-start(bf16[3,256,128]{2,1,0:T(8,128)(2,1)S(1)} %get-tuple-element.161), channel_id=1, source_target_pairs={{0,3},{1,2},{2,1},{3,0},{4,7},{5,6},{6,5},{7,4},{8,11},{9,10},{10,... | collective-permute-start | bytes 589832 | tf_op jit(solution)/shard_map/ppermute | solution.py:385
  111.7 14.8 %collective-permute-start.33 = (bf16[8,256,128]{2,1,0:T(8,128)(2,1)S(1)}, bf16[8,256,128]{2,1,0:T(8,128)(2,1)S(1)}, u32[]{:S(2)}, u32[]{:S(2)}) collective-permute-start(bf16[8,256,128]{2,1,0:T(8,128)(2,1)S(1)} %get-tuple-element.170.own), channel_id=1, source_target_pairs={{0,8},{1,9},{2,10},{3,11},{12,4},{13,5},{14,6},{15,7},{4,0},{5,1},... | collective-permute-start | bytes 1572872 | tf_op jit(solution)/shard_map/ppermute | solution.py:381
  115.8 24.1 %collective-permute-start.40 = (bf16[8,256,128]{2,1,0:T(8,128)(2,1)S(1)}, bf16[8,256,128]{2,1,0:T(8,128)(2,1)S(1)}, u32[]{:S(2)}, u32[]{:S(2)}) collective-permute-start(bf16[8,256,128]{2,1,0:T(8,128)(2,1)S(1)} %get-tuple-element.170.own), channel_id=1, source_target_pairs={{0,4},{1,5},{2,6},{3,7},{12,8},{13,9},{14,10},{15,11},{4,12},{5,13... | collective-permute-start | bytes 1572872 | tf_op jit(solution)/shard_map/ppermute | solution.py:381
  126.5 15.9 %collective-permute-start.36 = (bf16[8,256,128]{2,1,0:T(8,128)(2,1)S(1)}, bf16[8,256,128]{2,1,0:T(8,128)(2,1)S(1)}, u32[]{:S(2)}, u32[]{:S(2)}) collective-permute-start(bf16[8,256,128]{2,1,0:T(8,128)(2,1)S(1)} %get-tuple-element.170.own), channel_id=1, source_target_pairs={{4,8},{5,9},{6,10},{7,11},{8,4},{9,5},{10,6},{11,7},{20,24},{21,25... | collective-permute-start | bytes 1572872 | tf_op jit(solution)/shard_map/ppermute | solution.py:381
  127.2 23.8 %collective-permute-start.37 = (bf16[8,256,128]{2,1,0:T(8,128)(2,1)S(1)}, bf16[8,256,128]{2,1,0:T(8,128)(2,1)S(1)}, u32[]{:S(2)}, u32[]{:S(2)}) collective-permute-start(bf16[8,256,128]{2,1,0:T(8,128)(2,1)S(1)} %collective-permute-done.33.refs_1_.first), channel_id=1, source_target_pairs={{4,0},{5,1},{6,2},{7,3},{8,12},{9,13},{10,14},{11,15},{20,16},{21,... | collective-permute-start | bytes 1572872 | tf_op jit(solution)/shard_map/ppermute | solution.py:381
  140.4 13.2 %collective-permute-start.43 = (bf16[6,256,128]{2,1,0:T(8,128)(2,1)S(1)}, bf16[6,256,128]{2,1,0:T(8,128)(2,1)S(1)}, u32[]{:S(2)}, u32[]{:S(2)}) collective-permute-start(bf16[6,256,128]{2,1,0:T(8,128)(2,1)S(1)} %get-tuple-element.177), channel_id=1, source_target_pairs={{0,1},{1,0},{2,3},{3,2},{4,5},{5,4},{6,7},{7,6},{8,9},{9,8},{10,11... | collective-permute-start | bytes 1179656 | tf_op jit(solution)/shard_map/ppermute | solution.py:385
  140.9 12.3 %collective-permute-start.45 = (bf16[3,256,128]{2,1,0:T(8,128)(2,1)S(1)}, bf16[3,256,128]{2,1,0:T(8,128)(2,1)S(1)}, u32[]{:S(2)}, u32[]{:S(2)}) collective-permute-start(bf16[3,256,128]{2,1,0:T(8,128)(2,1)S(1)} %get-tuple-element.183), channel_id=1, source_target_pairs={{0,2},{1,3},{2,0},{3,1},{4,6},{5,7},{6,4},{7,5},{8,10},{9,11},{10,... | collective-permute-start | bytes 589832 | tf_op jit(solution)/shard_map/ppermute | solution.py:385
  142.4 11.2 %collective-permute-start.46 = (bf16[3,256,128]{2,1,0:T(8,128)(2,1)S(1)}, bf16[3,256,128]{2,1,0:T(8,128)(2,1)S(1)}, u32[]{:S(2)}, u32[]{:S(2)}) collective-permute-start(bf16[3,256,128]{2,1,0:T(8,128)(2,1)S(1)} %get-tuple-element.184), channel_id=1, source_target_pairs={{0,3},{1,2},{2,1},{3,0},{4,7},{5,6},{6,5},{7,4},{8,11},{9,10},{10,... | collective-permute-start | bytes 589832 | tf_op jit(solution)/shard_map/ppermute | solution.py:385
  164.1 14.3 %collective-permute-start.48 = (bf16[8,256,128]{2,1,0:T(8,128)(2,1)S(1)}, bf16[8,256,128]{2,1,0:T(8,128)(2,1)S(1)}, u32[]{:S(2)}, u32[]{:S(2)}) collective-permute-start(bf16[8,256,128]{2,1,0:T(8,128)(2,1)S(1)} %get-tuple-element.193.own), channel_id=1, source_target_pairs={{0,8},{1,9},{2,10},{3,11},{12,4},{13,5},{14,6},{15,7},{4,0},{5,1},... | collective-permute-start | bytes 1572872 | tf_op jit(solution)/shard_map/ppermute | solution.py:381
  167.8 23.2 %collective-permute-start.55 = (bf16[8,256,128]{2,1,0:T(8,128)(2,1)S(1)}, bf16[8,256,128]{2,1,0:T(8,128)(2,1)S(1)}, u32[]{:S(2)}, u32[]{:S(2)}) collective-permute-start(bf16[8,256,128]{2,1,0:T(8,128)(2,1)S(1)} %get-tuple-element.193.own), channel_id=1, source_target_pairs={{0,4},{1,5},{2,6},{3,7},{12,8},{13,9},{14,10},{15,11},{4,12},{5,13... | collective-permute-start | bytes 1572872 | tf_op jit(solution)/shard_map/ppermute | solution.py:381
  178.4 15.4 %collective-permute-start.51 = (bf16[8,256,128]{2,1,0:T(8,128)(2,1)S(1)}, bf16[8,256,128]{2,1,0:T(8,128)(2,1)S(1)}, u32[]{:S(2)}, u32[]{:S(2)}) collective-permute-start(bf16[8,256,128]{2,1,0:T(8,128)(2,1)S(1)} %get-tuple-element.193.own), channel_id=1, source_target_pairs={{4,8},{5,9},{6,10},{7,11},{8,4},{9,5},{10,6},{11,7},{20,24},{21,25... | collective-permute-start | bytes 1572872 | tf_op jit(solution)/shard_map/ppermute | solution.py:381
  179.1 23.1 %collective-permute-start.52 = (bf16[8,256,128]{2,1,0:T(8,128)(2,1)S(1)}, bf16[8,256,128]{2,1,0:T(8,128)(2,1)S(1)}, u32[]{:S(2)}, u32[]{:S(2)}) collective-permute-start(bf16[8,256,128]{2,1,0:T(8,128)(2,1)S(1)} %collective-permute-done.48.refs_1_.first), channel_id=1, source_target_pairs={{4,0},{5,1},{6,2},{7,3},{8,12},{9,13},{10,14},{11,15},{20,16},{21,... | collective-permute-start | bytes 1572872 | tf_op jit(solution)/shard_map/ppermute | solution.py:381
  191.7 13.1 %collective-permute-start.58 = (bf16[6,256,128]{2,1,0:T(8,128)(2,1)S(1)}, bf16[6,256,128]{2,1,0:T(8,128)(2,1)S(1)}, u32[]{:S(2)}, u32[]{:S(2)}) collective-permute-start(bf16[6,256,128]{2,1,0:T(8,128)(2,1)S(1)} %get-tuple-element.200), channel_id=1, source_target_pairs={{0,1},{1,0},{2,3},{3,2},{4,5},{5,4},{6,7},{7,6},{8,9},{9,8},{10,11... | collective-permute-start | bytes 1179656 | tf_op jit(solution)/shard_map/ppermute | solution.py:385
  192.3 12.1 %collective-permute-start.60 = (bf16[3,256,128]{2,1,0:T(8,128)(2,1)S(1)}, bf16[3,256,128]{2,1,0:T(8,128)(2,1)S(1)}, u32[]{:S(2)}, u32[]{:S(2)}) collective-permute-start(bf16[3,256,128]{2,1,0:T(8,128)(2,1)S(1)} %get-tuple-element.206), channel_id=1, source_target_pairs={{0,2},{1,3},{2,0},{3,1},{4,6},{5,7},{6,4},{7,5},{8,10},{9,11},{10,... | collective-permute-start | bytes 589832 | tf_op jit(solution)/shard_map/ppermute | solution.py:385
  193.8 10.9 %collective-permute-start.61 = (bf16[3,256,128]{2,1,0:T(8,128)(2,1)S(1)}, bf16[3,256,128]{2,1,0:T(8,128)(2,1)S(1)}, u32[]{:S(2)}, u32[]{:S(2)}) collective-permute-start(bf16[3,256,128]{2,1,0:T(8,128)(2,1)S(1)} %get-tuple-element.207), channel_id=1, source_target_pairs={{0,3},{1,2},{2,1},{3,0},{4,7},{5,6},{6,5},{7,4},{8,11},{9,10},{10,... | collective-permute-start | bytes 589832 | tf_op jit(solution)/shard_map/ppermute | solution.py:385
  215.6 11.2 %all-to-all-start = ((f32[16,1,128]{2,1,0:T(1,128)}), f32[16,1,128]{2,1,0:T(1,128)S(1)}, u32[]{:S(2)}, u32[]{:S(2)}) async-start(f32[16,1,128]{2,1,0:T(1,128)} %get-tuple-element.214), calls=%async_computation | async-start | bytes 16384 | tf_op jit(solution)/shard_map/all_to_all | solution.py:389
  (37 other events, 248.8 us)
